TPU v7x, 128 devices: a whole 4x4x4 slice. The times are simulated.
128 devices in a mesh: dp: 32 (over x, y, core), mp: 4 (over z).
Axes of the slice: x: 4, y: 4, z: 4, core: 2. Of those that a mesh axis runs over, the one named last changes fastest.
Arguments:
- context: bfloat16 [8192, 5120], P('dp', 'mp'), may hold values from -6 to 6
- residual: bfloat16 [8192, 5120], P('dp', 'mp'), may hold values from -36 to 36
- cotangent: bfloat16 [8192, 5120], P('dp', 'mp'), may hold values from -6 to 6
- out_proj: bfloat16 [5120, 5120], P(None, 'mp'), may hold values from -0.078125 to 0.078125
- norm_gain: float32 [5120], P('mp'), may hold values from 0.1 to 1.9
- rewards: float32 [128], P('dp'), may hold values from -4.2 to 10.2
- group_ids: int32 [128], P('dp'), may hold values from 0 to 7, as said below
- lengths: int32 [128], P('dp'), may hold values from 32 to 64
- destinations: int32 [2048, 1], P('dp'), may hold values from 0 to 31; in each aligned block of 64 rows (0 to 63, 64 to 127, ...) at most 3 rows name the same one
Outputs:
- d_context: bfloat16 [12288, 5120], P('dp', 'mp')
- d_residual: bfloat16 [12288, 5120], P('dp', 'mp')
- d_out_proj: float32 [5120, 5120], P('dp', 'mp')
Inputs may be any that keep to these rules, and one draw needn't show every extreme that they name: `group_ids`: each prompt id is held by exactly 16 responses. `destinations`: among the 64 blocks of one owner no learner is named more than 3 times, a bound that some block reaches.
All inputs are finite; a program needn't handle non-finite values.
Results may differ from a plain program's by a relative error of at most 0.015.
Values may be sent and summed in bfloat16 or wider, within the bound.
No kernel may reach another device: no remote copies, remote signals or barrier semaphores. Data moves between devices by JAX's collectives and lax.ppermute only.
A program may use at most 128 MiB of HBM per device.

v0:
```python
import jax
import jax.numpy as jnp
from jax import lax
from jax.sharding import PartitionSpec as P

LMAX = 64
GROUP = 16
PAIR = 3


EPSILON = 1e-06


def slot_sources(owner_dest, slots):
    count = owner_dest.shape[0]
    same = owner_dest[:, None] == owner_dest[None, :]
    earlier = jnp.arange(count)[None, :] < jnp.arange(count)[:, None]
    rank = jnp.sum((same & earlier).astype(jnp.int32), axis=1)
    target = owner_dest * PAIR + rank
    match = target[:, None] == jnp.arange(slots)[None, :]
    source = jnp.sum(jnp.where(match, jnp.arange(count)[:, None], 0), axis=0)
    filled = jnp.any(match, axis=0)
    return (source, filled)


def arrange(values, source, filled, count):
    blocks = values.reshape((count, values.shape[0] // count) + values.shape[1:])
    taken = jnp.take(blocks, source, axis=0)
    shaped = filled.reshape((-1,) + (1,) * (taken.ndim - 1))
    taken = jnp.where(shaped, taken, jnp.zeros_like(taken))
    return taken.reshape((-1,) + values.shape[1:])


def row_grads(context, residual, cotangent, weights, out_proj, norm_gain):
    attn_t = lax.psum_scatter(
        lax.dot_general(
            out_proj, context, (((1,), (1,)), ((), ())), preferred_element_type=jnp.float32
        ).astype(jnp.bfloat16),
        "mp",
        scatter_dimension=0,
        tiled=True,
    ).astype(jnp.float32)
    hidden_t = residual.T.astype(jnp.float32) + attn_t
    upstream_t = norm_gain[:, None] * (
        weights.astype(jnp.float32)[None, :] * cotangent.T.astype(jnp.float32)
    )
    width = residual.shape[1] * lax.axis_size("mp")
    square_sum, coupling = lax.psum(
        (jnp.sum(hidden_t * hidden_t, axis=0), jnp.sum(upstream_t * hidden_t, axis=0)), "mp"
    )
    inv_rms = lax.rsqrt(square_sum / width + EPSILON)
    grad_t = (
        inv_rms[None, :] * upstream_t - hidden_t * (inv_rms**3 * coupling / width)[None, :]
    ).astype(jnp.bfloat16)
    grad_full = lax.all_gather(grad_t, "mp", axis=0, tiled=True)
    context_grad = lax.dot_general(
        grad_full, out_proj, (((0,), (0,)), ((), ())), preferred_element_type=jnp.float32
    ).astype(jnp.bfloat16)
    return (context_grad, grad_t.T, grad_full)


def per_device(
    context, residual, cotangent, out_proj, norm_gain, rewards, group_ids, lengths, destinations
):
    lanes = lax.axis_size("dp")
    seq_count = rewards.shape[0]
    groups = seq_count * lanes // GROUP
    member = (group_ids[:, None] == jnp.arange(groups)[None, :]).astype(jnp.float32)
    group_total = lax.psum(jnp.sum(member * rewards[:, None], axis=0), "dp")
    advantage = rewards - jnp.sum(member * group_total[None, :], axis=1) / GROUP
    scale = advantage * LMAX / (2.0 * lengths.astype(jnp.float32))
    live = jnp.arange(LMAX)[None, :] < lengths[:, None]
    row_weights = jnp.where(live, scale[:, None], jnp.float32(0.0)).reshape(-1).astype(jnp.bfloat16)
    block_count = destinations.shape[0]
    source, filled = slot_sources(destinations[:, 0], lanes * PAIR)
    packed_context = arrange(context, source, filled, block_count)
    packed_residual = arrange(residual, source, filled, block_count)
    packed_cotangent = arrange(cotangent, source, filled, block_count)
    packed_weights = arrange(row_weights, source, filled, block_count)
    context_rows, residual_rows, cotangent_rows, weight_rows = (
        lax.all_to_all(packed_context, "dp", split_axis=0, concat_axis=0, tiled=True),
        lax.all_to_all(packed_residual, "dp", split_axis=0, concat_axis=0, tiled=True),
        lax.all_to_all(packed_cotangent, "dp", split_axis=0, concat_axis=0, tiled=True),
        lax.all_to_all(packed_weights, "dp", split_axis=0, concat_axis=0, tiled=True),
    )
    d_context, grad_rows, grad_full = row_grads(
        context_rows, residual_rows, cotangent_rows, weight_rows, out_proj, norm_gain
    )
    weight_grad = lax.psum_scatter(
        lax.dot_general(
            grad_full, context_rows, (((1,), (0,)), ((), ())), preferred_element_type=jnp.float32
        ).astype(jnp.bfloat16),
        "dp",
        scatter_dimension=0,
        tiled=True,
    ).astype(jnp.float32)
    return (d_context, grad_rows, weight_grad / lanes)


def solution(mesh):
    placed = (
        P("dp", "mp"),
        P("dp", "mp"),
        P("dp", "mp"),
        P(None, "mp"),
        P("mp"),
        P("dp"),
        P("dp"),
        P("dp"),
        P("dp", None),
    )
    return jax.shard_map(
        per_device,
        mesh=mesh,
        in_specs=placed,
        out_specs=(P("dp", "mp"), P("dp", "mp"), P("dp", "mp")),
        check_vma=False,
    )
```

profile of v0, /device:TPU:1, one launch (start us, length us, event | category | flops | bytes accessed | tf_op | source)
XLA Modules:
  0.0 384.5 jit_solution(18036897706893656696)
XLA Ops:
  7.2 0.9 convert_reduce_fusion
  8.1 0.7 fusion.9
  8.8 0.1 select_reduce_fusion
  8.9 0.1 fusion.4
  9.0 1.6 reshape.132
  10.6 1.6 reshape.133
  12.2 1.4 gather_fusion.1
  13.7 1.4 gather_fusion.2
  15.1 0.2 reshape.134
  15.3 2.4 gather_fusion.3
  17.7 4.3 %select_select_fusion.2 = (bf16[96,4,1280]{2,1,0:T(4,128)(2,1)}, bf16[96,4,1280]{2,1,0:T(4,128)(2,1)S(1)}, bf16[96,4,1280]{2,1,0:T(4,128)(2,1)}) fusion(bf16[96,4,1280]{2,1,0:T(4,128)(2,1)S(1)} %gather_fusion.1, pred[96]{0:T(512)(128)(4,1)S(1)} %compare_and_fusion.1, pred[96]{0:T(512)(128)(4,1)S(1)} %fusion.4, bf16[96,4,1280]{2,1,0:T(4,128)(2,1)S(1)} %gather_fusion.2, ...), kind=kLoop, calls=%fused_computation.18 | loop fusion | flops 2949120 | bytes 5898432 | tf_op jit(solution)/shard_map/jit(_where)/select_n | solution.py:30
  21.9 0.3 all_to_all.26
  22.2 28.6 %all_to_all.36 = bf16[32,12,1280]{2,1,0:T(8,128)(2,1)S(1)} all-to-all(bf16[32,12,1280]{2,1,0:T(8,128)(2,1)S(1)} %all_to_all.26), channel_id=1, replica_groups=mesh['dp'=32,'mp'=4] {'dp'}, dimensions={0} | all-to-all | bytes 1966080 | tf_op jit(solution)/shard_map/all_to_all | solution.py:81
  50.8 0.2 all_to_all.28
  51.1 19.2 %fusion = bf16[5120,384]{0,1:T(8,128)(2,1)} fusion(bf16[384,1280]{1,0:T(8,128)(2,1)S(1)} %all_to_all.28, bf16[5120,1280]{1,0:T(8,128)(2,1)} %param.14), kind=kOutput, calls=%fused_computation.6 | convolution fusion | flops 5035130880 | bytes 18022400 | tf_op jit(solution)/shard_map/dot_general | solution.py:36
  70.4 0.6 copy-done.7
  71.0 0.1 select_reduce_fusion.2
  71.1 62.2 %psum.22 = f32[8]{0:T(128)S(1)} all-reduce(f32[8]{0:T(128)S(1)} %select_reduce_fusion.2), channel_id=1, replica_groups=mesh['dp'=32,'mp'=4] {'dp'}, use_global_device_ids=true, to_apply=%region_7.9 | all-reduce | flops 8 | bytes 64 | tf_op jit(solution)/shard_map/psum | solution.py:69
  133.3 0.1 reduce_sum.64
  133.4 0.1 broadcast_in_dim.97
  133.5 0.2 select_reduce_fusion.1
  133.8 0.1 broadcast_in_dim.103
  133.9 0.1 lt.79
  134.0 0.1 select_convert_fusion
  134.1 0.7 gather_fusion
  134.8 0.1 gather.10
  135.0 0.1 copy.21
  135.1 0.1 copy.20
  135.3 0.7 copy.23
  136.0 5.9 %all-to-all-start.2 = ((bf16[32,12,1]{1,2,0:T(2,128)(2,1)}), bf16[32,12,1]{1,2,0:T(2,128)(2,1)S(1)}, u32[]{:S(2)}, u32[]{:S(2)}) async-start(bf16[32,12,1]{1,2,0:T(2,128)(2,1)} %copy.23), calls=%async_computation.3 | async-start | bytes 32768 | tf_op jit(solution)/shard_map/all_to_all | solution.py:84
  141.9 1.2 all_to_all.30
  143.2 5.7 %all-to-all-done.2 = bf16[32,12,1]{1,2,0:T(2,128)(2,1)S(1)} async-done(((bf16[32,12,1]{1,2,0:T(2,128)(2,1)}), bf16[32,12,1]{1,2,0:T(2,128)(2,1)S(1)}, u32[]{:S(2)}, u32[]{:S(2)}) %all-to-all-start.2) | async-done | bytes 800 | tf_op jit(solution)/shard_map/all_to_all | solution.py:84
  148.9 4.3 %all-to-all-start.3 = ((bf16[32,12,1280]{2,1,0:T(8,128)(2,1)}), bf16[32,12,1280]{2,1,0:T(8,128)(2,1)S(1)}, u32[]{:S(2)}, u32[]{:S(2)}) async-start(bf16[32,12,1280]{2,1,0:T(8,128)(2,1)} %all_to_all.30), calls=%async_computation.4 | async-start | bytes 2621440 | tf_op jit(solution)/shard_map/all_to_all | solution.py:83
  153.1 1.2 all_to_all.24
  154.4 18.6 %all-to-all-done.3 = bf16[32,12,1280]{2,1,0:T(8,128)(2,1)S(1)} async-done(((bf16[32,12,1280]{2,1,0:T(8,128)(2,1)}), bf16[32,12,1280]{2,1,0:T(8,128)(2,1)S(1)}, u32[]{:S(2)}, u32[]{:S(2)}) %all-to-all-start.3) | async-done | bytes 983072 | tf_op jit(solution)/shard_map/all_to_all | solution.py:83
  173.0 4.7 %all-to-all-start = ((bf16[32,12,1280]{2,1,0:T(8,128)(2,1)}), bf16[32,12,1280]{2,1,0:T(8,128)(2,1)}, u32[]{:S(2)}, u32[]{:S(2)}) async-start(bf16[32,12,1280]{2,1,0:T(8,128)(2,1)} %all_to_all.24), calls=%async_computation | async-start | bytes 2621440 | tf_op jit(solution)/shard_map/all_to_all | solution.py:82
  177.8 0.1 reshape.135
  177.9 0.2 reshape.136
  178.2 19.5 %all-to-all-done = bf16[32,12,1280]{2,1,0:T(8,128)(2,1)} async-done(((bf16[32,12,1280]{2,1,0:T(8,128)(2,1)}), bf16[32,12,1280]{2,1,0:T(8,128)(2,1)}, u32[]{:S(2)}, u32[]{:S(2)}) %all-to-all-start) | async-done | bytes 983072 | tf_op jit(solution)/shard_map/all_to_all | solution.py:82
  197.6 2.5 reshape.137
  200.1 2.5 multiply_reduce_fusion
  202.6 9.9 %all-reduce = (f32[384]{0:T(512)S(1)}, f32[384]{0:T(512)S(1)}) all-reduce(f32[384]{0:T(512)S(1)} %get-tuple-element.5, f32[384]{0:T(512)S(1)} %get-tuple-element.4), channel_id=1, replica_groups=mesh['dp'=32,'mp'=4] {'mp'}, use_global_device_ids=true, to_apply=%region_10.12 | all-reduce | flops 768 | bytes 6144 | tf_op jit(solution)/shard_map/psum | solution.py:48
  212.6 3.0 fusion.2
  215.7 43.7 %all-gather.2.cloned.1.call-done = bf16[5120,384]{0,1:T(8,128)(2,1)} async-done(((bf16[1280,384]{0,1:T(8,128)(2,1)}), bf16[5120,384]{0,1:T(8,128)(2,1)}) %all-gather.2.cloned.1.call-update) | async-done | bytes 3932176 | tf_op jit(solution)/shard_map/all_gather | solution.py:55
  259.4 11.7 %convolution_convert_fusion = bf16[5120,1280]{1,0:T(8,128)(2,1)} fusion(bf16[5120,384]{0,1:T(8,128)(2,1)} %all-gather.2.cloned.1.call-done, bf16[384,1280]{1,0:T(8,128)(2,1)} %copy-done.3), kind=kOutput, calls=%fused_computation.4 | convolution fusion | flops 5039718400 | bytes 18022400 | tf_op jit(solution)/shard_map/dot_general | solution.py:90
  271.1 11.5 %convolution_convert_fusion.2 = bf16[384,1280]{1,0:T(8,128)(2,1)} fusion(bf16[5120,384]{0,1:T(8,128)(2,1)} %all-gather.2.cloned.1.call-done, bf16[5120,1280]{1,0:T(8,128)(2,1)} %param.14), kind=kOutput, calls=%fused_computation.7 | convolution fusion | flops 5033656320 | bytes 18022400 | tf_op jit(solution)/shard_map/dot_general | solution.py:56
  282.7 93.4 %reduce-scatter.5.cloned.1.call-done = bf16[160,1280]{1,0:T(8,128)(2,1)} async-done(((bf16[5120,1280]{1,0:T(8,128)(2,1)}), bf16[160,1280]{1,0:T(8,128)(2,1)}) %reduce-scatter.5.cloned.1.call-update) | async-done | bytes 409616 | tf_op jit(solution)/shard_map/reduce_scatter | solution.py:89
  376.1 1.9 convert_multiply_fusion
  (42 shorter events, 0.7 us)
Async XLA Ops:
  7.2 192.9 %reduce-scatter.3.cloned.1.call-start = ((), (), s32[]{:S(2)}) async-start(), calls=%async_computation.6 | async-start | bytes 4915200 | tf_op jit(solution)/shard_map/reduce_scatter | solution.py:35
  12.2 2.9 copy-start.4
  51.1 19.2 %copy-start.3 = (bf16[384,1280]{1,0:T(8,128)(2,1)}, bf16[384,1280]{1,0:T(8,128)(2,1)S(1)}, u32[]{:S(2)}) copy-start(bf16[384,1280]{1,0:T(8,128)(2,1)S(1)} %all_to_all.28) | copy-start | bytes 2949124
  70.3 0.7 copy-start.7
  70.3 0.7 copy-start.8
  70.3 63.4 %copy-start.6 = (s32[4]{0:T(128)S(1)}, s32[4]{0:T(128)}, u32[]{:S(2)}) copy-start(s32[4]{0:T(128)} %param.18) | copy-start | bytes 52
  70.3 71.6 %copy-start.2 = (bf16[96,4,1280]{2,1,0:T(4,128)(2,1)S(1)}, bf16[96,4,1280]{2,1,0:T(4,128)(2,1)}, u32[]{:S(2)}) copy-start(bf16[96,4,1280]{2,1,0:T(4,128)(2,1)} %get-tuple-element.12) | copy-start | bytes 2949124
  136.0 12.9 %all-to-all-start.2 = ((bf16[32,12,1]{1,2,0:T(2,128)(2,1)}), bf16[32,12,1]{1,2,0:T(2,128)(2,1)S(1)}, u32[]{:S(2)}, u32[]{:S(2)}) async-start(bf16[32,12,1]{1,2,0:T(2,128)(2,1)} %copy.23), calls=%async_computation.3 | async-start | bytes 32768 | tf_op jit(solution)/shard_map/all_to_all | solution.py:84
  141.9 11.2 %copy-start.1 = (bf16[96,4,1280]{2,1,0:T(4,128)(2,1)S(1)}, bf16[96,4,1280]{2,1,0:T(4,128)(2,1)}, u32[]{:S(2)}) copy-start(bf16[96,4,1280]{2,1,0:T(4,128)(2,1)} %get-tuple-element.10) | copy-start | bytes 2949124
  148.9 24.2 %all-to-all-start.3 = ((bf16[32,12,1280]{2,1,0:T(8,128)(2,1)}), bf16[32,12,1280]{2,1,0:T(8,128)(2,1)S(1)}, u32[]{:S(2)}, u32[]{:S(2)}) async-start(bf16[32,12,1280]{2,1,0:T(8,128)(2,1)} %all_to_all.30), calls=%async_computation.4 | async-start | bytes 2621440 | tf_op jit(solution)/shard_map/all_to_all | solution.py:83
  173.0 24.6 %all-to-all-start = ((bf16[32,12,1280]{2,1,0:T(8,128)(2,1)}), bf16[32,12,1280]{2,1,0:T(8,128)(2,1)}, u32[]{:S(2)}, u32[]{:S(2)}) async-start(bf16[32,12,1280]{2,1,0:T(8,128)(2,1)} %all_to_all.24), calls=%async_computation | async-start | bytes 2621440 | tf_op jit(solution)/shard_map/all_to_all | solution.py:82
  177.7 81.7 %all-gather.2.cloned.1.call-start = ((), (), s32[]{:S(2)}) async-start(), calls=%async_computation.7 | async-start | bytes 4915200 | tf_op jit(solution)/shard_map/all_gather | solution.py:55
  178.1 22.0 %copy-start.5 = (f32[1280]{0:T(1024)S(1)}, f32[1280]{0:T(1024)}, u32[]{:S(2)}) copy-start(f32[1280]{0:T(1024)} %param.15) | copy-start | bytes 15364
  200.1 12.5 %copy-start = (bf16[1280,384]{0,1:T(8,128)(2,1)S(1)}, bf16[1280,384]{0,1:T(8,128)(2,1)}, u32[]{:S(2)}) copy-start(bf16[1280,384]{0,1:T(8,128)(2,1)} %reduce-scatter.3.cloned.1.call-done) | copy-start | bytes 2949124
  215.6 160.4 %reduce-scatter.5.cloned.1.call-start = ((), (), s32[]{:S(2)}) async-start(), calls=%async_computation.8 | async-start | bytes 13516800 | tf_op jit(solution)/shard_map/reduce_scatter | solution.py:89
Sparse Core Ops, SparseCore 0:
  70.5 43.2 reduce-scatter.2
  215.8 43.5 all-gather.1
  271.3 104.7 reduce-scatter.4
where the time goes:
time: 386 us; the launch traced here: 385 us
  waiting for transfers between devices  181 us (47%)
  blocking collectives  101 us (26%)
  matrix products  42.5 us (11%)
  local copies, waits for them, and re-layouts  17.4 us (5%)
  starting transfers between devices  14.9 us (4%)
  other arithmetic  14 us (4%)
  between operations  14 us (4%)
    reduce_scatter x1, waiting for transfers between devices, per_device(): lax.psum_scatter(lax.dot_general(grad_full, context_rows, (((1,), (0,)),...  93.4 us
    psum x1, blocking collectives, per_device(): group_total = lax.psum(jnp.sum(member * rewards[:, None], axis=0), 'dp')  62.2 us
    all_gather x1, waiting for transfers between devices, row_grads(): grad_full = lax.all_gather(grad_t, 'mp', axis=0, tiled=True)  43.7 us
    all_to_all x1, blocking collectives, per_device(): lax.all_to_all(packed_context, 'dp', split_axis=0, concat_axis=0, tiled=T...  28.6 us
    all_to_all x1, waiting for transfers between devices, per_device(): lax.all_to_all(packed_residual, 'dp', split_axis=0, concat_axis=0, tiled=...  19.5 us
    dot_general x1, matrix products, row_grads(): lax.dot_general(out_proj, context, (((1,), (1,)), ((), ())), preferred_el...  19.2 us
    all_to_all x1, waiting for transfers between devices, per_device(): lax.all_to_all(packed_cotangent, 'dp', split_axis=0, concat_axis=0, tiled...  18.6 us
    dot_general x1, matrix products, per_device(): lax.dot_general(grad_full, context_rows, (((1,), (0,)), ((), ())), prefer...  11.7 us
  transfers between devices with their start and end apart: 6, of which 5 were waited for; matrix products, arithmetic and copies ran while one was open for 4% of the time, Pallas kernels for 0%

commit v1 on v0

v1 whole, which is shorter than its diff:
```python
import jax
import jax.numpy as jnp
from jax import lax
from jax.sharding import Mesh
from jax.sharding import PartitionSpec as P

LMAX = 64
GROUP = 16
PAIR = 3
EPSILON = 1e-06
NX, NY, NC, NZ = 4, 4, 2, 4
DP = ("x", "y", "c")
HALF = 80
F32 = jnp.float32
BF16 = jnp.bfloat16


def shift(value, axis, step):
    size = lax.axis_size(axis)
    return lax.ppermute(value, axis, [(i, (i + step) % size) for i in range(size)])


def pick(values, index):
    return lax.dynamic_index_in_dim(values, index, 0, keepdims=False)


def group_sum(value):
    for axis, steps in (("c", (1,)), ("x", (1, 2)), ("y", (1, 2))):
        for step in steps:
            value = value + shift(value, axis, step)
    return value


def slot_matrix(owner_dest, slots, rows):
    count = owner_dest.shape[0]
    per_block = rows // count
    same = owner_dest[:, None] == owner_dest[None, :]
    earlier = jnp.arange(count)[None, :] < jnp.arange(count)[:, None]
    rank = jnp.sum((same & earlier).astype(jnp.int32), axis=1)
    target = owner_dest * PAIR + rank
    row_target = jnp.repeat(target * per_block, per_block) + jnp.tile(jnp.arange(per_block), count)
    return (jnp.arange(slots * per_block)[:, None] == row_target[None, :]).astype(BF16)


def exchange(packed, lanes):
    blocks = packed.reshape((lanes, packed.shape[0] // lanes, packed.shape[1]))
    return lax.all_to_all(blocks, DP, split_axis=0, concat_axis=0, tiled=True).reshape(packed.shape)


def per_device(
    context, residual, cotangent, out_proj, norm_gain, rewards, group_ids, lengths, destinations
):
    lanes = NX * NY * NC
    rows, width = residual.shape
    full = width * NZ
    x, y, c, z = (lax.axis_index(axis) for axis in ("x", "y", "c", "z"))

    groups = rewards.shape[0] * lanes // GROUP
    member = (group_ids[:, None] == jnp.arange(groups)[None, :]).astype(F32)
    group_total = group_sum(jnp.sum(member * rewards[:, None], axis=0))
    advantage = rewards - jnp.sum(member * group_total[None, :], axis=1) / GROUP
    scale = advantage * LMAX / (2.0 * lengths.astype(F32))
    live = jnp.arange(LMAX)[None, :] < lengths[:, None]
    row_weights = jnp.where(live, scale[:, None], F32(0.0)).reshape(-1).astype(BF16)

    proj = out_proj.reshape(NZ, width, width)

    def part(step):
        return lax.dot_general(
            pick(proj, (z + step) % NZ), context, (((1,), (1,)), ((), ())), preferred_element_type=F32
        )

    top = width // 2
    far = part(2).astype(BF16)
    far_left = shift(far[:top], "z", 1)
    far_right = shift(far[top:], "z", 3)
    near, back, own = part(1), part(3), part(0)
    near = jnp.concatenate([near[:top] + far_left.astype(F32), near[top:]], axis=0).astype(BF16)
    back = jnp.concatenate([back[:top], back[top:] + far_right.astype(F32)], axis=0).astype(BF16)
    attn_t = own + shift(near, "z", 1).astype(F32) + shift(back, "z", 3).astype(F32)

    context_x = jnp.concatenate([context] + [shift(context, "x", k) for k in (1, 2, 3)], axis=0)
    context_y = jnp.concatenate([context] + [shift(context, "y", k) for k in (1, 2, 3)], axis=0)

    hidden_t = residual.T.astype(F32) + attn_t
    upstream_t = norm_gain[:, None] * (row_weights.astype(F32)[None, :] * cotangent.T.astype(F32))
    stats = jnp.stack(
        [jnp.sum(hidden_t * hidden_t, axis=0), jnp.sum(upstream_t * hidden_t, axis=0)]
    )
    stats = stats + shift(stats, "z", 1) + shift(stats, "z", 2) + shift(stats, "z", 3)
    inv_rms = lax.rsqrt(stats[0] / full + EPSILON)
    grad_t = (
        inv_rms[None, :] * upstream_t - hidden_t * (inv_rms**3 * stats[1] / full)[None, :]
    ).astype(BF16)

    from_left, from_right = shift(grad_t, "z", 1), shift(grad_t, "z", 3)
    far_grad = jnp.concatenate(
        [shift(from_left[:top], "z", 1), shift(from_right[top:], "z", 3)], axis=0
    )
    chunks = [grad_t, from_right, far_grad, from_left]

    slots = slot_matrix(destinations[:, 0], lanes * PAIR, rows)
    d_residual = exchange(
        lax.dot_general(slots, grad_t, (((1,), (1,)), ((), ())), preferred_element_type=F32).astype(BF16),
        lanes,
    )

    grad_full = jnp.stack(chunks).reshape(NZ, NY, NC, 2, HALF, rows)
    along_x = [
        shift(pick(grad_full[:, :, :, 0], (x + k - z) % NZ).reshape(-1, rows), "x", k) if k
        else pick(grad_full[:, :, :, 0], (x - z) % NZ).reshape(-1, rows)
        for k in range(NX)
    ]
    halves_y = jnp.moveaxis(grad_full[:, :, :, 1], 1, 0)
    along_y = [
        shift(pick(halves_y, (y + k) % NY).reshape(-1, rows), "y", k) if k
        else pick(halves_y, y).reshape(-1, rows)
        for k in range(NY)
    ]
    part_x = jnp.dot(jnp.concatenate(along_x, axis=1), context_x, preferred_element_type=F32)
    part_y = jnp.dot(jnp.concatenate(along_y, axis=1), context_y, preferred_element_type=F32)

    def core_sum(value):
        value = jnp.moveaxis(value.reshape(4, NC, HALF, width), 1, 0)
        other = shift(pick(value, 1 - c).astype(BF16), "c", 1)
        return pick(value, c) + other.astype(F32)

    part_x, part_y = core_sum(part_x), core_sum(part_y)
    total_x, total_y = pick(part_x, y), pick(part_y, (x - z) % NZ)
    for k in (1, 2, 3):
        total_x = total_x + shift(pick(part_x, (y + k) % NY).astype(BF16), "y", k).astype(F32)
        total_y = total_y + shift(pick(part_y, (x + k - z) % NZ).astype(BF16), "x", k).astype(F32)
    d_out_proj = jnp.concatenate([total_x, total_y], axis=0) / lanes

    context_grad = sum(
        lax.dot_general(
            chunk, pick(proj, (z + j) % NZ), (((0,), (0,)), ((), ())), preferred_element_type=F32
        )
        for j, chunk in enumerate(chunks)
    ).astype(BF16)
    d_context = exchange(jnp.dot(slots, context_grad, preferred_element_type=F32).astype(BF16), lanes)
    return (d_context, d_residual, d_out_proj)


def solution(mesh):
    wide = Mesh(mesh.devices.reshape(NX, NY, NC, NZ), DP + ("z",))
    placed = (
        P(DP, "z"),
        P(DP, "z"),
        P(DP, "z"),
        P(None, "z"),
        P("z"),
        P(DP),
        P(DP),
        P(DP),
        P(DP, None),
    )
    return jax.shard_map(
        per_device,
        mesh=wide,
        in_specs=placed,
        out_specs=(P(DP, "z"), P(DP, "z"), P(DP, "z")),
        check_vma=False,
    )
```

time: 386 us -> 202 us (0.52)
  waiting for transfers between devices: 181 us -> 63 us
  blocking collectives: 101 us -> 0 us
  starting transfers between devices: 14.9 us -> 65.5 us
  between operations: 14 us -> 1.17 us
    reduce_scatter x2 -> x0, waiting for transfers between devices: 93.4 us -> none  [the longest x1 93.4 us: per_device(): lax.psum_scatter(lax.dot_general(grad_full, context_rows, (((1,), (0,)),...]
    psum x2 -> x0, blocking collectives: 72.1 us -> none  [the longest x1 62.2 us: per_device(): group_total = lax.psum(jnp.sum(member * rewards[:, None], axis=0), 'dp')]
    ppermute x0 -> x36, waiting for transfers between devices: none -> 56.7 us  [shift(): lax.ppermute(value, axis, [(i, (i + step) % size) for i in range(size)])]
    ppermute x0 -> x36, starting transfers between devices: none -> 44.6 us  [shift(): lax.ppermute(value, axis, [(i, (i + step) % size) for i in range(size)])]
    all_gather x1 -> x0, waiting for transfers between devices: 43.7 us -> none  [row_grads(): grad_full = lax.all_gather(grad_t, 'mp', axis=0, tiled=True)]
    all_to_all x3 -> x2, waiting for transfers between devices: 43.8 us -> 6.24 us  [exchange(): lax.all_to_all(blocks, DP, split_axis=0, concat_axis=0, tiled=True)]
    all_to_all x1 -> x0, blocking collectives: 28.6 us -> none  [per_device(): lax.all_to_all(packed_context, 'dp', split_axis=0, concat_axis=0, tiled=T...]
    gather x6 -> x0, local copies, waits for them, and re-layouts: 6.11 us -> none  [arrange(): taken = jnp.take(blocks, source, axis=0)]
  transfers between devices with their start and end apart: 6 -> 38, of which waited for: 5 -> 18; matrix products, arithmetic and copies ran while one was open for 4% -> 34% of each run, Pallas kernels for 0% -> 0%
where the time goes in v1:
time: 202 us; the launch traced here: 201 us
  starting transfers between devices  65.5 us (32%)
  waiting for transfers between devices  63 us (31%)
  matrix products  42.7 us (21%)
  local copies, waits for them, and re-layouts  17.9 us (9%)
  other arithmetic  10.9 us (5%)
    ppermute x36, waiting for transfers between devices, shift(): lax.ppermute(value, axis, [(i, (i + step) % size) for i in range(size)])  56.7 us
    ppermute x36, starting transfers between devices, shift(): lax.ppermute(value, axis, [(i, (i + step) % size) for i in range(size)])  44.6 us
    all_to_all x2, starting transfers between devices, exchange(): lax.all_to_all(blocks, DP, split_axis=0, concat_axis=0, tiled=True)  20.9 us
    dot_general x4, matrix products, part(): lax.dot_general(pick(proj, (z + step) % NZ), context, (((1,), (1,)), ((),...  14.8 us
    dot_general x3, matrix products, per_device(): lax.dot_general(chunk, pick(proj, (z + j) % NZ), (((0,), (0,)), ((), ()))...  12.2 us
    all_to_all x2, waiting for transfers between devices, exchange(): lax.all_to_all(blocks, DP, split_axis=0, concat_axis=0, tiled=True)  6.24 us
    dot_general x1, matrix products, per_device(): jnp.dot(slots, context_grad, preferred_element_type=F32).astype(BF16)  5.64 us
    dot_general x1, matrix products, per_device(): jnp.dot(jnp.concatenate(along_y, axis=1), context_y, preferred_element_ty...  5.6 us
  transfers between devices with their start and end apart: 38, of which 18 were waited for; matrix products, arithmetic and copies ran while one was open for 34% of the time, Pallas kernels for 0%

profile of v1, /device:TPU:1, one launch (start us, length us, event | category | flops | bytes accessed | tf_op | source)
XLA Modules:
  0.0 201.2 jit_solution(7572447819643429150)
XLA Ops:
  0.6 3.6 %collective-permute-start.31 = (bf16[256,1280]{1,0:T(8,128)(2,1)}, bf16[256,1280]{1,0:T(8,128)(2,1)}, u32[]{:S(2)}, u32[]{:S(2)}) collective-permute-start(bf16[256,1280]{1,0:T(8,128)(2,1)} %param.9), channel_id=1, source_target_pairs={{0,24},{8,0},{16,8},{24,16},{1,25},{9,1},{17,9},{25,17},{2,26},{10... | collective-permute-start | bytes 1966088 | tf_op jit(solution)/shard_map/ppermute | solution.py:20
  5.4 1.3 collective-permute-start.4
  6.7 3.1 %fusion.50 = bf16[1280,256]{1,0:T(8,128)(2,1)S(1)} fusion(bf16[256,1280]{1,0:T(8,128)(2,1)} %param.9, bf16[4,1280,1280]{2,1,0:T(8,128)(2,1)} %bitcast.122, s32[]{:T(128)S(6)} %select_n.144), kind=kOutput, calls=%fused_computation.45 | convolution fusion | flops 839188480 | bytes 4587524 | tf_op jit(solution)/shard_map/dot_general | solution.py:69
  10.6 3.8 %collective-permute-start.2 = (bf16[640,256]{1,0:T(8,128)(2,1)S(1)}, bf16[640,256]{1,0:T(8,128)(2,1)}, u32[]{:S(2)}, u32[]{:S(2)}) collective-permute-start(bf16[640,256]{1,0:T(8,128)(2,1)S(1)} %get-tuple-element.25), channel_id=1, source_target_pairs={{0,3},{1,0},{2,1},{3,2},{4,7},{5,4},{6,5},{7,6},{8,11},{9,8},{10,9... | collective-permute-start | bytes 983048 | tf_op jit(solution)/shard_map/ppermute | solution.py:20
  14.3 4.2 %fusion.2 = f32[1280,256]{1,0:T(8,128)} fusion(bf16[256,1280]{1,0:T(8,128)(2,1)} %param.9, bf16[4,1280,1280]{2,1,0:T(8,128)(2,1)} %bitcast.123, s32[]{:T(128)S(6)} %select_n.146), kind=kOutput, calls=%fused_computation.4 | convolution fusion | flops 838860800 | bytes 5242884 | tf_op jit(solution)/shard_map/dot_general | solution.py:69
  18.6 3.2 %fusion.10 = f32[1280,256]{1,0:T(8,128)S(1)} fusion(bf16[256,1280]{1,0:T(8,128)(2,1)} %param.9, bf16[4,1280,1280]{2,1,0:T(8,128)(2,1)} %bitcast.124, s32[]{:T(128)S(6)} %select_n.142), kind=kOutput, calls=%fused_computation.12 | convolution fusion | flops 838860800 | bytes 5242884 | tf_op jit(solution)/shard_map/dot_general | solution.py:69
  23.4 1.3 copy.20
  24.7 4.3 %fusion.14 = f32[1280,256]{1,0:T(8,128)} fusion(bf16[256,1280]{1,0:T(8,128)(2,1)} %param.9, bf16[4,1280,1280]{2,1,0:T(8,128)(2,1)} %bitcast.125, s32[]{:T(128)S(6)} %select_n.140), kind=kOutput, calls=%fused_computation.16 | convolution fusion | flops 838860800 | bytes 5242884 | tf_op jit(solution)/shard_map/dot_general | solution.py:69
  30.3 2.7 %collective-permute-start.3 = (bf16[1280,256]{1,0:T(8,128)(2,1)S(1)}, bf16[1280,256]{1,0:T(8,128)(2,1)}, u32[]{:S(2)}, u32[]{:S(2)}) collective-permute-start(bf16[1280,256]{1,0:T(8,128)(2,1)S(1)} %pad_maximum_fusion.4), channel_id=1, source_target_pairs={{0,3},{1,0},{2,1},{3,2},{4,7},{5,4},{6,5},{7,6},{8,11},{9,8},{10,9... | collective-permute-start | bytes 1966088 | tf_op jit(solution)/shard_map/ppermute | solution.py:20
  35.7 2.4 %collective-permute-done.5 = f32[8]{0:T(128)S(1)} collective-permute-done((f32[8]{0:T(128)S(1)}, f32[8]{0:T(128)S(1)}, u32[]{:S(2)}, u32[]{:S(2)}) %collective-permute-start.5) | collective-permute-done | bytes 64 | tf_op jit(solution)/shard_map/ppermute | solution.py:20
  38.1 1.9 collective-permute-start.6
  40.1 2.0 collective-permute-done.6
  42.7 3.3 %collective-permute-done.7 = f32[8]{0:T(128)S(1)} collective-permute-done((f32[8]{0:T(128)S(1)}, f32[8]{0:T(128)S(1)}, u32[]{:S(2)}, u32[]{:S(2)}) %collective-permute-start.7) | collective-permute-done | bytes 64 | tf_op jit(solution)/shard_map/ppermute | solution.py:20
  46.0 1.4 collective-permute-start.8
  47.5 2.5 %collective-permute-done.8 = f32[8]{0:T(128)S(1)} collective-permute-done((f32[8]{0:T(128)S(1)}, f32[8]{0:T(128)S(1)}, u32[]{:S(2)}, u32[]{:S(2)}) %collective-permute-start.8) | collective-permute-done | bytes 64 | tf_op jit(solution)/shard_map/ppermute | solution.py:20
  50.9 2.3 %multiply_reduce_fusion = (f32[256]{0:T(256)S(1)}, f32[256]{0:T(256)S(1)}, f32[1280,256]{1,0:T(8,128)S(1)}) fusion(bf16[256,1280]{0,1:T(8,128)(2,1)S(1)} %copy.21, f32[256]{0:T(256)S(1)} %reshape.167, f32[1280]{0:T(1024)S(1)} %copy-done.9, bf16[1280,256]{1,0:T(8,128)(2,1)} %collective-permute-done.3, f32[1280,256]{1,0:T(8,128)} %fusion.14, ...), kind=kLoop, calls=%fused_computation.71 | loop fusion | flops 4259328 | bytes 5251072 | tf_op jit(solution)/shard_map/reduce_sum | solution.py:88
  53.2 2.5 %collective-permute-start.11 = (f32[2,256]{1,0:T(2,128)S(1)}, f32[2,256]{1,0:T(2,128)S(1)}, u32[]{:S(2)}, u32[]{:S(2)}) collective-permute-start(f32[2,256]{1,0:T(2,128)S(1)} %pad_maximum_fusion.5), channel_id=1, source_target_pairs={{0,3},{1,0},{2,1},{3,2},{4,7},{5,4},{6,5},{7,6},{8,11},{9,8},{10,9... | collective-permute-start | bytes 6152 | tf_op jit(solution)/shard_map/ppermute | solution.py:20
  56.5 3.2 %collective-permute-done.10 = f32[2,256]{1,0:T(2,128)S(1)} collective-permute-done((f32[2,256]{1,0:T(2,128)S(1)}, f32[2,256]{1,0:T(2,128)S(1)}, u32[]{:S(2)}, u32[]{:S(2)}) %collective-permute-start.10) | collective-permute-done | bytes 2080 | tf_op jit(solution)/shard_map/ppermute | solution.py:20
  60.1 2.7 %collective-permute-start.12 = (bf16[1280,256]{1,0:T(8,128)(2,1)S(1)}, bf16[1280,256]{1,0:T(8,128)(2,1)S(1)}, u32[]{:S(2)}, u32[]{:S(2)}) collective-permute-start(bf16[1280,256]{1,0:T(8,128)(2,1)S(1)} %fusion.69), channel_id=1, source_target_pairs={{0,3},{1,0},{2,1},{3,2},{4,7},{5,4},{6,5},{7,6},{8,11},{9,8},{10,9... | collective-permute-start | bytes 1966088 | tf_op jit(solution)/shard_map/ppermute | solution.py:20
  63.0 4.1 %fusion.12 = f32[256,1280]{1,0:T(8,128)} fusion(bf16[1280,256]{1,0:T(8,128)(2,1)S(1)} %fusion.69, bf16[4,1280,1280]{2,1,0:T(8,128)(2,1)} %bitcast.126, s32[]{:T(128)S(6)} %select_n.140), kind=kOutput, calls=%fused_computation.14 | convolution fusion | flops 838860800 | bytes 5242884 | tf_op jit(solution)/shard_map/dot_general | solution.py:136
  67.1 4.1 %collective-permute-done.13 = bf16[1280,256]{1,0:T(8,128)(2,1)S(1)} collective-permute-done((bf16[1280,256]{1,0:T(8,128)(2,1)S(1)}, bf16[1280,256]{1,0:T(8,128)(2,1)S(1)}, u32[]{:S(2)}, u32[]{:S(2)}) %collective-permute-start.13) | collective-permute-done | bytes 655392 | tf_op jit(solution)/shard_map/ppermute | solution.py:20
  73.6 13.7 %all-to-all-start.1 = ((bf16[32,12,1280]{2,1,0:T(8,128)(2,1)}), bf16[32,12,1280]{2,1,0:T(8,128)(2,1)S(1)}, u32[]{:S(2)}, u32[]{:S(2)}) async-start(bf16[32,12,1280]{2,1,0:T(8,128)(2,1)} %reshape.155), calls=%async_computation.1 | async-start | bytes 2621440 | tf_op jit(solution)/shard_map/all_to_all | solution.py:47
  87.4 3.0 %collective-permute-start.15 = (bf16[640,256]{1,0:T(8,128)(2,1)S(1)}, bf16[640,256]{1,0:T(8,128)(2,1)S(1)}, u32[]{:S(2)}, u32[]{:S(2)}) collective-permute-start(bf16[640,256]{1,0:T(8,128)(2,1)S(1)} %slice.62), channel_id=1, source_target_pairs={{0,3},{1,0},{2,1},{3,2},{4,7},{5,4},{6,5},{7,6},{8,11},{9,8},{10,9... | collective-permute-start | bytes 983048 | tf_op jit(solution)/shard_map/ppermute | solution.py:20
  90.4 4.1 %fusion = f32[256,1280]{1,0:T(8,128)} fusion(bf16[1280,256]{1,0:T(8,128)(2,1)S(1)} %collective-permute-done.13, bf16[4,1280,1280]{2,1,0:T(8,128)(2,1)} %bitcast.127, s32[]{:T(128)S(6)} %select_n.146), kind=kOutput, calls=%fused_computation.2 | convolution fusion | flops 838860800 | bytes 5242884 | tf_op jit(solution)/shard_map/dot_general | solution.py:136
  94.5 2.6 %collective-permute-start.21 = (bf16[256,1280]{1,0:T(8,128)(2,1)}, bf16[256,1280]{1,0:T(8,128)(2,1)}, u32[]{:S(2)}, u32[]{:S(2)}) collective-permute-start(bf16[256,1280]{1,0:T(8,128)(2,1)} %param.9), channel_id=1, source_target_pairs={{0,96},{32,0},{64,32},{96,64},{1,97},{33,1},{65,33},{97,65},{2,98}... | collective-permute-start | bytes 1966088 | tf_op jit(solution)/shard_map/ppermute | solution.py:20
  98.2 4.0 %fusion.4 = f32[256,1280]{1,0:T(8,128)} fusion(bf16[1280,256]{1,0:T(8,128)(2,1)S(1)} %constant_dynamic-update-slice_fusion, bf16[4,1280,1280]{2,1,0:T(8,128)(2,1)} %bitcast.128, s32[]{:T(128)S(6)} %select_n.144), kind=kOutput, calls=%fused_computation.6 | convolution fusion | flops 838860800 | bytes 5242884 | tf_op jit(solution)/shard_map/dot_general | solution.py:136
  103.9 2.4 %collective-permute-start.28 = (bf16[640,256]{1,0:T(8,128)(2,1)}, bf16[640,256]{1,0:T(8,128)(2,1)}, u32[]{:S(2)}, u32[]{:S(2)}) collective-permute-start(bf16[640,256]{1,0:T(8,128)(2,1)} %bitcast.30), channel_id=1, source_target_pairs={{0,24},{8,0},{16,8},{24,16},{1,25},{9,1},{17,9},{25,17},{2,26},{10... | collective-permute-start | bytes 983048 | tf_op jit(solution)/shard_map/ppermute | solution.py:20
  107.4 5.6 %convolution_convert_fusion.1 = bf16[384,1280]{1,0:T(8,128)(2,1)} fusion(f32[256,1280]{1,0:T(8,128)} %fusion, f32[256,1280]{1,0:T(8,128)} %fusion.4, f32[256,1280]{1,0:T(8,128)} %fusion.12, bf16[1280,256]{1,0:T(8,128)(2,1)S(1)} %copy-done.1, bf16[4,1280,1280]{2,1,0:T(8,128)(2,1)} %bitcast.129, s32[]{:T(128)S(6)} %select_n.142, s32[256]{0:T(256)S(1)} %add.237), kind=kOutput, calls=%fused_computation.27 | convolution fusion | flops 1092419584 | bytes 8848388 | tf_op jit(solution)/shard_map/dot_general | solution.py:141
  113.1 2.3 %reshape.153 = bf16[32,12,1280]{2,1,0:T(8,128)(2,1)} reshape(bf16[384,1280]{1,0:T(8,128)(2,1)} %convolution_convert_fusion.1) | data formatting | bytes 1966080 | tf_op jit(solution)/shard_map/reshape | solution.py:46
  116.5 1.8 collective-permute-start.20
  118.9 2.0 %collective-permute-start.18 = (bf16[640,256]{1,0:T(8,128)(2,1)}, bf16[640,256]{1,0:T(8,128)(2,1)}, u32[]{:S(2)}, u32[]{:S(2)}) collective-permute-start(bf16[640,256]{1,0:T(8,128)(2,1)} %bitcast.19), channel_id=1, source_target_pairs={{0,96},{32,0},{64,32},{96,64},{1,97},{33,1},{65,33},{97,65},{2,98}... | collective-permute-start | bytes 983048 | tf_op jit(solution)/shard_map/ppermute | solution.py:20
  121.7 3.1 %collective-permute-done.26 = bf16[640,256]{1,0:T(8,128)(2,1)} collective-permute-done((bf16[640,256]{1,0:T(8,128)(2,1)}, bf16[640,256]{1,0:T(8,128)(2,1)}, u32[]{:S(2)}, u32[]{:S(2)}) %collective-permute-start.26) | collective-permute-done | bytes 327712 | tf_op jit(solution)/shard_map/ppermute | solution.py:20
  125.1 5.6 %fusion.39 = f32[640,1280]{1,0:T(8,128)} fusion(bf16[256,1280]{1,0:T(8,128)(2,1)} %param.9, bf16[256,1280]{1,0:T(8,128)(2,1)} %collective-permute-done.31, bf16[256,1280]{1,0:T(8,128)(2,1)} %collective-permute-done.30, bf16[256,1280]{1,0:T(8,128)(2,1)} %collective-permute-done.29, bf16[640,256]{1,0:T(8,128)(2,1)} %collective-permute-done.28, ...), kind=kOutput, calls=%fused_computation.36 | convolution fusion | flops 1693450240 | bytes 7208960 | tf_op jit(solution)/shard_map/dot_general | solution.py:121
  130.7 7.2 %all-to-all-start = ((bf16[32,12,1280]{2,1,0:T(8,128)(2,1)}), bf16[32,12,1280]{2,1,0:T(8,128)(2,1)S(1)}, u32[]{:S(2)}, u32[]{:S(2)}) async-start(bf16[32,12,1280]{2,1,0:T(8,128)(2,1)} %reshape.153), calls=%async_computation | async-start | bytes 2621440 | tf_op jit(solution)/shard_map/all_to_all | solution.py:47
  137.9 1.5 fusion.73
  140.0 11.1 %collective-permute-done.19 = bf16[256,1280]{1,0:T(8,128)(2,1)} collective-permute-done((bf16[256,1280]{1,0:T(8,128)(2,1)}, bf16[256,1280]{1,0:T(8,128)(2,1)}, u32[]{:S(2)}, u32[]{:S(2)}) %collective-permute-start.19) | collective-permute-done | bytes 655392 | tf_op jit(solution)/shard_map/ppermute | solution.py:20
  151.1 2.8 %collective-permute-done.17 = bf16[640,256]{1,0:T(8,128)(2,1)} collective-permute-done((bf16[640,256]{1,0:T(8,128)(2,1)}, bf16[640,256]{1,0:T(8,128)(2,1)}, u32[]{:S(2)}, u32[]{:S(2)}) %collective-permute-start.17) | collective-permute-done | bytes 327712 | tf_op jit(solution)/shard_map/ppermute | solution.py:20
  153.9 9.6 %collective-permute-done.16 = bf16[640,256]{1,0:T(8,128)(2,1)} collective-permute-done((bf16[640,256]{1,0:T(8,128)(2,1)}, bf16[640,256]{1,0:T(8,128)(2,1)}, u32[]{:S(2)}, u32[]{:S(2)}) %collective-permute-start.16) | collective-permute-done | bytes 327712 | tf_op jit(solution)/shard_map/ppermute | solution.py:20
  163.5 3.9 %fusion.35 = f32[640,1280]{1,0:T(8,128)S(1)} fusion(bf16[256,1280]{1,0:T(8,128)(2,1)} %param.9, bf16[256,1280]{1,0:T(8,128)(2,1)} %collective-permute-done.21, bf16[256,1280]{1,0:T(8,128)(2,1)} %collective-permute-done.20, bf16[256,1280]{1,0:T(8,128)(2,1)} %collective-permute-done.19, bf16[640,256]{1,0:T(8,128)(2,1)} %collective-permute-done.18, ...), kind=kOutput, calls=%fused_computation.33 | convolution fusion | flops 1693450240 | bytes 7208960 | tf_op jit(solution)/shard_map/dot_general | solution.py:120
  167.4 1.7 copy-done.2
  171.9 6.2 %all-to-all-done = bf16[32,12,1280]{2,1,0:T(8,128)(2,1)S(1)} async-done(((bf16[32,12,1280]{2,1,0:T(8,128)(2,1)}), bf16[32,12,1280]{2,1,0:T(8,128)(2,1)S(1)}, u32[]{:S(2)}, u32[]{:S(2)}) %all-to-all-start) | async-done | bytes 983072 | tf_op jit(solution)/shard_map/all_to_all | solution.py:47
  179.2 2.0 bitcast_add_fusion
  181.7 1.9 collective-permute-start.34
  184.1 1.3 bitcast_add_fusion.1
  185.5 2.0 collective-permute-start.25
  188.1 1.7 collective-permute-done.34
  189.8 4.8 %collective-permute-done.33 = bf16[80,1280]{1,0:T(8,128)(2,1)S(1)} collective-permute-done((bf16[80,1280]{1,0:T(8,128)(2,1)S(1)}, bf16[80,1280]{1,0:T(8,128)(2,1)S(1)}, u32[]{:S(2)}, u32[]{:S(2)}) %collective-permute-start.33) | collective-permute-done | bytes 204832 | tf_op jit(solution)/shard_map/ppermute | solution.py:20
  194.9 5.2 %collective-permute-done.23 = bf16[80,1280]{1,0:T(8,128)(2,1)S(1)} collective-permute-done((bf16[80,1280]{1,0:T(8,128)(2,1)S(1)}, bf16[80,1280]{1,0:T(8,128)(2,1)S(1)}, u32[]{:S(2)}, u32[]{:S(2)}) %collective-permute-start.23) | collective-permute-done | bytes 204832 | tf_op jit(solution)/shard_map/ppermute | solution.py:20
  (116 shorter events, 26.7 us)
Async XLA Ops:
  0.6 105.7 %collective-permute-start.31 = (bf16[256,1280]{1,0:T(8,128)(2,1)}, bf16[256,1280]{1,0:T(8,128)(2,1)}, u32[]{:S(2)}, u32[]{:S(2)}) collective-permute-start(bf16[256,1280]{1,0:T(8,128)(2,1)} %param.9), channel_id=1, source_target_pairs={{0,24},{8,0},{16,8},{24,16},{1,25},{9,1},{17,9},{25,17},{2,26},{10... | collective-permute-start | bytes 1966088 | tf_op jit(solution)/shard_map/ppermute | solution.py:20
  4.3 102.6 %collective-permute-start.30 = (bf16[256,1280]{1,0:T(8,128)(2,1)}, bf16[256,1280]{1,0:T(8,128)(2,1)}, u32[]{:S(2)}, u32[]{:S(2)}) collective-permute-start(bf16[256,1280]{1,0:T(8,128)(2,1)} %param.9), channel_id=1, source_target_pairs={{0,16},{8,24},{16,0},{24,8},{1,17},{9,25},{17,1},{25,9},{2,18},{10... | collective-permute-start | bytes 1966088 | tf_op jit(solution)/shard_map/ppermute | solution.py:20
  5.4 29.1 %collective-permute-start.4 = (f32[8]{0:T(128)S(1)}, f32[8]{0:T(128)S(1)}, u32[]{:S(2)}, u32[]{:S(2)}) collective-permute-start(f32[8]{0:T(128)S(1)} %select_reduce_fusion.1), channel_id=1, source_target_pairs={{0,4},{4,0},{1,5},{5,1},{2,6},{6,2},{3,7},{7,3},{8,12},{12,8},{9,1... | collective-permute-start | bytes 104 | tf_op jit(solution)/shard_map/ppermute | solution.py:20
  10.6 18.5 %collective-permute-start.2 = (bf16[640,256]{1,0:T(8,128)(2,1)S(1)}, bf16[640,256]{1,0:T(8,128)(2,1)}, u32[]{:S(2)}, u32[]{:S(2)}) collective-permute-start(bf16[640,256]{1,0:T(8,128)(2,1)S(1)} %get-tuple-element.25), channel_id=1, source_target_pairs={{0,3},{1,0},{2,1},{3,2},{4,7},{5,4},{6,5},{7,6},{8,11},{9,8},{10,9... | collective-permute-start | bytes 983048 | tf_op jit(solution)/shard_map/ppermute | solution.py:20
  14.3 18.7 %collective-permute-start = (bf16[640,256]{1,0:T(8,128)(2,1)}, bf16[640,256]{1,0:T(8,128)(2,1)}, u32[]{:S(2)}, u32[]{:S(2)}) collective-permute-start(bf16[640,256]{1,0:T(8,128)(2,1)} %get-tuple-element.24), channel_id=1, source_target_pairs={{0,1},{1,2},{2,3},{3,0},{4,5},{5,6},{6,7},{7,4},{8,9},{9,10},{10,1... | collective-permute-start | bytes 983048 | tf_op jit(solution)/shard_map/ppermute | solution.py:20
  24.7 4.3 %copy-start.6 = (f32[1280,256]{1,0:T(8,128)S(1)}, f32[1280,256]{1,0:T(8,128)}, u32[]{:S(2)}) copy-start(f32[1280,256]{1,0:T(8,128)} %fusion.2) | copy-start | bytes 3932164
  30.2 4.0 %copy-start.13 = (s32[64,1]{0,1:T(1,128)S(1)}, s32[64,1]{0,1:T(1,128)}, u32[]{:S(2)}) copy-start(s32[64,1]{0,1:T(1,128)} %param.17) | copy-start | bytes 772
  30.2 19.7 %copy-start.12 = (s32[4]{0:T(128)S(1)}, s32[4]{0:T(128)}, u32[]{:S(2)}) copy-start(s32[4]{0:T(128)} %param.15) | copy-start | bytes 52
  30.2 19.9 %copy-start.10 = (s32[4]{0:T(128)S(1)}, s32[4]{0:T(128)}, u32[]{:S(2)}) copy-start(s32[4]{0:T(128)} %param.16) | copy-start | bytes 52
  30.3 19.9 %copy-start.11 = (f32[4]{0:T(128)S(1)}, f32[4]{0:T(128)}, u32[]{:S(2)}) copy-start(f32[4]{0:T(128)} %param.14) | copy-start | bytes 52
  30.3 20.7 %copy-start.9 = (f32[1280]{0:T(1024)S(1)}, f32[1280]{0:T(1024)}, u32[]{:S(2)}) copy-start(f32[1280]{0:T(1024)} %param.13) | copy-start | bytes 15364
  30.3 20.0 %collective-permute-start.3 = (bf16[1280,256]{1,0:T(8,128)(2,1)S(1)}, bf16[1280,256]{1,0:T(8,128)(2,1)}, u32[]{:S(2)}, u32[]{:S(2)}) collective-permute-start(bf16[1280,256]{1,0:T(8,128)(2,1)S(1)} %pad_maximum_fusion.4), channel_id=1, source_target_pairs={{0,3},{1,0},{2,1},{3,2},{4,7},{5,4},{6,5},{7,6},{8,11},{9,8},{10,9... | collective-permute-start | bytes 1966088 | tf_op jit(solution)/shard_map/ppermute | solution.py:20
  34.2 16.7 %collective-permute-start.1 = (bf16[1280,256]{1,0:T(8,128)(2,1)S(1)}, bf16[1280,256]{1,0:T(8,128)(2,1)}, u32[]{:S(2)}, u32[]{:S(2)}) collective-permute-start(bf16[1280,256]{1,0:T(8,128)(2,1)S(1)} %pad_maximum_fusion.3), channel_id=1, source_target_pairs={{0,1},{1,2},{2,3},{3,0},{4,5},{5,6},{6,7},{7,4},{8,9},{9,10},{10,1... | collective-permute-start | bytes 1966088 | tf_op jit(solution)/shard_map/ppermute | solution.py:20
  34.5 3.7 %collective-permute-start.5 = (f32[8]{0:T(128)S(1)}, f32[8]{0:T(128)S(1)}, u32[]{:S(2)}, u32[]{:S(2)}) collective-permute-start(f32[8]{0:T(128)S(1)} %add.254), channel_id=1, source_target_pairs={{0,32},{32,64},{64,96},{96,0},{1,33},{33,65},{65,97},{97,1},{2,34}... | collective-permute-start | bytes 104 | tf_op jit(solution)/shard_map/ppermute | solution.py:20
  38.1 3.9 %collective-permute-start.6 = (f32[8]{0:T(128)S(1)}, f32[8]{0:T(128)S(1)}, u32[]{:S(2)}, u32[]{:S(2)}) collective-permute-start(f32[8]{0:T(128)S(1)} %add.255), channel_id=1, source_target_pairs={{0,64},{32,96},{64,0},{96,32},{1,65},{33,97},{65,1},{97,33},{2,66}... | collective-permute-start | bytes 104 | tf_op jit(solution)/shard_map/ppermute | solution.py:20
  42.0 4.0 %collective-permute-start.7 = (f32[8]{0:T(128)S(1)}, f32[8]{0:T(128)S(1)}, u32[]{:S(2)}, u32[]{:S(2)}) collective-permute-start(f32[8]{0:T(128)S(1)} %add.256), channel_id=1, source_target_pairs={{0,8},{8,16},{16,24},{24,0},{1,9},{9,17},{17,25},{25,1},{2,10},{10... | collective-permute-start | bytes 104 | tf_op jit(solution)/shard_map/ppermute | solution.py:20
  46.0 3.9 %collective-permute-start.8 = (f32[8]{0:T(128)S(1)}, f32[8]{0:T(128)S(1)}, u32[]{:S(2)}, u32[]{:S(2)}) collective-permute-start(f32[8]{0:T(128)S(1)} %add.257), channel_id=1, source_target_pairs={{0,16},{8,24},{16,0},{24,8},{1,17},{9,25},{17,1},{25,9},{2,18},{10... | collective-permute-start | bytes 104 | tf_op jit(solution)/shard_map/ppermute | solution.py:20
  53.2 3.3 %collective-permute-start.11 = (f32[2,256]{1,0:T(2,128)S(1)}, f32[2,256]{1,0:T(2,128)S(1)}, u32[]{:S(2)}, u32[]{:S(2)}) collective-permute-start(f32[2,256]{1,0:T(2,128)S(1)} %pad_maximum_fusion.5), channel_id=1, source_target_pairs={{0,3},{1,0},{2,1},{3,2},{4,7},{5,4},{6,5},{7,6},{8,11},{9,8},{10,9... | collective-permute-start | bytes 6152 | tf_op jit(solution)/shard_map/ppermute | solution.py:20
  55.7 3.9 %collective-permute-start.10 = (f32[2,256]{1,0:T(2,128)S(1)}, f32[2,256]{1,0:T(2,128)S(1)}, u32[]{:S(2)}, u32[]{:S(2)}) collective-permute-start(f32[2,256]{1,0:T(2,128)S(1)} %pad_maximum_fusion.5), channel_id=1, source_target_pairs={{0,2},{1,3},{2,0},{3,1},{4,6},{5,7},{6,4},{7,5},{8,10},{9,11},{10,... | collective-permute-start | bytes 6152 | tf_op jit(solution)/shard_map/ppermute | solution.py:20
  55.7 3.9 %collective-permute-start.9 = (f32[2,256]{1,0:T(2,128)S(1)}, f32[2,256]{1,0:T(2,128)S(1)}, u32[]{:S(2)}, u32[]{:S(2)}) collective-permute-start(f32[2,256]{1,0:T(2,128)S(1)} %pad_maximum_fusion.5), channel_id=1, source_target_pairs={{0,1},{1,2},{2,3},{3,0},{4,5},{5,6},{6,7},{7,4},{8,9},{9,10},{10,1... | collective-permute-start | bytes 6152 | tf_op jit(solution)/shard_map/ppermute | solution.py:20
  56.5 60.0 %collective-permute-start.29 = (bf16[256,1280]{1,0:T(8,128)(2,1)}, bf16[256,1280]{1,0:T(8,128)(2,1)}, u32[]{:S(2)}, u32[]{:S(2)}) collective-permute-start(bf16[256,1280]{1,0:T(8,128)(2,1)} %param.9), channel_id=1, source_target_pairs={{0,8},{8,16},{16,24},{24,0},{1,9},{9,17},{17,25},{25,1},{2,10},{10... | collective-permute-start | bytes 1966088 | tf_op jit(solution)/shard_map/ppermute | solution.py:20
  60.0 11.2 %collective-permute-start.13 = (bf16[1280,256]{1,0:T(8,128)(2,1)S(1)}, bf16[1280,256]{1,0:T(8,128)(2,1)S(1)}, u32[]{:S(2)}, u32[]{:S(2)}) collective-permute-start(bf16[1280,256]{1,0:T(8,128)(2,1)S(1)} %fusion.69), channel_id=1, source_target_pairs={{0,1},{1,2},{2,3},{3,0},{4,5},{5,6},{6,7},{7,4},{8,9},{9,10},{10,1... | collective-permute-start | bytes 1966088 | tf_op jit(solution)/shard_map/ppermute | solution.py:20
  60.1 27.2 %collective-permute-start.12 = (bf16[1280,256]{1,0:T(8,128)(2,1)S(1)}, bf16[1280,256]{1,0:T(8,128)(2,1)S(1)}, u32[]{:S(2)}, u32[]{:S(2)}) collective-permute-start(bf16[1280,256]{1,0:T(8,128)(2,1)S(1)} %fusion.69), channel_id=1, source_target_pairs={{0,3},{1,0},{2,1},{3,2},{4,7},{5,4},{6,5},{7,6},{8,11},{9,8},{10,9... | collective-permute-start | bytes 1966088 | tf_op jit(solution)/shard_map/ppermute | solution.py:20
  72.0 22.5 %collective-permute-start.14 = (bf16[640,256]{1,0:T(8,128)(2,1)}, bf16[640,256]{1,0:T(8,128)(2,1)}, u32[]{:S(2)}, u32[]{:S(2)}) collective-permute-start(bf16[640,256]{1,0:T(8,128)(2,1)} %slice.61), channel_id=1, source_target_pairs={{0,1},{1,2},{2,3},{3,0},{4,5},{5,6},{6,7},{7,4},{8,9},{9,10},{10,1... | collective-permute-start | bytes 983048 | tf_op jit(solution)/shard_map/ppermute | solution.py:20
  73.6 57.1 %all-to-all-start.1 = ((bf16[32,12,1280]{2,1,0:T(8,128)(2,1)}), bf16[32,12,1280]{2,1,0:T(8,128)(2,1)S(1)}, u32[]{:S(2)}, u32[]{:S(2)}) async-start(bf16[32,12,1280]{2,1,0:T(8,128)(2,1)} %reshape.155), calls=%async_computation.1 | async-start | bytes 2621440 | tf_op jit(solution)/shard_map/all_to_all | solution.py:47
  87.3 14.9 %copy-start = (bf16[1280,256]{1,0:T(8,128)(2,1)}, bf16[1280,256]{1,0:T(8,128)(2,1)S(1)}, u32[]{:S(2)}) copy-start(bf16[1280,256]{1,0:T(8,128)(2,1)S(1)} %collective-permute-done.12) | copy-start | bytes 1966084
  87.4 10.8 %collective-permute-start.15 = (bf16[640,256]{1,0:T(8,128)(2,1)S(1)}, bf16[640,256]{1,0:T(8,128)(2,1)S(1)}, u32[]{:S(2)}, u32[]{:S(2)}) collective-permute-start(bf16[640,256]{1,0:T(8,128)(2,1)S(1)} %slice.62), channel_id=1, source_target_pairs={{0,3},{1,0},{2,1},{3,2},{4,7},{5,4},{6,5},{7,6},{8,11},{9,8},{10,9... | collective-permute-start | bytes 983048 | tf_op jit(solution)/shard_map/ppermute | solution.py:20
  94.5 23.8 %collective-permute-start.21 = (bf16[256,1280]{1,0:T(8,128)(2,1)}, bf16[256,1280]{1,0:T(8,128)(2,1)}, u32[]{:S(2)}, u32[]{:S(2)}) collective-permute-start(bf16[256,1280]{1,0:T(8,128)(2,1)} %param.9), channel_id=1, source_target_pairs={{0,96},{32,0},{64,32},{96,64},{1,97},{33,1},{65,33},{97,65},{2,98}... | collective-permute-start | bytes 1966088 | tf_op jit(solution)/shard_map/ppermute | solution.py:20
  102.7 4.7 %copy-start.1 = (bf16[1280,256]{1,0:T(8,128)(2,1)S(1)}, bf16[1280,256]{1,0:T(8,128)(2,1)}, u32[]{:S(2)}) copy-start(bf16[1280,256]{1,0:T(8,128)(2,1)} %copy-done) | copy-start | bytes 1966084
  103.9 15.1 %collective-permute-start.28 = (bf16[640,256]{1,0:T(8,128)(2,1)}, bf16[640,256]{1,0:T(8,128)(2,1)}, u32[]{:S(2)}, u32[]{:S(2)}) collective-permute-start(bf16[640,256]{1,0:T(8,128)(2,1)} %bitcast.30), channel_id=1, source_target_pairs={{0,24},{8,0},{16,8},{24,16},{1,25},{9,1},{17,9},{25,17},{2,26},{10... | collective-permute-start | bytes 983048 | tf_op jit(solution)/shard_map/ppermute | solution.py:20
  106.3 14.7 %collective-permute-start.27 = (bf16[640,256]{1,0:T(8,128)(2,1)}, bf16[640,256]{1,0:T(8,128)(2,1)}, u32[]{:S(2)}, u32[]{:S(2)}) collective-permute-start(bf16[640,256]{1,0:T(8,128)(2,1)} %bitcast.29), channel_id=1, source_target_pairs={{0,16},{8,24},{16,0},{24,8},{1,17},{9,25},{17,1},{25,9},{2,18},{10... | collective-permute-start | bytes 983048 | tf_op jit(solution)/shard_map/ppermute | solution.py:20
  106.8 17.9 %collective-permute-start.26 = (bf16[640,256]{1,0:T(8,128)(2,1)}, bf16[640,256]{1,0:T(8,128)(2,1)}, u32[]{:S(2)}, u32[]{:S(2)}) collective-permute-start(bf16[640,256]{1,0:T(8,128)(2,1)} %bitcast.28), channel_id=1, source_target_pairs={{0,8},{8,16},{16,24},{24,0},{1,9},{9,17},{17,25},{25,1},{2,10},{10... | collective-permute-start | bytes 983048 | tf_op jit(solution)/shard_map/ppermute | solution.py:20
  113.1 12.0 %copy-start.8 = (bf16[4,1,2,1,80,256]{5,4,3,2,1,0:T(8,128)(2,1)S(1)}, bf16[4,1,2,1,80,256]{5,4,3,2,1,0:T(8,128)(2,1)}, u32[]{:S(2)}) copy-start(bf16[4,1,2,1,80,256]{5,4,3,2,1,0:T(8,128)(2,1)} %get-tuple-element.20) | copy-start | bytes 983044
  116.5 23.0 %collective-permute-start.20 = (bf16[256,1280]{1,0:T(8,128)(2,1)}, bf16[256,1280]{1,0:T(8,128)(2,1)}, u32[]{:S(2)}, u32[]{:S(2)}) collective-permute-start(bf16[256,1280]{1,0:T(8,128)(2,1)} %param.9), channel_id=1, source_target_pairs={{0,64},{32,96},{64,0},{96,32},{1,65},{33,97},{65,1},{97,33},{2,66}... | collective-permute-start | bytes 1966088 | tf_op jit(solution)/shard_map/ppermute | solution.py:20
  118.3 32.8 %collective-permute-start.19 = (bf16[256,1280]{1,0:T(8,128)(2,1)}, bf16[256,1280]{1,0:T(8,128)(2,1)}, u32[]{:S(2)}, u32[]{:S(2)}) collective-permute-start(bf16[256,1280]{1,0:T(8,128)(2,1)} %param.9), channel_id=1, source_target_pairs={{0,32},{32,64},{64,96},{96,0},{1,33},{33,65},{65,97},{97,1},{2,34}... | collective-permute-start | bytes 1966088 | tf_op jit(solution)/shard_map/ppermute | solution.py:20
  118.9 32.2 %collective-permute-start.18 = (bf16[640,256]{1,0:T(8,128)(2,1)}, bf16[640,256]{1,0:T(8,128)(2,1)}, u32[]{:S(2)}, u32[]{:S(2)}) collective-permute-start(bf16[640,256]{1,0:T(8,128)(2,1)} %bitcast.19), channel_id=1, source_target_pairs={{0,96},{32,0},{64,32},{96,64},{1,97},{33,1},{65,33},{97,65},{2,98}... | collective-permute-start | bytes 983048 | tf_op jit(solution)/shard_map/ppermute | solution.py:20
  121.0 32.9 %collective-permute-start.17 = (bf16[640,256]{1,0:T(8,128)(2,1)}, bf16[640,256]{1,0:T(8,128)(2,1)}, u32[]{:S(2)}, u32[]{:S(2)}) collective-permute-start(bf16[640,256]{1,0:T(8,128)(2,1)} %bitcast.18), channel_id=1, source_target_pairs={{0,64},{32,96},{64,0},{96,32},{1,65},{33,97},{65,1},{97,33},{2,66}... | collective-permute-start | bytes 983048 | tf_op jit(solution)/shard_map/ppermute | solution.py:20
  124.8 38.7 %collective-permute-start.16 = (bf16[640,256]{1,0:T(8,128)(2,1)}, bf16[640,256]{1,0:T(8,128)(2,1)}, u32[]{:S(2)}, u32[]{:S(2)}) collective-permute-start(bf16[640,256]{1,0:T(8,128)(2,1)} %bitcast.17), channel_id=1, source_target_pairs={{0,32},{32,64},{64,96},{96,0},{1,33},{33,65},{65,97},{97,1},{2,34}... | collective-permute-start | bytes 983048 | tf_op jit(solution)/shard_map/ppermute | solution.py:20
  130.7 47.4 %all-to-all-start = ((bf16[32,12,1280]{2,1,0:T(8,128)(2,1)}), bf16[32,12,1280]{2,1,0:T(8,128)(2,1)S(1)}, u32[]{:S(2)}, u32[]{:S(2)}) async-start(bf16[32,12,1280]{2,1,0:T(8,128)(2,1)} %reshape.153), calls=%async_computation | async-start | bytes 2621440 | tf_op jit(solution)/shard_map/all_to_all | solution.py:47
  139.4 39.7 %collective-permute-start.32 = (bf16[4,80,1280]{2,1,0:T(8,128)(2,1)S(1)}, bf16[4,80,1280]{2,1,0:T(8,128)(2,1)}, u32[]{:S(2)}, u32[]{:S(2)}) collective-permute-start(bf16[4,80,1280]{2,1,0:T(8,128)(2,1)S(1)} %fusion.73), channel_id=1, source_target_pairs={{0,4},{4,0},{1,5},{5,1},{2,6},{6,2},{3,7},{7,3},{8,12},{12,8},{9,1... | collective-permute-start | bytes 2457608 | tf_op jit(solution)/shard_map/ppermute | solution.py:20
  170.0 14.0 %collective-permute-start.22 = (bf16[4,80,1280]{2,1,0:T(8,128)(2,1)}, bf16[4,80,1280]{2,1,0:T(8,128)(2,1)}, u32[]{:S(2)}, u32[]{:S(2)}) collective-permute-start(bf16[4,80,1280]{2,1,0:T(8,128)(2,1)} %fusion.72), channel_id=1, source_target_pairs={{0,4},{4,0},{1,5},{5,1},{2,6},{6,2},{3,7},{7,3},{8,12},{12,8},{9,1... | collective-permute-start | bytes 2457608 | tf_op jit(solution)/shard_map/ppermute | solution.py:20
  179.2 4.9 %copy-start.3 = (f32[640,1280]{1,0:T(8,128)S(1)}, f32[640,1280]{1,0:T(8,128)}, u32[]{:S(2)}) copy-start(f32[640,1280]{1,0:T(8,128)} %copy-done.2) | copy-start | bytes 9830404
  181.2 6.3 %collective-permute-start.35 = (bf16[80,1280]{1,0:T(8,128)(2,1)S(1)}, bf16[80,1280]{1,0:T(8,128)(2,1)S(1)}, u32[]{:S(2)}, u32[]{:S(2)}) collective-permute-start(bf16[80,1280]{1,0:T(8,128)(2,1)S(1)} %get-tuple-element.14), channel_id=1, source_target_pairs={{0,96},{32,0},{64,32},{96,64},{1,97},{33,1},{65,33},{97,65},{2,98}... | collective-permute-start | bytes 614408 | tf_op jit(solution)/shard_map/ppermute | solution.py:20
  181.7 8.1 %collective-permute-start.34 = (bf16[80,1280]{1,0:T(8,128)(2,1)S(1)}, bf16[80,1280]{1,0:T(8,128)(2,1)S(1)}, u32[]{:S(2)}, u32[]{:S(2)}) collective-permute-start(bf16[80,1280]{1,0:T(8,128)(2,1)S(1)} %get-tuple-element.15), channel_id=1, source_target_pairs={{0,64},{32,96},{64,0},{96,32},{1,65},{33,97},{65,1},{97,33},{2,66}... | collective-permute-start | bytes 614408 | tf_op jit(solution)/shard_map/ppermute | solution.py:20
  183.6 11.0 %collective-permute-start.33 = (bf16[80,1280]{1,0:T(8,128)(2,1)S(1)}, bf16[80,1280]{1,0:T(8,128)(2,1)S(1)}, u32[]{:S(2)}, u32[]{:S(2)}) collective-permute-start(bf16[80,1280]{1,0:T(8,128)(2,1)S(1)} %get-tuple-element.13), channel_id=1, source_target_pairs={{0,32},{32,64},{64,96},{96,0},{1,33},{33,65},{65,97},{97,1},{2,34}... | collective-permute-start | bytes 614408 | tf_op jit(solution)/shard_map/ppermute | solution.py:20
  185.5 9.3 %collective-permute-start.25 = (bf16[80,1280]{1,0:T(8,128)(2,1)S(1)}, bf16[80,1280]{1,0:T(8,128)(2,1)S(1)}, u32[]{:S(2)}, u32[]{:S(2)}) collective-permute-start(bf16[80,1280]{1,0:T(8,128)(2,1)S(1)} %get-tuple-element.11), channel_id=1, source_target_pairs={{0,24},{8,0},{16,8},{24,16},{1,25},{9,1},{17,9},{25,17},{2,26},{10... | collective-permute-start | bytes 614408 | tf_op jit(solution)/shard_map/ppermute | solution.py:20
  187.5 7.5 %collective-permute-start.24 = (bf16[80,1280]{1,0:T(8,128)(2,1)S(1)}, bf16[80,1280]{1,0:T(8,128)(2,1)S(1)}, u32[]{:S(2)}, u32[]{:S(2)}) collective-permute-start(bf16[80,1280]{1,0:T(8,128)(2,1)S(1)} %get-tuple-element.12), channel_id=1, source_target_pairs={{0,16},{8,24},{16,0},{24,8},{1,17},{9,25},{17,1},{25,9},{2,18},{10... | collective-permute-start | bytes 614408 | tf_op jit(solution)/shard_map/ppermute | solution.py:20
  187.5 12.6 %collective-permute-start.23 = (bf16[80,1280]{1,0:T(8,128)(2,1)S(1)}, bf16[80,1280]{1,0:T(8,128)(2,1)S(1)}, u32[]{:S(2)}, u32[]{:S(2)}) collective-permute-start(bf16[80,1280]{1,0:T(8,128)(2,1)S(1)} %get-tuple-element.10), channel_id=1, source_target_pairs={{0,8},{8,16},{16,24},{24,0},{1,9},{9,17},{17,25},{25,1},{2,10},{10... | collective-permute-start | bytes 614408 | tf_op jit(solution)/shard_map/ppermute | solution.py:20
  (4 other events, 10.6 us)

commit v2 on v1

--- a/solution.py
+++ b/solution.py
@@ -1,6 +1,8 @@
 import jax
 import jax.numpy as jnp
 from jax import lax
+from jax.experimental import pallas as pl
+from jax.experimental.pallas import tpu as pltpu
 from jax.sharding import Mesh
 from jax.sharding import PartitionSpec as P
 
@@ -47,6 +49,35 @@
     return lax.all_to_all(blocks, DP, split_axis=0, concat_axis=0, tiled=True).reshape(packed.shape)
 
 
+def chunk_product(out_proj, context, chunk, dtype):
+    rows, width = context.shape
+    tile = 256
+
+    def body(which, proj_ref, context_ref, out_ref):
+        out_ref[...] = lax.dot_general(
+            proj_ref[...], context_ref[...], (((1,), (1,)), ((), ())), preferred_element_type=F32
+        ).astype(dtype)
+
+    tiles = width // tile
+    return pl.pallas_call(
+        body,
+        out_shape=jax.ShapeDtypeStruct((width, rows), dtype),
+        grid_spec=pltpu.PrefetchScalarGridSpec(
+            num_scalar_prefetch=1,
+            grid=(tiles,),
+            in_specs=[
+                pl.BlockSpec((tile, width), lambda i, which: (which[0] * tiles + i, 0)),
+                pl.BlockSpec((rows, width), lambda i, which: (0, 0)),
+            ],
+            out_specs=pl.BlockSpec((tile, rows), lambda i, which: (i, 0)),
+        ),
+        cost_estimate=pl.CostEstimate(
+            flops=2 * rows * width * width, bytes_accessed=2 * width * width, transcendentals=0
+        ),
+        name="forward_part",
+    )(chunk.reshape(1), out_proj, context)
+
+
 def per_device(
     context, residual, cotangent, out_proj, norm_gain, rewards, group_ids, lengths, destinations
 ):
@@ -65,13 +96,11 @@
 
     proj = out_proj.reshape(NZ, width, width)
 
-    def part(step):
-        return lax.dot_general(
-            pick(proj, (z + step) % NZ), context, (((1,), (1,)), ((), ())), preferred_element_type=F32
-        )
+    def part(step, dtype=F32):
+        return chunk_product(out_proj, context, (z + step) % NZ, dtype)
 
     top = width // 2
-    far = part(2).astype(BF16)
+    far = part(2, BF16)
     far_left = shift(far[:top], "z", 1)
     far_right = shift(far[top:], "z", 3)
     near, back, own = part(1), part(3), part(0)
@@ -79,8 +108,13 @@
     back = jnp.concatenate([back[:top], back[top:] + far_right.astype(F32)], axis=0).astype(BF16)
     attn_t = own + shift(near, "z", 1).astype(F32) + shift(back, "z", 3).astype(F32)
 
-    context_x = jnp.concatenate([context] + [shift(context, "x", k) for k in (1, 2, 3)], axis=0)
-    context_y = jnp.concatenate([context] + [shift(context, "y", k) for k in (1, 2, 3)], axis=0)
+    context_x, context_y = (
+        jnp.concatenate([pick(gathered, (place - k) % 4) for k in range(4)], axis=0)
+        for gathered, place in (
+            (lax.all_gather(context, "x", axis=0), x),
+            (lax.all_gather(context, "y", axis=0), y),
+        )
+    )
 
     hidden_t = residual.T.astype(F32) + attn_t
     upstream_t = norm_gain[:, None] * (row_weights.astype(F32)[None, :] * cotangent.T.astype(F32))

time: 202 us -> 195 us (0.965)
  Pallas kernels: 0 us -> 22.3 us
  waiting for transfers between devices: 63 us -> 44.2 us
  matrix products: 42.7 us -> 24.3 us
  between operations: 1.17 us -> 14.9 us
  starting transfers between devices: 65.5 us -> 56.4 us
  local copies, waits for them, and re-layouts: 17.9 us -> 20.7 us
    ppermute x36 -> x30, waiting for transfers between devices: 56.7 us -> 32.7 us  [shift(): lax.ppermute(value, axis, [(i, (i + step) % size) for i in range(size)])]
    pallas_call x0 -> x4, Pallas kernels: none -> 22.3 us  [chunk_product(): pl.pallas_call(body, out_shape=jax.ShapeDtypeStruct((width, rows), dtype)...]
    dot_general x4 -> x0, matrix products: 14.8 us -> none  [part(): lax.dot_general(pick(proj, (z + step) % NZ), context, (((1,), (1,)), ((),...]
    ppermute x36 -> x30, starting transfers between devices: 44.6 us -> 39.1 us  [shift(): lax.ppermute(value, axis, [(i, (i + step) % size) for i in range(size)])]
    all_to_all x2, waiting for transfers between devices: 6.24 us -> 10.8 us  [exchange(): lax.all_to_all(blocks, DP, split_axis=0, concat_axis=0, tiled=True)]
    squeeze x0 -> x2, local copies, waits for them, and re-layouts: none -> 3.75 us  [pick(): return lax.dynamic_index_in_dim(values, index, 0, keepdims=False)]
    all_to_all x2, starting transfers between devices: 20.9 us -> 17.3 us  [exchange(): lax.all_to_all(blocks, DP, split_axis=0, concat_axis=0, tiled=True)]
    dot_general x1, matrix products: 5.6 us -> 3.03 us  [per_device(): jnp.dot(jnp.concatenate(along_y, axis=1), context_y, preferred_element_ty...]
  transfers between devices with their start and end apart: 38 -> 34, of which waited for: 18 -> 12; matrix products, arithmetic and copies ran while one was open for 34% -> 27% of each run, Pallas kernels for 0% -> 12%
where the time goes in v2:
time: 195 us; the launch traced here: 194 us
  starting transfers between devices  56.4 us (29%)
  waiting for transfers between devices  44.2 us (23%)
  matrix products  24.3 us (12%)
  Pallas kernels  22.3 us (11%)
  local copies, waits for them, and re-layouts  20.7 us (11%)
  between operations  14.9 us (8%)
  other arithmetic  11.1 us (6%)
    ppermute x30, starting transfers between devices, shift(): lax.ppermute(value, axis, [(i, (i + step) % size) for i in range(size)])  39.1 us
    ppermute x30, waiting for transfers between devices, shift(): lax.ppermute(value, axis, [(i, (i + step) % size) for i in range(size)])  32.7 us
    pallas_call x4, Pallas kernels, chunk_product(): pl.pallas_call(body, out_shape=jax.ShapeDtypeStruct((width, rows), dtype)...  22.3 us
    all_to_all x2, starting transfers between devices, exchange(): lax.all_to_all(blocks, DP, split_axis=0, concat_axis=0, tiled=True)  17.3 us
    dot_general x3, matrix products, per_device(): lax.dot_general(chunk, pick(proj, (z + j) % NZ), (((0,), (0,)), ((), ()))...  12.1 us
    all_to_all x2, waiting for transfers between devices, exchange(): lax.all_to_all(blocks, DP, split_axis=0, concat_axis=0, tiled=True)  10.8 us
    dot_general x1, matrix products, per_device(): jnp.dot(slots, context_grad, preferred_element_type=F32).astype(BF16)  5.64 us
    unnamed x31, local copies, waits for them, and re-layouts  3.94 us
  transfers between devices with their start and end apart: 34, of which 12 were waited for; matrix products, arithmetic and copies ran while one was open for 27% of the time, Pallas kernels for 12%

profile of v2, /device:TPU:1, one launch (start us, length us, event | category | flops | bytes accessed | tf_op | source)
XLA Modules:
  0.0 194.1 jit_solution(3897969991610506427)
XLA Ops:
  8.0 5.4 %forward_part.6 = bf16[1280,256]{1,0:T(8,128)(2,1)} custom-call(s32[1]{0:T(128)} %bitcast.4.which, bf16[5120,1280]{1,0:T(8,128)(2,1)} %proj_ref.7, bf16[256,1280]{1,0:T(8,128)(2,1)} %context_ref.7), custom_call_target="tpu_custom_call" | custom-call | flops 838860800 | bytes 3276800 | tf_op jit(solution)/shard_map/forward_part/pallas_call | solution.py:62
  13.4 1.1 fusion.90
  14.5 4.7 %collective-permute-start.2 = (bf16[640,256]{1,0:T(8,128)(2,1)S(1)}, bf16[640,256]{1,0:T(8,128)(2,1)S(1)}, u32[]{:S(2)}, u32[]{:S(2)}) collective-permute-start(bf16[640,256]{1,0:T(8,128)(2,1)S(1)} %get-tuple-element.33), channel_id=1, source_target_pairs={{0,3},{1,0},{2,1},{3,2},{4,7},{5,4},{6,5},{7,6},{8,11},{9,8},{10,9... | collective-permute-start | bytes 983048 | tf_op jit(solution)/shard_map/ppermute | solution.py:22
  19.2 5.6 %forward_part.7 = f32[1280,256]{1,0:T(8,128)} custom-call(s32[1]{0:T(128)} %bitcast.5.which, bf16[5120,1280]{1,0:T(8,128)(2,1)} %proj_ref.7, bf16[256,1280]{1,0:T(8,128)(2,1)} %context_ref.7), custom_call_target="tpu_custom_call" | custom-call | flops 838860800 | bytes 3276800 | tf_op jit(solution)/shard_map/forward_part/pallas_call | solution.py:62
  24.8 1.1 slice.81
  25.9 5.7 %forward_part.5 = f32[1280,256]{1,0:T(8,128)} custom-call(s32[1]{0:T(128)} %bitcast.3.which, bf16[5120,1280]{1,0:T(8,128)(2,1)} %proj_ref.7, bf16[256,1280]{1,0:T(8,128)(2,1)} %context_ref.7), custom_call_target="tpu_custom_call" | custom-call | flops 838860800 | bytes 3276800 | tf_op jit(solution)/shard_map/forward_part/pallas_call | solution.py:62
  31.6 1.2 slice.82
  33.0 2.7 %collective-permute-start.3 = (bf16[1280,256]{1,0:T(8,128)(2,1)S(1)}, bf16[1280,256]{1,0:T(8,128)(2,1)}, u32[]{:S(2)}, u32[]{:S(2)}) collective-permute-start(bf16[1280,256]{1,0:T(8,128)(2,1)S(1)} %pad_maximum_fusion.2), channel_id=1, source_target_pairs={{0,3},{1,0},{2,1},{3,2},{4,7},{5,4},{6,5},{7,6},{8,11},{9,8},{10,9... | collective-permute-start | bytes 1966088 | tf_op jit(solution)/shard_map/ppermute | solution.py:22
  37.8 1.5 collective-permute-start.4
  39.9 5.6 %forward_part.4 = f32[1280,256]{1,0:T(8,128)} custom-call(s32[1]{0:T(128)} %bitcast.2.which, bf16[5120,1280]{1,0:T(8,128)(2,1)} %proj_ref.7, bf16[256,1280]{1,0:T(8,128)(2,1)} %context_ref.7), custom_call_target="tpu_custom_call" | custom-call | flops 838860800 | bytes 3276800 | tf_op jit(solution)/shard_map/forward_part/pallas_call | solution.py:62
  45.5 1.3 collective-permute-start.5
  46.8 2.8 %collective-permute-done.5 = f32[8]{0:T(128)S(1)} collective-permute-done((f32[8]{0:T(128)S(1)}, f32[8]{0:T(128)S(1)}, u32[]{:S(2)}, u32[]{:S(2)}) %collective-permute-start.5) | collective-permute-done | bytes 64 | tf_op jit(solution)/shard_map/ppermute | solution.py:22
  49.6 1.5 collective-permute-start.6
  51.1 2.4 %collective-permute-done.6 = f32[8]{0:T(128)S(1)} collective-permute-done((f32[8]{0:T(128)S(1)}, f32[8]{0:T(128)S(1)}, u32[]{:S(2)}, u32[]{:S(2)}) %collective-permute-start.6) | collective-permute-done | bytes 64 | tf_op jit(solution)/shard_map/ppermute | solution.py:22
  53.5 1.3 collective-permute-start.7
  54.8 2.4 %collective-permute-done.7 = f32[8]{0:T(128)S(1)} collective-permute-done((f32[8]{0:T(128)S(1)}, f32[8]{0:T(128)S(1)}, u32[]{:S(2)}, u32[]{:S(2)}) %collective-permute-start.7) | collective-permute-done | bytes 64 | tf_op jit(solution)/shard_map/ppermute | solution.py:22
  57.2 1.7 collective-permute-start.8
  58.9 2.2 %collective-permute-done.8 = f32[8]{0:T(128)S(1)} collective-permute-done((f32[8]{0:T(128)S(1)}, f32[8]{0:T(128)S(1)}, u32[]{:S(2)}, u32[]{:S(2)}) %collective-permute-start.8) | collective-permute-done | bytes 64 | tf_op jit(solution)/shard_map/ppermute | solution.py:22
  61.5 2.3 %multiply_reduce_fusion = (f32[256]{0:T(256)S(1)}, f32[256]{0:T(256)S(1)}, f32[1280,256]{1,0:T(8,128)S(1)}) fusion(bf16[256,1280]{0,1:T(8,128)(2,1)S(1)} %copy.21, f32[256]{0:T(256)S(1)} %reshape.183, f32[1280]{0:T(1024)S(1)} %copy-done.9, bf16[1280,256]{1,0:T(8,128)(2,1)} %collective-permute-done.3, f32[1280,256]{1,0:T(8,128)} %forward_part.4, ...), kind=kLoop, calls=%fused_computation.60 | loop fusion | flops 4259328 | bytes 5251072 | tf_op jit(solution)/shard_map/reduce_sum | solution.py:122
  63.7 3.0 %collective-permute-start.11 = (f32[2,256]{1,0:T(2,128)S(1)}, f32[2,256]{1,0:T(2,128)S(1)}, u32[]{:S(2)}, u32[]{:S(2)}) collective-permute-start(f32[2,256]{1,0:T(2,128)S(1)} %pad_maximum_fusion.3), channel_id=1, source_target_pairs={{0,3},{1,0},{2,1},{3,2},{4,7},{5,4},{6,5},{7,6},{8,11},{9,8},{10,9... | collective-permute-start | bytes 6152 | tf_op jit(solution)/shard_map/ppermute | solution.py:22
  67.6 3.1 %collective-permute-done.10 = f32[2,256]{1,0:T(2,128)S(1)} collective-permute-done((f32[2,256]{1,0:T(2,128)S(1)}, f32[2,256]{1,0:T(2,128)S(1)}, u32[]{:S(2)}, u32[]{:S(2)}) %collective-permute-start.10) | collective-permute-done | bytes 2080 | tf_op jit(solution)/shard_map/ppermute | solution.py:22
  71.5 2.4 %collective-permute-start.12 = (bf16[1280,256]{1,0:T(8,128)(2,1)S(1)}, bf16[1280,256]{1,0:T(8,128)(2,1)S(1)}, u32[]{:S(2)}, u32[]{:S(2)}) collective-permute-start(bf16[1280,256]{1,0:T(8,128)(2,1)S(1)} %fusion.56), channel_id=1, source_target_pairs={{0,3},{1,0},{2,1},{3,2},{4,7},{5,4},{6,5},{7,6},{8,11},{9,8},{10,9... | collective-permute-start | bytes 1966088 | tf_op jit(solution)/shard_map/ppermute | solution.py:22
  74.7 1.3 reshape.171
  76.0 10.8 %all-to-all-start.1 = ((bf16[32,12,1280]{2,1,0:T(8,128)(2,1)}), bf16[32,12,1280]{2,1,0:T(8,128)(2,1)S(1)}, u32[]{:S(2)}, u32[]{:S(2)}) async-start(bf16[32,12,1280]{2,1,0:T(8,128)(2,1)} %reshape.171), calls=%async_computation.1 | async-start | bytes 2621440 | tf_op jit(solution)/shard_map/all_to_all | solution.py:49
  86.9 4.0 %fusion.6 = f32[256,1280]{1,0:T(8,128)} fusion(bf16[1280,256]{1,0:T(8,128)(2,1)S(1)} %fusion.56, bf16[4,1280,1280]{2,1,0:T(8,128)(2,1)} %bitcast.122, s32[]{:T(128)S(6)} %select_n.197), kind=kOutput, calls=%fused_computation.6 | convolution fusion | flops 838860800 | bytes 5242884 | tf_op jit(solution)/shard_map/dot_general | solution.py:170
  91.0 2.9 %collective-permute-start.15 = (bf16[640,256]{1,0:T(8,128)(2,1)S(1)}, bf16[640,256]{1,0:T(8,128)(2,1)S(1)}, u32[]{:S(2)}, u32[]{:S(2)}) collective-permute-start(bf16[640,256]{1,0:T(8,128)(2,1)S(1)} %slice.62), channel_id=1, source_target_pairs={{0,3},{1,0},{2,1},{3,2},{4,7},{5,4},{6,5},{7,6},{8,11},{9,8},{10,9... | collective-permute-start | bytes 983048 | tf_op jit(solution)/shard_map/ppermute | solution.py:22
  93.9 4.0 %fusion = f32[256,1280]{1,0:T(8,128)} fusion(bf16[1280,256]{1,0:T(8,128)(2,1)S(1)} %collective-permute-done.13, bf16[4,1280,1280]{2,1,0:T(8,128)(2,1)} %bitcast.123, s32[]{:T(128)S(6)} %select_n.200), kind=kOutput, calls=%fused_computation | convolution fusion | flops 838860800 | bytes 5242884 | tf_op jit(solution)/shard_map/dot_general | solution.py:170
  98.8 4.0 %fusion.2 = f32[256,1280]{1,0:T(8,128)} fusion(bf16[1280,256]{1,0:T(8,128)(2,1)S(1)} %constant_dynamic-update-slice_fusion, bf16[4,1280,1280]{2,1,0:T(8,128)(2,1)} %bitcast.124, s32[]{:T(128)S(6)} %select_n.199), kind=kOutput, calls=%fused_computation.2 | convolution fusion | flops 838860800 | bytes 5242884 | tf_op jit(solution)/shard_map/dot_general | solution.py:170
  102.8 5.6 %convolution_convert_fusion.1 = bf16[384,1280]{1,0:T(8,128)(2,1)} fusion(f32[256,1280]{1,0:T(8,128)} %fusion, f32[256,1280]{1,0:T(8,128)} %fusion.2, f32[256,1280]{1,0:T(8,128)} %fusion.6, bf16[1280,256]{1,0:T(8,128)(2,1)S(1)} %collective-permute-done.12, bf16[4,1280,1280]{2,1,0:T(8,128)(2,1)} %bitcast.125, s32[]{:T(128)S(6)} %select_n.198, s32[256]{0:T(256)S(1)} %add.288), kind=kOutput, calls=%fused_computation.13 | convolution fusion | flops 1092419584 | bytes 8848388 | tf_op jit(solution)/shard_map/dot_general | solution.py:175
  108.5 2.3 %reshape.169 = bf16[32,12,1280]{2,1,0:T(8,128)(2,1)} reshape(bf16[384,1280]{1,0:T(8,128)(2,1)} %convolution_convert_fusion.1) | data formatting | bytes 1966080 | tf_op jit(solution)/shard_map/reshape | solution.py:48
  110.7 1.4 pad_maximum_fusion
  112.6 3.4 %collective-permute-start.25 = (bf16[640,256]{1,0:T(8,128)(2,1)S(1)}, bf16[640,256]{1,0:T(8,128)(2,1)}, u32[]{:S(2)}, u32[]{:S(2)}) collective-permute-start(bf16[640,256]{1,0:T(8,128)(2,1)S(1)} %bitcast.140), channel_id=1, source_target_pairs={{0,24},{8,0},{16,8},{24,16},{1,25},{9,1},{17,9},{25,17},{2,26},{10... | collective-permute-start | bytes 983048 | tf_op jit(solution)/shard_map/ppermute | solution.py:22
  118.4 3.7 %collective-permute-start.18 = (bf16[640,256]{1,0:T(8,128)(2,1)}, bf16[640,256]{1,0:T(8,128)(2,1)}, u32[]{:S(2)}, u32[]{:S(2)}) collective-permute-start(bf16[640,256]{1,0:T(8,128)(2,1)} %bitcast.23), channel_id=1, source_target_pairs={{0,96},{32,0},{64,32},{96,64},{1,97},{33,1},{65,33},{97,65},{2,98}... | collective-permute-start | bytes 983048 | tf_op jit(solution)/shard_map/ppermute | solution.py:22
  122.7 1.8 dynamic-slice_bitcast_fusion.3
  125.2 8.5 %collective-permute-done.23 = bf16[640,256]{1,0:T(8,128)(2,1)} collective-permute-done((bf16[640,256]{1,0:T(8,128)(2,1)S(1)}, bf16[640,256]{1,0:T(8,128)(2,1)}, u32[]{:S(2)}, u32[]{:S(2)}) %collective-permute-start.23) | collective-permute-done | bytes 327712 | tf_op jit(solution)/shard_map/ppermute | solution.py:22
  133.7 3.0 %fusion.29 = f32[640,1280]{1,0:T(8,128)S(1)} fusion(bf16[256,1280]{1,0:T(8,128)(2,1)S(1)} %get-tuple-element.15, bf16[256,1280]{1,0:T(8,128)(2,1)S(1)} %get-tuple-element.16, bf16[256,1280]{1,0:T(8,128)(2,1)S(1)} %get-tuple-element.17, bf16[256,1280]{1,0:T(8,128)(2,1)S(1)} %get-tuple-element.14, bf16[640,256]{1,0:T(8,128)(2,1)} %collective-permute-done.25, ...), kind=kOutput, calls=%fused_computation.26 | convolution fusion | flops 1693450240 | bytes 7208960 | tf_op jit(solution)/shard_map/dot_general | solution.py:155
  138.6 1.1 collective-permute-start.26
  139.7 6.5 %all-to-all-start = ((bf16[32,12,1280]{2,1,0:T(8,128)(2,1)}), bf16[32,12,1280]{2,1,0:T(8,128)(2,1)S(1)}, u32[]{:S(2)}, u32[]{:S(2)}) async-start(bf16[32,12,1280]{2,1,0:T(8,128)(2,1)} %reshape.169), calls=%async_computation | async-start | bytes 2621440 | tf_op jit(solution)/shard_map/all_to_all | solution.py:49
  146.2 1.9 dynamic-slice_bitcast_fusion.7
  148.2 3.0 %fusion.21 = f32[640,1280]{1,0:T(8,128)S(1)} fusion(bf16[256,1280]{1,0:T(8,128)(2,1)S(1)} %get-tuple-element.11, bf16[256,1280]{1,0:T(8,128)(2,1)S(1)} %get-tuple-element.12, bf16[256,1280]{1,0:T(8,128)(2,1)S(1)} %get-tuple-element.13, bf16[256,1280]{1,0:T(8,128)(2,1)S(1)} %get-tuple-element.10, bf16[640,256]{1,0:T(8,128)(2,1)} %collective-permute-done.18, ...), kind=kOutput, calls=%fused_computation.18 | convolution fusion | flops 1693450240 | bytes 7208960 | tf_op jit(solution)/shard_map/dot_general | solution.py:154
  151.2 1.7 copy-done.3
  155.2 10.8 %all-to-all-done = bf16[32,12,1280]{2,1,0:T(8,128)(2,1)S(1)} async-done(((bf16[32,12,1280]{2,1,0:T(8,128)(2,1)}), bf16[32,12,1280]{2,1,0:T(8,128)(2,1)S(1)}, u32[]{:S(2)}, u32[]{:S(2)}) %all-to-all-start) | async-done | bytes 983072 | tf_op jit(solution)/shard_map/all_to_all | solution.py:49
  167.1 2.0 %bitcast_add_fusion = f32[4,80,1280]{2,1,0:T(8,128)S(1)} fusion(bf16[4,80,1280]{2,1,0:T(8,128)(2,1)} %collective-permute-done.26, f32[4,2,80,1280]{3,2,1,0:T(8,128)} %bitcast.131, s32[]{:T(128)S(6)} %select_n.217), kind=kLoop, calls=%fused_computation.37 | loop fusion | flops 819200 | bytes 4096004 | tf_op jit(solution)/shard_map/add | solution.py:160
  171.2 1.3 bitcast_add_fusion.1
  172.6 1.3 collective-permute-start.22
  175.5 1.6 collective-permute-done.28
  177.0 5.7 %collective-permute-done.27 = bf16[80,1280]{1,0:T(8,128)(2,1)S(1)} collective-permute-done((bf16[80,1280]{1,0:T(8,128)(2,1)S(1)}, bf16[80,1280]{1,0:T(8,128)(2,1)S(1)}, u32[]{:S(2)}, u32[]{:S(2)}) %collective-permute-start.27) | collective-permute-done | bytes 204832 | tf_op jit(solution)/shard_map/ppermute | solution.py:22
  182.8 3.3 %collective-permute-done.20 = bf16[80,1280]{1,0:T(8,128)(2,1)S(1)} collective-permute-done((bf16[80,1280]{1,0:T(8,128)(2,1)S(1)}, bf16[80,1280]{1,0:T(8,128)(2,1)S(1)}, u32[]{:S(2)}, u32[]{:S(2)}) %collective-permute-start.20) | collective-permute-done | bytes 204832 | tf_op jit(solution)/shard_map/ppermute | solution.py:22
  (112 shorter events, 21.0 us)
Async XLA Ops:
  7.2 115.5 %all-gather.7.cloned.1.call-start = ((), (), s32[]{:S(2)}) async-start(), calls=%async_computation.3 | async-start | bytes 3276800 | tf_op jit(solution)/shard_map/all_gather | solution.py:115
  7.9 138.3 %all-gather.5.cloned.1.call-start = ((), (), s32[]{:S(2)}) async-start(), calls=%async_computation.2 | async-start | bytes 3276800 | tf_op jit(solution)/shard_map/all_gather | solution.py:114
  14.5 18.4 %collective-permute-start.2 = (bf16[640,256]{1,0:T(8,128)(2,1)S(1)}, bf16[640,256]{1,0:T(8,128)(2,1)S(1)}, u32[]{:S(2)}, u32[]{:S(2)}) collective-permute-start(bf16[640,256]{1,0:T(8,128)(2,1)S(1)} %get-tuple-element.33), channel_id=1, source_target_pairs={{0,3},{1,0},{2,1},{3,2},{4,7},{5,4},{6,5},{7,6},{8,11},{9,8},{10,9... | collective-permute-start | bytes 983048 | tf_op jit(solution)/shard_map/ppermute | solution.py:22
  19.1 16.6 %collective-permute-start = (bf16[640,256]{1,0:T(8,128)(2,1)S(1)}, bf16[640,256]{1,0:T(8,128)(2,1)}, u32[]{:S(2)}, u32[]{:S(2)}) collective-permute-start(bf16[640,256]{1,0:T(8,128)(2,1)S(1)} %get-tuple-element.32), channel_id=1, source_target_pairs={{0,1},{1,2},{2,3},{3,0},{4,5},{5,6},{6,7},{7,4},{8,9},{9,10},{10,1... | collective-permute-start | bytes 983048 | tf_op jit(solution)/shard_map/ppermute | solution.py:22
  25.9 6.9 %copy-start = (f32[1280,256]{1,0:T(8,128)S(1)}, f32[1280,256]{1,0:T(8,128)}, u32[]{:S(2)}) copy-start(f32[1280,256]{1,0:T(8,128)} %forward_part.7) | copy-start | bytes 3932164
  31.6 4.1 %copy-start.1 = (f32[1280,256]{1,0:T(8,128)S(1)}, f32[1280,256]{1,0:T(8,128)}, u32[]{:S(2)}) copy-start(f32[1280,256]{1,0:T(8,128)} %forward_part.5) | copy-start | bytes 3932164
  33.0 4.7 %copy-start.11 = (f32[4]{0:T(128)S(1)}, f32[4]{0:T(128)}, u32[]{:S(2)}) copy-start(f32[4]{0:T(128)} %param.14) | copy-start | bytes 52
  33.0 4.7 %copy-start.12 = (s32[4]{0:T(128)S(1)}, s32[4]{0:T(128)}, u32[]{:S(2)}) copy-start(s32[4]{0:T(128)} %param.15) | copy-start | bytes 52
  33.0 6.3 %copy-start.6 = (bf16[256,1280]{1,0:T(8,128)(2,1)S(1)}, bf16[256,1280]{1,0:T(8,128)(2,1)}, u32[]{:S(2)}) copy-start(bf16[256,1280]{1,0:T(8,128)(2,1)} %param.11) | copy-start | bytes 1966084
  33.0 28.4 %collective-permute-start.3 = (bf16[1280,256]{1,0:T(8,128)(2,1)S(1)}, bf16[1280,256]{1,0:T(8,128)(2,1)}, u32[]{:S(2)}, u32[]{:S(2)}) collective-permute-start(bf16[1280,256]{1,0:T(8,128)(2,1)S(1)} %pad_maximum_fusion.2), channel_id=1, source_target_pairs={{0,3},{1,0},{2,1},{3,2},{4,7},{5,4},{6,5},{7,6},{8,11},{9,8},{10,9... | collective-permute-start | bytes 1966088 | tf_op jit(solution)/shard_map/ppermute | solution.py:22
  36.8 2.8 %copy-start.7 = (bf16[256,1280]{1,0:T(8,128)(2,1)S(1)}, bf16[256,1280]{1,0:T(8,128)(2,1)}, u32[]{:S(2)}) copy-start(bf16[256,1280]{1,0:T(8,128)(2,1)} %param.10) | copy-start | bytes 1966084
  37.7 23.8 %collective-permute-start.1 = (bf16[1280,256]{1,0:T(8,128)(2,1)}, bf16[1280,256]{1,0:T(8,128)(2,1)}, u32[]{:S(2)}, u32[]{:S(2)}) collective-permute-start(bf16[1280,256]{1,0:T(8,128)(2,1)} %pad_maximum_fusion.1), channel_id=1, source_target_pairs={{0,1},{1,2},{2,3},{3,0},{4,5},{5,6},{6,7},{7,4},{8,9},{9,10},{10,1... | collective-permute-start | bytes 1966088 | tf_op jit(solution)/shard_map/ppermute | solution.py:22
  37.8 7.7 %collective-permute-start.4 = (f32[8]{0:T(128)S(1)}, f32[8]{0:T(128)S(1)}, u32[]{:S(2)}, u32[]{:S(2)}) collective-permute-start(f32[8]{0:T(128)S(1)} %select_reduce_fusion.1), channel_id=1, source_target_pairs={{0,4},{4,0},{1,5},{5,1},{2,6},{6,2},{3,7},{7,3},{8,12},{12,8},{9,1... | collective-permute-start | bytes 104 | tf_op jit(solution)/shard_map/ppermute | solution.py:22
  39.9 21.4 %copy-start.10 = (s32[4]{0:T(128)S(1)}, s32[4]{0:T(128)}, u32[]{:S(2)}) copy-start(s32[4]{0:T(128)} %param.16) | copy-start | bytes 52
  39.9 21.6 %copy-start.9 = (f32[1280]{0:T(1024)S(1)}, f32[1280]{0:T(1024)}, u32[]{:S(2)}) copy-start(f32[1280]{0:T(1024)} %param.13) | copy-start | bytes 15364
  45.5 4.1 %collective-permute-start.5 = (f32[8]{0:T(128)S(1)}, f32[8]{0:T(128)S(1)}, u32[]{:S(2)}, u32[]{:S(2)}) collective-permute-start(f32[8]{0:T(128)S(1)} %add.301), channel_id=1, source_target_pairs={{0,32},{32,64},{64,96},{96,0},{1,33},{33,65},{65,97},{97,1},{2,34}... | collective-permute-start | bytes 104 | tf_op jit(solution)/shard_map/ppermute | solution.py:22
  49.6 3.9 %collective-permute-start.6 = (f32[8]{0:T(128)S(1)}, f32[8]{0:T(128)S(1)}, u32[]{:S(2)}, u32[]{:S(2)}) collective-permute-start(f32[8]{0:T(128)S(1)} %add.302), channel_id=1, source_target_pairs={{0,64},{32,96},{64,0},{96,32},{1,65},{33,97},{65,1},{97,33},{2,66}... | collective-permute-start | bytes 104 | tf_op jit(solution)/shard_map/ppermute | solution.py:22
  53.5 3.7 %collective-permute-start.7 = (f32[8]{0:T(128)S(1)}, f32[8]{0:T(128)S(1)}, u32[]{:S(2)}, u32[]{:S(2)}) collective-permute-start(f32[8]{0:T(128)S(1)} %add.303), channel_id=1, source_target_pairs={{0,8},{8,16},{16,24},{24,0},{1,9},{9,17},{17,25},{25,1},{2,10},{10... | collective-permute-start | bytes 104 | tf_op jit(solution)/shard_map/ppermute | solution.py:22
  57.2 3.9 %collective-permute-start.8 = (f32[8]{0:T(128)S(1)}, f32[8]{0:T(128)S(1)}, u32[]{:S(2)}, u32[]{:S(2)}) collective-permute-start(f32[8]{0:T(128)S(1)} %add.304), channel_id=1, source_target_pairs={{0,16},{8,24},{16,0},{24,8},{1,17},{9,25},{17,1},{25,9},{2,18},{10... | collective-permute-start | bytes 104 | tf_op jit(solution)/shard_map/ppermute | solution.py:22
  61.5 6.0 %copy-start.13 = (s32[64,1]{0,1:T(1,128)S(1)}, s32[64,1]{0,1:T(1,128)}, u32[]{:S(2)}) copy-start(s32[64,1]{0,1:T(1,128)} %param.17) | copy-start | bytes 772
  63.7 3.9 %collective-permute-start.11 = (f32[2,256]{1,0:T(2,128)S(1)}, f32[2,256]{1,0:T(2,128)S(1)}, u32[]{:S(2)}, u32[]{:S(2)}) collective-permute-start(f32[2,256]{1,0:T(2,128)S(1)} %pad_maximum_fusion.3), channel_id=1, source_target_pairs={{0,3},{1,0},{2,1},{3,2},{4,7},{5,4},{6,5},{7,6},{8,11},{9,8},{10,9... | collective-permute-start | bytes 6152 | tf_op jit(solution)/shard_map/ppermute | solution.py:22
  66.8 4.0 %collective-permute-start.10 = (f32[2,256]{1,0:T(2,128)S(1)}, f32[2,256]{1,0:T(2,128)S(1)}, u32[]{:S(2)}, u32[]{:S(2)}) collective-permute-start(f32[2,256]{1,0:T(2,128)S(1)} %pad_maximum_fusion.3), channel_id=1, source_target_pairs={{0,2},{1,3},{2,0},{3,1},{4,6},{5,7},{6,4},{7,5},{8,10},{9,11},{10,... | collective-permute-start | bytes 6152 | tf_op jit(solution)/shard_map/ppermute | solution.py:22
  66.8 4.0 %collective-permute-start.9 = (f32[2,256]{1,0:T(2,128)S(1)}, f32[2,256]{1,0:T(2,128)S(1)}, u32[]{:S(2)}, u32[]{:S(2)}) collective-permute-start(f32[2,256]{1,0:T(2,128)S(1)} %pad_maximum_fusion.3), channel_id=1, source_target_pairs={{0,1},{1,2},{2,3},{3,0},{4,5},{5,6},{6,7},{7,4},{8,9},{9,10},{10,1... | collective-permute-start | bytes 6152 | tf_op jit(solution)/shard_map/ppermute | solution.py:22
  71.2 15.6 %collective-permute-start.13 = (bf16[1280,256]{1,0:T(8,128)(2,1)S(1)}, bf16[1280,256]{1,0:T(8,128)(2,1)S(1)}, u32[]{:S(2)}, u32[]{:S(2)}) collective-permute-start(bf16[1280,256]{1,0:T(8,128)(2,1)S(1)} %fusion.56), channel_id=1, source_target_pairs={{0,1},{1,2},{2,3},{3,0},{4,5},{5,6},{6,7},{7,4},{8,9},{9,10},{10,1... | collective-permute-start | bytes 1966088 | tf_op jit(solution)/shard_map/ppermute | solution.py:22
  71.5 19.4 %collective-permute-start.12 = (bf16[1280,256]{1,0:T(8,128)(2,1)S(1)}, bf16[1280,256]{1,0:T(8,128)(2,1)S(1)}, u32[]{:S(2)}, u32[]{:S(2)}) collective-permute-start(bf16[1280,256]{1,0:T(8,128)(2,1)S(1)} %fusion.56), channel_id=1, source_target_pairs={{0,3},{1,0},{2,1},{3,2},{4,7},{5,4},{6,5},{7,6},{8,11},{9,8},{10,9... | collective-permute-start | bytes 1966088 | tf_op jit(solution)/shard_map/ppermute | solution.py:22
  76.0 63.8 %all-to-all-start.1 = ((bf16[32,12,1280]{2,1,0:T(8,128)(2,1)}), bf16[32,12,1280]{2,1,0:T(8,128)(2,1)S(1)}, u32[]{:S(2)}, u32[]{:S(2)}) async-start(bf16[32,12,1280]{2,1,0:T(8,128)(2,1)} %reshape.171), calls=%async_computation.1 | async-start | bytes 2621440 | tf_op jit(solution)/shard_map/all_to_all | solution.py:49
  86.8 11.1 %collective-permute-start.14 = (bf16[640,256]{1,0:T(8,128)(2,1)S(1)}, bf16[640,256]{1,0:T(8,128)(2,1)S(1)}, u32[]{:S(2)}, u32[]{:S(2)}) collective-permute-start(bf16[640,256]{1,0:T(8,128)(2,1)S(1)} %slice.61), channel_id=1, source_target_pairs={{0,1},{1,2},{2,3},{3,0},{4,5},{5,6},{6,7},{7,4},{8,9},{9,10},{10,1... | collective-permute-start | bytes 983048 | tf_op jit(solution)/shard_map/ppermute | solution.py:22
  91.0 7.0 %collective-permute-start.15 = (bf16[640,256]{1,0:T(8,128)(2,1)S(1)}, bf16[640,256]{1,0:T(8,128)(2,1)S(1)}, u32[]{:S(2)}, u32[]{:S(2)}) collective-permute-start(bf16[640,256]{1,0:T(8,128)(2,1)S(1)} %slice.62), channel_id=1, source_target_pairs={{0,3},{1,0},{2,1},{3,2},{4,7},{5,4},{6,5},{7,6},{8,11},{9,8},{10,9... | collective-permute-start | bytes 983048 | tf_op jit(solution)/shard_map/ppermute | solution.py:22
  98.0 0.8 copy-start.5
  112.6 12.0 %collective-permute-start.25 = (bf16[640,256]{1,0:T(8,128)(2,1)S(1)}, bf16[640,256]{1,0:T(8,128)(2,1)}, u32[]{:S(2)}, u32[]{:S(2)}) collective-permute-start(bf16[640,256]{1,0:T(8,128)(2,1)S(1)} %bitcast.140), channel_id=1, source_target_pairs={{0,24},{8,0},{16,8},{24,16},{1,25},{9,1},{17,9},{25,17},{2,26},{10... | collective-permute-start | bytes 983048 | tf_op jit(solution)/shard_map/ppermute | solution.py:22
  116.0 9.2 %collective-permute-start.24 = (bf16[640,256]{1,0:T(8,128)(2,1)S(1)}, bf16[640,256]{1,0:T(8,128)(2,1)}, u32[]{:S(2)}, u32[]{:S(2)}) collective-permute-start(bf16[640,256]{1,0:T(8,128)(2,1)S(1)} %bitcast.139), channel_id=1, source_target_pairs={{0,16},{8,24},{16,0},{24,8},{1,17},{9,25},{17,1},{25,9},{2,18},{10... | collective-permute-start | bytes 983048 | tf_op jit(solution)/shard_map/ppermute | solution.py:22
  116.8 16.9 %collective-permute-start.23 = (bf16[640,256]{1,0:T(8,128)(2,1)S(1)}, bf16[640,256]{1,0:T(8,128)(2,1)}, u32[]{:S(2)}, u32[]{:S(2)}) collective-permute-start(bf16[640,256]{1,0:T(8,128)(2,1)S(1)} %bitcast.138), channel_id=1, source_target_pairs={{0,8},{8,16},{16,24},{24,0},{1,9},{9,17},{17,25},{25,1},{2,10},{10... | collective-permute-start | bytes 983048 | tf_op jit(solution)/shard_map/ppermute | solution.py:22
  118.4 29.8 %collective-permute-start.18 = (bf16[640,256]{1,0:T(8,128)(2,1)}, bf16[640,256]{1,0:T(8,128)(2,1)}, u32[]{:S(2)}, u32[]{:S(2)}) collective-permute-start(bf16[640,256]{1,0:T(8,128)(2,1)} %bitcast.23), channel_id=1, source_target_pairs={{0,96},{32,0},{64,32},{96,64},{1,97},{33,1},{65,33},{97,65},{2,98}... | collective-permute-start | bytes 983048 | tf_op jit(solution)/shard_map/ppermute | solution.py:22
  122.1 26.1 %collective-permute-start.17 = (bf16[640,256]{1,0:T(8,128)(2,1)}, bf16[640,256]{1,0:T(8,128)(2,1)}, u32[]{:S(2)}, u32[]{:S(2)}) collective-permute-start(bf16[640,256]{1,0:T(8,128)(2,1)} %bitcast.22), channel_id=1, source_target_pairs={{0,64},{32,96},{64,0},{96,32},{1,65},{33,97},{65,1},{97,33},{2,66}... | collective-permute-start | bytes 983048 | tf_op jit(solution)/shard_map/ppermute | solution.py:22
  124.6 23.6 %collective-permute-start.16 = (bf16[640,256]{1,0:T(8,128)(2,1)}, bf16[640,256]{1,0:T(8,128)(2,1)}, u32[]{:S(2)}, u32[]{:S(2)}) collective-permute-start(bf16[640,256]{1,0:T(8,128)(2,1)} %bitcast.21), channel_id=1, source_target_pairs={{0,32},{32,64},{64,96},{96,0},{1,33},{33,65},{65,97},{97,1},{2,34}... | collective-permute-start | bytes 983048 | tf_op jit(solution)/shard_map/ppermute | solution.py:22
  136.7 1.9 copy-start.2
  138.6 28.4 %collective-permute-start.26 = (bf16[4,80,1280]{2,1,0:T(8,128)(2,1)}, bf16[4,80,1280]{2,1,0:T(8,128)(2,1)}, u32[]{:S(2)}, u32[]{:S(2)}) collective-permute-start(bf16[4,80,1280]{2,1,0:T(8,128)(2,1)} %fusion.60), channel_id=1, source_target_pairs={{0,4},{4,0},{1,5},{5,1},{2,6},{6,2},{3,7},{7,3},{8,12},{12,8},{9,1... | collective-permute-start | bytes 2457608 | tf_op jit(solution)/shard_map/ppermute | solution.py:22
  139.7 26.3 %all-to-all-start = ((bf16[32,12,1280]{2,1,0:T(8,128)(2,1)}), bf16[32,12,1280]{2,1,0:T(8,128)(2,1)S(1)}, u32[]{:S(2)}, u32[]{:S(2)}) async-start(bf16[32,12,1280]{2,1,0:T(8,128)(2,1)} %reshape.169), calls=%async_computation | async-start | bytes 2621440 | tf_op jit(solution)/shard_map/all_to_all | solution.py:49
  146.2 2.0 %copy-start.8 = (bf16[1,4,2,1,80,256]{5,4,3,2,1,0:T(8,128)(2,1)S(1)}, bf16[1,4,2,1,80,256]{5,4,3,2,1,0:T(8,128)(2,1)}, u32[]{:S(2)}) copy-start(bf16[1,4,2,1,80,256]{5,4,3,2,1,0:T(8,128)(2,1)} %get-tuple-element.24) | copy-start | bytes 983044
  151.2 1.7 copy-start.3
  153.9 17.2 %collective-permute-start.19 = (bf16[4,80,1280]{2,1,0:T(8,128)(2,1)}, bf16[4,80,1280]{2,1,0:T(8,128)(2,1)}, u32[]{:S(2)}, u32[]{:S(2)}) collective-permute-start(bf16[4,80,1280]{2,1,0:T(8,128)(2,1)} %fusion.59), channel_id=1, source_target_pairs={{0,4},{4,0},{1,5},{5,1},{2,6},{6,2},{3,7},{7,3},{8,12},{12,8},{9,1... | collective-permute-start | bytes 2457608 | tf_op jit(solution)/shard_map/ppermute | solution.py:22
  167.1 4.1 %copy-start.4 = (f32[640,1280]{1,0:T(8,128)S(1)}, f32[640,1280]{1,0:T(8,128)}, u32[]{:S(2)}) copy-start(f32[640,1280]{1,0:T(8,128)} %copy-done.3) | copy-start | bytes 9830404
  169.1 6.3 %collective-permute-start.29 = (bf16[80,1280]{1,0:T(8,128)(2,1)S(1)}, bf16[80,1280]{1,0:T(8,128)(2,1)S(1)}, u32[]{:S(2)}, u32[]{:S(2)}) collective-permute-start(bf16[80,1280]{1,0:T(8,128)(2,1)S(1)} %get-tuple-element.22), channel_id=1, source_target_pairs={{0,96},{32,0},{64,32},{96,64},{1,97},{33,1},{65,33},{97,65},{2,98}... | collective-permute-start | bytes 614408 | tf_op jit(solution)/shard_map/ppermute | solution.py:22
  169.8 7.2 %collective-permute-start.28 = (bf16[80,1280]{1,0:T(8,128)(2,1)S(1)}, bf16[80,1280]{1,0:T(8,128)(2,1)S(1)}, u32[]{:S(2)}, u32[]{:S(2)}) collective-permute-start(bf16[80,1280]{1,0:T(8,128)(2,1)S(1)} %get-tuple-element.23), channel_id=1, source_target_pairs={{0,64},{32,96},{64,0},{96,32},{1,65},{33,97},{65,1},{97,33},{2,66}... | collective-permute-start | bytes 614408 | tf_op jit(solution)/shard_map/ppermute | solution.py:22
  170.4 12.3 %collective-permute-start.27 = (bf16[80,1280]{1,0:T(8,128)(2,1)S(1)}, bf16[80,1280]{1,0:T(8,128)(2,1)S(1)}, u32[]{:S(2)}, u32[]{:S(2)}) collective-permute-start(bf16[80,1280]{1,0:T(8,128)(2,1)S(1)} %get-tuple-element.21), channel_id=1, source_target_pairs={{0,32},{32,64},{64,96},{96,0},{1,33},{33,65},{65,97},{97,1},{2,34}... | collective-permute-start | bytes 614408 | tf_op jit(solution)/shard_map/ppermute | solution.py:22
  172.6 10.3 %collective-permute-start.22 = (bf16[80,1280]{1,0:T(8,128)(2,1)S(1)}, bf16[80,1280]{1,0:T(8,128)(2,1)S(1)}, u32[]{:S(2)}, u32[]{:S(2)}) collective-permute-start(bf16[80,1280]{1,0:T(8,128)(2,1)S(1)} %get-tuple-element.19), channel_id=1, source_target_pairs={{0,24},{8,0},{16,8},{24,16},{1,25},{9,1},{17,9},{25,17},{2,26},{10... | collective-permute-start | bytes 614408 | tf_op jit(solution)/shard_map/ppermute | solution.py:22
  173.8 9.0 %collective-permute-start.21 = (bf16[80,1280]{1,0:T(8,128)(2,1)S(1)}, bf16[80,1280]{1,0:T(8,128)(2,1)S(1)}, u32[]{:S(2)}, u32[]{:S(2)}) collective-permute-start(bf16[80,1280]{1,0:T(8,128)(2,1)S(1)} %get-tuple-element.20), channel_id=1, source_target_pairs={{0,16},{8,24},{16,0},{24,8},{1,17},{9,25},{17,1},{25,9},{2,18},{10... | collective-permute-start | bytes 614408 | tf_op jit(solution)/shard_map/ppermute | solution.py:22
  175.5 10.7 %collective-permute-start.20 = (bf16[80,1280]{1,0:T(8,128)(2,1)S(1)}, bf16[80,1280]{1,0:T(8,128)(2,1)S(1)}, u32[]{:S(2)}, u32[]{:S(2)}) collective-permute-start(bf16[80,1280]{1,0:T(8,128)(2,1)S(1)} %get-tuple-element.18), channel_id=1, source_target_pairs={{0,8},{8,16},{16,24},{24,0},{1,9},{9,17},{17,25},{25,1},{2,10},{10... | collective-permute-start | bytes 614408 | tf_op jit(solution)/shard_map/ppermute | solution.py:22
Sparse Core Ops, SparseCore 0:
  9.7 38.5 all-gather.6
  49.9 35.1 all-gather.4

commit v3 on v1

--- a/solution.py
+++ b/solution.py
@@ -10,7 +10,6 @@
 EPSILON = 1e-06
 NX, NY, NC, NZ = 4, 4, 2, 4
 DP = ("x", "y", "c")
-HALF = 80
 F32 = jnp.float32
 BF16 = jnp.bfloat16
 
@@ -24,11 +23,20 @@
     return lax.dynamic_index_in_dim(values, index, 0, keepdims=False)
 
 
+def cross(value, step, first):
+    pairs = []
+    for x in range(NX):
+        for y in range(NY):
+            for c in range(NC):
+                along_y = (c == 0) == first
+                to = (x, (y + step) % NY, c) if along_y else ((x + step) % NX, y, c)
+                pairs.append(((x * NY + y) * NC + c, (to[0] * NY + to[1]) * NC + to[2]))
+    return lax.ppermute(value, DP, pairs)
+
+
 def group_sum(value):
-    for axis, steps in (("c", (1,)), ("x", (1, 2)), ("y", (1, 2))):
-        for step in steps:
-            value = value + shift(value, axis, step)
-    return value
+    copies = jnp.broadcast_to(value, (NX * NY * NC,) + value.shape)
+    return jnp.sum(lax.all_to_all(copies, DP, split_axis=0, concat_axis=0, tiled=True), axis=0)
 
 
 def slot_matrix(owner_dest, slots, rows):
@@ -77,11 +85,19 @@
     near, back, own = part(1), part(3), part(0)
     near = jnp.concatenate([near[:top] + far_left.astype(F32), near[top:]], axis=0).astype(BF16)
     back = jnp.concatenate([back[:top], back[top:] + far_right.astype(F32)], axis=0).astype(BF16)
+    near, back, own = lax.optimization_barrier((near, back, own))
     attn_t = own + shift(near, "z", 1).astype(F32) + shift(back, "z", 3).astype(F32)
 
-    context_x = jnp.concatenate([context] + [shift(context, "x", k) for k in (1, 2, 3)], axis=0)
-    context_y = jnp.concatenate([context] + [shift(context, "y", k) for k in (1, 2, 3)], axis=0)
+    early, _ = lax.optimization_barrier((context, far))
+    others = [context, cross(early, 1, True), None, cross(early, 3, True)]
+    selves = [context, cross(early, 1, False), None, None]
+    late, _ = lax.optimization_barrier((context, near))
+    others[2] = cross(late, 2, True)
+    selves[2], selves[3] = cross(late, 2, False), cross(late, 3, False)
 
+    attn_t, others[1], others[3], selves[1] = lax.optimization_barrier(
+        (attn_t, others[1], others[3], selves[1])
+    )
     hidden_t = residual.T.astype(F32) + attn_t
     upstream_t = norm_gain[:, None] * (row_weights.astype(F32)[None, :] * cotangent.T.astype(F32))
     stats = jnp.stack(
@@ -92,52 +108,60 @@
     grad_t = (
         inv_rms[None, :] * upstream_t - hidden_t * (inv_rms**3 * stats[1] / full)[None, :]
     ).astype(BF16)
+    grad_t, others[2], selves[2], selves[3] = lax.optimization_barrier(
+        (grad_t, others[2], selves[2], selves[3])
+    )
 
+    def context_part(step, chunk):
+        return lax.dot_general(
+            chunk, pick(proj, (z + step) % NZ), (((0,), (0,)), ((), ())), preferred_element_type=F32
+        )
+
+    slots = slot_matrix(destinations[:, 0], lanes * PAIR, rows)
     from_left, from_right = shift(grad_t, "z", 1), shift(grad_t, "z", 3)
+    packed = lax.dot_general(
+        slots, grad_t, (((1,), (1,)), ((), ())), preferred_element_type=F32
+    ).astype(BF16)
+    d_residual = exchange(packed, lanes)
+    context_grad = context_part(0, grad_t)
+    from_left, from_right, context_grad = lax.optimization_barrier(
+        (from_left, from_right, context_grad)
+    )
     far_grad = jnp.concatenate(
         [shift(from_left[:top], "z", 1), shift(from_right[top:], "z", 3)], axis=0
     )
-    chunks = [grad_t, from_right, far_grad, from_left]
+    context_grad = context_grad + context_part(1, from_right) + context_part(3, from_left)
+    far_grad, context_grad = lax.optimization_barrier((far_grad, context_grad))
 
-    slots = slot_matrix(destinations[:, 0], lanes * PAIR, rows)
-    d_residual = exchange(
-        lax.dot_general(slots, grad_t, (((1,), (1,)), ((), ())), preferred_element_type=F32).astype(BF16),
-        lanes,
-    )
+    block = width // (NY * NC)
+    grad_full = jnp.stack([grad_t, from_right, far_grad, from_left]).reshape(NZ, NY, NC, block, rows)
 
-    grad_full = jnp.stack(chunks).reshape(NZ, NY, NC, 2, HALF, rows)
-    along_x = [
-        shift(pick(grad_full[:, :, :, 0], (x + k - z) % NZ).reshape(-1, rows), "x", k) if k
-        else pick(grad_full[:, :, :, 0], (x - z) % NZ).reshape(-1, rows)
-        for k in range(NX)
-    ]
-    halves_y = jnp.moveaxis(grad_full[:, :, :, 1], 1, 0)
-    along_y = [
-        shift(pick(halves_y, (y + k) % NY).reshape(-1, rows), "y", k) if k
-        else pick(halves_y, y).reshape(-1, rows)
-        for k in range(NY)
-    ]
-    part_x = jnp.dot(jnp.concatenate(along_x, axis=1), context_x, preferred_element_type=F32)
-    part_y = jnp.dot(jnp.concatenate(along_y, axis=1), context_y, preferred_element_type=F32)
+    def set_rows(step, first):
+        along_x = pick(grad_full[:, :, 0], (x + step - z) % NZ)
+        along_y = lax.dynamic_index_in_dim(grad_full[:, :, 1], (y + step) % NY, 1, keepdims=False)
+        return jnp.where((c == 0) == first, along_y, along_x).reshape(-1, rows)
 
-    def core_sum(value):
-        value = jnp.moveaxis(value.reshape(4, NC, HALF, width), 1, 0)
-        other = shift(pick(value, 1 - c).astype(BF16), "c", 1)
-        return pick(value, c) + other.astype(F32)
+    def partial_sum(first, contexts):
+        pieces = [set_rows(0, first)] + [cross(set_rows(k, first), k, first) for k in (1, 2, 3)]
+        return jnp.dot(
+            jnp.concatenate(pieces, axis=1),
+            jnp.concatenate(contexts, axis=0),
+            preferred_element_type=F32,
+        )
 
-    part_x, part_y = core_sum(part_x), core_sum(part_y)
-    total_x, total_y = pick(part_x, y), pick(part_y, (x - z) % NZ)
+    other = shift(partial_sum(True, others).astype(BF16), "c", 1)
+    total = partial_sum(False, selves) + other.astype(F32)
+    total = total.reshape(4, block, width)
+
+    def place(step):
+        return pick(total, jnp.where(c == 0, (y + step) % NY, (x + step - z) % NZ))
+
+    d_out_proj = place(0)
     for k in (1, 2, 3):
-        total_x = total_x + shift(pick(part_x, (y + k) % NY).astype(BF16), "y", k).astype(F32)
-        total_y = total_y + shift(pick(part_y, (x + k - z) % NZ).astype(BF16), "x", k).astype(F32)
-    d_out_proj = jnp.concatenate([total_x, total_y], axis=0) / lanes
+        d_out_proj = d_out_proj + cross(place(k).astype(BF16), k, True).astype(F32)
+    d_out_proj = d_out_proj / lanes
 
-    context_grad = sum(
-        lax.dot_general(
-            chunk, pick(proj, (z + j) % NZ), (((0,), (0,)), ((), ())), preferred_element_type=F32
-        )
-        for j, chunk in enumerate(chunks)
-    ).astype(BF16)
+    context_grad = (context_grad + context_part(2, far_grad)).astype(BF16)
     d_context = exchange(jnp.dot(slots, context_grad, preferred_element_type=F32).astype(BF16), lanes)
     return (d_context, d_residual, d_out_proj)
 

time: 202 us -> 201 us (level)
  waiting for transfers between devices: 63 us -> 81 us
  starting transfers between devices: 65.5 us -> 56.9 us
  matrix products: 42.7 us -> 37.3 us
  local copies, waits for them, and re-layouts: 17.9 us -> 12.9 us
    ppermute x0 -> x15, waiting for transfers between devices: none -> 40 us  [cross(): return lax.ppermute(value, DP, pairs)]
    ppermute x36 -> x12, waiting for transfers between devices: 56.7 us -> 18.3 us  [shift(): lax.ppermute(value, axis, [(i, (i + step) % size) for i in range(size)])]
    ppermute x36 -> x12, starting transfers between devices: 44.6 us -> 18.9 us  [shift(): lax.ppermute(value, axis, [(i, (i + step) % size) for i in range(size)])]
    ppermute x0 -> x15, starting transfers between devices: none -> 18.6 us  [cross(): return lax.ppermute(value, DP, pairs)]
    all_to_all x2, waiting for transfers between devices: 6.24 us -> 21.5 us  [exchange(): lax.all_to_all(blocks, DP, split_axis=0, concat_axis=0, tiled=True)]
    all_to_all x2, starting transfers between devices: 20.9 us -> 10.8 us  [exchange(): lax.all_to_all(blocks, DP, split_axis=0, concat_axis=0, tiled=True)]
    all_to_all x0 -> x1, starting transfers between devices: none -> 8.6 us  [group_sum(): lax.all_to_all(copies, DP, split_axis=0, concat_axis=0, tiled=True)]
    dot_general x5, matrix products: 21.8 us -> 18.8 us  [the longest x3 10 us: context_part(): lax.dot_general(chunk, pick(proj, (z + step) % NZ), (((0,), (0,)), ((), (...]
  transfers between devices with their start and end apart: 38 -> 30, of which waited for: 18 -> 16; matrix products, arithmetic and copies ran while one was open for 34% -> 21% of each run, Pallas kernels for 0% -> 0%
where the time goes in v3:
time: 201 us
  waiting for transfers between devices  81 us (40%)
  starting transfers between devices  56.9 us (28%)
  matrix products  37.3 us (19%)
  local copies, waits for them, and re-layouts  12.9 us (6%)
  other arithmetic  11.6 us (6%)
    ppermute x15, waiting for transfers between devices, cross(): return lax.ppermute(value, DP, pairs)  40 us
    all_to_all x2, waiting for transfers between devices, exchange(): lax.all_to_all(blocks, DP, split_axis=0, concat_axis=0, tiled=True)  21.5 us
    ppermute x12, starting transfers between devices, shift(): lax.ppermute(value, axis, [(i, (i + step) % size) for i in range(size)])  18.9 us
    ppermute x15, starting transfers between devices, cross(): return lax.ppermute(value, DP, pairs)  18.6 us
    ppermute x12, waiting for transfers between devices, shift(): lax.ppermute(value, axis, [(i, (i + step) % size) for i in range(size)])  18.3 us
    dot_general x4, matrix products, part(): lax.dot_general(pick(proj, (z + step) % NZ), context, (((1,), (1,)), ((),...  13.1 us
    all_to_all x2, starting transfers between devices, exchange(): lax.all_to_all(blocks, DP, split_axis=0, concat_axis=0, tiled=True)  10.8 us
    dot_general x3, matrix products, context_part(): lax.dot_general(chunk, pick(proj, (z + step) % NZ), (((0,), (0,)), ((), (...  10 us
  transfers between devices with their start and end apart: 30, of which 16 were waited for; matrix products, arithmetic and copies ran while one was open for 21% of the time, Pallas kernels for 0%

profile of v3, /device:TPU:1, one launch (start us, length us, event | category | flops | bytes accessed | tf_op | source)
XLA Modules:
  0.0 200.8 jit_solution(10777127938986055345)
XLA Ops:
  0.7 3.2 %fusion.36 = bf16[1280,256]{1,0:T(8,128)(2,1)S(1)} fusion(bf16[256,1280]{1,0:T(8,128)(2,1)} %param.9, bf16[4,1280,1280]{2,1,0:T(8,128)(2,1)} %bitcast.110, s32[]{:T(128)S(6)} %select_n.226), kind=kOutput, calls=%fused_computation.41 | convolution fusion | flops 839188480 | bytes 4587524 | tf_op jit(solution)/shard_map/dot_general | solution.py:77
  4.7 2.5 %collective-permute-start = (bf16[640,256]{1,0:T(8,128)(2,1)}, bf16[640,256]{1,0:T(8,128)(2,1)}, u32[]{:S(2)}, u32[]{:S(2)}) collective-permute-start(bf16[640,256]{1,0:T(8,128)(2,1)} %get-tuple-element.65), channel_id=1, source_target_pairs={{0,1},{1,2},{2,3},{3,0},{4,5},{5,6},{6,7},{7,4},{8,9},{9,10},{10,1... | collective-permute-start | bytes 983048 | tf_op jit(solution)/shard_map/ppermute | solution.py:19
  7.2 2.1 %collective-permute-start.1 = (bf16[640,256]{1,0:T(8,128)(2,1)}, bf16[640,256]{1,0:T(8,128)(2,1)}, u32[]{:S(2)}, u32[]{:S(2)}) collective-permute-start(bf16[640,256]{1,0:T(8,128)(2,1)} %get-tuple-element.64), channel_id=1, source_target_pairs={{0,3},{1,0},{2,1},{3,2},{4,7},{5,4},{6,5},{7,6},{8,11},{9,8},{10,9... | collective-permute-start | bytes 983048 | tf_op jit(solution)/shard_map/ppermute | solution.py:19
  9.3 3.0 %fusion.14 = f32[1280,256]{1,0:T(8,128)S(1)} fusion(bf16[256,1280]{1,0:T(8,128)(2,1)S(1)} %copy-done.9, bf16[4,1280,1280]{2,1,0:T(8,128)(2,1)} %bitcast.111, s32[]{:T(128)S(6)} %select_n.224), kind=kOutput, calls=%fused_computation.17 | convolution fusion | flops 838860800 | bytes 5242884 | tf_op jit(solution)/shard_map/dot_general | solution.py:77
  12.3 3.4 %fusion.6 = f32[1280,256]{1,0:T(8,128)S(1)} fusion(bf16[256,1280]{1,0:T(8,128)(2,1)S(1)} %copy-done.9, bf16[4,1280,1280]{2,1,0:T(8,128)(2,1)} %bitcast.112, s32[]{:T(128)S(6)} %select_n.228), kind=kOutput, calls=%fused_computation.9 | convolution fusion | flops 838860800 | bytes 5242884 | tf_op jit(solution)/shard_map/dot_general | solution.py:77
  15.9 3.5 %fusion.2 = f32[1280,256]{1,0:T(8,128)S(1)} fusion(bf16[256,1280]{1,0:T(8,128)(2,1)} %param.9, bf16[4,1280,1280]{2,1,0:T(8,128)(2,1)} %bitcast.113, s32[]{:T(128)S(6)} %select_n.230), kind=kOutput, calls=%fused_computation.5 | convolution fusion | flops 838860800 | bytes 5242884 | tf_op jit(solution)/shard_map/dot_general | solution.py:77
  23.5 1.5 collective-permute-start.3
  25.7 8.6 %all-to-all-start = ((f32[32,1,8]{2,1,0:T(1,128)}), f32[32,1,8]{2,1,0:T(1,128)S(1)}, u32[]{:S(2)}, u32[]{:S(2)}) async-start(f32[32,1,8]{2,1,0:T(1,128)} %broadcast_in_dim.17), calls=%async_computation | async-start | bytes 32768 | tf_op jit(solution)/shard_map/all_to_all | solution.py:39
  34.3 1.5 collective-permute-start.4
  35.8 1.3 collective-permute-start.5
  37.1 1.3 collective-permute-start.6
  38.7 1.3 copy.18
  40.0 1.2 all-to-all-done
  41.7 1.3 convert_add_fusion
  43.0 5.9 %collective-permute-done.4 = bf16[256,1280]{1,0:T(8,128)(2,1)} collective-permute-done((bf16[256,1280]{1,0:T(8,128)(2,1)}, bf16[256,1280]{1,0:T(8,128)(2,1)}, u32[]{:S(2)}, u32[]{:S(2)}) %collective-permute-start.4) | collective-permute-done | bytes 655392 | tf_op jit(solution)/shard_map/ppermute | solution.py:34
  48.9 4.3 %collective-permute-done.6 = bf16[256,1280]{1,0:T(8,128)(2,1)} collective-permute-done((bf16[256,1280]{1,0:T(8,128)(2,1)}, bf16[256,1280]{1,0:T(8,128)(2,1)}, u32[]{:S(2)}, u32[]{:S(2)}) %collective-permute-start.6) | collective-permute-done | bytes 655392 | tf_op jit(solution)/shard_map/ppermute | solution.py:34
  53.6 3.0 %collective-permute-start.9 = (f32[2,256]{1,0:T(2,128)S(1)}, f32[2,256]{1,0:T(2,128)S(1)}, u32[]{:S(2)}, u32[]{:S(2)}) collective-permute-start(f32[2,256]{1,0:T(2,128)S(1)} %pad_maximum_fusion.6), channel_id=1, source_target_pairs={{0,3},{1,0},{2,1},{3,2},{4,7},{5,4},{6,5},{7,6},{8,11},{9,8},{10,9... | collective-permute-start | bytes 6152 | tf_op jit(solution)/shard_map/ppermute | solution.py:19
  57.3 2.9 %collective-permute-start.10 = (bf16[256,1280]{1,0:T(8,128)(2,1)S(1)}, bf16[256,1280]{1,0:T(8,128)(2,1)S(1)}, u32[]{:S(2)}, u32[]{:S(2)}) collective-permute-start(bf16[256,1280]{1,0:T(8,128)(2,1)S(1)} %copy-done.10), channel_id=1, source_target_pairs={{0,16},{4,68},{8,24},{12,76},{16,0},{20,84},{24,8},{28,92},{32,48}... | collective-permute-start | bytes 1966088 | tf_op jit(solution)/shard_map/ppermute | solution.py:34
  60.3 1.5 collective-permute-start.11
  63.1 8.8 %collective-permute-done.10 = bf16[256,1280]{1,0:T(8,128)(2,1)S(1)} collective-permute-done((bf16[256,1280]{1,0:T(8,128)(2,1)S(1)}, bf16[256,1280]{1,0:T(8,128)(2,1)S(1)}, u32[]{:S(2)}, u32[]{:S(2)}) %collective-permute-start.10) | collective-permute-done | bytes 655392 | tf_op jit(solution)/shard_map/ppermute | solution.py:34
  71.9 4.4 %collective-permute-done.11 = bf16[256,1280]{1,0:T(8,128)(2,1)S(1)} collective-permute-done((bf16[256,1280]{1,0:T(8,128)(2,1)S(1)}, bf16[256,1280]{1,0:T(8,128)(2,1)S(1)}, u32[]{:S(2)}, u32[]{:S(2)}) %collective-permute-start.11) | collective-permute-done | bytes 655392 | tf_op jit(solution)/shard_map/ppermute | solution.py:34
  76.3 7.2 %collective-permute-done.12 = bf16[256,1280]{1,0:T(8,128)(2,1)S(1)} collective-permute-done((bf16[256,1280]{1,0:T(8,128)(2,1)S(1)}, bf16[256,1280]{1,0:T(8,128)(2,1)S(1)}, u32[]{:S(2)}, u32[]{:S(2)}) %collective-permute-start.12) | collective-permute-done | bytes 655392 | tf_op jit(solution)/shard_map/ppermute | solution.py:34
  84.4 2.3 %collective-permute-start.13 = (bf16[1280,256]{1,0:T(8,128)(2,1)S(1)}, bf16[1280,256]{1,0:T(8,128)(2,1)S(1)}, u32[]{:S(2)}, u32[]{:S(2)}) collective-permute-start(bf16[1280,256]{1,0:T(8,128)(2,1)S(1)} %fusion.55), channel_id=1, source_target_pairs={{0,1},{1,2},{2,3},{3,0},{4,5},{5,6},{6,7},{7,4},{8,9},{9,10},{10,1... | collective-permute-start | bytes 1966088 | tf_op jit(solution)/shard_map/ppermute | solution.py:19
  87.1 3.0 %fusion = f32[256,1280]{1,0:T(8,128)S(1)} fusion(bf16[1280,256]{1,0:T(8,128)(2,1)S(1)} %fusion.55, bf16[4,1280,1280]{2,1,0:T(8,128)(2,1)} %bitcast.114, s32[]{:T(128)S(6)} %select_n.230), kind=kOutput, calls=%fused_computation.3 | convolution fusion | flops 838860800 | bytes 5242884 | tf_op jit(solution)/shard_map/dot_general | solution.py:116
  90.0 12.1 %collective-permute-done.13 = bf16[1280,256]{1,0:T(8,128)(2,1)S(1)} collective-permute-done((bf16[1280,256]{1,0:T(8,128)(2,1)S(1)}, bf16[1280,256]{1,0:T(8,128)(2,1)S(1)}, u32[]{:S(2)}, u32[]{:S(2)}) %collective-permute-start.13) | collective-permute-done | bytes 655392 | tf_op jit(solution)/shard_map/ppermute | solution.py:19
  103.2 3.0 %fusion.12 = f32[256,1280]{1,0:T(8,128)S(1)} fusion(bf16[1280,256]{1,0:T(8,128)(2,1)S(1)} %collective-permute-done.14, bf16[4,1280,1280]{2,1,0:T(8,128)(2,1)} %bitcast.115, s32[]{:T(128)S(6)} %select_n.224), kind=kOutput, calls=%fused_computation.15 | convolution fusion | flops 838860800 | bytes 5242884 | tf_op jit(solution)/shard_map/dot_general | solution.py:116
  106.2 1.5 collective-permute-start.16
  107.8 4.1 %add_add_fusion = f32[256,1280]{1,0:T(8,128)} fusion(f32[256,1280]{1,0:T(8,128)S(1)} %fusion, f32[256,1280]{1,0:T(8,128)S(1)} %fusion.12, bf16[1280,256]{1,0:T(8,128)(2,1)S(1)} %collective-permute-done.13, bf16[4,1280,1280]{2,1,0:T(8,128)(2,1)} %bitcast.116, s32[]{:T(128)S(6)} %select_n.228), kind=kOutput, calls=%fused_computation.63 | convolution fusion | flops 839516160 | bytes 7864324 | tf_op jit(solution)/shard_map/dot_general | solution.py:116
  111.9 3.0 %collective-permute-done.16 = bf16[640,256]{1,0:T(8,128)(2,1)S(1)} collective-permute-done((bf16[640,256]{1,0:T(8,128)(2,1)S(1)}, bf16[640,256]{1,0:T(8,128)(2,1)S(1)}, u32[]{:S(2)}, u32[]{:S(2)}) %collective-permute-start.16) | collective-permute-done | bytes 327712 | tf_op jit(solution)/shard_map/ppermute | solution.py:19
  114.9 2.2 %collective-permute-done.15 = bf16[640,256]{1,0:T(8,128)(2,1)S(1)} collective-permute-done((bf16[640,256]{1,0:T(8,128)(2,1)S(1)}, bf16[640,256]{1,0:T(8,128)(2,1)S(1)}, u32[]{:S(2)}, u32[]{:S(2)}) %collective-permute-start.15) | collective-permute-done | bytes 327712 | tf_op jit(solution)/shard_map/ppermute | solution.py:19
  121.6 2.7 %collective-permute-done.22 = bf16[640,256]{1,0:T(8,128)(2,1)S(1)} collective-permute-done((bf16[640,256]{1,0:T(8,128)(2,1)S(1)}, bf16[640,256]{1,0:T(8,128)(2,1)S(1)}, u32[]{:S(2)}, u32[]{:S(2)}) %collective-permute-start.22) | collective-permute-done | bytes 327712 | tf_op jit(solution)/shard_map/ppermute | solution.py:34
  124.3 1.7 collective-permute-done.21
  126.0 3.7 %collective-permute-done.20 = bf16[640,256]{1,0:T(8,128)(2,1)S(1)} collective-permute-done((bf16[640,256]{1,0:T(8,128)(2,1)S(1)}, bf16[640,256]{1,0:T(8,128)(2,1)S(1)}, u32[]{:S(2)}, u32[]{:S(2)}) %collective-permute-start.20) | collective-permute-done | bytes 327712 | tf_op jit(solution)/shard_map/ppermute | solution.py:34
  129.7 4.3 %convolution_convert_fusion = bf16[640,1280]{1,0:T(8,128)(2,1)} fusion(bf16[256,1280]{1,0:T(8,128)(2,1)S(1)} %copy-done.11, bf16[256,1280]{1,0:T(8,128)(2,1)} %collective-permute-done.5, bf16[256,1280]{1,0:T(8,128)(2,1)S(1)} %copy-done.15, bf16[256,1280]{1,0:T(8,128)(2,1)} %collective-permute-done.4, bf16[640,256]{1,0:T(8,128)(2,1)S(1)} %collective-permute-done.22, ...), kind=kOutput, calls=%fused_computation.19 | convolution fusion | flops 1694269440 | bytes 5570560 | tf_op jit(solution)/shard_map/dot_general | solution.py:146
  134.0 4.8 %collective-permute-start.23 = (bf16[640,1280]{1,0:T(8,128)(2,1)}, bf16[640,1280]{1,0:T(8,128)(2,1)}, u32[]{:S(2)}, u32[]{:S(2)}) collective-permute-start(bf16[640,1280]{1,0:T(8,128)(2,1)} %convolution_convert_fusion), channel_id=1, source_target_pairs={{0,4},{4,0},{1,5},{5,1},{2,6},{6,2},{3,7},{7,3},{8,12},{12,8},{9,1... | collective-permute-start | bytes 4915208 | tf_op jit(solution)/shard_map/ppermute | solution.py:19
  139.5 1.2 reshape.127
  140.7 4.1 %all-to-all-start.2 = ((bf16[32,12,1280]{2,1,0:T(8,128)(2,1)}), bf16[32,12,1280]{2,1,0:T(8,128)(2,1)S(1)}, u32[]{:S(2)}, u32[]{:S(2)}) async-start(bf16[32,12,1280]{2,1,0:T(8,128)(2,1)} %reshape.127), calls=%async_computation.2 | async-start | bytes 2621440 | tf_op jit(solution)/shard_map/all_to_all | solution.py:55
  144.8 2.7 %collective-permute-start.19 = (bf16[640,256]{1,0:T(8,128)(2,1)S(1)}, bf16[640,256]{1,0:T(8,128)(2,1)}, u32[]{:S(2)}, u32[]{:S(2)}) collective-permute-start(bf16[640,256]{1,0:T(8,128)(2,1)S(1)} %get-tuple-element.62), channel_id=1, source_target_pairs={{0,96},{4,28},{8,104},{12,4},{16,112},{20,12},{24,120},{28,20},{32... | collective-permute-start | bytes 983048 | tf_op jit(solution)/shard_map/ppermute | solution.py:34
  148.7 4.9 %convolution_convert_fusion.2 = bf16[384,1280]{1,0:T(8,128)(2,1)} fusion(f32[256,1280]{1,0:T(8,128)} %add_add_fusion, bf16[1280,256]{1,0:T(8,128)(2,1)S(1)} %pad_maximum_fusion.5, bf16[4,1280,1280]{2,1,0:T(8,128)(2,1)} %bitcast.117, s32[]{:T(128)S(6)} %select_n.226, s32[256]{0:T(256)S(1)} %add.231), kind=kOutput, calls=%fused_computation.29 | convolution fusion | flops 1091764224 | bytes 6226948 | tf_op jit(solution)/shard_map/dot_general | solution.py:165
  153.5 2.2 %reshape.125 = bf16[32,12,1280]{2,1,0:T(8,128)(2,1)} reshape(bf16[384,1280]{1,0:T(8,128)(2,1)} %convolution_convert_fusion.2) | data formatting | bytes 1966080 | tf_op jit(solution)/shard_map/reshape | solution.py:54
  155.7 8.9 %all-to-all-done.2 = bf16[32,12,1280]{2,1,0:T(8,128)(2,1)S(1)} async-done(((bf16[32,12,1280]{2,1,0:T(8,128)(2,1)}), bf16[32,12,1280]{2,1,0:T(8,128)(2,1)S(1)}, u32[]{:S(2)}, u32[]{:S(2)}) %all-to-all-start.2) | async-done | bytes 983072 | tf_op jit(solution)/shard_map/all_to_all | solution.py:55
  164.6 6.7 %all-to-all-start.1 = ((bf16[32,12,1280]{2,1,0:T(8,128)(2,1)}), bf16[32,12,1280]{2,1,0:T(8,128)(2,1)S(1)}, u32[]{:S(2)}, u32[]{:S(2)}) async-start(bf16[32,12,1280]{2,1,0:T(8,128)(2,1)} %reshape.125), calls=%async_computation.1 | async-start | bytes 2621440 | tf_op jit(solution)/shard_map/all_to_all | solution.py:55
  171.4 4.5 %convolution_add_fusion = f32[640,1280]{1,0:T(8,128)S(1)} fusion(bf16[640,1280]{1,0:T(8,128)(2,1)} %collective-permute-done.23, bf16[256,1280]{1,0:T(8,128)(2,1)} %param.9, bf16[256,1280]{1,0:T(8,128)(2,1)} %copy-done.13, bf16[256,1280]{1,0:T(8,128)(2,1)} %copy-done.12, bf16[256,1280]{1,0:T(8,128)(2,1)} %collective-permute-done.6, ...), kind=kOutput, calls=%fused_computation | convolution fusion | flops 1695088640 | bytes 8847360 | tf_op jit(solution)/shard_map/dot_general | solution.py:146
  175.9 1.6 copy-done
  178.6 2.6 %collective-permute-start.26 = (bf16[160,1280]{1,0:T(8,128)(2,1)}, bf16[160,1280]{1,0:T(8,128)(2,1)S(1)}, u32[]{:S(2)}, u32[]{:S(2)}) collective-permute-start(bf16[160,1280]{1,0:T(8,128)(2,1)} %get-tuple-element.44), channel_id=1, source_target_pairs={{0,24},{4,100},{8,0},{12,108},{16,8},{20,116},{24,16},{28,124},{32... | collective-permute-start | bytes 1228808 | tf_op jit(solution)/shard_map/ppermute | solution.py:34
  183.4 12.6 %all-to-all-done.1 = bf16[32,12,1280]{2,1,0:T(8,128)(2,1)S(1)} async-done(((bf16[32,12,1280]{2,1,0:T(8,128)(2,1)}), bf16[32,12,1280]{2,1,0:T(8,128)(2,1)S(1)}, u32[]{:S(2)}, u32[]{:S(2)}) %all-to-all-start.1) | async-done | bytes 983072 | tf_op jit(solution)/shard_map/all_to_all | solution.py:55
  197.0 1.2 collective-permute-done.24
  198.3 2.5 %fusion.58 = f32[160,1280]{1,0:T(8,128)} fusion(bf16[160,1280]{1,0:T(8,128)(2,1)S(1)} %collective-permute-done.26, bf16[160,1280]{1,0:T(8,128)(2,1)} %collective-permute-done.25, bf16[160,1280]{1,0:T(8,128)(2,1)} %collective-permute-done.24, f32[4,160,1280]{2,1,0:T(8,128)} %bitcast.109, s32[]{:T(128)S(6)} %select_n.259), kind=kLoop, calls=%fused_computation.70 | loop fusion | flops 1433600 | bytes 2867204 | tf_op jit(solution)/shard_map/div | solution.py:162
  (102 shorter events, 21.8 us)
Async XLA Ops:
  0.6 8.7 %copy-start.9 = (bf16[256,1280]{1,0:T(8,128)(2,1)S(1)}, bf16[256,1280]{1,0:T(8,128)(2,1)}, u32[]{:S(2)}) copy-start(bf16[256,1280]{1,0:T(8,128)(2,1)} %param.9) | copy-start | bytes 1966084
  4.7 14.7 %collective-permute-start = (bf16[640,256]{1,0:T(8,128)(2,1)}, bf16[640,256]{1,0:T(8,128)(2,1)}, u32[]{:S(2)}, u32[]{:S(2)}) collective-permute-start(bf16[640,256]{1,0:T(8,128)(2,1)} %get-tuple-element.65), channel_id=1, source_target_pairs={{0,1},{1,2},{2,3},{3,0},{4,5},{5,6},{6,7},{7,4},{8,9},{9,10},{10,1... | collective-permute-start | bytes 983048 | tf_op jit(solution)/shard_map/ppermute | solution.py:19
  7.2 14.4 %collective-permute-start.1 = (bf16[640,256]{1,0:T(8,128)(2,1)}, bf16[640,256]{1,0:T(8,128)(2,1)}, u32[]{:S(2)}, u32[]{:S(2)}) collective-permute-start(bf16[640,256]{1,0:T(8,128)(2,1)} %get-tuple-element.64), channel_id=1, source_target_pairs={{0,3},{1,0},{2,1},{3,2},{4,7},{5,4},{6,5},{7,6},{8,11},{9,8},{10,9... | collective-permute-start | bytes 983048 | tf_op jit(solution)/shard_map/ppermute | solution.py:19
  12.3 3.5 %copy-start.3 = (f32[1280,256]{1,0:T(8,128)}, f32[1280,256]{1,0:T(8,128)S(1)}, u32[]{:S(2)}) copy-start(f32[1280,256]{1,0:T(8,128)S(1)} %fusion.14) | copy-start | bytes 3932164
  15.8 3.7 %copy-start.1 = (f32[1280,256]{1,0:T(8,128)}, f32[1280,256]{1,0:T(8,128)S(1)}, u32[]{:S(2)}) copy-start(f32[1280,256]{1,0:T(8,128)S(1)} %fusion.6) | copy-start | bytes 3932164
  15.9 3.6 %copy-start.4 = (f32[1280,256]{1,0:T(8,128)S(1)}, f32[1280,256]{1,0:T(8,128)}, u32[]{:S(2)}) copy-start(f32[1280,256]{1,0:T(8,128)} %copy-done.3) | copy-start | bytes 3932164
  19.4 5.6 %copy-start.8 = (f32[4]{0:T(128)S(1)}, f32[4]{0:T(128)}, u32[]{:S(2)}) copy-start(f32[4]{0:T(128)} %param.14) | copy-start | bytes 52
  19.4 5.5 %copy-start.16 = (s32[4]{0:T(128)S(1)}, s32[4]{0:T(128)}, u32[]{:S(2)}) copy-start(s32[4]{0:T(128)} %param.15) | copy-start | bytes 52
  19.5 2.1 %copy-start.2 = (f32[1280,256]{1,0:T(8,128)S(1)}, f32[1280,256]{1,0:T(8,128)}, u32[]{:S(2)}) copy-start(f32[1280,256]{1,0:T(8,128)} %copy-done.1) | copy-start | bytes 3932164
  19.5 19.0 %copy-start.5 = (bf16[256,1280]{1,0:T(8,128)(2,1)S(1)}, bf16[256,1280]{1,0:T(8,128)(2,1)}, u32[]{:S(2)}) copy-start(bf16[256,1280]{1,0:T(8,128)(2,1)} %param.11) | copy-start | bytes 1966084
  21.6 19.9 %copy-start.7 = (s32[4]{0:T(128)S(1)}, s32[4]{0:T(128)}, u32[]{:S(2)}) copy-start(s32[4]{0:T(128)} %param.16) | copy-start | bytes 52
  23.5 18.2 %collective-permute-start.3 = (bf16[1280,256]{1,0:T(8,128)(2,1)}, bf16[1280,256]{1,0:T(8,128)(2,1)S(1)}, u32[]{:S(2)}, u32[]{:S(2)}) collective-permute-start(bf16[1280,256]{1,0:T(8,128)(2,1)} %pad_maximum_fusion.4), channel_id=1, source_target_pairs={{0,3},{1,0},{2,1},{3,2},{4,7},{5,4},{6,5},{7,6},{8,11},{9,8},{10,9... | collective-permute-start | bytes 1966088 | tf_op jit(solution)/shard_map/ppermute | solution.py:19
  25.0 16.7 %collective-permute-start.2 = (bf16[1280,256]{1,0:T(8,128)(2,1)}, bf16[1280,256]{1,0:T(8,128)(2,1)}, u32[]{:S(2)}, u32[]{:S(2)}) collective-permute-start(bf16[1280,256]{1,0:T(8,128)(2,1)} %pad_maximum_fusion.3), channel_id=1, source_target_pairs={{0,1},{1,2},{2,3},{3,0},{4,5},{5,6},{6,7},{7,4},{8,9},{9,10},{10,1... | collective-permute-start | bytes 1966088 | tf_op jit(solution)/shard_map/ppermute | solution.py:19
  25.7 15.6 %all-to-all-start = ((f32[32,1,8]{2,1,0:T(1,128)}), f32[32,1,8]{2,1,0:T(1,128)S(1)}, u32[]{:S(2)}, u32[]{:S(2)}) async-start(f32[32,1,8]{2,1,0:T(1,128)} %broadcast_in_dim.17), calls=%async_computation | async-start | bytes 32768 | tf_op jit(solution)/shard_map/all_to_all | solution.py:39
  34.3 14.6 %collective-permute-start.4 = (bf16[256,1280]{1,0:T(8,128)(2,1)}, bf16[256,1280]{1,0:T(8,128)(2,1)}, u32[]{:S(2)}, u32[]{:S(2)}) collective-permute-start(bf16[256,1280]{1,0:T(8,128)(2,1)} %param.9), channel_id=1, source_target_pairs={{0,8},{4,36},{8,16},{12,44},{16,24},{20,52},{24,0},{28,60},{32,40}... | collective-permute-start | bytes 1966088 | tf_op jit(solution)/shard_map/ppermute | solution.py:34
  35.8 13.1 %collective-permute-start.5 = (bf16[256,1280]{1,0:T(8,128)(2,1)}, bf16[256,1280]{1,0:T(8,128)(2,1)}, u32[]{:S(2)}, u32[]{:S(2)}) collective-permute-start(bf16[256,1280]{1,0:T(8,128)(2,1)} %param.9), channel_id=1, source_target_pairs={{0,24},{4,100},{8,0},{12,108},{16,8},{20,116},{24,16},{28,124},{32... | collective-permute-start | bytes 1966088 | tf_op jit(solution)/shard_map/ppermute | solution.py:34
  37.1 16.1 %collective-permute-start.6 = (bf16[256,1280]{1,0:T(8,128)(2,1)}, bf16[256,1280]{1,0:T(8,128)(2,1)}, u32[]{:S(2)}, u32[]{:S(2)}) collective-permute-start(bf16[256,1280]{1,0:T(8,128)(2,1)} %param.9), channel_id=1, source_target_pairs={{0,32},{4,12},{8,40},{12,20},{16,48},{20,28},{24,56},{28,4},{32,64... | collective-permute-start | bytes 1966088 | tf_op jit(solution)/shard_map/ppermute | solution.py:34
  38.7 14.5 %copy-start.6 = (f32[1280]{0:T(1024)S(1)}, f32[1280]{0:T(1024)}, u32[]{:S(2)}) copy-start(f32[1280]{0:T(1024)} %param.13) | copy-start | bytes 15364
  41.7 15.7 %copy-start.10 = (bf16[256,1280]{1,0:T(8,128)(2,1)S(1)}, bf16[256,1280]{1,0:T(8,128)(2,1)}, u32[]{:S(2)}) copy-start(bf16[256,1280]{1,0:T(8,128)(2,1)} %param.9) | copy-start | bytes 1966084
  53.6 8.1 %collective-permute-start.9 = (f32[2,256]{1,0:T(2,128)S(1)}, f32[2,256]{1,0:T(2,128)S(1)}, u32[]{:S(2)}, u32[]{:S(2)}) collective-permute-start(f32[2,256]{1,0:T(2,128)S(1)} %pad_maximum_fusion.6), channel_id=1, source_target_pairs={{0,3},{1,0},{2,1},{3,2},{4,7},{5,4},{6,5},{7,6},{8,11},{9,8},{10,9... | collective-permute-start | bytes 6152 | tf_op jit(solution)/shard_map/ppermute | solution.py:19
  56.7 6.0 %collective-permute-start.8 = (f32[2,256]{1,0:T(2,128)S(1)}, f32[2,256]{1,0:T(2,128)S(1)}, u32[]{:S(2)}, u32[]{:S(2)}) collective-permute-start(f32[2,256]{1,0:T(2,128)S(1)} %pad_maximum_fusion.6), channel_id=1, source_target_pairs={{0,2},{1,3},{2,0},{3,1},{4,6},{5,7},{6,4},{7,5},{8,10},{9,11},{10,... | collective-permute-start | bytes 6152 | tf_op jit(solution)/shard_map/ppermute | solution.py:19
  56.7 6.0 %collective-permute-start.7 = (f32[2,256]{1,0:T(2,128)S(1)}, f32[2,256]{1,0:T(2,128)S(1)}, u32[]{:S(2)}, u32[]{:S(2)}) collective-permute-start(f32[2,256]{1,0:T(2,128)S(1)} %pad_maximum_fusion.6), channel_id=1, source_target_pairs={{0,1},{1,2},{2,3},{3,0},{4,5},{5,6},{6,7},{7,4},{8,9},{9,10},{10,1... | collective-permute-start | bytes 6152 | tf_op jit(solution)/shard_map/ppermute | solution.py:19
  57.3 14.6 %collective-permute-start.10 = (bf16[256,1280]{1,0:T(8,128)(2,1)S(1)}, bf16[256,1280]{1,0:T(8,128)(2,1)S(1)}, u32[]{:S(2)}, u32[]{:S(2)}) collective-permute-start(bf16[256,1280]{1,0:T(8,128)(2,1)S(1)} %copy-done.10), channel_id=1, source_target_pairs={{0,16},{4,68},{8,24},{12,76},{16,0},{20,84},{24,8},{28,92},{32,48}... | collective-permute-start | bytes 1966088 | tf_op jit(solution)/shard_map/ppermute | solution.py:34
  60.3 16.0 %collective-permute-start.11 = (bf16[256,1280]{1,0:T(8,128)(2,1)S(1)}, bf16[256,1280]{1,0:T(8,128)(2,1)S(1)}, u32[]{:S(2)}, u32[]{:S(2)}) collective-permute-start(bf16[256,1280]{1,0:T(8,128)(2,1)S(1)} %copy-done.10), channel_id=1, source_target_pairs={{0,64},{4,20},{8,72},{12,28},{16,80},{20,4},{24,88},{28,12},{32,96... | collective-permute-start | bytes 1966088 | tf_op jit(solution)/shard_map/ppermute | solution.py:34
  61.7 21.8 %collective-permute-start.12 = (bf16[256,1280]{1,0:T(8,128)(2,1)S(1)}, bf16[256,1280]{1,0:T(8,128)(2,1)S(1)}, u32[]{:S(2)}, u32[]{:S(2)}) collective-permute-start(bf16[256,1280]{1,0:T(8,128)(2,1)S(1)} %copy-done.10), channel_id=1, source_target_pairs={{0,96},{4,28},{8,104},{12,4},{16,112},{20,12},{24,120},{28,20},{32... | collective-permute-start | bytes 1966088 | tf_op jit(solution)/shard_map/ppermute | solution.py:34
  71.9 14.7 %copy-start.14 = (bf16[256,1280]{1,0:T(8,128)(2,1)}, bf16[256,1280]{1,0:T(8,128)(2,1)S(1)}, u32[]{:S(2)}) copy-start(bf16[256,1280]{1,0:T(8,128)(2,1)S(1)} %collective-permute-done.10) | copy-start | bytes 1966084
  76.3 13.7 %copy-start.12 = (bf16[256,1280]{1,0:T(8,128)(2,1)}, bf16[256,1280]{1,0:T(8,128)(2,1)S(1)}, u32[]{:S(2)}) copy-start(bf16[256,1280]{1,0:T(8,128)(2,1)S(1)} %collective-permute-done.11) | copy-start | bytes 1966084
  83.5 0.8 copy-start.13
  84.4 17.7 %collective-permute-start.13 = (bf16[1280,256]{1,0:T(8,128)(2,1)S(1)}, bf16[1280,256]{1,0:T(8,128)(2,1)S(1)}, u32[]{:S(2)}, u32[]{:S(2)}) collective-permute-start(bf16[1280,256]{1,0:T(8,128)(2,1)S(1)} %fusion.55), channel_id=1, source_target_pairs={{0,1},{1,2},{2,3},{3,0},{4,5},{5,6},{6,7},{7,4},{8,9},{9,10},{10,1... | collective-permute-start | bytes 1966088 | tf_op jit(solution)/shard_map/ppermute | solution.py:19
  86.6 16.5 %collective-permute-start.14 = (bf16[1280,256]{1,0:T(8,128)(2,1)S(1)}, bf16[1280,256]{1,0:T(8,128)(2,1)S(1)}, u32[]{:S(2)}, u32[]{:S(2)}) collective-permute-start(bf16[1280,256]{1,0:T(8,128)(2,1)S(1)} %fusion.55), channel_id=1, source_target_pairs={{0,3},{1,0},{2,1},{3,2},{4,7},{5,4},{6,5},{7,6},{8,11},{9,8},{10,9... | collective-permute-start | bytes 1966088 | tf_op jit(solution)/shard_map/ppermute | solution.py:19
  106.2 8.7 %collective-permute-start.16 = (bf16[640,256]{1,0:T(8,128)(2,1)S(1)}, bf16[640,256]{1,0:T(8,128)(2,1)S(1)}, u32[]{:S(2)}, u32[]{:S(2)}) collective-permute-start(bf16[640,256]{1,0:T(8,128)(2,1)S(1)} %slice.61), channel_id=1, source_target_pairs={{0,3},{1,0},{2,1},{3,2},{4,7},{5,4},{6,5},{7,6},{8,11},{9,8},{10,9... | collective-permute-start | bytes 983048 | tf_op jit(solution)/shard_map/ppermute | solution.py:19
  107.7 9.4 %collective-permute-start.15 = (bf16[640,256]{1,0:T(8,128)(2,1)S(1)}, bf16[640,256]{1,0:T(8,128)(2,1)S(1)}, u32[]{:S(2)}, u32[]{:S(2)}) collective-permute-start(bf16[640,256]{1,0:T(8,128)(2,1)S(1)} %slice.60), channel_id=1, source_target_pairs={{0,1},{1,2},{2,3},{3,0},{4,5},{5,6},{6,7},{7,4},{8,9},{9,10},{10,1... | collective-permute-start | bytes 983048 | tf_op jit(solution)/shard_map/ppermute | solution.py:19
  117.8 2.7 %copy-start.17 = (s32[64,1]{0,1:T(1,128)S(1)}, s32[64,1]{0,1:T(1,128)}, u32[]{:S(2)}) copy-start(s32[64,1]{0,1:T(1,128)} %param.17) | copy-start | bytes 772
  117.8 11.8 %copy-start.11 = (bf16[256,1280]{1,0:T(8,128)(2,1)S(1)}, bf16[256,1280]{1,0:T(8,128)(2,1)}, u32[]{:S(2)}) copy-start(bf16[256,1280]{1,0:T(8,128)(2,1)} %param.9) | copy-start | bytes 1966084
  117.9 11.8 %copy-start.15 = (bf16[256,1280]{1,0:T(8,128)(2,1)S(1)}, bf16[256,1280]{1,0:T(8,128)(2,1)}, u32[]{:S(2)}) copy-start(bf16[256,1280]{1,0:T(8,128)(2,1)} %copy-done.14) | copy-start | bytes 1966084
  118.0 6.3 %collective-permute-start.22 = (bf16[640,256]{1,0:T(8,128)(2,1)S(1)}, bf16[640,256]{1,0:T(8,128)(2,1)S(1)}, u32[]{:S(2)}, u32[]{:S(2)}) collective-permute-start(bf16[640,256]{1,0:T(8,128)(2,1)S(1)} %get-tuple-element.63), channel_id=1, source_target_pairs={{0,24},{4,100},{8,0},{12,108},{16,8},{20,116},{24,16},{28,124},{32... | collective-permute-start | bytes 983048 | tf_op jit(solution)/shard_map/ppermute | solution.py:34
  118.4 7.6 %collective-permute-start.21 = (bf16[640,256]{1,0:T(8,128)(2,1)S(1)}, bf16[640,256]{1,0:T(8,128)(2,1)S(1)}, u32[]{:S(2)}, u32[]{:S(2)}) collective-permute-start(bf16[640,256]{1,0:T(8,128)(2,1)S(1)} %get-tuple-element.61), channel_id=1, source_target_pairs={{0,16},{4,68},{8,24},{12,76},{16,0},{20,84},{24,8},{28,92},{32,48}... | collective-permute-start | bytes 983048 | tf_op jit(solution)/shard_map/ppermute | solution.py:34
  119.9 9.8 %collective-permute-start.20 = (bf16[640,256]{1,0:T(8,128)(2,1)S(1)}, bf16[640,256]{1,0:T(8,128)(2,1)S(1)}, u32[]{:S(2)}, u32[]{:S(2)}) collective-permute-start(bf16[640,256]{1,0:T(8,128)(2,1)S(1)} %get-tuple-element.59), channel_id=1, source_target_pairs={{0,8},{4,36},{8,16},{12,44},{16,24},{20,52},{24,0},{28,60},{32,40}... | collective-permute-start | bytes 983048 | tf_op jit(solution)/shard_map/ppermute | solution.py:34
  134.0 37.4 %collective-permute-start.23 = (bf16[640,1280]{1,0:T(8,128)(2,1)}, bf16[640,1280]{1,0:T(8,128)(2,1)}, u32[]{:S(2)}, u32[]{:S(2)}) collective-permute-start(bf16[640,1280]{1,0:T(8,128)(2,1)} %convolution_convert_fusion), channel_id=1, source_target_pairs={{0,4},{4,0},{1,5},{5,1},{2,6},{6,2},{3,7},{7,3},{8,12},{12,8},{9,1... | collective-permute-start | bytes 4915208 | tf_op jit(solution)/shard_map/ppermute | solution.py:19
  140.7 23.9 %all-to-all-start.2 = ((bf16[32,12,1280]{2,1,0:T(8,128)(2,1)}), bf16[32,12,1280]{2,1,0:T(8,128)(2,1)S(1)}, u32[]{:S(2)}, u32[]{:S(2)}) async-start(bf16[32,12,1280]{2,1,0:T(8,128)(2,1)} %reshape.127), calls=%async_computation.2 | async-start | bytes 2621440 | tf_op jit(solution)/shard_map/all_to_all | solution.py:55
  144.8 26.5 %collective-permute-start.19 = (bf16[640,256]{1,0:T(8,128)(2,1)S(1)}, bf16[640,256]{1,0:T(8,128)(2,1)}, u32[]{:S(2)}, u32[]{:S(2)}) collective-permute-start(bf16[640,256]{1,0:T(8,128)(2,1)S(1)} %get-tuple-element.62), channel_id=1, source_target_pairs={{0,96},{4,28},{8,104},{12,4},{16,112},{20,12},{24,120},{28,20},{32... | collective-permute-start | bytes 983048 | tf_op jit(solution)/shard_map/ppermute | solution.py:34
  147.5 23.9 %collective-permute-start.18 = (bf16[640,256]{1,0:T(8,128)(2,1)S(1)}, bf16[640,256]{1,0:T(8,128)(2,1)}, u32[]{:S(2)}, u32[]{:S(2)}) collective-permute-start(bf16[640,256]{1,0:T(8,128)(2,1)S(1)} %get-tuple-element.60), channel_id=1, source_target_pairs={{0,64},{4,20},{8,72},{12,28},{16,80},{20,4},{24,88},{28,12},{32,96... | collective-permute-start | bytes 983048 | tf_op jit(solution)/shard_map/ppermute | solution.py:34
  148.1 23.3 %collective-permute-start.17 = (bf16[640,256]{1,0:T(8,128)(2,1)}, bf16[640,256]{1,0:T(8,128)(2,1)}, u32[]{:S(2)}, u32[]{:S(2)}) collective-permute-start(bf16[640,256]{1,0:T(8,128)(2,1)} %get-tuple-element.58), channel_id=1, source_target_pairs={{0,32},{4,12},{8,40},{12,20},{16,48},{20,28},{24,56},{28,4},{32,64... | collective-permute-start | bytes 983048 | tf_op jit(solution)/shard_map/ppermute | solution.py:34
  164.6 31.3 %all-to-all-start.1 = ((bf16[32,12,1280]{2,1,0:T(8,128)(2,1)}), bf16[32,12,1280]{2,1,0:T(8,128)(2,1)S(1)}, u32[]{:S(2)}, u32[]{:S(2)}) async-start(bf16[32,12,1280]{2,1,0:T(8,128)(2,1)} %reshape.125), calls=%async_computation.1 | async-start | bytes 2621440 | tf_op jit(solution)/shard_map/all_to_all | solution.py:55
  175.9 1.7 copy-start
  178.6 18.4 %collective-permute-start.26 = (bf16[160,1280]{1,0:T(8,128)(2,1)}, bf16[160,1280]{1,0:T(8,128)(2,1)S(1)}, u32[]{:S(2)}, u32[]{:S(2)}) collective-permute-start(bf16[160,1280]{1,0:T(8,128)(2,1)} %get-tuple-element.44), channel_id=1, source_target_pairs={{0,24},{4,100},{8,0},{12,108},{16,8},{20,116},{24,16},{28,124},{32... | collective-permute-start | bytes 1228808 | tf_op jit(solution)/shard_map/ppermute | solution.py:34
  181.2 15.8 %collective-permute-start.25 = (bf16[160,1280]{1,0:T(8,128)(2,1)}, bf16[160,1280]{1,0:T(8,128)(2,1)}, u32[]{:S(2)}, u32[]{:S(2)}) collective-permute-start(bf16[160,1280]{1,0:T(8,128)(2,1)} %get-tuple-element.45), channel_id=1, source_target_pairs={{0,16},{4,68},{8,24},{12,76},{16,0},{20,84},{24,8},{28,92},{32,48}... | collective-permute-start | bytes 1228808 | tf_op jit(solution)/shard_map/ppermute | solution.py:34
  181.8 16.5 %collective-permute-start.24 = (bf16[160,1280]{1,0:T(8,128)(2,1)S(1)}, bf16[160,1280]{1,0:T(8,128)(2,1)}, u32[]{:S(2)}, u32[]{:S(2)}) collective-permute-start(bf16[160,1280]{1,0:T(8,128)(2,1)S(1)} %get-tuple-element.43), channel_id=1, source_target_pairs={{0,8},{4,36},{8,16},{12,44},{16,24},{20,52},{24,0},{28,60},{32,40}... | collective-permute-start | bytes 1228808 | tf_op jit(solution)/shard_map/ppermute | solution.py:34

commit v4 on v3

v4 whole, which is shorter than its diff:
```python
import jax
import jax.numpy as jnp
from jax import lax
from jax.experimental import pallas as pl
from jax.experimental.pallas import tpu as pltpu
from jax.sharding import Mesh
from jax.sharding import PartitionSpec as P

LMAX = 64
GROUP = 16
PAIR = 3
BLOCK_ROWS = 4
EPSILON = 1e-06
NX, NY, NC, NZ = 4, 4, 2, 4
DP = ("x", "y", "c")
F32 = jnp.float32
BF16 = jnp.bfloat16


def shift(value, axis, step):
    size = lax.axis_size(axis)
    return lax.ppermute(value, axis, [(i, (i + step) % size) for i in range(size)])


def pick(values, index):
    return lax.dynamic_index_in_dim(values, index, 0, keepdims=False)


def cross(value, step, first):
    pairs = []
    for x in range(NX):
        for y in range(NY):
            for c in range(NC):
                along_y = (c == 0) == first
                to = (x, (y + step) % NY, c) if along_y else ((x + step) % NX, y, c)
                pairs.append(((x * NY + y) * NC + c, (to[0] * NY + to[1]) * NC + to[2]))
    return lax.ppermute(value, DP, pairs)


def group_sum(value):
    copies = jnp.broadcast_to(value, (NX * NY * NC,) + value.shape)
    return jnp.sum(lax.all_to_all(copies, DP, split_axis=0, concat_axis=0, tiled=True), axis=0)


def slot_matrix(owner_dest, slots, rows, padded):
    count = owner_dest.shape[0]
    per_block = rows // count
    same = owner_dest[:, None] == owner_dest[None, :]
    earlier = jnp.arange(count)[None, :] < jnp.arange(count)[:, None]
    rank = jnp.sum((same & earlier).astype(jnp.int32), axis=1)
    target = owner_dest * padded + rank * per_block
    row_target = jnp.repeat(target, per_block) + jnp.tile(jnp.arange(per_block), count)
    return (jnp.arange(slots // PAIR * padded)[:, None] == row_target[None, :]).astype(BF16)


def exchange(packed, lanes):
    blocks = packed.reshape((lanes, packed.shape[0] // lanes, packed.shape[1]))
    got = lax.all_to_all(blocks, DP, split_axis=0, concat_axis=0, tiled=True)
    kept = PAIR * BLOCK_ROWS
    return got[:, :kept].reshape(lanes * kept, packed.shape[1])


FREE = pl.CostEstimate(flops=0, bytes_accessed=0, transcendentals=0)
PARAMS = pltpu.CompilerParams(vmem_limit_bytes=48 * 1024 * 1024)


def context_product(chunks, places, out_proj, before=None, slots=None):
    width, rows = chunks[0].shape
    count, tile = len(chunks), 640
    dtype = F32 if slots is None else BF16

    def body(which, *refs):
        refs = list(refs)
        out_ref = refs.pop()
        total = sum(
            lax.dot_general(
                refs[i][...], refs[count + i][...], (((0,), (0,)), ((), ())), preferred_element_type=F32
            )
            for i in range(count)
        )
        if before is not None:
            total = total + refs[2 * count][...]
        if slots is not None:
            total = jnp.dot(refs[-1][...], total.astype(BF16), preferred_element_type=F32)
        out_ref[...] = total.astype(dtype)

    in_specs = [pl.BlockSpec((width, rows), lambda n, which: (0, 0)) for _ in chunks]
    in_specs += [
        pl.BlockSpec((width, tile), lambda n, which, i=i: (which[i], n)) for i in range(count)
    ]
    operands = list(chunks) + [out_proj] * count
    out_rows = rows
    if before is not None:
        in_specs.append(pl.BlockSpec((rows, tile), lambda n, which: (0, n)))
        operands.append(before)
    if slots is not None:
        in_specs.append(pl.BlockSpec(slots.shape, lambda n, which: (0, 0)))
        operands.append(slots)
        out_rows = slots.shape[0]
    return pl.pallas_call(
        body,
        out_shape=jax.ShapeDtypeStruct((out_rows, width), dtype),
        grid_spec=pltpu.PrefetchScalarGridSpec(
            num_scalar_prefetch=1,
            grid=(width // tile,),
            in_specs=in_specs,
            out_specs=pl.BlockSpec((out_rows, tile), lambda n, which: (0, n)),
        ),
        cost_estimate=FREE,
        compiler_params=PARAMS,
        name="context_product",
    )(jnp.stack(places), *operands)


def place_rows(slots, grad_t):
    def body(slots_ref, grad_ref, out_ref):
        out_ref[...] = lax.dot_general(
            slots_ref[...], grad_ref[...], (((1,), (1,)), ((), ())), preferred_element_type=F32
        ).astype(BF16)

    return pl.pallas_call(
        body,
        out_shape=jax.ShapeDtypeStruct((slots.shape[0], grad_t.shape[0]), BF16),
        cost_estimate=FREE,
        compiler_params=PARAMS,
        name="place_rows",
    )(slots, grad_t)


def weight_product(pieces, contexts, before=None):
    count, height, tile = len(pieces), pieces[0].shape[0], 640
    rows, width = contexts[0].shape

    def body(*refs):
        total = sum(
            jnp.dot(refs[i][...], refs[count + i][...], preferred_element_type=F32)
            for i in range(count)
        )
        if before is not None:
            total = total + refs[2 * count][...].astype(F32)
        refs[-1][...] = total.astype(BF16)

    in_specs = [pl.BlockSpec((height, rows), lambda n: (0, 0)) for _ in pieces]
    in_specs += [pl.BlockSpec((rows, tile), lambda n: (0, n)) for _ in contexts]
    operands = list(pieces) + list(contexts)
    if before is not None:
        in_specs.append(pl.BlockSpec((height, tile), lambda n: (0, n)))
        operands.append(before)
    return pl.pallas_call(
        body,
        out_shape=jax.ShapeDtypeStruct((height, width), BF16),
        grid=(width // tile,),
        in_specs=in_specs,
        out_specs=pl.BlockSpec((height, tile), lambda n: (0, n)),
        cost_estimate=FREE,
        compiler_params=PARAMS,
        name="weight_product",
    )(*operands)


def per_device(
    context, residual, cotangent, out_proj, norm_gain, rewards, group_ids, lengths, destinations
):
    lanes = NX * NY * NC
    rows, width = residual.shape
    full = width * NZ
    x, y, c, z = (lax.axis_index(axis) for axis in ("x", "y", "c", "z"))

    groups = rewards.shape[0] * lanes // GROUP
    member = (group_ids[:, None] == jnp.arange(groups)[None, :]).astype(F32)
    group_total = group_sum(jnp.sum(member * rewards[:, None], axis=0))
    advantage = rewards - jnp.sum(member * group_total[None, :], axis=1) / GROUP
    scale = advantage * LMAX / (2.0 * lengths.astype(F32))
    live = jnp.arange(LMAX)[None, :] < lengths[:, None]
    row_weights = jnp.where(live, scale[:, None], F32(0.0)).reshape(-1).astype(BF16)

    proj = out_proj.reshape(NZ, width, width)

    def part(step, rows_in):
        return lax.dot_general(
            pick(proj, (z + step) % NZ), rows_in, (((1,), (1,)), ((), ())), preferred_element_type=F32
        )

    far = part(2, context).astype(BF16)
    near = part(1, lax.optimization_barrier((context, far))[0]).astype(BF16)
    back = part(3, lax.optimization_barrier((context, near))[0]).astype(BF16)
    parts = [shift(far, "z", 2), shift(near, "z", 1), shift(back, "z", 3)]

    after, _ = lax.optimization_barrier((context, near))
    others, selves = [context] * 4, [context] * 4
    others[1], others[3] = cross(after, 1, True), cross(after, 3, True)
    after, others[1], others[3] = lax.optimization_barrier((context, others[1], others[3]))
    own = part(0, after)
    others[2], selves[1] = cross(after, 2, True), cross(after, 1, False)
    after, others[2], selves[1] = lax.optimization_barrier((context, others[2], selves[1]))
    selves[2], selves[3] = cross(after, 2, False), cross(after, 3, False)

    attn_t = own + sum(value.astype(F32) for value in parts)
    attn_t, others[2], selves[1] = lax.optimization_barrier((attn_t, others[2], selves[1]))
    hidden_t = residual.T.astype(F32) + attn_t
    upstream_t = norm_gain[:, None] * (row_weights.astype(F32)[None, :] * cotangent.T.astype(F32))
    stats = jnp.stack(
        [jnp.sum(hidden_t * hidden_t, axis=0), jnp.sum(upstream_t * hidden_t, axis=0)]
    )
    stats = stats + shift(stats, "z", 1) + shift(stats, "z", 2) + shift(stats, "z", 3)
    inv_rms = lax.rsqrt(stats[0] / full + EPSILON)
    grad_t = (
        inv_rms[None, :] * upstream_t - hidden_t * (inv_rms**3 * stats[1] / full)[None, :]
    ).astype(BF16)
    grad_t, selves[2], selves[3] = lax.optimization_barrier((grad_t, selves[2], selves[3]))

    slots = slot_matrix(destinations[:, 0], lanes * PAIR, rows, 16)
    top = width // 2
    from_left, from_right = shift(grad_t, "z", 1), shift(grad_t, "z", 3)
    d_residual = exchange(place_rows(slots, grad_t), lanes)
    context_grad = context_product([grad_t], [z], out_proj)
    from_left, from_right, context_grad = lax.optimization_barrier(
        (from_left, from_right, context_grad)
    )
    far_left, far_right = shift(from_left[:top], "z", 1), shift(from_right[top:], "z", 3)
    context_grad = context_product(
        [from_right, from_left], [(z + 1) % NZ, (z + 3) % NZ], out_proj, before=context_grad
    )
    far_left, far_right, context_grad, d_residual = lax.optimization_barrier(
        (far_left, far_right, context_grad, d_residual)
    )
    far_grad = jnp.concatenate([far_left, far_right], axis=0)

    block = width // (NY * NC)
    grad_full = jnp.stack([grad_t, from_right, far_grad, from_left]).reshape(NZ, NY, NC, block, rows)

    def set_rows(step, first):
        along_x = pick(grad_full[:, :, 0], (x + step - z) % NZ)
        along_y = lax.dynamic_index_in_dim(grad_full[:, :, 1], (y + step) % NY, 1, keepdims=False)
        return jnp.where((c == 0) == first, along_y, along_x).reshape(-1, rows)

    def gather(first):
        return [set_rows(0, first)] + [cross(set_rows(k, first), k, first) for k in (1, 2, 3)]

    other_rows, self_rows = gather(True), gather(False)
    d_context = exchange(
        context_product([far_grad], [(z + 2) % NZ], out_proj, before=context_grad, slots=slots), lanes
    )
    other = shift(weight_product(other_rows, others), "c", 1)
    total = weight_product(self_rows, selves, before=other).reshape(4, block, width)

    def place(step):
        return pick(total, jnp.where(c == 0, (y + step) % NY, (x + step - z) % NZ))

    d_out_proj = place(0).astype(F32)
    for k in (1, 2, 3):
        d_out_proj = d_out_proj + cross(place(k), k, True).astype(F32)
    return (d_context, d_residual, d_out_proj / lanes)


def solution(mesh):
    wide = Mesh(mesh.devices.reshape(NX, NY, NC, NZ), DP + ("z",))
    placed = (
        P(DP, "z"),
        P(DP, "z"),
        P(DP, "z"),
        P(None, "z"),
        P("z"),
        P(DP),
        P(DP),
        P(DP),
        P(DP, None),
    )
    return jax.shard_map(
        per_device,
        mesh=wide,
        in_specs=placed,
        out_specs=(P(DP, "z"), P(DP, "z"), P(DP, "z")),
        check_vma=False,
    )
```

time: 201 us -> 207 us (1.030)
  matrix products: 37.3 us -> 15.3 us
  Pallas kernels: 0 us -> 21.4 us
  local copies, waits for them, and re-layouts: 12.9 us -> 23.4 us
  other arithmetic: 11.6 us -> 7.53 us
  waiting for transfers between devices: 81 us -> 77.7 us
  starting transfers between devices: 56.9 us -> 59.7 us
    dot_general x11 -> x4, matrix products: 37.3 us -> 15.3 us  [part(): lax.dot_general(pick(proj, (z + step) % NZ), rows_in, (((1,), (1,)), ((),...]
    all_to_all x2, waiting for transfers between devices: 21.5 us -> 0.01 us  [exchange(): got = lax.all_to_all(blocks, DP, split_axis=0, concat_axis=0, tiled=True)]
    pallas_call x0 -> x6, Pallas kernels: none -> 21.4 us  [the longest x3 12.4 us: context_product(): pl.pallas_call(body, out_shape=jax.ShapeDtypeStruct((out_rows, width), dt...]
    ppermute x15, waiting for transfers between devices: 40 us -> 54.4 us  [cross(): return lax.ppermute(value, DP, pairs)]
    unnamed x38 -> x77, local copies, waits for them, and re-layouts: 4.13 us -> 15.1 us
    all_to_all x2, starting transfers between devices: 10.8 us -> 16 us  [exchange(): got = lax.all_to_all(blocks, DP, split_axis=0, concat_axis=0, tiled=True)]
    all_to_all x1, waiting for transfers between devices: 1.23 us -> 4.12 us  [group_sum(): lax.all_to_all(copies, DP, split_axis=0, concat_axis=0, tiled=True)]
    ppermute x12 -> x11, starting transfers between devices: 18.9 us -> 16.5 us  [shift(): lax.ppermute(value, axis, [(i, (i + step) % size) for i in range(size)])]
  transfers between devices with their start and end apart: 30 -> 29, of which waited for: 16 -> 16; matrix products, arithmetic and copies ran while one was open for 21% -> 10% of each run, Pallas kernels for 0% -> 8%
where the time goes in v4:
time: 207 us; the launch traced here: 206 us
  waiting for transfers between devices  77.7 us (38%)
  starting transfers between devices  59.7 us (29%)
  local copies, waits for them, and re-layouts  23.4 us (11%)
  Pallas kernels  21.4 us (10%)
  matrix products  15.3 us (7%)
  other arithmetic  7.53 us (4%)
    ppermute x15, waiting for transfers between devices, cross(): return lax.ppermute(value, DP, pairs)  54.4 us
    ppermute x15, starting transfers between devices, cross(): return lax.ppermute(value, DP, pairs)  19.2 us
    ppermute x11, waiting for transfers between devices, shift(): lax.ppermute(value, axis, [(i, (i + step) % size) for i in range(size)])  19.2 us
    ppermute x11, starting transfers between devices, shift(): lax.ppermute(value, axis, [(i, (i + step) % size) for i in range(size)])  16.5 us
    all_to_all x2, starting transfers between devices, exchange(): got = lax.all_to_all(blocks, DP, split_axis=0, concat_axis=0, tiled=True)  16 us
    dot_general x4, matrix products, part(): lax.dot_general(pick(proj, (z + step) % NZ), rows_in, (((1,), (1,)), ((),...  15.3 us
    unnamed x77, local copies, waits for them, and re-layouts  15.1 us
    pallas_call x3, Pallas kernels, context_product(): pl.pallas_call(body, out_shape=jax.ShapeDtypeStruct((out_rows, width), dt...  12.4 us
  transfers between devices with their start and end apart: 29, of which 16 were waited for; matrix products, arithmetic and copies ran while one was open for 10% of the time, Pallas kernels for 8%

profile of v4, /device:TPU:1, one launch (start us, length us, event | category | flops | bytes accessed | tf_op | source)
XLA Modules:
  0.0 206.0 jit_solution(15002945622274014087)
XLA Ops:
  0.7 4.0 %fusion.18 = bf16[1280,256]{1,0:T(8,128)(2,1)} fusion(bf16[256,1280]{1,0:T(8,128)(2,1)} %refs_4_.3, bf16[4,1280,1280]{2,1,0:T(8,128)(2,1)} %bitcast.118, s32[]{:T(128)S(6)} %select_n.222), kind=kOutput, calls=%fused_computation.15 | convolution fusion | flops 839188480 | bytes 4587524 | tf_op jit(solution)/shard_map/dot_general | solution.py:180
  4.7 3.8 %fusion.15 = bf16[1280,256]{1,0:T(8,128)(2,1)} fusion(bf16[256,1280]{1,0:T(8,128)(2,1)S(1)} %copy-done.6, bf16[4,1280,1280]{2,1,0:T(8,128)(2,1)} %bitcast.119, s32[]{:T(128)S(6)} %select_n.221), kind=kOutput, calls=%fused_computation.14 | convolution fusion | flops 839188480 | bytes 4587524 | tf_op jit(solution)/shard_map/dot_general | solution.py:180
  8.5 2.0 collective-permute-start
  10.6 1.3 collective-permute-start.1
  11.8 1.8 collective-permute-start.3
  13.7 3.3 %collective-permute-start.2 = (bf16[1280,256]{1,0:T(8,128)(2,1)}, bf16[1280,256]{1,0:T(8,128)(2,1)}, u32[]{:S(2)}, u32[]{:S(2)}) collective-permute-start(bf16[1280,256]{1,0:T(8,128)(2,1)} %fusion.18), channel_id=1, source_target_pairs={{0,2},{1,3},{2,0},{3,1},{4,6},{5,7},{6,4},{7,5},{8,10},{9,11},{10,... | collective-permute-start | bytes 1966088 | tf_op jit(solution)/shard_map/ppermute | solution.py:22
  17.0 3.9 %fusion.21 = bf16[1280,256]{1,0:T(8,128)(2,1)} fusion(bf16[256,1280]{1,0:T(8,128)(2,1)S(1)} %copy-done.6, bf16[4,1280,1280]{2,1,0:T(8,128)(2,1)} %bitcast.120, s32[]{:T(128)S(6)} %select_n.224), kind=kOutput, calls=%fused_computation.16 | convolution fusion | flops 839188480 | bytes 4587524 | tf_op jit(solution)/shard_map/dot_general | solution.py:180
  22.3 7.9 %all-to-all-start = ((f32[32,1,8]{2,1,0:T(1,128)}), f32[32,1,8]{2,1,0:T(1,128)S(1)}, u32[]{:S(2)}, u32[]{:S(2)}) async-start(f32[32,1,8]{2,1,0:T(1,128)} %broadcast_in_dim.16), calls=%async_computation | async-start | bytes 32768 | tf_op jit(solution)/shard_map/all_to_all | solution.py:42
  30.8 2.2 %copy.30 = bf16[256,1280]{0,1:T(8,128)(2,1)} copy(bf16[256,1280]{1,0:T(8,128)(2,1)} %param.10) | data formatting | bytes 1310720 | tf_op args[1]
  33.1 4.1 %all-to-all-done = f32[32,1,8]{2,1,0:T(1,128)S(1)} async-done(((f32[32,1,8]{2,1,0:T(1,128)}), f32[32,1,8]{2,1,0:T(1,128)S(1)}, u32[]{:S(2)}, u32[]{:S(2)}) %all-to-all-start) | async-done | bytes 1056 | tf_op jit(solution)/shard_map/all_to_all | solution.py:42
  40.1 4.8 %collective-permute-done.4 = bf16[1280,256]{1,0:T(8,128)(2,1)} collective-permute-done((bf16[1280,256]{1,0:T(8,128)(2,1)}, bf16[1280,256]{1,0:T(8,128)(2,1)}, u32[]{:S(2)}, u32[]{:S(2)}) %collective-permute-start.4) | collective-permute-done | bytes 655392 | tf_op jit(solution)/shard_map/ppermute | solution.py:22
  44.9 3.6 %fusion.12 = f32[1280,256]{1,0:T(8,128)S(1)} fusion(bf16[256,1280]{1,0:T(8,128)(2,1)S(1)} %copy-done.6, bf16[4,1280,1280]{2,1,0:T(8,128)(2,1)} %bitcast.121, s32[]{:T(128)S(6)} %select_n.219, bf16[1280,256]{1,0:T(8,128)(2,1)} %collective-permute-done.4, bf16[1280,256]{1,0:T(8,128)(2,1)} %collective-permute-done.3, bf16[1280,256]{1,0:T(8,128)(2,1)} %collective-permute-done.2), kind=kOutput, calls=%fused_computation.12 | convolution fusion | flops 840826880 | bytes 7208964 | tf_op jit(solution)/shard_map/dot_general | solution.py:180
  48.5 6.6 %collective-permute-done.5.refs_6_ = bf16[256,1280]{1,0:T(8,128)(2,1)S(1)} collective-permute-done((bf16[256,1280]{1,0:T(8,128)(2,1)S(1)}, bf16[256,1280]{1,0:T(8,128)(2,1)S(1)}, u32[]{:S(2)}, u32[]{:S(2)}) %collective-permute-start.5) | collective-permute-done | bytes 655392 | tf_op jit(solution)/shard_map/ppermute | solution.py:37
  55.1 1.8 collective-permute-done.6.refs_5_
  57.8 2.5 %collective-permute-start.8 = (f32[2,256]{1,0:T(2,128)S(1)}, f32[2,256]{1,0:T(2,128)S(1)}, u32[]{:S(2)}, u32[]{:S(2)}) collective-permute-start(f32[2,256]{1,0:T(2,128)S(1)} %pad_maximum_fusion.1), channel_id=1, source_target_pairs={{0,2},{1,3},{2,0},{3,1},{4,6},{5,7},{6,4},{7,5},{8,10},{9,11},{10,... | collective-permute-start | bytes 6152 | tf_op jit(solution)/shard_map/ppermute | solution.py:22
  61.8 2.1 %collective-permute-done.7 = f32[2,256]{1,0:T(2,128)S(1)} collective-permute-done((f32[2,256]{1,0:T(2,128)S(1)}, f32[2,256]{1,0:T(2,128)S(1)}, u32[]{:S(2)}, u32[]{:S(2)}) %collective-permute-start.7) | collective-permute-done | bytes 2080 | tf_op jit(solution)/shard_map/ppermute | solution.py:22
  64.4 7.3 %collective-permute-done.10.refs_6_ = bf16[256,1280]{1,0:T(8,128)(2,1)S(1)} collective-permute-done((bf16[256,1280]{1,0:T(8,128)(2,1)S(1)}, bf16[256,1280]{1,0:T(8,128)(2,1)S(1)}, u32[]{:S(2)}, u32[]{:S(2)}) %collective-permute-start.10) | collective-permute-done | bytes 655392 | tf_op jit(solution)/shard_map/ppermute | solution.py:37
  71.7 4.2 %collective-permute-done.11.refs_7_ = bf16[256,1280]{1,0:T(8,128)(2,1)S(1)} collective-permute-done((bf16[256,1280]{1,0:T(8,128)(2,1)S(1)}, bf16[256,1280]{1,0:T(8,128)(2,1)S(1)}, u32[]{:S(2)}, u32[]{:S(2)}) %collective-permute-start.11) | collective-permute-done | bytes 655392 | tf_op jit(solution)/shard_map/ppermute | solution.py:37
  75.9 1.6 place_rows.1
  77.5 8.6 %all-to-all-start.1 = ((bf16[32,16,1280]{2,1,0:T(8,128)(2,1)}), bf16[32,16,1280]{2,1,0:T(8,128)(2,1)}, u32[]{:S(2)}, u32[]{:S(2)}) async-start(bf16[32,16,1280]{2,1,0:T(8,128)(2,1)} %bitcast.16), calls=%async_computation.1 | async-start | bytes 2621440 | tf_op jit(solution)/shard_map/all_to_all | solution.py:58
  86.3 2.9 %collective-permute-start.13 = (bf16[1280,256]{1,0:T(8,128)(2,1)S(1)}, bf16[1280,256]{1,0:T(8,128)(2,1)S(1)}, u32[]{:S(2)}, u32[]{:S(2)}) collective-permute-start(bf16[1280,256]{1,0:T(8,128)(2,1)S(1)} %fusion.26.refs_0_.grad_ref), channel_id=1, source_target_pairs={{0,3},{1,0},{2,1},{3,2},{4,7},{5,4},{6,5},{7,6},{8,11},{9,8},{10,9... | collective-permute-start | bytes 1966088 | tf_op jit(solution)/shard_map/ppermute | solution.py:22
  89.3 2.9 %context_product.3.refs_4_ = f32[256,1280]{1,0:T(8,128)S(1)} custom-call(s32[1]{0:T(128)} %bitcast.12.which, bf16[1280,256]{1,0:T(8,128)(2,1)S(1)} %fusion.26.refs_0_.grad_ref, bf16[5120,1280]{1,0:T(8,128)(2,1)} %refs_1_.3), custom_call_target="tpu_custom_call" | custom-call | tf_op jit(solution)/shard_map/context_product/pallas_call | solution.py:100
  92.2 12.0 %collective-permute-done.12.refs_1_ = bf16[1280,256]{1,0:T(8,128)(2,1)S(1)} collective-permute-done((bf16[1280,256]{1,0:T(8,128)(2,1)S(1)}, bf16[1280,256]{1,0:T(8,128)(2,1)S(1)}, u32[]{:S(2)}, u32[]{:S(2)}) %collective-permute-start.12) | collective-permute-done | bytes 655392 | tf_op jit(solution)/shard_map/ppermute | solution.py:22
  106.8 2.4 %collective-permute-start.15 = (bf16[640,256]{1,0:T(8,128)(2,1)}, bf16[640,256]{1,0:T(8,128)(2,1)}, u32[]{:S(2)}, u32[]{:S(2)}) collective-permute-start(bf16[640,256]{1,0:T(8,128)(2,1)} %slice.19), channel_id=1, source_target_pairs={{0,3},{1,0},{2,1},{3,2},{4,7},{5,4},{6,5},{7,6},{8,11},{9,8},{10,9... | collective-permute-start | bytes 983048 | tf_op jit(solution)/shard_map/ppermute | solution.py:22
  109.4 1.1 copy-done.1
  110.4 1.1 copy-done.4
  111.5 5.1 %context_product.4.refs_2_ = f32[256,1280]{1,0:T(8,128)S(1)} custom-call(s32[2]{0:T(128)S(1)} %pad_add_fusion.which, bf16[1280,256]{1,0:T(8,128)(2,1)S(1)} %copy-done.4, bf16[1280,256]{1,0:T(8,128)(2,1)S(1)} %copy-done.1, bf16[5120,1280]{1,0:T(8,128)(2,1)} %refs_1_.3, bf16[5120,1280]{1,0:T(8,128)(2,1)} %refs_1_.3, f32[256,1280]{1,0:T(8,128)S(1)} %context_product.3.refs_4_), custom_call_target="tpu_custom_call" | custom-call | tf_op jit(solution)/shard_map/context_product/pallas_call | solution.py:100
  116.6 2.2 %reshape.125 = bf16[384,1280]{1,0:T(8,128)(2,1)} reshape(bf16[32,12,1280]{2,1,0:T(8,128)(2,1)} %bitcast.110) | data formatting | bytes 1966080 | tf_op jit(solution)/shard_map/reshape | solution.py:60
  122.5 1.2 collective-permute-start.19
  124.6 2.4 %collective-permute-start.20 = (bf16[640,256]{1,0:T(8,128)(2,1)S(1)}, bf16[640,256]{1,0:T(8,128)(2,1)S(1)}, u32[]{:S(2)}, u32[]{:S(2)}) collective-permute-start(bf16[640,256]{1,0:T(8,128)(2,1)S(1)} %get-tuple-element.64), channel_id=1, source_target_pairs={{0,16},{4,68},{8,24},{12,76},{16,0},{20,84},{24,8},{28,92},{32,48}... | collective-permute-start | bytes 983048 | tf_op jit(solution)/shard_map/ppermute | solution.py:37
  127.9 1.1 collective-permute-start.21
  129.9 4.5 %collective-permute-done.20.refs_2_ = bf16[640,256]{1,0:T(8,128)(2,1)S(1)} collective-permute-done((bf16[640,256]{1,0:T(8,128)(2,1)S(1)}, bf16[640,256]{1,0:T(8,128)(2,1)S(1)}, u32[]{:S(2)}, u32[]{:S(2)}) %collective-permute-start.20) | collective-permute-done | bytes 327712 | tf_op jit(solution)/shard_map/ppermute | solution.py:37
  134.9 3.6 %weight_product.2 = bf16[640,1280]{1,0:T(8,128)(2,1)} custom-call(bf16[640,256]{1,0:T(8,128)(2,1)S(1)} %get-tuple-element.68.refs_0_, bf16[640,256]{1,0:T(8,128)(2,1)S(1)} %collective-permute-done.19.refs_1_, bf16[640,256]{1,0:T(8,128)(2,1)S(1)} %collective-permute-done.20.refs_2_, bf16[640,256]{1,0:T(8,128)(2,1)S(1)} %collective-permute-done.21.refs_3_, ...), custom_call_target="tpu_custom_call" | custom-call | tf_op jit(solution)/shard_map/weight_product/pallas_call | solution.py:149
  138.5 2.4 %collective-permute-start.22 = (bf16[640,1280]{1,0:T(8,128)(2,1)}, bf16[640,1280]{1,0:T(8,128)(2,1)}, u32[]{:S(2)}, u32[]{:S(2)}) collective-permute-start(bf16[640,1280]{1,0:T(8,128)(2,1)} %weight_product.2), channel_id=1, source_target_pairs={{0,4},{4,0},{1,5},{5,1},{2,6},{6,2},{3,7},{7,3},{8,12},{12,8},{9,1... | collective-permute-start | bytes 4915208 | tf_op jit(solution)/shard_map/ppermute | solution.py:22
  140.9 4.4 %context_product.5 = bf16[512,1280]{1,0:T(8,128)(2,1)} custom-call(s32[1]{0:T(128)} %bitcast.which, bf16[1280,256]{1,0:T(8,128)(2,1)S(1)} %constant_dynamic-update-slice_fusion.refs_0_, bf16[5120,1280]{1,0:T(8,128)(2,1)} %refs_1_.3, f32[256,1280]{1,0:T(8,128)S(1)} %context_product.4.refs_2_, bf16[512,256]{1,0:T(8,128)(2,1)S(1)} %fusion.30.slots_ref.refs_3_), custom_call_target="tpu_custom_call" | custom-call | tf_op jit(solution)/shard_map/context_product/pallas_call | solution.py:100
  145.3 7.4 %all-to-all-start.2 = ((bf16[32,16,1280]{2,1,0:T(8,128)(2,1)}), bf16[32,16,1280]{2,1,0:T(8,128)(2,1)}, u32[]{:S(2)}, u32[]{:S(2)}) async-start(bf16[32,16,1280]{2,1,0:T(8,128)(2,1)} %bitcast.17), calls=%async_computation.2 | async-start | bytes 2621440 | tf_op jit(solution)/shard_map/all_to_all | solution.py:58
  152.7 1.5 collective-permute-start.16
  154.1 2.4 %collective-permute-start.17 = (bf16[640,256]{1,0:T(8,128)(2,1)S(1)}, bf16[640,256]{1,0:T(8,128)(2,1)S(1)}, u32[]{:S(2)}, u32[]{:S(2)}) collective-permute-start(bf16[640,256]{1,0:T(8,128)(2,1)S(1)} %copy-done.31), channel_id=1, source_target_pairs={{0,64},{4,20},{8,72},{12,28},{16,80},{20,4},{24,88},{28,12},{32,96... | collective-permute-start | bytes 983048 | tf_op jit(solution)/shard_map/ppermute | solution.py:37
  156.5 1.2 collective-permute-start.18
  157.7 16.4 %collective-permute-done.16.refs_1_ = bf16[640,256]{1,0:T(8,128)(2,1)S(1)} collective-permute-done((bf16[640,256]{1,0:T(8,128)(2,1)S(1)}, bf16[640,256]{1,0:T(8,128)(2,1)S(1)}, u32[]{:S(2)}, u32[]{:S(2)}) %collective-permute-start.16) | collective-permute-done | bytes 327712 | tf_op jit(solution)/shard_map/ppermute | solution.py:37
  174.8 3.1 %collective-permute-done.17.refs_2_ = bf16[640,256]{1,0:T(8,128)(2,1)S(1)} collective-permute-done((bf16[640,256]{1,0:T(8,128)(2,1)S(1)}, bf16[640,256]{1,0:T(8,128)(2,1)S(1)}, u32[]{:S(2)}, u32[]{:S(2)}) %collective-permute-start.17) | collective-permute-done | bytes 327712 | tf_op jit(solution)/shard_map/ppermute | solution.py:37
  180.5 1.1 copy-done.15
  184.5 3.8 %weight_product.3 = bf16[640,1280]{1,0:T(8,128)(2,1)S(1)} custom-call(bf16[640,256]{1,0:T(8,128)(2,1)S(1)} %copy-done.9, bf16[640,256]{1,0:T(8,128)(2,1)S(1)} %copy-done.23, bf16[640,256]{1,0:T(8,128)(2,1)S(1)} %copy-done.25, bf16[640,256]{1,0:T(8,128)(2,1)S(1)} %copy-done.27, bf16[256,1280]{1,0:T(8,128)(2,1)S(1)} %copy-done.8, ...), custom_call_target="tpu_custom_call" | custom-call | tf_op jit(solution)/shard_map/weight_product/pallas_call | solution.py:149
  188.4 2.2 %collective-permute-start.25 = (bf16[160,1280]{1,0:T(8,128)(2,1)S(1)}, bf16[160,1280]{1,0:T(8,128)(2,1)S(1)}, u32[]{:S(2)}, u32[]{:S(2)}) collective-permute-start(bf16[160,1280]{1,0:T(8,128)(2,1)S(1)} %get-tuple-element.52), channel_id=1, source_target_pairs={{0,24},{4,100},{8,0},{12,108},{16,8},{20,116},{24,16},{28,124},{32... | collective-permute-start | bytes 1228808 | tf_op jit(solution)/shard_map/ppermute | solution.py:37
  191.8 2.2 %reshape.127 = bf16[384,1280]{1,0:T(8,128)(2,1)} reshape(bf16[32,12,1280]{2,1,0:T(8,128)(2,1)} %bitcast.111) | data formatting | bytes 1966080 | tf_op jit(solution)/shard_map/reshape | solution.py:60
  193.9 6.0 %collective-permute-done.25 = bf16[160,1280]{1,0:T(8,128)(2,1)S(1)} collective-permute-done((bf16[160,1280]{1,0:T(8,128)(2,1)S(1)}, bf16[160,1280]{1,0:T(8,128)(2,1)S(1)}, u32[]{:S(2)}, u32[]{:S(2)}) %collective-permute-start.25) | collective-permute-done | bytes 409632 | tf_op jit(solution)/shard_map/ppermute | solution.py:37
  200.0 3.8 %collective-permute-done.23 = bf16[160,1280]{1,0:T(8,128)(2,1)} collective-permute-done((bf16[160,1280]{1,0:T(8,128)(2,1)S(1)}, bf16[160,1280]{1,0:T(8,128)(2,1)}, u32[]{:S(2)}, u32[]{:S(2)}) %collective-permute-start.23) | collective-permute-done | bytes 409632 | tf_op jit(solution)/shard_map/ppermute | solution.py:37
  203.8 2.2 %fusion.29 = f32[160,1280]{1,0:T(8,128)} fusion(bf16[160,1280]{1,0:T(8,128)(2,1)S(1)} %collective-permute-done.25, bf16[160,1280]{1,0:T(8,128)(2,1)} %collective-permute-done.24, bf16[160,1280]{1,0:T(8,128)(2,1)} %collective-permute-done.23, bf16[4,160,1280]{2,1,0:T(8,128)(2,1)S(1)} %bitcast.114, s32[]{:T(128)S(6)} %select_n.253), kind=kLoop, calls=%fused_computation.28 | loop fusion | flops 1638400 | bytes 2457604 | tf_op jit(solution)/shard_map/div | solution.py:253
  (130 shorter events, 24.8 us)
Async XLA Ops:
  8.5 28.9 %collective-permute-start = (bf16[256,1280]{1,0:T(8,128)(2,1)S(1)}, bf16[256,1280]{1,0:T(8,128)(2,1)S(1)}, u32[]{:S(2)}, u32[]{:S(2)}) collective-permute-start(bf16[256,1280]{1,0:T(8,128)(2,1)S(1)} %copy-done.6), channel_id=1, source_target_pairs={{0,8},{4,36},{8,16},{12,44},{16,24},{20,52},{24,0},{28,60},{32,40}... | collective-permute-start | bytes 1966088 | tf_op jit(solution)/shard_map/ppermute | solution.py:37
  10.6 27.7 %collective-permute-start.1 = (bf16[256,1280]{1,0:T(8,128)(2,1)S(1)}, bf16[256,1280]{1,0:T(8,128)(2,1)S(1)}, u32[]{:S(2)}, u32[]{:S(2)}) collective-permute-start(bf16[256,1280]{1,0:T(8,128)(2,1)S(1)} %copy-done.6), channel_id=1, source_target_pairs={{0,24},{4,100},{8,0},{12,108},{16,8},{20,116},{24,16},{28,124},{32... | collective-permute-start | bytes 1966088 | tf_op jit(solution)/shard_map/ppermute | solution.py:37
  11.8 33.1 %collective-permute-start.3 = (bf16[1280,256]{1,0:T(8,128)(2,1)}, bf16[1280,256]{1,0:T(8,128)(2,1)}, u32[]{:S(2)}, u32[]{:S(2)}) collective-permute-start(bf16[1280,256]{1,0:T(8,128)(2,1)} %fusion.15), channel_id=1, source_target_pairs={{0,1},{1,2},{2,3},{3,0},{4,5},{5,6},{6,7},{7,4},{8,9},{9,10},{10,1... | collective-permute-start | bytes 1966088 | tf_op jit(solution)/shard_map/ppermute | solution.py:22
  13.7 31.2 %collective-permute-start.2 = (bf16[1280,256]{1,0:T(8,128)(2,1)}, bf16[1280,256]{1,0:T(8,128)(2,1)}, u32[]{:S(2)}, u32[]{:S(2)}) collective-permute-start(bf16[1280,256]{1,0:T(8,128)(2,1)} %fusion.18), channel_id=1, source_target_pairs={{0,2},{1,3},{2,0},{3,1},{4,6},{5,7},{6,4},{7,5},{8,10},{9,11},{10,... | collective-permute-start | bytes 1966088 | tf_op jit(solution)/shard_map/ppermute | solution.py:22
  17.0 4.6 %copy-start.34 = (f32[4]{0:T(128)S(1)}, f32[4]{0:T(128)}, u32[]{:S(2)}) copy-start(f32[4]{0:T(128)} %param.14) | copy-start | bytes 52
  17.0 4.6 %copy-start.36 = (s32[4]{0:T(128)S(1)}, s32[4]{0:T(128)}, u32[]{:S(2)}) copy-start(s32[4]{0:T(128)} %param.15) | copy-start | bytes 52
  17.0 13.3 %copy-start.35 = (s32[64,1]{0,1:T(1,128)S(1)}, s32[64,1]{0,1:T(1,128)}, u32[]{:S(2)}) copy-start(s32[64,1]{0,1:T(1,128)} %param.17) | copy-start | bytes 772
  17.0 13.5 %copy-start.29 = (bf16[256,1280]{1,0:T(8,128)(2,1)S(1)}, bf16[256,1280]{1,0:T(8,128)(2,1)}, u32[]{:S(2)}) copy-start(bf16[256,1280]{1,0:T(8,128)(2,1)} %param.11) | copy-start | bytes 1966084
  20.9 24.0 %collective-permute-start.4 = (bf16[1280,256]{1,0:T(8,128)(2,1)}, bf16[1280,256]{1,0:T(8,128)(2,1)}, u32[]{:S(2)}, u32[]{:S(2)}) collective-permute-start(bf16[1280,256]{1,0:T(8,128)(2,1)} %fusion.21), channel_id=1, source_target_pairs={{0,3},{1,0},{2,1},{3,2},{4,7},{5,4},{6,5},{7,6},{8,11},{9,8},{10,9... | collective-permute-start | bytes 1966088 | tf_op jit(solution)/shard_map/ppermute | solution.py:22
  22.3 14.9 %all-to-all-start = ((f32[32,1,8]{2,1,0:T(1,128)}), f32[32,1,8]{2,1,0:T(1,128)S(1)}, u32[]{:S(2)}, u32[]{:S(2)}) async-start(f32[32,1,8]{2,1,0:T(1,128)} %broadcast_in_dim.16), calls=%async_computation | async-start | bytes 32768 | tf_op jit(solution)/shard_map/all_to_all | solution.py:42
  30.5 9.4 %copy-start.33 = (s32[4]{0:T(128)S(1)}, s32[4]{0:T(128)}, u32[]{:S(2)}) copy-start(s32[4]{0:T(128)} %param.16) | copy-start | bytes 52
  38.3 10.2 %copy-start.18 = (bf16[256,1280]{1,0:T(8,128)(2,1)}, bf16[256,1280]{1,0:T(8,128)(2,1)S(1)}, u32[]{:S(2)}) copy-start(bf16[256,1280]{1,0:T(8,128)(2,1)S(1)} %collective-permute-done.1.refs_7_) | copy-start | bytes 1966084
  38.3 16.8 %collective-permute-start.5 = (bf16[256,1280]{1,0:T(8,128)(2,1)S(1)}, bf16[256,1280]{1,0:T(8,128)(2,1)S(1)}, u32[]{:S(2)}, u32[]{:S(2)}) collective-permute-start(bf16[256,1280]{1,0:T(8,128)(2,1)S(1)} %copy-done.6), channel_id=1, source_target_pairs={{0,16},{4,68},{8,24},{12,76},{16,0},{20,84},{24,8},{28,92},{32,48}... | collective-permute-start | bytes 1966088 | tf_op jit(solution)/shard_map/ppermute | solution.py:37
  39.3 17.7 %collective-permute-start.6 = (bf16[256,1280]{1,0:T(8,128)(2,1)S(1)}, bf16[256,1280]{1,0:T(8,128)(2,1)S(1)}, u32[]{:S(2)}, u32[]{:S(2)}) collective-permute-start(bf16[256,1280]{1,0:T(8,128)(2,1)S(1)} %copy-done.6), channel_id=1, source_target_pairs={{0,32},{4,12},{8,40},{12,20},{16,48},{20,28},{24,56},{28,4},{32,64... | collective-permute-start | bytes 1966088 | tf_op jit(solution)/shard_map/ppermute | solution.py:37
  40.1 16.9 %copy-start.28 = (bf16[256,1280]{0,1:T(8,128)(2,1)S(1)}, bf16[256,1280]{0,1:T(8,128)(2,1)}, u32[]{:S(2)}) copy-start(bf16[256,1280]{0,1:T(8,128)(2,1)} %copy.30) | copy-start | bytes 1966084
  40.1 16.9 %copy-start.32 = (f32[1280]{0:T(1024)S(1)}, f32[1280]{0:T(1024)}, u32[]{:S(2)}) copy-start(f32[1280]{0:T(1024)} %param.13) | copy-start | bytes 15364
  57.8 3.7 %collective-permute-start.9 = (f32[2,256]{1,0:T(2,128)S(1)}, f32[2,256]{1,0:T(2,128)S(1)}, u32[]{:S(2)}, u32[]{:S(2)}) collective-permute-start(f32[2,256]{1,0:T(2,128)S(1)} %pad_maximum_fusion.1), channel_id=1, source_target_pairs={{0,3},{1,0},{2,1},{3,2},{4,7},{5,4},{6,5},{7,6},{8,11},{9,8},{10,9... | collective-permute-start | bytes 6152 | tf_op jit(solution)/shard_map/ppermute | solution.py:22
  57.8 4.0 %collective-permute-start.8 = (f32[2,256]{1,0:T(2,128)S(1)}, f32[2,256]{1,0:T(2,128)S(1)}, u32[]{:S(2)}, u32[]{:S(2)}) collective-permute-start(f32[2,256]{1,0:T(2,128)S(1)} %pad_maximum_fusion.1), channel_id=1, source_target_pairs={{0,2},{1,3},{2,0},{3,1},{4,6},{5,7},{6,4},{7,5},{8,10},{9,11},{10,... | collective-permute-start | bytes 6152 | tf_op jit(solution)/shard_map/ppermute | solution.py:22
  60.3 3.6 %collective-permute-start.7 = (f32[2,256]{1,0:T(2,128)S(1)}, f32[2,256]{1,0:T(2,128)S(1)}, u32[]{:S(2)}, u32[]{:S(2)}) collective-permute-start(f32[2,256]{1,0:T(2,128)S(1)} %pad_maximum_fusion.1), channel_id=1, source_target_pairs={{0,1},{1,2},{2,3},{3,0},{4,5},{5,6},{6,7},{7,4},{8,9},{9,10},{10,1... | collective-permute-start | bytes 6152 | tf_op jit(solution)/shard_map/ppermute | solution.py:22
  60.4 11.3 %collective-permute-start.10 = (bf16[256,1280]{1,0:T(8,128)(2,1)S(1)}, bf16[256,1280]{1,0:T(8,128)(2,1)S(1)}, u32[]{:S(2)}, u32[]{:S(2)}) collective-permute-start(bf16[256,1280]{1,0:T(8,128)(2,1)S(1)} %copy-done.6), channel_id=1, source_target_pairs={{0,64},{4,20},{8,72},{12,28},{16,80},{20,4},{24,88},{28,12},{32,96... | collective-permute-start | bytes 1966088 | tf_op jit(solution)/shard_map/ppermute | solution.py:37
  60.5 15.5 %collective-permute-start.11 = (bf16[256,1280]{1,0:T(8,128)(2,1)S(1)}, bf16[256,1280]{1,0:T(8,128)(2,1)S(1)}, u32[]{:S(2)}, u32[]{:S(2)}) collective-permute-start(bf16[256,1280]{1,0:T(8,128)(2,1)S(1)} %copy-done.6), channel_id=1, source_target_pairs={{0,96},{4,28},{8,104},{12,4},{16,112},{20,12},{24,120},{28,20},{32... | collective-permute-start | bytes 1966088 | tf_op jit(solution)/shard_map/ppermute | solution.py:37
  71.7 5.8 %copy-start.12 = (bf16[256,1280]{1,0:T(8,128)(2,1)}, bf16[256,1280]{1,0:T(8,128)(2,1)S(1)}, u32[]{:S(2)}) copy-start(bf16[256,1280]{1,0:T(8,128)(2,1)S(1)} %collective-permute-done.10.refs_6_) | copy-start | bytes 1966084
  77.5 39.1 %all-to-all-start.1 = ((bf16[32,16,1280]{2,1,0:T(8,128)(2,1)}), bf16[32,16,1280]{2,1,0:T(8,128)(2,1)}, u32[]{:S(2)}, u32[]{:S(2)}) async-start(bf16[32,16,1280]{2,1,0:T(8,128)(2,1)} %bitcast.16), calls=%async_computation.1 | async-start | bytes 2621440 | tf_op jit(solution)/shard_map/all_to_all | solution.py:58
  86.2 18.0 %collective-permute-start.12 = (bf16[1280,256]{1,0:T(8,128)(2,1)S(1)}, bf16[1280,256]{1,0:T(8,128)(2,1)S(1)}, u32[]{:S(2)}, u32[]{:S(2)}) collective-permute-start(bf16[1280,256]{1,0:T(8,128)(2,1)S(1)} %fusion.26.refs_0_.grad_ref), channel_id=1, source_target_pairs={{0,1},{1,2},{2,3},{3,0},{4,5},{5,6},{6,7},{7,4},{8,9},{9,10},{10,1... | collective-permute-start | bytes 1966088 | tf_op jit(solution)/shard_map/ppermute | solution.py:22
  86.3 17.8 %collective-permute-start.13 = (bf16[1280,256]{1,0:T(8,128)(2,1)S(1)}, bf16[1280,256]{1,0:T(8,128)(2,1)S(1)}, u32[]{:S(2)}, u32[]{:S(2)}) collective-permute-start(bf16[1280,256]{1,0:T(8,128)(2,1)S(1)} %fusion.26.refs_0_.grad_ref), channel_id=1, source_target_pairs={{0,3},{1,0},{2,1},{3,2},{4,7},{5,4},{6,5},{7,6},{8,11},{9,8},{10,9... | collective-permute-start | bytes 1966088 | tf_op jit(solution)/shard_map/ppermute | solution.py:22
  105.8 13.1 %collective-permute-start.14 = (bf16[640,256]{1,0:T(8,128)(2,1)}, bf16[640,256]{1,0:T(8,128)(2,1)}, u32[]{:S(2)}, u32[]{:S(2)}) collective-permute-start(bf16[640,256]{1,0:T(8,128)(2,1)} %slice.18), channel_id=1, source_target_pairs={{0,1},{1,2},{2,3},{3,0},{4,5},{5,6},{6,7},{7,4},{8,9},{9,10},{10,1... | collective-permute-start | bytes 983048 | tf_op jit(solution)/shard_map/ppermute | solution.py:22
  106.8 12.0 %collective-permute-start.15 = (bf16[640,256]{1,0:T(8,128)(2,1)}, bf16[640,256]{1,0:T(8,128)(2,1)}, u32[]{:S(2)}, u32[]{:S(2)}) collective-permute-start(bf16[640,256]{1,0:T(8,128)(2,1)} %slice.19), channel_id=1, source_target_pairs={{0,3},{1,0},{2,1},{3,2},{4,7},{5,4},{6,5},{7,6},{8,11},{9,8},{10,9... | collective-permute-start | bytes 983048 | tf_op jit(solution)/shard_map/ppermute | solution.py:22
  116.6 4.3 %copy-start.2 = (bf16[1280,256]{1,0:T(8,128)(2,1)S(1)}, bf16[1280,256]{1,0:T(8,128)(2,1)}, u32[]{:S(2)}) copy-start(bf16[1280,256]{1,0:T(8,128)(2,1)} %copy-done) | copy-start | bytes 1966084
  122.5 7.4 %collective-permute-start.19 = (bf16[640,256]{1,0:T(8,128)(2,1)S(1)}, bf16[640,256]{1,0:T(8,128)(2,1)S(1)}, u32[]{:S(2)}, u32[]{:S(2)}) collective-permute-start(bf16[640,256]{1,0:T(8,128)(2,1)S(1)} %get-tuple-element.66), channel_id=1, source_target_pairs={{0,8},{4,36},{8,16},{12,44},{16,24},{20,52},{24,0},{28,60},{32,40}... | collective-permute-start | bytes 983048 | tf_op jit(solution)/shard_map/ppermute | solution.py:37
  124.6 9.9 %collective-permute-start.20 = (bf16[640,256]{1,0:T(8,128)(2,1)S(1)}, bf16[640,256]{1,0:T(8,128)(2,1)S(1)}, u32[]{:S(2)}, u32[]{:S(2)}) collective-permute-start(bf16[640,256]{1,0:T(8,128)(2,1)S(1)} %get-tuple-element.64), channel_id=1, source_target_pairs={{0,16},{4,68},{8,24},{12,76},{16,0},{20,84},{24,8},{28,92},{32,48}... | collective-permute-start | bytes 983048 | tf_op jit(solution)/shard_map/ppermute | solution.py:37
  127.0 7.9 %copy-start.7 = (bf16[256,1280]{1,0:T(8,128)(2,1)S(1)}, bf16[256,1280]{1,0:T(8,128)(2,1)}, u32[]{:S(2)}) copy-start(bf16[256,1280]{1,0:T(8,128)(2,1)} %refs_4_.3) | copy-start | bytes 1966084
  127.0 7.9 %copy-start.17 = (bf16[256,1280]{1,0:T(8,128)(2,1)S(1)}, bf16[256,1280]{1,0:T(8,128)(2,1)}, u32[]{:S(2)}) copy-start(bf16[256,1280]{1,0:T(8,128)(2,1)} %copy-done.16) | copy-start | bytes 1966084
  127.0 7.9 %copy-start.19 = (bf16[256,1280]{1,0:T(8,128)(2,1)S(1)}, bf16[256,1280]{1,0:T(8,128)(2,1)}, u32[]{:S(2)}) copy-start(bf16[256,1280]{1,0:T(8,128)(2,1)} %copy-done.18) | copy-start | bytes 1966084
  127.0 7.9 %copy-start.21 = (bf16[256,1280]{1,0:T(8,128)(2,1)S(1)}, bf16[256,1280]{1,0:T(8,128)(2,1)}, u32[]{:S(2)}) copy-start(bf16[256,1280]{1,0:T(8,128)(2,1)} %copy-done.20) | copy-start | bytes 1966084
  127.9 7.0 %collective-permute-start.21 = (bf16[640,256]{1,0:T(8,128)(2,1)S(1)}, bf16[640,256]{1,0:T(8,128)(2,1)S(1)}, u32[]{:S(2)}, u32[]{:S(2)}) collective-permute-start(bf16[640,256]{1,0:T(8,128)(2,1)S(1)} %get-tuple-element.62), channel_id=1, source_target_pairs={{0,24},{4,100},{8,0},{12,108},{16,8},{20,116},{24,16},{28,124},{32... | collective-permute-start | bytes 983048 | tf_op jit(solution)/shard_map/ppermute | solution.py:37
  138.5 40.9 %collective-permute-start.22 = (bf16[640,1280]{1,0:T(8,128)(2,1)}, bf16[640,1280]{1,0:T(8,128)(2,1)}, u32[]{:S(2)}, u32[]{:S(2)}) collective-permute-start(bf16[640,1280]{1,0:T(8,128)(2,1)} %weight_product.2), channel_id=1, source_target_pairs={{0,4},{4,0},{1,5},{5,1},{2,6},{6,2},{3,7},{7,3},{8,12},{12,8},{9,1... | collective-permute-start | bytes 4915208 | tf_op jit(solution)/shard_map/ppermute | solution.py:22
  145.2 7.4 %copy-start.30 = (bf16[640,256]{1,0:T(8,128)(2,1)S(1)}, bf16[640,256]{1,0:T(8,128)(2,1)}, u32[]{:S(2)}) copy-start(bf16[640,256]{1,0:T(8,128)(2,1)} %get-tuple-element.67) | copy-start | bytes 983044
  145.2 8.9 %copy-start.31 = (bf16[640,256]{1,0:T(8,128)(2,1)S(1)}, bf16[640,256]{1,0:T(8,128)(2,1)}, u32[]{:S(2)}) copy-start(bf16[640,256]{1,0:T(8,128)(2,1)} %get-tuple-element.65) | copy-start | bytes 983044
  145.2 34.2 %copy-start.8 = (bf16[256,1280]{1,0:T(8,128)(2,1)S(1)}, bf16[256,1280]{1,0:T(8,128)(2,1)}, u32[]{:S(2)}) copy-start(bf16[256,1280]{1,0:T(8,128)(2,1)} %refs_4_.3) | copy-start | bytes 1966084
  145.3 34.2 %copy-start.9 = (bf16[640,256]{1,0:T(8,128)(2,1)S(1)}, bf16[640,256]{1,0:T(8,128)(2,1)}, u32[]{:S(2)}) copy-start(bf16[640,256]{1,0:T(8,128)(2,1)} %get-tuple-element.69.refs_0_) | copy-start | bytes 983044
  145.3 34.2 %copy-start.11 = (bf16[256,1280]{1,0:T(8,128)(2,1)S(1)}, bf16[256,1280]{1,0:T(8,128)(2,1)}, u32[]{:S(2)}) copy-start(bf16[256,1280]{1,0:T(8,128)(2,1)} %copy-done.10) | copy-start | bytes 1966084
  145.3 46.5 %all-to-all-start.2 = ((bf16[32,16,1280]{2,1,0:T(8,128)(2,1)}), bf16[32,16,1280]{2,1,0:T(8,128)(2,1)}, u32[]{:S(2)}, u32[]{:S(2)}) async-start(bf16[32,16,1280]{2,1,0:T(8,128)(2,1)} %bitcast.17), calls=%async_computation.2 | async-start | bytes 2621440 | tf_op jit(solution)/shard_map/all_to_all | solution.py:58
  152.7 21.4 %collective-permute-start.16 = (bf16[640,256]{1,0:T(8,128)(2,1)S(1)}, bf16[640,256]{1,0:T(8,128)(2,1)S(1)}, u32[]{:S(2)}, u32[]{:S(2)}) collective-permute-start(bf16[640,256]{1,0:T(8,128)(2,1)S(1)} %copy-done.30), channel_id=1, source_target_pairs={{0,32},{4,12},{8,40},{12,20},{16,48},{20,28},{24,56},{28,4},{32,64... | collective-permute-start | bytes 983048 | tf_op jit(solution)/shard_map/ppermute | solution.py:37
  154.1 23.8 %collective-permute-start.17 = (bf16[640,256]{1,0:T(8,128)(2,1)S(1)}, bf16[640,256]{1,0:T(8,128)(2,1)S(1)}, u32[]{:S(2)}, u32[]{:S(2)}) collective-permute-start(bf16[640,256]{1,0:T(8,128)(2,1)S(1)} %copy-done.31), channel_id=1, source_target_pairs={{0,64},{4,20},{8,72},{12,28},{16,80},{20,4},{24,88},{28,12},{32,96... | collective-permute-start | bytes 983048 | tf_op jit(solution)/shard_map/ppermute | solution.py:37
  156.5 22.1 %collective-permute-start.18 = (bf16[640,256]{1,0:T(8,128)(2,1)}, bf16[640,256]{1,0:T(8,128)(2,1)S(1)}, u32[]{:S(2)}, u32[]{:S(2)}) collective-permute-start(bf16[640,256]{1,0:T(8,128)(2,1)} %get-tuple-element.63), channel_id=1, source_target_pairs={{0,96},{4,28},{8,104},{12,4},{16,112},{20,12},{24,120},{28,20},{32... | collective-permute-start | bytes 983048 | tf_op jit(solution)/shard_map/ppermute | solution.py:37
  188.4 11.5 %collective-permute-start.25 = (bf16[160,1280]{1,0:T(8,128)(2,1)S(1)}, bf16[160,1280]{1,0:T(8,128)(2,1)S(1)}, u32[]{:S(2)}, u32[]{:S(2)}) collective-permute-start(bf16[160,1280]{1,0:T(8,128)(2,1)S(1)} %get-tuple-element.52), channel_id=1, source_target_pairs={{0,24},{4,100},{8,0},{12,108},{16,8},{20,116},{24,16},{28,124},{32... | collective-permute-start | bytes 1228808 | tf_op jit(solution)/shard_map/ppermute | solution.py:37
  190.7 9.3 %collective-permute-start.24 = (bf16[160,1280]{1,0:T(8,128)(2,1)S(1)}, bf16[160,1280]{1,0:T(8,128)(2,1)}, u32[]{:S(2)}, u32[]{:S(2)}) collective-permute-start(bf16[160,1280]{1,0:T(8,128)(2,1)S(1)} %get-tuple-element.53), channel_id=1, source_target_pairs={{0,16},{4,68},{8,24},{12,76},{16,0},{20,84},{24,8},{28,92},{32,48}... | collective-permute-start | bytes 1228808 | tf_op jit(solution)/shard_map/ppermute | solution.py:37
  191.2 12.6 %collective-permute-start.23 = (bf16[160,1280]{1,0:T(8,128)(2,1)S(1)}, bf16[160,1280]{1,0:T(8,128)(2,1)}, u32[]{:S(2)}, u32[]{:S(2)}) collective-permute-start(bf16[160,1280]{1,0:T(8,128)(2,1)S(1)} %get-tuple-element.51), channel_id=1, source_target_pairs={{0,8},{4,36},{8,16},{12,44},{16,24},{20,52},{24,0},{28,60},{32,40}... | collective-permute-start | bytes 1228808 | tf_op jit(solution)/shard_map/ppermute | solution.py:37
  (18 other events, 23.9 us)

commit v5 on v4

--- a/solution.py
+++ b/solution.py
@@ -31,8 +31,8 @@
     for x in range(NX):
         for y in range(NY):
             for c in range(NC):
-                along_y = (c == 0) == first
-                to = (x, (y + step) % NY, c) if along_y else ((x + step) % NX, y, c)
+                along_x = (c == 0) == first
+                to = ((x + step) % NX, y, c) if along_x else (x, (y + step) % NY, c)
                 pairs.append(((x * NY + y) * NC + c, (to[0] * NY + to[1]) * NC + to[2]))
     return lax.ppermute(value, DP, pairs)
 
@@ -127,35 +127,137 @@
     )(slots, grad_t)
 
 
-def weight_product(pieces, contexts, before=None):
-    count, height, tile = len(pieces), pieces[0].shape[0], 640
-    rows, width = contexts[0].shape
+def forward_product(out_proj, context, place, split):
+    rows, width = context.shape
+    tile = width // 2
+
+    def body(which, proj_ref, context_ref, *out_refs):
+        value = lax.dot_general(
+            proj_ref[...], context_ref[...], (((1,), (1,)), ((), ())), preferred_element_type=F32
+        )
+        if split:
+            for half in (0, 1):
+
+                @pl.when(pl.program_id(0) == half)
+                def _(half=half):
+                    out_refs[half][...] = value.astype(BF16)
+        else:
+            out_refs[0][...] = value
+
+    half_spec = pl.BlockSpec((tile, rows), lambda i, which: (0, 0))
+    out = pl.pallas_call(
+        body,
+        out_shape=[jax.ShapeDtypeStruct((tile, rows), BF16)] * 2
+        if split
+        else [jax.ShapeDtypeStruct((width, rows), F32)],
+        grid_spec=pltpu.PrefetchScalarGridSpec(
+            num_scalar_prefetch=1,
+            grid=(2,),
+            in_specs=[
+                pl.BlockSpec((tile, width), lambda i, which: (which[0] * 2 + i, 0)),
+                pl.BlockSpec((rows, width), lambda i, which: (0, 0)),
+            ],
+            out_specs=[half_spec] * 2
+            if split
+            else [pl.BlockSpec((tile, rows), lambda i, which: (i, 0))],
+        ),
+        cost_estimate=FREE,
+        compiler_params=PARAMS,
+        name="forward_product",
+    )(place.reshape(1), out_proj, context)
+    return out if split else out[0]
+
+
+def lay_out(chunks, siblings, x, y, c, z):
+    rows = chunks[0][0].shape[1]
+    block = 160
+    flat = [piece for group in (chunks, siblings) for pieces in group for piece in pieces]
+    counts = [[len(pieces) for pieces in group] for group in (chunks, siblings)]
+
+    def body(where, *refs):
+        ins, outs, sems = refs[: len(flat)], refs[len(flat) : len(flat) + 4], refs[-1]
+        here = [where[i] for i in range(4)]
+        wx, wy, wc, wz = here
+        position = 0
+        for owner, group in enumerate(counts):
+            pitch = 2 * block if owner == 0 else block
+            shift_rows = wc * block if owner == 0 else 0
+            for j, count in enumerate(group):
+                pieces = ins[position : position + count]
+                position += count
+                per_piece = 4 // count
+
+                def source(piece, slot, pitch=pitch, shift_rows=shift_rows):
+                    start = pl.multiple_of(slot * pitch + shift_rows, 32)
+                    return piece.at[pl.ds(start, block), :]
+
+                for k in range(4):
+                    target = outs[k]
+
+                    def send(src, slot, target=target, k=k, owner=owner):
+                        dst = target.at[pl.ds((owner * 4 + slot) * block, block), :]
+                        pltpu.make_async_copy(src, dst, sems.at[k]).start()
+
+                    @pl.when((wc == 0) & (lax.rem(j + wz - wx + 4, 4) == k))
+                    def _(pieces=pieces, per_piece=per_piece, send=send, source=source):
+                        for slot in range(4):
+                            send(source(pieces[slot // per_piece], slot % per_piece), slot)
+
+                    wanted = lax.rem(wy + k, 4)
+                    for number, piece in enumerate(pieces):
+
+                        @pl.when((wc == 1) & (wanted // per_piece == number))
+                        def _(piece=piece, number=number, per_piece=per_piece, send=send,
+                              source=source, wanted=wanted, j=j):
+                            send(source(piece, wanted - number * per_piece), j)
+
+        for k in range(4):
+            pltpu.make_async_copy(outs[k], outs[k], sems.at[k]).wait()
+
+    return pl.pallas_call(
+        body,
+        out_shape=[jax.ShapeDtypeStruct((8 * block, rows), BF16)] * 4,
+        grid_spec=pltpu.PrefetchScalarGridSpec(
+            num_scalar_prefetch=1,
+            grid=(1,),
+            in_specs=[pl.BlockSpec(memory_space=pl.ANY)] * len(flat),
+            out_specs=[pl.BlockSpec(memory_space=pl.ANY)] * 4,
+            scratch_shapes=[pltpu.SemaphoreType.DMA((4,))],
+        ),
+        cost_estimate=FREE,
+        compiler_params=PARAMS,
+        name="lay_out",
+    )(jnp.stack([x, y, c, z]).astype(jnp.int32), *flat)
+
+
+def weight_product(pieces, contexts):
+    count, tile = len(pieces), 640
+    height, rows = pieces[0].shape[0] // 2, pieces[0].shape[1]
+    width = contexts[0].shape[1]
 
     def body(*refs):
         total = sum(
-            jnp.dot(refs[i][...], refs[count + i][...], preferred_element_type=F32)
+            jnp.dot(
+                refs[i][core * height : (core + 1) * height, :],
+                refs[count + i][core * rows : (core + 1) * rows, :],
+                preferred_element_type=F32,
+            )
             for i in range(count)
-        )
-        if before is not None:
-            total = total + refs[2 * count][...].astype(F32)
+            for core in (0, 1)
+        )
         refs[-1][...] = total.astype(BF16)
 
-    in_specs = [pl.BlockSpec((height, rows), lambda n: (0, 0)) for _ in pieces]
-    in_specs += [pl.BlockSpec((rows, tile), lambda n: (0, n)) for _ in contexts]
-    operands = list(pieces) + list(contexts)
-    if before is not None:
-        in_specs.append(pl.BlockSpec((height, tile), lambda n: (0, n)))
-        operands.append(before)
     return pl.pallas_call(
         body,
         out_shape=jax.ShapeDtypeStruct((height, width), BF16),
         grid=(width // tile,),
-        in_specs=in_specs,
+        in_specs=[pl.BlockSpec((2 * height, rows), lambda n: (0, 0)) for _ in pieces]
+        + [pl.BlockSpec((2 * rows, tile), lambda n: (0, n)) for _ in contexts],
         out_specs=pl.BlockSpec((height, tile), lambda n: (0, n)),
         cost_estimate=FREE,
         compiler_params=PARAMS,
         name="weight_product",
-    )(*operands)
+    )(*pieces, *contexts)
 
 
 def per_device(
@@ -174,29 +276,22 @@
     live = jnp.arange(LMAX)[None, :] < lengths[:, None]
     row_weights = jnp.where(live, scale[:, None], F32(0.0)).reshape(-1).astype(BF16)
 
-    proj = out_proj.reshape(NZ, width, width)
-
-    def part(step, rows_in):
-        return lax.dot_general(
-            pick(proj, (z + step) % NZ), rows_in, (((1,), (1,)), ((), ())), preferred_element_type=F32
-        )
-
-    far = part(2, context).astype(BF16)
-    near = part(1, lax.optimization_barrier((context, far))[0]).astype(BF16)
-    back = part(3, lax.optimization_barrier((context, near))[0]).astype(BF16)
-    parts = [shift(far, "z", 2), shift(near, "z", 1), shift(back, "z", 3)]
-
-    after, _ = lax.optimization_barrier((context, near))
-    others, selves = [context] * 4, [context] * 4
-    others[1], others[3] = cross(after, 1, True), cross(after, 3, True)
-    after, others[1], others[3] = lax.optimization_barrier((context, others[1], others[3]))
-    own = part(0, after)
-    others[2], selves[1] = cross(after, 2, True), cross(after, 1, False)
-    after, others[2], selves[1] = lax.optimization_barrier((context, others[2], selves[1]))
-    selves[2], selves[3] = cross(after, 2, False), cross(after, 3, False)
-
-    attn_t = own + sum(value.astype(F32) for value in parts)
-    attn_t, others[2], selves[1] = lax.optimization_barrier((attn_t, others[2], selves[1]))
+    top = width // 2
+    far_top, far_bottom = forward_product(out_proj, context, (z + 2) % NZ, True)
+    far_top, far_bottom = shift(far_top, "z", 1), shift(far_bottom, "z", 3)
+    near = forward_product(out_proj, context, (z + 1) % NZ, False)
+    back = forward_product(out_proj, context, (z + 3) % NZ, False)
+    near = jnp.concatenate([near[:top] + far_top.astype(F32), near[top:]], axis=0).astype(BF16)
+    back = jnp.concatenate([back[:top], back[top:] + far_bottom.astype(F32)], axis=0).astype(BF16)
+
+    pair = jnp.concatenate([context, shift(context, "c", 1)], axis=0)
+    contexts = [pair, cross(pair, 1, True), None, cross(pair, 3, True)]
+    after, contexts[1], contexts[3] = lax.optimization_barrier((context, contexts[1], contexts[3]))
+    own = forward_product(out_proj, after, z, False)
+    again, _ = lax.optimization_barrier((pair, own))
+    contexts[2] = cross(again, 2, True)
+
+    attn_t = own + shift(near, "z", 1).astype(F32) + shift(back, "z", 3).astype(F32)
     hidden_t = residual.T.astype(F32) + attn_t
     upstream_t = norm_gain[:, None] * (row_weights.astype(F32)[None, :] * cotangent.T.astype(F32))
     stats = jnp.stack(
@@ -207,49 +302,52 @@
     grad_t = (
         inv_rms[None, :] * upstream_t - hidden_t * (inv_rms**3 * stats[1] / full)[None, :]
     ).astype(BF16)
-    grad_t, selves[2], selves[3] = lax.optimization_barrier((grad_t, selves[2], selves[3]))
+
+    block = width // (NY * NC)
+
+    def swap(value):
+        parted = value.reshape(-1, NC, block, rows)
+        return shift(
+            lax.dynamic_index_in_dim(parted, 1 - c, 1, keepdims=False).reshape(-1, rows), "c", 1
+        )
 
     slots = slot_matrix(destinations[:, 0], lanes * PAIR, rows, 16)
-    top = width // 2
     from_left, from_right = shift(grad_t, "z", 1), shift(grad_t, "z", 3)
+    swapped = swap(grad_t)
     d_residual = exchange(place_rows(slots, grad_t), lanes)
     context_grad = context_product([grad_t], [z], out_proj)
-    from_left, from_right, context_grad = lax.optimization_barrier(
-        (from_left, from_right, context_grad)
+    from_left, from_right, context_grad, swapped, contexts[2] = lax.optimization_barrier(
+        (from_left, from_right, context_grad, swapped, contexts[2])
     )
     far_left, far_right = shift(from_left[:top], "z", 1), shift(from_right[top:], "z", 3)
+    swapped_left, swapped_right = swap(from_left), swap(from_right)
     context_grad = context_product(
         [from_right, from_left], [(z + 1) % NZ, (z + 3) % NZ], out_proj, before=context_grad
     )
-    far_left, far_right, context_grad, d_residual = lax.optimization_barrier(
-        (far_left, far_right, context_grad, d_residual)
+    far_left, far_right, context_grad, swapped_left, swapped_right, d_residual = (
+        lax.optimization_barrier(
+            (far_left, far_right, context_grad, swapped_left, swapped_right, d_residual)
+        )
     )
     far_grad = jnp.concatenate([far_left, far_right], axis=0)
 
-    block = width // (NY * NC)
-    grad_full = jnp.stack([grad_t, from_right, far_grad, from_left]).reshape(NZ, NY, NC, block, rows)
-
-    def set_rows(step, first):
-        along_x = pick(grad_full[:, :, 0], (x + step - z) % NZ)
-        along_y = lax.dynamic_index_in_dim(grad_full[:, :, 1], (y + step) % NY, 1, keepdims=False)
-        return jnp.where((c == 0) == first, along_y, along_x).reshape(-1, rows)
-
-    def gather(first):
-        return [set_rows(0, first)] + [cross(set_rows(k, first), k, first) for k in (1, 2, 3)]
-
-    other_rows, self_rows = gather(True), gather(False)
+    sends = lay_out(
+        [[grad_t], [from_right], [far_left, far_right], [from_left]],
+        [[swapped], [swapped_right], [swap(far_grad)], [swapped_left]],
+        x, y, c, z,
+    )
+    pieces = [sends[0]] + [cross(sends[k], k, True) for k in (1, 2, 3)]
     d_context = exchange(
         context_product([far_grad], [(z + 2) % NZ], out_proj, before=context_grad, slots=slots), lanes
     )
-    other = shift(weight_product(other_rows, others), "c", 1)
-    total = weight_product(self_rows, selves, before=other).reshape(4, block, width)
+    total = weight_product(pieces, contexts).reshape(4, block, width)
 
     def place(step):
         return pick(total, jnp.where(c == 0, (y + step) % NY, (x + step - z) % NZ))
 
     d_out_proj = place(0).astype(F32)
     for k in (1, 2, 3):
-        d_out_proj = d_out_proj + cross(place(k), k, True).astype(F32)
+        d_out_proj = d_out_proj + cross(place(k), k, False).astype(F32)
     return (d_context, d_residual, d_out_proj / lanes)
 
 

time: 207 us -> 214 us (1.034)
  the two profiles are of different devices: /device:TPU:1 before, /device:TPU:14 now
where the time goes in v5:
time: 214 us; the launch traced here: 213 us
  starting transfers between devices  72.6 us (34%)
  Pallas kernels  65.5 us (31%)
  waiting for transfers between devices  40.4 us (19%)
  local copies, waits for them, and re-layouts  23.9 us (11%)
  other arithmetic  9.7 us (5%)
    pallas_call x1, Pallas kernels, lay_out(): pl.pallas_call(body, out_shape=[jax.ShapeDtypeStruct((8 * block, rows), B...  31.6 us
    ppermute x9, starting transfers between devices, cross(): return lax.ppermute(value, DP, pairs)  31 us
    ppermute x9, waiting for transfers between devices, cross(): return lax.ppermute(value, DP, pairs)  21.3 us
    ppermute x16, waiting for transfers between devices, shift(): lax.ppermute(value, axis, [(i, (i + step) % size) for i in range(size)])  19.2 us
    all_to_all x2, starting transfers between devices, exchange(): got = lax.all_to_all(blocks, DP, split_axis=0, concat_axis=0, tiled=True)  17.9 us
    ppermute x16, starting transfers between devices, shift(): lax.ppermute(value, axis, [(i, (i + step) % size) for i in range(size)])  16.2 us
    pallas_call x3, Pallas kernels, context_product(): pl.pallas_call(body, out_shape=jax.ShapeDtypeStruct((out_rows, width), dt...  12.4 us
    pallas_call x4, Pallas kernels, forward_product(): pl.pallas_call(body, out_shape=[jax.ShapeDtypeStruct((tile, rows), BF16)]...  12.4 us
  transfers between devices with their start and end apart: 28, of which 10 were waited for; matrix products, arithmetic and copies ran while one was open for 9% of the time, Pallas kernels for 16%

profile of v5, /device:TPU:14, one launch (start us, length us, event | category | flops | bytes accessed | tf_op | source)
XLA Modules:
  0.0 213.4 jit_solution(1212112588150050048)
XLA Ops:
  2.0 7.5 %all-to-all-start = ((f32[32,1,8]{2,1,0:T(1,128)}), f32[32,1,8]{2,1,0:T(1,128)S(1)}, u32[]{:S(2)}, u32[]{:S(2)}) async-start(f32[32,1,8]{2,1,0:T(1,128)} %broadcast_in_dim.16), calls=%async_computation | async-start | bytes 32768 | tf_op jit(solution)/shard_map/all_to_all | solution.py:42
  9.7 1.1 copy-done
  10.8 3.7 %forward_product.6 = (bf16[640,256]{1,0:T(8,128)(2,1)}, bf16[640,256]{1,0:T(8,128)(2,1)}) custom-call(s32[1]{0:T(128)} %bitcast.which, bf16[5120,1280]{1,0:T(8,128)(2,1)} %refs_1_.3, bf16[256,1280]{1,0:T(8,128)(2,1)S(1)} %copy-done), custom_call_target="tpu_custom_call" | custom-call | tf_op jit(solution)/shard_map/forward_product/pallas_call | solution.py:148
  14.5 1.9 collective-permute-start.3
  16.4 2.1 %collective-permute-start.5 = (bf16[640,256]{1,0:T(8,128)(2,1)}, bf16[640,256]{1,0:T(8,128)(2,1)}, u32[]{:S(2)}, u32[]{:S(2)}) collective-permute-start(bf16[640,256]{1,0:T(8,128)(2,1)} %get-tuple-element.26), channel_id=1, source_target_pairs={{0,3},{1,0},{2,1},{3,2},{4,7},{5,4},{6,5},{7,6},{8,11},{9,8},{10,9... | collective-permute-start | bytes 983048 | tf_op jit(solution)/shard_map/ppermute | solution.py:22
  18.8 2.7 %forward_product.5 = f32[1280,256]{1,0:T(8,128)S(1)} custom-call(s32[1]{0:T(128)} %bitcast.3.which, bf16[5120,1280]{1,0:T(8,128)(2,1)} %refs_1_.3, bf16[256,1280]{1,0:T(8,128)(2,1)S(1)} %copy-done.1), custom_call_target="tpu_custom_call" | custom-call | tf_op jit(solution)/shard_map/forward_product/pallas_call | solution.py:148
  22.3 2.7 %forward_product.7 = f32[1280,256]{1,0:T(8,128)S(1)} custom-call(s32[1]{0:T(128)} %bitcast.4.which, bf16[5120,1280]{1,0:T(8,128)(2,1)} %refs_1_.3, bf16[256,1280]{1,0:T(8,128)(2,1)S(1)} %copy-done.1), custom_call_target="tpu_custom_call" | custom-call | tf_op jit(solution)/shard_map/forward_product/pallas_call | solution.py:148
  25.1 2.0 collective-permute-done.3
  27.1 1.0 fusion.7
  28.2 1.1 constant_dynamic-update-slice_fusion.refs_4_
  30.2 2.4 %collective-permute-start.1 = (bf16[512,1280]{1,0:T(8,128)(2,1)S(1)}, bf16[512,1280]{1,0:T(8,128)(2,1)S(1)}, u32[]{:S(2)}, u32[]{:S(2)}) collective-permute-start(bf16[512,1280]{1,0:T(8,128)(2,1)S(1)} %constant_dynamic-update-slice_fusion.refs_4_), channel_id=1, source_target_pairs={{0,32},{4,12},{8,40},{12,20},{16,48},{20,28},{24,56},{28,4},{32,64... | collective-permute-start | bytes 3932168 | tf_op jit(solution)/shard_map/ppermute | solution.py:37
  33.5 1.0 fusion.6
  35.4 3.2 %collective-permute-start.6 = (bf16[1280,256]{1,0:T(8,128)(2,1)}, bf16[1280,256]{1,0:T(8,128)(2,1)}, u32[]{:S(2)}, u32[]{:S(2)}) collective-permute-start(bf16[1280,256]{1,0:T(8,128)(2,1)} %pad_maximum_fusion.1), channel_id=1, source_target_pairs={{0,3},{1,0},{2,1},{3,2},{4,7},{5,4},{6,5},{7,6},{8,11},{9,8},{10,9... | collective-permute-start | bytes 1966088 | tf_op jit(solution)/shard_map/ppermute | solution.py:22
  38.9 2.2 %copy.32 = bf16[256,1280]{0,1:T(8,128)(2,1)} copy(bf16[256,1280]{1,0:T(8,128)(2,1)} %param.11) | data formatting | bytes 1310720 | tf_op args[2]
  41.1 2.2 %copy.30 = bf16[256,1280]{0,1:T(8,128)(2,1)} copy(bf16[256,1280]{1,0:T(8,128)(2,1)} %param.10) | data formatting | bytes 1310720 | tf_op args[1]
  43.6 4.7 %collective-permute-done.2.refs_7_ = bf16[512,1280]{1,0:T(8,128)(2,1)} collective-permute-done((bf16[512,1280]{1,0:T(8,128)(2,1)S(1)}, bf16[512,1280]{1,0:T(8,128)(2,1)}, u32[]{:S(2)}, u32[]{:S(2)}) %collective-permute-start.2) | collective-permute-done | bytes 1310752 | tf_op jit(solution)/shard_map/ppermute | solution.py:37
  48.3 3.2 %forward_product.4 = f32[1280,256]{1,0:T(8,128)S(1)} custom-call(s32[1]{0:T(128)} %bitcast.2.which, bf16[5120,1280]{1,0:T(8,128)(2,1)} %refs_1_.3, bf16[256,1280]{1,0:T(8,128)(2,1)S(1)} %copy-done.1), custom_call_target="tpu_custom_call" | custom-call | tf_op jit(solution)/shard_map/forward_product/pallas_call | solution.py:148
  51.6 1.9 multiply_reduce_fusion
  53.5 1.6 collective-permute-start.8
  55.1 1.5 collective-permute-start.9
  57.5 1.5 collective-permute-start.13
  59.0 2.4 %collective-permute-done.7 = f32[2,256]{1,0:T(2,128)S(1)} collective-permute-done((f32[2,256]{1,0:T(2,128)S(1)}, f32[2,256]{1,0:T(2,128)S(1)}, u32[]{:S(2)}, u32[]{:S(2)}) %collective-permute-start.7) | collective-permute-done | bytes 2080 | tf_op jit(solution)/shard_map/ppermute | solution.py:22
  61.7 1.7 place_rows.1
  63.4 8.4 %all-to-all-start.1 = ((bf16[32,16,1280]{2,1,0:T(8,128)(2,1)}), bf16[32,16,1280]{2,1,0:T(8,128)(2,1)}, u32[]{:S(2)}, u32[]{:S(2)}) async-start(bf16[32,16,1280]{2,1,0:T(8,128)(2,1)} %bitcast.17), calls=%async_computation.1 | async-start | bytes 2621440 | tf_op jit(solution)/shard_map/all_to_all | solution.py:58
  72.1 1.8 collective-permute-start.10
  74.0 3.0 %context_product.3.refs_4_ = f32[256,1280]{1,0:T(8,128)S(1)} custom-call(s32[1]{0:T(128)} %bitcast.2.which, bf16[1280,256]{1,0:T(8,128)(2,1)S(1)} %fusion.2.refs_0_.grad_ref, bf16[5120,1280]{1,0:T(8,128)(2,1)} %refs_1_.3), custom_call_target="tpu_custom_call" | custom-call | tf_op jit(solution)/shard_map/context_product/pallas_call | solution.py:100
  77.0 11.6 %collective-permute-done.11.refs_0_.refs_1_ = bf16[1280,256]{1,0:T(8,128)(2,1)S(1)} collective-permute-done((bf16[1280,256]{1,0:T(8,128)(2,1)S(1)}, bf16[1280,256]{1,0:T(8,128)(2,1)S(1)}, u32[]{:S(2)}, u32[]{:S(2)}) %collective-permute-start.11) | collective-permute-done | bytes 655392 | tf_op jit(solution)/shard_map/ppermute | solution.py:22
  88.7 1.3 collective-permute-done.10.refs_1_.refs_4_
  92.1 1.4 collective-permute-start.14
  95.6 2.2 %reshape.119 = bf16[384,1280]{1,0:T(8,128)(2,1)} reshape(bf16[32,12,1280]{2,1,0:T(8,128)(2,1)} %bitcast.53) | data formatting | bytes 1966080 | tf_op jit(solution)/shard_map/reshape | solution.py:60
  97.8 1.3 copy-done.4
  99.1 5.1 %context_product.4.refs_2_ = f32[256,1280]{1,0:T(8,128)S(1)} custom-call(s32[2]{0:T(128)S(1)} %pad_add_fusion.which, bf16[1280,256]{1,0:T(8,128)(2,1)S(1)} %collective-permute-done.11.refs_0_.refs_1_, bf16[1280,256]{1,0:T(8,128)(2,1)S(1)} %collective-permute-done.10.refs_1_.refs_4_, bf16[5120,1280]{1,0:T(8,128)(2,1)} %refs_1_.3, bf16[5120,1280]{1,0:T(8,128)(2,1)} %refs_1_.3, ...), custom_call_target="tpu_custom_call" | custom-call | tf_op jit(solution)/shard_map/context_product/pallas_call | solution.py:100
  105.2 1.0 constant_dynamic-update-slice_fusion.2.refs_0_
  107.1 1.8 collective-permute-done.18.refs_7_
  109.9 31.6 %lay_out.1 = (bf16[1280,256]{1,0:T(8,128)(2,1)S(1)}, bf16[1280,256]{1,0:T(8,128)(2,1)}, bf16[1280,256]{1,0:T(8,128)(2,1)}, bf16[1280,256]{1,0:T(8,128)(2,1)}) custom-call(s32[4]{0:T(128)S(1)} %pad_add_fusion.1.where, bf16[1280,256]{1,0:T(8,128)(2,1)S(1)} %fusion.2.refs_0_.grad_ref, bf16[1280,256]{1,0:T(8,128)(2,1)S(1)} %collective-permute-done.11.refs_0_.refs_1_, ...), custom_call_target="tpu_custom_call" | custom-call | tf_op jit(solution)/shard_map/lay_out/pallas_call | solution.py:217
  142.4 20.8 %collective-permute-start.19 = (bf16[1280,256]{1,0:T(8,128)(2,1)}, bf16[1280,256]{1,0:T(8,128)(2,1)}, u32[]{:S(2)}, u32[]{:S(2)}) collective-permute-start(bf16[1280,256]{1,0:T(8,128)(2,1)} %get-tuple-element.39), channel_id=1, source_target_pairs={{0,32},{4,12},{8,40},{12,20},{16,48},{20,28},{24,56},{28,4},{32,64... | collective-permute-start | bytes 1966088 | tf_op jit(solution)/shard_map/ppermute | solution.py:37
  164.0 4.4 %context_product.5 = bf16[512,1280]{1,0:T(8,128)(2,1)} custom-call(s32[1]{0:T(128)} %bitcast.which, bf16[1280,256]{1,0:T(8,128)(2,1)S(1)} %constant_dynamic-update-slice_fusion.2.refs_0_, bf16[5120,1280]{1,0:T(8,128)(2,1)} %refs_1_.3, f32[256,1280]{1,0:T(8,128)S(1)} %context_product.4.refs_2_, bf16[512,256]{1,0:T(8,128)(2,1)S(1)} %fusion.8.slots_ref.refs_3_), custom_call_target="tpu_custom_call" | custom-call | tf_op jit(solution)/shard_map/context_product/pallas_call | solution.py:100
  168.4 9.5 %all-to-all-start.2 = ((bf16[32,16,1280]{2,1,0:T(8,128)(2,1)}), bf16[32,16,1280]{2,1,0:T(8,128)(2,1)}, u32[]{:S(2)}, u32[]{:S(2)}) async-start(bf16[32,16,1280]{2,1,0:T(8,128)(2,1)} %bitcast.18), calls=%async_computation.2 | async-start | bytes 2621440 | tf_op jit(solution)/shard_map/all_to_all | solution.py:58
  178.6 7.6 %collective-permute-done.21.refs_3_ = bf16[1280,256]{1,0:T(8,128)(2,1)} collective-permute-done((bf16[1280,256]{1,0:T(8,128)(2,1)}, bf16[1280,256]{1,0:T(8,128)(2,1)}, u32[]{:S(2)}, u32[]{:S(2)}) %collective-permute-start.21) | collective-permute-done | bytes 655392 | tf_op jit(solution)/shard_map/ppermute | solution.py:37
  186.2 1.1 copy-done.10
  187.3 7.4 %weight_product.1 = bf16[640,1280]{1,0:T(8,128)(2,1)} custom-call(bf16[1280,256]{1,0:T(8,128)(2,1)S(1)} %copy-done.10, bf16[1280,256]{1,0:T(8,128)(2,1)} %collective-permute-done.19.refs_1_, bf16[1280,256]{1,0:T(8,128)(2,1)} %collective-permute-done.20.refs_2_, bf16[1280,256]{1,0:T(8,128)(2,1)} %collective-permute-done.21.refs_3_, ...), custom_call_target="tpu_custom_call" | custom-call | tf_op jit(solution)/shard_map/weight_product/pallas_call | solution.py:250
  194.8 1.3 dynamic-slice_bitcast_fusion.2
  196.1 2.9 %collective-permute-start.22 = (bf16[160,1280]{1,0:T(8,128)(2,1)S(1)}, bf16[160,1280]{1,0:T(8,128)(2,1)S(1)}, u32[]{:S(2)}, u32[]{:S(2)}) collective-permute-start(bf16[160,1280]{1,0:T(8,128)(2,1)S(1)} %get-tuple-element.50), channel_id=1, source_target_pairs={{0,8},{4,36},{8,16},{12,44},{16,24},{20,52},{24,0},{28,60},{32,40}... | collective-permute-start | bytes 1228808 | tf_op jit(solution)/shard_map/ppermute | solution.py:37
  198.9 1.7 collective-permute-start.23
  200.7 2.2 %reshape.121 = bf16[384,1280]{1,0:T(8,128)(2,1)} reshape(bf16[32,12,1280]{2,1,0:T(8,128)(2,1)} %bitcast.54) | data formatting | bytes 1966080 | tf_op jit(solution)/shard_map/reshape | solution.py:60
  202.9 5.9 %collective-permute-done.22 = bf16[160,1280]{1,0:T(8,128)(2,1)S(1)} collective-permute-done((bf16[160,1280]{1,0:T(8,128)(2,1)S(1)}, bf16[160,1280]{1,0:T(8,128)(2,1)S(1)}, u32[]{:S(2)}, u32[]{:S(2)}) %collective-permute-start.22) | collective-permute-done | bytes 409632 | tf_op jit(solution)/shard_map/ppermute | solution.py:37
  208.8 2.5 %collective-permute-done.24 = bf16[160,1280]{1,0:T(8,128)(2,1)S(1)} collective-permute-done((bf16[160,1280]{1,0:T(8,128)(2,1)S(1)}, bf16[160,1280]{1,0:T(8,128)(2,1)S(1)}, u32[]{:S(2)}, u32[]{:S(2)}) %collective-permute-start.24) | collective-permute-done | bytes 409632 | tf_op jit(solution)/shard_map/ppermute | solution.py:37
  211.3 2.1 fusion.5
  (101 shorter events, 16.9 us)
Async XLA Ops:
  2.0 41.2 %all-to-all-start = ((f32[32,1,8]{2,1,0:T(1,128)}), f32[32,1,8]{2,1,0:T(1,128)S(1)}, u32[]{:S(2)}, u32[]{:S(2)}) async-start(f32[32,1,8]{2,1,0:T(1,128)} %broadcast_in_dim.16), calls=%async_computation | async-start | bytes 32768 | tf_op jit(solution)/shard_map/all_to_all | solution.py:42
  9.5 18.6 %collective-permute-start = (bf16[256,1280]{1,0:T(8,128)(2,1)}, bf16[256,1280]{1,0:T(8,128)(2,1)}, u32[]{:S(2)}, u32[]{:S(2)}) collective-permute-start(bf16[256,1280]{1,0:T(8,128)(2,1)} %context_ref.6), channel_id=1, source_target_pairs={{0,4},{4,0},{1,5},{5,1},{2,6},{6,2},{3,7},{7,3},{8,12},{12,8},{9,1... | collective-permute-start | bytes 1966088 | tf_op jit(solution)/shard_map/ppermute | solution.py:22
  9.7 1.1 copy-start
  10.8 7.7 %copy-start.19 = (s32[64,1]{0,1:T(1,128)S(1)}, s32[64,1]{0,1:T(1,128)}, u32[]{:S(2)}) copy-start(s32[64,1]{0,1:T(1,128)} %param.17) | copy-start | bytes 772
  10.8 7.9 %copy-start.1 = (bf16[256,1280]{1,0:T(8,128)(2,1)S(1)}, bf16[256,1280]{1,0:T(8,128)(2,1)}, u32[]{:S(2)}) copy-start(bf16[256,1280]{1,0:T(8,128)(2,1)} %context_ref.6) | copy-start | bytes 1966084
  14.5 12.6 %collective-permute-start.3 = (bf16[640,256]{1,0:T(8,128)(2,1)}, bf16[640,256]{1,0:T(8,128)(2,1)}, u32[]{:S(2)}, u32[]{:S(2)}) collective-permute-start(bf16[640,256]{1,0:T(8,128)(2,1)} %get-tuple-element.25), channel_id=1, source_target_pairs={{0,1},{1,2},{2,3},{3,0},{4,5},{5,6},{6,7},{7,4},{8,9},{9,10},{10,1... | collective-permute-start | bytes 983048 | tf_op jit(solution)/shard_map/ppermute | solution.py:22
  16.4 17.1 %collective-permute-start.5 = (bf16[640,256]{1,0:T(8,128)(2,1)}, bf16[640,256]{1,0:T(8,128)(2,1)}, u32[]{:S(2)}, u32[]{:S(2)}) collective-permute-start(bf16[640,256]{1,0:T(8,128)(2,1)} %get-tuple-element.26), channel_id=1, source_target_pairs={{0,3},{1,0},{2,1},{3,2},{4,7},{5,4},{6,5},{7,6},{8,11},{9,8},{10,9... | collective-permute-start | bytes 983048 | tf_op jit(solution)/shard_map/ppermute | solution.py:22
  25.1 7.5 %copy-start.15 = (bf16[640,256]{1,0:T(8,128)(2,1)S(1)}, bf16[640,256]{1,0:T(8,128)(2,1)}, u32[]{:S(2)}) copy-start(bf16[640,256]{1,0:T(8,128)(2,1)} %slice.67) | copy-start | bytes 983044
  29.3 28.2 %copy-start.5 = (bf16[512,1280]{1,0:T(8,128)(2,1)}, bf16[512,1280]{1,0:T(8,128)(2,1)S(1)}, u32[]{:S(2)}) copy-start(bf16[512,1280]{1,0:T(8,128)(2,1)S(1)} %constant_dynamic-update-slice_fusion.refs_4_) | copy-start | bytes 3932164
  29.3 19.0 %collective-permute-start.2 = (bf16[512,1280]{1,0:T(8,128)(2,1)S(1)}, bf16[512,1280]{1,0:T(8,128)(2,1)}, u32[]{:S(2)}, u32[]{:S(2)}) collective-permute-start(bf16[512,1280]{1,0:T(8,128)(2,1)S(1)} %constant_dynamic-update-slice_fusion.refs_4_), channel_id=1, source_target_pairs={{0,96},{4,28},{8,104},{12,4},{16,112},{20,12},{24,120},{28,20},{32... | collective-permute-start | bytes 3932168 | tf_op jit(solution)/shard_map/ppermute | solution.py:37
  30.2 18.1 %collective-permute-start.1 = (bf16[512,1280]{1,0:T(8,128)(2,1)S(1)}, bf16[512,1280]{1,0:T(8,128)(2,1)S(1)}, u32[]{:S(2)}, u32[]{:S(2)}) collective-permute-start(bf16[512,1280]{1,0:T(8,128)(2,1)S(1)} %constant_dynamic-update-slice_fusion.refs_4_), channel_id=1, source_target_pairs={{0,32},{4,12},{8,40},{12,20},{16,48},{20,28},{24,56},{28,4},{32,64... | collective-permute-start | bytes 3932168 | tf_op jit(solution)/shard_map/ppermute | solution.py:37
  33.5 18.1 %collective-permute-start.4 = (bf16[1280,256]{1,0:T(8,128)(2,1)}, bf16[1280,256]{1,0:T(8,128)(2,1)}, u32[]{:S(2)}, u32[]{:S(2)}) collective-permute-start(bf16[1280,256]{1,0:T(8,128)(2,1)} %pad_maximum_fusion), channel_id=1, source_target_pairs={{0,1},{1,2},{2,3},{3,0},{4,5},{5,6},{6,7},{7,4},{8,9},{9,10},{10,1... | collective-permute-start | bytes 1966088 | tf_op jit(solution)/shard_map/ppermute | solution.py:22
  35.4 16.2 %collective-permute-start.6 = (bf16[1280,256]{1,0:T(8,128)(2,1)}, bf16[1280,256]{1,0:T(8,128)(2,1)}, u32[]{:S(2)}, u32[]{:S(2)}) collective-permute-start(bf16[1280,256]{1,0:T(8,128)(2,1)} %pad_maximum_fusion.1), channel_id=1, source_target_pairs={{0,3},{1,0},{2,1},{3,2},{4,7},{5,4},{6,5},{7,6},{8,11},{9,8},{10,9... | collective-permute-start | bytes 1966088 | tf_op jit(solution)/shard_map/ppermute | solution.py:22
  38.8 4.4 %copy-start.20 = (s32[4]{0:T(128)S(1)}, s32[4]{0:T(128)}, u32[]{:S(2)}) copy-start(s32[4]{0:T(128)} %param.15) | copy-start | bytes 52
  38.8 4.6 %copy-start.17 = (s32[4]{0:T(128)S(1)}, s32[4]{0:T(128)}, u32[]{:S(2)}) copy-start(s32[4]{0:T(128)} %param.16) | copy-start | bytes 52
  38.9 4.6 %copy-start.18 = (f32[4]{0:T(128)S(1)}, f32[4]{0:T(128)}, u32[]{:S(2)}) copy-start(f32[4]{0:T(128)} %param.14) | copy-start | bytes 52
  48.3 3.3 %copy-start.7 = (bf16[512,1280]{1,0:T(8,128)(2,1)}, bf16[512,1280]{1,0:T(8,128)(2,1)S(1)}, u32[]{:S(2)}) copy-start(bf16[512,1280]{1,0:T(8,128)(2,1)S(1)} %collective-permute-done.1.refs_5_) | copy-start | bytes 3932164
  48.3 3.3 %copy-start.13 = (bf16[256,1280]{0,1:T(8,128)(2,1)S(1)}, bf16[256,1280]{0,1:T(8,128)(2,1)}, u32[]{:S(2)}) copy-start(bf16[256,1280]{0,1:T(8,128)(2,1)} %copy.32) | copy-start | bytes 1966084
  48.3 3.3 %copy-start.14 = (bf16[256,1280]{0,1:T(8,128)(2,1)S(1)}, bf16[256,1280]{0,1:T(8,128)(2,1)}, u32[]{:S(2)}) copy-start(bf16[256,1280]{0,1:T(8,128)(2,1)} %copy.30) | copy-start | bytes 1966084
  48.3 3.3 %copy-start.16 = (f32[1280]{0:T(1024)S(1)}, f32[1280]{0:T(1024)}, u32[]{:S(2)}) copy-start(f32[1280]{0:T(1024)} %param.13) | copy-start | bytes 15364
  53.5 5.5 %collective-permute-start.8 = (f32[2,256]{1,0:T(2,128)S(1)}, f32[2,256]{1,0:T(2,128)S(1)}, u32[]{:S(2)}, u32[]{:S(2)}) collective-permute-start(f32[2,256]{1,0:T(2,128)S(1)} %pad_maximum_fusion.2), channel_id=1, source_target_pairs={{0,2},{1,3},{2,0},{3,1},{4,6},{5,7},{6,4},{7,5},{8,10},{9,11},{10,... | collective-permute-start | bytes 6152 | tf_op jit(solution)/shard_map/ppermute | solution.py:22
  55.1 3.8 %collective-permute-start.9 = (f32[2,256]{1,0:T(2,128)S(1)}, f32[2,256]{1,0:T(2,128)S(1)}, u32[]{:S(2)}, u32[]{:S(2)}) collective-permute-start(f32[2,256]{1,0:T(2,128)S(1)} %pad_maximum_fusion.2), channel_id=1, source_target_pairs={{0,3},{1,0},{2,1},{3,2},{4,7},{5,4},{6,5},{7,6},{8,11},{9,8},{10,9... | collective-permute-start | bytes 6152 | tf_op jit(solution)/shard_map/ppermute | solution.py:22
  56.6 4.8 %collective-permute-start.7 = (f32[2,256]{1,0:T(2,128)S(1)}, f32[2,256]{1,0:T(2,128)S(1)}, u32[]{:S(2)}, u32[]{:S(2)}) collective-permute-start(f32[2,256]{1,0:T(2,128)S(1)} %pad_maximum_fusion.2), channel_id=1, source_target_pairs={{0,1},{1,2},{2,3},{3,0},{4,5},{5,6},{6,7},{7,4},{8,9},{9,10},{10,1... | collective-permute-start | bytes 6152 | tf_op jit(solution)/shard_map/ppermute | solution.py:22
  57.5 32.5 %collective-permute-start.13 = (bf16[512,1280]{1,0:T(8,128)(2,1)S(1)}, bf16[512,1280]{1,0:T(8,128)(2,1)}, u32[]{:S(2)}, u32[]{:S(2)}) collective-permute-start(bf16[512,1280]{1,0:T(8,128)(2,1)S(1)} %constant_dynamic-update-slice_fusion.refs_4_), channel_id=1, source_target_pairs={{0,64},{4,20},{8,72},{12,28},{16,80},{20,4},{24,88},{28,12},{32,96... | collective-permute-start | bytes 3932168 | tf_op jit(solution)/shard_map/ppermute | solution.py:37
  63.4 32.2 %all-to-all-start.1 = ((bf16[32,16,1280]{2,1,0:T(8,128)(2,1)}), bf16[32,16,1280]{2,1,0:T(8,128)(2,1)}, u32[]{:S(2)}, u32[]{:S(2)}) async-start(bf16[32,16,1280]{2,1,0:T(8,128)(2,1)} %bitcast.17), calls=%async_computation.1 | async-start | bytes 2621440 | tf_op jit(solution)/shard_map/all_to_all | solution.py:58
  71.8 16.9 %collective-permute-start.11 = (bf16[1280,256]{1,0:T(8,128)(2,1)S(1)}, bf16[1280,256]{1,0:T(8,128)(2,1)S(1)}, u32[]{:S(2)}, u32[]{:S(2)}) collective-permute-start(bf16[1280,256]{1,0:T(8,128)(2,1)S(1)} %fusion.2.refs_0_.grad_ref), channel_id=1, source_target_pairs={{0,3},{1,0},{2,1},{3,2},{4,7},{5,4},{6,5},{7,6},{8,11},{9,8},{10,9... | collective-permute-start | bytes 1966088 | tf_op jit(solution)/shard_map/ppermute | solution.py:22
  72.1 17.8 %collective-permute-start.10 = (bf16[1280,256]{1,0:T(8,128)(2,1)S(1)}, bf16[1280,256]{1,0:T(8,128)(2,1)S(1)}, u32[]{:S(2)}, u32[]{:S(2)}) collective-permute-start(bf16[1280,256]{1,0:T(8,128)(2,1)S(1)} %fusion.2.refs_0_.grad_ref), channel_id=1, source_target_pairs={{0,1},{1,2},{2,3},{3,0},{4,5},{5,6},{6,7},{7,4},{8,9},{9,10},{10,1... | collective-permute-start | bytes 1966088 | tf_op jit(solution)/shard_map/ppermute | solution.py:22
  73.9 3.1 %collective-permute-start.12 = (bf16[640,256]{1,0:T(8,128)(2,1)S(1)}, bf16[640,256]{1,0:T(8,128)(2,1)S(1)}, u32[]{:S(2)}, u32[]{:S(2)}) collective-permute-start(bf16[640,256]{1,0:T(8,128)(2,1)S(1)} %bitcast.61), channel_id=1, source_target_pairs={{0,4},{4,0},{1,5},{5,1},{2,6},{6,2},{3,7},{7,3},{8,12},{12,8},{9,1... | collective-permute-start | bytes 983048 | tf_op jit(solution)/shard_map/ppermute | solution.py:22
  77.0 18.0 %copy-start.3 = (f32[256,1280]{1,0:T(8,128)}, f32[256,1280]{1,0:T(8,128)S(1)}, u32[]{:S(2)}) copy-start(f32[256,1280]{1,0:T(8,128)S(1)} %context_product.3.refs_4_) | copy-start | bytes 3932164
  77.0 18.0 %copy-start.11 = (bf16[640,256]{1,0:T(8,128)(2,1)}, bf16[640,256]{1,0:T(8,128)(2,1)S(1)}, u32[]{:S(2)}) copy-start(bf16[640,256]{1,0:T(8,128)(2,1)S(1)} %collective-permute-done.12.refs_5_) | copy-start | bytes 983044
  90.0 7.8 %copy-start.2 = (bf16[1280,256]{1,0:T(8,128)(2,1)}, bf16[1280,256]{1,0:T(8,128)(2,1)S(1)}, u32[]{:S(2)}) copy-start(bf16[1280,256]{1,0:T(8,128)(2,1)S(1)} %collective-permute-done.10.refs_1_.refs_4_) | copy-start | bytes 1966084
  91.5 12.7 %collective-permute-start.15 = (bf16[640,256]{1,0:T(8,128)(2,1)}, bf16[640,256]{1,0:T(8,128)(2,1)}, u32[]{:S(2)}, u32[]{:S(2)}) collective-permute-start(bf16[640,256]{1,0:T(8,128)(2,1)} %slice.39), channel_id=1, source_target_pairs={{0,3},{1,0},{2,1},{3,2},{4,7},{5,4},{6,5},{7,6},{8,11},{9,8},{10,9... | collective-permute-start | bytes 983048 | tf_op jit(solution)/shard_map/ppermute | solution.py:22
  92.1 12.1 %collective-permute-start.14 = (bf16[640,256]{1,0:T(8,128)(2,1)}, bf16[640,256]{1,0:T(8,128)(2,1)}, u32[]{:S(2)}, u32[]{:S(2)}) collective-permute-start(bf16[640,256]{1,0:T(8,128)(2,1)} %slice.38), channel_id=1, source_target_pairs={{0,1},{1,2},{2,3},{3,0},{4,5},{5,6},{6,7},{7,4},{8,9},{9,10},{10,1... | collective-permute-start | bytes 983048 | tf_op jit(solution)/shard_map/ppermute | solution.py:22
  95.0 9.2 %collective-permute-start.16 = (bf16[640,256]{1,0:T(8,128)(2,1)}, bf16[640,256]{1,0:T(8,128)(2,1)}, u32[]{:S(2)}, u32[]{:S(2)}) collective-permute-start(bf16[640,256]{1,0:T(8,128)(2,1)} %bitcast.13), channel_id=1, source_target_pairs={{0,4},{4,0},{1,5},{5,1},{2,6},{6,2},{3,7},{7,3},{8,12},{12,8},{9,1... | collective-permute-start | bytes 983048 | tf_op jit(solution)/shard_map/ppermute | solution.py:22
  95.0 9.2 %collective-permute-start.17 = (bf16[640,256]{1,0:T(8,128)(2,1)}, bf16[640,256]{1,0:T(8,128)(2,1)}, u32[]{:S(2)}, u32[]{:S(2)}) collective-permute-start(bf16[640,256]{1,0:T(8,128)(2,1)} %bitcast.15), channel_id=1, source_target_pairs={{0,4},{4,0},{1,5},{5,1},{2,6},{6,2},{3,7},{7,3},{8,12},{12,8},{9,1... | collective-permute-start | bytes 983048 | tf_op jit(solution)/shard_map/ppermute | solution.py:22
  97.8 1.3 copy-start.4
  107.0 2.0 collective-permute-start.18
  108.9 1.0 copy-start.12
  142.4 36.2 %collective-permute-start.19 = (bf16[1280,256]{1,0:T(8,128)(2,1)}, bf16[1280,256]{1,0:T(8,128)(2,1)}, u32[]{:S(2)}, u32[]{:S(2)}) collective-permute-start(bf16[1280,256]{1,0:T(8,128)(2,1)} %get-tuple-element.39), channel_id=1, source_target_pairs={{0,32},{4,12},{8,40},{12,20},{16,48},{20,28},{24,56},{28,4},{32,64... | collective-permute-start | bytes 1966088 | tf_op jit(solution)/shard_map/ppermute | solution.py:37
  163.1 15.4 %collective-permute-start.20 = (bf16[1280,256]{1,0:T(8,128)(2,1)}, bf16[1280,256]{1,0:T(8,128)(2,1)}, u32[]{:S(2)}, u32[]{:S(2)}) collective-permute-start(bf16[1280,256]{1,0:T(8,128)(2,1)} %get-tuple-element.40), channel_id=1, source_target_pairs={{0,64},{4,20},{8,72},{12,28},{16,80},{20,4},{24,88},{28,12},{32,96... | collective-permute-start | bytes 1966088 | tf_op jit(solution)/shard_map/ppermute | solution.py:37
  163.1 23.1 %collective-permute-start.21 = (bf16[1280,256]{1,0:T(8,128)(2,1)}, bf16[1280,256]{1,0:T(8,128)(2,1)}, u32[]{:S(2)}, u32[]{:S(2)}) collective-permute-start(bf16[1280,256]{1,0:T(8,128)(2,1)} %get-tuple-element.41), channel_id=1, source_target_pairs={{0,96},{4,28},{8,104},{12,4},{16,112},{20,12},{24,120},{28,20},{32... | collective-permute-start | bytes 1966088 | tf_op jit(solution)/shard_map/ppermute | solution.py:37
  168.4 17.8 %copy-start.6 = (bf16[512,1280]{1,0:T(8,128)(2,1)S(1)}, bf16[512,1280]{1,0:T(8,128)(2,1)}, u32[]{:S(2)}) copy-start(bf16[512,1280]{1,0:T(8,128)(2,1)} %copy-done.5) | copy-start | bytes 3932164
  168.4 17.8 %copy-start.8 = (bf16[512,1280]{1,0:T(8,128)(2,1)S(1)}, bf16[512,1280]{1,0:T(8,128)(2,1)}, u32[]{:S(2)}) copy-start(bf16[512,1280]{1,0:T(8,128)(2,1)} %copy-done.7) | copy-start | bytes 3932164
  168.4 32.3 %all-to-all-start.2 = ((bf16[32,16,1280]{2,1,0:T(8,128)(2,1)}), bf16[32,16,1280]{2,1,0:T(8,128)(2,1)}, u32[]{:S(2)}, u32[]{:S(2)}) async-start(bf16[32,16,1280]{2,1,0:T(8,128)(2,1)} %bitcast.18), calls=%async_computation.2 | async-start | bytes 2621440 | tf_op jit(solution)/shard_map/all_to_all | solution.py:58
  186.2 1.1 copy-start.10
  196.1 12.7 %collective-permute-start.22 = (bf16[160,1280]{1,0:T(8,128)(2,1)S(1)}, bf16[160,1280]{1,0:T(8,128)(2,1)S(1)}, u32[]{:S(2)}, u32[]{:S(2)}) collective-permute-start(bf16[160,1280]{1,0:T(8,128)(2,1)S(1)} %get-tuple-element.50), channel_id=1, source_target_pairs={{0,8},{4,36},{8,16},{12,44},{16,24},{20,52},{24,0},{28,60},{32,40}... | collective-permute-start | bytes 1228808 | tf_op jit(solution)/shard_map/ppermute | solution.py:37
  198.9 12.3 %collective-permute-start.24 = (bf16[160,1280]{1,0:T(8,128)(2,1)S(1)}, bf16[160,1280]{1,0:T(8,128)(2,1)S(1)}, u32[]{:S(2)}, u32[]{:S(2)}) collective-permute-start(bf16[160,1280]{1,0:T(8,128)(2,1)S(1)} %get-tuple-element.51), channel_id=1, source_target_pairs={{0,24},{4,100},{8,0},{12,108},{16,8},{20,116},{24,16},{28,124},{32... | collective-permute-start | bytes 1228808 | tf_op jit(solution)/shard_map/ppermute | solution.py:37
  198.9 12.3 %collective-permute-start.23 = (bf16[160,1280]{1,0:T(8,128)(2,1)S(1)}, bf16[160,1280]{1,0:T(8,128)(2,1)S(1)}, u32[]{:S(2)}, u32[]{:S(2)}) collective-permute-start(bf16[160,1280]{1,0:T(8,128)(2,1)S(1)} %get-tuple-element.52), channel_id=1, source_target_pairs={{0,16},{4,68},{8,24},{12,76},{16,0},{20,84},{24,8},{28,92},{32,48}... | collective-permute-start | bytes 1228808 | tf_op jit(solution)/shard_map/ppermute | solution.py:37
  (1 other events, 0.8 us)

commit v6 on v5

--- a/solution.py
+++ b/solution.py
@@ -61,11 +61,11 @@
 
 
 FREE = pl.CostEstimate(flops=0, bytes_accessed=0, transcendentals=0)
-PARAMS = pltpu.CompilerParams(vmem_limit_bytes=48 * 1024 * 1024)
+PARAMS = pltpu.CompilerParams(vmem_limit_bytes=20 * 1024 * 1024)
 
 
 def context_product(chunks, places, out_proj, before=None, slots=None):
-    width, rows = chunks[0].shape
+    width, rows = out_proj.shape[1], chunks[0].shape[1]
     count, tile = len(chunks), 640
     dtype = F32 if slots is None else BF16
 
@@ -84,9 +84,10 @@
             total = jnp.dot(refs[-1][...], total.astype(BF16), preferred_element_type=F32)
         out_ref[...] = total.astype(dtype)
 
-    in_specs = [pl.BlockSpec((width, rows), lambda n, which: (0, 0)) for _ in chunks]
+    in_specs = [pl.BlockSpec(chunk.shape, lambda n, which: (0, 0)) for chunk in chunks]
     in_specs += [
-        pl.BlockSpec((width, tile), lambda n, which, i=i: (which[i], n)) for i in range(count)
+        pl.BlockSpec((chunk.shape[0], tile), lambda n, which, i=i: (which[i], n))
+        for i, chunk in enumerate(chunks)
     ]
     operands = list(chunks) + [out_proj] * count
     out_rows = rows
@@ -221,7 +222,7 @@
             num_scalar_prefetch=1,
             grid=(1,),
             in_specs=[pl.BlockSpec(memory_space=pl.ANY)] * len(flat),
-            out_specs=[pl.BlockSpec(memory_space=pl.ANY)] * 4,
+            out_specs=[pl.BlockSpec((8 * block, rows), lambda i, where: (0, 0))] * 4,
             scratch_shapes=[pltpu.SemaphoreType.DMA((4,))],
         ),
         cost_estimate=FREE,
@@ -268,30 +269,34 @@
     full = width * NZ
     x, y, c, z = (lax.axis_index(axis) for axis in ("x", "y", "c", "z"))
 
+    top = width // 2
+    far_top, far_bottom = forward_product(out_proj, context, (z + 2) % NZ, True)
+    pair = jnp.concatenate(
+        [context, shift(lax.optimization_barrier((context, far_top))[0], "c", 1)], axis=0
+    )
+    far_top, far_bottom = shift(far_top, "z", 1), shift(far_bottom, "z", 3)
+    ready, pair = lax.optimization_barrier((context, pair))
+    near = forward_product(out_proj, ready, (z + 1) % NZ, False)
+    back = forward_product(out_proj, ready, (z + 3) % NZ, False)
+    near = jnp.concatenate([near[:top] + far_top.astype(F32), near[top:]], axis=0).astype(BF16)
+    back = jnp.concatenate([back[:top], back[top:] + far_bottom.astype(F32)], axis=0).astype(BF16)
+
     groups = rewards.shape[0] * lanes // GROUP
     member = (group_ids[:, None] == jnp.arange(groups)[None, :]).astype(F32)
-    group_total = group_sum(jnp.sum(member * rewards[:, None], axis=0))
+    share, _ = lax.optimization_barrier((jnp.sum(member * rewards[:, None], axis=0), near))
+    group_total = group_sum(share)
     advantage = rewards - jnp.sum(member * group_total[None, :], axis=1) / GROUP
     scale = advantage * LMAX / (2.0 * lengths.astype(F32))
     live = jnp.arange(LMAX)[None, :] < lengths[:, None]
     row_weights = jnp.where(live, scale[:, None], F32(0.0)).reshape(-1).astype(BF16)
 
-    top = width // 2
-    far_top, far_bottom = forward_product(out_proj, context, (z + 2) % NZ, True)
-    far_top, far_bottom = shift(far_top, "z", 1), shift(far_bottom, "z", 3)
-    near = forward_product(out_proj, context, (z + 1) % NZ, False)
-    back = forward_product(out_proj, context, (z + 3) % NZ, False)
-    near = jnp.concatenate([near[:top] + far_top.astype(F32), near[top:]], axis=0).astype(BF16)
-    back = jnp.concatenate([back[:top], back[top:] + far_bottom.astype(F32)], axis=0).astype(BF16)
-
-    pair = jnp.concatenate([context, shift(context, "c", 1)], axis=0)
     contexts = [pair, cross(pair, 1, True), None, cross(pair, 3, True)]
-    after, contexts[1], contexts[3] = lax.optimization_barrier((context, contexts[1], contexts[3]))
-    own = forward_product(out_proj, after, z, False)
-    again, _ = lax.optimization_barrier((pair, own))
-    contexts[2] = cross(again, 2, True)
-
+    own = forward_product(out_proj, lax.optimization_barrier((context, near))[0], z, False)
     attn_t = own + shift(near, "z", 1).astype(F32) + shift(back, "z", 3).astype(F32)
+    attn_t, contexts[1], contexts[3] = lax.optimization_barrier(
+        (attn_t, contexts[1], contexts[3])
+    )
+    contexts[2] = cross(lax.optimization_barrier((pair, contexts[1]))[0], 2, True)
     hidden_t = residual.T.astype(F32) + attn_t
     upstream_t = norm_gain[:, None] * (row_weights.astype(F32)[None, :] * cotangent.T.astype(F32))
     stats = jnp.stack(
@@ -305,16 +310,16 @@
 
     block = width // (NY * NC)
 
-    def swap(value):
-        parted = value.reshape(-1, NC, block, rows)
-        return shift(
-            lax.dynamic_index_in_dim(parted, 1 - c, 1, keepdims=False).reshape(-1, rows), "c", 1
-        )
+    def swap(*values):
+        parted = [value.reshape(-1, NC, block, rows) for value in values]
+        asked = [lax.dynamic_index_in_dim(value, 1 - c, 1, keepdims=False) for value in parted]
+        return shift(jnp.concatenate(asked, axis=0).reshape(-1, rows), "c", 1)
 
     slots = slot_matrix(destinations[:, 0], lanes * PAIR, rows, 16)
     from_left, from_right = shift(grad_t, "z", 1), shift(grad_t, "z", 3)
     swapped = swap(grad_t)
-    d_residual = exchange(place_rows(slots, grad_t), lanes)
+    grad_rows, _ = lax.optimization_barrier((grad_t, swapped))
+    d_residual = exchange(place_rows(slots, grad_rows), lanes)
     context_grad = context_product([grad_t], [z], out_proj)
     from_left, from_right, context_grad, swapped, contexts[2] = lax.optimization_barrier(
         (from_left, from_right, context_grad, swapped, contexts[2])
@@ -329,17 +334,17 @@
             (far_left, far_right, context_grad, swapped_left, swapped_right, d_residual)
         )
     )
-    far_grad = jnp.concatenate([far_left, far_right], axis=0)
-
     sends = lay_out(
         [[grad_t], [from_right], [far_left, far_right], [from_left]],
-        [[swapped], [swapped_right], [swap(far_grad)], [swapped_left]],
+        [[swapped], [swapped_right], [swap(far_left, far_right)], [swapped_left]],
         x, y, c, z,
     )
     pieces = [sends[0]] + [cross(sends[k], k, True) for k in (1, 2, 3)]
-    d_context = exchange(
-        context_product([far_grad], [(z + 2) % NZ], out_proj, before=context_grad, slots=slots), lanes
-    )
+    far_place = (z + 2) % NZ * 2
+    placed = context_product(
+        [far_left, far_right], [far_place, far_place + 1], out_proj, before=context_grad, slots=slots
+    )
+    d_context = exchange(placed, lanes)
     total = weight_product(pieces, contexts).reshape(4, block, width)
 
     def place(step):

time: 214 us -> 166 us (0.78)
  the two profiles are of different devices: /device:TPU:14 before, /device:TPU:1 now
where the time goes in v6:
time: 166 us; the launch traced here: 164 us
  starting transfers between devices  56 us (34%)
  local copies, waits for them, and re-layouts  42.1 us (25%)
  Pallas kernels  33.4 us (20%)
  waiting for transfers between devices  21 us (13%)
  other arithmetic  10.7 us (6%)
    unnamed x54, local copies, waits for them, and re-layouts  32.8 us
    ppermute x16, starting transfers between devices, shift(): lax.ppermute(value, axis, [(i, (i + step) % size) for i in range(size)])  19.3 us
    ppermute x9, starting transfers between devices, cross(): return lax.ppermute(value, DP, pairs)  15 us
    all_to_all x2, starting transfers between devices, exchange(): got = lax.all_to_all(blocks, DP, split_axis=0, concat_axis=0, tiled=True)  13.6 us
    ppermute x16, waiting for transfers between devices, shift(): lax.ppermute(value, axis, [(i, (i + step) % size) for i in range(size)])  12 us
    pallas_call x3, Pallas kernels, context_product(): pl.pallas_call(body, out_shape=jax.ShapeDtypeStruct((out_rows, width), dt...  10.6 us
    pallas_call x4, Pallas kernels, forward_product(): pl.pallas_call(body, out_shape=[jax.ShapeDtypeStruct((tile, rows), BF16)]...  9.66 us
    all_to_all x1, starting transfers between devices, group_sum(): lax.all_to_all(copies, DP, split_axis=0, concat_axis=0, tiled=True)  7.99 us
  transfers between devices with their start and end apart: 28, of which 7 were waited for; matrix products, arithmetic and copies ran while one was open for 10% of the time, Pallas kernels for 16%

profile of v6, /device:TPU:1, one launch (start us, length us, event | category | flops | bytes accessed | tf_op | source)
XLA Modules:
  0.0 164.3 jit_solution(9886290030086884612)
XLA Ops:
  0.7 4.7 %copy-done = bf16[5120,1280]{1,0:T(8,128)(2,1)S(1)} copy-done((bf16[5120,1280]{1,0:T(8,128)(2,1)S(1)}, bf16[5120,1280]{1,0:T(8,128)(2,1)}, u32[]{:S(2)}) %copy-start) | copy-done | bytes 13107224
  5.4 2.4 %forward_product.4 = (bf16[640,256]{1,0:T(8,128)(2,1)S(1)}, bf16[640,256]{1,0:T(8,128)(2,1)S(1)}) custom-call(s32[1]{0:T(128)} %bitcast.5.which, bf16[5120,1280]{1,0:T(8,128)(2,1)S(1)} %copy-done, bf16[256,1280]{1,0:T(8,128)(2,1)} %context_ref.4), custom_call_target="tpu_custom_call" | custom-call | tf_op jit(solution)/shard_map/forward_product/pallas_call | solution.py:149
  7.8 1.5 collective-permute-start
  9.3 1.7 %collective-permute-start.1 = (bf16[640,256]{1,0:T(8,128)(2,1)S(1)}, bf16[640,256]{1,0:T(8,128)(2,1)S(1)}, u32[]{:S(2)}, u32[]{:S(2)}) collective-permute-start(bf16[640,256]{1,0:T(8,128)(2,1)S(1)} %get-tuple-element.30), channel_id=1, source_target_pairs={{0,1},{1,2},{2,3},{3,0},{4,5},{5,6},{6,7},{7,4},{8,9},{9,10},{10,1... | collective-permute-start | bytes 983048 | tf_op jit(solution)/shard_map/ppermute | solution.py:22
  11.1 2.1 %collective-permute-start.3 = (bf16[640,256]{1,0:T(8,128)(2,1)S(1)}, bf16[640,256]{1,0:T(8,128)(2,1)S(1)}, u32[]{:S(2)}, u32[]{:S(2)}) collective-permute-start(bf16[640,256]{1,0:T(8,128)(2,1)S(1)} %get-tuple-element.34), channel_id=1, source_target_pairs={{0,3},{1,0},{2,1},{3,2},{4,7},{5,4},{6,5},{7,6},{8,11},{9,8},{10,9... | collective-permute-start | bytes 983048 | tf_op jit(solution)/shard_map/ppermute | solution.py:22
  13.3 1.2 pad_maximum_fusion.refs_4_
  14.4 2.8 %collective-permute-start.6 = (bf16[512,1280]{1,0:T(8,128)(2,1)S(1)}, bf16[512,1280]{1,0:T(8,128)(2,1)}, u32[]{:S(2)}, u32[]{:S(2)}) collective-permute-start(bf16[512,1280]{1,0:T(8,128)(2,1)S(1)} %pad_maximum_fusion.refs_4_), channel_id=1, source_target_pairs={{0,96},{4,28},{8,104},{12,4},{16,112},{20,12},{24,120},{28,20},{32... | collective-permute-start | bytes 3932168 | tf_op jit(solution)/shard_map/ppermute | solution.py:37
  17.3 4.7 %copy-done.1 = bf16[5120,1280]{1,0:T(8,128)(2,1)S(1)} copy-done((bf16[5120,1280]{1,0:T(8,128)(2,1)S(1)}, bf16[5120,1280]{1,0:T(8,128)(2,1)}, u32[]{:S(2)}) %copy-start.1) | copy-done | bytes 13107224
  22.0 2.5 %forward_product.7 = f32[1280,256]{1,0:T(8,128)S(1)} custom-call(s32[1]{0:T(128)} %bitcast.6.which, bf16[5120,1280]{1,0:T(8,128)(2,1)S(1)} %copy-done.1, bf16[256,1280]{1,0:T(8,128)(2,1)} %context_ref.4), custom_call_target="tpu_custom_call" | custom-call | tf_op jit(solution)/shard_map/forward_product/pallas_call | solution.py:149
  25.5 1.8 %collective-permute-start.4 = (bf16[1280,256]{1,0:T(8,128)(2,1)}, bf16[1280,256]{1,0:T(8,128)(2,1)}, u32[]{:S(2)}, u32[]{:S(2)}) collective-permute-start(bf16[1280,256]{1,0:T(8,128)(2,1)} %pad_maximum_fusion.2), channel_id=1, source_target_pairs={{0,3},{1,0},{2,1},{3,2},{4,7},{5,4},{6,5},{7,6},{8,11},{9,8},{10,9... | collective-permute-start | bytes 1966088 | tf_op jit(solution)/shard_map/ppermute | solution.py:22
  27.4 2.3 %forward_product.5 = f32[1280,256]{1,0:T(8,128)S(1)} custom-call(s32[1]{0:T(128)} %bitcast.4.which, bf16[5120,1280]{1,0:T(8,128)(2,1)S(1)} %copy-done.2, bf16[256,1280]{1,0:T(8,128)(2,1)} %context_ref.4), custom_call_target="tpu_custom_call" | custom-call | tf_op jit(solution)/shard_map/forward_product/pallas_call | solution.py:149
  31.4 8.0 %all-to-all-start = ((f32[32,1,8]{2,1,0:T(1,128)}), f32[32,1,8]{2,1,0:T(1,128)S(1)}, u32[]{:S(2)}, u32[]{:S(2)}) async-start(f32[32,1,8]{2,1,0:T(1,128)} %broadcast_in_dim.16), calls=%async_computation | async-start | bytes 32768 | tf_op jit(solution)/shard_map/all_to_all | solution.py:42
  40.9 4.7 %copy-done.3 = bf16[5120,1280]{1,0:T(8,128)(2,1)S(1)} copy-done((bf16[5120,1280]{1,0:T(8,128)(2,1)S(1)}, bf16[5120,1280]{1,0:T(8,128)(2,1)}, u32[]{:S(2)}) %copy-start.3) | copy-done | bytes 13107224
  45.6 2.4 %forward_product.6 = f32[1280,256]{1,0:T(8,128)S(1)} custom-call(s32[1]{0:T(128)} %bitcast.3.which, bf16[5120,1280]{1,0:T(8,128)(2,1)S(1)} %copy-done.3, bf16[256,1280]{1,0:T(8,128)(2,1)} %context_ref.4), custom_call_target="tpu_custom_call" | custom-call | tf_op jit(solution)/shard_map/forward_product/pallas_call | solution.py:149
  48.5 1.5 convert_add_fusion
  51.5 2.9 %collective-permute-start.8 = (f32[2,256]{1,0:T(2,128)S(1)}, f32[2,256]{1,0:T(2,128)S(1)}, u32[]{:S(2)}, u32[]{:S(2)}) collective-permute-start(f32[2,256]{1,0:T(2,128)S(1)} %pad_maximum_fusion.4), channel_id=1, source_target_pairs={{0,2},{1,3},{2,0},{3,1},{4,6},{5,7},{6,4},{7,5},{8,10},{9,11},{10,... | collective-permute-start | bytes 6152 | tf_op jit(solution)/shard_map/ppermute | solution.py:22
  55.9 2.9 %collective-permute-start.13 = (bf16[512,1280]{1,0:T(8,128)(2,1)S(1)}, bf16[512,1280]{1,0:T(8,128)(2,1)}, u32[]{:S(2)}, u32[]{:S(2)}) collective-permute-start(bf16[512,1280]{1,0:T(8,128)(2,1)S(1)} %pad_maximum_fusion.refs_4_), channel_id=1, source_target_pairs={{0,64},{4,20},{8,72},{12,28},{16,80},{20,4},{24,88},{28,12},{32,96... | collective-permute-start | bytes 3932168 | tf_op jit(solution)/shard_map/ppermute | solution.py:37
  58.8 1.7 %fusion.2.refs_0_.grad_ref = bf16[1280,256]{1,0:T(8,128)(2,1)S(1)} fusion(bf16[256,1280]{0,1:T(8,128)(2,1)S(1)} %copy-done.18, f32[256]{0:T(256)S(1)} %bitcast.75, f32[256]{0:T(256)S(1)} %bitcast.76, f32[256]{0:T(256)S(1)} %reshape.131, f32[1280]{0:T(1024)S(1)} %copy-done.21, f32[1280,256]{1,0:T(8,128)} %copy-done.16, bf16[256,1280]{0,1:T(8,128)(2,1)S(1)} %copy.27), kind=kLoop, calls=%fused_computation.5 | loop fusion | flops 2949120 | bytes 3284992 | tf_op jit(solution)/shard_map/convert_element_type | solution.py:309
  60.6 2.0 %collective-permute-start.12 = (bf16[640,256]{1,0:T(8,128)(2,1)S(1)}, bf16[640,256]{1,0:T(8,128)(2,1)S(1)}, u32[]{:S(2)}, u32[]{:S(2)}) collective-permute-start(bf16[640,256]{1,0:T(8,128)(2,1)S(1)} %bitcast.70), channel_id=1, source_target_pairs={{0,4},{4,0},{1,5},{5,1},{2,6},{6,2},{3,7},{7,3},{8,12},{12,8},{9,1... | collective-permute-start | bytes 983048 | tf_op jit(solution)/shard_map/ppermute | solution.py:22
  63.8 1.6 place_rows.1
  65.5 7.6 %all-to-all-start.1 = ((bf16[32,16,1280]{2,1,0:T(8,128)(2,1)}), bf16[32,16,1280]{2,1,0:T(8,128)(2,1)}, u32[]{:S(2)}, u32[]{:S(2)}) async-start(bf16[32,16,1280]{2,1,0:T(8,128)(2,1)} %bitcast.19), calls=%async_computation.1 | async-start | bytes 2621440 | tf_op jit(solution)/shard_map/all_to_all | solution.py:58
  73.1 1.5 collective-permute-start.10
  74.6 4.7 %copy-done.4 = bf16[5120,1280]{1,0:T(8,128)(2,1)S(1)} copy-done((bf16[5120,1280]{1,0:T(8,128)(2,1)S(1)}, bf16[5120,1280]{1,0:T(8,128)(2,1)}, u32[]{:S(2)}) %copy-start.4) | copy-done | bytes 13107224
  79.3 1.8 %context_product.3.refs_4_ = f32[256,1280]{1,0:T(8,128)S(1)} custom-call(s32[1]{0:T(128)} %bitcast.3.which, bf16[1280,256]{1,0:T(8,128)(2,1)S(1)} %fusion.2.refs_0_.grad_ref, bf16[5120,1280]{1,0:T(8,128)(2,1)S(1)} %copy-done.4), custom_call_target="tpu_custom_call" | custom-call | tf_op jit(solution)/shard_map/context_product/pallas_call | solution.py:101
  81.1 8.1 %collective-permute-done.11.refs_0_.refs_1_ = bf16[1280,256]{1,0:T(8,128)(2,1)S(1)} collective-permute-done((bf16[1280,256]{1,0:T(8,128)(2,1)S(1)}, bf16[1280,256]{1,0:T(8,128)(2,1)S(1)}, u32[]{:S(2)}, u32[]{:S(2)}) %collective-permute-start.11) | collective-permute-done | bytes 655392 | tf_op jit(solution)/shard_map/ppermute | solution.py:22
  89.3 1.3 collective-permute-done.10.refs_1_.refs_4_
  92.3 1.2 collective-permute-start.14
  95.0 1.6 collective-permute-start.16
  96.7 3.8 %context_product.4.refs_4_ = f32[256,1280]{1,0:T(8,128)S(1)} custom-call(s32[2]{0:T(128)S(1)} %pad_add_fusion.1.which, bf16[1280,256]{1,0:T(8,128)(2,1)S(1)} %collective-permute-done.11.refs_0_.refs_1_, bf16[1280,256]{1,0:T(8,128)(2,1)S(1)} %collective-permute-done.10.refs_1_.refs_4_, bf16[5120,1280]{1,0:T(8,128)(2,1)S(1)} %copy-done.4, ...), custom_call_target="tpu_custom_call" | custom-call | tf_op jit(solution)/shard_map/context_product/pallas_call | solution.py:101
  100.5 2.2 %reshape.124 = bf16[384,1280]{1,0:T(8,128)(2,1)} reshape(bf16[32,12,1280]{2,1,0:T(8,128)(2,1)} %bitcast.63) | data formatting | bytes 1966080 | tf_op jit(solution)/shard_map/reshape | solution.py:60
  104.5 1.2 collective-permute-start.18
  105.8 1.5 collective-permute-done.18.refs_7_
  108.3 5.2 %lay_out.1 = (bf16[1280,256]{1,0:T(8,128)(2,1)S(1)}, bf16[1280,256]{1,0:T(8,128)(2,1)}, bf16[1280,256]{1,0:T(8,128)(2,1)}, bf16[1280,256]{1,0:T(8,128)(2,1)}) custom-call(s32[4]{0:T(128)S(1)} %pad_add_fusion.2.where, bf16[1280,256]{1,0:T(8,128)(2,1)S(1)} %fusion.2.refs_0_.grad_ref, bf16[1280,256]{1,0:T(8,128)(2,1)S(1)} %collective-permute-done.11.refs_0_.refs_1_, ...), custom_call_target="tpu_custom_call" | custom-call | tf_op jit(solution)/shard_map/lay_out/pallas_call | solution.py:218
  114.3 1.3 collective-permute-start.19
  115.6 2.3 %collective-permute-start.20 = (bf16[1280,256]{1,0:T(8,128)(2,1)}, bf16[1280,256]{1,0:T(8,128)(2,1)S(1)}, u32[]{:S(2)}, u32[]{:S(2)}) collective-permute-start(bf16[1280,256]{1,0:T(8,128)(2,1)} %get-tuple-element.53), channel_id=1, source_target_pairs={{0,64},{4,20},{8,72},{12,28},{16,80},{20,4},{24,88},{28,12},{32,96... | collective-permute-start | bytes 1966088 | tf_op jit(solution)/shard_map/ppermute | solution.py:37
  117.9 1.3 collective-permute-start.21
  119.3 4.7 %copy-done.5 = bf16[5120,1280]{1,0:T(8,128)(2,1)S(1)} copy-done((bf16[5120,1280]{1,0:T(8,128)(2,1)S(1)}, bf16[5120,1280]{1,0:T(8,128)(2,1)}, u32[]{:S(2)}) %copy-start.5) | copy-done | bytes 13107224
  124.0 5.0 %context_product.5 = bf16[512,1280]{1,0:T(8,128)(2,1)} custom-call(s32[2]{0:T(128)S(1)} %pad_add_fusion.which, bf16[640,256]{1,0:T(8,128)(2,1)} %collective-permute-done.14.refs_0_.refs_2_, bf16[640,256]{1,0:T(8,128)(2,1)} %collective-permute-done.15.refs_1_.refs_3_, bf16[5120,1280]{1,0:T(8,128)(2,1)S(1)} %copy-done.5, bf16[5120,1280]{1,0:T(8,128)(2,1)S(1)} %copy-done.5, ...), custom_call_target="tpu_custom_call" | custom-call | tf_op jit(solution)/shard_map/context_product/pallas_call | solution.py:101
  129.0 6.0 %all-to-all-start.2 = ((bf16[32,16,1280]{2,1,0:T(8,128)(2,1)}), bf16[32,16,1280]{2,1,0:T(8,128)(2,1)}, u32[]{:S(2)}, u32[]{:S(2)}) async-start(bf16[32,16,1280]{2,1,0:T(8,128)(2,1)} %bitcast.20), calls=%async_computation.2 | async-start | bytes 2621440 | tf_op jit(solution)/shard_map/all_to_all | solution.py:58
  136.8 1.1 copy-done.9
  140.1 6.3 %weight_product.1 = bf16[640,1280]{1,0:T(8,128)(2,1)S(1)} custom-call(bf16[1280,256]{1,0:T(8,128)(2,1)S(1)} %copy-done.9, bf16[1280,256]{1,0:T(8,128)(2,1)S(1)} %copy-done.11, bf16[1280,256]{1,0:T(8,128)(2,1)S(1)} %copy-done.13, bf16[1280,256]{1,0:T(8,128)(2,1)} %collective-permute-done.21.refs_3_, bf16[512,1280]{1,0:T(8,128)(2,1)S(1)} %copy-done.7, ...), custom_call_target="tpu_custom_call" | custom-call | tf_op jit(solution)/shard_map/weight_product/pallas_call | solution.py:251
  146.5 1.5 collective-permute-start.22
  148.0 1.3 collective-permute-start.24
  149.3 1.6 collective-permute-start.23
  150.9 4.0 %all-to-all-done.2 = bf16[32,16,1280]{2,1,0:T(8,128)(2,1)} async-done(((bf16[32,16,1280]{2,1,0:T(8,128)(2,1)}), bf16[32,16,1280]{2,1,0:T(8,128)(2,1)}, u32[]{:S(2)}, u32[]{:S(2)}) %all-to-all-start.2) | async-done | bytes 1310752 | tf_op jit(solution)/shard_map/all_to_all | solution.py:58
  154.9 2.2 %reshape.126 = bf16[384,1280]{1,0:T(8,128)(2,1)} reshape(bf16[32,12,1280]{2,1,0:T(8,128)(2,1)} %bitcast.64) | data formatting | bytes 1966080 | tf_op jit(solution)/shard_map/reshape | solution.py:60
  157.4 4.7 %collective-permute-done.23 = bf16[160,1280]{1,0:T(8,128)(2,1)} collective-permute-done((bf16[160,1280]{1,0:T(8,128)(2,1)S(1)}, bf16[160,1280]{1,0:T(8,128)(2,1)}, u32[]{:S(2)}, u32[]{:S(2)}) %collective-permute-start.23) | collective-permute-done | bytes 409632 | tf_op jit(solution)/shard_map/ppermute | solution.py:37
  162.1 2.2 %fusion.5 = f32[160,1280]{1,0:T(8,128)} fusion(bf16[160,1280]{1,0:T(8,128)(2,1)} %collective-permute-done.24, bf16[160,1280]{1,0:T(8,128)(2,1)} %collective-permute-done.23, bf16[160,1280]{1,0:T(8,128)(2,1)S(1)} %collective-permute-done.22, bf16[4,160,1280]{2,1,0:T(8,128)(2,1)S(1)} %bitcast.67, s32[]{:T(128)S(6)} %select_n.105), kind=kLoop, calls=%fused_computation.13 | loop fusion | flops 1638400 | bytes 2457604 | tf_op jit(solution)/shard_map/div | solution.py:356
  (111 shorter events, 20.3 us)
Async XLA Ops:
  0.6 4.7 %copy-start = (bf16[5120,1280]{1,0:T(8,128)(2,1)S(1)}, bf16[5120,1280]{1,0:T(8,128)(2,1)}, u32[]{:S(2)}) copy-start(bf16[5120,1280]{1,0:T(8,128)(2,1)} %refs_3_.3) | copy-start | bytes 39321604
  5.4 7.8 %copy-start.23 = (f32[4]{0:T(128)S(1)}, f32[4]{0:T(128)}, u32[]{:S(2)}) copy-start(f32[4]{0:T(128)} %param.14) | copy-start | bytes 52
  5.4 7.8 %copy-start.24 = (s32[4]{0:T(128)S(1)}, s32[4]{0:T(128)}, u32[]{:S(2)}) copy-start(s32[4]{0:T(128)} %param.15) | copy-start | bytes 52
  7.8 5.4 %collective-permute-start = (bf16[256,1280]{1,0:T(8,128)(2,1)}, bf16[256,1280]{1,0:T(8,128)(2,1)S(1)}, u32[]{:S(2)}, u32[]{:S(2)}) collective-permute-start(bf16[256,1280]{1,0:T(8,128)(2,1)} %context_ref.4), channel_id=1, source_target_pairs={{0,4},{4,0},{1,5},{5,1},{2,6},{6,2},{3,7},{7,3},{8,12},{12,8},{9,1... | collective-permute-start | bytes 1966088 | tf_op jit(solution)/shard_map/ppermute | solution.py:22
  9.3 20.5 %collective-permute-start.1 = (bf16[640,256]{1,0:T(8,128)(2,1)S(1)}, bf16[640,256]{1,0:T(8,128)(2,1)S(1)}, u32[]{:S(2)}, u32[]{:S(2)}) collective-permute-start(bf16[640,256]{1,0:T(8,128)(2,1)S(1)} %get-tuple-element.30), channel_id=1, source_target_pairs={{0,1},{1,2},{2,3},{3,0},{4,5},{5,6},{6,7},{7,4},{8,9},{9,10},{10,1... | collective-permute-start | bytes 983048 | tf_op jit(solution)/shard_map/ppermute | solution.py:22
  11.1 13.5 %collective-permute-start.3 = (bf16[640,256]{1,0:T(8,128)(2,1)S(1)}, bf16[640,256]{1,0:T(8,128)(2,1)S(1)}, u32[]{:S(2)}, u32[]{:S(2)}) collective-permute-start(bf16[640,256]{1,0:T(8,128)(2,1)S(1)} %get-tuple-element.34), channel_id=1, source_target_pairs={{0,3},{1,0},{2,1},{3,2},{4,7},{5,4},{6,5},{7,6},{8,11},{9,8},{10,9... | collective-permute-start | bytes 983048 | tf_op jit(solution)/shard_map/ppermute | solution.py:22
  14.4 41.5 %copy-start.6 = (bf16[512,1280]{1,0:T(8,128)(2,1)}, bf16[512,1280]{1,0:T(8,128)(2,1)S(1)}, u32[]{:S(2)}) copy-start(bf16[512,1280]{1,0:T(8,128)(2,1)S(1)} %pad_maximum_fusion.refs_4_) | copy-start | bytes 3932164
  14.4 35.6 %collective-permute-start.6 = (bf16[512,1280]{1,0:T(8,128)(2,1)S(1)}, bf16[512,1280]{1,0:T(8,128)(2,1)}, u32[]{:S(2)}, u32[]{:S(2)}) collective-permute-start(bf16[512,1280]{1,0:T(8,128)(2,1)S(1)} %pad_maximum_fusion.refs_4_), channel_id=1, source_target_pairs={{0,96},{4,28},{8,104},{12,4},{16,112},{20,12},{24,120},{28,20},{32... | collective-permute-start | bytes 3932168 | tf_op jit(solution)/shard_map/ppermute | solution.py:37
  17.3 32.8 %collective-permute-start.5 = (bf16[512,1280]{1,0:T(8,128)(2,1)S(1)}, bf16[512,1280]{1,0:T(8,128)(2,1)}, u32[]{:S(2)}, u32[]{:S(2)}) collective-permute-start(bf16[512,1280]{1,0:T(8,128)(2,1)S(1)} %pad_maximum_fusion.refs_4_), channel_id=1, source_target_pairs={{0,32},{4,12},{8,40},{12,20},{16,48},{20,28},{24,56},{28,4},{32,64... | collective-permute-start | bytes 3932168 | tf_op jit(solution)/shard_map/ppermute | solution.py:37
  17.3 4.7 %copy-start.1 = (bf16[5120,1280]{1,0:T(8,128)(2,1)S(1)}, bf16[5120,1280]{1,0:T(8,128)(2,1)}, u32[]{:S(2)}) copy-start(bf16[5120,1280]{1,0:T(8,128)(2,1)} %refs_3_.3) | copy-start | bytes 39321604
  22.0 5.4 %copy-start.2 = (bf16[5120,1280]{1,0:T(8,128)(2,1)S(1)}, bf16[5120,1280]{1,0:T(8,128)(2,1)}, u32[]{:S(2)}) copy-start(bf16[5120,1280]{1,0:T(8,128)(2,1)} %refs_3_.3) | copy-start | bytes 39321604
  25.5 22.9 %collective-permute-start.4 = (bf16[1280,256]{1,0:T(8,128)(2,1)}, bf16[1280,256]{1,0:T(8,128)(2,1)}, u32[]{:S(2)}, u32[]{:S(2)}) collective-permute-start(bf16[1280,256]{1,0:T(8,128)(2,1)} %pad_maximum_fusion.2), channel_id=1, source_target_pairs={{0,3},{1,0},{2,1},{3,2},{4,7},{5,4},{6,5},{7,6},{8,11},{9,8},{10,9... | collective-permute-start | bytes 1966088 | tf_op jit(solution)/shard_map/ppermute | solution.py:22
  29.8 9.6 %copy-start.25 = (s32[64,1]{0,1:T(1,128)S(1)}, s32[64,1]{0,1:T(1,128)}, u32[]{:S(2)}) copy-start(s32[64,1]{0,1:T(1,128)} %param.17) | copy-start | bytes 772
  29.8 9.8 %copy-start.19 = (bf16[256,1280]{1,0:T(8,128)(2,1)S(1)}, bf16[256,1280]{1,0:T(8,128)(2,1)}, u32[]{:S(2)}) copy-start(bf16[256,1280]{1,0:T(8,128)(2,1)} %param.10) | copy-start | bytes 1966084
  30.8 9.1 %copy-start.20 = (bf16[256,1280]{1,0:T(8,128)(2,1)S(1)}, bf16[256,1280]{1,0:T(8,128)(2,1)}, u32[]{:S(2)}) copy-start(bf16[256,1280]{1,0:T(8,128)(2,1)} %param.11) | copy-start | bytes 1966084
  30.8 17.7 %collective-permute-start.2 = (bf16[1280,256]{1,0:T(8,128)(2,1)}, bf16[1280,256]{1,0:T(8,128)(2,1)}, u32[]{:S(2)}, u32[]{:S(2)}) collective-permute-start(bf16[1280,256]{1,0:T(8,128)(2,1)} %pad_maximum_fusion.1), channel_id=1, source_target_pairs={{0,1},{1,2},{2,3},{3,0},{4,5},{5,6},{6,7},{7,4},{8,9},{9,10},{10,1... | collective-permute-start | bytes 1966088 | tf_op jit(solution)/shard_map/ppermute | solution.py:22
  31.4 16.6 %all-to-all-start = ((f32[32,1,8]{2,1,0:T(1,128)}), f32[32,1,8]{2,1,0:T(1,128)S(1)}, u32[]{:S(2)}, u32[]{:S(2)}) async-start(f32[32,1,8]{2,1,0:T(1,128)} %broadcast_in_dim.16), calls=%async_computation | async-start | bytes 32768 | tf_op jit(solution)/shard_map/all_to_all | solution.py:42
  40.9 4.7 %copy-start.3 = (bf16[5120,1280]{1,0:T(8,128)(2,1)S(1)}, bf16[5120,1280]{1,0:T(8,128)(2,1)}, u32[]{:S(2)}) copy-start(bf16[5120,1280]{1,0:T(8,128)(2,1)} %refs_3_.3) | copy-start | bytes 39321604
  45.6 2.6 %copy-start.22 = (s32[4]{0:T(128)S(1)}, s32[4]{0:T(128)}, u32[]{:S(2)}) copy-start(s32[4]{0:T(128)} %param.16) | copy-start | bytes 52
  48.5 2.7 %copy-start.17 = (bf16[256,1280]{0,1:T(8,128)(2,1)S(1)}, bf16[256,1280]{0,1:T(8,128)(2,1)}, u32[]{:S(2)}) copy-start(bf16[256,1280]{0,1:T(8,128)(2,1)} %copy.29) | copy-start | bytes 1966084
  48.5 2.7 %copy-start.21 = (f32[1280]{0:T(1024)S(1)}, f32[1280]{0:T(1024)}, u32[]{:S(2)}) copy-start(f32[1280]{0:T(1024)} %param.13) | copy-start | bytes 15364
  50.0 1.1 copy-start.16
  50.0 8.8 %copy-start.18 = (bf16[256,1280]{0,1:T(8,128)(2,1)S(1)}, bf16[256,1280]{0,1:T(8,128)(2,1)}, u32[]{:S(2)}) copy-start(bf16[256,1280]{0,1:T(8,128)(2,1)} %copy.29) | copy-start | bytes 1966084
  51.5 7.2 %collective-permute-start.8 = (f32[2,256]{1,0:T(2,128)S(1)}, f32[2,256]{1,0:T(2,128)S(1)}, u32[]{:S(2)}, u32[]{:S(2)}) collective-permute-start(f32[2,256]{1,0:T(2,128)S(1)} %pad_maximum_fusion.4), channel_id=1, source_target_pairs={{0,2},{1,3},{2,0},{3,1},{4,6},{5,7},{6,4},{7,5},{8,10},{9,11},{10,... | collective-permute-start | bytes 6152 | tf_op jit(solution)/shard_map/ppermute | solution.py:22
  54.4 4.4 %collective-permute-start.9 = (f32[2,256]{1,0:T(2,128)S(1)}, f32[2,256]{1,0:T(2,128)S(1)}, u32[]{:S(2)}, u32[]{:S(2)}) collective-permute-start(f32[2,256]{1,0:T(2,128)S(1)} %pad_maximum_fusion.4), channel_id=1, source_target_pairs={{0,3},{1,0},{2,1},{3,2},{4,7},{5,4},{6,5},{7,6},{8,11},{9,8},{10,9... | collective-permute-start | bytes 6152 | tf_op jit(solution)/shard_map/ppermute | solution.py:22
  55.1 3.7 %collective-permute-start.7 = (f32[2,256]{1,0:T(2,128)S(1)}, f32[2,256]{1,0:T(2,128)S(1)}, u32[]{:S(2)}, u32[]{:S(2)}) collective-permute-start(f32[2,256]{1,0:T(2,128)S(1)} %pad_maximum_fusion.4), channel_id=1, source_target_pairs={{0,1},{1,2},{2,3},{3,0},{4,5},{5,6},{6,7},{7,4},{8,9},{9,10},{10,1... | collective-permute-start | bytes 6152 | tf_op jit(solution)/shard_map/ppermute | solution.py:22
  55.9 34.6 %collective-permute-start.13 = (bf16[512,1280]{1,0:T(8,128)(2,1)S(1)}, bf16[512,1280]{1,0:T(8,128)(2,1)}, u32[]{:S(2)}, u32[]{:S(2)}) collective-permute-start(bf16[512,1280]{1,0:T(8,128)(2,1)S(1)} %pad_maximum_fusion.refs_4_), channel_id=1, source_target_pairs={{0,64},{4,20},{8,72},{12,28},{16,80},{20,4},{24,88},{28,12},{32,96... | collective-permute-start | bytes 3932168 | tf_op jit(solution)/shard_map/ppermute | solution.py:37
  60.6 3.2 %collective-permute-start.12 = (bf16[640,256]{1,0:T(8,128)(2,1)S(1)}, bf16[640,256]{1,0:T(8,128)(2,1)S(1)}, u32[]{:S(2)}, u32[]{:S(2)}) collective-permute-start(bf16[640,256]{1,0:T(8,128)(2,1)S(1)} %bitcast.70), channel_id=1, source_target_pairs={{0,4},{4,0},{1,5},{5,1},{2,6},{6,2},{3,7},{7,3},{8,12},{12,8},{9,1... | collective-permute-start | bytes 983048 | tf_op jit(solution)/shard_map/ppermute | solution.py:22
  63.8 1.6 copy-start.14
  65.5 35.0 %all-to-all-start.1 = ((bf16[32,16,1280]{2,1,0:T(8,128)(2,1)}), bf16[32,16,1280]{2,1,0:T(8,128)(2,1)}, u32[]{:S(2)}, u32[]{:S(2)}) async-start(bf16[32,16,1280]{2,1,0:T(8,128)(2,1)} %bitcast.19), calls=%async_computation.1 | async-start | bytes 2621440 | tf_op jit(solution)/shard_map/all_to_all | solution.py:58
  73.0 16.2 %collective-permute-start.11 = (bf16[1280,256]{1,0:T(8,128)(2,1)S(1)}, bf16[1280,256]{1,0:T(8,128)(2,1)S(1)}, u32[]{:S(2)}, u32[]{:S(2)}) collective-permute-start(bf16[1280,256]{1,0:T(8,128)(2,1)S(1)} %fusion.2.refs_0_.grad_ref), channel_id=1, source_target_pairs={{0,3},{1,0},{2,1},{3,2},{4,7},{5,4},{6,5},{7,6},{8,11},{9,8},{10,9... | collective-permute-start | bytes 1966088 | tf_op jit(solution)/shard_map/ppermute | solution.py:22
  73.1 17.4 %collective-permute-start.10 = (bf16[1280,256]{1,0:T(8,128)(2,1)S(1)}, bf16[1280,256]{1,0:T(8,128)(2,1)S(1)}, u32[]{:S(2)}, u32[]{:S(2)}) collective-permute-start(bf16[1280,256]{1,0:T(8,128)(2,1)S(1)} %fusion.2.refs_0_.grad_ref), channel_id=1, source_target_pairs={{0,1},{1,2},{2,3},{3,0},{4,5},{5,6},{6,7},{7,4},{8,9},{9,10},{10,1... | collective-permute-start | bytes 1966088 | tf_op jit(solution)/shard_map/ppermute | solution.py:22
  74.6 4.7 %copy-start.4 = (bf16[5120,1280]{1,0:T(8,128)(2,1)S(1)}, bf16[5120,1280]{1,0:T(8,128)(2,1)}, u32[]{:S(2)}) copy-start(bf16[5120,1280]{1,0:T(8,128)(2,1)} %refs_3_.3) | copy-start | bytes 39321604
  92.0 10.6 %collective-permute-start.15 = (bf16[640,256]{1,0:T(8,128)(2,1)}, bf16[640,256]{1,0:T(8,128)(2,1)}, u32[]{:S(2)}, u32[]{:S(2)}) collective-permute-start(bf16[640,256]{1,0:T(8,128)(2,1)} %slice.39), channel_id=1, source_target_pairs={{0,3},{1,0},{2,1},{3,2},{4,7},{5,4},{6,5},{7,6},{8,11},{9,8},{10,9... | collective-permute-start | bytes 983048 | tf_op jit(solution)/shard_map/ppermute | solution.py:22
  92.3 10.4 %collective-permute-start.14 = (bf16[640,256]{1,0:T(8,128)(2,1)}, bf16[640,256]{1,0:T(8,128)(2,1)}, u32[]{:S(2)}, u32[]{:S(2)}) collective-permute-start(bf16[640,256]{1,0:T(8,128)(2,1)} %slice.38), channel_id=1, source_target_pairs={{0,1},{1,2},{2,3},{3,0},{4,5},{5,6},{6,7},{7,4},{8,9},{9,10},{10,1... | collective-permute-start | bytes 983048 | tf_op jit(solution)/shard_map/ppermute | solution.py:22
  95.0 7.7 %collective-permute-start.16 = (bf16[640,256]{1,0:T(8,128)(2,1)}, bf16[640,256]{1,0:T(8,128)(2,1)}, u32[]{:S(2)}, u32[]{:S(2)}) collective-permute-start(bf16[640,256]{1,0:T(8,128)(2,1)} %bitcast.15), channel_id=1, source_target_pairs={{0,4},{4,0},{1,5},{5,1},{2,6},{6,2},{3,7},{7,3},{8,12},{12,8},{9,1... | collective-permute-start | bytes 983048 | tf_op jit(solution)/shard_map/ppermute | solution.py:22
  96.6 6.1 %collective-permute-start.17 = (bf16[640,256]{1,0:T(8,128)(2,1)}, bf16[640,256]{1,0:T(8,128)(2,1)}, u32[]{:S(2)}, u32[]{:S(2)}) collective-permute-start(bf16[640,256]{1,0:T(8,128)(2,1)} %bitcast.17), channel_id=1, source_target_pairs={{0,4},{4,0},{1,5},{5,1},{2,6},{6,2},{3,7},{7,3},{8,12},{12,8},{9,1... | collective-permute-start | bytes 983048 | tf_op jit(solution)/shard_map/ppermute | solution.py:22
  104.5 2.8 %collective-permute-start.18 = (bf16[640,256]{1,0:T(8,128)(2,1)}, bf16[640,256]{1,0:T(8,128)(2,1)}, u32[]{:S(2)}, u32[]{:S(2)}) collective-permute-start(bf16[640,256]{1,0:T(8,128)(2,1)} %bitcast.28), channel_id=1, source_target_pairs={{0,4},{4,0},{1,5},{5,1},{2,6},{6,2},{3,7},{7,3},{8,12},{12,8},{9,1... | collective-permute-start | bytes 983048 | tf_op jit(solution)/shard_map/ppermute | solution.py:22
  114.3 20.8 %collective-permute-start.19 = (bf16[1280,256]{1,0:T(8,128)(2,1)}, bf16[1280,256]{1,0:T(8,128)(2,1)S(1)}, u32[]{:S(2)}, u32[]{:S(2)}) collective-permute-start(bf16[1280,256]{1,0:T(8,128)(2,1)} %get-tuple-element.52), channel_id=1, source_target_pairs={{0,32},{4,12},{8,40},{12,20},{16,48},{20,28},{24,56},{28,4},{32,64... | collective-permute-start | bytes 1966088 | tf_op jit(solution)/shard_map/ppermute | solution.py:37
  115.6 20.4 %collective-permute-start.20 = (bf16[1280,256]{1,0:T(8,128)(2,1)}, bf16[1280,256]{1,0:T(8,128)(2,1)S(1)}, u32[]{:S(2)}, u32[]{:S(2)}) collective-permute-start(bf16[1280,256]{1,0:T(8,128)(2,1)} %get-tuple-element.53), channel_id=1, source_target_pairs={{0,64},{4,20},{8,72},{12,28},{16,80},{20,4},{24,88},{28,12},{32,96... | collective-permute-start | bytes 1966088 | tf_op jit(solution)/shard_map/ppermute | solution.py:37
  117.9 18.9 %collective-permute-start.21 = (bf16[1280,256]{1,0:T(8,128)(2,1)}, bf16[1280,256]{1,0:T(8,128)(2,1)}, u32[]{:S(2)}, u32[]{:S(2)}) collective-permute-start(bf16[1280,256]{1,0:T(8,128)(2,1)} %get-tuple-element.54), channel_id=1, source_target_pairs={{0,96},{4,28},{8,104},{12,4},{16,112},{20,12},{24,120},{28,20},{32... | collective-permute-start | bytes 1966088 | tf_op jit(solution)/shard_map/ppermute | solution.py:37
  119.3 4.7 %copy-start.5 = (bf16[5120,1280]{1,0:T(8,128)(2,1)S(1)}, bf16[5120,1280]{1,0:T(8,128)(2,1)}, u32[]{:S(2)}) copy-start(bf16[5120,1280]{1,0:T(8,128)(2,1)} %refs_3_.3) | copy-start | bytes 39321604
  129.0 7.8 %copy-start.7 = (bf16[512,1280]{1,0:T(8,128)(2,1)S(1)}, bf16[512,1280]{1,0:T(8,128)(2,1)}, u32[]{:S(2)}) copy-start(bf16[512,1280]{1,0:T(8,128)(2,1)} %copy-done.6) | copy-start | bytes 3932164
  129.0 26.0 %all-to-all-start.2 = ((bf16[32,16,1280]{2,1,0:T(8,128)(2,1)}), bf16[32,16,1280]{2,1,0:T(8,128)(2,1)}, u32[]{:S(2)}, u32[]{:S(2)}) async-start(bf16[32,16,1280]{2,1,0:T(8,128)(2,1)} %bitcast.20), calls=%async_computation.2 | async-start | bytes 2621440 | tf_op jit(solution)/shard_map/all_to_all | solution.py:58
  136.8 1.1 copy-start.9
  146.5 10.9 %collective-permute-start.22 = (bf16[160,1280]{1,0:T(8,128)(2,1)S(1)}, bf16[160,1280]{1,0:T(8,128)(2,1)S(1)}, u32[]{:S(2)}, u32[]{:S(2)}) collective-permute-start(bf16[160,1280]{1,0:T(8,128)(2,1)S(1)} %get-tuple-element.61), channel_id=1, source_target_pairs={{0,8},{4,36},{8,16},{12,44},{16,24},{20,52},{24,0},{28,60},{32,40}... | collective-permute-start | bytes 1228808 | tf_op jit(solution)/shard_map/ppermute | solution.py:37
  148.0 9.4 %collective-permute-start.24 = (bf16[160,1280]{1,0:T(8,128)(2,1)S(1)}, bf16[160,1280]{1,0:T(8,128)(2,1)}, u32[]{:S(2)}, u32[]{:S(2)}) collective-permute-start(bf16[160,1280]{1,0:T(8,128)(2,1)S(1)} %get-tuple-element.62), channel_id=1, source_target_pairs={{0,24},{4,100},{8,0},{12,108},{16,8},{20,116},{24,16},{28,124},{32... | collective-permute-start | bytes 1228808 | tf_op jit(solution)/shard_map/ppermute | solution.py:37
  149.3 12.8 %collective-permute-start.23 = (bf16[160,1280]{1,0:T(8,128)(2,1)S(1)}, bf16[160,1280]{1,0:T(8,128)(2,1)}, u32[]{:S(2)}, u32[]{:S(2)}) collective-permute-start(bf16[160,1280]{1,0:T(8,128)(2,1)S(1)} %get-tuple-element.63), channel_id=1, source_target_pairs={{0,16},{4,68},{8,24},{12,76},{16,0},{20,84},{24,8},{28,92},{32,48}... | collective-permute-start | bytes 1228808 | tf_op jit(solution)/shard_map/ppermute | solution.py:37
  (6 other events, 5.6 us)

commit v7 on v6

--- a/solution.py
+++ b/solution.py
@@ -62,6 +62,7 @@
 
 FREE = pl.CostEstimate(flops=0, bytes_accessed=0, transcendentals=0)
 PARAMS = pltpu.CompilerParams(vmem_limit_bytes=20 * 1024 * 1024)
+WIDE = pltpu.CompilerParams(vmem_limit_bytes=56 * 1024 * 1024)
 
 
 def context_product(chunks, places, out_proj, before=None, slots=None):
@@ -108,7 +109,7 @@
             out_specs=pl.BlockSpec((out_rows, tile), lambda n, which: (0, n)),
         ),
         cost_estimate=FREE,
-        compiler_params=PARAMS,
+        compiler_params=WIDE,
         name="context_product",
     )(jnp.stack(places), *operands)
 
@@ -163,7 +164,7 @@
             else [pl.BlockSpec((tile, rows), lambda i, which: (i, 0))],
         ),
         cost_estimate=FREE,
-        compiler_params=PARAMS,
+        compiler_params=WIDE,
         name="forward_product",
     )(place.reshape(1), out_proj, context)
     return out if split else out[0]
@@ -256,7 +257,7 @@
         + [pl.BlockSpec((2 * rows, tile), lambda n: (0, n)) for _ in contexts],
         out_specs=pl.BlockSpec((height, tile), lambda n: (0, n)),
         cost_estimate=FREE,
-        compiler_params=PARAMS,
+        compiler_params=WIDE,
         name="weight_product",
     )(*pieces, *contexts)
 
@@ -329,10 +330,8 @@
     context_grad = context_product(
         [from_right, from_left], [(z + 1) % NZ, (z + 3) % NZ], out_proj, before=context_grad
     )
-    far_left, far_right, context_grad, swapped_left, swapped_right, d_residual = (
-        lax.optimization_barrier(
-            (far_left, far_right, context_grad, swapped_left, swapped_right, d_residual)
-        )
+    far_left, far_right, context_grad, swapped_left, swapped_right = lax.optimization_barrier(
+        (far_left, far_right, context_grad, swapped_left, swapped_right)
     )
     sends = lay_out(
         [[grad_t], [from_right], [far_left, far_right], [from_left]],
@@ -344,6 +343,7 @@
     placed = context_product(
         [far_left, far_right], [far_place, far_place + 1], out_proj, before=context_grad, slots=slots
     )
+    placed, d_residual = lax.optimization_barrier((placed, d_residual))
     d_context = exchange(placed, lanes)
     total = weight_product(pieces, contexts).reshape(4, block, width)
 

time: 166 us -> 150 us (0.904)
  local copies, waits for them, and re-layouts: 42.1 us -> 13.3 us
  Pallas kernels: 33.4 us -> 48.3 us
  waiting for transfers between devices: 21 us -> 15.8 us
  other arithmetic: 10.7 us -> 13.2 us
    unnamed x54 -> x50, local copies, waits for them, and re-layouts: 32.8 us -> 5.53 us
    ppermute x16, waiting for transfers between devices: 12 us -> 3.11 us  [shift(): lax.ppermute(value, axis, [(i, (i + step) % size) for i in range(size)])]
    pallas_call x3, Pallas kernels: 10.6 us -> 17.6 us  [context_product(): pl.pallas_call(body, out_shape=jax.ShapeDtypeStruct((out_rows, width), dt...]
    pallas_call x4, Pallas kernels: 9.66 us -> 15.1 us  [forward_product(): pl.pallas_call(body, out_shape=[jax.ShapeDtypeStruct((tile, rows), BF16)]...]
    all_to_all x1, waiting for transfers between devices: 0.01 us -> 2.58 us  [group_sum(): lax.all_to_all(copies, DP, split_axis=0, concat_axis=0, tiled=True)]
    another operation x2, other arithmetic: 0.17 us -> 2.38 us
    pallas_call x1, Pallas kernels: 6.34 us -> 8.14 us  [weight_product(): pl.pallas_call(body, out_shape=jax.ShapeDtypeStruct((height, width), BF16...]
  transfers between devices with their start and end apart: 28 -> 28, of which waited for: 7 -> 7; matrix products, arithmetic and copies ran while one was open for 10% -> 13% of each run, Pallas kernels for 16% -> 30%
where the time goes in v7:
time: 150 us; the launch traced here: 149 us
  starting transfers between devices  57.4 us (38%)
  Pallas kernels  48.3 us (32%)
  waiting for transfers between devices  15.8 us (11%)
  local copies, waits for them, and re-layouts  13.3 us (9%)
  other arithmetic  13.2 us (9%)
    ppermute x16, starting transfers between devices, shift(): lax.ppermute(value, axis, [(i, (i + step) % size) for i in range(size)])  21 us
    pallas_call x3, Pallas kernels, context_product(): pl.pallas_call(body, out_shape=jax.ShapeDtypeStruct((out_rows, width), dt...  17.6 us
    pallas_call x4, Pallas kernels, forward_product(): pl.pallas_call(body, out_shape=[jax.ShapeDtypeStruct((tile, rows), BF16)]...  15.1 us
    ppermute x9, starting transfers between devices, cross(): return lax.ppermute(value, DP, pairs)  14.8 us
    all_to_all x2, starting transfers between devices, exchange(): got = lax.all_to_all(blocks, DP, split_axis=0, concat_axis=0, tiled=True)  13.4 us
    all_to_all x1, starting transfers between devices, group_sum(): lax.all_to_all(copies, DP, split_axis=0, concat_axis=0, tiled=True)  8.27 us
    pallas_call x1, Pallas kernels, weight_product(): pl.pallas_call(body, out_shape=jax.ShapeDtypeStruct((height, width), BF16...  8.14 us
    ppermute x9, waiting for transfers between devices, cross(): return lax.ppermute(value, DP, pairs)  6.17 us
  transfers between devices with their start and end apart: 28, of which 7 were waited for; matrix products, arithmetic and copies ran while one was open for 13% of the time, Pallas kernels for 30%

profile of v7, /device:TPU:1, one launch (start us, length us, event | category | flops | bytes accessed | tf_op | source)
XLA Modules:
  0.0 149.1 jit_solution(9099940515257417388)
XLA Ops:
  0.7 3.8 %forward_product.4 = (bf16[640,256]{1,0:T(8,128)(2,1)}, bf16[640,256]{1,0:T(8,128)(2,1)}) custom-call(s32[1]{0:T(128)} %bitcast.5.which, bf16[5120,1280]{1,0:T(8,128)(2,1)} %refs_3_.3, bf16[256,1280]{1,0:T(8,128)(2,1)} %context_ref.4), custom_call_target="tpu_custom_call" | custom-call | tf_op jit(solution)/shard_map/forward_product/pallas_call | solution.py:150
  4.5 1.4 collective-permute-start
  5.9 1.7 %collective-permute-start.1 = (bf16[640,256]{1,0:T(8,128)(2,1)}, bf16[640,256]{1,0:T(8,128)(2,1)S(1)}, u32[]{:S(2)}, u32[]{:S(2)}) collective-permute-start(bf16[640,256]{1,0:T(8,128)(2,1)} %get-tuple-element.31), channel_id=1, source_target_pairs={{0,1},{1,2},{2,3},{3,0},{4,5},{5,6},{6,7},{7,4},{8,9},{9,10},{10,1... | collective-permute-start | bytes 983048 | tf_op jit(solution)/shard_map/ppermute | solution.py:22
  7.6 2.1 %collective-permute-start.3 = (bf16[640,256]{1,0:T(8,128)(2,1)}, bf16[640,256]{1,0:T(8,128)(2,1)S(1)}, u32[]{:S(2)}, u32[]{:S(2)}) collective-permute-start(bf16[640,256]{1,0:T(8,128)(2,1)} %get-tuple-element.35), channel_id=1, source_target_pairs={{0,3},{1,0},{2,1},{3,2},{4,7},{5,4},{6,5},{7,6},{8,11},{9,8},{10,9... | collective-permute-start | bytes 983048 | tf_op jit(solution)/shard_map/ppermute | solution.py:22
  9.7 1.2 pad_maximum_fusion.refs_4_
  10.9 1.3 collective-permute-start.5
  12.2 1.4 collective-permute-start.6
  13.6 3.7 %forward_product.5 = f32[1280,256]{1,0:T(8,128)} custom-call(s32[1]{0:T(128)} %bitcast.4.which, bf16[5120,1280]{1,0:T(8,128)(2,1)} %refs_3_.3, bf16[256,1280]{1,0:T(8,128)(2,1)} %context_ref.4), custom_call_target="tpu_custom_call" | custom-call | tf_op jit(solution)/shard_map/forward_product/pallas_call | solution.py:150
  18.0 1.2 fusion.7
  19.1 1.1 slice.67
  21.1 3.7 %forward_product.7 = f32[1280,256]{1,0:T(8,128)} custom-call(s32[1]{0:T(128)} %bitcast.6.which, bf16[5120,1280]{1,0:T(8,128)(2,1)} %refs_3_.3, bf16[256,1280]{1,0:T(8,128)(2,1)} %context_ref.4), custom_call_target="tpu_custom_call" | custom-call | tf_op jit(solution)/shard_map/forward_product/pallas_call | solution.py:150
  24.9 1.1 slice.66
  26.0 1.2 fusion.6
  28.2 2.7 %collective-permute-start.4 = (bf16[1280,256]{1,0:T(8,128)(2,1)}, bf16[1280,256]{1,0:T(8,128)(2,1)}, u32[]{:S(2)}, u32[]{:S(2)}) collective-permute-start(bf16[1280,256]{1,0:T(8,128)(2,1)} %pad_maximum_fusion.2), channel_id=1, source_target_pairs={{0,3},{1,0},{2,1},{3,2},{4,7},{5,4},{6,5},{7,6},{8,11},{9,8},{10,9... | collective-permute-start | bytes 1966088 | tf_op jit(solution)/shard_map/ppermute | solution.py:22
  31.6 8.3 %all-to-all-start = ((f32[32,1,8]{2,1,0:T(1,128)}), f32[32,1,8]{2,1,0:T(1,128)S(1)}, u32[]{:S(2)}, u32[]{:S(2)}) async-start(f32[32,1,8]{2,1,0:T(1,128)} %broadcast_in_dim.16), calls=%async_computation | async-start | bytes 32768 | tf_op jit(solution)/shard_map/all_to_all | solution.py:42
  40.4 3.8 %forward_product.6 = f32[1280,256]{1,0:T(8,128)} custom-call(s32[1]{0:T(128)} %bitcast.3.which, bf16[5120,1280]{1,0:T(8,128)(2,1)} %refs_3_.3, bf16[256,1280]{1,0:T(8,128)(2,1)} %context_ref.4), custom_call_target="tpu_custom_call" | custom-call | tf_op jit(solution)/shard_map/forward_product/pallas_call | solution.py:150
  44.1 2.6 %all-to-all-done = f32[32,1,8]{2,1,0:T(1,128)S(1)} async-done(((f32[32,1,8]{2,1,0:T(1,128)}), f32[32,1,8]{2,1,0:T(1,128)S(1)}, u32[]{:S(2)}, u32[]{:S(2)}) %all-to-all-start) | async-done | bytes 1056 | tf_op jit(solution)/shard_map/all_to_all | solution.py:42
  47.1 1.9 %convert_add_fusion = f32[1280,256]{1,0:T(8,128)S(1)} fusion(bf16[1280,256]{1,0:T(8,128)(2,1)} %collective-permute-done.4, f32[1280,256]{1,0:T(8,128)} %forward_product.6, bf16[1280,256]{1,0:T(8,128)(2,1)} %collective-permute-done.2), kind=kLoop, calls=%fused_computation.9 | loop fusion | flops 1310720 | bytes 3932160 | tf_op jit(solution)/shard_map/add | solution.py:296
  50.1 1.7 %collective-permute-start.8 = (f32[2,256]{1,0:T(2,128)S(1)}, f32[2,256]{1,0:T(2,128)S(1)}, u32[]{:S(2)}, u32[]{:S(2)}) collective-permute-start(f32[2,256]{1,0:T(2,128)S(1)} %pad_maximum_fusion.4), channel_id=1, source_target_pairs={{0,2},{1,3},{2,0},{3,1},{4,6},{5,7},{6,4},{7,5},{8,10},{9,11},{10,... | collective-permute-start | bytes 6152 | tf_op jit(solution)/shard_map/ppermute | solution.py:22
  53.0 2.0 %collective-permute-start.13 = (bf16[512,1280]{1,0:T(8,128)(2,1)}, bf16[512,1280]{1,0:T(8,128)(2,1)}, u32[]{:S(2)}, u32[]{:S(2)}) collective-permute-start(bf16[512,1280]{1,0:T(8,128)(2,1)} %pad_maximum_fusion.refs_4_), channel_id=1, source_target_pairs={{0,64},{4,20},{8,72},{12,28},{16,80},{20,4},{24,88},{28,12},{32,96... | collective-permute-start | bytes 3932168 | tf_op jit(solution)/shard_map/ppermute | solution.py:37
  55.5 1.5 %collective-permute-start.10 = (bf16[1280,256]{1,0:T(8,128)(2,1)S(1)}, bf16[1280,256]{1,0:T(8,128)(2,1)S(1)}, u32[]{:S(2)}, u32[]{:S(2)}) collective-permute-start(bf16[1280,256]{1,0:T(8,128)(2,1)S(1)} %fusion.2.refs_0_.grad_ref), channel_id=1, source_target_pairs={{0,1},{1,2},{2,3},{3,0},{4,5},{5,6},{6,7},{7,4},{8,9},{9,10},{10,1... | collective-permute-start | bytes 1966088 | tf_op jit(solution)/shard_map/ppermute | solution.py:22
  57.0 1.2 collective-permute-start.11
  58.2 3.5 %collective-permute-start.12 = (bf16[640,256]{1,0:T(8,128)(2,1)S(1)}, bf16[640,256]{1,0:T(8,128)(2,1)S(1)}, u32[]{:S(2)}, u32[]{:S(2)}) collective-permute-start(bf16[640,256]{1,0:T(8,128)(2,1)S(1)} %bitcast.76), channel_id=1, source_target_pairs={{0,4},{4,0},{1,5},{5,1},{2,6},{6,2},{3,7},{7,3},{8,12},{12,8},{9,1... | collective-permute-start | bytes 983048 | tf_op jit(solution)/shard_map/ppermute | solution.py:22
  62.0 1.0 collective-permute-done.12.refs_5_
  63.0 1.7 %place_rows.1 = bf16[512,1280]{1,0:T(8,128)(2,1)} custom-call(bf16[512,256]{1,0:T(8,128)(2,1)S(1)} %fusion.8.refs_5_.slots_ref, bf16[1280,256]{1,0:T(8,128)(2,1)S(1)} %fusion.2.refs_0_.grad_ref), custom_call_target="tpu_custom_call" | custom-call | tf_op jit(solution)/shard_map/place_rows/pallas_call | solution.py:123
  64.7 7.5 %all-to-all-start.1 = ((bf16[32,16,1280]{2,1,0:T(8,128)(2,1)}), bf16[32,16,1280]{2,1,0:T(8,128)(2,1)}, u32[]{:S(2)}, u32[]{:S(2)}) async-start(bf16[32,16,1280]{2,1,0:T(8,128)(2,1)} %bitcast.19), calls=%async_computation.1 | async-start | bytes 2621440 | tf_op jit(solution)/shard_map/all_to_all | solution.py:58
  72.2 3.9 %context_product.3.refs_4_ = f32[256,1280]{1,0:T(8,128)} custom-call(s32[1]{0:T(128)} %bitcast.3.which, bf16[1280,256]{1,0:T(8,128)(2,1)} %copy-done, bf16[5120,1280]{1,0:T(8,128)(2,1)} %refs_3_.3), custom_call_target="tpu_custom_call" | custom-call | tf_op jit(solution)/shard_map/context_product/pallas_call | solution.py:102
  78.1 2.0 %collective-permute-start.15 = (bf16[640,256]{1,0:T(8,128)(2,1)S(1)}, bf16[640,256]{1,0:T(8,128)(2,1)S(1)}, u32[]{:S(2)}, u32[]{:S(2)}) collective-permute-start(bf16[640,256]{1,0:T(8,128)(2,1)S(1)} %slice.39), channel_id=1, source_target_pairs={{0,3},{1,0},{2,1},{3,2},{4,7},{5,4},{6,5},{7,6},{8,11},{9,8},{10,9... | collective-permute-start | bytes 983048 | tf_op jit(solution)/shard_map/ppermute | solution.py:22
  80.8 7.7 %context_product.4.refs_4_ = f32[256,1280]{1,0:T(8,128)} custom-call(s32[2]{0:T(128)} %pad_add_fusion.1.which, bf16[1280,256]{1,0:T(8,128)(2,1)} %copy-done.4, bf16[1280,256]{1,0:T(8,128)(2,1)} %copy-done.2, bf16[5120,1280]{1,0:T(8,128)(2,1)} %refs_3_.3, bf16[5120,1280]{1,0:T(8,128)(2,1)} %refs_3_.3, f32[256,1280]{1,0:T(8,128)} %context_product.3.refs_4_), custom_call_target="tpu_custom_call" | custom-call | tf_op jit(solution)/shard_map/context_product/pallas_call | solution.py:102
  91.0 1.5 %collective-permute-done.18.refs_7_ = bf16[640,256]{1,0:T(8,128)(2,1)} collective-permute-done((bf16[640,256]{1,0:T(8,128)(2,1)}, bf16[640,256]{1,0:T(8,128)(2,1)}, u32[]{:S(2)}, u32[]{:S(2)}) %collective-permute-start.18) | collective-permute-done | bytes 327712 | tf_op jit(solution)/shard_map/ppermute | solution.py:22
  92.6 1.0 copy-done.11
  93.5 5.8 %lay_out.1 = (bf16[1280,256]{1,0:T(8,128)(2,1)S(1)}, bf16[1280,256]{1,0:T(8,128)(2,1)}, bf16[1280,256]{1,0:T(8,128)(2,1)}, bf16[1280,256]{1,0:T(8,128)(2,1)}) custom-call(s32[4]{0:T(128)S(1)} %pad_add_fusion.2.where, bf16[1280,256]{1,0:T(8,128)(2,1)S(1)} %copy-done.1, bf16[1280,256]{1,0:T(8,128)(2,1)S(1)} %copy-done.5, ...), custom_call_target="tpu_custom_call" | custom-call | tf_op jit(solution)/shard_map/lay_out/pallas_call | solution.py:219
  100.2 1.4 collective-permute-start.19
  101.6 2.4 %collective-permute-start.20 = (bf16[1280,256]{1,0:T(8,128)(2,1)}, bf16[1280,256]{1,0:T(8,128)(2,1)S(1)}, u32[]{:S(2)}, u32[]{:S(2)}) collective-permute-start(bf16[1280,256]{1,0:T(8,128)(2,1)} %get-tuple-element.55), channel_id=1, source_target_pairs={{0,64},{4,20},{8,72},{12,28},{16,80},{20,4},{24,88},{28,12},{32,96... | collective-permute-start | bytes 1966088 | tf_op jit(solution)/shard_map/ppermute | solution.py:37
  104.0 1.2 collective-permute-start.21
  105.8 2.2 %reshape.124 = bf16[384,1280]{1,0:T(8,128)(2,1)} reshape(bf16[32,12,1280]{2,1,0:T(8,128)(2,1)} %bitcast.63) | data formatting | bytes 1966080 | tf_op jit(solution)/shard_map/reshape | solution.py:60
  107.9 6.0 %context_product.5 = bf16[512,1280]{1,0:T(8,128)(2,1)} custom-call(s32[2]{0:T(128)} %pad_add_fusion.which, bf16[640,256]{1,0:T(8,128)(2,1)} %copy-done.7, bf16[640,256]{1,0:T(8,128)(2,1)} %copy-done.8, bf16[5120,1280]{1,0:T(8,128)(2,1)} %refs_3_.3, bf16[5120,1280]{1,0:T(8,128)(2,1)} %refs_3_.3, f32[256,1280]{1,0:T(8,128)} %context_product.4.refs_4_, ...), custom_call_target="tpu_custom_call" | custom-call | tf_op jit(solution)/shard_map/context_product/pallas_call | solution.py:102
  113.9 5.9 %all-to-all-start.2 = ((bf16[32,16,1280]{2,1,0:T(8,128)(2,1)}), bf16[32,16,1280]{2,1,0:T(8,128)(2,1)S(1)}, u32[]{:S(2)}, u32[]{:S(2)}) async-start(bf16[32,16,1280]{2,1,0:T(8,128)(2,1)} %bitcast.72), calls=%async_computation.2 | async-start | bytes 2621440 | tf_op jit(solution)/shard_map/all_to_all | solution.py:58
  121.3 8.1 %weight_product.1 = bf16[640,1280]{1,0:T(8,128)(2,1)} custom-call(bf16[1280,256]{1,0:T(8,128)(2,1)} %copy-done.9, bf16[1280,256]{1,0:T(8,128)(2,1)} %copy-done.14, bf16[1280,256]{1,0:T(8,128)(2,1)} %copy-done.15, bf16[1280,256]{1,0:T(8,128)(2,1)} %copy-done.16, bf16[512,1280]{1,0:T(8,128)(2,1)} %pad_maximum_fusion.refs_4_, bf16[512,1280]{1,0:T(8,128)(2,1)} %copy-done.13, ...), custom_call_target="tpu_custom_call" | custom-call | tf_op jit(solution)/shard_map/weight_product/pallas_call | solution.py:252
  129.4 1.3 dynamic-slice_bitcast_fusion.2
  130.7 1.5 collective-permute-start.22
  132.2 2.4 %collective-permute-start.23 = (bf16[160,1280]{1,0:T(8,128)(2,1)S(1)}, bf16[160,1280]{1,0:T(8,128)(2,1)S(1)}, u32[]{:S(2)}, u32[]{:S(2)}) collective-permute-start(bf16[160,1280]{1,0:T(8,128)(2,1)S(1)} %get-tuple-element.65), channel_id=1, source_target_pairs={{0,16},{4,68},{8,24},{12,76},{16,0},{20,84},{24,8},{28,92},{32,48}... | collective-permute-start | bytes 1228808 | tf_op jit(solution)/shard_map/ppermute | solution.py:37
  134.6 1.1 collective-permute-start.24
  135.8 3.9 %all-to-all-done.2 = bf16[32,16,1280]{2,1,0:T(8,128)(2,1)S(1)} async-done(((bf16[32,16,1280]{2,1,0:T(8,128)(2,1)}), bf16[32,16,1280]{2,1,0:T(8,128)(2,1)S(1)}, u32[]{:S(2)}, u32[]{:S(2)}) %all-to-all-start.2) | async-done | bytes 1310752 | tf_op jit(solution)/shard_map/all_to_all | solution.py:58
  139.7 1.1 reshape.126
  140.7 1.5 %collective-permute-done.22 = bf16[160,1280]{1,0:T(8,128)(2,1)S(1)} collective-permute-done((bf16[160,1280]{1,0:T(8,128)(2,1)S(1)}, bf16[160,1280]{1,0:T(8,128)(2,1)S(1)}, u32[]{:S(2)}, u32[]{:S(2)}) %collective-permute-start.22) | collective-permute-done | bytes 409632 | tf_op jit(solution)/shard_map/ppermute | solution.py:37
  142.2 4.6 %collective-permute-done.23 = bf16[160,1280]{1,0:T(8,128)(2,1)S(1)} collective-permute-done((bf16[160,1280]{1,0:T(8,128)(2,1)S(1)}, bf16[160,1280]{1,0:T(8,128)(2,1)S(1)}, u32[]{:S(2)}, u32[]{:S(2)}) %collective-permute-start.23) | collective-permute-done | bytes 409632 | tf_op jit(solution)/shard_map/ppermute | solution.py:37
  146.9 2.2 %fusion.5 = f32[160,1280]{1,0:T(8,128)} fusion(bf16[160,1280]{1,0:T(8,128)(2,1)} %collective-permute-done.24, bf16[160,1280]{1,0:T(8,128)(2,1)S(1)} %collective-permute-done.23, bf16[160,1280]{1,0:T(8,128)(2,1)S(1)} %collective-permute-done.22, bf16[4,160,1280]{2,1,0:T(8,128)(2,1)} %bitcast.71, s32[]{:T(128)S(6)} %select_n.105), kind=kLoop, calls=%fused_computation.13 | loop fusion | flops 1638400 | bytes 2457604 | tf_op jit(solution)/shard_map/div | solution.py:356
  (107 shorter events, 14.8 us)
Async XLA Ops:
  0.6 3.8 %copy-start.12 = (bf16[256,1280]{1,0:T(8,128)(2,1)S(1)}, bf16[256,1280]{1,0:T(8,128)(2,1)}, u32[]{:S(2)}) copy-start(bf16[256,1280]{1,0:T(8,128)(2,1)} %context_ref.4) | copy-start | bytes 1966084
  4.5 5.3 %collective-permute-start = (bf16[256,1280]{1,0:T(8,128)(2,1)S(1)}, bf16[256,1280]{1,0:T(8,128)(2,1)S(1)}, u32[]{:S(2)}, u32[]{:S(2)}) collective-permute-start(bf16[256,1280]{1,0:T(8,128)(2,1)S(1)} %copy-done.12), channel_id=1, source_target_pairs={{0,4},{4,0},{1,5},{5,1},{2,6},{6,2},{3,7},{7,3},{8,12},{12,8},{9,1... | collective-permute-start | bytes 1966088 | tf_op jit(solution)/shard_map/ppermute | solution.py:22
  5.9 12.1 %collective-permute-start.1 = (bf16[640,256]{1,0:T(8,128)(2,1)}, bf16[640,256]{1,0:T(8,128)(2,1)S(1)}, u32[]{:S(2)}, u32[]{:S(2)}) collective-permute-start(bf16[640,256]{1,0:T(8,128)(2,1)} %get-tuple-element.31), channel_id=1, source_target_pairs={{0,1},{1,2},{2,3},{3,0},{4,5},{5,6},{6,7},{7,4},{8,9},{9,10},{10,1... | collective-permute-start | bytes 983048 | tf_op jit(solution)/shard_map/ppermute | solution.py:22
  7.6 18.4 %collective-permute-start.3 = (bf16[640,256]{1,0:T(8,128)(2,1)}, bf16[640,256]{1,0:T(8,128)(2,1)S(1)}, u32[]{:S(2)}, u32[]{:S(2)}) collective-permute-start(bf16[640,256]{1,0:T(8,128)(2,1)} %get-tuple-element.35), channel_id=1, source_target_pairs={{0,3},{1,0},{2,1},{3,2},{4,7},{5,4},{6,5},{7,6},{8,11},{9,8},{10,9... | collective-permute-start | bytes 983048 | tf_op jit(solution)/shard_map/ppermute | solution.py:22
  10.9 38.1 %collective-permute-start.5 = (bf16[512,1280]{1,0:T(8,128)(2,1)}, bf16[512,1280]{1,0:T(8,128)(2,1)S(1)}, u32[]{:S(2)}, u32[]{:S(2)}) collective-permute-start(bf16[512,1280]{1,0:T(8,128)(2,1)} %pad_maximum_fusion.refs_4_), channel_id=1, source_target_pairs={{0,32},{4,12},{8,40},{12,20},{16,48},{20,28},{24,56},{28,4},{32,64... | collective-permute-start | bytes 3932168 | tf_op jit(solution)/shard_map/ppermute | solution.py:37
  12.2 36.8 %collective-permute-start.6 = (bf16[512,1280]{1,0:T(8,128)(2,1)}, bf16[512,1280]{1,0:T(8,128)(2,1)}, u32[]{:S(2)}, u32[]{:S(2)}) collective-permute-start(bf16[512,1280]{1,0:T(8,128)(2,1)} %pad_maximum_fusion.refs_4_), channel_id=1, source_target_pairs={{0,96},{4,28},{8,104},{12,4},{16,112},{20,12},{24,120},{28,20},{32... | collective-permute-start | bytes 3932168 | tf_op jit(solution)/shard_map/ppermute | solution.py:37
  21.1 26.0 %collective-permute-start.2 = (bf16[1280,256]{1,0:T(8,128)(2,1)}, bf16[1280,256]{1,0:T(8,128)(2,1)}, u32[]{:S(2)}, u32[]{:S(2)}) collective-permute-start(bf16[1280,256]{1,0:T(8,128)(2,1)} %pad_maximum_fusion.1), channel_id=1, source_target_pairs={{0,1},{1,2},{2,3},{3,0},{4,5},{5,6},{6,7},{7,4},{8,9},{9,10},{10,1... | collective-permute-start | bytes 1966088 | tf_op jit(solution)/shard_map/ppermute | solution.py:22
  26.0 4.9 %copy-start.21 = (f32[4]{0:T(128)S(1)}, f32[4]{0:T(128)}, u32[]{:S(2)}) copy-start(f32[4]{0:T(128)} %param.14) | copy-start | bytes 52
  26.0 4.8 %copy-start.22 = (s32[4]{0:T(128)S(1)}, s32[4]{0:T(128)}, u32[]{:S(2)}) copy-start(s32[4]{0:T(128)} %param.15) | copy-start | bytes 52
  26.0 13.8 %copy-start.17 = (bf16[256,1280]{1,0:T(8,128)(2,1)S(1)}, bf16[256,1280]{1,0:T(8,128)(2,1)}, u32[]{:S(2)}) copy-start(bf16[256,1280]{1,0:T(8,128)(2,1)} %param.10) | copy-start | bytes 1966084
  27.3 12.8 %copy-start.18 = (bf16[256,1280]{1,0:T(8,128)(2,1)S(1)}, bf16[256,1280]{1,0:T(8,128)(2,1)}, u32[]{:S(2)}) copy-start(bf16[256,1280]{1,0:T(8,128)(2,1)} %param.11) | copy-start | bytes 1966084
  28.2 19.0 %collective-permute-start.4 = (bf16[1280,256]{1,0:T(8,128)(2,1)}, bf16[1280,256]{1,0:T(8,128)(2,1)}, u32[]{:S(2)}, u32[]{:S(2)}) collective-permute-start(bf16[1280,256]{1,0:T(8,128)(2,1)} %pad_maximum_fusion.2), channel_id=1, source_target_pairs={{0,3},{1,0},{2,1},{3,2},{4,7},{5,4},{6,5},{7,6},{8,11},{9,8},{10,9... | collective-permute-start | bytes 1966088 | tf_op jit(solution)/shard_map/ppermute | solution.py:22
  31.6 15.1 %all-to-all-start = ((f32[32,1,8]{2,1,0:T(1,128)}), f32[32,1,8]{2,1,0:T(1,128)S(1)}, u32[]{:S(2)}, u32[]{:S(2)}) async-start(f32[32,1,8]{2,1,0:T(1,128)} %broadcast_in_dim.16), calls=%async_computation | async-start | bytes 32768 | tf_op jit(solution)/shard_map/all_to_all | solution.py:42
  40.3 6.6 %copy-start.20 = (s32[4]{0:T(128)S(1)}, s32[4]{0:T(128)}, u32[]{:S(2)}) copy-start(s32[4]{0:T(128)} %param.16) | copy-start | bytes 52
  47.1 1.9 %copy-start.19 = (f32[1280]{0:T(1024)S(1)}, f32[1280]{0:T(1024)}, u32[]{:S(2)}) copy-start(f32[1280]{0:T(1024)} %param.13) | copy-start | bytes 15364
  49.0 3.8 %copy-start.23 = (s32[64,1]{0,1:T(1,128)S(1)}, s32[64,1]{0,1:T(1,128)}, u32[]{:S(2)}) copy-start(s32[64,1]{0,1:T(1,128)} %param.17) | copy-start | bytes 772
  49.0 1.1 copy-start.13
  50.1 4.9 %collective-permute-start.7 = (f32[2,256]{1,0:T(2,128)S(1)}, f32[2,256]{1,0:T(2,128)S(1)}, u32[]{:S(2)}, u32[]{:S(2)}) collective-permute-start(f32[2,256]{1,0:T(2,128)S(1)} %pad_maximum_fusion.4), channel_id=1, source_target_pairs={{0,1},{1,2},{2,3},{3,0},{4,5},{5,6},{6,7},{7,4},{8,9},{9,10},{10,1... | collective-permute-start | bytes 6152 | tf_op jit(solution)/shard_map/ppermute | solution.py:22
  50.1 4.9 %collective-permute-start.8 = (f32[2,256]{1,0:T(2,128)S(1)}, f32[2,256]{1,0:T(2,128)S(1)}, u32[]{:S(2)}, u32[]{:S(2)}) collective-permute-start(f32[2,256]{1,0:T(2,128)S(1)} %pad_maximum_fusion.4), channel_id=1, source_target_pairs={{0,2},{1,3},{2,0},{3,1},{4,6},{5,7},{6,4},{7,5},{8,10},{9,11},{10,... | collective-permute-start | bytes 6152 | tf_op jit(solution)/shard_map/ppermute | solution.py:22
  51.9 3.1 %collective-permute-start.9 = (f32[2,256]{1,0:T(2,128)S(1)}, f32[2,256]{1,0:T(2,128)S(1)}, u32[]{:S(2)}, u32[]{:S(2)}) collective-permute-start(f32[2,256]{1,0:T(2,128)S(1)} %pad_maximum_fusion.4), channel_id=1, source_target_pairs={{0,3},{1,0},{2,1},{3,2},{4,7},{5,4},{6,5},{7,6},{8,11},{9,8},{10,9... | collective-permute-start | bytes 6152 | tf_op jit(solution)/shard_map/ppermute | solution.py:22
  53.0 23.1 %collective-permute-start.13 = (bf16[512,1280]{1,0:T(8,128)(2,1)}, bf16[512,1280]{1,0:T(8,128)(2,1)}, u32[]{:S(2)}, u32[]{:S(2)}) collective-permute-start(bf16[512,1280]{1,0:T(8,128)(2,1)} %pad_maximum_fusion.refs_4_), channel_id=1, source_target_pairs={{0,64},{4,20},{8,72},{12,28},{16,80},{20,4},{24,88},{28,12},{32,96... | collective-permute-start | bytes 3932168 | tf_op jit(solution)/shard_map/ppermute | solution.py:37
  55.5 9.2 %copy-start = (bf16[1280,256]{1,0:T(8,128)(2,1)}, bf16[1280,256]{1,0:T(8,128)(2,1)S(1)}, u32[]{:S(2)}) copy-start(bf16[1280,256]{1,0:T(8,128)(2,1)S(1)} %fusion.2.refs_0_.grad_ref) | copy-start | bytes 1966084
  55.5 20.6 %collective-permute-start.10 = (bf16[1280,256]{1,0:T(8,128)(2,1)S(1)}, bf16[1280,256]{1,0:T(8,128)(2,1)S(1)}, u32[]{:S(2)}, u32[]{:S(2)}) collective-permute-start(bf16[1280,256]{1,0:T(8,128)(2,1)S(1)} %fusion.2.refs_0_.grad_ref), channel_id=1, source_target_pairs={{0,1},{1,2},{2,3},{3,0},{4,5},{5,6},{6,7},{7,4},{8,9},{9,10},{10,1... | collective-permute-start | bytes 1966088 | tf_op jit(solution)/shard_map/ppermute | solution.py:22
  57.0 19.1 %collective-permute-start.11 = (bf16[1280,256]{1,0:T(8,128)(2,1)S(1)}, bf16[1280,256]{1,0:T(8,128)(2,1)S(1)}, u32[]{:S(2)}, u32[]{:S(2)}) collective-permute-start(bf16[1280,256]{1,0:T(8,128)(2,1)S(1)} %fusion.2.refs_0_.grad_ref), channel_id=1, source_target_pairs={{0,3},{1,0},{2,1},{3,2},{4,7},{5,4},{6,5},{7,6},{8,11},{9,8},{10,9... | collective-permute-start | bytes 1966088 | tf_op jit(solution)/shard_map/ppermute | solution.py:22
  58.2 4.7 %collective-permute-start.12 = (bf16[640,256]{1,0:T(8,128)(2,1)S(1)}, bf16[640,256]{1,0:T(8,128)(2,1)S(1)}, u32[]{:S(2)}, u32[]{:S(2)}) collective-permute-start(bf16[640,256]{1,0:T(8,128)(2,1)S(1)} %bitcast.76), channel_id=1, source_target_pairs={{0,4},{4,0},{1,5},{5,1},{2,6},{6,2},{3,7},{7,3},{8,12},{12,8},{9,1... | collective-permute-start | bytes 983048 | tf_op jit(solution)/shard_map/ppermute | solution.py:22
  62.0 2.7 %copy-start.6 = (bf16[512,256]{1,0:T(8,128)(2,1)}, bf16[512,256]{1,0:T(8,128)(2,1)S(1)}, u32[]{:S(2)}) copy-start(bf16[512,256]{1,0:T(8,128)(2,1)S(1)} %fusion.8.refs_5_.slots_ref) | copy-start | bytes 786436
  64.7 41.1 %all-to-all-start.1 = ((bf16[32,16,1280]{2,1,0:T(8,128)(2,1)}), bf16[32,16,1280]{2,1,0:T(8,128)(2,1)}, u32[]{:S(2)}, u32[]{:S(2)}) async-start(bf16[32,16,1280]{2,1,0:T(8,128)(2,1)} %bitcast.19), calls=%async_computation.1 | async-start | bytes 2621440 | tf_op jit(solution)/shard_map/all_to_all | solution.py:58
  76.1 1.0 copy-start.4
  76.2 12.3 %collective-permute-start.16 = (bf16[640,256]{1,0:T(8,128)(2,1)S(1)}, bf16[640,256]{1,0:T(8,128)(2,1)S(1)}, u32[]{:S(2)}, u32[]{:S(2)}) collective-permute-start(bf16[640,256]{1,0:T(8,128)(2,1)S(1)} %bitcast.74), channel_id=1, source_target_pairs={{0,4},{4,0},{1,5},{5,1},{2,6},{6,2},{3,7},{7,3},{8,12},{12,8},{9,1... | collective-permute-start | bytes 983048 | tf_op jit(solution)/shard_map/ppermute | solution.py:22
  77.1 11.4 %collective-permute-start.17 = (bf16[640,256]{1,0:T(8,128)(2,1)S(1)}, bf16[640,256]{1,0:T(8,128)(2,1)S(1)}, u32[]{:S(2)}, u32[]{:S(2)}) collective-permute-start(bf16[640,256]{1,0:T(8,128)(2,1)S(1)} %bitcast.75), channel_id=1, source_target_pairs={{0,4},{4,0},{1,5},{5,1},{2,6},{6,2},{3,7},{7,3},{8,12},{12,8},{9,1... | collective-permute-start | bytes 983048 | tf_op jit(solution)/shard_map/ppermute | solution.py:22
  77.4 11.8 %collective-permute-start.14 = (bf16[640,256]{1,0:T(8,128)(2,1)S(1)}, bf16[640,256]{1,0:T(8,128)(2,1)S(1)}, u32[]{:S(2)}, u32[]{:S(2)}) collective-permute-start(bf16[640,256]{1,0:T(8,128)(2,1)S(1)} %slice.38), channel_id=1, source_target_pairs={{0,1},{1,2},{2,3},{3,0},{4,5},{5,6},{6,7},{7,4},{8,9},{9,10},{10,1... | collective-permute-start | bytes 983048 | tf_op jit(solution)/shard_map/ppermute | solution.py:22
  78.1 11.2 %collective-permute-start.15 = (bf16[640,256]{1,0:T(8,128)(2,1)S(1)}, bf16[640,256]{1,0:T(8,128)(2,1)S(1)}, u32[]{:S(2)}, u32[]{:S(2)}) collective-permute-start(bf16[640,256]{1,0:T(8,128)(2,1)S(1)} %slice.39), channel_id=1, source_target_pairs={{0,3},{1,0},{2,1},{3,2},{4,7},{5,4},{6,5},{7,6},{8,11},{9,8},{10,9... | collective-permute-start | bytes 983048 | tf_op jit(solution)/shard_map/ppermute | solution.py:22
  80.8 11.8 %copy-start.5 = (bf16[1280,256]{1,0:T(8,128)(2,1)S(1)}, bf16[1280,256]{1,0:T(8,128)(2,1)}, u32[]{:S(2)}) copy-start(bf16[1280,256]{1,0:T(8,128)(2,1)} %copy-done.4) | copy-start | bytes 1966084
  88.5 4.0 %copy-start.1 = (bf16[1280,256]{1,0:T(8,128)(2,1)S(1)}, bf16[1280,256]{1,0:T(8,128)(2,1)}, u32[]{:S(2)}) copy-start(bf16[1280,256]{1,0:T(8,128)(2,1)} %copy-done) | copy-start | bytes 1966084
  88.5 4.0 %copy-start.3 = (bf16[1280,256]{1,0:T(8,128)(2,1)S(1)}, bf16[1280,256]{1,0:T(8,128)(2,1)}, u32[]{:S(2)}) copy-start(bf16[1280,256]{1,0:T(8,128)(2,1)} %copy-done.2) | copy-start | bytes 1966084
  89.3 10.1 %copy-start.7 = (bf16[640,256]{1,0:T(8,128)(2,1)}, bf16[640,256]{1,0:T(8,128)(2,1)S(1)}, u32[]{:S(2)}) copy-start(bf16[640,256]{1,0:T(8,128)(2,1)S(1)} %collective-permute-done.14.refs_0_.refs_2_) | copy-start | bytes 983044
  89.3 10.1 %copy-start.8 = (bf16[640,256]{1,0:T(8,128)(2,1)}, bf16[640,256]{1,0:T(8,128)(2,1)S(1)}, u32[]{:S(2)}) copy-start(bf16[640,256]{1,0:T(8,128)(2,1)S(1)} %collective-permute-done.15.refs_1_.refs_3_) | copy-start | bytes 983044
  90.2 2.4 %collective-permute-start.18 = (bf16[640,256]{1,0:T(8,128)(2,1)}, bf16[640,256]{1,0:T(8,128)(2,1)}, u32[]{:S(2)}, u32[]{:S(2)}) collective-permute-start(bf16[640,256]{1,0:T(8,128)(2,1)} %bitcast.28), channel_id=1, source_target_pairs={{0,4},{4,0},{1,5},{5,1},{2,6},{6,2},{3,7},{7,3},{8,12},{12,8},{9,1... | collective-permute-start | bytes 983048 | tf_op jit(solution)/shard_map/ppermute | solution.py:22
  92.6 1.0 copy-start.11
  100.2 19.7 %collective-permute-start.19 = (bf16[1280,256]{1,0:T(8,128)(2,1)}, bf16[1280,256]{1,0:T(8,128)(2,1)S(1)}, u32[]{:S(2)}, u32[]{:S(2)}) collective-permute-start(bf16[1280,256]{1,0:T(8,128)(2,1)} %get-tuple-element.54), channel_id=1, source_target_pairs={{0,32},{4,12},{8,40},{12,20},{16,48},{20,28},{24,56},{28,4},{32,64... | collective-permute-start | bytes 1966088 | tf_op jit(solution)/shard_map/ppermute | solution.py:37
  101.6 18.3 %collective-permute-start.20 = (bf16[1280,256]{1,0:T(8,128)(2,1)}, bf16[1280,256]{1,0:T(8,128)(2,1)S(1)}, u32[]{:S(2)}, u32[]{:S(2)}) collective-permute-start(bf16[1280,256]{1,0:T(8,128)(2,1)} %get-tuple-element.55), channel_id=1, source_target_pairs={{0,64},{4,20},{8,72},{12,28},{16,80},{20,4},{24,88},{28,12},{32,96... | collective-permute-start | bytes 1966088 | tf_op jit(solution)/shard_map/ppermute | solution.py:37
  104.0 15.9 %collective-permute-start.21 = (bf16[1280,256]{1,0:T(8,128)(2,1)}, bf16[1280,256]{1,0:T(8,128)(2,1)S(1)}, u32[]{:S(2)}, u32[]{:S(2)}) collective-permute-start(bf16[1280,256]{1,0:T(8,128)(2,1)} %get-tuple-element.56), channel_id=1, source_target_pairs={{0,96},{4,28},{8,104},{12,4},{16,112},{20,12},{24,120},{28,20},{32... | collective-permute-start | bytes 1966088 | tf_op jit(solution)/shard_map/ppermute | solution.py:37
  113.9 25.8 %all-to-all-start.2 = ((bf16[32,16,1280]{2,1,0:T(8,128)(2,1)}), bf16[32,16,1280]{2,1,0:T(8,128)(2,1)S(1)}, u32[]{:S(2)}, u32[]{:S(2)}) async-start(bf16[32,16,1280]{2,1,0:T(8,128)(2,1)} %bitcast.72), calls=%async_computation.2 | async-start | bytes 2621440 | tf_op jit(solution)/shard_map/all_to_all | solution.py:58
  119.9 1.0 copy-start.15
  120.0 1.3 copy-start.16
  130.7 11.5 %collective-permute-start.22 = (bf16[160,1280]{1,0:T(8,128)(2,1)S(1)}, bf16[160,1280]{1,0:T(8,128)(2,1)S(1)}, u32[]{:S(2)}, u32[]{:S(2)}) collective-permute-start(bf16[160,1280]{1,0:T(8,128)(2,1)S(1)} %get-tuple-element.63), channel_id=1, source_target_pairs={{0,8},{4,36},{8,16},{12,44},{16,24},{20,52},{24,0},{28,60},{32,40}... | collective-permute-start | bytes 1228808 | tf_op jit(solution)/shard_map/ppermute | solution.py:37
  132.2 14.7 %collective-permute-start.23 = (bf16[160,1280]{1,0:T(8,128)(2,1)S(1)}, bf16[160,1280]{1,0:T(8,128)(2,1)S(1)}, u32[]{:S(2)}, u32[]{:S(2)}) collective-permute-start(bf16[160,1280]{1,0:T(8,128)(2,1)S(1)} %get-tuple-element.65), channel_id=1, source_target_pairs={{0,16},{4,68},{8,24},{12,76},{16,0},{20,84},{24,8},{28,92},{32,48}... | collective-permute-start | bytes 1228808 | tf_op jit(solution)/shard_map/ppermute | solution.py:37
  134.6 12.2 %collective-permute-start.24 = (bf16[160,1280]{1,0:T(8,128)(2,1)S(1)}, bf16[160,1280]{1,0:T(8,128)(2,1)}, u32[]{:S(2)}, u32[]{:S(2)}) collective-permute-start(bf16[160,1280]{1,0:T(8,128)(2,1)S(1)} %get-tuple-element.64), channel_id=1, source_target_pairs={{0,24},{4,100},{8,0},{12,108},{16,8},{20,116},{24,16},{28,124},{32... | collective-permute-start | bytes 1228808 | tf_op jit(solution)/shard_map/ppermute | solution.py:37
  (4 other events, 3.3 us)

commit v8 on v6

v8 whole, which is shorter than its diff:
```python
import jax
import jax.numpy as jnp
from jax import lax
from jax.experimental import pallas as pl
from jax.experimental.pallas import tpu as pltpu
from jax.sharding import Mesh
from jax.sharding import PartitionSpec as P

LMAX = 64
GROUP = 16
PAIR = 3
EPSILON = 1e-06
NX, NY, NC, NZ = 4, 4, 2, 4
DP = ("x", "y", "c")
F32 = jnp.float32
BF16 = jnp.bfloat16


def shift(value, axis, step):
    size = lax.axis_size(axis)
    return lax.ppermute(value, axis, [(i, (i + step) % size) for i in range(size)])


def pick(values, index):
    return lax.dynamic_index_in_dim(values, index, 0, keepdims=False)


def cross(value, step, first):
    pairs = []
    for x in range(NX):
        for y in range(NY):
            for c in range(NC):
                along_x = (c == 0) == first
                to = ((x + step) % NX, y, c) if along_x else (x, (y + step) % NY, c)
                pairs.append(((x * NY + y) * NC + c, (to[0] * NY + to[1]) * NC + to[2]))
    return lax.ppermute(value, DP, pairs)


def group_sum(value):
    copies = jnp.broadcast_to(value, (NX * NY * NC,) + value.shape)
    return jnp.sum(lax.all_to_all(copies, DP, split_axis=0, concat_axis=0, tiled=True), axis=0)


def slot_matrix(owner_dest, lanes, rows):
    count = owner_dest.shape[0]
    per_block = rows // count
    kept = PAIR * per_block
    same = owner_dest[:, None] == owner_dest[None, :]
    earlier = jnp.arange(count)[None, :] < jnp.arange(count)[:, None]
    rank = jnp.sum((same & earlier).astype(jnp.int32), axis=1)
    target = owner_dest * 2 * kept + rank * per_block
    row_target = jnp.repeat(target, per_block) + jnp.tile(jnp.arange(per_block), count)
    row_target = row_target[None, None, :] + kept * jnp.arange(2)[:, None, None]
    return (jnp.arange(lanes * 2 * kept)[None, :, None] == row_target).astype(BF16)


def exchange(packed, lanes):
    height, half = packed.shape
    blocks = packed.reshape((lanes, height // lanes, half))
    got = lax.all_to_all(blocks, DP, split_axis=0, concat_axis=0, tiled=True)
    got = got.reshape((lanes, 2, height // lanes // 2, half))
    return jnp.swapaxes(got, 1, 2).reshape(height // 2, 2 * half)


FREE = pl.CostEstimate(flops=0, bytes_accessed=0, transcendentals=0)
PARAMS = pltpu.CompilerParams(vmem_limit_bytes=48 * 1024 * 1024)


def context_product(chunks, places, out_proj, before=None, slots=None):
    width, rows = out_proj.shape[1], chunks[0].shape[1]
    count, tile = len(chunks), 640
    dtype = F32 if slots is None else BF16

    def body(which, *refs):
        refs = list(refs)
        out_ref = refs.pop()
        total = sum(
            lax.dot_general(
                refs[i][...], refs[count + i][...], (((0,), (0,)), ((), ())), preferred_element_type=F32
            )
            for i in range(count)
        )
        if before is not None:
            total = total + refs[2 * count][...]
        if slots is None:
            out_ref[...] = total
            return
        total = jnp.dot(refs[-1][0], total.astype(BF16), preferred_element_type=F32)

        @pl.when(pl.program_id(0) == 0)
        def _():
            out_ref[...] = total.astype(BF16)

        @pl.when(pl.program_id(0) == 1)
        def _():
            out_ref[...] += total.astype(BF16)

    in_specs = [pl.BlockSpec(chunk.shape, lambda n, which: (0, 0)) for chunk in chunks]
    in_specs += [
        pl.BlockSpec((chunk.shape[0], tile), lambda n, which, i=i: (which[i], n))
        for i, chunk in enumerate(chunks)
    ]
    operands = list(chunks) + [out_proj] * count
    out_rows = rows
    if before is not None:
        in_specs.append(pl.BlockSpec((rows, tile), lambda n, which: (0, n)))
        operands.append(before)
    if slots is not None:
        in_specs.append(pl.BlockSpec((1,) + slots.shape[1:], lambda n, which: (n, 0, 0)))
        operands.append(slots)
        out_rows = slots.shape[1]
    return pl.pallas_call(
        body,
        out_shape=jax.ShapeDtypeStruct((out_rows, width if slots is None else tile), dtype),
        grid_spec=pltpu.PrefetchScalarGridSpec(
            num_scalar_prefetch=1,
            grid=(width // tile,),
            in_specs=in_specs,
            out_specs=pl.BlockSpec(
                (out_rows, tile), lambda n, which: (0, n if slots is None else 0)
            ),
        ),
        cost_estimate=FREE,
        compiler_params=PARAMS,
        name="context_product",
    )(jnp.stack(places), *operands)


def place_rows(slots, grad_t):
    half = grad_t.shape[0] // 2

    def body(slots_ref, grad_ref, out_ref):
        out_ref[...] = sum(
            lax.dot_general(
                slots_ref[i],
                grad_ref[i * half : (i + 1) * half, :],
                (((1,), (1,)), ((), ())),
                preferred_element_type=F32,
            )
            for i in (0, 1)
        ).astype(BF16)

    return pl.pallas_call(
        body,
        out_shape=jax.ShapeDtypeStruct((slots.shape[1], half), BF16),
        cost_estimate=FREE,
        compiler_params=PARAMS,
        name="place_rows",
    )(slots, grad_t)


def top_up(whole, part, half):
    height, rows = part.shape

    def body(whole_ref, part_ref, out_ref):
        value = whole_ref[...].astype(F32) + part_ref[...].astype(F32)
        out_ref[...] = value.astype(BF16)

    spec = pl.BlockSpec((height, rows), lambda i: (half, 0))
    return pl.pallas_call(
        body,
        out_shape=jax.ShapeDtypeStruct(whole.shape, BF16),
        grid=(1,),
        in_specs=[spec, pl.BlockSpec((height, rows), lambda i: (0, 0))],
        out_specs=spec,
        input_output_aliases={0: 0},
        cost_estimate=FREE,
        compiler_params=PARAMS,
        name="top_up",
    )(whole, part)


def forward_product(out_proj, context, place, split, dtype=F32):
    rows, width = context.shape
    tile = width // 2

    def body(which, proj_ref, context_ref, *out_refs):
        value = lax.dot_general(
            proj_ref[...], context_ref[...], (((1,), (1,)), ((), ())), preferred_element_type=F32
        )
        if split:
            for half in (0, 1):

                @pl.when(pl.program_id(0) == half)
                def _(half=half):
                    out_refs[half][...] = value.astype(BF16)
        else:
            out_refs[0][...] = value.astype(dtype)

    half_spec = pl.BlockSpec((tile, rows), lambda i, which: (0, 0))
    out = pl.pallas_call(
        body,
        out_shape=[jax.ShapeDtypeStruct((tile, rows), BF16)] * 2
        if split
        else [jax.ShapeDtypeStruct((width, rows), dtype)],
        grid_spec=pltpu.PrefetchScalarGridSpec(
            num_scalar_prefetch=1,
            grid=(2,),
            in_specs=[
                pl.BlockSpec((tile, width), lambda i, which: (which[0] * 2 + i, 0)),
                pl.BlockSpec((rows, width), lambda i, which: (0, 0)),
            ],
            out_specs=[half_spec] * 2
            if split
            else [pl.BlockSpec((tile, rows), lambda i, which: (i, 0))],
        ),
        cost_estimate=FREE,
        compiler_params=PARAMS,
        name="forward_product",
    )(place.reshape(1), out_proj, context)
    return out if split else out[0]


def lay_out(chunks, siblings, x, y, c, z):
    block, rows = chunks[0][0].shape[-2:]
    flat = [piece for group in (chunks, siblings) for pieces in group for piece in pieces]
    counts = [[len(pieces) for pieces in group] for group in (chunks, siblings)]

    def body(where, *refs):
        ins, outs, sems = refs[: len(flat)], refs[len(flat) : len(flat) + 4], refs[-1]
        wx, wy, wc, wz = (where[i] for i in range(4))

        def send(src, k, first, slots):
            pltpu.make_async_copy(src, outs[k].at[pl.ds(first, slots)], sems.at[k]).start()

        position = 0
        for owner, group in enumerate(counts):
            for j, count in enumerate(group):
                pieces = ins[position : position + count]
                position += count
                per_piece = 4 // count
                if owner == 0:
                    pieces = [piece.at[:, wc] for piece in pieces]
                for k in range(4):
                    wanted = lax.rem(wy + k, 4)

                    @pl.when((wc == 0) & (lax.rem(j + wz - wx + 4, 4) == k))
                    def _(pieces=pieces, per_piece=per_piece, k=k, owner=owner):
                        for number, piece in enumerate(pieces):
                            send(piece, k, owner * 4 + number * per_piece, per_piece)

                    for number, piece in enumerate(pieces):

                        @pl.when((wc == 1) & (wanted // per_piece == number))
                        def _(piece=piece, number=number, per_piece=per_piece, k=k, owner=owner,
                              j=j, wanted=wanted):
                            slot = wanted - number * per_piece
                            send(piece.at[pl.ds(slot, 1)], k, owner * 4 + j, 1)

        for k in range(4):
            pltpu.make_async_copy(outs[k], outs[k], sems.at[k]).wait()

    out = pl.pallas_call(
        body,
        out_shape=[jax.ShapeDtypeStruct((8, block, rows), BF16)] * 4,
        grid_spec=pltpu.PrefetchScalarGridSpec(
            num_scalar_prefetch=1,
            grid=(1,),
            in_specs=[pl.BlockSpec(memory_space=pltpu.HBM)] * len(flat),
            out_specs=[pl.BlockSpec((8, block, rows), lambda i, where: (0, 0, 0))] * 4,
            scratch_shapes=[pltpu.SemaphoreType.DMA((4,))],
        ),
        cost_estimate=FREE,
        compiler_params=PARAMS,
        name="lay_out",
    )(jnp.stack([x, y, c, z]).astype(jnp.int32), *flat)
    return [value.reshape(8 * block, rows) for value in out]


def weight_product(pieces, contexts, order, block):
    count, tile = len(pieces), 640
    height, rows = pieces[0].shape[0] // 2, pieces[0].shape[1]
    width = contexts[0].shape[1]

    def body(order_ref, *refs):
        outs, total = refs[2 * count : 2 * count + 4], refs[-1]
        total[...] = sum(
            jnp.dot(
                refs[i][core * height : (core + 1) * height, :],
                refs[count + i][core * rows : (core + 1) * rows, :],
                preferred_element_type=F32,
            )
            for i in range(count)
            for core in (0, 1)
        )
        for k in range(4):
            first = pl.multiple_of(order_ref[k] * block, block)
            outs[k][...] = total[pl.ds(first, block), :].astype(outs[k].dtype)

    return pl.pallas_call(
        body,
        out_shape=[jax.ShapeDtypeStruct((block, width), BF16 if k else F32) for k in range(4)],
        grid_spec=pltpu.PrefetchScalarGridSpec(
            num_scalar_prefetch=1,
            grid=(width // tile,),
            in_specs=[pl.BlockSpec((2 * height, rows), lambda n, order: (0, 0)) for _ in pieces]
            + [pl.BlockSpec((2 * rows, tile), lambda n, order: (0, n)) for _ in contexts],
            out_specs=[pl.BlockSpec((block, tile), lambda n, order: (0, n))] * 4,
            scratch_shapes=[pltpu.VMEM((height, tile), F32)],
        ),
        cost_estimate=FREE,
        compiler_params=PARAMS,
        name="weight_product",
    )(order, *pieces, *contexts)


def per_device(
    context, residual, cotangent, out_proj, norm_gain, rewards, group_ids, lengths, destinations
):
    lanes = NX * NY * NC
    rows, width = residual.shape
    full = width * NZ
    x, y, c, z = (lax.axis_index(axis) for axis in ("x", "y", "c", "z"))

    top = width // 2
    far_top, far_bottom = forward_product(out_proj, context, (z + 2) % NZ, True)
    sent_top, sent_bottom = shift(far_top, "z", 1), shift(far_bottom, "z", 3)
    near = forward_product(out_proj, context, (z + 1) % NZ, False, BF16)
    back = forward_product(out_proj, context, (z + 3) % NZ, False, BF16)
    sent_top, sent_bottom, near, back = lax.optimization_barrier(
        (sent_top, sent_bottom, near, back)
    )
    near, back = top_up(near, sent_top, 0), top_up(back, sent_bottom, 1)

    groups = rewards.shape[0] * lanes // GROUP
    member = (group_ids[:, None] == jnp.arange(groups)[None, :]).astype(F32)
    share, _ = lax.optimization_barrier((jnp.sum(member * rewards[:, None], axis=0), near))
    group_total = group_sum(share)
    advantage = rewards - jnp.sum(member * group_total[None, :], axis=1) / GROUP
    scale = advantage * LMAX / (2.0 * lengths.astype(F32))
    live = jnp.arange(LMAX)[None, :] < lengths[:, None]
    row_weights = jnp.where(live, scale[:, None], F32(0.0)).reshape(-1).astype(BF16)

    ready, _ = lax.optimization_barrier((context, near))
    pair = jnp.concatenate([context, shift(ready, "c", 1)], axis=0)
    contexts = [pair, cross(pair, 1, True), None, cross(pair, 3, True)]
    own = forward_product(out_proj, ready, z, False)
    attn_t = own + shift(near, "z", 1).astype(F32) + shift(back, "z", 3).astype(F32)
    attn_t, pair = lax.optimization_barrier((attn_t, pair))
    hidden_t = residual.T.astype(F32) + attn_t
    upstream_t = norm_gain[:, None] * (row_weights.astype(F32)[None, :] * cotangent.T.astype(F32))
    stats = jnp.stack(
        [jnp.sum(hidden_t * hidden_t, axis=0), jnp.sum(upstream_t * hidden_t, axis=0)]
    )
    stats = stats + shift(stats, "z", 1) + shift(stats, "z", 2) + shift(stats, "z", 3)
    inv_rms = lax.rsqrt(stats[0] / full + EPSILON)
    grad_t = (
        inv_rms[None, :] * upstream_t - hidden_t * (inv_rms**3 * stats[1] / full)[None, :]
    ).astype(BF16)

    block = width // (NY * NC)

    def swap(*values):
        parted = [value.reshape(-1, NC, block, rows) for value in values]
        asked = [lax.dynamic_index_in_dim(value, 1 - c, 1, keepdims=False) for value in parted]
        return shift(jnp.concatenate(asked, axis=0).reshape(-1, rows), "c", 1)

    slots = slot_matrix(destinations[:, 0], lanes, rows)
    from_left, from_right = shift(grad_t, "z", 1), shift(grad_t, "z", 3)
    swapped = swap(grad_t)
    grad_rows, _ = lax.optimization_barrier((grad_t, swapped))
    d_residual = exchange(place_rows(slots, grad_rows), lanes)
    context_grad = context_product([grad_t], [z], out_proj)
    from_left, from_right, context_grad, swapped, contexts[1], contexts[3] = (
        lax.optimization_barrier(
            (from_left, from_right, context_grad, swapped, contexts[1], contexts[3])
        )
    )
    contexts[2] = cross(lax.optimization_barrier((pair, contexts[1]))[0], 2, True)
    far_left, far_right = shift(from_left[:top], "z", 1), shift(from_right[top:], "z", 3)
    swapped_left, swapped_right = swap(from_left), swap(from_right)
    context_grad = context_product(
        [from_right, from_left], [(z + 1) % NZ, (z + 3) % NZ], out_proj, before=context_grad
    )
    far_left, far_right, context_grad, swapped_left, swapped_right, contexts[2] = (
        lax.optimization_barrier(
            (far_left, far_right, context_grad, swapped_left, swapped_right, contexts[2])
        )
    )
    def parted(*values):
        return [value.reshape(-1, NC, block, rows) for value in values]

    def single(value):
        return [value.reshape(-1, block, rows)]

    sends = lay_out(
        [parted(grad_t), parted(from_right), parted(far_left, far_right), parted(from_left)],
        [single(value) for value in (swapped, swapped_right, swap(far_left, far_right), swapped_left)],
        x, y, c, z,
    )
    pieces = [sends[0]] + [cross(sends[k], k, True) for k in (1, 2, 3)]
    far_place = (z + 2) % NZ * 2
    placed = context_product(
        [far_left, far_right], [far_place, far_place + 1], out_proj, before=context_grad, slots=slots
    )
    placed, d_residual = lax.optimization_barrier((placed, d_residual))
    d_context = exchange(placed, lanes)
    order = [jnp.where(c == 0, (y + k) % NY, (x + k - z) % NZ) for k in range(4)]
    d_out_proj, *parts = weight_product(pieces, contexts, jnp.stack(order), block)
    for k in (1, 2, 3):
        d_out_proj = d_out_proj + cross(parts[k - 1], k, False).astype(F32)
    return (d_context, d_residual, d_out_proj / lanes)


def solution(mesh):
    wide = Mesh(mesh.devices.reshape(NX, NY, NC, NZ), DP + ("z",))
    placed = (
        P(DP, "z"),
        P(DP, "z"),
        P(DP, "z"),
        P(None, "z"),
        P("z"),
        P(DP),
        P(DP),
        P(DP),
        P(DP, None),
    )
    return jax.shard_map(
        per_device,
        mesh=wide,
        in_specs=placed,
        out_specs=(P(DP, "z"), P(DP, "z"), P(DP, "z")),
        check_vma=False,
    )
```

time: 166 us -> 161 us (0.970)
  local copies, waits for them, and re-layouts: 42.1 us -> 29.5 us
  Pallas kernels: 33.4 us -> 39.8 us
  other arithmetic: 10.7 us -> 4.74 us
  starting transfers between devices: 56 us -> 60.2 us
  waiting for transfers between devices: 21 us -> 25.2 us
    unnamed x54 -> x57, local copies, waits for them, and re-layouts: 32.8 us -> 18.9 us
    ppermute x16, starting transfers between devices: 19.3 us -> 27.3 us  [shift(): lax.ppermute(value, axis, [(i, (i + step) % size) for i in range(size)])]
    ppermute x16, waiting for transfers between devices: 12 us -> 19.2 us  [shift(): lax.ppermute(value, axis, [(i, (i + step) % size) for i in range(size)])]
    pallas_call x6 -> x8, Pallas kernels: 23.7 us -> 28.7 us  [the longest x3 13.8 us: context_product(): pl.pallas_call(body, out_shape=jax.ShapeDtypeStruct((out_rows, width if s...]
    reshape x2 -> x0, local copies, waits for them, and re-layouts: 4.36 us -> none  [exchange(): return got[:, :kept].reshape(lanes * kept, packed.shape[1])]
    all_to_all x2, waiting for transfers between devices: 4 us -> 0.01 us  [exchange(): got = lax.all_to_all(blocks, DP, split_axis=0, concat_axis=0, tiled=True)]
    all_to_all x2, starting transfers between devices: 13.6 us -> 10.6 us  [exchange(): got = lax.all_to_all(blocks, DP, split_axis=0, concat_axis=0, tiled=True)]
    concatenate x3 -> x0, other arithmetic: 2.93 us -> none  [the longest x1 1.17 us: per_device(): jnp.concatenate([context, shift(lax.optimization_barrier((context, far_to...]
  transfers between devices with their start and end apart: 28 -> 28, of which waited for: 7 -> 8; matrix products, arithmetic and copies ran while one was open for 10% -> 12% of each run, Pallas kernels for 16% -> 23%
where the time goes in v8:
time: 161 us; the launch traced here: 160 us
  starting transfers between devices  60.2 us (37%)
  Pallas kernels  39.8 us (25%)
  local copies, waits for them, and re-layouts  29.5 us (18%)
  waiting for transfers between devices  25.2 us (16%)
  other arithmetic  4.74 us (3%)
    ppermute x16, starting transfers between devices, shift(): lax.ppermute(value, axis, [(i, (i + step) % size) for i in range(size)])  27.3 us
    ppermute x16, waiting for transfers between devices, shift(): lax.ppermute(value, axis, [(i, (i + step) % size) for i in range(size)])  19.2 us
    unnamed x57, local copies, waits for them, and re-layouts  18.9 us
    ppermute x9, starting transfers between devices, cross(): return lax.ppermute(value, DP, pairs)  15.1 us
    pallas_call x3, Pallas kernels, context_product(): pl.pallas_call(body, out_shape=jax.ShapeDtypeStruct((out_rows, width if s...  13.8 us
    pallas_call x4, Pallas kernels, forward_product(): pl.pallas_call(body, out_shape=[jax.ShapeDtypeStruct((tile, rows), BF16)]...  11.1 us
    all_to_all x2, starting transfers between devices, exchange(): got = lax.all_to_all(blocks, DP, split_axis=0, concat_axis=0, tiled=True)  10.6 us
    pallas_call x1, Pallas kernels, weight_product(): pl.pallas_call(body, out_shape=[jax.ShapeDtypeStruct((block, width), BF16...  8.25 us
  transfers between devices with their start and end apart: 28, of which 8 were waited for; matrix products, arithmetic and copies ran while one was open for 12% of the time, Pallas kernels for 23%

profile of v8, /device:TPU:1, one launch (start us, length us, event | category | flops | bytes accessed | tf_op | source)
XLA Modules:
  0.0 160.5 jit_solution(3504203755418154391)
XLA Ops:
  1.7 2.8 %forward_product.4 = (bf16[640,256]{1,0:T(8,128)(2,1)S(1)}, bf16[640,256]{1,0:T(8,128)(2,1)S(1)}) custom-call(s32[1]{0:T(128)} %bitcast.4.which, bf16[5120,1280]{1,0:T(8,128)(2,1)} %refs_3_.3, bf16[256,1280]{1,0:T(8,128)(2,1)S(1)} %copy-done), custom_call_target="tpu_custom_call" | custom-call | tf_op jit(solution)/shard_map/forward_product/pallas_call | solution.py:191
  4.6 2.5 %collective-permute-start = (bf16[640,256]{1,0:T(8,128)(2,1)S(1)}, bf16[640,256]{1,0:T(8,128)(2,1)S(1)}, u32[]{:S(2)}, u32[]{:S(2)}) collective-permute-start(bf16[640,256]{1,0:T(8,128)(2,1)S(1)} %get-tuple-element.37), channel_id=1, source_target_pairs={{0,1},{1,2},{2,3},{3,0},{4,5},{5,6},{6,7},{7,4},{8,9},{9,10},{10,1... | collective-permute-start | bytes 983048 | tf_op jit(solution)/shard_map/ppermute | solution.py:21
  7.1 2.2 %collective-permute-start.1 = (bf16[640,256]{1,0:T(8,128)(2,1)S(1)}, bf16[640,256]{1,0:T(8,128)(2,1)S(1)}, u32[]{:S(2)}, u32[]{:S(2)}) collective-permute-start(bf16[640,256]{1,0:T(8,128)(2,1)S(1)} %get-tuple-element.38), channel_id=1, source_target_pairs={{0,3},{1,0},{2,1},{3,2},{4,7},{5,4},{6,5},{7,6},{8,11},{9,8},{10,9... | collective-permute-start | bytes 983048 | tf_op jit(solution)/shard_map/ppermute | solution.py:21
  9.3 2.7 %forward_product.5.whole_ref = bf16[1280,256]{1,0:T(8,128)(2,1)S(1)} custom-call(s32[1]{0:T(128)} %bitcast.5.which, bf16[5120,1280]{1,0:T(8,128)(2,1)} %refs_3_.3, bf16[256,1280]{1,0:T(8,128)(2,1)S(1)} %copy-done.1), custom_call_target="tpu_custom_call" | custom-call | tf_op jit(solution)/shard_map/forward_product/pallas_call | solution.py:191
  12.1 2.7 %forward_product.6.whole_ref = bf16[1280,256]{1,0:T(8,128)(2,1)S(1)} custom-call(s32[1]{0:T(128)} %bitcast.6.which, bf16[5120,1280]{1,0:T(8,128)(2,1)} %refs_3_.3, bf16[256,1280]{1,0:T(8,128)(2,1)S(1)} %copy-done.1), custom_call_target="tpu_custom_call" | custom-call | tf_op jit(solution)/shard_map/forward_product/pallas_call | solution.py:191
  14.9 1.7 %collective-permute-done.part_ref = bf16[640,256]{1,0:T(8,128)(2,1)S(1)} collective-permute-done((bf16[640,256]{1,0:T(8,128)(2,1)S(1)}, bf16[640,256]{1,0:T(8,128)(2,1)S(1)}, u32[]{:S(2)}, u32[]{:S(2)}) %collective-permute-start) | collective-permute-done | bytes 327712 | tf_op jit(solution)/shard_map/ppermute | solution.py:21
  16.9 1.3 collective-permute-start.4
  18.9 7.2 %all-to-all-start = ((f32[32,1,8]{2,1,0:T(1,128)}), f32[32,1,8]{2,1,0:T(1,128)S(1)}, u32[]{:S(2)}, u32[]{:S(2)}) async-start(f32[32,1,8]{2,1,0:T(1,128)} %broadcast_in_dim.16), calls=%async_computation | async-start | bytes 32768 | tf_op jit(solution)/shard_map/all_to_all | solution.py:41
  27.0 2.2 %copy.40 = bf16[256,1280]{0,1:T(8,128)(2,1)} copy(bf16[256,1280]{1,0:T(8,128)(2,1)} %param.10) | data formatting | bytes 1310720 | tf_op args[1]
  31.2 2.8 %forward_product.7 = f32[1280,256]{1,0:T(8,128)S(1)} custom-call(s32[1]{0:T(128)} %bitcast.3.which, bf16[5120,1280]{1,0:T(8,128)(2,1)} %refs_3_.3, bf16[256,1280]{1,0:T(8,128)(2,1)S(1)} %copy-done.1), custom_call_target="tpu_custom_call" | custom-call | tf_op jit(solution)/shard_map/forward_product/pallas_call | solution.py:191
  34.2 1.8 %collective-permute-start.3 = (bf16[1280,256]{1,0:T(8,128)(2,1)S(1)}, bf16[1280,256]{1,0:T(8,128)(2,1)}, u32[]{:S(2)}, u32[]{:S(2)}) collective-permute-start(bf16[1280,256]{1,0:T(8,128)(2,1)S(1)} %top_up.3), channel_id=1, source_target_pairs={{0,3},{1,0},{2,1},{3,2},{4,7},{5,4},{6,5},{7,6},{8,11},{9,8},{10,9... | collective-permute-start | bytes 1966088 | tf_op jit(solution)/shard_map/ppermute | solution.py:21
  36.5 2.0 %constant_dynamic-update-slice_fusion.refs_4_ = bf16[512,1280]{1,0:T(8,128)(2,1)} fusion(bf16[512,1280]{1,0:T(8,128)(2,1)} %constant_dynamic-update-slice_fusion.1, bf16[256,1280]{1,0:T(8,128)(2,1)} %collective-permute-done.4), kind=kLoop, calls=%fused_computation.19 | loop fusion | bytes 1310720 | tf_op jit(solution)/shard_map/concatenate | solution.py:335
  38.5 9.3 %collective-permute-done.2 = bf16[1280,256]{1,0:T(8,128)(2,1)} collective-permute-done((bf16[1280,256]{1,0:T(8,128)(2,1)S(1)}, bf16[1280,256]{1,0:T(8,128)(2,1)}, u32[]{:S(2)}, u32[]{:S(2)}) %collective-permute-start.2) | collective-permute-done | bytes 655392 | tf_op jit(solution)/shard_map/ppermute | solution.py:21
  47.8 2.4 %collective-permute-done.3 = bf16[1280,256]{1,0:T(8,128)(2,1)} collective-permute-done((bf16[1280,256]{1,0:T(8,128)(2,1)S(1)}, bf16[1280,256]{1,0:T(8,128)(2,1)}, u32[]{:S(2)}, u32[]{:S(2)}) %collective-permute-start.3) | collective-permute-done | bytes 655392 | tf_op jit(solution)/shard_map/ppermute | solution.py:21
  50.2 1.5 convert_add_fusion
  52.1 1.4 collective-permute-start.5
  53.5 2.9 %collective-permute-start.6 = (f32[2,256]{1,0:T(2,128)S(1)}, f32[2,256]{1,0:T(2,128)S(1)}, u32[]{:S(2)}, u32[]{:S(2)}) collective-permute-start(f32[2,256]{1,0:T(2,128)S(1)} %pad_maximum_fusion.1), channel_id=1, source_target_pairs={{0,2},{1,3},{2,0},{3,1},{4,6},{5,7},{6,4},{7,5},{8,10},{9,11},{10,... | collective-permute-start | bytes 6152 | tf_op jit(solution)/shard_map/ppermute | solution.py:21
  57.2 1.2 collective-permute-start.11
  58.4 1.5 collective-permute-start.12
  61.1 2.0 %collective-permute-start.9 = (bf16[1280,256]{1,0:T(8,128)(2,1)S(1)}, bf16[1280,256]{1,0:T(8,128)(2,1)S(1)}, u32[]{:S(2)}, u32[]{:S(2)}) collective-permute-start(bf16[1280,256]{1,0:T(8,128)(2,1)S(1)} %fusion.3.refs_0_.grad_ref), channel_id=1, source_target_pairs={{0,3},{1,0},{2,1},{3,2},{4,7},{5,4},{6,5},{7,6},{8,11},{9,8},{10,9... | collective-permute-start | bytes 1966088 | tf_op jit(solution)/shard_map/ppermute | solution.py:21
  63.1 3.4 %collective-permute-start.10 = (bf16[640,256]{1,0:T(8,128)(2,1)S(1)}, bf16[640,256]{1,0:T(8,128)(2,1)S(1)}, u32[]{:S(2)}, u32[]{:S(2)}) collective-permute-start(bf16[640,256]{1,0:T(8,128)(2,1)S(1)} %bitcast.92), channel_id=1, source_target_pairs={{0,4},{4,0},{1,5},{5,1},{2,6},{6,2},{3,7},{7,3},{8,12},{12,8},{9,1... | collective-permute-start | bytes 983048 | tf_op jit(solution)/shard_map/ppermute | solution.py:21
  66.7 3.0 %context_product.3.refs_4_ = f32[256,1280]{1,0:T(8,128)S(1)} custom-call(s32[1]{0:T(128)} %bitcast.3.which, bf16[1280,256]{1,0:T(8,128)(2,1)S(1)} %fusion.3.refs_0_.grad_ref, bf16[5120,1280]{1,0:T(8,128)(2,1)} %refs_3_.3), custom_call_target="tpu_custom_call" | custom-call | tf_op jit(solution)/shard_map/context_product/pallas_call | solution.py:112
  69.7 1.1 copy-done.5
  70.8 4.4 %collective-permute-done.8.refs_1_ = bf16[1280,256]{1,0:T(8,128)(2,1)S(1)} collective-permute-done((bf16[1280,256]{1,0:T(8,128)(2,1)S(1)}, bf16[1280,256]{1,0:T(8,128)(2,1)S(1)}, u32[]{:S(2)}, u32[]{:S(2)}) %collective-permute-start.8) | collective-permute-done | bytes 655392 | tf_op jit(solution)/shard_map/ppermute | solution.py:21
  75.5 2.4 %collective-permute-start.17 = (bf16[512,1280]{1,0:T(8,128)(2,1)}, bf16[512,1280]{1,0:T(8,128)(2,1)}, u32[]{:S(2)}, u32[]{:S(2)}) collective-permute-start(bf16[512,1280]{1,0:T(8,128)(2,1)} %constant_dynamic-update-slice_fusion.refs_4_), channel_id=1, source_target_pairs={{0,64},{4,20},{8,72},{12,28},{16,80},{20,4},{24,88},{28,12},{32,96... | collective-permute-start | bytes 3932168 | tf_op jit(solution)/shard_map/ppermute | solution.py:36
  79.7 4.0 %collective-permute-start.15 = (bf16[640,256]{1,0:T(8,128)(2,1)}, bf16[640,256]{1,0:T(8,128)(2,1)}, u32[]{:S(2)}, u32[]{:S(2)}) collective-permute-start(bf16[640,256]{1,0:T(8,128)(2,1)} %bitcast.15), channel_id=1, source_target_pairs={{0,4},{4,0},{1,5},{5,1},{2,6},{6,2},{3,7},{7,3},{8,12},{12,8},{9,1... | collective-permute-start | bytes 983048 | tf_op jit(solution)/shard_map/ppermute | solution.py:21
  85.6 2.4 %collective-permute-start.14 = (bf16[640,256]{1,0:T(8,128)(2,1)}, bf16[640,256]{1,0:T(8,128)(2,1)S(1)}, u32[]{:S(2)}, u32[]{:S(2)}) collective-permute-start(bf16[640,256]{1,0:T(8,128)(2,1)} %slice.15), channel_id=1, source_target_pairs={{0,3},{1,0},{2,1},{3,2},{4,7},{5,4},{6,5},{7,6},{8,11},{9,8},{10,9... | collective-permute-start | bytes 983048 | tf_op jit(solution)/shard_map/ppermute | solution.py:21
  90.1 6.0 %all-to-all-start.1 = ((bf16[32,24,640]{2,1,0:T(8,128)(2,1)}), bf16[32,24,640]{2,1,0:T(8,128)(2,1)}, u32[]{:S(2)}, u32[]{:S(2)}) async-start(bf16[32,24,640]{2,1,0:T(8,128)(2,1)} %bitcast.77), calls=%async_computation.1 | async-start | bytes 1966080 | tf_op jit(solution)/shard_map/all_to_all | solution.py:60
  96.2 1.3 copy-done.6
  97.5 5.1 %context_product.4.refs_4_ = f32[256,1280]{1,0:T(8,128)S(1)} custom-call(s32[2]{0:T(128)S(1)} %pad_add_fusion.1.which, bf16[1280,256]{1,0:T(8,128)(2,1)S(1)} %collective-permute-done.9.refs_0_, bf16[1280,256]{1,0:T(8,128)(2,1)S(1)} %collective-permute-done.8.refs_1_, bf16[5120,1280]{1,0:T(8,128)(2,1)} %refs_3_.3, bf16[5120,1280]{1,0:T(8,128)(2,1)} %refs_3_.3, ...), custom_call_target="tpu_custom_call" | custom-call | tf_op jit(solution)/shard_map/context_product/pallas_call | solution.py:112
  102.6 1.1 copy-done.3
  104.2 1.3 collective-permute-done.18
  108.2 5.4 %lay_out.1 = (bf16[8,160,256]{2,1,0:T(8,128)(2,1)S(1)}, bf16[8,160,256]{2,1,0:T(8,128)(2,1)}, bf16[8,160,256]{2,1,0:T(8,128)(2,1)}, bf16[8,160,256]{2,1,0:T(8,128)(2,1)}) custom-call(s32[4]{0:T(128)S(1)} %pad_add_fusion.3.where, bf16[4,2,160,256]{3,2,1,0:T(8,128)(2,1)S(1)} %bitcast.72, bf16[4,2,160,256]{3,2,1,0:T(8,128)(2,1)S(1)} %bitcast.76, ...), custom_call_target="tpu_custom_call" | custom-call | tf_op jit(solution)/shard_map/lay_out/pallas_call | solution.py:253
  113.6 1.4 collective-permute-start.19
  115.0 2.4 %collective-permute-start.20 = (bf16[1280,256]{1,0:T(8,128)(2,1)}, bf16[1280,256]{1,0:T(8,128)(2,1)S(1)}, u32[]{:S(2)}, u32[]{:S(2)}) collective-permute-start(bf16[1280,256]{1,0:T(8,128)(2,1)} %bitcast.43), channel_id=1, source_target_pairs={{0,64},{4,20},{8,72},{12,28},{16,80},{20,4},{24,88},{28,12},{32,96... | collective-permute-start | bytes 1966088 | tf_op jit(solution)/shard_map/ppermute | solution.py:36
  117.4 1.2 collective-permute-start.21
  118.7 1.3 copy.43
  122.7 5.8 %context_product.5 = bf16[768,640]{1,0:T(8,128)(2,1)} custom-call(s32[2]{0:T(128)S(1)} %pad_add_fusion.which, bf16[640,256]{1,0:T(8,128)(2,1)S(1)} %collective-permute-done.13.refs_0_, bf16[640,256]{1,0:T(8,128)(2,1)S(1)} %collective-permute-done.14.refs_1_, bf16[5120,1280]{1,0:T(8,128)(2,1)} %refs_3_.3, bf16[5120,1280]{1,0:T(8,128)(2,1)} %refs_3_.3, ...), custom_call_target="tpu_custom_call" | custom-call | tf_op jit(solution)/shard_map/context_product/pallas_call | solution.py:112
  128.4 4.6 %all-to-all-start.2 = ((bf16[32,24,640]{2,1,0:T(8,128)(2,1)}), bf16[32,24,640]{2,1,0:T(8,128)(2,1)}, u32[]{:S(2)}, u32[]{:S(2)}) async-start(bf16[32,24,640]{2,1,0:T(8,128)(2,1)} %bitcast.22), calls=%async_computation.2 | async-start | bytes 1966080 | tf_op jit(solution)/shard_map/all_to_all | solution.py:60
  134.9 1.1 copy-done.9
  136.0 1.1 copy-done.11
  137.1 8.2 %weight_product.1 = (f32[160,1280]{1,0:T(8,128)S(1)}, bf16[160,1280]{1,0:T(8,128)(2,1)}, bf16[160,1280]{1,0:T(8,128)(2,1)S(1)}, bf16[160,1280]{1,0:T(8,128)(2,1)S(1)}) custom-call(s32[4]{0:T(128)S(1)} %pad_add_fusion.2.order_ref, bf16[1280,256]{1,0:T(8,128)(2,1)S(1)} %bitcast.82, bf16[1280,256]{1,0:T(8,128)(2,1)S(1)} %copy-done.9, ...), custom_call_target="tpu_custom_call" | custom-call | tf_op jit(solution)/shard_map/weight_product/pallas_call | solution.py:290
  145.3 1.4 collective-permute-start.22
  146.7 2.4 %collective-permute-start.23 = (bf16[160,1280]{1,0:T(8,128)(2,1)S(1)}, bf16[160,1280]{1,0:T(8,128)(2,1)S(1)}, u32[]{:S(2)}, u32[]{:S(2)}) collective-permute-start(bf16[160,1280]{1,0:T(8,128)(2,1)S(1)} %get-tuple-element.69), channel_id=1, source_target_pairs={{0,16},{4,68},{8,24},{12,76},{16,0},{20,84},{24,8},{28,92},{32,48}... | collective-permute-start | bytes 1228808 | tf_op jit(solution)/shard_map/ppermute | solution.py:36
  149.1 1.1 collective-permute-start.24
  150.3 1.3 copy.45
  153.8 5.5 %collective-permute-done.23 = bf16[160,1280]{1,0:T(8,128)(2,1)S(1)} collective-permute-done((bf16[160,1280]{1,0:T(8,128)(2,1)S(1)}, bf16[160,1280]{1,0:T(8,128)(2,1)S(1)}, u32[]{:S(2)}, u32[]{:S(2)}) %collective-permute-start.23) | collective-permute-done | bytes 409632 | tf_op jit(solution)/shard_map/ppermute | solution.py:36
  159.4 1.1 add_multiply_fusion
  (114 shorter events, 24.3 us)
Async XLA Ops:
  0.6 1.1 copy-start
  1.7 7.6 %copy-start.1 = (bf16[256,1280]{1,0:T(8,128)(2,1)S(1)}, bf16[256,1280]{1,0:T(8,128)(2,1)}, u32[]{:S(2)}) copy-start(bf16[256,1280]{1,0:T(8,128)(2,1)} %context_ref.6) | copy-start | bytes 1966084
  4.6 12.1 %collective-permute-start = (bf16[640,256]{1,0:T(8,128)(2,1)S(1)}, bf16[640,256]{1,0:T(8,128)(2,1)S(1)}, u32[]{:S(2)}, u32[]{:S(2)}) collective-permute-start(bf16[640,256]{1,0:T(8,128)(2,1)S(1)} %get-tuple-element.37), channel_id=1, source_target_pairs={{0,1},{1,2},{2,3},{3,0},{4,5},{5,6},{6,7},{7,4},{8,9},{9,10},{10,1... | collective-permute-start | bytes 983048 | tf_op jit(solution)/shard_map/ppermute | solution.py:21
  7.1 9.6 %collective-permute-start.1 = (bf16[640,256]{1,0:T(8,128)(2,1)S(1)}, bf16[640,256]{1,0:T(8,128)(2,1)S(1)}, u32[]{:S(2)}, u32[]{:S(2)}) collective-permute-start(bf16[640,256]{1,0:T(8,128)(2,1)S(1)} %get-tuple-element.38), channel_id=1, source_target_pairs={{0,3},{1,0},{2,1},{3,2},{4,7},{5,4},{6,5},{7,6},{8,11},{9,8},{10,9... | collective-permute-start | bytes 983048 | tf_op jit(solution)/shard_map/ppermute | solution.py:21
  12.1 2.8 %copy-start.23 = (f32[4]{0:T(128)S(1)}, f32[4]{0:T(128)}, u32[]{:S(2)}) copy-start(f32[4]{0:T(128)} %param.14) | copy-start | bytes 52
  12.1 2.8 %copy-start.24 = (s32[4]{0:T(128)S(1)}, s32[4]{0:T(128)}, u32[]{:S(2)}) copy-start(s32[4]{0:T(128)} %param.15) | copy-start | bytes 52
  16.7 10.3 %copy-start.16 = (bf16[640,256]{1,0:T(8,128)(2,1)}, bf16[640,256]{1,0:T(8,128)(2,1)S(1)}, u32[]{:S(2)}) copy-start(bf16[640,256]{1,0:T(8,128)(2,1)S(1)} %collective-permute-done.1.part_ref) | copy-start | bytes 983044
  16.9 19.5 %collective-permute-start.4 = (bf16[256,1280]{1,0:T(8,128)(2,1)S(1)}, bf16[256,1280]{1,0:T(8,128)(2,1)}, u32[]{:S(2)}, u32[]{:S(2)}) collective-permute-start(bf16[256,1280]{1,0:T(8,128)(2,1)S(1)} %copy-done.1), channel_id=1, source_target_pairs={{0,4},{4,0},{1,5},{5,1},{2,6},{6,2},{3,7},{7,3},{8,12},{12,8},{9,1... | collective-permute-start | bytes 1966088 | tf_op jit(solution)/shard_map/ppermute | solution.py:21
  18.9 17.2 %all-to-all-start = ((f32[32,1,8]{2,1,0:T(1,128)}), f32[32,1,8]{2,1,0:T(1,128)S(1)}, u32[]{:S(2)}, u32[]{:S(2)}) async-start(f32[32,1,8]{2,1,0:T(1,128)} %broadcast_in_dim.16), calls=%async_computation | async-start | bytes 32768 | tf_op jit(solution)/shard_map/all_to_all | solution.py:41
  26.0 3.1 %copy-start.20 = (bf16[256,1280]{1,0:T(8,128)(2,1)S(1)}, bf16[256,1280]{1,0:T(8,128)(2,1)}, u32[]{:S(2)}) copy-start(bf16[256,1280]{1,0:T(8,128)(2,1)} %param.11) | copy-start | bytes 1966084
  30.2 17.6 %collective-permute-start.2 = (bf16[1280,256]{1,0:T(8,128)(2,1)S(1)}, bf16[1280,256]{1,0:T(8,128)(2,1)}, u32[]{:S(2)}, u32[]{:S(2)}) collective-permute-start(bf16[1280,256]{1,0:T(8,128)(2,1)S(1)} %top_up.2), channel_id=1, source_target_pairs={{0,1},{1,2},{2,3},{3,0},{4,5},{5,6},{6,7},{7,4},{8,9},{9,10},{10,1... | collective-permute-start | bytes 1966088 | tf_op jit(solution)/shard_map/ppermute | solution.py:21
  31.2 2.8 %copy-start.17 = (bf16[640,256]{1,0:T(8,128)(2,1)S(1)}, bf16[640,256]{1,0:T(8,128)(2,1)}, u32[]{:S(2)}) copy-start(bf16[640,256]{1,0:T(8,128)(2,1)} %copy-done.16) | copy-start | bytes 983044
  34.0 2.3 %copy-start.22 = (s32[4]{0:T(128)S(1)}, s32[4]{0:T(128)}, u32[]{:S(2)}) copy-start(s32[4]{0:T(128)} %param.16) | copy-start | bytes 52
  34.2 16.0 %collective-permute-start.3 = (bf16[1280,256]{1,0:T(8,128)(2,1)S(1)}, bf16[1280,256]{1,0:T(8,128)(2,1)}, u32[]{:S(2)}, u32[]{:S(2)}) collective-permute-start(bf16[1280,256]{1,0:T(8,128)(2,1)S(1)} %top_up.3), channel_id=1, source_target_pairs={{0,3},{1,0},{2,1},{3,2},{4,7},{5,4},{6,5},{7,6},{8,11},{9,8},{10,9... | collective-permute-start | bytes 1966088 | tf_op jit(solution)/shard_map/ppermute | solution.py:21
  38.5 13.2 %copy-start.18 = (bf16[256,1280]{0,1:T(8,128)(2,1)S(1)}, bf16[256,1280]{0,1:T(8,128)(2,1)}, u32[]{:S(2)}) copy-start(bf16[256,1280]{0,1:T(8,128)(2,1)} %copy.40) | copy-start | bytes 1966084
  38.5 13.2 %copy-start.19 = (bf16[256,1280]{0,1:T(8,128)(2,1)S(1)}, bf16[256,1280]{0,1:T(8,128)(2,1)}, u32[]{:S(2)}) copy-start(bf16[256,1280]{0,1:T(8,128)(2,1)} %copy.42) | copy-start | bytes 1966084
  38.5 13.2 %copy-start.21 = (f32[1280]{0:T(1024)S(1)}, f32[1280]{0:T(1024)}, u32[]{:S(2)}) copy-start(f32[1280]{0:T(1024)} %param.13) | copy-start | bytes 15364
  52.1 7.8 %collective-permute-start.5 = (f32[2,256]{1,0:T(2,128)S(1)}, f32[2,256]{1,0:T(2,128)S(1)}, u32[]{:S(2)}, u32[]{:S(2)}) collective-permute-start(f32[2,256]{1,0:T(2,128)S(1)} %pad_maximum_fusion.1), channel_id=1, source_target_pairs={{0,1},{1,2},{2,3},{3,0},{4,5},{5,6},{6,7},{7,4},{8,9},{9,10},{10,1... | collective-permute-start | bytes 6152 | tf_op jit(solution)/shard_map/ppermute | solution.py:21
  53.5 6.4 %collective-permute-start.6 = (f32[2,256]{1,0:T(2,128)S(1)}, f32[2,256]{1,0:T(2,128)S(1)}, u32[]{:S(2)}, u32[]{:S(2)}) collective-permute-start(f32[2,256]{1,0:T(2,128)S(1)} %pad_maximum_fusion.1), channel_id=1, source_target_pairs={{0,2},{1,3},{2,0},{3,1},{4,6},{5,7},{6,4},{7,5},{8,10},{9,11},{10,... | collective-permute-start | bytes 6152 | tf_op jit(solution)/shard_map/ppermute | solution.py:21
  56.4 3.5 %collective-permute-start.7 = (f32[2,256]{1,0:T(2,128)S(1)}, f32[2,256]{1,0:T(2,128)S(1)}, u32[]{:S(2)}, u32[]{:S(2)}) collective-permute-start(f32[2,256]{1,0:T(2,128)S(1)} %pad_maximum_fusion.1), channel_id=1, source_target_pairs={{0,3},{1,0},{2,1},{3,2},{4,7},{5,4},{6,5},{7,6},{8,11},{9,8},{10,9... | collective-permute-start | bytes 6152 | tf_op jit(solution)/shard_map/ppermute | solution.py:21
  57.2 18.3 %collective-permute-start.11 = (bf16[512,1280]{1,0:T(8,128)(2,1)}, bf16[512,1280]{1,0:T(8,128)(2,1)}, u32[]{:S(2)}, u32[]{:S(2)}) collective-permute-start(bf16[512,1280]{1,0:T(8,128)(2,1)} %constant_dynamic-update-slice_fusion.refs_4_), channel_id=1, source_target_pairs={{0,32},{4,12},{8,40},{12,20},{16,48},{20,28},{24,56},{28,4},{32,64... | collective-permute-start | bytes 3932168 | tf_op jit(solution)/shard_map/ppermute | solution.py:36
  58.4 17.1 %collective-permute-start.12 = (bf16[512,1280]{1,0:T(8,128)(2,1)}, bf16[512,1280]{1,0:T(8,128)(2,1)}, u32[]{:S(2)}, u32[]{:S(2)}) collective-permute-start(bf16[512,1280]{1,0:T(8,128)(2,1)} %constant_dynamic-update-slice_fusion.refs_4_), channel_id=1, source_target_pairs={{0,96},{4,28},{8,104},{12,4},{16,112},{20,12},{24,120},{28,20},{32... | collective-permute-start | bytes 3932168 | tf_op jit(solution)/shard_map/ppermute | solution.py:36
  59.9 6.6 %copy-start.25 = (s32[64,1]{0,1:T(1,128)S(1)}, s32[64,1]{0,1:T(1,128)}, u32[]{:S(2)}) copy-start(s32[64,1]{0,1:T(1,128)} %param.17) | copy-start | bytes 772
  60.4 14.9 %collective-permute-start.8 = (bf16[1280,256]{1,0:T(8,128)(2,1)S(1)}, bf16[1280,256]{1,0:T(8,128)(2,1)S(1)}, u32[]{:S(2)}, u32[]{:S(2)}) collective-permute-start(bf16[1280,256]{1,0:T(8,128)(2,1)S(1)} %fusion.3.refs_0_.grad_ref), channel_id=1, source_target_pairs={{0,1},{1,2},{2,3},{3,0},{4,5},{5,6},{6,7},{7,4},{8,9},{9,10},{10,1... | collective-permute-start | bytes 1966088 | tf_op jit(solution)/shard_map/ppermute | solution.py:21
  61.1 14.1 %collective-permute-start.9 = (bf16[1280,256]{1,0:T(8,128)(2,1)S(1)}, bf16[1280,256]{1,0:T(8,128)(2,1)S(1)}, u32[]{:S(2)}, u32[]{:S(2)}) collective-permute-start(bf16[1280,256]{1,0:T(8,128)(2,1)S(1)} %fusion.3.refs_0_.grad_ref), channel_id=1, source_target_pairs={{0,3},{1,0},{2,1},{3,2},{4,7},{5,4},{6,5},{7,6},{8,11},{9,8},{10,9... | collective-permute-start | bytes 1966088 | tf_op jit(solution)/shard_map/ppermute | solution.py:21
  63.1 7.7 %collective-permute-start.10 = (bf16[640,256]{1,0:T(8,128)(2,1)S(1)}, bf16[640,256]{1,0:T(8,128)(2,1)S(1)}, u32[]{:S(2)}, u32[]{:S(2)}) collective-permute-start(bf16[640,256]{1,0:T(8,128)(2,1)S(1)} %bitcast.92), channel_id=1, source_target_pairs={{0,4},{4,0},{1,5},{5,1},{2,6},{6,2},{3,7},{7,3},{8,12},{12,8},{9,1... | collective-permute-start | bytes 983048 | tf_op jit(solution)/shard_map/ppermute | solution.py:21
  69.7 1.1 copy-start.5
  70.8 14.4 %copy-start.12 = (bf16[640,256]{1,0:T(8,128)(2,1)}, bf16[640,256]{1,0:T(8,128)(2,1)S(1)}, u32[]{:S(2)}) copy-start(bf16[640,256]{1,0:T(8,128)(2,1)S(1)} %collective-permute-done.10) | copy-start | bytes 983044
  75.2 21.0 %copy-start.2 = (bf16[1280,256]{1,0:T(8,128)(2,1)}, bf16[1280,256]{1,0:T(8,128)(2,1)S(1)}, u32[]{:S(2)}) copy-start(bf16[1280,256]{1,0:T(8,128)(2,1)S(1)} %collective-permute-done.8.refs_1_) | copy-start | bytes 1966084
  75.5 28.2 %collective-permute-start.17 = (bf16[512,1280]{1,0:T(8,128)(2,1)}, bf16[512,1280]{1,0:T(8,128)(2,1)}, u32[]{:S(2)}, u32[]{:S(2)}) collective-permute-start(bf16[512,1280]{1,0:T(8,128)(2,1)} %constant_dynamic-update-slice_fusion.refs_4_), channel_id=1, source_target_pairs={{0,64},{4,20},{8,72},{12,28},{16,80},{20,4},{24,88},{28,12},{32,96... | collective-permute-start | bytes 3932168 | tf_op jit(solution)/shard_map/ppermute | solution.py:36
  79.7 24.0 %collective-permute-start.15 = (bf16[640,256]{1,0:T(8,128)(2,1)}, bf16[640,256]{1,0:T(8,128)(2,1)}, u32[]{:S(2)}, u32[]{:S(2)}) collective-permute-start(bf16[640,256]{1,0:T(8,128)(2,1)} %bitcast.15), channel_id=1, source_target_pairs={{0,4},{4,0},{1,5},{5,1},{2,6},{6,2},{3,7},{7,3},{8,12},{12,8},{9,1... | collective-permute-start | bytes 983048 | tf_op jit(solution)/shard_map/ppermute | solution.py:21
  85.2 18.5 %collective-permute-start.16 = (bf16[640,256]{1,0:T(8,128)(2,1)}, bf16[640,256]{1,0:T(8,128)(2,1)}, u32[]{:S(2)}, u32[]{:S(2)}) collective-permute-start(bf16[640,256]{1,0:T(8,128)(2,1)} %bitcast.17), channel_id=1, source_target_pairs={{0,4},{4,0},{1,5},{5,1},{2,6},{6,2},{3,7},{7,3},{8,12},{12,8},{9,1... | collective-permute-start | bytes 983048 | tf_op jit(solution)/shard_map/ppermute | solution.py:21
  85.2 18.5 %collective-permute-start.13 = (bf16[640,256]{1,0:T(8,128)(2,1)}, bf16[640,256]{1,0:T(8,128)(2,1)S(1)}, u32[]{:S(2)}, u32[]{:S(2)}) collective-permute-start(bf16[640,256]{1,0:T(8,128)(2,1)} %slice.14), channel_id=1, source_target_pairs={{0,1},{1,2},{2,3},{3,0},{4,5},{5,6},{6,7},{7,4},{8,9},{9,10},{10,1... | collective-permute-start | bytes 983048 | tf_op jit(solution)/shard_map/ppermute | solution.py:21
  85.6 18.1 %collective-permute-start.14 = (bf16[640,256]{1,0:T(8,128)(2,1)}, bf16[640,256]{1,0:T(8,128)(2,1)S(1)}, u32[]{:S(2)}, u32[]{:S(2)}) collective-permute-start(bf16[640,256]{1,0:T(8,128)(2,1)} %slice.15), channel_id=1, source_target_pairs={{0,3},{1,0},{2,1},{3,2},{4,7},{5,4},{6,5},{7,6},{8,11},{9,8},{10,9... | collective-permute-start | bytes 983048 | tf_op jit(solution)/shard_map/ppermute | solution.py:21
  90.1 28.6 %all-to-all-start.1 = ((bf16[32,24,640]{2,1,0:T(8,128)(2,1)}), bf16[32,24,640]{2,1,0:T(8,128)(2,1)}, u32[]{:S(2)}, u32[]{:S(2)}) async-start(bf16[32,24,640]{2,1,0:T(8,128)(2,1)} %bitcast.77), calls=%async_computation.1 | async-start | bytes 1966080 | tf_op jit(solution)/shard_map/all_to_all | solution.py:60
  96.2 1.3 copy-start.6
  102.6 1.1 copy-start.3
  103.8 1.7 %collective-permute-start.18 = (bf16[640,256]{1,0:T(8,128)(2,1)S(1)}, bf16[640,256]{1,0:T(8,128)(2,1)S(1)}, u32[]{:S(2)}, u32[]{:S(2)}) collective-permute-start(bf16[640,256]{1,0:T(8,128)(2,1)S(1)} %bitcast.91), channel_id=1, source_target_pairs={{0,4},{4,0},{1,5},{5,1},{2,6},{6,2},{3,7},{7,3},{8,12},{12,8},{9,1... | collective-permute-start | bytes 983048 | tf_op jit(solution)/shard_map/ppermute | solution.py:21
  113.6 19.7 %collective-permute-start.19 = (bf16[1280,256]{1,0:T(8,128)(2,1)}, bf16[1280,256]{1,0:T(8,128)(2,1)S(1)}, u32[]{:S(2)}, u32[]{:S(2)}) collective-permute-start(bf16[1280,256]{1,0:T(8,128)(2,1)} %bitcast.42), channel_id=1, source_target_pairs={{0,32},{4,12},{8,40},{12,20},{16,48},{20,28},{24,56},{28,4},{32,64... | collective-permute-start | bytes 1966088 | tf_op jit(solution)/shard_map/ppermute | solution.py:36
  115.0 19.1 %collective-permute-start.20 = (bf16[1280,256]{1,0:T(8,128)(2,1)}, bf16[1280,256]{1,0:T(8,128)(2,1)S(1)}, u32[]{:S(2)}, u32[]{:S(2)}) collective-permute-start(bf16[1280,256]{1,0:T(8,128)(2,1)} %bitcast.43), channel_id=1, source_target_pairs={{0,64},{4,20},{8,72},{12,28},{16,80},{20,4},{24,88},{28,12},{32,96... | collective-permute-start | bytes 1966088 | tf_op jit(solution)/shard_map/ppermute | solution.py:36
  117.4 17.5 %collective-permute-start.21 = (bf16[1280,256]{1,0:T(8,128)(2,1)}, bf16[1280,256]{1,0:T(8,128)(2,1)}, u32[]{:S(2)}, u32[]{:S(2)}) collective-permute-start(bf16[1280,256]{1,0:T(8,128)(2,1)} %bitcast.44), channel_id=1, source_target_pairs={{0,96},{4,28},{8,104},{12,4},{16,112},{20,12},{24,120},{28,20},{32... | collective-permute-start | bytes 1966088 | tf_op jit(solution)/shard_map/ppermute | solution.py:36
  121.0 1.7 %copy-start.4 = (f32[256,1280]{1,0:T(8,128)S(1)}, f32[256,1280]{1,0:T(8,128)}, u32[]{:S(2)}) copy-start(f32[256,1280]{1,0:T(8,128)} %copy-done.3) | copy-start | bytes 3932164
  128.4 21.8 %all-to-all-start.2 = ((bf16[32,24,640]{2,1,0:T(8,128)(2,1)}), bf16[32,24,640]{2,1,0:T(8,128)(2,1)}, u32[]{:S(2)}, u32[]{:S(2)}) async-start(bf16[32,24,640]{2,1,0:T(8,128)(2,1)} %bitcast.22), calls=%async_computation.2 | async-start | bytes 1966080 | tf_op jit(solution)/shard_map/all_to_all | solution.py:60
  134.9 1.1 copy-start.9
  136.0 1.1 copy-start.11
  145.3 8.5 %collective-permute-start.22 = (bf16[160,1280]{1,0:T(8,128)(2,1)}, bf16[160,1280]{1,0:T(8,128)(2,1)S(1)}, u32[]{:S(2)}, u32[]{:S(2)}) collective-permute-start(bf16[160,1280]{1,0:T(8,128)(2,1)} %get-tuple-element.68), channel_id=1, source_target_pairs={{0,8},{4,36},{8,16},{12,44},{16,24},{20,52},{24,0},{28,60},{32,40}... | collective-permute-start | bytes 1228808 | tf_op jit(solution)/shard_map/ppermute | solution.py:36
  146.7 12.7 %collective-permute-start.23 = (bf16[160,1280]{1,0:T(8,128)(2,1)S(1)}, bf16[160,1280]{1,0:T(8,128)(2,1)S(1)}, u32[]{:S(2)}, u32[]{:S(2)}) collective-permute-start(bf16[160,1280]{1,0:T(8,128)(2,1)S(1)} %get-tuple-element.69), channel_id=1, source_target_pairs={{0,16},{4,68},{8,24},{12,76},{16,0},{20,84},{24,8},{28,92},{32,48}... | collective-permute-start | bytes 1228808 | tf_op jit(solution)/shard_map/ppermute | solution.py:36
  149.1 10.2 %collective-permute-start.24 = (bf16[160,1280]{1,0:T(8,128)(2,1)S(1)}, bf16[160,1280]{1,0:T(8,128)(2,1)S(1)}, u32[]{:S(2)}, u32[]{:S(2)}) collective-permute-start(bf16[160,1280]{1,0:T(8,128)(2,1)S(1)} %get-tuple-element.70), channel_id=1, source_target_pairs={{0,24},{4,100},{8,0},{12,108},{16,8},{20,116},{24,16},{28,124},{32... | collective-permute-start | bytes 1228808 | tf_op jit(solution)/shard_map/ppermute | solution.py:36
  (6 other events, 5.3 us)

commit v9 on v8

--- a/solution.py
+++ b/solution.py
@@ -126,27 +126,22 @@
     )(jnp.stack(places), *operands)
 
 
-def place_rows(slots, grad_t):
-    half = grad_t.shape[0] // 2
-
-    def body(slots_ref, grad_ref, out_ref):
-        out_ref[...] = sum(
+def place_rows(slots, grad):
+    def body(slots_ref, *refs):
+        refs[-1][...] = sum(
             lax.dot_general(
-                slots_ref[i],
-                grad_ref[i * half : (i + 1) * half, :],
-                (((1,), (1,)), ((), ())),
-                preferred_element_type=F32,
+                slots_ref[i], refs[i][...], (((1,), (1,)), ((), ())), preferred_element_type=F32
             )
             for i in (0, 1)
         ).astype(BF16)
 
     return pl.pallas_call(
         body,
-        out_shape=jax.ShapeDtypeStruct((slots.shape[1], half), BF16),
+        out_shape=jax.ShapeDtypeStruct((slots.shape[1], grad[0].shape[0]), BF16),
         cost_estimate=FREE,
         compiler_params=PARAMS,
         name="place_rows",
-    )(slots, grad_t)
+    )(slots, *grad)
 
 
 def top_up(whole, part, half):
@@ -267,43 +262,6 @@
     return [value.reshape(8 * block, rows) for value in out]
 
 
-def weight_product(pieces, contexts, order, block):
-    count, tile = len(pieces), 640
-    height, rows = pieces[0].shape[0] // 2, pieces[0].shape[1]
-    width = contexts[0].shape[1]
-
-    def body(order_ref, *refs):
-        outs, total = refs[2 * count : 2 * count + 4], refs[-1]
-        total[...] = sum(
-            jnp.dot(
-                refs[i][core * height : (core + 1) * height, :],
-                refs[count + i][core * rows : (core + 1) * rows, :],
-                preferred_element_type=F32,
-            )
-            for i in range(count)
-            for core in (0, 1)
-        )
-        for k in range(4):
-            first = pl.multiple_of(order_ref[k] * block, block)
-            outs[k][...] = total[pl.ds(first, block), :].astype(outs[k].dtype)
-
-    return pl.pallas_call(
-        body,
-        out_shape=[jax.ShapeDtypeStruct((block, width), BF16 if k else F32) for k in range(4)],
-        grid_spec=pltpu.PrefetchScalarGridSpec(
-            num_scalar_prefetch=1,
-            grid=(width // tile,),
-            in_specs=[pl.BlockSpec((2 * height, rows), lambda n, order: (0, 0)) for _ in pieces]
-            + [pl.BlockSpec((2 * rows, tile), lambda n, order: (0, n)) for _ in contexts],
-            out_specs=[pl.BlockSpec((block, tile), lambda n, order: (0, n))] * 4,
-            scratch_shapes=[pltpu.VMEM((height, tile), F32)],
-        ),
-        cost_estimate=FREE,
-        compiler_params=PARAMS,
-        name="weight_product",
-    )(order, *pieces, *contexts)
-
-
 def per_device(
     context, residual, cotangent, out_proj, norm_gain, rewards, group_ids, lengths, destinations
 ):
@@ -314,39 +272,46 @@
 
     top = width // 2
     far_top, far_bottom = forward_product(out_proj, context, (z + 2) % NZ, True)
+    ready, _ = lax.optimization_barrier((context, far_top))
+    pair = jnp.concatenate([context, shift(ready, "c", 1)], axis=0)
     sent_top, sent_bottom = shift(far_top, "z", 1), shift(far_bottom, "z", 3)
     near = forward_product(out_proj, context, (z + 1) % NZ, False, BF16)
     back = forward_product(out_proj, context, (z + 3) % NZ, False, BF16)
-    sent_top, sent_bottom, near, back = lax.optimization_barrier(
-        (sent_top, sent_bottom, near, back)
+    sent_top, sent_bottom, near, back, pair = lax.optimization_barrier(
+        (sent_top, sent_bottom, near, back, pair)
     )
     near, back = top_up(near, sent_top, 0), top_up(back, sent_bottom, 1)
+
+    contexts = [pair, cross(pair, 1, True), None, cross(pair, 3, True)]
+    ready, _ = lax.optimization_barrier((context, near))
+    own = forward_product(out_proj, ready, z, False)
+    attn_t = own + shift(near, "z", 1).astype(F32) + shift(back, "z", 3).astype(F32)
+    attn_t, contexts[1], contexts[3] = lax.optimization_barrier(
+        (attn_t, contexts[1], contexts[3])
+    )
 
     groups = rewards.shape[0] * lanes // GROUP
     member = (group_ids[:, None] == jnp.arange(groups)[None, :]).astype(F32)
-    share, _ = lax.optimization_barrier((jnp.sum(member * rewards[:, None], axis=0), near))
+    share, _ = lax.optimization_barrier((jnp.sum(member * rewards[:, None], axis=0), own))
     group_total = group_sum(share)
     advantage = rewards - jnp.sum(member * group_total[None, :], axis=1) / GROUP
     scale = advantage * LMAX / (2.0 * lengths.astype(F32))
     live = jnp.arange(LMAX)[None, :] < lengths[:, None]
-    row_weights = jnp.where(live, scale[:, None], F32(0.0)).reshape(-1).astype(BF16)
-
-    ready, _ = lax.optimization_barrier((context, near))
-    pair = jnp.concatenate([context, shift(ready, "c", 1)], axis=0)
-    contexts = [pair, cross(pair, 1, True), None, cross(pair, 3, True)]
-    own = forward_product(out_proj, ready, z, False)
-    attn_t = own + shift(near, "z", 1).astype(F32) + shift(back, "z", 3).astype(F32)
-    attn_t, pair = lax.optimization_barrier((attn_t, pair))
+    row_weights = jnp.where(live, scale[:, None], F32(0.0)).reshape(-1).astype(BF16).astype(F32)
+
     hidden_t = residual.T.astype(F32) + attn_t
-    upstream_t = norm_gain[:, None] * (row_weights.astype(F32)[None, :] * cotangent.T.astype(F32))
+    gained_t = norm_gain[:, None] * cotangent.T.astype(F32)
     stats = jnp.stack(
-        [jnp.sum(hidden_t * hidden_t, axis=0), jnp.sum(upstream_t * hidden_t, axis=0)]
+        [jnp.sum(hidden_t * hidden_t, axis=0), jnp.sum(gained_t * hidden_t, axis=0)]
     )
     stats = stats + shift(stats, "z", 1) + shift(stats, "z", 2) + shift(stats, "z", 3)
     inv_rms = lax.rsqrt(stats[0] / full + EPSILON)
-    grad_t = (
-        inv_rms[None, :] * upstream_t - hidden_t * (inv_rms**3 * stats[1] / full)[None, :]
-    ).astype(BF16)
+    up_scale = inv_rms * row_weights
+    hidden_scale = inv_rms**3 * (row_weights * stats[1]) / full
+    grad = [
+        (up_scale[None, :] * gained_t[rows_of] - hidden_t[rows_of] * hidden_scale[None, :]).astype(BF16)
+        for rows_of in (slice(0, top), slice(top, width))
+    ]
 
     block = width // (NY * NC)
 
@@ -355,50 +320,60 @@
         asked = [lax.dynamic_index_in_dim(value, 1 - c, 1, keepdims=False) for value in parted]
         return shift(jnp.concatenate(asked, axis=0).reshape(-1, rows), "c", 1)
 
+    def places(step):
+        return [(z + step) % NZ * 2, (z + step) % NZ * 2 + 1]
+
     slots = slot_matrix(destinations[:, 0], lanes, rows)
-    from_left, from_right = shift(grad_t, "z", 1), shift(grad_t, "z", 3)
-    swapped = swap(grad_t)
-    grad_rows, _ = lax.optimization_barrier((grad_t, swapped))
+    left, right = [shift(grad[0], "z", 1), None], [None, shift(grad[1], "z", 3)]
+    left[1], right[0] = shift(grad[1], "z", 1), shift(grad[0], "z", 3)
+    far = [shift(left[0], "z", 1), shift(right[1], "z", 3)]
+    swapped = swap(*grad)
+    grad_rows, late_pair, _ = lax.optimization_barrier((tuple(grad), pair, swapped))
+    contexts[2] = cross(late_pair, 2, True)
     d_residual = exchange(place_rows(slots, grad_rows), lanes)
-    context_grad = context_product([grad_t], [z], out_proj)
-    from_left, from_right, context_grad, swapped, contexts[1], contexts[3] = (
-        lax.optimization_barrier(
-            (from_left, from_right, context_grad, swapped, contexts[1], contexts[3])
-        )
-    )
-    contexts[2] = cross(lax.optimization_barrier((pair, contexts[1]))[0], 2, True)
-    far_left, far_right = shift(from_left[:top], "z", 1), shift(from_right[top:], "z", 3)
-    swapped_left, swapped_right = swap(from_left), swap(from_right)
+    context_grad = context_product(grad, places(0), out_proj)
+    (left, right, context_grad, contexts[2]) = lax.optimization_barrier(
+        (left, right, context_grad, contexts[2])
+    )
     context_grad = context_product(
-        [from_right, from_left], [(z + 1) % NZ, (z + 3) % NZ], out_proj, before=context_grad
-    )
-    far_left, far_right, context_grad, swapped_left, swapped_right, contexts[2] = (
-        lax.optimization_barrier(
-            (far_left, far_right, context_grad, swapped_left, swapped_right, contexts[2])
-        )
-    )
-    def parted(*values):
+        right + left, places(1) + places(3), out_proj, before=context_grad
+    )
+    swap_left, swap_right, _ = lax.optimization_barrier((left, right, context_grad))
+    swapped_near = swap(*swap_right, *swap_left)
+    far, context_grad, swapped_near = lax.optimization_barrier((far, context_grad, swapped_near))
+
+    def blocks(values):
         return [value.reshape(-1, NC, block, rows) for value in values]
 
-    def single(value):
-        return [value.reshape(-1, block, rows)]
-
+    swapped_near = swapped_near.reshape(2, 4, block, rows)
     sends = lay_out(
-        [parted(grad_t), parted(from_right), parted(far_left, far_right), parted(from_left)],
-        [single(value) for value in (swapped, swapped_right, swap(far_left, far_right), swapped_left)],
+        [blocks(grad), blocks(right), blocks(far), blocks(left)],
+        [
+            [swapped.reshape(4, block, rows)],
+            [swapped_near[0]],
+            [swap(*far).reshape(4, block, rows)],
+            [swapped_near[1]],
+        ],
         x, y, c, z,
     )
+    sends, d_residual = lax.optimization_barrier((sends, d_residual))
     pieces = [sends[0]] + [cross(sends[k], k, True) for k in (1, 2, 3)]
-    far_place = (z + 2) % NZ * 2
-    placed = context_product(
-        [far_left, far_right], [far_place, far_place + 1], out_proj, before=context_grad, slots=slots
-    )
-    placed, d_residual = lax.optimization_barrier((placed, d_residual))
+    placed = context_product(far, places(2), out_proj, before=context_grad, slots=slots)
     d_context = exchange(placed, lanes)
+
+    total = 0.0
+    for k in (0, 1, 3, 2):
+        for core in (0, 1):
+            total = total + jnp.dot(
+                pieces[k].reshape(2, -1, rows)[core],
+                contexts[k].reshape(2, rows, width)[core],
+                preferred_element_type=F32,
+            )
+    total = total.reshape(4, block, width)
     order = [jnp.where(c == 0, (y + k) % NY, (x + k - z) % NZ) for k in range(4)]
-    d_out_proj, *parts = weight_product(pieces, contexts, jnp.stack(order), block)
+    d_out_proj = pick(total, order[0])
     for k in (1, 2, 3):
-        d_out_proj = d_out_proj + cross(parts[k - 1], k, False).astype(F32)
+        d_out_proj = d_out_proj + cross(pick(total, order[k]).astype(BF16), k, False).astype(F32)
     return (d_context, d_residual, d_out_proj / lanes)
 
 

time: 161 us -> 183 us (1.14)
  waiting for transfers between devices: 25.2 us -> 49.8 us
  matrix products: 0 us -> 14.4 us
  local copies, waits for them, and re-layouts: 29.5 us -> 16.6 us
  Pallas kernels: 39.8 us -> 31.9 us
  other arithmetic: 4.74 us -> 12.6 us
  starting transfers between devices: 60.2 us -> 55.8 us
    ppermute x9, waiting for transfers between devices: 5.96 us -> 22.2 us  [cross(): return lax.ppermute(value, DP, pairs)]
    dot_general x0 -> x8, matrix products: none -> 14.4 us  [per_device(): jnp.dot(pieces[k].reshape(2, -1, rows)[core], contexts[k].reshape(2, rows...]
    unnamed x57 -> x34, local copies, waits for them, and re-layouts: 18.9 us -> 9.96 us
    pallas_call x2 -> x1, Pallas kernels: 9.04 us -> 0.8 us  [place_rows(): pl.pallas_call(body, out_shape=jax.ShapeDtypeStruct((slots.shape[1], grad...]
    ppermute x16 -> x17, waiting for transfers between devices: 19.2 us -> 24.2 us  [shift(): lax.ppermute(value, axis, [(i, (i + step) % size) for i in range(size)])]
    ppermute x16 -> x17, starting transfers between devices: 27.3 us -> 23.8 us  [shift(): lax.ppermute(value, axis, [(i, (i + step) % size) for i in range(size)])]
    all_to_all x1, waiting for transfers between devices: 0.01 us -> 3.34 us  [group_sum(): lax.all_to_all(copies, DP, split_axis=0, concat_axis=0, tiled=True)]
    ppermute x9, starting transfers between devices: 15.1 us -> 12.1 us  [cross(): return lax.ppermute(value, DP, pairs)]
  transfers between devices with their start and end apart: 28 -> 29, of which waited for: 8 -> 13; matrix products, arithmetic and copies ran while one was open for 12% -> 19% of each run, Pallas kernels for 23% -> 13%
where the time goes in v9:
time: 183 us; the launch traced here: 182 us
  starting transfers between devices  55.8 us (30%)
  waiting for transfers between devices  49.8 us (27%)
  Pallas kernels  31.9 us (17%)
  local copies, waits for them, and re-layouts  16.6 us (9%)
  matrix products  14.4 us (8%)
  other arithmetic  12.6 us (7%)
    ppermute x17, waiting for transfers between devices, shift(): lax.ppermute(value, axis, [(i, (i + step) % size) for i in range(size)])  24.2 us
    ppermute x17, starting transfers between devices, shift(): lax.ppermute(value, axis, [(i, (i + step) % size) for i in range(size)])  23.8 us
    ppermute x9, waiting for transfers between devices, cross(): return lax.ppermute(value, DP, pairs)  22.2 us
    dot_general x8, matrix products, per_device(): jnp.dot(pieces[k].reshape(2, -1, rows)[core], contexts[k].reshape(2, rows...  14.4 us
    pallas_call x3, Pallas kernels, context_product(): pl.pallas_call(body, out_shape=jax.ShapeDtypeStruct((out_rows, width if s...  14 us
    ppermute x9, starting transfers between devices, cross(): return lax.ppermute(value, DP, pairs)  12.1 us
    all_to_all x2, starting transfers between devices, exchange(): got = lax.all_to_all(blocks, DP, split_axis=0, concat_axis=0, tiled=True)  11.6 us
    pallas_call x4, Pallas kernels, forward_product(): pl.pallas_call(body, out_shape=[jax.ShapeDtypeStruct((tile, rows), BF16)]...  11.6 us
  transfers between devices with their start and end apart: 29, of which 13 were waited for; matrix products, arithmetic and copies ran while one was open for 19% of the time, Pallas kernels for 13%

profile of v9, /device:TPU:1, one launch (start us, length us, event | category | flops | bytes accessed | tf_op | source)
XLA Modules:
  0.0 182.3 jit_solution(1381525372247666879)
XLA Ops:
  0.7 2.9 %forward_product.4 = (bf16[640,256]{1,0:T(8,128)(2,1)S(1)}, bf16[640,256]{1,0:T(8,128)(2,1)S(1)}) custom-call(s32[1]{0:T(128)} %bitcast.4.which, bf16[5120,1280]{1,0:T(8,128)(2,1)} %refs_3_.3, bf16[256,1280]{1,0:T(8,128)(2,1)} %context_ref.6), custom_call_target="tpu_custom_call" | custom-call | tf_op jit(solution)/shard_map/forward_product/pallas_call | solution.py:186
  3.6 1.5 collective-permute-start.2
  5.1 1.7 collective-permute-start
  6.9 2.1 %collective-permute-start.1 = (bf16[640,256]{1,0:T(8,128)(2,1)S(1)}, bf16[640,256]{1,0:T(8,128)(2,1)S(1)}, u32[]{:S(2)}, u32[]{:S(2)}) collective-permute-start(bf16[640,256]{1,0:T(8,128)(2,1)S(1)} %get-tuple-element.43), channel_id=1, source_target_pairs={{0,3},{1,0},{2,1},{3,2},{4,7},{5,4},{6,5},{7,6},{8,11},{9,8},{10,9... | collective-permute-start | bytes 983048 | tf_op jit(solution)/shard_map/ppermute | solution.py:21
  9.0 2.9 %forward_product.6.whole_ref = bf16[1280,256]{1,0:T(8,128)(2,1)S(1)} custom-call(s32[1]{0:T(128)} %bitcast.6.which, bf16[5120,1280]{1,0:T(8,128)(2,1)} %refs_3_.3, bf16[256,1280]{1,0:T(8,128)(2,1)} %context_ref.6), custom_call_target="tpu_custom_call" | custom-call | tf_op jit(solution)/shard_map/forward_product/pallas_call | solution.py:186
  11.9 2.9 %forward_product.5.whole_ref = bf16[1280,256]{1,0:T(8,128)(2,1)S(1)} custom-call(s32[1]{0:T(128)} %bitcast.5.which, bf16[5120,1280]{1,0:T(8,128)(2,1)} %refs_3_.3, bf16[256,1280]{1,0:T(8,128)(2,1)} %context_ref.6), custom_call_target="tpu_custom_call" | custom-call | tf_op jit(solution)/shard_map/forward_product/pallas_call | solution.py:186
  16.2 2.4 %pad_maximum_fusion = bf16[512,1280]{1,0:T(8,128)(2,1)} fusion(bf16[256,1280]{1,0:T(8,128)(2,1)} %collective-permute-done.2, bf16[256,1280]{1,0:T(8,128)(2,1)} %context_ref.6), kind=kLoop, calls=%fused_computation.9 | loop fusion | flops 2621440 | bytes 2621440 | tf_op jit(solution)/shard_map/concatenate | solution.py:276
  19.0 2.8 %collective-permute-start.6 = (bf16[512,1280]{1,0:T(8,128)(2,1)}, bf16[512,1280]{1,0:T(8,128)(2,1)}, u32[]{:S(2)}, u32[]{:S(2)}) collective-permute-start(bf16[512,1280]{1,0:T(8,128)(2,1)} %pad_maximum_fusion), channel_id=1, source_target_pairs={{0,96},{4,28},{8,104},{12,4},{16,112},{20,12},{24,120},{28,20},{32... | collective-permute-start | bytes 3932168 | tf_op jit(solution)/shard_map/ppermute | solution.py:36
  22.0 2.7 %collective-permute-start.4 = (bf16[1280,256]{1,0:T(8,128)(2,1)S(1)}, bf16[1280,256]{1,0:T(8,128)(2,1)}, u32[]{:S(2)}, u32[]{:S(2)}) collective-permute-start(bf16[1280,256]{1,0:T(8,128)(2,1)S(1)} %top_up.3), channel_id=1, source_target_pairs={{0,3},{1,0},{2,1},{3,2},{4,7},{5,4},{6,5},{7,6},{8,11},{9,8},{10,9... | collective-permute-start | bytes 1966088 | tf_op jit(solution)/shard_map/ppermute | solution.py:21
  24.7 2.9 %forward_product.7 = f32[1280,256]{1,0:T(8,128)S(1)} custom-call(s32[1]{0:T(128)} %bitcast.3.which, bf16[5120,1280]{1,0:T(8,128)(2,1)} %refs_3_.3, bf16[256,1280]{1,0:T(8,128)(2,1)} %context_ref.6), custom_call_target="tpu_custom_call" | custom-call | tf_op jit(solution)/shard_map/forward_product/pallas_call | solution.py:186
  28.2 8.3 %all-to-all-start = ((f32[32,1,8]{2,1,0:T(1,128)}), f32[32,1,8]{2,1,0:T(1,128)S(1)}, u32[]{:S(2)}, u32[]{:S(2)}) async-start(f32[32,1,8]{2,1,0:T(1,128)} %broadcast_in_dim.16), calls=%async_computation | async-start | bytes 32768 | tf_op jit(solution)/shard_map/all_to_all | solution.py:41
  37.8 2.2 %copy.40 = bf16[256,1280]{0,1:T(8,128)(2,1)} copy(bf16[256,1280]{1,0:T(8,128)(2,1)} %param.10) | data formatting | bytes 1310720 | tf_op args[1]
  40.0 3.3 %all-to-all-done = f32[32,1,8]{2,1,0:T(1,128)S(1)} async-done(((f32[32,1,8]{2,1,0:T(1,128)}), f32[32,1,8]{2,1,0:T(1,128)S(1)}, u32[]{:S(2)}, u32[]{:S(2)}) %all-to-all-start) | async-done | bytes 1056 | tf_op jit(solution)/shard_map/all_to_all | solution.py:41
  43.6 1.5 convert_add_fusion
  45.6 3.1 %collective-permute-start.8 = (f32[2,256]{1,0:T(2,128)S(1)}, f32[2,256]{1,0:T(2,128)S(1)}, u32[]{:S(2)}, u32[]{:S(2)}) collective-permute-start(f32[2,256]{1,0:T(2,128)S(1)} %pad_maximum_fusion.4), channel_id=1, source_target_pairs={{0,2},{1,3},{2,0},{3,1},{4,6},{5,7},{6,4},{7,5},{8,10},{9,11},{10,... | collective-permute-start | bytes 6152 | tf_op jit(solution)/shard_map/ppermute | solution.py:21
  51.2 1.9 %collective-permute-done.7 = f32[2,256]{1,0:T(2,128)S(1)} collective-permute-done((f32[2,256]{1,0:T(2,128)S(1)}, f32[2,256]{1,0:T(2,128)S(1)}, u32[]{:S(2)}, u32[]{:S(2)}) %collective-permute-start.7) | collective-permute-done | bytes 2080 | tf_op jit(solution)/shard_map/ppermute | solution.py:21
  53.1 1.5 fusion.10
  54.7 2.5 %collective-permute-start.16 = (bf16[640,256]{1,0:T(8,128)(2,1)S(1)}, bf16[640,256]{1,0:T(8,128)(2,1)S(1)}, u32[]{:S(2)}, u32[]{:S(2)}) collective-permute-start(bf16[640,256]{1,0:T(8,128)(2,1)S(1)} %bitcast.125), channel_id=1, source_target_pairs={{0,4},{4,0},{1,5},{5,1},{2,6},{6,2},{3,7},{7,3},{8,12},{12,8},{9,1... | collective-permute-start | bytes 983048 | tf_op jit(solution)/shard_map/ppermute | solution.py:21
  60.6 2.7 %collective-permute-start.12 = (bf16[640,256]{1,0:T(8,128)(2,1)S(1)}, bf16[640,256]{1,0:T(8,128)(2,1)S(1)}, u32[]{:S(2)}, u32[]{:S(2)}) collective-permute-start(bf16[640,256]{1,0:T(8,128)(2,1)S(1)} %get-tuple-element.72.refs_1_), channel_id=1, source_target_pairs={{0,3},{1,0},{2,1},{3,2},{4,7},{5,4},{6,5},{7,6},{8,11},{9,8},{10,9... | collective-permute-start | bytes 983048 | tf_op jit(solution)/shard_map/ppermute | solution.py:21
  63.3 1.4 collective-permute-start.10
  64.9 3.6 %context_product.3.refs_8_ = f32[256,1280]{1,0:T(8,128)S(1)} custom-call(s32[2]{0:T(128)S(1)} %pad_add_fusion.2.which, bf16[640,256]{1,0:T(8,128)(2,1)S(1)} %get-tuple-element.71.refs_0_, bf16[640,256]{1,0:T(8,128)(2,1)S(1)} %get-tuple-element.72.refs_1_, bf16[5120,1280]{1,0:T(8,128)(2,1)} %refs_3_.3, bf16[5120,1280]{1,0:T(8,128)(2,1)} %refs_3_.3), custom_call_target="tpu_custom_call" | custom-call | tf_op jit(solution)/shard_map/context_product/pallas_call | solution.py:112
  68.6 2.9 %collective-permute-done.14.refs_3_ = bf16[640,256]{1,0:T(8,128)(2,1)S(1)} collective-permute-done((bf16[640,256]{1,0:T(8,128)(2,1)S(1)}, bf16[640,256]{1,0:T(8,128)(2,1)S(1)}, u32[]{:S(2)}, u32[]{:S(2)}) %collective-permute-start.14) | collective-permute-done | bytes 327712 | tf_op jit(solution)/shard_map/ppermute | solution.py:21
  71.5 6.0 %collective-permute-done.15.refs_0_ = bf16[640,256]{1,0:T(8,128)(2,1)S(1)} collective-permute-done((bf16[640,256]{1,0:T(8,128)(2,1)S(1)}, bf16[640,256]{1,0:T(8,128)(2,1)S(1)}, u32[]{:S(2)}, u32[]{:S(2)}) %collective-permute-start.15) | collective-permute-done | bytes 327712 | tf_op jit(solution)/shard_map/ppermute | solution.py:21
  78.5 5.3 %context_product.4.refs_4_ = f32[256,1280]{1,0:T(8,128)S(1)} custom-call(s32[4]{0:T(128)S(1)} %pad_add_fusion.1.which, bf16[640,256]{1,0:T(8,128)(2,1)S(1)} %collective-permute-done.15.refs_0_, bf16[640,256]{1,0:T(8,128)(2,1)S(1)} %collective-permute-done.12.refs_1_, bf16[640,256]{1,0:T(8,128)(2,1)S(1)} %collective-permute-done.10.refs_2_, ...), custom_call_target="tpu_custom_call" | custom-call | tf_op jit(solution)/shard_map/context_product/pallas_call | solution.py:112
  87.4 4.4 %all-to-all-start.2 = ((bf16[32,24,640]{2,1,0:T(8,128)(2,1)}), bf16[32,24,640]{2,1,0:T(8,128)(2,1)}, u32[]{:S(2)}, u32[]{:S(2)}) async-start(bf16[32,24,640]{2,1,0:T(8,128)(2,1)} %bitcast.100), calls=%async_computation.2 | async-start | bytes 1966080 | tf_op jit(solution)/shard_map/all_to_all | solution.py:60
  91.8 2.8 %collective-permute-start.13 = (bf16[640,256]{1,0:T(8,128)(2,1)S(1)}, bf16[640,256]{1,0:T(8,128)(2,1)}, u32[]{:S(2)}, u32[]{:S(2)}) collective-permute-start(bf16[640,256]{1,0:T(8,128)(2,1)S(1)} %collective-permute-done.12.refs_1_), channel_id=1, source_target_pairs={{0,3},{1,0},{2,1},{3,2},{4,7},{5,4},{6,5},{7,6},{8,11},{9,8},{10,9... | collective-permute-start | bytes 983048 | tf_op jit(solution)/shard_map/ppermute | solution.py:21
  94.7 6.8 %collective-permute-done.13.refs_1_ = bf16[640,256]{1,0:T(8,128)(2,1)} collective-permute-done((bf16[640,256]{1,0:T(8,128)(2,1)S(1)}, bf16[640,256]{1,0:T(8,128)(2,1)}, u32[]{:S(2)}, u32[]{:S(2)}) %collective-permute-start.13) | collective-permute-done | bytes 327712 | tf_op jit(solution)/shard_map/ppermute | solution.py:21
  101.5 3.4 %collective-permute-done.11.refs_0_ = bf16[640,256]{1,0:T(8,128)(2,1)} collective-permute-done((bf16[640,256]{1,0:T(8,128)(2,1)}, bf16[640,256]{1,0:T(8,128)(2,1)}, u32[]{:S(2)}, u32[]{:S(2)}) %collective-permute-start.11) | collective-permute-done | bytes 327712 | tf_op jit(solution)/shard_map/ppermute | solution.py:21
  111.5 5.0 %context_product.5 = bf16[768,640]{1,0:T(8,128)(2,1)S(1)} custom-call(s32[2]{0:T(128)S(1)} %pad_add_fusion.which, bf16[640,256]{1,0:T(8,128)(2,1)} %collective-permute-done.11.refs_0_, bf16[640,256]{1,0:T(8,128)(2,1)} %collective-permute-done.13.refs_1_, bf16[5120,1280]{1,0:T(8,128)(2,1)} %refs_3_.3, bf16[5120,1280]{1,0:T(8,128)(2,1)} %refs_3_.3, ...), custom_call_target="tpu_custom_call" | custom-call | tf_op jit(solution)/shard_map/context_product/pallas_call | solution.py:112
  117.5 7.2 %all-to-all-start.1 = ((bf16[32,24,640]{2,1,0:T(8,128)(2,1)}), bf16[32,24,640]{2,1,0:T(8,128)(2,1)S(1)}, u32[]{:S(2)}, u32[]{:S(2)}) async-start(bf16[32,24,640]{2,1,0:T(8,128)(2,1)} %bitcast.101), calls=%async_computation.1 | async-start | bytes 1966080 | tf_op jit(solution)/shard_map/all_to_all | solution.py:60
  125.9 5.0 %lay_out.1 = (bf16[8,160,256]{2,1,0:T(8,128)(2,1)S(1)}, bf16[8,160,256]{2,1,0:T(8,128)(2,1)S(1)}, bf16[8,160,256]{2,1,0:T(8,128)(2,1)S(1)}, bf16[8,160,256]{2,1,0:T(8,128)(2,1)}) custom-call(s32[4]{0:T(128)S(1)} %pad_add_fusion.3.where, bf16[2,2,160,256]{3,2,1,0:T(8,128)(2,1)S(1)} %bitcast.99, bf16[2,2,160,256]{3,2,1,0:T(8,128)(2,1)S(1)} %bitcast.97, ...), custom_call_target="tpu_custom_call" | custom-call | tf_op jit(solution)/shard_map/lay_out/pallas_call | solution.py:248
  130.9 1.5 collective-permute-start.20
  133.6 1.7 collective-permute-start.22
  135.3 1.7 fusion.24
  137.0 1.7 convolution_add_fusion.1
  138.7 14.8 %collective-permute-done.22 = bf16[1280,256]{1,0:T(8,128)(2,1)S(1)} collective-permute-done((bf16[1280,256]{1,0:T(8,128)(2,1)S(1)}, bf16[1280,256]{1,0:T(8,128)(2,1)S(1)}, u32[]{:S(2)}, u32[]{:S(2)}) %collective-permute-start.22) | collective-permute-done | bytes 655392 | tf_op jit(solution)/shard_map/ppermute | solution.py:36
  153.6 1.7 fusion.13
  155.2 1.7 fusion.15
  156.9 1.7 fusion.17
  158.6 1.7 fusion.19
  160.3 1.7 fusion.21
  162.0 2.6 %fusion.4 = f32[640,1280]{1,0:T(8,128)S(1)} fusion(f32[640,1280]{1,0:T(8,128)S(1)} %fusion.13, f32[640,1280]{1,0:T(8,128)S(1)} %fusion.15, f32[640,1280]{1,0:T(8,128)S(1)} %fusion.17, f32[640,1280]{1,0:T(8,128)S(1)} %fusion.19, f32[640,1280]{1,0:T(8,128)S(1)} %fusion.21, f32[640,1280]{1,0:T(8,128)S(1)} %convolution_add_fusion.1, ...), kind=kOutput, calls=%fused_computation.6 | convolution fusion | flops 424345600 | bytes 23920640 | tf_op jit(solution)/shard_map/dot_general | solution.py:367
  164.6 1.7 copy-done.8
  167.3 1.8 collective-permute-start.25
  172.5 2.3 %collective-permute-done.23 = bf16[160,1280]{1,0:T(8,128)(2,1)S(1)} collective-permute-done((bf16[160,1280]{1,0:T(8,128)(2,1)S(1)}, bf16[160,1280]{1,0:T(8,128)(2,1)S(1)}, u32[]{:S(2)}, u32[]{:S(2)}) %collective-permute-start.23) | collective-permute-done | bytes 409632 | tf_op jit(solution)/shard_map/ppermute | solution.py:36
  174.8 3.7 %collective-permute-done.25 = bf16[160,1280]{1,0:T(8,128)(2,1)S(1)} collective-permute-done((bf16[160,1280]{1,0:T(8,128)(2,1)S(1)}, bf16[160,1280]{1,0:T(8,128)(2,1)S(1)}, u32[]{:S(2)}, u32[]{:S(2)}) %collective-permute-start.25) | collective-permute-done | bytes 409632 | tf_op jit(solution)/shard_map/ppermute | solution.py:36
  178.4 1.5 collective-permute-done.24
  179.9 2.4 %fusion.8 = f32[160,1280]{1,0:T(8,128)} fusion(bf16[160,1280]{1,0:T(8,128)(2,1)S(1)} %collective-permute-done.25, bf16[160,1280]{1,0:T(8,128)(2,1)} %collective-permute-done.24, bf16[160,1280]{1,0:T(8,128)(2,1)S(1)} %collective-permute-done.23, f32[4,160,1280]{2,1,0:T(8,128)} %bitcast.118, s32[]{:T(128)S(6)} %select_n.124), kind=kLoop, calls=%fused_computation.18 | loop fusion | flops 1433600 | bytes 2867204 | tf_op jit(solution)/shard_map/div | solution.py:377
  (106 shorter events, 29.8 us)
Async XLA Ops:
  0.6 8.3 %copy-start.12 = (f32[4]{0:T(128)S(1)}, f32[4]{0:T(128)}, u32[]{:S(2)}) copy-start(f32[4]{0:T(128)} %param.14) | copy-start | bytes 52
  0.7 8.3 %copy-start.13 = (s32[4]{0:T(128)S(1)}, s32[4]{0:T(128)}, u32[]{:S(2)}) copy-start(s32[4]{0:T(128)} %param.15) | copy-start | bytes 52
  3.6 12.6 %collective-permute-start.2 = (bf16[256,1280]{1,0:T(8,128)(2,1)}, bf16[256,1280]{1,0:T(8,128)(2,1)}, u32[]{:S(2)}, u32[]{:S(2)}) collective-permute-start(bf16[256,1280]{1,0:T(8,128)(2,1)} %context_ref.6), channel_id=1, source_target_pairs={{0,4},{4,0},{1,5},{5,1},{2,6},{6,2},{3,7},{7,3},{8,12},{12,8},{9,1... | collective-permute-start | bytes 1966088 | tf_op jit(solution)/shard_map/ppermute | solution.py:21
  5.1 13.5 %collective-permute-start = (bf16[640,256]{1,0:T(8,128)(2,1)S(1)}, bf16[640,256]{1,0:T(8,128)(2,1)S(1)}, u32[]{:S(2)}, u32[]{:S(2)}) collective-permute-start(bf16[640,256]{1,0:T(8,128)(2,1)S(1)} %get-tuple-element.42), channel_id=1, source_target_pairs={{0,1},{1,2},{2,3},{3,0},{4,5},{5,6},{6,7},{7,4},{8,9},{9,10},{10,1... | collective-permute-start | bytes 983048 | tf_op jit(solution)/shard_map/ppermute | solution.py:21
  6.9 11.8 %collective-permute-start.1 = (bf16[640,256]{1,0:T(8,128)(2,1)S(1)}, bf16[640,256]{1,0:T(8,128)(2,1)S(1)}, u32[]{:S(2)}, u32[]{:S(2)}) collective-permute-start(bf16[640,256]{1,0:T(8,128)(2,1)S(1)} %get-tuple-element.43), channel_id=1, source_target_pairs={{0,3},{1,0},{2,1},{3,2},{4,7},{5,4},{6,5},{7,6},{8,11},{9,8},{10,9... | collective-permute-start | bytes 983048 | tf_op jit(solution)/shard_map/ppermute | solution.py:21
  18.9 24.8 %collective-permute-start.3 = (bf16[1280,256]{1,0:T(8,128)(2,1)S(1)}, bf16[1280,256]{1,0:T(8,128)(2,1)}, u32[]{:S(2)}, u32[]{:S(2)}) collective-permute-start(bf16[1280,256]{1,0:T(8,128)(2,1)S(1)} %top_up.2), channel_id=1, source_target_pairs={{0,1},{1,2},{2,3},{3,0},{4,5},{5,6},{6,7},{7,4},{8,9},{9,10},{10,1... | collective-permute-start | bytes 1966088 | tf_op jit(solution)/shard_map/ppermute | solution.py:21
  19.0 26.2 %collective-permute-start.6 = (bf16[512,1280]{1,0:T(8,128)(2,1)}, bf16[512,1280]{1,0:T(8,128)(2,1)}, u32[]{:S(2)}, u32[]{:S(2)}) collective-permute-start(bf16[512,1280]{1,0:T(8,128)(2,1)} %pad_maximum_fusion), channel_id=1, source_target_pairs={{0,96},{4,28},{8,104},{12,4},{16,112},{20,12},{24,120},{28,20},{32... | collective-permute-start | bytes 3932168 | tf_op jit(solution)/shard_map/ppermute | solution.py:36
  21.7 23.4 %collective-permute-start.5 = (bf16[512,1280]{1,0:T(8,128)(2,1)}, bf16[512,1280]{1,0:T(8,128)(2,1)}, u32[]{:S(2)}, u32[]{:S(2)}) collective-permute-start(bf16[512,1280]{1,0:T(8,128)(2,1)} %pad_maximum_fusion), channel_id=1, source_target_pairs={{0,32},{4,12},{8,40},{12,20},{16,48},{20,28},{24,56},{28,4},{32,64... | collective-permute-start | bytes 3932168 | tf_op jit(solution)/shard_map/ppermute | solution.py:36
  22.0 21.6 %collective-permute-start.4 = (bf16[1280,256]{1,0:T(8,128)(2,1)S(1)}, bf16[1280,256]{1,0:T(8,128)(2,1)}, u32[]{:S(2)}, u32[]{:S(2)}) collective-permute-start(bf16[1280,256]{1,0:T(8,128)(2,1)S(1)} %top_up.3), channel_id=1, source_target_pairs={{0,3},{1,0},{2,1},{3,2},{4,7},{5,4},{6,5},{7,6},{8,11},{9,8},{10,9... | collective-permute-start | bytes 1966088 | tf_op jit(solution)/shard_map/ppermute | solution.py:21
  24.7 11.8 %copy-start.10 = (f32[1280]{0:T(1024)S(1)}, f32[1280]{0:T(1024)}, u32[]{:S(2)}) copy-start(f32[1280]{0:T(1024)} %param.13) | copy-start | bytes 15364
  28.2 15.2 %all-to-all-start = ((f32[32,1,8]{2,1,0:T(1,128)}), f32[32,1,8]{2,1,0:T(1,128)S(1)}, u32[]{:S(2)}, u32[]{:S(2)}) async-start(f32[32,1,8]{2,1,0:T(1,128)} %broadcast_in_dim.16), calls=%async_computation | async-start | bytes 32768 | tf_op jit(solution)/shard_map/all_to_all | solution.py:41
  36.5 7.1 %copy-start.11 = (s32[4]{0:T(128)S(1)}, s32[4]{0:T(128)}, u32[]{:S(2)}) copy-start(s32[4]{0:T(128)} %param.16) | copy-start | bytes 52
  43.6 1.6 copy-start.9
  45.6 4.7 %collective-permute-start.8 = (f32[2,256]{1,0:T(2,128)S(1)}, f32[2,256]{1,0:T(2,128)S(1)}, u32[]{:S(2)}, u32[]{:S(2)}) collective-permute-start(f32[2,256]{1,0:T(2,128)S(1)} %pad_maximum_fusion.4), channel_id=1, source_target_pairs={{0,2},{1,3},{2,0},{3,1},{4,6},{5,7},{6,4},{7,5},{8,10},{9,11},{10,... | collective-permute-start | bytes 6152 | tf_op jit(solution)/shard_map/ppermute | solution.py:21
  48.7 2.4 %collective-permute-start.9 = (f32[2,256]{1,0:T(2,128)S(1)}, f32[2,256]{1,0:T(2,128)S(1)}, u32[]{:S(2)}, u32[]{:S(2)}) collective-permute-start(f32[2,256]{1,0:T(2,128)S(1)} %pad_maximum_fusion.4), channel_id=1, source_target_pairs={{0,3},{1,0},{2,1},{3,2},{4,7},{5,4},{6,5},{7,6},{8,11},{9,8},{10,9... | collective-permute-start | bytes 6152 | tf_op jit(solution)/shard_map/ppermute | solution.py:21
  49.4 3.6 %collective-permute-start.7 = (f32[2,256]{1,0:T(2,128)S(1)}, f32[2,256]{1,0:T(2,128)S(1)}, u32[]{:S(2)}, u32[]{:S(2)}) collective-permute-start(f32[2,256]{1,0:T(2,128)S(1)} %pad_maximum_fusion.4), channel_id=1, source_target_pairs={{0,1},{1,2},{2,3},{3,0},{4,5},{5,6},{6,7},{7,4},{8,9},{9,10},{10,1... | collective-permute-start | bytes 6152 | tf_op jit(solution)/shard_map/ppermute | solution.py:21
  54.6 5.5 %copy-start.14 = (s32[64,1]{0,1:T(1,128)S(1)}, s32[64,1]{0,1:T(1,128)}, u32[]{:S(2)}) copy-start(s32[64,1]{0,1:T(1,128)} %param.17) | copy-start | bytes 772
  54.7 3.7 %collective-permute-start.16 = (bf16[640,256]{1,0:T(8,128)(2,1)S(1)}, bf16[640,256]{1,0:T(8,128)(2,1)S(1)}, u32[]{:S(2)}, u32[]{:S(2)}) collective-permute-start(bf16[640,256]{1,0:T(8,128)(2,1)S(1)} %bitcast.125), channel_id=1, source_target_pairs={{0,4},{4,0},{1,5},{5,1},{2,6},{6,2},{3,7},{7,3},{8,12},{12,8},{9,1... | collective-permute-start | bytes 983048 | tf_op jit(solution)/shard_map/ppermute | solution.py:21
  58.5 0.7 copy-start.6
  59.2 19.4 %collective-permute-start.17 = (bf16[512,1280]{1,0:T(8,128)(2,1)}, bf16[512,1280]{1,0:T(8,128)(2,1)}, u32[]{:S(2)}, u32[]{:S(2)}) collective-permute-start(bf16[512,1280]{1,0:T(8,128)(2,1)} %pad_maximum_fusion), channel_id=1, source_target_pairs={{0,64},{4,20},{8,72},{12,28},{16,80},{20,4},{24,88},{28,12},{32,96... | collective-permute-start | bytes 3932168 | tf_op jit(solution)/shard_map/ppermute | solution.py:36
  60.6 10.9 %collective-permute-start.14 = (bf16[640,256]{1,0:T(8,128)(2,1)S(1)}, bf16[640,256]{1,0:T(8,128)(2,1)S(1)}, u32[]{:S(2)}, u32[]{:S(2)}) collective-permute-start(bf16[640,256]{1,0:T(8,128)(2,1)S(1)} %get-tuple-element.72.refs_1_), channel_id=1, source_target_pairs={{0,1},{1,2},{2,3},{3,0},{4,5},{5,6},{6,7},{7,4},{8,9},{9,10},{10,1... | collective-permute-start | bytes 983048 | tf_op jit(solution)/shard_map/ppermute | solution.py:21
  60.6 10.9 %collective-permute-start.12 = (bf16[640,256]{1,0:T(8,128)(2,1)S(1)}, bf16[640,256]{1,0:T(8,128)(2,1)S(1)}, u32[]{:S(2)}, u32[]{:S(2)}) collective-permute-start(bf16[640,256]{1,0:T(8,128)(2,1)S(1)} %get-tuple-element.72.refs_1_), channel_id=1, source_target_pairs={{0,3},{1,0},{2,1},{3,2},{4,7},{5,4},{6,5},{7,6},{8,11},{9,8},{10,9... | collective-permute-start | bytes 983048 | tf_op jit(solution)/shard_map/ppermute | solution.py:21
  63.3 14.2 %collective-permute-start.15 = (bf16[640,256]{1,0:T(8,128)(2,1)S(1)}, bf16[640,256]{1,0:T(8,128)(2,1)S(1)}, u32[]{:S(2)}, u32[]{:S(2)}) collective-permute-start(bf16[640,256]{1,0:T(8,128)(2,1)S(1)} %get-tuple-element.71.refs_0_), channel_id=1, source_target_pairs={{0,3},{1,0},{2,1},{3,2},{4,7},{5,4},{6,5},{7,6},{8,11},{9,8},{10,9... | collective-permute-start | bytes 983048 | tf_op jit(solution)/shard_map/ppermute | solution.py:21
  63.3 15.2 %collective-permute-start.10 = (bf16[640,256]{1,0:T(8,128)(2,1)S(1)}, bf16[640,256]{1,0:T(8,128)(2,1)S(1)}, u32[]{:S(2)}, u32[]{:S(2)}) collective-permute-start(bf16[640,256]{1,0:T(8,128)(2,1)S(1)} %get-tuple-element.71.refs_0_), channel_id=1, source_target_pairs={{0,1},{1,2},{2,3},{3,0},{4,5},{5,6},{6,7},{7,4},{8,9},{9,10},{10,1... | collective-permute-start | bytes 983048 | tf_op jit(solution)/shard_map/ppermute | solution.py:21
  77.5 6.4 %copy-start.2 = (bf16[640,256]{1,0:T(8,128)(2,1)}, bf16[640,256]{1,0:T(8,128)(2,1)S(1)}, u32[]{:S(2)}) copy-start(bf16[640,256]{1,0:T(8,128)(2,1)S(1)} %collective-permute-done.15.refs_0_) | copy-start | bytes 983044
  78.5 5.4 %copy-start.4 = (bf16[640,256]{1,0:T(8,128)(2,1)}, bf16[640,256]{1,0:T(8,128)(2,1)S(1)}, u32[]{:S(2)}) copy-start(bf16[640,256]{1,0:T(8,128)(2,1)S(1)} %collective-permute-done.10.refs_2_) | copy-start | bytes 983044
  84.9 20.0 %collective-permute-start.18 = (bf16[1280,256]{1,0:T(8,128)(2,1)}, bf16[1280,256]{1,0:T(8,128)(2,1)}, u32[]{:S(2)}, u32[]{:S(2)}) collective-permute-start(bf16[1280,256]{1,0:T(8,128)(2,1)} %bitcast.31), channel_id=1, source_target_pairs={{0,4},{4,0},{1,5},{5,1},{2,6},{6,2},{3,7},{7,3},{8,12},{12,8},{9,1... | collective-permute-start | bytes 1966088 | tf_op jit(solution)/shard_map/ppermute | solution.py:21
  86.5 0.9 copy-start
  87.4 20.7 %all-to-all-start.2 = ((bf16[32,24,640]{2,1,0:T(8,128)(2,1)}), bf16[32,24,640]{2,1,0:T(8,128)(2,1)}, u32[]{:S(2)}, u32[]{:S(2)}) async-start(bf16[32,24,640]{2,1,0:T(8,128)(2,1)} %bitcast.100), calls=%async_computation.2 | async-start | bytes 1966080 | tf_op jit(solution)/shard_map/all_to_all | solution.py:60
  91.8 9.7 %collective-permute-start.13 = (bf16[640,256]{1,0:T(8,128)(2,1)S(1)}, bf16[640,256]{1,0:T(8,128)(2,1)}, u32[]{:S(2)}, u32[]{:S(2)}) collective-permute-start(bf16[640,256]{1,0:T(8,128)(2,1)S(1)} %collective-permute-done.12.refs_1_), channel_id=1, source_target_pairs={{0,3},{1,0},{2,1},{3,2},{4,7},{5,4},{6,5},{7,6},{8,11},{9,8},{10,9... | collective-permute-start | bytes 983048 | tf_op jit(solution)/shard_map/ppermute | solution.py:21
  94.6 10.3 %collective-permute-start.11 = (bf16[640,256]{1,0:T(8,128)(2,1)}, bf16[640,256]{1,0:T(8,128)(2,1)}, u32[]{:S(2)}, u32[]{:S(2)}) collective-permute-start(bf16[640,256]{1,0:T(8,128)(2,1)} %copy-done.4), channel_id=1, source_target_pairs={{0,1},{1,2},{2,3},{3,0},{4,5},{5,6},{6,7},{7,4},{8,9},{9,10},{10,1... | collective-permute-start | bytes 983048 | tf_op jit(solution)/shard_map/ppermute | solution.py:21
  106.7 19.2 %collective-permute-start.19 = (bf16[640,256]{1,0:T(8,128)(2,1)}, bf16[640,256]{1,0:T(8,128)(2,1)}, u32[]{:S(2)}, u32[]{:S(2)}) collective-permute-start(bf16[640,256]{1,0:T(8,128)(2,1)} %bitcast.49), channel_id=1, source_target_pairs={{0,4},{4,0},{1,5},{5,1},{2,6},{6,2},{3,7},{7,3},{8,12},{12,8},{9,1... | collective-permute-start | bytes 983048 | tf_op jit(solution)/shard_map/ppermute | solution.py:21
  116.6 0.9 copy-start.1
  117.5 8.3 %copy-start.3 = (bf16[640,256]{1,0:T(8,128)(2,1)S(1)}, bf16[640,256]{1,0:T(8,128)(2,1)}, u32[]{:S(2)}) copy-start(bf16[640,256]{1,0:T(8,128)(2,1)} %copy-done.2) | copy-start | bytes 983044
  117.5 8.3 %copy-start.5 = (bf16[640,256]{1,0:T(8,128)(2,1)S(1)}, bf16[640,256]{1,0:T(8,128)(2,1)}, u32[]{:S(2)}) copy-start(bf16[640,256]{1,0:T(8,128)(2,1)} %copy-done.4) | copy-start | bytes 983044
  117.5 8.3 %copy-start.7 = (bf16[640,256]{1,0:T(8,128)(2,1)S(1)}, bf16[640,256]{1,0:T(8,128)(2,1)}, u32[]{:S(2)}) copy-start(bf16[640,256]{1,0:T(8,128)(2,1)} %copy-done.6) | copy-start | bytes 983044
  117.5 52.8 %all-to-all-start.1 = ((bf16[32,24,640]{2,1,0:T(8,128)(2,1)}), bf16[32,24,640]{2,1,0:T(8,128)(2,1)S(1)}, u32[]{:S(2)}, u32[]{:S(2)}) async-start(bf16[32,24,640]{2,1,0:T(8,128)(2,1)} %bitcast.101), calls=%async_computation.1 | async-start | bytes 1966080 | tf_op jit(solution)/shard_map/all_to_all | solution.py:60
  130.9 29.4 %collective-permute-start.20 = (bf16[1280,256]{1,0:T(8,128)(2,1)S(1)}, bf16[1280,256]{1,0:T(8,128)(2,1)S(1)}, u32[]{:S(2)}, u32[]{:S(2)}) collective-permute-start(bf16[1280,256]{1,0:T(8,128)(2,1)S(1)} %bitcast.115), channel_id=1, source_target_pairs={{0,32},{4,12},{8,40},{12,20},{16,48},{20,28},{24,56},{28,4},{32,64... | collective-permute-start | bytes 1966088 | tf_op jit(solution)/shard_map/ppermute | solution.py:36
  132.3 24.6 %collective-permute-start.21 = (bf16[1280,256]{1,0:T(8,128)(2,1)}, bf16[1280,256]{1,0:T(8,128)(2,1)S(1)}, u32[]{:S(2)}, u32[]{:S(2)}) collective-permute-start(bf16[1280,256]{1,0:T(8,128)(2,1)} %bitcast.132), channel_id=1, source_target_pairs={{0,96},{4,28},{8,104},{12,4},{16,112},{20,12},{24,120},{28,20},{32... | collective-permute-start | bytes 1966088 | tf_op jit(solution)/shard_map/ppermute | solution.py:36
  133.6 19.9 %collective-permute-start.22 = (bf16[1280,256]{1,0:T(8,128)(2,1)S(1)}, bf16[1280,256]{1,0:T(8,128)(2,1)S(1)}, u32[]{:S(2)}, u32[]{:S(2)}) collective-permute-start(bf16[1280,256]{1,0:T(8,128)(2,1)S(1)} %bitcast.116), channel_id=1, source_target_pairs={{0,64},{4,20},{8,72},{12,28},{16,80},{20,4},{24,88},{28,12},{32,96... | collective-permute-start | bytes 1966088 | tf_op jit(solution)/shard_map/ppermute | solution.py:36
  164.6 1.7 copy-start.8
  166.4 8.4 %collective-permute-start.23 = (bf16[160,1280]{1,0:T(8,128)(2,1)S(1)}, bf16[160,1280]{1,0:T(8,128)(2,1)S(1)}, u32[]{:S(2)}, u32[]{:S(2)}) collective-permute-start(bf16[160,1280]{1,0:T(8,128)(2,1)S(1)} %get-tuple-element.84), channel_id=1, source_target_pairs={{0,8},{4,36},{8,16},{12,44},{16,24},{20,52},{24,0},{28,60},{32,40}... | collective-permute-start | bytes 1228808 | tf_op jit(solution)/shard_map/ppermute | solution.py:36
  167.3 11.1 %collective-permute-start.25 = (bf16[160,1280]{1,0:T(8,128)(2,1)S(1)}, bf16[160,1280]{1,0:T(8,128)(2,1)S(1)}, u32[]{:S(2)}, u32[]{:S(2)}) collective-permute-start(bf16[160,1280]{1,0:T(8,128)(2,1)S(1)} %get-tuple-element.85), channel_id=1, source_target_pairs={{0,24},{4,100},{8,0},{12,108},{16,8},{20,116},{24,16},{28,124},{32... | collective-permute-start | bytes 1228808 | tf_op jit(solution)/shard_map/ppermute | solution.py:36
  169.2 10.8 %collective-permute-start.24 = (bf16[160,1280]{1,0:T(8,128)(2,1)S(1)}, bf16[160,1280]{1,0:T(8,128)(2,1)}, u32[]{:S(2)}, u32[]{:S(2)}) collective-permute-start(bf16[160,1280]{1,0:T(8,128)(2,1)S(1)} %get-tuple-element.86), channel_id=1, source_target_pairs={{0,16},{4,68},{8,24},{12,76},{16,0},{20,84},{24,8},{28,92},{32,48}... | collective-permute-start | bytes 1228808 | tf_op jit(solution)/shard_map/ppermute | solution.py:36

commit v10 on v8

--- a/solution.py
+++ b/solution.py
@@ -9,6 +9,7 @@
 LMAX = 64
 GROUP = 16
 PAIR = 3
+BLOCK_ROWS = 4
 EPSILON = 1e-06
 NX, NY, NC, NZ = 4, 4, 2, 4
 DP = ("x", "y", "c")
@@ -36,30 +37,27 @@
     return lax.ppermute(value, DP, pairs)
 
 
-def group_sum(value):
+def all_shares(value):
     copies = jnp.broadcast_to(value, (NX * NY * NC,) + value.shape)
-    return jnp.sum(lax.all_to_all(copies, DP, split_axis=0, concat_axis=0, tiled=True), axis=0)
-
-
-def slot_matrix(owner_dest, lanes, rows):
+    return lax.all_to_all(copies, DP, split_axis=0, concat_axis=0, tiled=True)
+
+
+def slot_matrix(owner_dest, slots, rows, padded):
     count = owner_dest.shape[0]
     per_block = rows // count
-    kept = PAIR * per_block
     same = owner_dest[:, None] == owner_dest[None, :]
     earlier = jnp.arange(count)[None, :] < jnp.arange(count)[:, None]
     rank = jnp.sum((same & earlier).astype(jnp.int32), axis=1)
-    target = owner_dest * 2 * kept + rank * per_block
+    target = owner_dest * padded + rank * per_block
     row_target = jnp.repeat(target, per_block) + jnp.tile(jnp.arange(per_block), count)
-    row_target = row_target[None, None, :] + kept * jnp.arange(2)[:, None, None]
-    return (jnp.arange(lanes * 2 * kept)[None, :, None] == row_target).astype(BF16)
+    return (jnp.arange(slots // PAIR * padded)[:, None] == row_target[None, :]).astype(BF16)
 
 
 def exchange(packed, lanes):
-    height, half = packed.shape
-    blocks = packed.reshape((lanes, height // lanes, half))
+    blocks = packed.reshape((lanes, packed.shape[0] // lanes, packed.shape[1]))
     got = lax.all_to_all(blocks, DP, split_axis=0, concat_axis=0, tiled=True)
-    got = got.reshape((lanes, 2, height // lanes // 2, half))
-    return jnp.swapaxes(got, 1, 2).reshape(height // 2, 2 * half)
+    kept = PAIR * BLOCK_ROWS
+    return got[:, :kept].reshape(lanes * kept, packed.shape[1])
 
 
 FREE = pl.CostEstimate(flops=0, bytes_accessed=0, transcendentals=0)
@@ -82,18 +80,9 @@
         )
         if before is not None:
             total = total + refs[2 * count][...]
-        if slots is None:
-            out_ref[...] = total
-            return
-        total = jnp.dot(refs[-1][0], total.astype(BF16), preferred_element_type=F32)
-
-        @pl.when(pl.program_id(0) == 0)
-        def _():
-            out_ref[...] = total.astype(BF16)
-
-        @pl.when(pl.program_id(0) == 1)
-        def _():
-            out_ref[...] += total.astype(BF16)
+        if slots is not None:
+            total = jnp.dot(refs[-1][...], total.astype(BF16), preferred_element_type=F32)
+        out_ref[...] = total.astype(dtype)
 
     in_specs = [pl.BlockSpec(chunk.shape, lambda n, which: (0, 0)) for chunk in chunks]
     in_specs += [
@@ -106,19 +95,17 @@
         in_specs.append(pl.BlockSpec((rows, tile), lambda n, which: (0, n)))
         operands.append(before)
     if slots is not None:
-        in_specs.append(pl.BlockSpec((1,) + slots.shape[1:], lambda n, which: (n, 0, 0)))
+        in_specs.append(pl.BlockSpec(slots.shape, lambda n, which: (0, 0)))
         operands.append(slots)
-        out_rows = slots.shape[1]
+        out_rows = slots.shape[0]
     return pl.pallas_call(
         body,
-        out_shape=jax.ShapeDtypeStruct((out_rows, width if slots is None else tile), dtype),
+        out_shape=jax.ShapeDtypeStruct((out_rows, width), dtype),
         grid_spec=pltpu.PrefetchScalarGridSpec(
             num_scalar_prefetch=1,
             grid=(width // tile,),
             in_specs=in_specs,
-            out_specs=pl.BlockSpec(
-                (out_rows, tile), lambda n, which: (0, n if slots is None else 0)
-            ),
+            out_specs=pl.BlockSpec((out_rows, tile), lambda n, which: (0, n)),
         ),
         cost_estimate=FREE,
         compiler_params=PARAMS,
@@ -127,22 +114,14 @@
 
 
 def place_rows(slots, grad_t):
-    half = grad_t.shape[0] // 2
-
     def body(slots_ref, grad_ref, out_ref):
-        out_ref[...] = sum(
-            lax.dot_general(
-                slots_ref[i],
-                grad_ref[i * half : (i + 1) * half, :],
-                (((1,), (1,)), ((), ())),
-                preferred_element_type=F32,
-            )
-            for i in (0, 1)
+        out_ref[...] = lax.dot_general(
+            slots_ref[...], grad_ref[...], (((1,), (1,)), ((), ())), preferred_element_type=F32
         ).astype(BF16)
 
     return pl.pallas_call(
         body,
-        out_shape=jax.ShapeDtypeStruct((slots.shape[1], half), BF16),
+        out_shape=jax.ShapeDtypeStruct((slots.shape[0], grad_t.shape[0]), BF16),
         cost_estimate=FREE,
         compiler_params=PARAMS,
         name="place_rows",
@@ -256,7 +235,7 @@
         grid_spec=pltpu.PrefetchScalarGridSpec(
             num_scalar_prefetch=1,
             grid=(1,),
-            in_specs=[pl.BlockSpec(memory_space=pltpu.HBM)] * len(flat),
+            in_specs=[pl.BlockSpec(memory_space=pl.ANY)] * len(flat),
             out_specs=[pl.BlockSpec((8, block, rows), lambda i, where: (0, 0, 0))] * 4,
             scratch_shapes=[pltpu.SemaphoreType.DMA((4,))],
         ),
@@ -314,39 +293,43 @@
 
     top = width // 2
     far_top, far_bottom = forward_product(out_proj, context, (z + 2) % NZ, True)
+    ready, _ = lax.optimization_barrier((context, far_top))
+    pair = jnp.concatenate([context, shift(ready, "c", 1)], axis=0)
     sent_top, sent_bottom = shift(far_top, "z", 1), shift(far_bottom, "z", 3)
     near = forward_product(out_proj, context, (z + 1) % NZ, False, BF16)
     back = forward_product(out_proj, context, (z + 3) % NZ, False, BF16)
-    sent_top, sent_bottom, near, back = lax.optimization_barrier(
-        (sent_top, sent_bottom, near, back)
+    sent_top, sent_bottom, near, back, pair = lax.optimization_barrier(
+        (sent_top, sent_bottom, near, back, pair)
     )
     near, back = top_up(near, sent_top, 0), top_up(back, sent_bottom, 1)
 
+    ready, _, _ = lax.optimization_barrier((context, near, back))
+    own = forward_product(out_proj, ready, z, False)
+    late_pair, _ = lax.optimization_barrier((pair, own))
+    contexts = [pair] + [cross(late_pair, k, True) for k in (1, 2, 3)]
+    attn_t = own + shift(near, "z", 1).astype(F32) + shift(back, "z", 3).astype(F32)
+
+    hidden_t = residual.T.astype(F32) + attn_t
+    gained_t = norm_gain[:, None] * cotangent.T.astype(F32)
+    stats = jnp.stack(
+        [jnp.sum(hidden_t * hidden_t, axis=0), jnp.sum(gained_t * hidden_t, axis=0)]
+    )
     groups = rewards.shape[0] * lanes // GROUP
     member = (group_ids[:, None] == jnp.arange(groups)[None, :]).astype(F32)
-    share, _ = lax.optimization_barrier((jnp.sum(member * rewards[:, None], axis=0), near))
-    group_total = group_sum(share)
+    share, _ = lax.optimization_barrier((jnp.sum(member * rewards[:, None], axis=0), own))
+    shares, _ = lax.optimization_barrier((all_shares(share), stats))
+    group_total = jnp.sum(shares, axis=0)
     advantage = rewards - jnp.sum(member * group_total[None, :], axis=1) / GROUP
     scale = advantage * LMAX / (2.0 * lengths.astype(F32))
     live = jnp.arange(LMAX)[None, :] < lengths[:, None]
-    row_weights = jnp.where(live, scale[:, None], F32(0.0)).reshape(-1).astype(BF16)
-
-    ready, _ = lax.optimization_barrier((context, near))
-    pair = jnp.concatenate([context, shift(ready, "c", 1)], axis=0)
-    contexts = [pair, cross(pair, 1, True), None, cross(pair, 3, True)]
-    own = forward_product(out_proj, ready, z, False)
-    attn_t = own + shift(near, "z", 1).astype(F32) + shift(back, "z", 3).astype(F32)
-    attn_t, pair = lax.optimization_barrier((attn_t, pair))
-    hidden_t = residual.T.astype(F32) + attn_t
-    upstream_t = norm_gain[:, None] * (row_weights.astype(F32)[None, :] * cotangent.T.astype(F32))
-    stats = jnp.stack(
-        [jnp.sum(hidden_t * hidden_t, axis=0), jnp.sum(upstream_t * hidden_t, axis=0)]
-    )
+    row_weights = jnp.where(live, scale[:, None], F32(0.0)).reshape(-1).astype(BF16).astype(F32)
+
     stats = stats + shift(stats, "z", 1) + shift(stats, "z", 2) + shift(stats, "z", 3)
     inv_rms = lax.rsqrt(stats[0] / full + EPSILON)
-    grad_t = (
-        inv_rms[None, :] * upstream_t - hidden_t * (inv_rms**3 * stats[1] / full)[None, :]
-    ).astype(BF16)
+    up_scale = inv_rms * row_weights
+    hidden_scale = inv_rms**3 * (row_weights * stats[1]) / full
+    grad_t = (up_scale[None, :] * gained_t - hidden_t * hidden_scale[None, :]).astype(BF16)
+    grad_t, contexts[1], contexts[3] = lax.optimization_barrier((grad_t, contexts[1], contexts[3]))
 
     block = width // (NY * NC)
 
@@ -355,28 +338,24 @@
         asked = [lax.dynamic_index_in_dim(value, 1 - c, 1, keepdims=False) for value in parted]
         return shift(jnp.concatenate(asked, axis=0).reshape(-1, rows), "c", 1)
 
-    slots = slot_matrix(destinations[:, 0], lanes, rows)
+    slots = slot_matrix(destinations[:, 0], lanes * PAIR, rows, 16)
     from_left, from_right = shift(grad_t, "z", 1), shift(grad_t, "z", 3)
     swapped = swap(grad_t)
     grad_rows, _ = lax.optimization_barrier((grad_t, swapped))
     d_residual = exchange(place_rows(slots, grad_rows), lanes)
     context_grad = context_product([grad_t], [z], out_proj)
-    from_left, from_right, context_grad, swapped, contexts[1], contexts[3] = (
-        lax.optimization_barrier(
-            (from_left, from_right, context_grad, swapped, contexts[1], contexts[3])
-        )
-    )
-    contexts[2] = cross(lax.optimization_barrier((pair, contexts[1]))[0], 2, True)
+    from_left, from_right, context_grad, swapped, contexts[2] = lax.optimization_barrier(
+        (from_left, from_right, context_grad, swapped, contexts[2])
+    )
     far_left, far_right = shift(from_left[:top], "z", 1), shift(from_right[top:], "z", 3)
-    swapped_left, swapped_right = swap(from_left), swap(from_right)
     context_grad = context_product(
         [from_right, from_left], [(z + 1) % NZ, (z + 3) % NZ], out_proj, before=context_grad
     )
-    far_left, far_right, context_grad, swapped_left, swapped_right, contexts[2] = (
-        lax.optimization_barrier(
-            (far_left, far_right, context_grad, swapped_left, swapped_right, contexts[2])
-        )
-    )
+    far_left, far_right, context_grad = lax.optimization_barrier(
+        (far_left, far_right, context_grad)
+    )
+    swapped_right, swapped_left = jnp.split(swap(from_right, from_left), 2)
+    swapped_far = swap(far_left, far_right)
     def parted(*values):
         return [value.reshape(-1, NC, block, rows) for value in values]
 
@@ -385,9 +364,10 @@
 
     sends = lay_out(
         [parted(grad_t), parted(from_right), parted(far_left, far_right), parted(from_left)],
-        [single(value) for value in (swapped, swapped_right, swap(far_left, far_right), swapped_left)],
+        [single(value) for value in (swapped, swapped_right, swapped_far, swapped_left)],
         x, y, c, z,
     )
+    far_left, far_right, sends = lax.optimization_barrier((far_left, far_right, sends))
     pieces = [sends[0]] + [cross(sends[k], k, True) for k in (1, 2, 3)]
     far_place = (z + 2) % NZ * 2
     placed = context_product(

time: 161 us -> 140 us (0.87)
  local copies, waits for them, and re-layouts: 29.5 us -> 16.1 us
  starting transfers between devices: 60.2 us -> 50.6 us
  other arithmetic: 4.74 us -> 9.37 us
  waiting for transfers between devices: 25.2 us -> 21.2 us
    ppermute x16 -> x15, waiting for transfers between devices: 19.2 us -> 0.56 us  [shift(): lax.ppermute(value, axis, [(i, (i + step) % size) for i in range(size)])]
    unnamed x57 -> x28, local copies, waits for them, and re-layouts: 18.9 us -> 7.57 us
    ppermute x9, waiting for transfers between devices: 5.96 us -> 15.4 us  [cross(): return lax.ppermute(value, DP, pairs)]
    all_to_all x1, waiting for transfers between devices: 0.01 us -> 5.18 us  [all_shares(): return lax.all_to_all(copies, DP, split_axis=0, concat_axis=0, tiled=True)]
    ppermute x16 -> x15, starting transfers between devices: 27.3 us -> 22.1 us  [shift(): lax.ppermute(value, axis, [(i, (i + step) % size) for i in range(size)])]
    ppermute x9, starting transfers between devices: 15.1 us -> 11.8 us  [cross(): return lax.ppermute(value, DP, pairs)]
    reshape x0 -> x2, local copies, waits for them, and re-layouts: none -> 3.23 us  [exchange(): return got[:, :kept].reshape(lanes * kept, packed.shape[1])]
    reduce_sum x1, other arithmetic: 0.41 us -> 3.32 us  [per_device(): jnp.sum(hidden_t * hidden_t, axis=0)]
  transfers between devices with their start and end apart: 28 -> 27, of which waited for: 8 -> 7; matrix products, arithmetic and copies ran while one was open for 12% -> 15% of each run, Pallas kernels for 23% -> 27%
where the time goes in v10:
time: 140 us
  starting transfers between devices  50.6 us (36%)
  Pallas kernels  41.2 us (29%)
  waiting for transfers between devices  21.2 us (15%)
  local copies, waits for them, and re-layouts  16.1 us (12%)
  other arithmetic  9.37 us (7%)
    ppermute x15, starting transfers between devices, shift(): lax.ppermute(value, axis, [(i, (i + step) % size) for i in range(size)])  22.1 us
    ppermute x9, waiting for transfers between devices, cross(): return lax.ppermute(value, DP, pairs)  15.4 us
    pallas_call x3, Pallas kernels, context_product(): pl.pallas_call(body, out_shape=jax.ShapeDtypeStruct((out_rows, width), dt...  13.4 us
    pallas_call x4, Pallas kernels, forward_product(): pl.pallas_call(body, out_shape=[jax.ShapeDtypeStruct((tile, rows), BF16)]...  12.3 us
    ppermute x9, starting transfers between devices, cross(): return lax.ppermute(value, DP, pairs)  11.8 us
    all_to_all x2, starting transfers between devices, exchange(): got = lax.all_to_all(blocks, DP, split_axis=0, concat_axis=0, tiled=True)  9.12 us
    unnamed x28, local copies, waits for them, and re-layouts  7.57 us
    all_to_all x1, starting transfers between devices, all_shares(): return lax.all_to_all(copies, DP, split_axis=0, concat_axis=0, tiled=True)  7.55 us
  transfers between devices with their start and end apart: 27, of which 7 were waited for; matrix products, arithmetic and copies ran while one was open for 15% of the time, Pallas kernels for 27%

profile of v10, /device:TPU:1, one launch (start us, length us, event | category | flops | bytes accessed | tf_op | source)
XLA Modules:
  0.0 139.6 jit_solution(12331440136896392090)
XLA Ops:
  0.6 2.9 %forward_product.4 = (bf16[640,256]{1,0:T(8,128)(2,1)S(1)}, bf16[640,256]{1,0:T(8,128)(2,1)S(1)}) custom-call(s32[1]{0:T(128)} %bitcast.4.which, bf16[5120,1280]{1,0:T(8,128)(2,1)} %refs_3_.3, bf16[256,1280]{1,0:T(8,128)(2,1)} %context_ref.6), custom_call_target="tpu_custom_call" | custom-call | tf_op jit(solution)/shard_map/forward_product/pallas_call | solution.py:170
  3.6 1.5 %collective-permute-start.2 = (bf16[256,1280]{1,0:T(8,128)(2,1)}, bf16[256,1280]{1,0:T(8,128)(2,1)}, u32[]{:S(2)}, u32[]{:S(2)}) collective-permute-start(bf16[256,1280]{1,0:T(8,128)(2,1)} %context_ref.6), channel_id=1, source_target_pairs={{0,4},{4,0},{1,5},{5,1},{2,6},{6,2},{3,7},{7,3},{8,12},{12,8},{9,1... | collective-permute-start | bytes 1966088 | tf_op jit(solution)/shard_map/ppermute | solution.py:22
  5.1 1.8 %collective-permute-start = (bf16[640,256]{1,0:T(8,128)(2,1)S(1)}, bf16[640,256]{1,0:T(8,128)(2,1)S(1)}, u32[]{:S(2)}, u32[]{:S(2)}) collective-permute-start(bf16[640,256]{1,0:T(8,128)(2,1)S(1)} %get-tuple-element.43), channel_id=1, source_target_pairs={{0,1},{1,2},{2,3},{3,0},{4,5},{5,6},{6,7},{7,4},{8,9},{9,10},{10,1... | collective-permute-start | bytes 983048 | tf_op jit(solution)/shard_map/ppermute | solution.py:22
  6.8 2.1 %collective-permute-start.1 = (bf16[640,256]{1,0:T(8,128)(2,1)S(1)}, bf16[640,256]{1,0:T(8,128)(2,1)S(1)}, u32[]{:S(2)}, u32[]{:S(2)}) collective-permute-start(bf16[640,256]{1,0:T(8,128)(2,1)S(1)} %get-tuple-element.44), channel_id=1, source_target_pairs={{0,3},{1,0},{2,1},{3,2},{4,7},{5,4},{6,5},{7,6},{8,11},{9,8},{10,9... | collective-permute-start | bytes 983048 | tf_op jit(solution)/shard_map/ppermute | solution.py:22
  8.9 2.9 %forward_product.5.whole_ref = bf16[1280,256]{1,0:T(8,128)(2,1)S(1)} custom-call(s32[1]{0:T(128)} %bitcast.5.which, bf16[5120,1280]{1,0:T(8,128)(2,1)} %refs_3_.3, bf16[256,1280]{1,0:T(8,128)(2,1)} %context_ref.6), custom_call_target="tpu_custom_call" | custom-call | tf_op jit(solution)/shard_map/forward_product/pallas_call | solution.py:170
  11.8 3.6 %forward_product.6.whole_ref = bf16[1280,256]{1,0:T(8,128)(2,1)} custom-call(s32[1]{0:T(128)} %bitcast.6.which, bf16[5120,1280]{1,0:T(8,128)(2,1)} %refs_3_.3, bf16[256,1280]{1,0:T(8,128)(2,1)} %context_ref.6), custom_call_target="tpu_custom_call" | custom-call | tf_op jit(solution)/shard_map/forward_product/pallas_call | solution.py:170
  15.4 1.4 pad_maximum_fusion.refs_4_
  17.7 1.8 %top_up.3 = bf16[1280,256]{1,0:T(8,128)(2,1)} custom-call(bf16[1280,256]{1,0:T(8,128)(2,1)} %forward_product.6.whole_ref, bf16[640,256]{1,0:T(8,128)(2,1)S(1)} %collective-permute-done.1.part_ref), custom_call_target="tpu_custom_call", output_to_operand_aliasing={{}: (0, {})} | custom-call | tf_op jit(solution)/shard_map/top_up/pallas_call | solution.py:139
  19.5 2.2 %collective-permute-start.4 = (bf16[1280,256]{1,0:T(8,128)(2,1)}, bf16[1280,256]{1,0:T(8,128)(2,1)}, u32[]{:S(2)}, u32[]{:S(2)}) collective-permute-start(bf16[1280,256]{1,0:T(8,128)(2,1)} %top_up.3), channel_id=1, source_target_pairs={{0,3},{1,0},{2,1},{3,2},{4,7},{5,4},{6,5},{7,6},{8,11},{9,8},{10,9... | collective-permute-start | bytes 1966088 | tf_op jit(solution)/shard_map/ppermute | solution.py:22
  21.7 2.2 %copy.19 = bf16[256,1280]{0,1:T(8,128)(2,1)} copy(bf16[256,1280]{1,0:T(8,128)(2,1)} %param.11) | data formatting | bytes 1310720 | tf_op args[2]
  23.9 2.2 %copy.18 = bf16[256,1280]{0,1:T(8,128)(2,1)} copy(bf16[256,1280]{1,0:T(8,128)(2,1)} %param.10) | data formatting | bytes 1310720 | tf_op args[1]
  26.3 2.9 %forward_product.7 = f32[1280,256]{1,0:T(8,128)S(1)} custom-call(s32[1]{0:T(128)} %bitcast.3.which, bf16[5120,1280]{1,0:T(8,128)(2,1)} %refs_3_.3, bf16[256,1280]{1,0:T(8,128)(2,1)} %context_ref.6), custom_call_target="tpu_custom_call" | custom-call | tf_op jit(solution)/shard_map/forward_product/pallas_call | solution.py:170
  29.2 1.4 collective-permute-start.8
  30.6 1.5 %collective-permute-start.9 = (bf16[512,1280]{1,0:T(8,128)(2,1)S(1)}, bf16[512,1280]{1,0:T(8,128)(2,1)}, u32[]{:S(2)}, u32[]{:S(2)}) collective-permute-start(bf16[512,1280]{1,0:T(8,128)(2,1)S(1)} %pad_maximum_fusion.refs_4_), channel_id=1, source_target_pairs={{0,96},{4,28},{8,104},{12,4},{16,112},{20,12},{24,120},{28,20},{32... | collective-permute-start | bytes 3932168 | tf_op jit(solution)/shard_map/ppermute | solution.py:37
  32.7 7.5 %all-to-all-start = ((f32[32,1,8]{2,1,0:T(1,128)}), f32[32,1,8]{2,1,0:T(1,128)S(1)}, u32[]{:S(2)}, u32[]{:S(2)}) async-start(f32[32,1,8]{2,1,0:T(1,128)} %broadcast_in_dim.12), calls=%async_computation | async-start | bytes 32768 | tf_op jit(solution)/shard_map/all_to_all | solution.py:42
  40.3 3.3 %multiply_reduce_fusion = (f32[256]{0:T(256)S(1)}, f32[256]{0:T(256)S(1)}, f32[1280,256]{1,0:T(8,128)}) fusion(bf16[256,1280]{0,1:T(8,128)(2,1)} %copy.19, f32[1280]{0:T(1024)S(1)} %copy-done.8, bf16[1280,256]{1,0:T(8,128)(2,1)} %collective-permute-done.4, f32[1280,256]{1,0:T(8,128)S(1)} %forward_product.7, bf16[1280,256]{1,0:T(8,128)(2,1)} %collective-permute-done.3, ...), kind=kLoop, calls=%fused_computation.8 | loop fusion | flops 3931648 | bytes 5250048 | tf_op jit(solution)/shard_map/reduce_sum | solution.py:315
  43.7 2.6 %collective-permute-start.6 = (f32[2,256]{1,0:T(2,128)S(1)}, f32[2,256]{1,0:T(2,128)S(1)}, u32[]{:S(2)}, u32[]{:S(2)}) collective-permute-start(f32[2,256]{1,0:T(2,128)S(1)} %pad_maximum_fusion.3), channel_id=1, source_target_pairs={{0,2},{1,3},{2,0},{3,1},{4,6},{5,7},{6,4},{7,5},{8,10},{9,11},{10,... | collective-permute-start | bytes 6152 | tf_op jit(solution)/shard_map/ppermute | solution.py:22
  46.3 0.9 collective-permute-start.7
  47.2 5.2 %all-to-all-done = f32[32,1,8]{2,1,0:T(1,128)S(1)} async-done(((f32[32,1,8]{2,1,0:T(1,128)}), f32[32,1,8]{2,1,0:T(1,128)S(1)}, u32[]{:S(2)}, u32[]{:S(2)}) %all-to-all-start) | async-done | bytes 1056 | tf_op jit(solution)/shard_map/all_to_all | solution.py:42
  52.8 1.0 collective-permute-start.13
  53.8 1.6 %fusion.2.refs_0_.grad_ref = bf16[1280,256]{1,0:T(8,128)(2,1)S(1)} fusion(f32[1280,256]{1,0:T(8,128)} %get-tuple-element.85, bf16[256,1280]{0,1:T(8,128)(2,1)S(1)} %copy-done.7, f32[256]{0:T(256)S(1)} %bitcast.78, f32[256]{0:T(256)S(1)} %bitcast.77, f32[1280]{0:T(1024)S(1)} %copy-done.8), kind=kLoop, calls=%fused_computation.5 | loop fusion | flops 1966080 | bytes 2628608 | tf_op jit(solution)/shard_map/convert_element_type | solution.py:331
  55.6 2.7 %collective-permute-start.11 = (bf16[1280,256]{1,0:T(8,128)(2,1)S(1)}, bf16[1280,256]{1,0:T(8,128)(2,1)S(1)}, u32[]{:S(2)}, u32[]{:S(2)}) collective-permute-start(bf16[1280,256]{1,0:T(8,128)(2,1)S(1)} %fusion.2.refs_0_.grad_ref), channel_id=1, source_target_pairs={{0,3},{1,0},{2,1},{3,2},{4,7},{5,4},{6,5},{7,6},{8,11},{9,8},{10,9... | collective-permute-start | bytes 1966088 | tf_op jit(solution)/shard_map/ppermute | solution.py:22
  59.0 2.3 %collective-permute-start.12 = (bf16[640,256]{1,0:T(8,128)(2,1)}, bf16[640,256]{1,0:T(8,128)(2,1)}, u32[]{:S(2)}, u32[]{:S(2)}) collective-permute-start(bf16[640,256]{1,0:T(8,128)(2,1)} %bitcast.14), channel_id=1, source_target_pairs={{0,4},{4,0},{1,5},{5,1},{2,6},{6,2},{3,7},{7,3},{8,12},{12,8},{9,1... | collective-permute-start | bytes 983048 | tf_op jit(solution)/shard_map/ppermute | solution.py:22
  61.5 3.0 %context_product.3.refs_4_ = f32[256,1280]{1,0:T(8,128)S(1)} custom-call(s32[1]{0:T(128)} %bitcast.3.which, bf16[1280,256]{1,0:T(8,128)(2,1)S(1)} %fusion.2.refs_0_.grad_ref, bf16[5120,1280]{1,0:T(8,128)(2,1)} %refs_3_.3), custom_call_target="tpu_custom_call" | custom-call | tf_op jit(solution)/shard_map/context_product/pallas_call | solution.py:101
  64.5 1.1 copy-done.1
  65.6 1.7 %place_rows.1 = bf16[512,1280]{1,0:T(8,128)(2,1)} custom-call(bf16[512,256]{1,0:T(8,128)(2,1)S(1)} %fusion.3.refs_5_.slots_ref, bf16[1280,256]{1,0:T(8,128)(2,1)S(1)} %fusion.2.refs_0_.grad_ref), custom_call_target="tpu_custom_call" | custom-call | tf_op jit(solution)/shard_map/place_rows/pallas_call | solution.py:122
  67.3 4.5 %all-to-all-start.1 = ((bf16[32,16,1280]{2,1,0:T(8,128)(2,1)}), bf16[32,16,1280]{2,1,0:T(8,128)(2,1)}, u32[]{:S(2)}, u32[]{:S(2)}) async-start(bf16[32,16,1280]{2,1,0:T(8,128)(2,1)} %bitcast.37), calls=%async_computation.1 | async-start | bytes 2621440 | tf_op jit(solution)/shard_map/all_to_all | solution.py:58
  73.4 2.7 %collective-permute-start.15 = (bf16[640,256]{1,0:T(8,128)(2,1)}, bf16[640,256]{1,0:T(8,128)(2,1)}, u32[]{:S(2)}, u32[]{:S(2)}) collective-permute-start(bf16[640,256]{1,0:T(8,128)(2,1)} %slice.21), channel_id=1, source_target_pairs={{0,3},{1,0},{2,1},{3,2},{4,7},{5,4},{6,5},{7,6},{8,11},{9,8},{10,9... | collective-permute-start | bytes 983048 | tf_op jit(solution)/shard_map/ppermute | solution.py:22
  76.1 0.9 pad_maximum_fusion.1
  77.0 2.7 %collective-permute-start.16 = (bf16[1280,256]{1,0:T(8,128)(2,1)}, bf16[1280,256]{1,0:T(8,128)(2,1)}, u32[]{:S(2)}, u32[]{:S(2)}) collective-permute-start(bf16[1280,256]{1,0:T(8,128)(2,1)} %bitcast.25), channel_id=1, source_target_pairs={{0,4},{4,0},{1,5},{5,1},{2,6},{6,2},{3,7},{7,3},{8,12},{12,8},{9,1... | collective-permute-start | bytes 1966088 | tf_op jit(solution)/shard_map/ppermute | solution.py:22
  79.8 1.3 copy-done.2
  81.1 5.1 %context_product.4.refs_4_ = f32[256,1280]{1,0:T(8,128)S(1)} custom-call(s32[2]{0:T(128)S(1)} %pad_add_fusion.1.which, bf16[1280,256]{1,0:T(8,128)(2,1)S(1)} %collective-permute-done.11.refs_0_, bf16[1280,256]{1,0:T(8,128)(2,1)S(1)} %collective-permute-done.10.refs_1_, bf16[5120,1280]{1,0:T(8,128)(2,1)} %refs_3_.3, bf16[5120,1280]{1,0:T(8,128)(2,1)} %refs_3_.3, ...), custom_call_target="tpu_custom_call" | custom-call | tf_op jit(solution)/shard_map/context_product/pallas_call | solution.py:101
  86.2 1.0 dynamic-slice_bitcast_fusion.2
  87.4 1.1 fusion.11
  89.0 4.3 %lay_out.1 = (bf16[8,160,256]{2,1,0:T(8,128)(2,1)S(1)}, bf16[8,160,256]{2,1,0:T(8,128)(2,1)}, bf16[8,160,256]{2,1,0:T(8,128)(2,1)}, bf16[8,160,256]{2,1,0:T(8,128)(2,1)}) custom-call(s32[4]{0:T(128)S(1)} %pad_add_fusion.2.where, bf16[4,2,160,256]{3,2,1,0:T(8,128)(2,1)S(1)} %bitcast.61, bf16[4,2,160,256]{3,2,1,0:T(8,128)(2,1)S(1)} %bitcast.65, ...), custom_call_target="tpu_custom_call" | custom-call | tf_op jit(solution)/shard_map/lay_out/pallas_call | solution.py:232
  94.5 2.6 %collective-permute-start.19 = (bf16[1280,256]{1,0:T(8,128)(2,1)}, bf16[1280,256]{1,0:T(8,128)(2,1)}, u32[]{:S(2)}, u32[]{:S(2)}) collective-permute-start(bf16[1280,256]{1,0:T(8,128)(2,1)} %bitcast.34), channel_id=1, source_target_pairs={{0,64},{4,20},{8,72},{12,28},{16,80},{20,4},{24,88},{28,12},{32,96... | collective-permute-start | bytes 1966088 | tf_op jit(solution)/shard_map/ppermute | solution.py:37
  97.1 1.1 collective-permute-start.20
  98.2 5.4 %context_product.5 = bf16[512,1280]{1,0:T(8,128)(2,1)} custom-call(s32[2]{0:T(128)S(1)} %pad_add_fusion.which, bf16[640,256]{1,0:T(8,128)(2,1)} %collective-permute-done.14.refs_0_, bf16[640,256]{1,0:T(8,128)(2,1)} %collective-permute-done.15.refs_1_, bf16[5120,1280]{1,0:T(8,128)(2,1)} %refs_3_.3, bf16[5120,1280]{1,0:T(8,128)(2,1)} %refs_3_.3, ...), custom_call_target="tpu_custom_call" | custom-call | tf_op jit(solution)/shard_map/context_product/pallas_call | solution.py:101
  103.6 2.2 %reshape.173 = bf16[384,1280]{1,0:T(8,128)(2,1)} reshape(bf16[32,12,1280]{2,1,0:T(8,128)(2,1)} %bitcast.58) | data formatting | bytes 1966080 | tf_op jit(solution)/shard_map/reshape | solution.py:60
  105.8 4.7 %all-to-all-start.2 = ((bf16[32,16,1280]{2,1,0:T(8,128)(2,1)}), bf16[32,16,1280]{2,1,0:T(8,128)(2,1)S(1)}, u32[]{:S(2)}, u32[]{:S(2)}) async-start(bf16[32,16,1280]{2,1,0:T(8,128)(2,1)} %bitcast.38), calls=%async_computation.2 | async-start | bytes 2621440 | tf_op jit(solution)/shard_map/all_to_all | solution.py:58
  110.6 1.9 %collective-permute-done.19.refs_2_ = bf16[1280,256]{1,0:T(8,128)(2,1)} collective-permute-done((bf16[1280,256]{1,0:T(8,128)(2,1)}, bf16[1280,256]{1,0:T(8,128)(2,1)}, u32[]{:S(2)}, u32[]{:S(2)}) %collective-permute-start.19) | collective-permute-done | bytes 655392 | tf_op jit(solution)/shard_map/ppermute | solution.py:37
  112.9 7.5 %weight_product.1 = (f32[160,1280]{1,0:T(8,128)S(1)}, bf16[160,1280]{1,0:T(8,128)(2,1)S(1)}, bf16[160,1280]{1,0:T(8,128)(2,1)S(1)}, bf16[160,1280]{1,0:T(8,128)(2,1)S(1)}) custom-call(s32[4]{0:T(128)S(1)} %pad_add_fusion.3.order_ref, bf16[1280,256]{1,0:T(8,128)(2,1)S(1)} %bitcast.68, bf16[1280,256]{1,0:T(8,128)(2,1)} %collective-permute-done.18.refs_1_, ...), custom_call_target="tpu_custom_call" | custom-call | tf_op jit(solution)/shard_map/weight_product/pallas_call | solution.py:269
  120.5 1.2 collective-permute-start.21
  121.6 2.2 %collective-permute-start.22 = (bf16[160,1280]{1,0:T(8,128)(2,1)S(1)}, bf16[160,1280]{1,0:T(8,128)(2,1)S(1)}, u32[]{:S(2)}, u32[]{:S(2)}) collective-permute-start(bf16[160,1280]{1,0:T(8,128)(2,1)S(1)} %get-tuple-element.81), channel_id=1, source_target_pairs={{0,16},{4,68},{8,24},{12,76},{16,0},{20,84},{24,8},{28,92},{32,48}... | collective-permute-start | bytes 1228808 | tf_op jit(solution)/shard_map/ppermute | solution.py:37
  124.4 8.5 %collective-permute-done.21 = bf16[160,1280]{1,0:T(8,128)(2,1)S(1)} collective-permute-done((bf16[160,1280]{1,0:T(8,128)(2,1)S(1)}, bf16[160,1280]{1,0:T(8,128)(2,1)S(1)}, u32[]{:S(2)}, u32[]{:S(2)}) %collective-permute-start.21) | collective-permute-done | bytes 409632 | tf_op jit(solution)/shard_map/ppermute | solution.py:37
  132.8 4.6 %collective-permute-done.22 = bf16[160,1280]{1,0:T(8,128)(2,1)S(1)} collective-permute-done((bf16[160,1280]{1,0:T(8,128)(2,1)S(1)}, bf16[160,1280]{1,0:T(8,128)(2,1)S(1)}, u32[]{:S(2)}, u32[]{:S(2)}) %collective-permute-start.22) | collective-permute-done | bytes 409632 | tf_op jit(solution)/shard_map/ppermute | solution.py:37
  137.5 1.1 add_multiply_fusion
  138.6 1.1 reshape.175
  (80 shorter events, 8.1 us)
Async XLA Ops:
  3.6 11.8 %collective-permute-start.2 = (bf16[256,1280]{1,0:T(8,128)(2,1)}, bf16[256,1280]{1,0:T(8,128)(2,1)}, u32[]{:S(2)}, u32[]{:S(2)}) collective-permute-start(bf16[256,1280]{1,0:T(8,128)(2,1)} %context_ref.6), channel_id=1, source_target_pairs={{0,4},{4,0},{1,5},{5,1},{2,6},{6,2},{3,7},{7,3},{8,12},{12,8},{9,1... | collective-permute-start | bytes 1966088 | tf_op jit(solution)/shard_map/ppermute | solution.py:22
  5.1 11.8 %collective-permute-start = (bf16[640,256]{1,0:T(8,128)(2,1)S(1)}, bf16[640,256]{1,0:T(8,128)(2,1)S(1)}, u32[]{:S(2)}, u32[]{:S(2)}) collective-permute-start(bf16[640,256]{1,0:T(8,128)(2,1)S(1)} %get-tuple-element.43), channel_id=1, source_target_pairs={{0,1},{1,2},{2,3},{3,0},{4,5},{5,6},{6,7},{7,4},{8,9},{9,10},{10,1... | collective-permute-start | bytes 983048 | tf_op jit(solution)/shard_map/ppermute | solution.py:22
  6.8 10.1 %collective-permute-start.1 = (bf16[640,256]{1,0:T(8,128)(2,1)S(1)}, bf16[640,256]{1,0:T(8,128)(2,1)S(1)}, u32[]{:S(2)}, u32[]{:S(2)}) collective-permute-start(bf16[640,256]{1,0:T(8,128)(2,1)S(1)} %get-tuple-element.44), channel_id=1, source_target_pairs={{0,3},{1,0},{2,1},{3,2},{4,7},{5,4},{6,5},{7,6},{8,11},{9,8},{10,9... | collective-permute-start | bytes 983048 | tf_op jit(solution)/shard_map/ppermute | solution.py:22
  16.8 36.0 %copy-start.3 = (bf16[512,1280]{1,0:T(8,128)(2,1)}, bf16[512,1280]{1,0:T(8,128)(2,1)S(1)}, u32[]{:S(2)}) copy-start(bf16[512,1280]{1,0:T(8,128)(2,1)S(1)} %pad_maximum_fusion.refs_4_) | copy-start | bytes 3932164
  17.2 23.1 %collective-permute-start.3 = (bf16[1280,256]{1,0:T(8,128)(2,1)S(1)}, bf16[1280,256]{1,0:T(8,128)(2,1)}, u32[]{:S(2)}, u32[]{:S(2)}) collective-permute-start(bf16[1280,256]{1,0:T(8,128)(2,1)S(1)} %top_up.2), channel_id=1, source_target_pairs={{0,1},{1,2},{2,3},{3,0},{4,5},{5,6},{6,7},{7,4},{8,9},{9,10},{10,1... | collective-permute-start | bytes 1966088 | tf_op jit(solution)/shard_map/ppermute | solution.py:22
  19.5 6.5 %copy-start.12 = (s32[64,1]{0,1:T(1,128)S(1)}, s32[64,1]{0,1:T(1,128)}, u32[]{:S(2)}) copy-start(s32[64,1]{0,1:T(1,128)} %param.17) | copy-start | bytes 772
  19.5 6.7 %copy-start.10 = (f32[4]{0:T(128)S(1)}, f32[4]{0:T(128)}, u32[]{:S(2)}) copy-start(f32[4]{0:T(128)} %param.14) | copy-start | bytes 52
  19.5 6.7 %copy-start.11 = (s32[4]{0:T(128)S(1)}, s32[4]{0:T(128)}, u32[]{:S(2)}) copy-start(s32[4]{0:T(128)} %param.15) | copy-start | bytes 52
  19.5 20.8 %collective-permute-start.4 = (bf16[1280,256]{1,0:T(8,128)(2,1)}, bf16[1280,256]{1,0:T(8,128)(2,1)}, u32[]{:S(2)}, u32[]{:S(2)}) collective-permute-start(bf16[1280,256]{1,0:T(8,128)(2,1)} %top_up.3), channel_id=1, source_target_pairs={{0,3},{1,0},{2,1},{3,2},{4,7},{5,4},{6,5},{7,6},{8,11},{9,8},{10,9... | collective-permute-start | bytes 1966088 | tf_op jit(solution)/shard_map/ppermute | solution.py:22
  26.3 14.0 %copy-start.8 = (f32[1280]{0:T(1024)S(1)}, f32[1280]{0:T(1024)}, u32[]{:S(2)}) copy-start(f32[1280]{0:T(1024)} %param.13) | copy-start | bytes 15364
  29.2 26.3 %collective-permute-start.8 = (bf16[512,1280]{1,0:T(8,128)(2,1)S(1)}, bf16[512,1280]{1,0:T(8,128)(2,1)}, u32[]{:S(2)}, u32[]{:S(2)}) collective-permute-start(bf16[512,1280]{1,0:T(8,128)(2,1)S(1)} %pad_maximum_fusion.refs_4_), channel_id=1, source_target_pairs={{0,32},{4,12},{8,40},{12,20},{16,48},{20,28},{24,56},{28,4},{32,64... | collective-permute-start | bytes 3932168 | tf_op jit(solution)/shard_map/ppermute | solution.py:37
  30.6 24.9 %collective-permute-start.9 = (bf16[512,1280]{1,0:T(8,128)(2,1)S(1)}, bf16[512,1280]{1,0:T(8,128)(2,1)}, u32[]{:S(2)}, u32[]{:S(2)}) collective-permute-start(bf16[512,1280]{1,0:T(8,128)(2,1)S(1)} %pad_maximum_fusion.refs_4_), channel_id=1, source_target_pairs={{0,96},{4,28},{8,104},{12,4},{16,112},{20,12},{24,120},{28,20},{32... | collective-permute-start | bytes 3932168 | tf_op jit(solution)/shard_map/ppermute | solution.py:37
  32.7 19.7 %all-to-all-start = ((f32[32,1,8]{2,1,0:T(1,128)}), f32[32,1,8]{2,1,0:T(1,128)S(1)}, u32[]{:S(2)}, u32[]{:S(2)}) async-start(f32[32,1,8]{2,1,0:T(1,128)} %broadcast_in_dim.12), calls=%async_computation | async-start | bytes 32768 | tf_op jit(solution)/shard_map/all_to_all | solution.py:42
  40.2 12.4 %copy-start.9 = (s32[4]{0:T(128)S(1)}, s32[4]{0:T(128)}, u32[]{:S(2)}) copy-start(s32[4]{0:T(128)} %param.16) | copy-start | bytes 52
  40.3 13.6 %copy-start.7 = (bf16[256,1280]{0,1:T(8,128)(2,1)S(1)}, bf16[256,1280]{0,1:T(8,128)(2,1)}, u32[]{:S(2)}) copy-start(bf16[256,1280]{0,1:T(8,128)(2,1)} %copy.19) | copy-start | bytes 1966084
  43.6 9.2 %collective-permute-start.5 = (f32[2,256]{1,0:T(2,128)S(1)}, f32[2,256]{1,0:T(2,128)S(1)}, u32[]{:S(2)}, u32[]{:S(2)}) collective-permute-start(f32[2,256]{1,0:T(2,128)S(1)} %pad_maximum_fusion.3), channel_id=1, source_target_pairs={{0,1},{1,2},{2,3},{3,0},{4,5},{5,6},{6,7},{7,4},{8,9},{9,10},{10,1... | collective-permute-start | bytes 6152 | tf_op jit(solution)/shard_map/ppermute | solution.py:22
  43.7 10.1 %collective-permute-start.6 = (f32[2,256]{1,0:T(2,128)S(1)}, f32[2,256]{1,0:T(2,128)S(1)}, u32[]{:S(2)}, u32[]{:S(2)}) collective-permute-start(f32[2,256]{1,0:T(2,128)S(1)} %pad_maximum_fusion.3), channel_id=1, source_target_pairs={{0,2},{1,3},{2,0},{3,1},{4,6},{5,7},{6,4},{7,5},{8,10},{9,11},{10,... | collective-permute-start | bytes 6152 | tf_op jit(solution)/shard_map/ppermute | solution.py:22
  46.3 7.5 %collective-permute-start.7 = (f32[2,256]{1,0:T(2,128)S(1)}, f32[2,256]{1,0:T(2,128)S(1)}, u32[]{:S(2)}, u32[]{:S(2)}) collective-permute-start(f32[2,256]{1,0:T(2,128)S(1)} %pad_maximum_fusion.3), channel_id=1, source_target_pairs={{0,3},{1,0},{2,1},{3,2},{4,7},{5,4},{6,5},{7,6},{8,11},{9,8},{10,9... | collective-permute-start | bytes 6152 | tf_op jit(solution)/shard_map/ppermute | solution.py:22
  52.8 18.9 %collective-permute-start.13 = (bf16[512,1280]{1,0:T(8,128)(2,1)S(1)}, bf16[512,1280]{1,0:T(8,128)(2,1)}, u32[]{:S(2)}, u32[]{:S(2)}) collective-permute-start(bf16[512,1280]{1,0:T(8,128)(2,1)S(1)} %pad_maximum_fusion.refs_4_), channel_id=1, source_target_pairs={{0,64},{4,20},{8,72},{12,28},{16,80},{20,4},{24,88},{28,12},{32,96... | collective-permute-start | bytes 3932168 | tf_op jit(solution)/shard_map/ppermute | solution.py:37
  55.5 16.2 %collective-permute-start.10 = (bf16[1280,256]{1,0:T(8,128)(2,1)S(1)}, bf16[1280,256]{1,0:T(8,128)(2,1)S(1)}, u32[]{:S(2)}, u32[]{:S(2)}) collective-permute-start(bf16[1280,256]{1,0:T(8,128)(2,1)S(1)} %fusion.2.refs_0_.grad_ref), channel_id=1, source_target_pairs={{0,1},{1,2},{2,3},{3,0},{4,5},{5,6},{6,7},{7,4},{8,9},{9,10},{10,1... | collective-permute-start | bytes 1966088 | tf_op jit(solution)/shard_map/ppermute | solution.py:22
  55.6 16.2 %collective-permute-start.11 = (bf16[1280,256]{1,0:T(8,128)(2,1)S(1)}, bf16[1280,256]{1,0:T(8,128)(2,1)S(1)}, u32[]{:S(2)}, u32[]{:S(2)}) collective-permute-start(bf16[1280,256]{1,0:T(8,128)(2,1)S(1)} %fusion.2.refs_0_.grad_ref), channel_id=1, source_target_pairs={{0,3},{1,0},{2,1},{3,2},{4,7},{5,4},{6,5},{7,6},{8,11},{9,8},{10,9... | collective-permute-start | bytes 1966088 | tf_op jit(solution)/shard_map/ppermute | solution.py:22
  59.0 6.6 %collective-permute-start.12 = (bf16[640,256]{1,0:T(8,128)(2,1)}, bf16[640,256]{1,0:T(8,128)(2,1)}, u32[]{:S(2)}, u32[]{:S(2)}) collective-permute-start(bf16[640,256]{1,0:T(8,128)(2,1)} %bitcast.14), channel_id=1, source_target_pairs={{0,4},{4,0},{1,5},{5,1},{2,6},{6,2},{3,7},{7,3},{8,12},{12,8},{9,1... | collective-permute-start | bytes 983048 | tf_op jit(solution)/shard_map/ppermute | solution.py:22
  64.5 1.1 copy-start.1
  67.3 36.3 %all-to-all-start.1 = ((bf16[32,16,1280]{2,1,0:T(8,128)(2,1)}), bf16[32,16,1280]{2,1,0:T(8,128)(2,1)}, u32[]{:S(2)}, u32[]{:S(2)}) async-start(bf16[32,16,1280]{2,1,0:T(8,128)(2,1)} %bitcast.37), calls=%async_computation.1 | async-start | bytes 2621440 | tf_op jit(solution)/shard_map/all_to_all | solution.py:58
  71.8 8.0 %copy-start = (bf16[1280,256]{1,0:T(8,128)(2,1)}, bf16[1280,256]{1,0:T(8,128)(2,1)S(1)}, u32[]{:S(2)}) copy-start(bf16[1280,256]{1,0:T(8,128)(2,1)S(1)} %collective-permute-done.10.refs_1_) | copy-start | bytes 1966084
  72.6 13.6 %collective-permute-start.14 = (bf16[640,256]{1,0:T(8,128)(2,1)}, bf16[640,256]{1,0:T(8,128)(2,1)}, u32[]{:S(2)}, u32[]{:S(2)}) collective-permute-start(bf16[640,256]{1,0:T(8,128)(2,1)} %slice.20), channel_id=1, source_target_pairs={{0,1},{1,2},{2,3},{3,0},{4,5},{5,6},{6,7},{7,4},{8,9},{9,10},{10,1... | collective-permute-start | bytes 983048 | tf_op jit(solution)/shard_map/ppermute | solution.py:22
  73.4 12.8 %collective-permute-start.15 = (bf16[640,256]{1,0:T(8,128)(2,1)}, bf16[640,256]{1,0:T(8,128)(2,1)}, u32[]{:S(2)}, u32[]{:S(2)}) collective-permute-start(bf16[640,256]{1,0:T(8,128)(2,1)} %slice.21), channel_id=1, source_target_pairs={{0,3},{1,0},{2,1},{3,2},{4,7},{5,4},{6,5},{7,6},{8,11},{9,8},{10,9... | collective-permute-start | bytes 983048 | tf_op jit(solution)/shard_map/ppermute | solution.py:22
  77.0 10.4 %collective-permute-start.16 = (bf16[1280,256]{1,0:T(8,128)(2,1)}, bf16[1280,256]{1,0:T(8,128)(2,1)}, u32[]{:S(2)}, u32[]{:S(2)}) collective-permute-start(bf16[1280,256]{1,0:T(8,128)(2,1)} %bitcast.25), channel_id=1, source_target_pairs={{0,4},{4,0},{1,5},{5,1},{2,6},{6,2},{3,7},{7,3},{8,12},{12,8},{9,1... | collective-permute-start | bytes 1966088 | tf_op jit(solution)/shard_map/ppermute | solution.py:22
  79.8 1.3 copy-start.2
  87.3 1.7 %collective-permute-start.17 = (bf16[640,256]{1,0:T(8,128)(2,1)S(1)}, bf16[640,256]{1,0:T(8,128)(2,1)S(1)}, u32[]{:S(2)}, u32[]{:S(2)}) collective-permute-start(bf16[640,256]{1,0:T(8,128)(2,1)S(1)} %bitcast.71), channel_id=1, source_target_pairs={{0,4},{4,0},{1,5},{5,1},{2,6},{6,2},{3,7},{7,3},{8,12},{12,8},{9,1... | collective-permute-start | bytes 983048 | tf_op jit(solution)/shard_map/ppermute | solution.py:22
  93.3 0.8 copy-start.5
  94.1 16.5 %collective-permute-start.18 = (bf16[1280,256]{1,0:T(8,128)(2,1)}, bf16[1280,256]{1,0:T(8,128)(2,1)}, u32[]{:S(2)}, u32[]{:S(2)}) collective-permute-start(bf16[1280,256]{1,0:T(8,128)(2,1)} %bitcast.33), channel_id=1, source_target_pairs={{0,32},{4,12},{8,40},{12,20},{16,48},{20,28},{24,56},{28,4},{32,64... | collective-permute-start | bytes 1966088 | tf_op jit(solution)/shard_map/ppermute | solution.py:37
  94.5 18.1 %collective-permute-start.19 = (bf16[1280,256]{1,0:T(8,128)(2,1)}, bf16[1280,256]{1,0:T(8,128)(2,1)}, u32[]{:S(2)}, u32[]{:S(2)}) collective-permute-start(bf16[1280,256]{1,0:T(8,128)(2,1)} %bitcast.34), channel_id=1, source_target_pairs={{0,64},{4,20},{8,72},{12,28},{16,80},{20,4},{24,88},{28,12},{32,96... | collective-permute-start | bytes 1966088 | tf_op jit(solution)/shard_map/ppermute | solution.py:37
  97.1 15.8 %collective-permute-start.20 = (bf16[1280,256]{1,0:T(8,128)(2,1)}, bf16[1280,256]{1,0:T(8,128)(2,1)}, u32[]{:S(2)}, u32[]{:S(2)}) collective-permute-start(bf16[1280,256]{1,0:T(8,128)(2,1)} %bitcast.35), channel_id=1, source_target_pairs={{0,96},{4,28},{8,104},{12,4},{16,112},{20,12},{24,120},{28,20},{32... | collective-permute-start | bytes 1966088 | tf_op jit(solution)/shard_map/ppermute | solution.py:37
  105.8 7.2 %copy-start.4 = (bf16[512,1280]{1,0:T(8,128)(2,1)S(1)}, bf16[512,1280]{1,0:T(8,128)(2,1)}, u32[]{:S(2)}) copy-start(bf16[512,1280]{1,0:T(8,128)(2,1)} %copy-done.3) | copy-start | bytes 3932164
  105.8 7.2 %copy-start.6 = (bf16[8,160,256]{2,1,0:T(8,128)(2,1)S(1)}, bf16[8,160,256]{2,1,0:T(8,128)(2,1)}, u32[]{:S(2)}) copy-start(bf16[8,160,256]{2,1,0:T(8,128)(2,1)} %copy-done.5) | copy-start | bytes 1966084
  105.8 32.8 %all-to-all-start.2 = ((bf16[32,16,1280]{2,1,0:T(8,128)(2,1)}), bf16[32,16,1280]{2,1,0:T(8,128)(2,1)S(1)}, u32[]{:S(2)}, u32[]{:S(2)}) async-start(bf16[32,16,1280]{2,1,0:T(8,128)(2,1)} %bitcast.38), calls=%async_computation.2 | async-start | bytes 2621440 | tf_op jit(solution)/shard_map/all_to_all | solution.py:58
  120.5 12.4 %collective-permute-start.21 = (bf16[160,1280]{1,0:T(8,128)(2,1)S(1)}, bf16[160,1280]{1,0:T(8,128)(2,1)S(1)}, u32[]{:S(2)}, u32[]{:S(2)}) collective-permute-start(bf16[160,1280]{1,0:T(8,128)(2,1)S(1)} %get-tuple-element.80), channel_id=1, source_target_pairs={{0,8},{4,36},{8,16},{12,44},{16,24},{20,52},{24,0},{28,60},{32,40}... | collective-permute-start | bytes 1228808 | tf_op jit(solution)/shard_map/ppermute | solution.py:37
  121.6 15.9 %collective-permute-start.22 = (bf16[160,1280]{1,0:T(8,128)(2,1)S(1)}, bf16[160,1280]{1,0:T(8,128)(2,1)S(1)}, u32[]{:S(2)}, u32[]{:S(2)}) collective-permute-start(bf16[160,1280]{1,0:T(8,128)(2,1)S(1)} %get-tuple-element.81), channel_id=1, source_target_pairs={{0,16},{4,68},{8,24},{12,76},{16,0},{20,84},{24,8},{28,92},{32,48}... | collective-permute-start | bytes 1228808 | tf_op jit(solution)/shard_map/ppermute | solution.py:37
  123.8 13.7 %collective-permute-start.23 = (bf16[160,1280]{1,0:T(8,128)(2,1)S(1)}, bf16[160,1280]{1,0:T(8,128)(2,1)S(1)}, u32[]{:S(2)}, u32[]{:S(2)}) collective-permute-start(bf16[160,1280]{1,0:T(8,128)(2,1)S(1)} %get-tuple-element.82), channel_id=1, source_target_pairs={{0,24},{4,100},{8,0},{12,108},{16,8},{20,116},{24,16},{28,124},{32... | collective-permute-start | bytes 1228808 | tf_op jit(solution)/shard_map/ppermute | solution.py:37

commit v11 on v10

--- a/solution.py
+++ b/solution.py
@@ -55,9 +55,12 @@
 
 def exchange(packed, lanes):
     blocks = packed.reshape((lanes, packed.shape[0] // lanes, packed.shape[1]))
-    got = lax.all_to_all(blocks, DP, split_axis=0, concat_axis=0, tiled=True)
+    return lax.all_to_all(blocks, DP, split_axis=0, concat_axis=0, tiled=True)
+
+
+def learner_rows(got):
     kept = PAIR * BLOCK_ROWS
-    return got[:, :kept].reshape(lanes * kept, packed.shape[1])
+    return got[:, :kept].reshape(got.shape[0] * kept, got.shape[2])
 
 
 FREE = pl.CostEstimate(flops=0, bytes_accessed=0, transcendentals=0)
@@ -128,25 +131,27 @@
     )(slots, grad_t)
 
 
-def top_up(whole, part, half):
-    height, rows = part.shape
-
-    def body(whole_ref, part_ref, out_ref):
-        value = whole_ref[...].astype(F32) + part_ref[...].astype(F32)
-        out_ref[...] = value.astype(BF16)
-
-    spec = pl.BlockSpec((height, rows), lambda i: (half, 0))
+def top_up(near, near_part, back, back_part):
+    height, rows = near_part.shape
+
+    def body(*refs):
+        for i in (0, 1):
+            value = refs[2 * i][...].astype(F32) + refs[2 * i + 1][...].astype(F32)
+            refs[4 + i][...] = value.astype(BF16)
+
+    top = pl.BlockSpec((height, rows), lambda i: (0, 0))
+    bottom = pl.BlockSpec((height, rows), lambda i: (1, 0))
     return pl.pallas_call(
         body,
-        out_shape=jax.ShapeDtypeStruct(whole.shape, BF16),
+        out_shape=[jax.ShapeDtypeStruct(near.shape, BF16)] * 2,
         grid=(1,),
-        in_specs=[spec, pl.BlockSpec((height, rows), lambda i: (0, 0))],
-        out_specs=spec,
-        input_output_aliases={0: 0},
+        in_specs=[top, top, bottom, top],
+        out_specs=[top, bottom],
+        input_output_aliases={0: 0, 2: 1},
         cost_estimate=FREE,
         compiler_params=PARAMS,
         name="top_up",
-    )(whole, part)
+    )(near, near_part, back, back_part)
 
 
 def forward_product(out_proj, context, place, split, dtype=F32):
@@ -190,59 +195,100 @@
     return out if split else out[0]
 
 
-def lay_out(chunks, siblings, x, y, c, z):
+def hidden_part(out_proj, context, residual, cotangent, norm_gain, place):
+    rows, width = context.shape
+    tile = width // 2
+
+    def body(which, proj_ref, context_ref, residual_ref, cotangent_ref, gain_ref, hidden_ref, gained_ref):
+        value = lax.dot_general(
+            proj_ref[...], context_ref[...], (((1,), (1,)), ((), ())), preferred_element_type=F32
+        )
+        hidden_ref[...] = value + residual_ref[...].astype(F32).T
+        gained_ref[...] = (gain_ref[...] * cotangent_ref[...].astype(F32)).T
+
+    columns = pl.BlockSpec((rows, tile), lambda i, which: (0, i))
+    return pl.pallas_call(
+        body,
+        out_shape=[jax.ShapeDtypeStruct((width, rows), F32)] * 2,
+        grid_spec=pltpu.PrefetchScalarGridSpec(
+            num_scalar_prefetch=1,
+            grid=(2,),
+            in_specs=[
+                pl.BlockSpec((tile, width), lambda i, which: (which[0] * 2 + i, 0)),
+                pl.BlockSpec((rows, width), lambda i, which: (0, 0)),
+                columns,
+                columns,
+                pl.BlockSpec((1, tile), lambda i, which: (0, i)),
+            ],
+            out_specs=[pl.BlockSpec((tile, rows), lambda i, which: (i, 0))] * 2,
+        ),
+        cost_estimate=FREE,
+        compiler_params=PARAMS,
+        name="hidden_part",
+    )(place.reshape(1), out_proj, context, residual, cotangent, norm_gain.reshape(1, width))
+
+
+def lay_out(steps, chunks, siblings, x, y, c, z):
     block, rows = chunks[0][0].shape[-2:]
-    flat = [piece for group in (chunks, siblings) for pieces in group for piece in pieces]
-    counts = [[len(pieces) for pieces in group] for group in (chunks, siblings)]
+    arrays, places = [], []
+    for value in [piece for pieces in chunks for piece in pieces] + [pieces[0][0] for pieces in siblings]:
+        known = [i for i, other in enumerate(arrays) if other is value]
+        places.append(known[0] if known else len(arrays))
+        if not known:
+            arrays.append(value)
+    count_of = len(arrays)
 
     def body(where, *refs):
-        ins, outs, sems = refs[: len(flat)], refs[len(flat) : len(flat) + 4], refs[-1]
+        ins, outs, sems = refs[:count_of], refs[count_of : count_of + len(steps)], refs[-1]
         wx, wy, wc, wz = (where[i] for i in range(4))
 
-        def send(src, k, first, slots):
-            pltpu.make_async_copy(src, outs[k].at[pl.ds(first, slots)], sems.at[k]).start()
+        def send(src, number, first, slots):
+            pltpu.make_async_copy(
+                src, outs[number].at[pl.ds(first, slots)], sems.at[number]
+            ).start()
 
         position = 0
-        for owner, group in enumerate(counts):
-            for j, count in enumerate(group):
-                pieces = ins[position : position + count]
-                position += count
-                per_piece = 4 // count
-                if owner == 0:
-                    pieces = [piece.at[:, wc] for piece in pieces]
-                for k in range(4):
+        for owner, group in enumerate((chunks, siblings)):
+            for j, members in enumerate(group):
+                per_piece = 4 // len(members)
+                pieces = []
+                for member in members:
+                    ref = ins[places[position]]
+                    position += 1
+                    pieces.append(ref.at[:, wc] if owner == 0 else ref.at[pl.ds(member[1], 4)])
+                for number, k in enumerate(steps):
                     wanted = lax.rem(wy + k, 4)
 
                     @pl.when((wc == 0) & (lax.rem(j + wz - wx + 4, 4) == k))
-                    def _(pieces=pieces, per_piece=per_piece, k=k, owner=owner):
-                        for number, piece in enumerate(pieces):
-                            send(piece, k, owner * 4 + number * per_piece, per_piece)
-
-                    for number, piece in enumerate(pieces):
-
-                        @pl.when((wc == 1) & (wanted // per_piece == number))
-                        def _(piece=piece, number=number, per_piece=per_piece, k=k, owner=owner,
+                    def _(pieces=pieces, per_piece=per_piece, number=number, owner=owner):
+                        for i, piece in enumerate(pieces):
+                            send(piece, number, owner * 4 + i * per_piece, per_piece)
+
+                    for i, piece in enumerate(pieces):
+
+                        @pl.when((wc == 1) & (wanted // per_piece == i))
+                        def _(piece=piece, i=i, per_piece=per_piece, number=number, owner=owner,
                               j=j, wanted=wanted):
-                            slot = wanted - number * per_piece
-                            send(piece.at[pl.ds(slot, 1)], k, owner * 4 + j, 1)
-
-        for k in range(4):
-            pltpu.make_async_copy(outs[k], outs[k], sems.at[k]).wait()
+                            slot = wanted - i * per_piece
+                            send(piece.at[pl.ds(slot, 1)], number, owner * 4 + j, 1)
+
+        for number in range(len(steps)):
+            pltpu.make_async_copy(outs[number], outs[number], sems.at[number]).wait()
 
     out = pl.pallas_call(
         body,
-        out_shape=[jax.ShapeDtypeStruct((8, block, rows), BF16)] * 4,
+        out_shape=[jax.ShapeDtypeStruct((8, block, rows), BF16)] * len(steps),
         grid_spec=pltpu.PrefetchScalarGridSpec(
             num_scalar_prefetch=1,
             grid=(1,),
-            in_specs=[pl.BlockSpec(memory_space=pl.ANY)] * len(flat),
-            out_specs=[pl.BlockSpec((8, block, rows), lambda i, where: (0, 0, 0))] * 4,
-            scratch_shapes=[pltpu.SemaphoreType.DMA((4,))],
+            in_specs=[pl.BlockSpec(memory_space=pl.ANY)] * count_of,
+            out_specs=[pl.BlockSpec((8, block, rows), lambda i, where: (0, 0, 0))] * len(steps),
+            scratch_shapes=[pltpu.SemaphoreType.DMA((len(steps),))],
         ),
         cost_estimate=FREE,
-        compiler_params=PARAMS,
+        compiler_params=pltpu.CompilerParams(vmem_limit_bytes=16 * 1024 * 1024),
         name="lay_out",
-    )(jnp.stack([x, y, c, z]).astype(jnp.int32), *flat)
+    )(jnp.stack([x, y, c, z]).astype(jnp.int32), *arrays)
     return [value.reshape(8 * block, rows) for value in out]
 
 
@@ -278,7 +324,7 @@
             scratch_shapes=[pltpu.VMEM((height, tile), F32)],
         ),
         cost_estimate=FREE,
-        compiler_params=PARAMS,
+        compiler_params=pltpu.CompilerParams(vmem_limit_bytes=56 * 1024 * 1024),
         name="weight_product",
     )(order, *pieces, *contexts)
 
@@ -298,25 +344,23 @@
     sent_top, sent_bottom = shift(far_top, "z", 1), shift(far_bottom, "z", 3)
     near = forward_product(out_proj, context, (z + 1) % NZ, False, BF16)
     back = forward_product(out_proj, context, (z + 3) % NZ, False, BF16)
-    sent_top, sent_bottom, near, back, pair = lax.optimization_barrier(
-        (sent_top, sent_bottom, near, back, pair)
-    )
-    near, back = top_up(near, sent_top, 0), top_up(back, sent_bottom, 1)
-
-    ready, _, _ = lax.optimization_barrier((context, near, back))
-    own = forward_product(out_proj, ready, z, False)
+    sent_top, sent_bottom, near, back = lax.optimization_barrier(
+        (sent_top, sent_bottom, near, back)
+    )
+    near, back = top_up(near, sent_top, back, sent_bottom)
+
+    groups = rewards.shape[0] * lanes // GROUP
+    member = (group_ids[:, None] == jnp.arange(groups)[None, :]).astype(F32)
+    share, _ = lax.optimization_barrier((jnp.sum(member * rewards[:, None], axis=0), near))
+    ready, _ = lax.optimization_barrier((context, share))
+    own, gained_t = hidden_part(out_proj, ready, residual, cotangent, norm_gain, z)
     late_pair, _ = lax.optimization_barrier((pair, own))
     contexts = [pair] + [cross(late_pair, k, True) for k in (1, 2, 3)]
-    attn_t = own + shift(near, "z", 1).astype(F32) + shift(back, "z", 3).astype(F32)
-
-    hidden_t = residual.T.astype(F32) + attn_t
-    gained_t = norm_gain[:, None] * cotangent.T.astype(F32)
+    hidden_t = own + shift(near, "z", 1).astype(F32) + shift(back, "z", 3).astype(F32)
+
     stats = jnp.stack(
         [jnp.sum(hidden_t * hidden_t, axis=0), jnp.sum(gained_t * hidden_t, axis=0)]
     )
-    groups = rewards.shape[0] * lanes // GROUP
-    member = (group_ids[:, None] == jnp.arange(groups)[None, :]).astype(F32)
-    share, _ = lax.optimization_barrier((jnp.sum(member * rewards[:, None], axis=0), own))
     shares, _ = lax.optimization_barrier((all_shares(share), stats))
     group_total = jnp.sum(shares, axis=0)
     advantage = rewards - jnp.sum(member * group_total[None, :], axis=1) / GROUP
@@ -354,19 +398,18 @@
     far_left, far_right, context_grad = lax.optimization_barrier(
         (far_left, far_right, context_grad)
     )
-    swapped_right, swapped_left = jnp.split(swap(from_right, from_left), 2)
-    swapped_far = swap(far_left, far_right)
+    swapped_near = swap(from_right, from_left).reshape(8, block, rows)
+    swapped_far = swap(far_left, far_right).reshape(4, block, rows)
+    swapped_own = swapped.reshape(4, block, rows)
+
     def parted(*values):
         return [value.reshape(-1, NC, block, rows) for value in values]
 
-    def single(value):
-        return [value.reshape(-1, block, rows)]
-
-    sends = lay_out(
-        [parted(grad_t), parted(from_right), parted(far_left, far_right), parted(from_left)],
-        [single(value) for value in (swapped, swapped_right, swapped_far, swapped_left)],
-        x, y, c, z,
-    )
+    chunks = [parted(grad_t), parted(from_right), parted(far_left, far_right), parted(from_left)]
+    siblings = [
+        [(swapped_own, 0)], [(swapped_near[:4], 0)], [(swapped_far, 0)], [(swapped_near[4:], 0)]
+    ]
+    sends = lay_out((0, 1, 2, 3), chunks, siblings, x, y, c, z)
     far_left, far_right, sends = lax.optimization_barrier((far_left, far_right, sends))
     pieces = [sends[0]] + [cross(sends[k], k, True) for k in (1, 2, 3)]
     far_place = (z + 2) % NZ * 2
@@ -377,9 +420,10 @@
     d_context = exchange(placed, lanes)
     order = [jnp.where(c == 0, (y + k) % NY, (x + k - z) % NZ) for k in range(4)]
     d_out_proj, *parts = weight_product(pieces, contexts, jnp.stack(order), block)
-    for k in (1, 2, 3):
-        d_out_proj = d_out_proj + cross(parts[k - 1], k, False).astype(F32)
-    return (d_context, d_residual, d_out_proj / lanes)
+    parts = [cross(part, k, False) for k, part in zip((1, 2, 3), parts)]
+    for part in parts:
+        d_out_proj = d_out_proj + part.astype(F32)
+    return (learner_rows(d_context), learner_rows(d_residual), d_out_proj / lanes)
 
 
 def solution(mesh):

time: 140 us -> 166 us (1.19)
  starting transfers between devices: 50.6 us -> 69.7 us
  waiting for transfers between devices: 21.2 us -> 27.3 us
  other arithmetic: 9.37 us -> 6.9 us
  Pallas kernels: 41.2 us -> 43.2 us
    all_to_all x2, starting transfers between devices: 9.12 us -> 25.6 us  [exchange(): return lax.all_to_all(blocks, DP, split_axis=0, concat_axis=0, tiled=True)]
    ppermute x9, waiting for transfers between devices: 15.4 us -> 26.7 us  [cross(): return lax.ppermute(value, DP, pairs)]
    all_to_all x1, waiting for transfers between devices: 5.18 us -> 0.01 us  [all_shares(): return lax.all_to_all(copies, DP, split_axis=0, concat_axis=0, tiled=True)]
    ppermute x9, starting transfers between devices: 11.8 us -> 15 us  [cross(): return lax.ppermute(value, DP, pairs)]
    pallas_call x4 -> x3, Pallas kernels: 12.3 us -> 9.4 us  [forward_product(): pl.pallas_call(body, out_shape=[jax.ShapeDtypeStruct((tile, rows), BF16)]...]
    pallas_call x2, Pallas kernels: 2.02 us -> 4.69 us  [the longest x1 2.89 us: hidden_part(): pl.pallas_call(body, out_shape=[jax.ShapeDtypeStruct((width, rows), F32)]...]
    concatenate x0 -> x1, local copies, waits for them, and re-layouts: none -> 1.99 us  [per_device(): pair = jnp.concatenate([context, shift(ready, 'c', 1)], axis=0)]
    ppermute x15, starting transfers between devices: 22.1 us -> 20.4 us  [shift(): lax.ppermute(value, axis, [(i, (i + step) % size) for i in range(size)])]
  transfers between devices with their start and end apart: 27 -> 27, of which waited for: 7 -> 8; matrix products, arithmetic and copies ran while one was open for 15% -> 11% of each run, Pallas kernels for 27% -> 24%
where the time goes in v11:
time: 166 us; the launch traced here: 165 us
  starting transfers between devices  69.7 us (42%)
  Pallas kernels  43.2 us (26%)
  waiting for transfers between devices  27.3 us (16%)
  local copies, waits for them, and re-layouts  17.3 us (10%)
  other arithmetic  6.9 us (4%)
    ppermute x9, waiting for transfers between devices, cross(): return lax.ppermute(value, DP, pairs)  26.7 us
    all_to_all x2, starting transfers between devices, exchange(): return lax.all_to_all(blocks, DP, split_axis=0, concat_axis=0, tiled=True)  25.6 us
    ppermute x15, starting transfers between devices, shift(): lax.ppermute(value, axis, [(i, (i + step) % size) for i in range(size)])  20.4 us
    ppermute x9, starting transfers between devices, cross(): return lax.ppermute(value, DP, pairs)  15 us
    pallas_call x3, Pallas kernels, context_product(): pl.pallas_call(body, out_shape=jax.ShapeDtypeStruct((out_rows, width), dt...  13.4 us
    pallas_call x3, Pallas kernels, forward_product(): pl.pallas_call(body, out_shape=[jax.ShapeDtypeStruct((tile, rows), BF16)]...  9.4 us
    pallas_call x1, Pallas kernels, weight_product(): pl.pallas_call(body, out_shape=[jax.ShapeDtypeStruct((block, width), BF16...  8.92 us
    all_to_all x1, starting transfers between devices, all_shares(): return lax.all_to_all(copies, DP, split_axis=0, concat_axis=0, tiled=True)  8.74 us
  transfers between devices with their start and end apart: 27, of which 8 were waited for; matrix products, arithmetic and copies ran while one was open for 11% of the time, Pallas kernels for 24%

profile of v11, /device:TPU:1, one launch (start us, length us, event | category | flops | bytes accessed | tf_op | source)
XLA Modules:
  0.0 165.5 jit_solution(5368203089050372536)
XLA Ops:
  0.6 2.9 %forward_product.3 = (bf16[640,256]{1,0:T(8,128)(2,1)S(1)}, bf16[640,256]{1,0:T(8,128)(2,1)S(1)}) custom-call(s32[1]{0:T(128)} %bitcast.3.which, bf16[5120,1280]{1,0:T(8,128)(2,1)} %refs_3_.3, bf16[256,1280]{1,0:T(8,128)(2,1)} %context_ref.6), custom_call_target="tpu_custom_call" | custom-call | tf_op jit(solution)/shard_map/forward_product/pallas_call | solution.py:175
  3.6 2.5 %collective-permute-start = (bf16[640,256]{1,0:T(8,128)(2,1)S(1)}, bf16[640,256]{1,0:T(8,128)(2,1)S(1)}, u32[]{:S(2)}, u32[]{:S(2)}) collective-permute-start(bf16[640,256]{1,0:T(8,128)(2,1)S(1)} %get-tuple-element.46), channel_id=1, source_target_pairs={{0,1},{1,2},{2,3},{3,0},{4,5},{5,6},{6,7},{7,4},{8,9},{9,10},{10,1... | collective-permute-start | bytes 983048 | tf_op jit(solution)/shard_map/ppermute | solution.py:22
  6.1 2.2 %collective-permute-start.1 = (bf16[640,256]{1,0:T(8,128)(2,1)S(1)}, bf16[640,256]{1,0:T(8,128)(2,1)S(1)}, u32[]{:S(2)}, u32[]{:S(2)}) collective-permute-start(bf16[640,256]{1,0:T(8,128)(2,1)S(1)} %get-tuple-element.47), channel_id=1, source_target_pairs={{0,3},{1,0},{2,1},{3,2},{4,7},{5,4},{6,5},{7,6},{8,11},{9,8},{10,9... | collective-permute-start | bytes 983048 | tf_op jit(solution)/shard_map/ppermute | solution.py:22
  8.3 1.0 collective-permute-start.7
  9.3 2.9 %forward_product.4.refs_0_ = bf16[1280,256]{1,0:T(8,128)(2,1)S(1)} custom-call(s32[1]{0:T(128)} %bitcast.4.which, bf16[5120,1280]{1,0:T(8,128)(2,1)} %refs_3_.3, bf16[256,1280]{1,0:T(8,128)(2,1)} %context_ref.6), custom_call_target="tpu_custom_call" | custom-call | tf_op jit(solution)/shard_map/forward_product/pallas_call | solution.py:175
  12.2 3.6 %forward_product.5.refs_2_ = bf16[1280,256]{1,0:T(8,128)(2,1)} custom-call(s32[1]{0:T(128)} %bitcast.5.which, bf16[5120,1280]{1,0:T(8,128)(2,1)} %refs_3_.3, bf16[256,1280]{1,0:T(8,128)(2,1)} %context_ref.6), custom_call_target="tpu_custom_call" | custom-call | tf_op jit(solution)/shard_map/forward_product/pallas_call | solution.py:175
  15.8 1.8 %top_up.1 = (bf16[1280,256]{1,0:T(8,128)(2,1)S(1)}, bf16[1280,256]{1,0:T(8,128)(2,1)}) custom-call(bf16[1280,256]{1,0:T(8,128)(2,1)S(1)} %forward_product.4.refs_0_, bf16[640,256]{1,0:T(8,128)(2,1)S(1)} %collective-permute-done.refs_1_, bf16[1280,256]{1,0:T(8,128)(2,1)} %forward_product.5.refs_2_, ...), custom_call_target="tpu_custom_call", output_to_operand_aliasing={{0}: (0, {}), {1}: (2, {})} | custom-call | tf_op jit(solution)/shard_map/top_up/pallas_call | solution.py:144
  17.8 2.5 %collective-permute-start.3 = (bf16[1280,256]{1,0:T(8,128)(2,1)}, bf16[1280,256]{1,0:T(8,128)(2,1)}, u32[]{:S(2)}, u32[]{:S(2)}) collective-permute-start(bf16[1280,256]{1,0:T(8,128)(2,1)} %get-tuple-element.56), channel_id=1, source_target_pairs={{0,3},{1,0},{2,1},{3,2},{4,7},{5,4},{6,5},{7,6},{8,11},{9,8},{10,9... | collective-permute-start | bytes 1966088 | tf_op jit(solution)/shard_map/ppermute | solution.py:22
  20.6 2.0 %constant_dynamic-update-slice_fusion.1 = bf16[512,1280]{1,0:T(8,128)(2,1)} fusion(bf16[256,1280]{1,0:T(8,128)(2,1)} %context_ref.6), kind=kLoop, calls=%fused_computation.18 | loop fusion | bytes 1310720
  23.2 8.7 %all-to-all-start = ((f32[32,1,8]{2,1,0:T(1,128)}), f32[32,1,8]{2,1,0:T(1,128)S(1)}, u32[]{:S(2)}, u32[]{:S(2)}) async-start(f32[32,1,8]{2,1,0:T(1,128)} %broadcast_in_dim.16), calls=%async_computation | async-start | bytes 32768 | tf_op jit(solution)/shard_map/all_to_all | solution.py:42
  31.9 1.1 copy-done.3
  33.0 1.1 copy-done.4
  34.1 2.9 %hidden_part.1 = (f32[1280,256]{1,0:T(8,128)S(1)}, f32[1280,256]{1,0:T(8,128)S(1)}) custom-call(s32[1]{0:T(128)} %bitcast.2.which, bf16[5120,1280]{1,0:T(8,128)(2,1)} %refs_3_.3, bf16[256,1280]{1,0:T(8,128)(2,1)} %context_ref.6, bf16[256,1280]{1,0:T(8,128)(2,1)S(1)} %copy-done.3, bf16[256,1280]{1,0:T(8,128)(2,1)S(1)} %copy-done.4, ...), custom_call_target="tpu_custom_call" | custom-call | tf_op jit(solution)/shard_map/hidden_part/pallas_call | solution.py:210
  37.0 2.0 %constant_dynamic-update-slice_fusion.refs_4_ = bf16[512,1280]{1,0:T(8,128)(2,1)} fusion(bf16[512,1280]{1,0:T(8,128)(2,1)} %constant_dynamic-update-slice_fusion.1, bf16[256,1280]{1,0:T(8,128)(2,1)} %collective-permute-done.7), kind=kLoop, calls=%fused_computation.17 | loop fusion | bytes 1310720 | tf_op jit(solution)/shard_map/concatenate | solution.py:343
  39.0 1.4 collective-permute-start.8
  40.4 1.3 collective-permute-start.9
  41.7 1.7 multiply_reduce_fusion.1
  43.4 2.7 %collective-permute-start.5 = (f32[2,256]{1,0:T(2,128)S(1)}, f32[2,256]{1,0:T(2,128)S(1)}, u32[]{:S(2)}, u32[]{:S(2)}) collective-permute-start(f32[2,256]{1,0:T(2,128)S(1)} %pad_maximum_fusion.2), channel_id=1, source_target_pairs={{0,2},{1,3},{2,0},{3,1},{4,6},{5,7},{6,4},{7,5},{8,10},{9,11},{10,... | collective-permute-start | bytes 6152 | tf_op jit(solution)/shard_map/ppermute | solution.py:22
  47.5 1.7 %collective-permute-start.13 = (bf16[512,1280]{1,0:T(8,128)(2,1)}, bf16[512,1280]{1,0:T(8,128)(2,1)}, u32[]{:S(2)}, u32[]{:S(2)}) collective-permute-start(bf16[512,1280]{1,0:T(8,128)(2,1)} %constant_dynamic-update-slice_fusion.refs_4_), channel_id=1, source_target_pairs={{0,64},{4,20},{8,72},{12,28},{16,80},{20,4},{24,88},{28,12},{32,96... | collective-permute-start | bytes 3932168 | tf_op jit(solution)/shard_map/ppermute | solution.py:37
  49.2 1.6 subtract_convert_fusion.refs_0_.grad_ref
  50.8 6.5 %collective-permute-done.8.refs_5_ = bf16[512,1280]{1,0:T(8,128)(2,1)} collective-permute-done((bf16[512,1280]{1,0:T(8,128)(2,1)}, bf16[512,1280]{1,0:T(8,128)(2,1)}, u32[]{:S(2)}, u32[]{:S(2)}) %collective-permute-start.8) | collective-permute-done | bytes 1310752 | tf_op jit(solution)/shard_map/ppermute | solution.py:37
  57.5 2.7 %collective-permute-start.11 = (bf16[1280,256]{1,0:T(8,128)(2,1)S(1)}, bf16[1280,256]{1,0:T(8,128)(2,1)S(1)}, u32[]{:S(2)}, u32[]{:S(2)}) collective-permute-start(bf16[1280,256]{1,0:T(8,128)(2,1)S(1)} %subtract_convert_fusion.refs_0_.grad_ref), channel_id=1, source_target_pairs={{0,3},{1,0},{2,1},{3,2},{4,7},{5,4},{6,5},{7,6},{8,11},{9,8},{10,9... | collective-permute-start | bytes 1966088 | tf_op jit(solution)/shard_map/ppermute | solution.py:22
  60.2 2.1 %collective-permute-start.12 = (bf16[640,256]{1,0:T(8,128)(2,1)S(1)}, bf16[640,256]{1,0:T(8,128)(2,1)S(1)}, u32[]{:S(2)}, u32[]{:S(2)}) collective-permute-start(bf16[640,256]{1,0:T(8,128)(2,1)S(1)} %bitcast.61), channel_id=1, source_target_pairs={{0,4},{4,0},{1,5},{5,1},{2,6},{6,2},{3,7},{7,3},{8,12},{12,8},{9,1... | collective-permute-start | bytes 983048 | tf_op jit(solution)/shard_map/ppermute | solution.py:22
  62.6 3.0 %context_product.3.refs_4_ = f32[256,1280]{1,0:T(8,128)S(1)} custom-call(s32[1]{0:T(128)} %bitcast.2.which, bf16[1280,256]{1,0:T(8,128)(2,1)S(1)} %subtract_convert_fusion.refs_0_.grad_ref, bf16[5120,1280]{1,0:T(8,128)(2,1)} %refs_3_.3), custom_call_target="tpu_custom_call" | custom-call | tf_op jit(solution)/shard_map/context_product/pallas_call | solution.py:104
  65.5 1.1 copy-done
  66.7 1.6 place_rows.1
  68.3 21.0 %all-to-all-start.1 = ((bf16[32,16,1280]{2,1,0:T(8,128)(2,1)}), bf16[32,16,1280]{2,1,0:T(8,128)(2,1)}, u32[]{:S(2)}, u32[]{:S(2)}) async-start(bf16[32,16,1280]{2,1,0:T(8,128)(2,1)} %bitcast.35), calls=%async_computation.1 | async-start | bytes 2621440 | tf_op jit(solution)/shard_map/all_to_all | solution.py:58
  90.9 2.7 %collective-permute-start.15 = (bf16[640,256]{1,0:T(8,128)(2,1)}, bf16[640,256]{1,0:T(8,128)(2,1)}, u32[]{:S(2)}, u32[]{:S(2)}) collective-permute-start(bf16[640,256]{1,0:T(8,128)(2,1)} %slice.33), channel_id=1, source_target_pairs={{0,3},{1,0},{2,1},{3,2},{4,7},{5,4},{6,5},{7,6},{8,11},{9,8},{10,9... | collective-permute-start | bytes 983048 | tf_op jit(solution)/shard_map/ppermute | solution.py:22
  95.4 1.3 copy-done.1
  96.7 5.1 %context_product.4.refs_4_ = f32[256,1280]{1,0:T(8,128)S(1)} custom-call(s32[2]{0:T(128)S(1)} %pad_add_fusion.1.which, bf16[1280,256]{1,0:T(8,128)(2,1)S(1)} %collective-permute-done.11.refs_0_, bf16[1280,256]{1,0:T(8,128)(2,1)S(1)} %collective-permute-done.10.refs_1_, bf16[5120,1280]{1,0:T(8,128)(2,1)} %refs_3_.3, bf16[5120,1280]{1,0:T(8,128)(2,1)} %refs_3_.3, ...), custom_call_target="tpu_custom_call" | custom-call | tf_op jit(solution)/shard_map/context_product/pallas_call | solution.py:104
  101.9 1.1 dynamic-slice_bitcast_fusion.2
  103.1 1.1 fusion.8
  104.7 5.2 %lay_out.1 = (bf16[8,160,256]{2,1,0:T(8,128)(2,1)S(1)}, bf16[8,160,256]{2,1,0:T(8,128)(2,1)}, bf16[8,160,256]{2,1,0:T(8,128)(2,1)}, bf16[8,160,256]{2,1,0:T(8,128)(2,1)}) custom-call(s32[4]{0:T(128)S(1)} %pad_add_fusion.2.where, bf16[4,2,160,256]{3,2,1,0:T(8,128)(2,1)S(1)} %bitcast.49, bf16[4,2,160,256]{3,2,1,0:T(8,128)(2,1)S(1)} %bitcast.53, ...), custom_call_target="tpu_custom_call" | custom-call | tf_op jit(solution)/shard_map/lay_out/pallas_call | solution.py:278
  110.8 1.4 collective-permute-start.18
  112.2 2.4 %collective-permute-start.19 = (bf16[1280,256]{1,0:T(8,128)(2,1)}, bf16[1280,256]{1,0:T(8,128)(2,1)}, u32[]{:S(2)}, u32[]{:S(2)}) collective-permute-start(bf16[1280,256]{1,0:T(8,128)(2,1)} %bitcast.32), channel_id=1, source_target_pairs={{0,64},{4,20},{8,72},{12,28},{16,80},{20,4},{24,88},{28,12},{32,96... | collective-permute-start | bytes 1966088 | tf_op jit(solution)/shard_map/ppermute | solution.py:37
  114.6 1.2 collective-permute-start.20
  115.9 5.3 %context_product.5 = bf16[512,1280]{1,0:T(8,128)(2,1)} custom-call(s32[2]{0:T(128)S(1)} %pad_add_fusion.which, bf16[640,256]{1,0:T(8,128)(2,1)} %collective-permute-done.14.refs_0_, bf16[640,256]{1,0:T(8,128)(2,1)} %collective-permute-done.15.refs_1_, bf16[5120,1280]{1,0:T(8,128)(2,1)} %refs_3_.3, bf16[5120,1280]{1,0:T(8,128)(2,1)} %refs_3_.3, ...), custom_call_target="tpu_custom_call" | custom-call | tf_op jit(solution)/shard_map/context_product/pallas_call | solution.py:104
  121.2 4.5 %all-to-all-start.2 = ((bf16[32,16,1280]{2,1,0:T(8,128)(2,1)}), bf16[32,16,1280]{2,1,0:T(8,128)(2,1)S(1)}, u32[]{:S(2)}, u32[]{:S(2)}) async-start(bf16[32,16,1280]{2,1,0:T(8,128)(2,1)} %bitcast.36), calls=%async_computation.2 | async-start | bytes 2621440 | tf_op jit(solution)/shard_map/all_to_all | solution.py:58
  126.5 3.5 %collective-permute-done.19.refs_2_ = bf16[1280,256]{1,0:T(8,128)(2,1)} collective-permute-done((bf16[1280,256]{1,0:T(8,128)(2,1)}, bf16[1280,256]{1,0:T(8,128)(2,1)}, u32[]{:S(2)}, u32[]{:S(2)}) %collective-permute-start.19) | collective-permute-done | bytes 655392 | tf_op jit(solution)/shard_map/ppermute | solution.py:37
  130.0 10.1 %collective-permute-done.20.refs_3_ = bf16[1280,256]{1,0:T(8,128)(2,1)} collective-permute-done((bf16[1280,256]{1,0:T(8,128)(2,1)}, bf16[1280,256]{1,0:T(8,128)(2,1)}, u32[]{:S(2)}, u32[]{:S(2)}) %collective-permute-start.20) | collective-permute-done | bytes 655392 | tf_op jit(solution)/shard_map/ppermute | solution.py:37
  140.0 8.9 %weight_product.1 = (f32[160,1280]{1,0:T(8,128)}, bf16[160,1280]{1,0:T(8,128)(2,1)}, bf16[160,1280]{1,0:T(8,128)(2,1)}, bf16[160,1280]{1,0:T(8,128)(2,1)}) custom-call(s32[4]{0:T(128)} %pad_add_fusion.3.order_ref, bf16[1280,256]{1,0:T(8,128)(2,1)} %bitcast.56, bf16[1280,256]{1,0:T(8,128)(2,1)} %copy-done.8, ...), custom_call_target="tpu_custom_call" | custom-call | tf_op jit(solution)/shard_map/weight_product/pallas_call | solution.py:315
  149.0 1.5 collective-permute-start.21
  150.5 2.9 %collective-permute-start.22 = (bf16[160,1280]{1,0:T(8,128)(2,1)}, bf16[160,1280]{1,0:T(8,128)(2,1)S(1)}, u32[]{:S(2)}, u32[]{:S(2)}) collective-permute-start(bf16[160,1280]{1,0:T(8,128)(2,1)} %get-tuple-element.87), channel_id=1, source_target_pairs={{0,16},{4,68},{8,24},{12,76},{16,0},{20,84},{24,8},{28,92},{32,48}... | collective-permute-start | bytes 1228808 | tf_op jit(solution)/shard_map/ppermute | solution.py:37
  153.4 1.2 collective-permute-start.23
  154.6 2.2 %reshape.173 = bf16[384,1280]{1,0:T(8,128)(2,1)} reshape(bf16[32,12,1280]{2,1,0:T(8,128)(2,1)} %bitcast.47) | data formatting | bytes 1966080 | tf_op jit(solution)/shard_map/reshape | solution.py:63
  157.8 5.6 %collective-permute-done.22 = bf16[160,1280]{1,0:T(8,128)(2,1)S(1)} collective-permute-done((bf16[160,1280]{1,0:T(8,128)(2,1)}, bf16[160,1280]{1,0:T(8,128)(2,1)S(1)}, u32[]{:S(2)}, u32[]{:S(2)}) %collective-permute-start.22) | collective-permute-done | bytes 409632 | tf_op jit(solution)/shard_map/ppermute | solution.py:37
  163.3 1.1 add_multiply_fusion
  164.4 1.1 reshape.172
  (81 shorter events, 9.6 us)
Async XLA Ops:
  3.6 12.2 %collective-permute-start = (bf16[640,256]{1,0:T(8,128)(2,1)S(1)}, bf16[640,256]{1,0:T(8,128)(2,1)S(1)}, u32[]{:S(2)}, u32[]{:S(2)}) collective-permute-start(bf16[640,256]{1,0:T(8,128)(2,1)S(1)} %get-tuple-element.46), channel_id=1, source_target_pairs={{0,1},{1,2},{2,3},{3,0},{4,5},{5,6},{6,7},{7,4},{8,9},{9,10},{10,1... | collective-permute-start | bytes 983048 | tf_op jit(solution)/shard_map/ppermute | solution.py:22
  6.1 9.7 %collective-permute-start.1 = (bf16[640,256]{1,0:T(8,128)(2,1)S(1)}, bf16[640,256]{1,0:T(8,128)(2,1)S(1)}, u32[]{:S(2)}, u32[]{:S(2)}) collective-permute-start(bf16[640,256]{1,0:T(8,128)(2,1)S(1)} %get-tuple-element.47), channel_id=1, source_target_pairs={{0,3},{1,0},{2,1},{3,2},{4,7},{5,4},{6,5},{7,6},{8,11},{9,8},{10,9... | collective-permute-start | bytes 983048 | tf_op jit(solution)/shard_map/ppermute | solution.py:22
  8.3 28.7 %collective-permute-start.7 = (bf16[256,1280]{1,0:T(8,128)(2,1)}, bf16[256,1280]{1,0:T(8,128)(2,1)}, u32[]{:S(2)}, u32[]{:S(2)}) collective-permute-start(bf16[256,1280]{1,0:T(8,128)(2,1)} %context_ref.6), channel_id=1, source_target_pairs={{0,4},{4,0},{1,5},{5,1},{2,6},{6,2},{3,7},{7,3},{8,12},{12,8},{9,1... | collective-permute-start | bytes 1966088 | tf_op jit(solution)/shard_map/ppermute | solution.py:22
  15.8 4.5 %copy-start.13 = (s32[64,1]{0,1:T(1,128)S(1)}, s32[64,1]{0,1:T(1,128)}, u32[]{:S(2)}) copy-start(s32[64,1]{0,1:T(1,128)} %param.17) | copy-start | bytes 772
  15.8 4.7 %copy-start.9 = (f32[1280]{0:T(1024)S(1)}, f32[1280]{0:T(1024)}, u32[]{:S(2)}) copy-start(f32[1280]{0:T(1024)} %param.13) | copy-start | bytes 15364
  15.8 4.7 %copy-start.11 = (f32[4]{0:T(128)S(1)}, f32[4]{0:T(128)}, u32[]{:S(2)}) copy-start(f32[4]{0:T(128)} %param.14) | copy-start | bytes 52
  15.8 4.7 %copy-start.12 = (s32[4]{0:T(128)S(1)}, s32[4]{0:T(128)}, u32[]{:S(2)}) copy-start(s32[4]{0:T(128)} %param.15) | copy-start | bytes 52
  17.6 24.1 %collective-permute-start.2 = (bf16[1280,256]{1,0:T(8,128)(2,1)S(1)}, bf16[1280,256]{1,0:T(8,128)(2,1)}, u32[]{:S(2)}, u32[]{:S(2)}) collective-permute-start(bf16[1280,256]{1,0:T(8,128)(2,1)S(1)} %get-tuple-element.52), channel_id=1, source_target_pairs={{0,1},{1,2},{2,3},{3,0},{4,5},{5,6},{6,7},{7,4},{8,9},{9,10},{10,1... | collective-permute-start | bytes 1966088 | tf_op jit(solution)/shard_map/ppermute | solution.py:22
  17.8 23.9 %collective-permute-start.3 = (bf16[1280,256]{1,0:T(8,128)(2,1)}, bf16[1280,256]{1,0:T(8,128)(2,1)}, u32[]{:S(2)}, u32[]{:S(2)}) collective-permute-start(bf16[1280,256]{1,0:T(8,128)(2,1)} %get-tuple-element.56), channel_id=1, source_target_pairs={{0,3},{1,0},{2,1},{3,2},{4,7},{5,4},{6,5},{7,6},{8,11},{9,8},{10,9... | collective-permute-start | bytes 1966088 | tf_op jit(solution)/shard_map/ppermute | solution.py:22
  23.2 23.8 %all-to-all-start = ((f32[32,1,8]{2,1,0:T(1,128)}), f32[32,1,8]{2,1,0:T(1,128)S(1)}, u32[]{:S(2)}, u32[]{:S(2)}) async-start(f32[32,1,8]{2,1,0:T(1,128)} %broadcast_in_dim.16), calls=%async_computation | async-start | bytes 32768 | tf_op jit(solution)/shard_map/all_to_all | solution.py:42
  31.9 1.1 copy-start.3
  33.0 1.1 copy-start.4
  39.0 18.3 %collective-permute-start.8 = (bf16[512,1280]{1,0:T(8,128)(2,1)}, bf16[512,1280]{1,0:T(8,128)(2,1)}, u32[]{:S(2)}, u32[]{:S(2)}) collective-permute-start(bf16[512,1280]{1,0:T(8,128)(2,1)} %constant_dynamic-update-slice_fusion.refs_4_), channel_id=1, source_target_pairs={{0,32},{4,12},{8,40},{12,20},{16,48},{20,28},{24,56},{28,4},{32,64... | collective-permute-start | bytes 3932168 | tf_op jit(solution)/shard_map/ppermute | solution.py:37
  40.4 17.1 %collective-permute-start.9 = (bf16[512,1280]{1,0:T(8,128)(2,1)}, bf16[512,1280]{1,0:T(8,128)(2,1)}, u32[]{:S(2)}, u32[]{:S(2)}) collective-permute-start(bf16[512,1280]{1,0:T(8,128)(2,1)} %constant_dynamic-update-slice_fusion.refs_4_), channel_id=1, source_target_pairs={{0,96},{4,28},{8,104},{12,4},{16,112},{20,12},{24,120},{28,20},{32... | collective-permute-start | bytes 3932168 | tf_op jit(solution)/shard_map/ppermute | solution.py:37
  41.7 5.5 %copy-start.10 = (s32[4]{0:T(128)S(1)}, s32[4]{0:T(128)}, u32[]{:S(2)}) copy-start(s32[4]{0:T(128)} %param.16) | copy-start | bytes 52
  43.3 4.1 %collective-permute-start.4 = (f32[2,256]{1,0:T(2,128)S(1)}, f32[2,256]{1,0:T(2,128)S(1)}, u32[]{:S(2)}, u32[]{:S(2)}) collective-permute-start(f32[2,256]{1,0:T(2,128)S(1)} %pad_maximum_fusion.2), channel_id=1, source_target_pairs={{0,1},{1,2},{2,3},{3,0},{4,5},{5,6},{6,7},{7,4},{8,9},{9,10},{10,1... | collective-permute-start | bytes 6152 | tf_op jit(solution)/shard_map/ppermute | solution.py:22
  43.4 5.7 %collective-permute-start.5 = (f32[2,256]{1,0:T(2,128)S(1)}, f32[2,256]{1,0:T(2,128)S(1)}, u32[]{:S(2)}, u32[]{:S(2)}) collective-permute-start(f32[2,256]{1,0:T(2,128)S(1)} %pad_maximum_fusion.2), channel_id=1, source_target_pairs={{0,2},{1,3},{2,0},{3,1},{4,6},{5,7},{6,4},{7,5},{8,10},{9,11},{10,... | collective-permute-start | bytes 6152 | tf_op jit(solution)/shard_map/ppermute | solution.py:22
  46.1 3.0 %collective-permute-start.6 = (f32[2,256]{1,0:T(2,128)S(1)}, f32[2,256]{1,0:T(2,128)S(1)}, u32[]{:S(2)}, u32[]{:S(2)}) collective-permute-start(f32[2,256]{1,0:T(2,128)S(1)} %pad_maximum_fusion.2), channel_id=1, source_target_pairs={{0,3},{1,0},{2,1},{3,2},{4,7},{5,4},{6,5},{7,6},{8,11},{9,8},{10,9... | collective-permute-start | bytes 6152 | tf_op jit(solution)/shard_map/ppermute | solution.py:22
  47.5 41.9 %collective-permute-start.13 = (bf16[512,1280]{1,0:T(8,128)(2,1)}, bf16[512,1280]{1,0:T(8,128)(2,1)}, u32[]{:S(2)}, u32[]{:S(2)}) collective-permute-start(bf16[512,1280]{1,0:T(8,128)(2,1)} %constant_dynamic-update-slice_fusion.refs_4_), channel_id=1, source_target_pairs={{0,64},{4,20},{8,72},{12,28},{16,80},{20,4},{24,88},{28,12},{32,96... | collective-permute-start | bytes 3932168 | tf_op jit(solution)/shard_map/ppermute | solution.py:37
  57.5 31.9 %collective-permute-start.10 = (bf16[1280,256]{1,0:T(8,128)(2,1)S(1)}, bf16[1280,256]{1,0:T(8,128)(2,1)S(1)}, u32[]{:S(2)}, u32[]{:S(2)}) collective-permute-start(bf16[1280,256]{1,0:T(8,128)(2,1)S(1)} %subtract_convert_fusion.refs_0_.grad_ref), channel_id=1, source_target_pairs={{0,1},{1,2},{2,3},{3,0},{4,5},{5,6},{6,7},{7,4},{8,9},{9,10},{10,1... | collective-permute-start | bytes 1966088 | tf_op jit(solution)/shard_map/ppermute | solution.py:22
  57.5 31.9 %collective-permute-start.11 = (bf16[1280,256]{1,0:T(8,128)(2,1)S(1)}, bf16[1280,256]{1,0:T(8,128)(2,1)S(1)}, u32[]{:S(2)}, u32[]{:S(2)}) collective-permute-start(bf16[1280,256]{1,0:T(8,128)(2,1)S(1)} %subtract_convert_fusion.refs_0_.grad_ref), channel_id=1, source_target_pairs={{0,3},{1,0},{2,1},{3,2},{4,7},{5,4},{6,5},{7,6},{8,11},{9,8},{10,9... | collective-permute-start | bytes 1966088 | tf_op jit(solution)/shard_map/ppermute | solution.py:22
  60.2 6.5 %collective-permute-start.12 = (bf16[640,256]{1,0:T(8,128)(2,1)S(1)}, bf16[640,256]{1,0:T(8,128)(2,1)S(1)}, u32[]{:S(2)}, u32[]{:S(2)}) collective-permute-start(bf16[640,256]{1,0:T(8,128)(2,1)S(1)} %bitcast.61), channel_id=1, source_target_pairs={{0,4},{4,0},{1,5},{5,1},{2,6},{6,2},{3,7},{7,3},{8,12},{12,8},{9,1... | collective-permute-start | bytes 983048 | tf_op jit(solution)/shard_map/ppermute | solution.py:22
  65.5 1.2 copy-start
  66.7 1.6 copy-start.5
  68.3 52.9 %all-to-all-start.1 = ((bf16[32,16,1280]{2,1,0:T(8,128)(2,1)}), bf16[32,16,1280]{2,1,0:T(8,128)(2,1)}, u32[]{:S(2)}, u32[]{:S(2)}) async-start(bf16[32,16,1280]{2,1,0:T(8,128)(2,1)} %bitcast.35), calls=%async_computation.1 | async-start | bytes 2621440 | tf_op jit(solution)/shard_map/all_to_all | solution.py:58
  90.1 11.7 %collective-permute-start.14 = (bf16[640,256]{1,0:T(8,128)(2,1)}, bf16[640,256]{1,0:T(8,128)(2,1)}, u32[]{:S(2)}, u32[]{:S(2)}) collective-permute-start(bf16[640,256]{1,0:T(8,128)(2,1)} %slice.32), channel_id=1, source_target_pairs={{0,1},{1,2},{2,3},{3,0},{4,5},{5,6},{6,7},{7,4},{8,9},{9,10},{10,1... | collective-permute-start | bytes 983048 | tf_op jit(solution)/shard_map/ppermute | solution.py:22
  90.9 11.0 %collective-permute-start.15 = (bf16[640,256]{1,0:T(8,128)(2,1)}, bf16[640,256]{1,0:T(8,128)(2,1)}, u32[]{:S(2)}, u32[]{:S(2)}) collective-permute-start(bf16[640,256]{1,0:T(8,128)(2,1)} %slice.33), channel_id=1, source_target_pairs={{0,3},{1,0},{2,1},{3,2},{4,7},{5,4},{6,5},{7,6},{8,11},{9,8},{10,9... | collective-permute-start | bytes 983048 | tf_op jit(solution)/shard_map/ppermute | solution.py:22
  94.5 8.7 %collective-permute-start.16 = (bf16[1280,256]{1,0:T(8,128)(2,1)}, bf16[1280,256]{1,0:T(8,128)(2,1)}, u32[]{:S(2)}, u32[]{:S(2)}) collective-permute-start(bf16[1280,256]{1,0:T(8,128)(2,1)} %bitcast.23), channel_id=1, source_target_pairs={{0,4},{4,0},{1,5},{5,1},{2,6},{6,2},{3,7},{7,3},{8,12},{12,8},{9,1... | collective-permute-start | bytes 1966088 | tf_op jit(solution)/shard_map/ppermute | solution.py:22
  95.4 1.3 copy-start.1
  101.8 2.8 %copy-start.6 = (bf16[640,256]{1,0:T(8,128)(2,1)S(1)}, bf16[640,256]{1,0:T(8,128)(2,1)}, u32[]{:S(2)}) copy-start(bf16[640,256]{1,0:T(8,128)(2,1)} %copy-done.5) | copy-start | bytes 983044
  103.0 1.7 %collective-permute-start.17 = (bf16[640,256]{1,0:T(8,128)(2,1)S(1)}, bf16[640,256]{1,0:T(8,128)(2,1)S(1)}, u32[]{:S(2)}, u32[]{:S(2)}) collective-permute-start(bf16[640,256]{1,0:T(8,128)(2,1)S(1)} %bitcast.60), channel_id=1, source_target_pairs={{0,4},{4,0},{1,5},{5,1},{2,6},{6,2},{3,7},{7,3},{8,12},{12,8},{9,1... | collective-permute-start | bytes 983048 | tf_op jit(solution)/shard_map/ppermute | solution.py:22
  109.9 0.9 copy-start.2
  110.8 15.8 %collective-permute-start.18 = (bf16[1280,256]{1,0:T(8,128)(2,1)}, bf16[1280,256]{1,0:T(8,128)(2,1)S(1)}, u32[]{:S(2)}, u32[]{:S(2)}) collective-permute-start(bf16[1280,256]{1,0:T(8,128)(2,1)} %bitcast.31), channel_id=1, source_target_pairs={{0,32},{4,12},{8,40},{12,20},{16,48},{20,28},{24,56},{28,4},{32,64... | collective-permute-start | bytes 1966088 | tf_op jit(solution)/shard_map/ppermute | solution.py:37
  112.2 17.8 %collective-permute-start.19 = (bf16[1280,256]{1,0:T(8,128)(2,1)}, bf16[1280,256]{1,0:T(8,128)(2,1)}, u32[]{:S(2)}, u32[]{:S(2)}) collective-permute-start(bf16[1280,256]{1,0:T(8,128)(2,1)} %bitcast.32), channel_id=1, source_target_pairs={{0,64},{4,20},{8,72},{12,28},{16,80},{20,4},{24,88},{28,12},{32,96... | collective-permute-start | bytes 1966088 | tf_op jit(solution)/shard_map/ppermute | solution.py:37
  114.6 25.4 %collective-permute-start.20 = (bf16[1280,256]{1,0:T(8,128)(2,1)}, bf16[1280,256]{1,0:T(8,128)(2,1)}, u32[]{:S(2)}, u32[]{:S(2)}) collective-permute-start(bf16[1280,256]{1,0:T(8,128)(2,1)} %bitcast.33), channel_id=1, source_target_pairs={{0,96},{4,28},{8,104},{12,4},{16,112},{20,12},{24,120},{28,20},{32... | collective-permute-start | bytes 1966088 | tf_op jit(solution)/shard_map/ppermute | solution.py:37
  121.2 43.2 %all-to-all-start.2 = ((bf16[32,16,1280]{2,1,0:T(8,128)(2,1)}), bf16[32,16,1280]{2,1,0:T(8,128)(2,1)S(1)}, u32[]{:S(2)}, u32[]{:S(2)}) async-start(bf16[32,16,1280]{2,1,0:T(8,128)(2,1)} %bitcast.36), calls=%async_computation.2 | async-start | bytes 2621440 | tf_op jit(solution)/shard_map/all_to_all | solution.py:58
  126.5 13.5 %copy-start.8 = (bf16[1280,256]{1,0:T(8,128)(2,1)}, bf16[1280,256]{1,0:T(8,128)(2,1)S(1)}, u32[]{:S(2)}) copy-start(bf16[1280,256]{1,0:T(8,128)(2,1)S(1)} %collective-permute-done.18.refs_1_) | copy-start | bytes 1966084
  149.0 14.4 %copy-start.7 = (f32[160,1280]{1,0:T(8,128)S(1)}, f32[160,1280]{1,0:T(8,128)}, u32[]{:S(2)}) copy-start(f32[160,1280]{1,0:T(8,128)} %get-tuple-element.85) | copy-start | bytes 2457604
  149.0 8.8 %collective-permute-start.21 = (bf16[160,1280]{1,0:T(8,128)(2,1)}, bf16[160,1280]{1,0:T(8,128)(2,1)S(1)}, u32[]{:S(2)}, u32[]{:S(2)}) collective-permute-start(bf16[160,1280]{1,0:T(8,128)(2,1)} %get-tuple-element.86), channel_id=1, source_target_pairs={{0,8},{4,36},{8,16},{12,44},{16,24},{20,52},{24,0},{28,60},{32,40}... | collective-permute-start | bytes 1228808 | tf_op jit(solution)/shard_map/ppermute | solution.py:37
  150.5 12.8 %collective-permute-start.22 = (bf16[160,1280]{1,0:T(8,128)(2,1)}, bf16[160,1280]{1,0:T(8,128)(2,1)S(1)}, u32[]{:S(2)}, u32[]{:S(2)}) collective-permute-start(bf16[160,1280]{1,0:T(8,128)(2,1)} %get-tuple-element.87), channel_id=1, source_target_pairs={{0,16},{4,68},{8,24},{12,76},{16,0},{20,84},{24,8},{28,92},{32,48}... | collective-permute-start | bytes 1228808 | tf_op jit(solution)/shard_map/ppermute | solution.py:37
  153.4 9.9 %collective-permute-start.23 = (bf16[160,1280]{1,0:T(8,128)(2,1)}, bf16[160,1280]{1,0:T(8,128)(2,1)S(1)}, u32[]{:S(2)}, u32[]{:S(2)}) collective-permute-start(bf16[160,1280]{1,0:T(8,128)(2,1)} %get-tuple-element.88), channel_id=1, source_target_pairs={{0,24},{4,100},{8,0},{12,108},{16,8},{20,116},{24,16},{28,124},{32... | collective-permute-start | bytes 1228808 | tf_op jit(solution)/shard_map/ppermute | solution.py:37

commit v12 on v11

--- a/solution.py
+++ b/solution.py
@@ -344,23 +344,23 @@
     sent_top, sent_bottom = shift(far_top, "z", 1), shift(far_bottom, "z", 3)
     near = forward_product(out_proj, context, (z + 1) % NZ, False, BF16)
     back = forward_product(out_proj, context, (z + 3) % NZ, False, BF16)
-    sent_top, sent_bottom, near, back = lax.optimization_barrier(
-        (sent_top, sent_bottom, near, back)
+    sent_top, sent_bottom, near, back, pair = lax.optimization_barrier(
+        (sent_top, sent_bottom, near, back, pair)
     )
     near, back = top_up(near, sent_top, back, sent_bottom)
 
+    ready, _, _ = lax.optimization_barrier((context, near, back))
+    own, gained_t = hidden_part(out_proj, ready, residual, cotangent, norm_gain, z)
+    late_pair, _ = lax.optimization_barrier((pair, near))
+    contexts = [pair] + [cross(late_pair, k, True) for k in (1, 2, 3)]
+    hidden_t = own + shift(near, "z", 1).astype(F32) + shift(back, "z", 3).astype(F32)
+
+    stats = jnp.stack(
+        [jnp.sum(hidden_t * hidden_t, axis=0), jnp.sum(gained_t * hidden_t, axis=0)]
+    )
     groups = rewards.shape[0] * lanes // GROUP
     member = (group_ids[:, None] == jnp.arange(groups)[None, :]).astype(F32)
-    share, _ = lax.optimization_barrier((jnp.sum(member * rewards[:, None], axis=0), near))
-    ready, _ = lax.optimization_barrier((context, share))
-    own, gained_t = hidden_part(out_proj, ready, residual, cotangent, norm_gain, z)
-    late_pair, _ = lax.optimization_barrier((pair, own))
-    contexts = [pair] + [cross(late_pair, k, True) for k in (1, 2, 3)]
-    hidden_t = own + shift(near, "z", 1).astype(F32) + shift(back, "z", 3).astype(F32)
-
-    stats = jnp.stack(
-        [jnp.sum(hidden_t * hidden_t, axis=0), jnp.sum(gained_t * hidden_t, axis=0)]
-    )
+    share, _ = lax.optimization_barrier((jnp.sum(member * rewards[:, None], axis=0), own))
     shares, _ = lax.optimization_barrier((all_shares(share), stats))
     group_total = jnp.sum(shares, axis=0)
     advantage = rewards - jnp.sum(member * group_total[None, :], axis=1) / GROUP

time: 166 us -> 143 us (0.86)
  starting transfers between devices: 69.7 us -> 53.1 us
  local copies, waits for them, and re-layouts: 17.3 us -> 11.2 us
  waiting for transfers between devices: 27.3 us -> 24 us
  other arithmetic: 6.9 us -> 9.15 us
    all_to_all x2, starting transfers between devices: 25.6 us -> 11 us  [exchange(): return lax.all_to_all(blocks, DP, split_axis=0, concat_axis=0, tiled=True)]
    ppermute x9, waiting for transfers between devices: 26.7 us -> 19.5 us  [cross(): return lax.ppermute(value, DP, pairs)]
    unnamed x29 -> x28, local copies, waits for them, and re-layouts: 7.52 us -> 3.39 us
    all_to_all x1, waiting for transfers between devices: 0.01 us -> 3.42 us  [all_shares(): return lax.all_to_all(copies, DP, split_axis=0, concat_axis=0, tiled=True)]
    concatenate x0 -> x1, other arithmetic: none -> 2.25 us  [per_device(): pair = jnp.concatenate([context, shift(ready, 'c', 1)], axis=0)]
    concatenate x1 -> x0, local copies, waits for them, and re-layouts: 1.99 us -> none  [per_device(): pair = jnp.concatenate([context, shift(ready, 'c', 1)], axis=0)]
  transfers between devices with their start and end apart: 27 -> 27, of which waited for: 8 -> 7; matrix products, arithmetic and copies ran while one was open for 11% -> 11% of each run, Pallas kernels for 24% -> 27%
where the time goes in v12:
time: 143 us; the launch traced here: 142 us
  starting transfers between devices  53.1 us (37%)
  Pallas kernels  43.2 us (30%)
  waiting for transfers between devices  24 us (17%)
  local copies, waits for them, and re-layouts  11.2 us (8%)
  other arithmetic  9.15 us (6%)
    ppermute x15, starting transfers between devices, shift(): lax.ppermute(value, axis, [(i, (i + step) % size) for i in range(size)])  21 us
    ppermute x9, waiting for transfers between devices, cross(): return lax.ppermute(value, DP, pairs)  19.5 us
    ppermute x9, starting transfers between devices, cross(): return lax.ppermute(value, DP, pairs)  13.8 us
    pallas_call x3, Pallas kernels, context_product(): pl.pallas_call(body, out_shape=jax.ShapeDtypeStruct((out_rows, width), dt...  13.4 us
    all_to_all x2, starting transfers between devices, exchange(): return lax.all_to_all(blocks, DP, split_axis=0, concat_axis=0, tiled=True)  11 us
    pallas_call x3, Pallas kernels, forward_product(): pl.pallas_call(body, out_shape=[jax.ShapeDtypeStruct((tile, rows), BF16)]...  9.41 us
    pallas_call x1, Pallas kernels, weight_product(): pl.pallas_call(body, out_shape=[jax.ShapeDtypeStruct((block, width), BF16...  8.92 us
    all_to_all x1, starting transfers between devices, all_shares(): return lax.all_to_all(copies, DP, split_axis=0, concat_axis=0, tiled=True)  7.31 us
  transfers between devices with their start and end apart: 27, of which 7 were waited for; matrix products, arithmetic and copies ran while one was open for 11% of the time, Pallas kernels for 27%

profile of v12, /device:TPU:1, one launch (start us, length us, event | category | flops | bytes accessed | tf_op | source)
XLA Modules:
  0.0 141.7 jit_solution(1497988961050593818)
XLA Ops:
  0.6 2.9 %forward_product.3 = (bf16[640,256]{1,0:T(8,128)(2,1)S(1)}, bf16[640,256]{1,0:T(8,128)(2,1)S(1)}) custom-call(s32[1]{0:T(128)} %bitcast.3.which, bf16[5120,1280]{1,0:T(8,128)(2,1)} %refs_3_.3, bf16[256,1280]{1,0:T(8,128)(2,1)} %context_ref.6), custom_call_target="tpu_custom_call" | custom-call | tf_op jit(solution)/shard_map/forward_product/pallas_call | solution.py:175
  3.6 1.5 %collective-permute-start.2 = (bf16[256,1280]{1,0:T(8,128)(2,1)}, bf16[256,1280]{1,0:T(8,128)(2,1)S(1)}, u32[]{:S(2)}, u32[]{:S(2)}) collective-permute-start(bf16[256,1280]{1,0:T(8,128)(2,1)} %context_ref.6), channel_id=1, source_target_pairs={{0,4},{4,0},{1,5},{5,1},{2,6},{6,2},{3,7},{7,3},{8,12},{12,8},{9,1... | collective-permute-start | bytes 1966088 | tf_op jit(solution)/shard_map/ppermute | solution.py:22
  5.1 1.8 %collective-permute-start = (bf16[640,256]{1,0:T(8,128)(2,1)S(1)}, bf16[640,256]{1,0:T(8,128)(2,1)S(1)}, u32[]{:S(2)}, u32[]{:S(2)}) collective-permute-start(bf16[640,256]{1,0:T(8,128)(2,1)S(1)} %get-tuple-element.47), channel_id=1, source_target_pairs={{0,1},{1,2},{2,3},{3,0},{4,5},{5,6},{6,7},{7,4},{8,9},{9,10},{10,1... | collective-permute-start | bytes 983048 | tf_op jit(solution)/shard_map/ppermute | solution.py:22
  6.8 2.1 %collective-permute-start.1 = (bf16[640,256]{1,0:T(8,128)(2,1)S(1)}, bf16[640,256]{1,0:T(8,128)(2,1)S(1)}, u32[]{:S(2)}, u32[]{:S(2)}) collective-permute-start(bf16[640,256]{1,0:T(8,128)(2,1)S(1)} %get-tuple-element.48), channel_id=1, source_target_pairs={{0,3},{1,0},{2,1},{3,2},{4,7},{5,4},{6,5},{7,6},{8,11},{9,8},{10,9... | collective-permute-start | bytes 983048 | tf_op jit(solution)/shard_map/ppermute | solution.py:22
  8.9 2.9 %forward_product.4.refs_0_ = bf16[1280,256]{1,0:T(8,128)(2,1)S(1)} custom-call(s32[1]{0:T(128)} %bitcast.4.which, bf16[5120,1280]{1,0:T(8,128)(2,1)} %refs_3_.3, bf16[256,1280]{1,0:T(8,128)(2,1)} %context_ref.6), custom_call_target="tpu_custom_call" | custom-call | tf_op jit(solution)/shard_map/forward_product/pallas_call | solution.py:175
  11.8 3.6 %forward_product.5.refs_2_ = bf16[1280,256]{1,0:T(8,128)(2,1)} custom-call(s32[1]{0:T(128)} %bitcast.5.which, bf16[5120,1280]{1,0:T(8,128)(2,1)} %refs_3_.3, bf16[256,1280]{1,0:T(8,128)(2,1)} %context_ref.6), custom_call_target="tpu_custom_call" | custom-call | tf_op jit(solution)/shard_map/forward_product/pallas_call | solution.py:175
  15.4 2.2 %pad_maximum_fusion.refs_4_ = bf16[512,1280]{1,0:T(8,128)(2,1)} fusion(bf16[256,1280]{1,0:T(8,128)(2,1)S(1)} %collective-permute-done.2, bf16[256,1280]{1,0:T(8,128)(2,1)} %context_ref.6), kind=kLoop, calls=%fused_computation | loop fusion | flops 2621440 | bytes 2621440 | tf_op jit(solution)/shard_map/concatenate | solution.py:343
  17.7 1.9 %top_up.1 = (bf16[1280,256]{1,0:T(8,128)(2,1)S(1)}, bf16[1280,256]{1,0:T(8,128)(2,1)}) custom-call(bf16[1280,256]{1,0:T(8,128)(2,1)S(1)} %forward_product.4.refs_0_, bf16[640,256]{1,0:T(8,128)(2,1)S(1)} %collective-permute-done.refs_1_, bf16[1280,256]{1,0:T(8,128)(2,1)} %forward_product.5.refs_2_, ...), custom_call_target="tpu_custom_call", output_to_operand_aliasing={{0}: (0, {}), {1}: (2, {})} | custom-call | tf_op jit(solution)/shard_map/top_up/pallas_call | solution.py:144
  19.6 2.7 %collective-permute-start.4 = (bf16[1280,256]{1,0:T(8,128)(2,1)}, bf16[1280,256]{1,0:T(8,128)(2,1)}, u32[]{:S(2)}, u32[]{:S(2)}) collective-permute-start(bf16[1280,256]{1,0:T(8,128)(2,1)} %get-tuple-element.55), channel_id=1, source_target_pairs={{0,3},{1,0},{2,1},{3,2},{4,7},{5,4},{6,5},{7,6},{8,11},{9,8},{10,9... | collective-permute-start | bytes 1966088 | tf_op jit(solution)/shard_map/ppermute | solution.py:22
  22.6 1.3 collective-permute-start.8
  23.9 1.5 %collective-permute-start.9 = (bf16[512,1280]{1,0:T(8,128)(2,1)}, bf16[512,1280]{1,0:T(8,128)(2,1)}, u32[]{:S(2)}, u32[]{:S(2)}) collective-permute-start(bf16[512,1280]{1,0:T(8,128)(2,1)} %pad_maximum_fusion.refs_4_), channel_id=1, source_target_pairs={{0,96},{4,28},{8,104},{12,4},{16,112},{20,12},{24,120},{28,20},{32... | collective-permute-start | bytes 3932168 | tf_op jit(solution)/shard_map/ppermute | solution.py:37
  25.4 2.9 %hidden_part.1 = (f32[1280,256]{1,0:T(8,128)S(1)}, f32[1280,256]{1,0:T(8,128)S(1)}) custom-call(s32[1]{0:T(128)} %bitcast.2.which, bf16[5120,1280]{1,0:T(8,128)(2,1)} %refs_3_.3, bf16[256,1280]{1,0:T(8,128)(2,1)} %context_ref.6, bf16[256,1280]{1,0:T(8,128)(2,1)S(1)} %copy-done.3, bf16[256,1280]{1,0:T(8,128)(2,1)S(1)} %copy-done.4, ...), custom_call_target="tpu_custom_call" | custom-call | tf_op jit(solution)/shard_map/hidden_part/pallas_call | solution.py:210
  28.9 7.3 %all-to-all-start = ((f32[32,1,8]{2,1,0:T(1,128)}), f32[32,1,8]{2,1,0:T(1,128)S(1)}, u32[]{:S(2)}, u32[]{:S(2)}) async-start(f32[32,1,8]{2,1,0:T(1,128)} %broadcast_in_dim.16), calls=%async_computation | async-start | bytes 32768 | tf_op jit(solution)/shard_map/all_to_all | solution.py:42
  36.8 1.7 %multiply_reduce_fusion.1 = (f32[256]{0:T(256)S(1)}, f32[256]{0:T(256)S(1)}) fusion(bf16[1280,256]{1,0:T(8,128)(2,1)} %collective-permute-done.4, f32[1280,256]{1,0:T(8,128)S(1)} %get-tuple-element.57, bf16[1280,256]{1,0:T(8,128)(2,1)} %collective-permute-done.3, f32[1280,256]{1,0:T(8,128)S(1)} %get-tuple-element.58), kind=kLoop, calls=%fused_computation.3 | loop fusion | flops 2620928 | bytes 3934208 | tf_op jit(solution)/shard_map/reduce_sum | solution.py:359
  38.6 3.7 %collective-permute-start.6 = (f32[2,256]{1,0:T(2,128)S(1)}, f32[2,256]{1,0:T(2,128)S(1)}, u32[]{:S(2)}, u32[]{:S(2)}) collective-permute-start(f32[2,256]{1,0:T(2,128)S(1)} %pad_maximum_fusion.3), channel_id=1, source_target_pairs={{0,2},{1,3},{2,0},{3,1},{4,6},{5,7},{6,4},{7,5},{8,10},{9,11},{10,... | collective-permute-start | bytes 6152 | tf_op jit(solution)/shard_map/ppermute | solution.py:22
  42.3 3.4 %all-to-all-done = f32[32,1,8]{2,1,0:T(1,128)S(1)} async-done(((f32[32,1,8]{2,1,0:T(1,128)}), f32[32,1,8]{2,1,0:T(1,128)S(1)}, u32[]{:S(2)}, u32[]{:S(2)}) %all-to-all-start) | async-done | bytes 1056 | tf_op jit(solution)/shard_map/all_to_all | solution.py:42
  46.1 1.0 collective-permute-start.13
  47.1 1.6 %subtract_convert_fusion.refs_0_.grad_ref = bf16[1280,256]{1,0:T(8,128)(2,1)S(1)} fusion(f32[1280,256]{1,0:T(8,128)S(1)} %get-tuple-element.58, f32[256]{0:T(256)S(1)} %bitcast.68, f32[256]{0:T(256)S(1)} %bitcast.67, bf16[1280,256]{1,0:T(8,128)(2,1)} %collective-permute-done.4, f32[1280,256]{1,0:T(8,128)S(1)} %get-tuple-element.57, ...), kind=kLoop, calls=%fused_computation.1 | loop fusion | flops 2621440 | bytes 4589568 | tf_op jit(solution)/shard_map/convert_element_type | solution.py:375
  48.8 2.7 %collective-permute-start.11 = (bf16[1280,256]{1,0:T(8,128)(2,1)S(1)}, bf16[1280,256]{1,0:T(8,128)(2,1)S(1)}, u32[]{:S(2)}, u32[]{:S(2)}) collective-permute-start(bf16[1280,256]{1,0:T(8,128)(2,1)S(1)} %subtract_convert_fusion.refs_0_.grad_ref), channel_id=1, source_target_pairs={{0,3},{1,0},{2,1},{3,2},{4,7},{5,4},{6,5},{7,6},{8,11},{9,8},{10,9... | collective-permute-start | bytes 1966088 | tf_op jit(solution)/shard_map/ppermute | solution.py:22
  51.5 2.3 %collective-permute-start.12 = (bf16[640,256]{1,0:T(8,128)(2,1)S(1)}, bf16[640,256]{1,0:T(8,128)(2,1)S(1)}, u32[]{:S(2)}, u32[]{:S(2)}) collective-permute-start(bf16[640,256]{1,0:T(8,128)(2,1)S(1)} %bitcast.61), channel_id=1, source_target_pairs={{0,4},{4,0},{1,5},{5,1},{2,6},{6,2},{3,7},{7,3},{8,12},{12,8},{9,1... | collective-permute-start | bytes 983048 | tf_op jit(solution)/shard_map/ppermute | solution.py:22
  54.2 3.0 %context_product.3.refs_4_ = f32[256,1280]{1,0:T(8,128)S(1)} custom-call(s32[1]{0:T(128)} %bitcast.2.which, bf16[1280,256]{1,0:T(8,128)(2,1)S(1)} %subtract_convert_fusion.refs_0_.grad_ref, bf16[5120,1280]{1,0:T(8,128)(2,1)} %refs_3_.3), custom_call_target="tpu_custom_call" | custom-call | tf_op jit(solution)/shard_map/context_product/pallas_call | solution.py:104
  57.1 1.1 copy-done
  58.3 1.6 %place_rows.1 = bf16[512,1280]{1,0:T(8,128)(2,1)} custom-call(bf16[512,256]{1,0:T(8,128)(2,1)S(1)} %fusion.refs_5_.slots_ref, bf16[1280,256]{1,0:T(8,128)(2,1)S(1)} %subtract_convert_fusion.refs_0_.grad_ref), custom_call_target="tpu_custom_call" | custom-call | tf_op jit(solution)/shard_map/place_rows/pallas_call | solution.py:125
  59.9 6.5 %all-to-all-start.1 = ((bf16[32,16,1280]{2,1,0:T(8,128)(2,1)}), bf16[32,16,1280]{2,1,0:T(8,128)(2,1)}, u32[]{:S(2)}, u32[]{:S(2)}) async-start(bf16[32,16,1280]{2,1,0:T(8,128)(2,1)} %bitcast.35), calls=%async_computation.1 | async-start | bytes 2621440 | tf_op jit(solution)/shard_map/all_to_all | solution.py:58
  67.9 2.7 %collective-permute-start.15 = (bf16[640,256]{1,0:T(8,128)(2,1)}, bf16[640,256]{1,0:T(8,128)(2,1)}, u32[]{:S(2)}, u32[]{:S(2)}) collective-permute-start(bf16[640,256]{1,0:T(8,128)(2,1)} %slice.33), channel_id=1, source_target_pairs={{0,3},{1,0},{2,1},{3,2},{4,7},{5,4},{6,5},{7,6},{8,11},{9,8},{10,9... | collective-permute-start | bytes 983048 | tf_op jit(solution)/shard_map/ppermute | solution.py:22
  70.7 0.9 pad_maximum_fusion.1
  71.6 1.3 collective-permute-start.16
  73.0 1.3 copy-done.1
  74.3 5.1 %context_product.4.refs_4_ = f32[256,1280]{1,0:T(8,128)S(1)} custom-call(s32[2]{0:T(128)S(1)} %pad_add_fusion.1.which, bf16[1280,256]{1,0:T(8,128)(2,1)S(1)} %collective-permute-done.11.refs_0_, bf16[1280,256]{1,0:T(8,128)(2,1)S(1)} %collective-permute-done.10.refs_1_, bf16[5120,1280]{1,0:T(8,128)(2,1)} %refs_3_.3, bf16[5120,1280]{1,0:T(8,128)(2,1)} %refs_3_.3, ...), custom_call_target="tpu_custom_call" | custom-call | tf_op jit(solution)/shard_map/context_product/pallas_call | solution.py:104
  79.4 1.1 dynamic-slice_bitcast_fusion.2
  80.7 1.1 fusion.8
  82.2 5.2 %lay_out.1 = (bf16[8,160,256]{2,1,0:T(8,128)(2,1)S(1)}, bf16[8,160,256]{2,1,0:T(8,128)(2,1)}, bf16[8,160,256]{2,1,0:T(8,128)(2,1)}, bf16[8,160,256]{2,1,0:T(8,128)(2,1)}) custom-call(s32[4]{0:T(128)S(1)} %pad_add_fusion.2.where, bf16[4,2,160,256]{3,2,1,0:T(8,128)(2,1)S(1)} %bitcast.49, bf16[4,2,160,256]{3,2,1,0:T(8,128)(2,1)S(1)} %bitcast.53, ...), custom_call_target="tpu_custom_call" | custom-call | tf_op jit(solution)/shard_map/lay_out/pallas_call | solution.py:278
  87.4 0.9 copy-done.2
  88.3 1.0 collective-permute-start.18
  89.3 2.4 %collective-permute-start.19 = (bf16[1280,256]{1,0:T(8,128)(2,1)}, bf16[1280,256]{1,0:T(8,128)(2,1)}, u32[]{:S(2)}, u32[]{:S(2)}) collective-permute-start(bf16[1280,256]{1,0:T(8,128)(2,1)} %bitcast.32), channel_id=1, source_target_pairs={{0,64},{4,20},{8,72},{12,28},{16,80},{20,4},{24,88},{28,12},{32,96... | collective-permute-start | bytes 1966088 | tf_op jit(solution)/shard_map/ppermute | solution.py:37
  91.6 1.2 collective-permute-start.20
  92.9 5.3 %context_product.5 = bf16[512,1280]{1,0:T(8,128)(2,1)} custom-call(s32[2]{0:T(128)S(1)} %pad_add_fusion.which, bf16[640,256]{1,0:T(8,128)(2,1)} %collective-permute-done.14.refs_0_, bf16[640,256]{1,0:T(8,128)(2,1)} %collective-permute-done.15.refs_1_, bf16[5120,1280]{1,0:T(8,128)(2,1)} %refs_3_.3, bf16[5120,1280]{1,0:T(8,128)(2,1)} %refs_3_.3, ...), custom_call_target="tpu_custom_call" | custom-call | tf_op jit(solution)/shard_map/context_product/pallas_call | solution.py:104
  98.2 4.5 %all-to-all-start.2 = ((bf16[32,16,1280]{2,1,0:T(8,128)(2,1)}), bf16[32,16,1280]{2,1,0:T(8,128)(2,1)S(1)}, u32[]{:S(2)}, u32[]{:S(2)}) async-start(bf16[32,16,1280]{2,1,0:T(8,128)(2,1)} %bitcast.36), calls=%async_computation.2 | async-start | bytes 2621440 | tf_op jit(solution)/shard_map/all_to_all | solution.py:58
  103.6 3.4 %collective-permute-done.19.refs_2_ = bf16[1280,256]{1,0:T(8,128)(2,1)} collective-permute-done((bf16[1280,256]{1,0:T(8,128)(2,1)}, bf16[1280,256]{1,0:T(8,128)(2,1)}, u32[]{:S(2)}, u32[]{:S(2)}) %collective-permute-start.19) | collective-permute-done | bytes 655392 | tf_op jit(solution)/shard_map/ppermute | solution.py:37
  107.0 10.4 %collective-permute-done.20.refs_3_ = bf16[1280,256]{1,0:T(8,128)(2,1)} collective-permute-done((bf16[1280,256]{1,0:T(8,128)(2,1)}, bf16[1280,256]{1,0:T(8,128)(2,1)}, u32[]{:S(2)}, u32[]{:S(2)}) %collective-permute-start.20) | collective-permute-done | bytes 655392 | tf_op jit(solution)/shard_map/ppermute | solution.py:37
  117.4 8.9 %weight_product.1 = (f32[160,1280]{1,0:T(8,128)}, bf16[160,1280]{1,0:T(8,128)(2,1)}, bf16[160,1280]{1,0:T(8,128)(2,1)}, bf16[160,1280]{1,0:T(8,128)(2,1)}) custom-call(s32[4]{0:T(128)} %pad_add_fusion.3.order_ref, bf16[1280,256]{1,0:T(8,128)(2,1)} %bitcast.56, bf16[1280,256]{1,0:T(8,128)(2,1)} %copy-done.8, ...), custom_call_target="tpu_custom_call" | custom-call | tf_op jit(solution)/shard_map/weight_product/pallas_call | solution.py:315
  126.3 1.3 collective-permute-start.21
  127.6 2.1 %collective-permute-start.22 = (bf16[160,1280]{1,0:T(8,128)(2,1)}, bf16[160,1280]{1,0:T(8,128)(2,1)S(1)}, u32[]{:S(2)}, u32[]{:S(2)}) collective-permute-start(bf16[160,1280]{1,0:T(8,128)(2,1)} %get-tuple-element.89), channel_id=1, source_target_pairs={{0,16},{4,68},{8,24},{12,76},{16,0},{20,84},{24,8},{28,92},{32,48}... | collective-permute-start | bytes 1228808 | tf_op jit(solution)/shard_map/ppermute | solution.py:37
  129.7 2.0 %collective-permute-start.23 = (bf16[160,1280]{1,0:T(8,128)(2,1)}, bf16[160,1280]{1,0:T(8,128)(2,1)S(1)}, u32[]{:S(2)}, u32[]{:S(2)}) collective-permute-start(bf16[160,1280]{1,0:T(8,128)(2,1)} %get-tuple-element.90), channel_id=1, source_target_pairs={{0,24},{4,100},{8,0},{12,108},{16,8},{20,116},{24,16},{28,124},{32... | collective-permute-start | bytes 1228808 | tf_op jit(solution)/shard_map/ppermute | solution.py:37
  131.7 2.2 %reshape.173 = bf16[384,1280]{1,0:T(8,128)(2,1)} reshape(bf16[32,12,1280]{2,1,0:T(8,128)(2,1)} %bitcast.47) | data formatting | bytes 1966080 | tf_op jit(solution)/shard_map/reshape | solution.py:63
  134.6 5.0 %collective-permute-done.22 = bf16[160,1280]{1,0:T(8,128)(2,1)S(1)} collective-permute-done((bf16[160,1280]{1,0:T(8,128)(2,1)}, bf16[160,1280]{1,0:T(8,128)(2,1)S(1)}, u32[]{:S(2)}, u32[]{:S(2)}) %collective-permute-start.22) | collective-permute-done | bytes 409632 | tf_op jit(solution)/shard_map/ppermute | solution.py:37
  139.6 1.1 add_multiply_fusion
  140.7 1.1 reshape.172
  (80 shorter events, 6.1 us)
Async XLA Ops:
  3.6 11.8 %collective-permute-start.2 = (bf16[256,1280]{1,0:T(8,128)(2,1)}, bf16[256,1280]{1,0:T(8,128)(2,1)S(1)}, u32[]{:S(2)}, u32[]{:S(2)}) collective-permute-start(bf16[256,1280]{1,0:T(8,128)(2,1)} %context_ref.6), channel_id=1, source_target_pairs={{0,4},{4,0},{1,5},{5,1},{2,6},{6,2},{3,7},{7,3},{8,12},{12,8},{9,1... | collective-permute-start | bytes 1966088 | tf_op jit(solution)/shard_map/ppermute | solution.py:22
  5.1 12.6 %collective-permute-start = (bf16[640,256]{1,0:T(8,128)(2,1)S(1)}, bf16[640,256]{1,0:T(8,128)(2,1)S(1)}, u32[]{:S(2)}, u32[]{:S(2)}) collective-permute-start(bf16[640,256]{1,0:T(8,128)(2,1)S(1)} %get-tuple-element.47), channel_id=1, source_target_pairs={{0,1},{1,2},{2,3},{3,0},{4,5},{5,6},{6,7},{7,4},{8,9},{9,10},{10,1... | collective-permute-start | bytes 983048 | tf_op jit(solution)/shard_map/ppermute | solution.py:22
  6.8 10.9 %collective-permute-start.1 = (bf16[640,256]{1,0:T(8,128)(2,1)S(1)}, bf16[640,256]{1,0:T(8,128)(2,1)S(1)}, u32[]{:S(2)}, u32[]{:S(2)}) collective-permute-start(bf16[640,256]{1,0:T(8,128)(2,1)S(1)} %get-tuple-element.48), channel_id=1, source_target_pairs={{0,3},{1,0},{2,1},{3,2},{4,7},{5,4},{6,5},{7,6},{8,11},{9,8},{10,9... | collective-permute-start | bytes 983048 | tf_op jit(solution)/shard_map/ppermute | solution.py:22
  17.7 4.6 %copy-start.9 = (f32[1280]{0:T(1024)S(1)}, f32[1280]{0:T(1024)}, u32[]{:S(2)}) copy-start(f32[1280]{0:T(1024)} %param.13) | copy-start | bytes 15364
  17.7 4.6 %copy-start.13 = (s32[64,1]{0,1:T(1,128)S(1)}, s32[64,1]{0,1:T(1,128)}, u32[]{:S(2)}) copy-start(s32[64,1]{0,1:T(1,128)} %param.17) | copy-start | bytes 772
  17.7 4.8 %copy-start.11 = (f32[4]{0:T(128)S(1)}, f32[4]{0:T(128)}, u32[]{:S(2)}) copy-start(f32[4]{0:T(128)} %param.14) | copy-start | bytes 52
  17.7 4.8 %copy-start.12 = (s32[4]{0:T(128)S(1)}, s32[4]{0:T(128)}, u32[]{:S(2)}) copy-start(s32[4]{0:T(128)} %param.15) | copy-start | bytes 52
  17.7 7.7 %copy-start.3 = (bf16[256,1280]{1,0:T(8,128)(2,1)S(1)}, bf16[256,1280]{1,0:T(8,128)(2,1)}, u32[]{:S(2)}) copy-start(bf16[256,1280]{1,0:T(8,128)(2,1)} %residual_ref.1) | copy-start | bytes 1966084
  17.7 7.7 %copy-start.4 = (bf16[256,1280]{1,0:T(8,128)(2,1)S(1)}, bf16[256,1280]{1,0:T(8,128)(2,1)}, u32[]{:S(2)}) copy-start(bf16[256,1280]{1,0:T(8,128)(2,1)} %cotangent_ref.1) | copy-start | bytes 1966084
  19.6 17.2 %collective-permute-start.3 = (bf16[1280,256]{1,0:T(8,128)(2,1)S(1)}, bf16[1280,256]{1,0:T(8,128)(2,1)}, u32[]{:S(2)}, u32[]{:S(2)}) collective-permute-start(bf16[1280,256]{1,0:T(8,128)(2,1)S(1)} %get-tuple-element.54), channel_id=1, source_target_pairs={{0,1},{1,2},{2,3},{3,0},{4,5},{5,6},{6,7},{7,4},{8,9},{9,10},{10,1... | collective-permute-start | bytes 1966088 | tf_op jit(solution)/shard_map/ppermute | solution.py:22
  19.6 17.2 %collective-permute-start.4 = (bf16[1280,256]{1,0:T(8,128)(2,1)}, bf16[1280,256]{1,0:T(8,128)(2,1)}, u32[]{:S(2)}, u32[]{:S(2)}) collective-permute-start(bf16[1280,256]{1,0:T(8,128)(2,1)} %get-tuple-element.55), channel_id=1, source_target_pairs={{0,3},{1,0},{2,1},{3,2},{4,7},{5,4},{6,5},{7,6},{8,11},{9,8},{10,9... | collective-permute-start | bytes 1966088 | tf_op jit(solution)/shard_map/ppermute | solution.py:22
  22.6 26.2 %collective-permute-start.8 = (bf16[512,1280]{1,0:T(8,128)(2,1)}, bf16[512,1280]{1,0:T(8,128)(2,1)}, u32[]{:S(2)}, u32[]{:S(2)}) collective-permute-start(bf16[512,1280]{1,0:T(8,128)(2,1)} %pad_maximum_fusion.refs_4_), channel_id=1, source_target_pairs={{0,32},{4,12},{8,40},{12,20},{16,48},{20,28},{24,56},{28,4},{32,64... | collective-permute-start | bytes 3932168 | tf_op jit(solution)/shard_map/ppermute | solution.py:37
  23.9 24.9 %collective-permute-start.9 = (bf16[512,1280]{1,0:T(8,128)(2,1)}, bf16[512,1280]{1,0:T(8,128)(2,1)}, u32[]{:S(2)}, u32[]{:S(2)}) collective-permute-start(bf16[512,1280]{1,0:T(8,128)(2,1)} %pad_maximum_fusion.refs_4_), channel_id=1, source_target_pairs={{0,96},{4,28},{8,104},{12,4},{16,112},{20,12},{24,120},{28,20},{32... | collective-permute-start | bytes 3932168 | tf_op jit(solution)/shard_map/ppermute | solution.py:37
  28.9 16.8 %all-to-all-start = ((f32[32,1,8]{2,1,0:T(1,128)}), f32[32,1,8]{2,1,0:T(1,128)S(1)}, u32[]{:S(2)}, u32[]{:S(2)}) async-start(f32[32,1,8]{2,1,0:T(1,128)} %broadcast_in_dim.16), calls=%async_computation | async-start | bytes 32768 | tf_op jit(solution)/shard_map/all_to_all | solution.py:42
  36.8 9.1 %copy-start.10 = (s32[4]{0:T(128)S(1)}, s32[4]{0:T(128)}, u32[]{:S(2)}) copy-start(s32[4]{0:T(128)} %param.16) | copy-start | bytes 52
  38.5 7.6 %collective-permute-start.5 = (f32[2,256]{1,0:T(2,128)S(1)}, f32[2,256]{1,0:T(2,128)S(1)}, u32[]{:S(2)}, u32[]{:S(2)}) collective-permute-start(f32[2,256]{1,0:T(2,128)S(1)} %pad_maximum_fusion.3), channel_id=1, source_target_pairs={{0,1},{1,2},{2,3},{3,0},{4,5},{5,6},{6,7},{7,4},{8,9},{9,10},{10,1... | collective-permute-start | bytes 6152 | tf_op jit(solution)/shard_map/ppermute | solution.py:22
  38.6 8.5 %collective-permute-start.6 = (f32[2,256]{1,0:T(2,128)S(1)}, f32[2,256]{1,0:T(2,128)S(1)}, u32[]{:S(2)}, u32[]{:S(2)}) collective-permute-start(f32[2,256]{1,0:T(2,128)S(1)} %pad_maximum_fusion.3), channel_id=1, source_target_pairs={{0,2},{1,3},{2,0},{3,1},{4,6},{5,7},{6,4},{7,5},{8,10},{9,11},{10,... | collective-permute-start | bytes 6152 | tf_op jit(solution)/shard_map/ppermute | solution.py:22
  42.3 4.8 %collective-permute-start.7 = (f32[2,256]{1,0:T(2,128)S(1)}, f32[2,256]{1,0:T(2,128)S(1)}, u32[]{:S(2)}, u32[]{:S(2)}) collective-permute-start(f32[2,256]{1,0:T(2,128)S(1)} %pad_maximum_fusion.3), channel_id=1, source_target_pairs={{0,3},{1,0},{2,1},{3,2},{4,7},{5,4},{6,5},{7,6},{8,11},{9,8},{10,9... | collective-permute-start | bytes 6152 | tf_op jit(solution)/shard_map/ppermute | solution.py:22
  46.1 20.3 %collective-permute-start.13 = (bf16[512,1280]{1,0:T(8,128)(2,1)}, bf16[512,1280]{1,0:T(8,128)(2,1)}, u32[]{:S(2)}, u32[]{:S(2)}) collective-permute-start(bf16[512,1280]{1,0:T(8,128)(2,1)} %pad_maximum_fusion.refs_4_), channel_id=1, source_target_pairs={{0,64},{4,20},{8,72},{12,28},{16,80},{20,4},{24,88},{28,12},{32,96... | collective-permute-start | bytes 3932168 | tf_op jit(solution)/shard_map/ppermute | solution.py:37
  48.8 17.6 %collective-permute-start.10 = (bf16[1280,256]{1,0:T(8,128)(2,1)S(1)}, bf16[1280,256]{1,0:T(8,128)(2,1)S(1)}, u32[]{:S(2)}, u32[]{:S(2)}) collective-permute-start(bf16[1280,256]{1,0:T(8,128)(2,1)S(1)} %subtract_convert_fusion.refs_0_.grad_ref), channel_id=1, source_target_pairs={{0,1},{1,2},{2,3},{3,0},{4,5},{5,6},{6,7},{7,4},{8,9},{9,10},{10,1... | collective-permute-start | bytes 1966088 | tf_op jit(solution)/shard_map/ppermute | solution.py:22
  48.8 17.6 %collective-permute-start.11 = (bf16[1280,256]{1,0:T(8,128)(2,1)S(1)}, bf16[1280,256]{1,0:T(8,128)(2,1)S(1)}, u32[]{:S(2)}, u32[]{:S(2)}) collective-permute-start(bf16[1280,256]{1,0:T(8,128)(2,1)S(1)} %subtract_convert_fusion.refs_0_.grad_ref), channel_id=1, source_target_pairs={{0,3},{1,0},{2,1},{3,2},{4,7},{5,4},{6,5},{7,6},{8,11},{9,8},{10,9... | collective-permute-start | bytes 1966088 | tf_op jit(solution)/shard_map/ppermute | solution.py:22
  51.5 6.7 %collective-permute-start.12 = (bf16[640,256]{1,0:T(8,128)(2,1)S(1)}, bf16[640,256]{1,0:T(8,128)(2,1)S(1)}, u32[]{:S(2)}, u32[]{:S(2)}) collective-permute-start(bf16[640,256]{1,0:T(8,128)(2,1)S(1)} %bitcast.61), channel_id=1, source_target_pairs={{0,4},{4,0},{1,5},{5,1},{2,6},{6,2},{3,7},{7,3},{8,12},{12,8},{9,1... | collective-permute-start | bytes 983048 | tf_op jit(solution)/shard_map/ppermute | solution.py:22
  57.1 1.2 copy-start
  58.3 1.6 %copy-start.5 = (bf16[640,256]{1,0:T(8,128)(2,1)}, bf16[640,256]{1,0:T(8,128)(2,1)S(1)}, u32[]{:S(2)}) copy-start(bf16[640,256]{1,0:T(8,128)(2,1)S(1)} %collective-permute-done.12) | copy-start | bytes 983044
  59.9 38.3 %all-to-all-start.1 = ((bf16[32,16,1280]{2,1,0:T(8,128)(2,1)}), bf16[32,16,1280]{2,1,0:T(8,128)(2,1)}, u32[]{:S(2)}, u32[]{:S(2)}) async-start(bf16[32,16,1280]{2,1,0:T(8,128)(2,1)} %bitcast.35), calls=%async_computation.1 | async-start | bytes 2621440 | tf_op jit(solution)/shard_map/all_to_all | solution.py:58
  67.2 12.2 %collective-permute-start.14 = (bf16[640,256]{1,0:T(8,128)(2,1)}, bf16[640,256]{1,0:T(8,128)(2,1)}, u32[]{:S(2)}, u32[]{:S(2)}) collective-permute-start(bf16[640,256]{1,0:T(8,128)(2,1)} %slice.32), channel_id=1, source_target_pairs={{0,1},{1,2},{2,3},{3,0},{4,5},{5,6},{6,7},{7,4},{8,9},{9,10},{10,1... | collective-permute-start | bytes 983048 | tf_op jit(solution)/shard_map/ppermute | solution.py:22
  67.9 11.4 %collective-permute-start.15 = (bf16[640,256]{1,0:T(8,128)(2,1)}, bf16[640,256]{1,0:T(8,128)(2,1)}, u32[]{:S(2)}, u32[]{:S(2)}) collective-permute-start(bf16[640,256]{1,0:T(8,128)(2,1)} %slice.33), channel_id=1, source_target_pairs={{0,3},{1,0},{2,1},{3,2},{4,7},{5,4},{6,5},{7,6},{8,11},{9,8},{10,9... | collective-permute-start | bytes 983048 | tf_op jit(solution)/shard_map/ppermute | solution.py:22
  71.6 9.1 %collective-permute-start.16 = (bf16[1280,256]{1,0:T(8,128)(2,1)}, bf16[1280,256]{1,0:T(8,128)(2,1)}, u32[]{:S(2)}, u32[]{:S(2)}) collective-permute-start(bf16[1280,256]{1,0:T(8,128)(2,1)} %bitcast.23), channel_id=1, source_target_pairs={{0,4},{4,0},{1,5},{5,1},{2,6},{6,2},{3,7},{7,3},{8,12},{12,8},{9,1... | collective-permute-start | bytes 1966088 | tf_op jit(solution)/shard_map/ppermute | solution.py:22
  73.0 1.3 copy-start.1
  79.4 2.8 %copy-start.6 = (bf16[640,256]{1,0:T(8,128)(2,1)S(1)}, bf16[640,256]{1,0:T(8,128)(2,1)}, u32[]{:S(2)}) copy-start(bf16[640,256]{1,0:T(8,128)(2,1)} %copy-done.5) | copy-start | bytes 983044
  80.5 1.7 %collective-permute-start.17 = (bf16[640,256]{1,0:T(8,128)(2,1)S(1)}, bf16[640,256]{1,0:T(8,128)(2,1)S(1)}, u32[]{:S(2)}, u32[]{:S(2)}) collective-permute-start(bf16[640,256]{1,0:T(8,128)(2,1)S(1)} %bitcast.60), channel_id=1, source_target_pairs={{0,4},{4,0},{1,5},{5,1},{2,6},{6,2},{3,7},{7,3},{8,12},{12,8},{9,1... | collective-permute-start | bytes 983048 | tf_op jit(solution)/shard_map/ppermute | solution.py:22
  87.4 0.9 copy-start.2
  88.3 15.3 %collective-permute-start.18 = (bf16[1280,256]{1,0:T(8,128)(2,1)}, bf16[1280,256]{1,0:T(8,128)(2,1)S(1)}, u32[]{:S(2)}, u32[]{:S(2)}) collective-permute-start(bf16[1280,256]{1,0:T(8,128)(2,1)} %bitcast.31), channel_id=1, source_target_pairs={{0,32},{4,12},{8,40},{12,20},{16,48},{20,28},{24,56},{28,4},{32,64... | collective-permute-start | bytes 1966088 | tf_op jit(solution)/shard_map/ppermute | solution.py:37
  89.3 17.7 %collective-permute-start.19 = (bf16[1280,256]{1,0:T(8,128)(2,1)}, bf16[1280,256]{1,0:T(8,128)(2,1)}, u32[]{:S(2)}, u32[]{:S(2)}) collective-permute-start(bf16[1280,256]{1,0:T(8,128)(2,1)} %bitcast.32), channel_id=1, source_target_pairs={{0,64},{4,20},{8,72},{12,28},{16,80},{20,4},{24,88},{28,12},{32,96... | collective-permute-start | bytes 1966088 | tf_op jit(solution)/shard_map/ppermute | solution.py:37
  91.6 25.7 %collective-permute-start.20 = (bf16[1280,256]{1,0:T(8,128)(2,1)}, bf16[1280,256]{1,0:T(8,128)(2,1)}, u32[]{:S(2)}, u32[]{:S(2)}) collective-permute-start(bf16[1280,256]{1,0:T(8,128)(2,1)} %bitcast.33), channel_id=1, source_target_pairs={{0,96},{4,28},{8,104},{12,4},{16,112},{20,12},{24,120},{28,20},{32... | collective-permute-start | bytes 1966088 | tf_op jit(solution)/shard_map/ppermute | solution.py:37
  98.2 42.4 %all-to-all-start.2 = ((bf16[32,16,1280]{2,1,0:T(8,128)(2,1)}), bf16[32,16,1280]{2,1,0:T(8,128)(2,1)S(1)}, u32[]{:S(2)}, u32[]{:S(2)}) async-start(bf16[32,16,1280]{2,1,0:T(8,128)(2,1)} %bitcast.36), calls=%async_computation.2 | async-start | bytes 2621440 | tf_op jit(solution)/shard_map/all_to_all | solution.py:58
  103.6 13.8 %copy-start.8 = (bf16[1280,256]{1,0:T(8,128)(2,1)}, bf16[1280,256]{1,0:T(8,128)(2,1)S(1)}, u32[]{:S(2)}) copy-start(bf16[1280,256]{1,0:T(8,128)(2,1)S(1)} %collective-permute-done.18.refs_1_) | copy-start | bytes 1966084
  126.3 13.3 %copy-start.7 = (f32[160,1280]{1,0:T(8,128)S(1)}, f32[160,1280]{1,0:T(8,128)}, u32[]{:S(2)}) copy-start(f32[160,1280]{1,0:T(8,128)} %get-tuple-element.87) | copy-start | bytes 2457604
  126.3 8.3 %collective-permute-start.21 = (bf16[160,1280]{1,0:T(8,128)(2,1)}, bf16[160,1280]{1,0:T(8,128)(2,1)S(1)}, u32[]{:S(2)}, u32[]{:S(2)}) collective-permute-start(bf16[160,1280]{1,0:T(8,128)(2,1)} %get-tuple-element.88), channel_id=1, source_target_pairs={{0,8},{4,36},{8,16},{12,44},{16,24},{20,52},{24,0},{28,60},{32,40}... | collective-permute-start | bytes 1228808 | tf_op jit(solution)/shard_map/ppermute | solution.py:37
  127.6 12.0 %collective-permute-start.22 = (bf16[160,1280]{1,0:T(8,128)(2,1)}, bf16[160,1280]{1,0:T(8,128)(2,1)S(1)}, u32[]{:S(2)}, u32[]{:S(2)}) collective-permute-start(bf16[160,1280]{1,0:T(8,128)(2,1)} %get-tuple-element.89), channel_id=1, source_target_pairs={{0,16},{4,68},{8,24},{12,76},{16,0},{20,84},{24,8},{28,92},{32,48}... | collective-permute-start | bytes 1228808 | tf_op jit(solution)/shard_map/ppermute | solution.py:37
  129.7 9.9 %collective-permute-start.23 = (bf16[160,1280]{1,0:T(8,128)(2,1)}, bf16[160,1280]{1,0:T(8,128)(2,1)S(1)}, u32[]{:S(2)}, u32[]{:S(2)}) collective-permute-start(bf16[160,1280]{1,0:T(8,128)(2,1)} %get-tuple-element.90), channel_id=1, source_target_pairs={{0,24},{4,100},{8,0},{12,108},{16,8},{20,116},{24,16},{28,124},{32... | collective-permute-start | bytes 1228808 | tf_op jit(solution)/shard_map/ppermute | solution.py:37

commit v13 on v12

--- a/solution.py
+++ b/solution.py
@@ -416,7 +416,7 @@
     placed = context_product(
         [far_left, far_right], [far_place, far_place + 1], out_proj, before=context_grad, slots=slots
     )
-    placed, d_residual = lax.optimization_barrier((placed, d_residual))
+    placed, d_residual, pieces[3] = lax.optimization_barrier((placed, d_residual, pieces[3]))
     d_context = exchange(placed, lanes)
     order = [jnp.where(c == 0, (y + k) % NY, (x + k - z) % NZ) for k in range(4)]
     d_out_proj, *parts = weight_product(pieces, contexts, jnp.stack(order), block)

time: 143 us -> 152 us (1.063)
  waiting for transfers between devices: 24 us -> 29 us
  starting transfers between devices: 53.1 us -> 55.4 us
  local copies, waits for them, and re-layouts: 11.2 us -> 13 us
    ppermute x9, waiting for transfers between devices: 19.5 us -> 26.2 us  [cross(): return lax.ppermute(value, DP, pairs)]
    all_to_all x2, starting transfers between devices: 11 us -> 13.6 us  [exchange(): return lax.all_to_all(blocks, DP, split_axis=0, concat_axis=0, tiled=True)]
    unnamed x28, local copies, waits for them, and re-layouts: 3.39 us -> 5.24 us
    ppermute x9, starting transfers between devices: 13.8 us -> 11.9 us  [cross(): return lax.ppermute(value, DP, pairs)]
  transfers between devices with their start and end apart: 27 -> 27, of which waited for: 7 -> 10; matrix products, arithmetic and copies ran while one was open for 11% -> 10% of each run, Pallas kernels for 27% -> 25%
where the time goes in v13:
time: 152 us; the launch traced here: 151 us
  starting transfers between devices  55.4 us (36%)
  Pallas kernels  43.1 us (28%)
  waiting for transfers between devices  29 us (19%)
  local copies, waits for them, and re-layouts  13 us (9%)
  other arithmetic  9.15 us (6%)
    ppermute x9, waiting for transfers between devices, cross(): return lax.ppermute(value, DP, pairs)  26.2 us
    ppermute x15, starting transfers between devices, shift(): lax.ppermute(value, axis, [(i, (i + step) % size) for i in range(size)])  22.3 us
    all_to_all x2, starting transfers between devices, exchange(): return lax.all_to_all(blocks, DP, split_axis=0, concat_axis=0, tiled=True)  13.6 us
    pallas_call x3, Pallas kernels, context_product(): pl.pallas_call(body, out_shape=jax.ShapeDtypeStruct((out_rows, width), dt...  13.3 us
    ppermute x9, starting transfers between devices, cross(): return lax.ppermute(value, DP, pairs)  11.9 us
    pallas_call x3, Pallas kernels, forward_product(): pl.pallas_call(body, out_shape=[jax.ShapeDtypeStruct((tile, rows), BF16)]...  9.41 us
    pallas_call x1, Pallas kernels, weight_product(): pl.pallas_call(body, out_shape=[jax.ShapeDtypeStruct((block, width), BF16...  8.92 us
    all_to_all x1, starting transfers between devices, all_shares(): return lax.all_to_all(copies, DP, split_axis=0, concat_axis=0, tiled=True)  7.54 us
  transfers between devices with their start and end apart: 27, of which 10 were waited for; matrix products, arithmetic and copies ran while one was open for 10% of the time, Pallas kernels for 25%

profile of v13, /device:TPU:1, one launch (start us, length us, event | category | flops | bytes accessed | tf_op | source)
XLA Modules:
  0.0 150.8 jit_solution(185999361561977977)
XLA Ops:
  0.6 2.9 %forward_product.3 = (bf16[640,256]{1,0:T(8,128)(2,1)S(1)}, bf16[640,256]{1,0:T(8,128)(2,1)S(1)}) custom-call(s32[1]{0:T(128)} %bitcast.3.which, bf16[5120,1280]{1,0:T(8,128)(2,1)} %refs_3_.3, bf16[256,1280]{1,0:T(8,128)(2,1)} %context_ref.6), custom_call_target="tpu_custom_call" | custom-call | tf_op jit(solution)/shard_map/forward_product/pallas_call | solution.py:175
  3.6 1.5 collective-permute-start.2
  5.1 1.8 %collective-permute-start = (bf16[640,256]{1,0:T(8,128)(2,1)S(1)}, bf16[640,256]{1,0:T(8,128)(2,1)S(1)}, u32[]{:S(2)}, u32[]{:S(2)}) collective-permute-start(bf16[640,256]{1,0:T(8,128)(2,1)S(1)} %get-tuple-element.48), channel_id=1, source_target_pairs={{0,1},{1,2},{2,3},{3,0},{4,5},{5,6},{6,7},{7,4},{8,9},{9,10},{10,1... | collective-permute-start | bytes 983048 | tf_op jit(solution)/shard_map/ppermute | solution.py:22
  6.8 2.1 %collective-permute-start.1 = (bf16[640,256]{1,0:T(8,128)(2,1)S(1)}, bf16[640,256]{1,0:T(8,128)(2,1)S(1)}, u32[]{:S(2)}, u32[]{:S(2)}) collective-permute-start(bf16[640,256]{1,0:T(8,128)(2,1)S(1)} %get-tuple-element.49), channel_id=1, source_target_pairs={{0,3},{1,0},{2,1},{3,2},{4,7},{5,4},{6,5},{7,6},{8,11},{9,8},{10,9... | collective-permute-start | bytes 983048 | tf_op jit(solution)/shard_map/ppermute | solution.py:22
  8.9 2.9 %forward_product.4.refs_0_ = bf16[1280,256]{1,0:T(8,128)(2,1)S(1)} custom-call(s32[1]{0:T(128)} %bitcast.4.which, bf16[5120,1280]{1,0:T(8,128)(2,1)} %refs_3_.3, bf16[256,1280]{1,0:T(8,128)(2,1)} %context_ref.6), custom_call_target="tpu_custom_call" | custom-call | tf_op jit(solution)/shard_map/forward_product/pallas_call | solution.py:175
  11.8 3.6 %forward_product.5.refs_2_ = bf16[1280,256]{1,0:T(8,128)(2,1)} custom-call(s32[1]{0:T(128)} %bitcast.5.which, bf16[5120,1280]{1,0:T(8,128)(2,1)} %refs_3_.3, bf16[256,1280]{1,0:T(8,128)(2,1)} %context_ref.6), custom_call_target="tpu_custom_call" | custom-call | tf_op jit(solution)/shard_map/forward_product/pallas_call | solution.py:175
  15.4 2.2 %pad_maximum_fusion.refs_4_ = bf16[512,1280]{1,0:T(8,128)(2,1)} fusion(bf16[256,1280]{1,0:T(8,128)(2,1)S(1)} %collective-permute-done.2, bf16[256,1280]{1,0:T(8,128)(2,1)} %context_ref.6), kind=kLoop, calls=%fused_computation | loop fusion | flops 2621440 | bytes 2621440 | tf_op jit(solution)/shard_map/concatenate | solution.py:343
  17.7 1.8 %top_up.1 = (bf16[1280,256]{1,0:T(8,128)(2,1)S(1)}, bf16[1280,256]{1,0:T(8,128)(2,1)}) custom-call(bf16[1280,256]{1,0:T(8,128)(2,1)S(1)} %forward_product.4.refs_0_, bf16[640,256]{1,0:T(8,128)(2,1)S(1)} %collective-permute-done.refs_1_, bf16[1280,256]{1,0:T(8,128)(2,1)} %forward_product.5.refs_2_, ...), custom_call_target="tpu_custom_call", output_to_operand_aliasing={{0}: (0, {}), {1}: (2, {})} | custom-call | tf_op jit(solution)/shard_map/top_up/pallas_call | solution.py:144
  19.5 1.6 %collective-permute-start.4 = (bf16[1280,256]{1,0:T(8,128)(2,1)}, bf16[1280,256]{1,0:T(8,128)(2,1)}, u32[]{:S(2)}, u32[]{:S(2)}) collective-permute-start(bf16[1280,256]{1,0:T(8,128)(2,1)} %get-tuple-element.56), channel_id=1, source_target_pairs={{0,3},{1,0},{2,1},{3,2},{4,7},{5,4},{6,5},{7,6},{8,11},{9,8},{10,9... | collective-permute-start | bytes 1966088 | tf_op jit(solution)/shard_map/ppermute | solution.py:22
  21.2 1.3 collective-permute-start.8
  22.5 1.5 %collective-permute-start.9 = (bf16[512,1280]{1,0:T(8,128)(2,1)}, bf16[512,1280]{1,0:T(8,128)(2,1)}, u32[]{:S(2)}, u32[]{:S(2)}) collective-permute-start(bf16[512,1280]{1,0:T(8,128)(2,1)} %pad_maximum_fusion.refs_4_), channel_id=1, source_target_pairs={{0,96},{4,28},{8,104},{12,4},{16,112},{20,12},{24,120},{28,20},{32... | collective-permute-start | bytes 3932168 | tf_op jit(solution)/shard_map/ppermute | solution.py:37
  24.0 1.1 copy-done.3
  25.1 1.1 copy-done.4
  26.2 2.9 %hidden_part.1 = (f32[1280,256]{1,0:T(8,128)S(1)}, f32[1280,256]{1,0:T(8,128)S(1)}) custom-call(s32[1]{0:T(128)} %bitcast.2.which, bf16[5120,1280]{1,0:T(8,128)(2,1)} %refs_3_.3, bf16[256,1280]{1,0:T(8,128)(2,1)} %context_ref.6, bf16[256,1280]{1,0:T(8,128)(2,1)S(1)} %copy-done.3, bf16[256,1280]{1,0:T(8,128)(2,1)S(1)} %copy-done.4, ...), custom_call_target="tpu_custom_call" | custom-call | tf_op jit(solution)/shard_map/hidden_part/pallas_call | solution.py:210
  29.7 7.5 %all-to-all-start = ((f32[32,1,8]{2,1,0:T(1,128)}), f32[32,1,8]{2,1,0:T(1,128)S(1)}, u32[]{:S(2)}, u32[]{:S(2)}) async-start(f32[32,1,8]{2,1,0:T(1,128)} %broadcast_in_dim.16), calls=%async_computation | async-start | bytes 32768 | tf_op jit(solution)/shard_map/all_to_all | solution.py:42
  37.4 1.7 %multiply_reduce_fusion.1 = (f32[256]{0:T(256)S(1)}, f32[256]{0:T(256)S(1)}) fusion(bf16[1280,256]{1,0:T(8,128)(2,1)} %collective-permute-done.4, f32[1280,256]{1,0:T(8,128)S(1)} %get-tuple-element.58, bf16[1280,256]{1,0:T(8,128)(2,1)} %collective-permute-done.3, f32[1280,256]{1,0:T(8,128)S(1)} %get-tuple-element.59), kind=kLoop, calls=%fused_computation.3 | loop fusion | flops 2620928 | bytes 3934208 | tf_op jit(solution)/shard_map/reduce_sum | solution.py:359
  39.0 2.9 %collective-permute-start.7 = (f32[2,256]{1,0:T(2,128)S(1)}, f32[2,256]{1,0:T(2,128)S(1)}, u32[]{:S(2)}, u32[]{:S(2)}) collective-permute-start(f32[2,256]{1,0:T(2,128)S(1)} %pad_maximum_fusion.3), channel_id=1, source_target_pairs={{0,3},{1,0},{2,1},{3,2},{4,7},{5,4},{6,5},{7,6},{8,11},{9,8},{10,9... | collective-permute-start | bytes 6152 | tf_op jit(solution)/shard_map/ppermute | solution.py:22
  42.7 1.9 %all-to-all-done = f32[32,1,8]{2,1,0:T(1,128)S(1)} async-done(((f32[32,1,8]{2,1,0:T(1,128)}), f32[32,1,8]{2,1,0:T(1,128)S(1)}, u32[]{:S(2)}, u32[]{:S(2)}) %all-to-all-start) | async-done | bytes 1056 | tf_op jit(solution)/shard_map/all_to_all | solution.py:42
  45.0 1.0 collective-permute-start.13
  46.0 1.6 %subtract_convert_fusion.refs_0_.grad_ref = bf16[1280,256]{1,0:T(8,128)(2,1)S(1)} fusion(f32[1280,256]{1,0:T(8,128)S(1)} %get-tuple-element.59, f32[256]{0:T(256)S(1)} %bitcast.68, f32[256]{0:T(256)S(1)} %bitcast.67, bf16[1280,256]{1,0:T(8,128)(2,1)} %collective-permute-done.4, f32[1280,256]{1,0:T(8,128)S(1)} %get-tuple-element.58, ...), kind=kLoop, calls=%fused_computation.1 | loop fusion | flops 2621440 | bytes 4589568 | tf_op jit(solution)/shard_map/convert_element_type | solution.py:375
  47.6 2.0 %collective-permute-start.10 = (bf16[1280,256]{1,0:T(8,128)(2,1)S(1)}, bf16[1280,256]{1,0:T(8,128)(2,1)S(1)}, u32[]{:S(2)}, u32[]{:S(2)}) collective-permute-start(bf16[1280,256]{1,0:T(8,128)(2,1)S(1)} %subtract_convert_fusion.refs_0_.grad_ref), channel_id=1, source_target_pairs={{0,1},{1,2},{2,3},{3,0},{4,5},{5,6},{6,7},{7,4},{8,9},{9,10},{10,1... | collective-permute-start | bytes 1966088 | tf_op jit(solution)/shard_map/ppermute | solution.py:22
  49.7 1.0 collective-permute-start.11
  50.9 2.3 %collective-permute-start.12 = (bf16[640,256]{1,0:T(8,128)(2,1)S(1)}, bf16[640,256]{1,0:T(8,128)(2,1)S(1)}, u32[]{:S(2)}, u32[]{:S(2)}) collective-permute-start(bf16[640,256]{1,0:T(8,128)(2,1)S(1)} %bitcast.61), channel_id=1, source_target_pairs={{0,4},{4,0},{1,5},{5,1},{2,6},{6,2},{3,7},{7,3},{8,12},{12,8},{9,1... | collective-permute-start | bytes 983048 | tf_op jit(solution)/shard_map/ppermute | solution.py:22
  53.4 3.0 %context_product.3.refs_4_ = f32[256,1280]{1,0:T(8,128)S(1)} custom-call(s32[1]{0:T(128)} %bitcast.2.which, bf16[1280,256]{1,0:T(8,128)(2,1)S(1)} %subtract_convert_fusion.refs_0_.grad_ref, bf16[5120,1280]{1,0:T(8,128)(2,1)} %refs_3_.3), custom_call_target="tpu_custom_call" | custom-call | tf_op jit(solution)/shard_map/context_product/pallas_call | solution.py:104
  56.4 7.2 %collective-permute-done.13.refs_6_ = bf16[512,1280]{1,0:T(8,128)(2,1)} collective-permute-done((bf16[512,1280]{1,0:T(8,128)(2,1)}, bf16[512,1280]{1,0:T(8,128)(2,1)}, u32[]{:S(2)}, u32[]{:S(2)}) %collective-permute-start.13) | collective-permute-done | bytes 1310752 | tf_op jit(solution)/shard_map/ppermute | solution.py:37
  66.0 2.4 %collective-permute-start.15 = (bf16[640,256]{1,0:T(8,128)(2,1)}, bf16[640,256]{1,0:T(8,128)(2,1)}, u32[]{:S(2)}, u32[]{:S(2)}) collective-permute-start(bf16[640,256]{1,0:T(8,128)(2,1)} %slice.33), channel_id=1, source_target_pairs={{0,3},{1,0},{2,1},{3,2},{4,7},{5,4},{6,5},{7,6},{8,11},{9,8},{10,9... | collective-permute-start | bytes 983048 | tf_op jit(solution)/shard_map/ppermute | solution.py:22
  68.5 0.9 pad_maximum_fusion.1
  69.4 3.1 %collective-permute-start.16 = (bf16[1280,256]{1,0:T(8,128)(2,1)}, bf16[1280,256]{1,0:T(8,128)(2,1)}, u32[]{:S(2)}, u32[]{:S(2)}) collective-permute-start(bf16[1280,256]{1,0:T(8,128)(2,1)} %bitcast.23), channel_id=1, source_target_pairs={{0,4},{4,0},{1,5},{5,1},{2,6},{6,2},{3,7},{7,3},{8,12},{12,8},{9,1... | collective-permute-start | bytes 1966088 | tf_op jit(solution)/shard_map/ppermute | solution.py:22
  72.6 1.6 %place_rows.1 = bf16[512,1280]{1,0:T(8,128)(2,1)} custom-call(bf16[512,256]{1,0:T(8,128)(2,1)S(1)} %fusion.refs_5_.slots_ref, bf16[1280,256]{1,0:T(8,128)(2,1)S(1)} %subtract_convert_fusion.refs_0_.grad_ref), custom_call_target="tpu_custom_call" | custom-call | tf_op jit(solution)/shard_map/place_rows/pallas_call | solution.py:125
  74.2 6.4 %all-to-all-start.1 = ((bf16[32,16,1280]{2,1,0:T(8,128)(2,1)}), bf16[32,16,1280]{2,1,0:T(8,128)(2,1)}, u32[]{:S(2)}, u32[]{:S(2)}) async-start(bf16[32,16,1280]{2,1,0:T(8,128)(2,1)} %bitcast.35), calls=%async_computation.1 | async-start | bytes 2621440 | tf_op jit(solution)/shard_map/all_to_all | solution.py:58
  80.7 1.3 copy-done.1
  82.0 5.1 %context_product.4.refs_4_ = f32[256,1280]{1,0:T(8,128)S(1)} custom-call(s32[2]{0:T(128)S(1)} %pad_add_fusion.1.which, bf16[1280,256]{1,0:T(8,128)(2,1)S(1)} %collective-permute-done.11.refs_0_, bf16[1280,256]{1,0:T(8,128)(2,1)S(1)} %collective-permute-done.10.refs_1_, bf16[5120,1280]{1,0:T(8,128)(2,1)} %refs_3_.3, bf16[5120,1280]{1,0:T(8,128)(2,1)} %refs_3_.3, ...), custom_call_target="tpu_custom_call" | custom-call | tf_op jit(solution)/shard_map/context_product/pallas_call | solution.py:104
  87.1 1.1 dynamic-slice_bitcast_fusion.2
  88.9 1.1 fusion.8
  90.0 5.2 %lay_out.1 = (bf16[8,160,256]{2,1,0:T(8,128)(2,1)S(1)}, bf16[8,160,256]{2,1,0:T(8,128)(2,1)}, bf16[8,160,256]{2,1,0:T(8,128)(2,1)}, bf16[8,160,256]{2,1,0:T(8,128)(2,1)}) custom-call(s32[4]{0:T(128)S(1)} %pad_add_fusion.2.where, bf16[4,2,160,256]{3,2,1,0:T(8,128)(2,1)S(1)} %bitcast.49, bf16[4,2,160,256]{3,2,1,0:T(8,128)(2,1)S(1)} %bitcast.53, ...), custom_call_target="tpu_custom_call" | custom-call | tf_op jit(solution)/shard_map/lay_out/pallas_call | solution.py:278
  96.1 2.5 %collective-permute-start.18 = (bf16[1280,256]{1,0:T(8,128)(2,1)}, bf16[1280,256]{1,0:T(8,128)(2,1)S(1)}, u32[]{:S(2)}, u32[]{:S(2)}) collective-permute-start(bf16[1280,256]{1,0:T(8,128)(2,1)} %bitcast.33), channel_id=1, source_target_pairs={{0,96},{4,28},{8,104},{12,4},{16,112},{20,12},{24,120},{28,20},{32... | collective-permute-start | bytes 1966088 | tf_op jit(solution)/shard_map/ppermute | solution.py:37
  98.6 1.8 %collective-permute-start.20 = (bf16[1280,256]{1,0:T(8,128)(2,1)}, bf16[1280,256]{1,0:T(8,128)(2,1)}, u32[]{:S(2)}, u32[]{:S(2)}) collective-permute-start(bf16[1280,256]{1,0:T(8,128)(2,1)} %bitcast.32), channel_id=1, source_target_pairs={{0,64},{4,20},{8,72},{12,28},{16,80},{20,4},{24,88},{28,12},{32,96... | collective-permute-start | bytes 1966088 | tf_op jit(solution)/shard_map/ppermute | solution.py:37
  100.5 5.3 %context_product.5 = bf16[512,1280]{1,0:T(8,128)(2,1)} custom-call(s32[2]{0:T(128)S(1)} %pad_add_fusion.which, bf16[640,256]{1,0:T(8,128)(2,1)} %collective-permute-done.14.refs_0_, bf16[640,256]{1,0:T(8,128)(2,1)} %collective-permute-done.15.refs_1_, bf16[5120,1280]{1,0:T(8,128)(2,1)} %refs_3_.3, bf16[5120,1280]{1,0:T(8,128)(2,1)} %refs_3_.3, ...), custom_call_target="tpu_custom_call" | custom-call | tf_op jit(solution)/shard_map/context_product/pallas_call | solution.py:104
  105.8 7.7 %collective-permute-done.18.refs_3_ = bf16[1280,256]{1,0:T(8,128)(2,1)S(1)} collective-permute-done((bf16[1280,256]{1,0:T(8,128)(2,1)}, bf16[1280,256]{1,0:T(8,128)(2,1)S(1)}, u32[]{:S(2)}, u32[]{:S(2)}) %collective-permute-start.18) | collective-permute-done | bytes 655392 | tf_op jit(solution)/shard_map/ppermute | solution.py:37
  114.4 7.2 %all-to-all-start.2 = ((bf16[32,16,1280]{2,1,0:T(8,128)(2,1)}), bf16[32,16,1280]{2,1,0:T(8,128)(2,1)S(1)}, u32[]{:S(2)}, u32[]{:S(2)}) async-start(bf16[32,16,1280]{2,1,0:T(8,128)(2,1)} %bitcast.36), calls=%async_computation.2 | async-start | bytes 2621440 | tf_op jit(solution)/shard_map/all_to_all | solution.py:58
  122.4 8.9 %weight_product.1 = (f32[160,1280]{1,0:T(8,128)}, bf16[160,1280]{1,0:T(8,128)(2,1)}, bf16[160,1280]{1,0:T(8,128)(2,1)}, bf16[160,1280]{1,0:T(8,128)(2,1)}) custom-call(s32[4]{0:T(128)} %pad_add_fusion.3.order_ref, bf16[1280,256]{1,0:T(8,128)(2,1)} %bitcast.56, bf16[1280,256]{1,0:T(8,128)(2,1)} %collective-permute-done.19.refs_1_, ...), custom_call_target="tpu_custom_call" | custom-call | tf_op jit(solution)/shard_map/weight_product/pallas_call | solution.py:315
  131.3 2.7 %collective-permute-start.23 = (bf16[160,1280]{1,0:T(8,128)(2,1)}, bf16[160,1280]{1,0:T(8,128)(2,1)S(1)}, u32[]{:S(2)}, u32[]{:S(2)}) collective-permute-start(bf16[160,1280]{1,0:T(8,128)(2,1)} %get-tuple-element.92), channel_id=1, source_target_pairs={{0,24},{4,100},{8,0},{12,108},{16,8},{20,116},{24,16},{28,124},{32... | collective-permute-start | bytes 1228808 | tf_op jit(solution)/shard_map/ppermute | solution.py:37
  135.1 2.2 %reshape.173 = bf16[384,1280]{1,0:T(8,128)(2,1)} reshape(bf16[32,12,1280]{2,1,0:T(8,128)(2,1)} %bitcast.47) | data formatting | bytes 1966080 | tf_op jit(solution)/shard_map/reshape | solution.py:63
  137.3 5.4 %collective-permute-done.23 = bf16[160,1280]{1,0:T(8,128)(2,1)S(1)} collective-permute-done((bf16[160,1280]{1,0:T(8,128)(2,1)}, bf16[160,1280]{1,0:T(8,128)(2,1)S(1)}, u32[]{:S(2)}, u32[]{:S(2)}) %collective-permute-start.23) | collective-permute-done | bytes 409632 | tf_op jit(solution)/shard_map/ppermute | solution.py:37
  142.8 1.5 %collective-permute-done.22 = bf16[160,1280]{1,0:T(8,128)(2,1)S(1)} collective-permute-done((bf16[160,1280]{1,0:T(8,128)(2,1)}, bf16[160,1280]{1,0:T(8,128)(2,1)S(1)}, u32[]{:S(2)}, u32[]{:S(2)}) %collective-permute-start.22) | collective-permute-done | bytes 409632 | tf_op jit(solution)/shard_map/ppermute | solution.py:37
  144.3 4.4 %collective-permute-done.21 = bf16[160,1280]{1,0:T(8,128)(2,1)S(1)} collective-permute-done((bf16[160,1280]{1,0:T(8,128)(2,1)}, bf16[160,1280]{1,0:T(8,128)(2,1)S(1)}, u32[]{:S(2)}, u32[]{:S(2)}) %collective-permute-start.21) | collective-permute-done | bytes 409632 | tf_op jit(solution)/shard_map/ppermute | solution.py:37
  148.7 1.1 add_multiply_fusion
  149.7 1.1 reshape.172
  (80 shorter events, 9.3 us)
Async XLA Ops:
  3.6 11.8 %collective-permute-start.2 = (bf16[256,1280]{1,0:T(8,128)(2,1)}, bf16[256,1280]{1,0:T(8,128)(2,1)S(1)}, u32[]{:S(2)}, u32[]{:S(2)}) collective-permute-start(bf16[256,1280]{1,0:T(8,128)(2,1)} %context_ref.6), channel_id=1, source_target_pairs={{0,4},{4,0},{1,5},{5,1},{2,6},{6,2},{3,7},{7,3},{8,12},{12,8},{9,1... | collective-permute-start | bytes 1966088 | tf_op jit(solution)/shard_map/ppermute | solution.py:22
  5.1 12.6 %collective-permute-start = (bf16[640,256]{1,0:T(8,128)(2,1)S(1)}, bf16[640,256]{1,0:T(8,128)(2,1)S(1)}, u32[]{:S(2)}, u32[]{:S(2)}) collective-permute-start(bf16[640,256]{1,0:T(8,128)(2,1)S(1)} %get-tuple-element.48), channel_id=1, source_target_pairs={{0,1},{1,2},{2,3},{3,0},{4,5},{5,6},{6,7},{7,4},{8,9},{9,10},{10,1... | collective-permute-start | bytes 983048 | tf_op jit(solution)/shard_map/ppermute | solution.py:22
  6.8 10.9 %collective-permute-start.1 = (bf16[640,256]{1,0:T(8,128)(2,1)S(1)}, bf16[640,256]{1,0:T(8,128)(2,1)S(1)}, u32[]{:S(2)}, u32[]{:S(2)}) collective-permute-start(bf16[640,256]{1,0:T(8,128)(2,1)S(1)} %get-tuple-element.49), channel_id=1, source_target_pairs={{0,3},{1,0},{2,1},{3,2},{4,7},{5,4},{6,5},{7,6},{8,11},{9,8},{10,9... | collective-permute-start | bytes 983048 | tf_op jit(solution)/shard_map/ppermute | solution.py:22
  17.7 3.4 %copy-start.9 = (f32[1280]{0:T(1024)S(1)}, f32[1280]{0:T(1024)}, u32[]{:S(2)}) copy-start(f32[1280]{0:T(1024)} %param.13) | copy-start | bytes 15364
  17.7 3.4 %copy-start.11 = (f32[4]{0:T(128)S(1)}, f32[4]{0:T(128)}, u32[]{:S(2)}) copy-start(f32[4]{0:T(128)} %param.14) | copy-start | bytes 52
  17.7 3.4 %copy-start.12 = (s32[4]{0:T(128)S(1)}, s32[4]{0:T(128)}, u32[]{:S(2)}) copy-start(s32[4]{0:T(128)} %param.15) | copy-start | bytes 52
  19.5 17.8 %collective-permute-start.4 = (bf16[1280,256]{1,0:T(8,128)(2,1)}, bf16[1280,256]{1,0:T(8,128)(2,1)}, u32[]{:S(2)}, u32[]{:S(2)}) collective-permute-start(bf16[1280,256]{1,0:T(8,128)(2,1)} %get-tuple-element.56), channel_id=1, source_target_pairs={{0,3},{1,0},{2,1},{3,2},{4,7},{5,4},{6,5},{7,6},{8,11},{9,8},{10,9... | collective-permute-start | bytes 1966088 | tf_op jit(solution)/shard_map/ppermute | solution.py:22
  21.1 16.3 %collective-permute-start.3 = (bf16[1280,256]{1,0:T(8,128)(2,1)S(1)}, bf16[1280,256]{1,0:T(8,128)(2,1)}, u32[]{:S(2)}, u32[]{:S(2)}) collective-permute-start(bf16[1280,256]{1,0:T(8,128)(2,1)S(1)} %get-tuple-element.55), channel_id=1, source_target_pairs={{0,1},{1,2},{2,3},{3,0},{4,5},{5,6},{6,7},{7,4},{8,9},{9,10},{10,1... | collective-permute-start | bytes 1966088 | tf_op jit(solution)/shard_map/ppermute | solution.py:22
  21.2 26.4 %collective-permute-start.8 = (bf16[512,1280]{1,0:T(8,128)(2,1)}, bf16[512,1280]{1,0:T(8,128)(2,1)}, u32[]{:S(2)}, u32[]{:S(2)}) collective-permute-start(bf16[512,1280]{1,0:T(8,128)(2,1)} %pad_maximum_fusion.refs_4_), channel_id=1, source_target_pairs={{0,32},{4,12},{8,40},{12,20},{16,48},{20,28},{24,56},{28,4},{32,64... | collective-permute-start | bytes 3932168 | tf_op jit(solution)/shard_map/ppermute | solution.py:37
  22.5 25.1 %collective-permute-start.9 = (bf16[512,1280]{1,0:T(8,128)(2,1)}, bf16[512,1280]{1,0:T(8,128)(2,1)}, u32[]{:S(2)}, u32[]{:S(2)}) collective-permute-start(bf16[512,1280]{1,0:T(8,128)(2,1)} %pad_maximum_fusion.refs_4_), channel_id=1, source_target_pairs={{0,96},{4,28},{8,104},{12,4},{16,112},{20,12},{24,120},{28,20},{32... | collective-permute-start | bytes 3932168 | tf_op jit(solution)/shard_map/ppermute | solution.py:37
  24.0 1.1 copy-start.3
  25.1 1.1 copy-start.4
  29.7 14.8 %all-to-all-start = ((f32[32,1,8]{2,1,0:T(1,128)}), f32[32,1,8]{2,1,0:T(1,128)S(1)}, u32[]{:S(2)}, u32[]{:S(2)}) async-start(f32[32,1,8]{2,1,0:T(1,128)} %broadcast_in_dim.16), calls=%async_computation | async-start | bytes 32768 | tf_op jit(solution)/shard_map/all_to_all | solution.py:42
  37.4 7.4 %copy-start.10 = (s32[4]{0:T(128)S(1)}, s32[4]{0:T(128)}, u32[]{:S(2)}) copy-start(s32[4]{0:T(128)} %param.16) | copy-start | bytes 52
  39.0 5.9 %collective-permute-start.7 = (f32[2,256]{1,0:T(2,128)S(1)}, f32[2,256]{1,0:T(2,128)S(1)}, u32[]{:S(2)}, u32[]{:S(2)}) collective-permute-start(f32[2,256]{1,0:T(2,128)S(1)} %pad_maximum_fusion.3), channel_id=1, source_target_pairs={{0,3},{1,0},{2,1},{3,2},{4,7},{5,4},{6,5},{7,6},{8,11},{9,8},{10,9... | collective-permute-start | bytes 6152 | tf_op jit(solution)/shard_map/ppermute | solution.py:22
  42.0 4.0 %collective-permute-start.6 = (f32[2,256]{1,0:T(2,128)S(1)}, f32[2,256]{1,0:T(2,128)S(1)}, u32[]{:S(2)}, u32[]{:S(2)}) collective-permute-start(f32[2,256]{1,0:T(2,128)S(1)} %pad_maximum_fusion.3), channel_id=1, source_target_pairs={{0,2},{1,3},{2,0},{3,1},{4,6},{5,7},{6,4},{7,5},{8,10},{9,11},{10,... | collective-permute-start | bytes 6152 | tf_op jit(solution)/shard_map/ppermute | solution.py:22
  42.0 4.0 %collective-permute-start.5 = (f32[2,256]{1,0:T(2,128)S(1)}, f32[2,256]{1,0:T(2,128)S(1)}, u32[]{:S(2)}, u32[]{:S(2)}) collective-permute-start(f32[2,256]{1,0:T(2,128)S(1)} %pad_maximum_fusion.3), channel_id=1, source_target_pairs={{0,1},{1,2},{2,3},{3,0},{4,5},{5,6},{6,7},{7,4},{8,9},{9,10},{10,1... | collective-permute-start | bytes 6152 | tf_op jit(solution)/shard_map/ppermute | solution.py:22
  45.0 18.6 %collective-permute-start.13 = (bf16[512,1280]{1,0:T(8,128)(2,1)}, bf16[512,1280]{1,0:T(8,128)(2,1)}, u32[]{:S(2)}, u32[]{:S(2)}) collective-permute-start(bf16[512,1280]{1,0:T(8,128)(2,1)} %pad_maximum_fusion.refs_4_), channel_id=1, source_target_pairs={{0,64},{4,20},{8,72},{12,28},{16,80},{20,4},{24,88},{28,12},{32,96... | collective-permute-start | bytes 3932168 | tf_op jit(solution)/shard_map/ppermute | solution.py:37
  46.0 4.7 %copy-start.13 = (s32[64,1]{0,1:T(1,128)S(1)}, s32[64,1]{0,1:T(1,128)}, u32[]{:S(2)}) copy-start(s32[64,1]{0,1:T(1,128)} %param.17) | copy-start | bytes 772
  47.6 16.2 %collective-permute-start.10 = (bf16[1280,256]{1,0:T(8,128)(2,1)S(1)}, bf16[1280,256]{1,0:T(8,128)(2,1)S(1)}, u32[]{:S(2)}, u32[]{:S(2)}) collective-permute-start(bf16[1280,256]{1,0:T(8,128)(2,1)S(1)} %subtract_convert_fusion.refs_0_.grad_ref), channel_id=1, source_target_pairs={{0,1},{1,2},{2,3},{3,0},{4,5},{5,6},{6,7},{7,4},{8,9},{9,10},{10,1... | collective-permute-start | bytes 1966088 | tf_op jit(solution)/shard_map/ppermute | solution.py:22
  49.7 14.6 %collective-permute-start.11 = (bf16[1280,256]{1,0:T(8,128)(2,1)S(1)}, bf16[1280,256]{1,0:T(8,128)(2,1)S(1)}, u32[]{:S(2)}, u32[]{:S(2)}) collective-permute-start(bf16[1280,256]{1,0:T(8,128)(2,1)S(1)} %subtract_convert_fusion.refs_0_.grad_ref), channel_id=1, source_target_pairs={{0,3},{1,0},{2,1},{3,2},{4,7},{5,4},{6,5},{7,6},{8,11},{9,8},{10,9... | collective-permute-start | bytes 1966088 | tf_op jit(solution)/shard_map/ppermute | solution.py:22
  50.9 12.6 %collective-permute-start.12 = (bf16[640,256]{1,0:T(8,128)(2,1)S(1)}, bf16[640,256]{1,0:T(8,128)(2,1)S(1)}, u32[]{:S(2)}, u32[]{:S(2)}) collective-permute-start(bf16[640,256]{1,0:T(8,128)(2,1)S(1)} %bitcast.61), channel_id=1, source_target_pairs={{0,4},{4,0},{1,5},{5,1},{2,6},{6,2},{3,7},{7,3},{8,12},{12,8},{9,1... | collective-permute-start | bytes 983048 | tf_op jit(solution)/shard_map/ppermute | solution.py:22
  56.4 12.1 %copy-start = (f32[256,1280]{1,0:T(8,128)}, f32[256,1280]{1,0:T(8,128)S(1)}, u32[]{:S(2)}) copy-start(f32[256,1280]{1,0:T(8,128)S(1)} %context_product.3.refs_4_) | copy-start | bytes 3932164
  63.5 5.0 %copy-start.5 = (bf16[640,256]{1,0:T(8,128)(2,1)}, bf16[640,256]{1,0:T(8,128)(2,1)S(1)}, u32[]{:S(2)}) copy-start(bf16[640,256]{1,0:T(8,128)(2,1)S(1)} %collective-permute-done.12) | copy-start | bytes 983044
  65.0 22.1 %collective-permute-start.14 = (bf16[640,256]{1,0:T(8,128)(2,1)}, bf16[640,256]{1,0:T(8,128)(2,1)}, u32[]{:S(2)}, u32[]{:S(2)}) collective-permute-start(bf16[640,256]{1,0:T(8,128)(2,1)} %slice.32), channel_id=1, source_target_pairs={{0,1},{1,2},{2,3},{3,0},{4,5},{5,6},{6,7},{7,4},{8,9},{9,10},{10,1... | collective-permute-start | bytes 983048 | tf_op jit(solution)/shard_map/ppermute | solution.py:22
  66.0 21.1 %collective-permute-start.15 = (bf16[640,256]{1,0:T(8,128)(2,1)}, bf16[640,256]{1,0:T(8,128)(2,1)}, u32[]{:S(2)}, u32[]{:S(2)}) collective-permute-start(bf16[640,256]{1,0:T(8,128)(2,1)} %slice.33), channel_id=1, source_target_pairs={{0,3},{1,0},{2,1},{3,2},{4,7},{5,4},{6,5},{7,6},{8,11},{9,8},{10,9... | collective-permute-start | bytes 983048 | tf_op jit(solution)/shard_map/ppermute | solution.py:22
  69.4 19.5 %collective-permute-start.16 = (bf16[1280,256]{1,0:T(8,128)(2,1)}, bf16[1280,256]{1,0:T(8,128)(2,1)}, u32[]{:S(2)}, u32[]{:S(2)}) collective-permute-start(bf16[1280,256]{1,0:T(8,128)(2,1)} %bitcast.23), channel_id=1, source_target_pairs={{0,4},{4,0},{1,5},{5,1},{2,6},{6,2},{3,7},{7,3},{8,12},{12,8},{9,1... | collective-permute-start | bytes 1966088 | tf_op jit(solution)/shard_map/ppermute | solution.py:22
  74.2 31.6 %all-to-all-start.1 = ((bf16[32,16,1280]{2,1,0:T(8,128)(2,1)}), bf16[32,16,1280]{2,1,0:T(8,128)(2,1)}, u32[]{:S(2)}, u32[]{:S(2)}) async-start(bf16[32,16,1280]{2,1,0:T(8,128)(2,1)} %bitcast.35), calls=%async_computation.1 | async-start | bytes 2621440 | tf_op jit(solution)/shard_map/all_to_all | solution.py:58
  80.7 1.3 copy-start.1
  87.1 2.9 %copy-start.6 = (bf16[640,256]{1,0:T(8,128)(2,1)S(1)}, bf16[640,256]{1,0:T(8,128)(2,1)}, u32[]{:S(2)}) copy-start(bf16[640,256]{1,0:T(8,128)(2,1)} %copy-done.5) | copy-start | bytes 983044
  88.2 1.8 %collective-permute-start.17 = (bf16[640,256]{1,0:T(8,128)(2,1)S(1)}, bf16[640,256]{1,0:T(8,128)(2,1)S(1)}, u32[]{:S(2)}, u32[]{:S(2)}) collective-permute-start(bf16[640,256]{1,0:T(8,128)(2,1)S(1)} %bitcast.60), channel_id=1, source_target_pairs={{0,4},{4,0},{1,5},{5,1},{2,6},{6,2},{3,7},{7,3},{8,12},{12,8},{9,1... | collective-permute-start | bytes 983048 | tf_op jit(solution)/shard_map/ppermute | solution.py:22
  95.2 0.9 copy-start.2
  96.1 17.4 %collective-permute-start.18 = (bf16[1280,256]{1,0:T(8,128)(2,1)}, bf16[1280,256]{1,0:T(8,128)(2,1)S(1)}, u32[]{:S(2)}, u32[]{:S(2)}) collective-permute-start(bf16[1280,256]{1,0:T(8,128)(2,1)} %bitcast.33), channel_id=1, source_target_pairs={{0,96},{4,28},{8,104},{12,4},{16,112},{20,12},{24,120},{28,20},{32... | collective-permute-start | bytes 1966088 | tf_op jit(solution)/shard_map/ppermute | solution.py:37
  98.6 23.8 %collective-permute-start.19 = (bf16[1280,256]{1,0:T(8,128)(2,1)}, bf16[1280,256]{1,0:T(8,128)(2,1)}, u32[]{:S(2)}, u32[]{:S(2)}) collective-permute-start(bf16[1280,256]{1,0:T(8,128)(2,1)} %bitcast.31), channel_id=1, source_target_pairs={{0,32},{4,12},{8,40},{12,20},{16,48},{20,28},{24,56},{28,4},{32,64... | collective-permute-start | bytes 1966088 | tf_op jit(solution)/shard_map/ppermute | solution.py:37
  98.6 23.8 %collective-permute-start.20 = (bf16[1280,256]{1,0:T(8,128)(2,1)}, bf16[1280,256]{1,0:T(8,128)(2,1)}, u32[]{:S(2)}, u32[]{:S(2)}) collective-permute-start(bf16[1280,256]{1,0:T(8,128)(2,1)} %bitcast.32), channel_id=1, source_target_pairs={{0,64},{4,20},{8,72},{12,28},{16,80},{20,4},{24,88},{28,12},{32,96... | collective-permute-start | bytes 1966088 | tf_op jit(solution)/shard_map/ppermute | solution.py:37
  113.5 0.8 copy-start.8
  114.4 35.4 %all-to-all-start.2 = ((bf16[32,16,1280]{2,1,0:T(8,128)(2,1)}), bf16[32,16,1280]{2,1,0:T(8,128)(2,1)S(1)}, u32[]{:S(2)}, u32[]{:S(2)}) async-start(bf16[32,16,1280]{2,1,0:T(8,128)(2,1)} %bitcast.36), calls=%async_computation.2 | async-start | bytes 2621440 | tf_op jit(solution)/shard_map/all_to_all | solution.py:58
  131.3 17.3 %copy-start.7 = (f32[160,1280]{1,0:T(8,128)S(1)}, f32[160,1280]{1,0:T(8,128)}, u32[]{:S(2)}) copy-start(f32[160,1280]{1,0:T(8,128)} %get-tuple-element.89) | copy-start | bytes 2457604
  131.3 11.4 %collective-permute-start.23 = (bf16[160,1280]{1,0:T(8,128)(2,1)}, bf16[160,1280]{1,0:T(8,128)(2,1)S(1)}, u32[]{:S(2)}, u32[]{:S(2)}) collective-permute-start(bf16[160,1280]{1,0:T(8,128)(2,1)} %get-tuple-element.92), channel_id=1, source_target_pairs={{0,24},{4,100},{8,0},{12,108},{16,8},{20,116},{24,16},{28,124},{32... | collective-permute-start | bytes 1228808 | tf_op jit(solution)/shard_map/ppermute | solution.py:37
  134.0 10.2 %collective-permute-start.22 = (bf16[160,1280]{1,0:T(8,128)(2,1)}, bf16[160,1280]{1,0:T(8,128)(2,1)S(1)}, u32[]{:S(2)}, u32[]{:S(2)}) collective-permute-start(bf16[160,1280]{1,0:T(8,128)(2,1)} %get-tuple-element.91), channel_id=1, source_target_pairs={{0,16},{4,68},{8,24},{12,76},{16,0},{20,84},{24,8},{28,92},{32,48}... | collective-permute-start | bytes 1228808 | tf_op jit(solution)/shard_map/ppermute | solution.py:37
  134.6 14.1 %collective-permute-start.21 = (bf16[160,1280]{1,0:T(8,128)(2,1)}, bf16[160,1280]{1,0:T(8,128)(2,1)S(1)}, u32[]{:S(2)}, u32[]{:S(2)}) collective-permute-start(bf16[160,1280]{1,0:T(8,128)(2,1)} %get-tuple-element.90), channel_id=1, source_target_pairs={{0,8},{4,36},{8,16},{12,44},{16,24},{20,52},{24,0},{28,60},{32,40}... | collective-permute-start | bytes 1228808 | tf_op jit(solution)/shard_map/ppermute | solution.py:37

commit v14 on v13

--- a/solution.py
+++ b/solution.py
@@ -416,14 +416,14 @@
     placed = context_product(
         [far_left, far_right], [far_place, far_place + 1], out_proj, before=context_grad, slots=slots
     )
-    placed, d_residual, pieces[3] = lax.optimization_barrier((placed, d_residual, pieces[3]))
+    placed, d_residual = lax.optimization_barrier((placed, learner_rows(d_residual)))
     d_context = exchange(placed, lanes)
     order = [jnp.where(c == 0, (y + k) % NY, (x + k - z) % NZ) for k in range(4)]
     d_out_proj, *parts = weight_product(pieces, contexts, jnp.stack(order), block)
     parts = [cross(part, k, False) for k, part in zip((1, 2, 3), parts)]
     for part in parts:
         d_out_proj = d_out_proj + part.astype(F32)
-    return (learner_rows(d_context), learner_rows(d_residual), d_out_proj / lanes)
+    return (learner_rows(d_context), d_residual, d_out_proj / lanes)
 
 
 def solution(mesh):

time: 152 us -> 136 us (0.89)
  waiting for transfers between devices: 29 us -> 17.1 us
  starting transfers between devices: 55.4 us -> 52.5 us
  local copies, waits for them, and re-layouts: 13 us -> 11 us
    ppermute x9, waiting for transfers between devices: 26.2 us -> 12.7 us  [cross(): return lax.ppermute(value, DP, pairs)]
    all_to_all x2, starting transfers between devices: 13.6 us -> 11 us  [exchange(): return lax.all_to_all(blocks, DP, split_axis=0, concat_axis=0, tiled=True)]
    unnamed x28 -> x26, local copies, waits for them, and re-layouts: 5.24 us -> 3.24 us
  transfers between devices with their start and end apart: 27 -> 27, of which waited for: 10 -> 7; matrix products, arithmetic and copies ran while one was open for 10% -> 13% of each run, Pallas kernels for 25% -> 28%
where the time goes in v14:
time: 136 us; the launch traced here: 135 us
  starting transfers between devices  52.5 us (39%)
  Pallas kernels  43.2 us (32%)
  waiting for transfers between devices  17.1 us (13%)
  local copies, waits for them, and re-layouts  11 us (8%)
  other arithmetic  10.2 us (7%)
    ppermute x15, starting transfers between devices, shift(): lax.ppermute(value, axis, [(i, (i + step) % size) for i in range(size)])  21.1 us
    pallas_call x3, Pallas kernels, context_product(): pl.pallas_call(body, out_shape=jax.ShapeDtypeStruct((out_rows, width), dt...  13.3 us
    ppermute x9, starting transfers between devices, cross(): return lax.ppermute(value, DP, pairs)  13 us
    ppermute x9, waiting for transfers between devices, cross(): return lax.ppermute(value, DP, pairs)  12.7 us
    all_to_all x2, starting transfers between devices, exchange(): return lax.all_to_all(blocks, DP, split_axis=0, concat_axis=0, tiled=True)  11 us
    pallas_call x3, Pallas kernels, forward_product(): pl.pallas_call(body, out_shape=[jax.ShapeDtypeStruct((tile, rows), BF16)]...  9.41 us
    pallas_call x1, Pallas kernels, weight_product(): pl.pallas_call(body, out_shape=[jax.ShapeDtypeStruct((block, width), BF16...  8.92 us
    all_to_all x1, starting transfers between devices, all_shares(): return lax.all_to_all(copies, DP, split_axis=0, concat_axis=0, tiled=True)  7.31 us
  transfers between devices with their start and end apart: 27, of which 7 were waited for; matrix products, arithmetic and copies ran while one was open for 13% of the time, Pallas kernels for 28%

profile of v14, /device:TPU:1, one launch (start us, length us, event | category | flops | bytes accessed | tf_op | source)
XLA Modules:
  0.0 135.1 jit_solution(82923954879287062)
XLA Ops:
  0.6 2.9 %forward_product.3 = (bf16[640,256]{1,0:T(8,128)(2,1)S(1)}, bf16[640,256]{1,0:T(8,128)(2,1)S(1)}) custom-call(s32[1]{0:T(128)} %bitcast.3.which, bf16[5120,1280]{1,0:T(8,128)(2,1)} %refs_3_.3, bf16[256,1280]{1,0:T(8,128)(2,1)} %context_ref.6), custom_call_target="tpu_custom_call" | custom-call | tf_op jit(solution)/shard_map/forward_product/pallas_call | solution.py:175
  3.6 1.5 %collective-permute-start.2 = (bf16[256,1280]{1,0:T(8,128)(2,1)}, bf16[256,1280]{1,0:T(8,128)(2,1)S(1)}, u32[]{:S(2)}, u32[]{:S(2)}) collective-permute-start(bf16[256,1280]{1,0:T(8,128)(2,1)} %context_ref.6), channel_id=1, source_target_pairs={{0,4},{4,0},{1,5},{5,1},{2,6},{6,2},{3,7},{7,3},{8,12},{12,8},{9,1... | collective-permute-start | bytes 1966088 | tf_op jit(solution)/shard_map/ppermute | solution.py:22
  5.1 1.8 %collective-permute-start = (bf16[640,256]{1,0:T(8,128)(2,1)S(1)}, bf16[640,256]{1,0:T(8,128)(2,1)S(1)}, u32[]{:S(2)}, u32[]{:S(2)}) collective-permute-start(bf16[640,256]{1,0:T(8,128)(2,1)S(1)} %get-tuple-element.47), channel_id=1, source_target_pairs={{0,1},{1,2},{2,3},{3,0},{4,5},{5,6},{6,7},{7,4},{8,9},{9,10},{10,1... | collective-permute-start | bytes 983048 | tf_op jit(solution)/shard_map/ppermute | solution.py:22
  6.8 2.1 %collective-permute-start.1 = (bf16[640,256]{1,0:T(8,128)(2,1)S(1)}, bf16[640,256]{1,0:T(8,128)(2,1)S(1)}, u32[]{:S(2)}, u32[]{:S(2)}) collective-permute-start(bf16[640,256]{1,0:T(8,128)(2,1)S(1)} %get-tuple-element.48), channel_id=1, source_target_pairs={{0,3},{1,0},{2,1},{3,2},{4,7},{5,4},{6,5},{7,6},{8,11},{9,8},{10,9... | collective-permute-start | bytes 983048 | tf_op jit(solution)/shard_map/ppermute | solution.py:22
  8.9 2.9 %forward_product.4.refs_0_ = bf16[1280,256]{1,0:T(8,128)(2,1)S(1)} custom-call(s32[1]{0:T(128)} %bitcast.4.which, bf16[5120,1280]{1,0:T(8,128)(2,1)} %refs_3_.3, bf16[256,1280]{1,0:T(8,128)(2,1)} %context_ref.6), custom_call_target="tpu_custom_call" | custom-call | tf_op jit(solution)/shard_map/forward_product/pallas_call | solution.py:175
  11.8 3.6 %forward_product.5.refs_2_ = bf16[1280,256]{1,0:T(8,128)(2,1)} custom-call(s32[1]{0:T(128)} %bitcast.5.which, bf16[5120,1280]{1,0:T(8,128)(2,1)} %refs_3_.3, bf16[256,1280]{1,0:T(8,128)(2,1)} %context_ref.6), custom_call_target="tpu_custom_call" | custom-call | tf_op jit(solution)/shard_map/forward_product/pallas_call | solution.py:175
  15.4 2.3 %pad_maximum_fusion.refs_4_ = bf16[512,1280]{1,0:T(8,128)(2,1)} fusion(bf16[256,1280]{1,0:T(8,128)(2,1)S(1)} %collective-permute-done.2, bf16[256,1280]{1,0:T(8,128)(2,1)} %context_ref.6), kind=kLoop, calls=%fused_computation | loop fusion | flops 2621440 | bytes 2621440 | tf_op jit(solution)/shard_map/concatenate | solution.py:343
  17.7 1.9 %top_up.1 = (bf16[1280,256]{1,0:T(8,128)(2,1)S(1)}, bf16[1280,256]{1,0:T(8,128)(2,1)}) custom-call(bf16[1280,256]{1,0:T(8,128)(2,1)S(1)} %forward_product.4.refs_0_, bf16[640,256]{1,0:T(8,128)(2,1)S(1)} %collective-permute-done.refs_1_, bf16[1280,256]{1,0:T(8,128)(2,1)} %forward_product.5.refs_2_, ...), custom_call_target="tpu_custom_call", output_to_operand_aliasing={{0}: (0, {}), {1}: (2, {})} | custom-call | tf_op jit(solution)/shard_map/top_up/pallas_call | solution.py:144
  19.6 2.7 %collective-permute-start.4 = (bf16[1280,256]{1,0:T(8,128)(2,1)}, bf16[1280,256]{1,0:T(8,128)(2,1)}, u32[]{:S(2)}, u32[]{:S(2)}) collective-permute-start(bf16[1280,256]{1,0:T(8,128)(2,1)} %get-tuple-element.55), channel_id=1, source_target_pairs={{0,3},{1,0},{2,1},{3,2},{4,7},{5,4},{6,5},{7,6},{8,11},{9,8},{10,9... | collective-permute-start | bytes 1966088 | tf_op jit(solution)/shard_map/ppermute | solution.py:22
  22.6 1.3 collective-permute-start.8
  23.9 1.5 %collective-permute-start.9 = (bf16[512,1280]{1,0:T(8,128)(2,1)}, bf16[512,1280]{1,0:T(8,128)(2,1)}, u32[]{:S(2)}, u32[]{:S(2)}) collective-permute-start(bf16[512,1280]{1,0:T(8,128)(2,1)} %pad_maximum_fusion.refs_4_), channel_id=1, source_target_pairs={{0,96},{4,28},{8,104},{12,4},{16,112},{20,12},{24,120},{28,20},{32... | collective-permute-start | bytes 3932168 | tf_op jit(solution)/shard_map/ppermute | solution.py:37
  25.4 2.9 %hidden_part.1 = (f32[1280,256]{1,0:T(8,128)S(1)}, f32[1280,256]{1,0:T(8,128)S(1)}) custom-call(s32[1]{0:T(128)} %bitcast.2.which, bf16[5120,1280]{1,0:T(8,128)(2,1)} %refs_3_.3, bf16[256,1280]{1,0:T(8,128)(2,1)} %context_ref.6, bf16[256,1280]{1,0:T(8,128)(2,1)S(1)} %copy-done.3, bf16[256,1280]{1,0:T(8,128)(2,1)S(1)} %copy-done.4, ...), custom_call_target="tpu_custom_call" | custom-call | tf_op jit(solution)/shard_map/hidden_part/pallas_call | solution.py:210
  29.0 7.3 %all-to-all-start = ((f32[32,1,8]{2,1,0:T(1,128)}), f32[32,1,8]{2,1,0:T(1,128)S(1)}, u32[]{:S(2)}, u32[]{:S(2)}) async-start(f32[32,1,8]{2,1,0:T(1,128)} %broadcast_in_dim.16), calls=%async_computation | async-start | bytes 32768 | tf_op jit(solution)/shard_map/all_to_all | solution.py:42
  36.8 1.7 %multiply_reduce_fusion.1 = (f32[256]{0:T(256)S(1)}, f32[256]{0:T(256)S(1)}) fusion(bf16[1280,256]{1,0:T(8,128)(2,1)} %collective-permute-done.4, f32[1280,256]{1,0:T(8,128)S(1)} %get-tuple-element.57, bf16[1280,256]{1,0:T(8,128)(2,1)} %collective-permute-done.3, f32[1280,256]{1,0:T(8,128)S(1)} %get-tuple-element.58), kind=kLoop, calls=%fused_computation.3 | loop fusion | flops 2620928 | bytes 3934208 | tf_op jit(solution)/shard_map/reduce_sum | solution.py:359
  38.6 3.7 %collective-permute-start.6 = (f32[2,256]{1,0:T(2,128)S(1)}, f32[2,256]{1,0:T(2,128)S(1)}, u32[]{:S(2)}, u32[]{:S(2)}) collective-permute-start(f32[2,256]{1,0:T(2,128)S(1)} %pad_maximum_fusion.3), channel_id=1, source_target_pairs={{0,2},{1,3},{2,0},{3,1},{4,6},{5,7},{6,4},{7,5},{8,10},{9,11},{10,... | collective-permute-start | bytes 6152 | tf_op jit(solution)/shard_map/ppermute | solution.py:22
  42.3 3.4 %all-to-all-done = f32[32,1,8]{2,1,0:T(1,128)S(1)} async-done(((f32[32,1,8]{2,1,0:T(1,128)}), f32[32,1,8]{2,1,0:T(1,128)S(1)}, u32[]{:S(2)}, u32[]{:S(2)}) %all-to-all-start) | async-done | bytes 1056 | tf_op jit(solution)/shard_map/all_to_all | solution.py:42
  46.1 1.0 collective-permute-start.13
  47.1 1.6 %subtract_convert_fusion.refs_0_.grad_ref = bf16[1280,256]{1,0:T(8,128)(2,1)S(1)} fusion(f32[1280,256]{1,0:T(8,128)S(1)} %get-tuple-element.58, f32[256]{0:T(256)S(1)} %bitcast.68, f32[256]{0:T(256)S(1)} %bitcast.67, bf16[1280,256]{1,0:T(8,128)(2,1)} %collective-permute-done.4, f32[1280,256]{1,0:T(8,128)S(1)} %get-tuple-element.57, ...), kind=kLoop, calls=%fused_computation.1 | loop fusion | flops 2621440 | bytes 4589568 | tf_op jit(solution)/shard_map/convert_element_type | solution.py:375
  48.9 2.7 %collective-permute-start.11 = (bf16[1280,256]{1,0:T(8,128)(2,1)S(1)}, bf16[1280,256]{1,0:T(8,128)(2,1)S(1)}, u32[]{:S(2)}, u32[]{:S(2)}) collective-permute-start(bf16[1280,256]{1,0:T(8,128)(2,1)S(1)} %subtract_convert_fusion.refs_0_.grad_ref), channel_id=1, source_target_pairs={{0,3},{1,0},{2,1},{3,2},{4,7},{5,4},{6,5},{7,6},{8,11},{9,8},{10,9... | collective-permute-start | bytes 1966088 | tf_op jit(solution)/shard_map/ppermute | solution.py:22
  51.5 2.3 %collective-permute-start.12 = (bf16[640,256]{1,0:T(8,128)(2,1)S(1)}, bf16[640,256]{1,0:T(8,128)(2,1)S(1)}, u32[]{:S(2)}, u32[]{:S(2)}) collective-permute-start(bf16[640,256]{1,0:T(8,128)(2,1)S(1)} %bitcast.61), channel_id=1, source_target_pairs={{0,4},{4,0},{1,5},{5,1},{2,6},{6,2},{3,7},{7,3},{8,12},{12,8},{9,1... | collective-permute-start | bytes 983048 | tf_op jit(solution)/shard_map/ppermute | solution.py:22
  54.2 3.0 %context_product.3.refs_4_ = f32[256,1280]{1,0:T(8,128)S(1)} custom-call(s32[1]{0:T(128)} %bitcast.2.which, bf16[1280,256]{1,0:T(8,128)(2,1)S(1)} %subtract_convert_fusion.refs_0_.grad_ref, bf16[5120,1280]{1,0:T(8,128)(2,1)} %refs_3_.3), custom_call_target="tpu_custom_call" | custom-call | tf_op jit(solution)/shard_map/context_product/pallas_call | solution.py:104
  57.1 1.1 copy-done
  58.2 1.6 %place_rows.1 = bf16[512,1280]{1,0:T(8,128)(2,1)} custom-call(bf16[512,256]{1,0:T(8,128)(2,1)S(1)} %fusion.refs_5_.slots_ref, bf16[1280,256]{1,0:T(8,128)(2,1)S(1)} %subtract_convert_fusion.refs_0_.grad_ref), custom_call_target="tpu_custom_call" | custom-call | tf_op jit(solution)/shard_map/place_rows/pallas_call | solution.py:125
  59.8 6.5 %all-to-all-start.1 = ((bf16[32,16,1280]{2,1,0:T(8,128)(2,1)}), bf16[32,16,1280]{2,1,0:T(8,128)(2,1)}, u32[]{:S(2)}, u32[]{:S(2)}) async-start(bf16[32,16,1280]{2,1,0:T(8,128)(2,1)} %bitcast.35), calls=%async_computation.1 | async-start | bytes 2621440 | tf_op jit(solution)/shard_map/all_to_all | solution.py:58
  67.8 2.7 %collective-permute-start.15 = (bf16[640,256]{1,0:T(8,128)(2,1)}, bf16[640,256]{1,0:T(8,128)(2,1)}, u32[]{:S(2)}, u32[]{:S(2)}) collective-permute-start(bf16[640,256]{1,0:T(8,128)(2,1)} %slice.33), channel_id=1, source_target_pairs={{0,3},{1,0},{2,1},{3,2},{4,7},{5,4},{6,5},{7,6},{8,11},{9,8},{10,9... | collective-permute-start | bytes 983048 | tf_op jit(solution)/shard_map/ppermute | solution.py:22
  70.5 0.9 pad_maximum_fusion.1
  71.4 1.5 %collective-permute-start.16 = (bf16[1280,256]{1,0:T(8,128)(2,1)}, bf16[1280,256]{1,0:T(8,128)(2,1)}, u32[]{:S(2)}, u32[]{:S(2)}) collective-permute-start(bf16[1280,256]{1,0:T(8,128)(2,1)} %bitcast.23), channel_id=1, source_target_pairs={{0,4},{4,0},{1,5},{5,1},{2,6},{6,2},{3,7},{7,3},{8,12},{12,8},{9,1... | collective-permute-start | bytes 1966088 | tf_op jit(solution)/shard_map/ppermute | solution.py:22
  73.0 1.3 copy-done.1
  74.3 5.1 %context_product.4.refs_4_ = f32[256,1280]{1,0:T(8,128)S(1)} custom-call(s32[2]{0:T(128)S(1)} %pad_add_fusion.1.which, bf16[1280,256]{1,0:T(8,128)(2,1)S(1)} %collective-permute-done.11.refs_0_, bf16[1280,256]{1,0:T(8,128)(2,1)S(1)} %collective-permute-done.10.refs_1_, bf16[5120,1280]{1,0:T(8,128)(2,1)} %refs_3_.3, bf16[5120,1280]{1,0:T(8,128)(2,1)} %refs_3_.3, ...), custom_call_target="tpu_custom_call" | custom-call | tf_op jit(solution)/shard_map/context_product/pallas_call | solution.py:104
  79.4 1.1 dynamic-slice_bitcast_fusion.2
  80.7 1.1 fusion.8
  82.2 5.2 %lay_out.1 = (bf16[8,160,256]{2,1,0:T(8,128)(2,1)S(1)}, bf16[8,160,256]{2,1,0:T(8,128)(2,1)}, bf16[8,160,256]{2,1,0:T(8,128)(2,1)}, bf16[8,160,256]{2,1,0:T(8,128)(2,1)}) custom-call(s32[4]{0:T(128)S(1)} %pad_add_fusion.2.where, bf16[4,2,160,256]{3,2,1,0:T(8,128)(2,1)S(1)} %bitcast.49, bf16[4,2,160,256]{3,2,1,0:T(8,128)(2,1)S(1)} %bitcast.53, ...), custom_call_target="tpu_custom_call" | custom-call | tf_op jit(solution)/shard_map/lay_out/pallas_call | solution.py:278
  87.4 0.8 copy-done.2
  88.3 0.8 collective-permute-start.18
  89.1 2.4 %collective-permute-start.19 = (bf16[1280,256]{1,0:T(8,128)(2,1)}, bf16[1280,256]{1,0:T(8,128)(2,1)}, u32[]{:S(2)}, u32[]{:S(2)}) collective-permute-start(bf16[1280,256]{1,0:T(8,128)(2,1)} %bitcast.32), channel_id=1, source_target_pairs={{0,64},{4,20},{8,72},{12,28},{16,80},{20,4},{24,88},{28,12},{32,96... | collective-permute-start | bytes 1966088 | tf_op jit(solution)/shard_map/ppermute | solution.py:37
  91.5 1.2 collective-permute-start.20
  92.8 5.3 %context_product.5 = bf16[512,1280]{1,0:T(8,128)(2,1)} custom-call(s32[2]{0:T(128)S(1)} %pad_add_fusion.which, bf16[640,256]{1,0:T(8,128)(2,1)} %collective-permute-done.14.refs_0_, bf16[640,256]{1,0:T(8,128)(2,1)} %collective-permute-done.15.refs_1_, bf16[5120,1280]{1,0:T(8,128)(2,1)} %refs_3_.3, bf16[5120,1280]{1,0:T(8,128)(2,1)} %refs_3_.3, ...), custom_call_target="tpu_custom_call" | custom-call | tf_op jit(solution)/shard_map/context_product/pallas_call | solution.py:104
  98.1 2.2 %reshape.171 = bf16[384,1280]{1,0:T(8,128)(2,1)} reshape(bf16[32,12,1280]{2,1,0:T(8,128)(2,1)} %bitcast.46) | data formatting | bytes 1966080 | tf_op jit(solution)/shard_map/reshape | solution.py:63
  100.2 4.5 %all-to-all-start.2 = ((bf16[32,16,1280]{2,1,0:T(8,128)(2,1)}), bf16[32,16,1280]{2,1,0:T(8,128)(2,1)S(1)}, u32[]{:S(2)}, u32[]{:S(2)}) async-start(bf16[32,16,1280]{2,1,0:T(8,128)(2,1)} %bitcast.36), calls=%async_computation.2 | async-start | bytes 2621440 | tf_op jit(solution)/shard_map/all_to_all | solution.py:58
  105.5 1.3 collective-permute-done.19.refs_2_
  106.9 8.9 %weight_product.1 = (f32[160,1280]{1,0:T(8,128)}, bf16[160,1280]{1,0:T(8,128)(2,1)}, bf16[160,1280]{1,0:T(8,128)(2,1)}, bf16[160,1280]{1,0:T(8,128)(2,1)}) custom-call(s32[4]{0:T(128)} %pad_add_fusion.3.order_ref, bf16[1280,256]{1,0:T(8,128)(2,1)} %bitcast.56, bf16[1280,256]{1,0:T(8,128)(2,1)} %copy-done.7, ...), custom_call_target="tpu_custom_call" | custom-call | tf_op jit(solution)/shard_map/weight_product/pallas_call | solution.py:315
  115.8 1.2 collective-permute-start.21
  117.0 2.5 %collective-permute-start.22 = (bf16[160,1280]{1,0:T(8,128)(2,1)}, bf16[160,1280]{1,0:T(8,128)(2,1)S(1)}, u32[]{:S(2)}, u32[]{:S(2)}) collective-permute-start(bf16[160,1280]{1,0:T(8,128)(2,1)} %get-tuple-element.89), channel_id=1, source_target_pairs={{0,16},{4,68},{8,24},{12,76},{16,0},{20,84},{24,8},{28,92},{32,48}... | collective-permute-start | bytes 1228808 | tf_op jit(solution)/shard_map/ppermute | solution.py:37
  119.5 1.1 collective-permute-start.23
  120.6 6.6 %collective-permute-done.21 = bf16[160,1280]{1,0:T(8,128)(2,1)S(1)} collective-permute-done((bf16[160,1280]{1,0:T(8,128)(2,1)}, bf16[160,1280]{1,0:T(8,128)(2,1)S(1)}, u32[]{:S(2)}, u32[]{:S(2)}) %collective-permute-start.21) | collective-permute-done | bytes 409632 | tf_op jit(solution)/shard_map/ppermute | solution.py:37
  127.2 4.6 %collective-permute-done.22 = bf16[160,1280]{1,0:T(8,128)(2,1)S(1)} collective-permute-done((bf16[160,1280]{1,0:T(8,128)(2,1)}, bf16[160,1280]{1,0:T(8,128)(2,1)S(1)}, u32[]{:S(2)}, u32[]{:S(2)}) %collective-permute-start.22) | collective-permute-done | bytes 409632 | tf_op jit(solution)/shard_map/ppermute | solution.py:37
  131.9 2.2 %add_multiply_fusion = f32[160,1280]{1,0:T(8,128)} fusion(bf16[160,1280]{1,0:T(8,128)(2,1)S(1)} %collective-permute-done.23, bf16[160,1280]{1,0:T(8,128)(2,1)S(1)} %collective-permute-done.22, f32[160,1280]{1,0:T(8,128)} %get-tuple-element.87, bf16[160,1280]{1,0:T(8,128)(2,1)S(1)} %collective-permute-done.21), kind=kLoop, calls=%fused_computation.5 | loop fusion | flops 1433600 | bytes 2867200 | tf_op jit(solution)/shard_map/div | solution.py:426
  134.1 1.1 reshape.173
  (78 shorter events, 5.3 us)
Async XLA Ops:
  3.6 11.8 %collective-permute-start.2 = (bf16[256,1280]{1,0:T(8,128)(2,1)}, bf16[256,1280]{1,0:T(8,128)(2,1)S(1)}, u32[]{:S(2)}, u32[]{:S(2)}) collective-permute-start(bf16[256,1280]{1,0:T(8,128)(2,1)} %context_ref.6), channel_id=1, source_target_pairs={{0,4},{4,0},{1,5},{5,1},{2,6},{6,2},{3,7},{7,3},{8,12},{12,8},{9,1... | collective-permute-start | bytes 1966088 | tf_op jit(solution)/shard_map/ppermute | solution.py:22
  5.1 12.6 %collective-permute-start = (bf16[640,256]{1,0:T(8,128)(2,1)S(1)}, bf16[640,256]{1,0:T(8,128)(2,1)S(1)}, u32[]{:S(2)}, u32[]{:S(2)}) collective-permute-start(bf16[640,256]{1,0:T(8,128)(2,1)S(1)} %get-tuple-element.47), channel_id=1, source_target_pairs={{0,1},{1,2},{2,3},{3,0},{4,5},{5,6},{6,7},{7,4},{8,9},{9,10},{10,1... | collective-permute-start | bytes 983048 | tf_op jit(solution)/shard_map/ppermute | solution.py:22
  6.8 10.9 %collective-permute-start.1 = (bf16[640,256]{1,0:T(8,128)(2,1)S(1)}, bf16[640,256]{1,0:T(8,128)(2,1)S(1)}, u32[]{:S(2)}, u32[]{:S(2)}) collective-permute-start(bf16[640,256]{1,0:T(8,128)(2,1)S(1)} %get-tuple-element.48), channel_id=1, source_target_pairs={{0,3},{1,0},{2,1},{3,2},{4,7},{5,4},{6,5},{7,6},{8,11},{9,8},{10,9... | collective-permute-start | bytes 983048 | tf_op jit(solution)/shard_map/ppermute | solution.py:22
  17.7 4.6 %copy-start.8 = (f32[1280]{0:T(1024)S(1)}, f32[1280]{0:T(1024)}, u32[]{:S(2)}) copy-start(f32[1280]{0:T(1024)} %param.13) | copy-start | bytes 15364
  17.7 4.6 %copy-start.12 = (s32[64,1]{0,1:T(1,128)S(1)}, s32[64,1]{0,1:T(1,128)}, u32[]{:S(2)}) copy-start(s32[64,1]{0,1:T(1,128)} %param.17) | copy-start | bytes 772
  17.7 4.8 %copy-start.10 = (f32[4]{0:T(128)S(1)}, f32[4]{0:T(128)}, u32[]{:S(2)}) copy-start(f32[4]{0:T(128)} %param.14) | copy-start | bytes 52
  17.7 4.8 %copy-start.11 = (s32[4]{0:T(128)S(1)}, s32[4]{0:T(128)}, u32[]{:S(2)}) copy-start(s32[4]{0:T(128)} %param.15) | copy-start | bytes 52
  17.7 7.7 %copy-start.3 = (bf16[256,1280]{1,0:T(8,128)(2,1)S(1)}, bf16[256,1280]{1,0:T(8,128)(2,1)}, u32[]{:S(2)}) copy-start(bf16[256,1280]{1,0:T(8,128)(2,1)} %residual_ref.1) | copy-start | bytes 1966084
  17.7 7.7 %copy-start.4 = (bf16[256,1280]{1,0:T(8,128)(2,1)S(1)}, bf16[256,1280]{1,0:T(8,128)(2,1)}, u32[]{:S(2)}) copy-start(bf16[256,1280]{1,0:T(8,128)(2,1)} %cotangent_ref.1) | copy-start | bytes 1966084
  19.6 17.2 %collective-permute-start.3 = (bf16[1280,256]{1,0:T(8,128)(2,1)S(1)}, bf16[1280,256]{1,0:T(8,128)(2,1)}, u32[]{:S(2)}, u32[]{:S(2)}) collective-permute-start(bf16[1280,256]{1,0:T(8,128)(2,1)S(1)} %get-tuple-element.54), channel_id=1, source_target_pairs={{0,1},{1,2},{2,3},{3,0},{4,5},{5,6},{6,7},{7,4},{8,9},{9,10},{10,1... | collective-permute-start | bytes 1966088 | tf_op jit(solution)/shard_map/ppermute | solution.py:22
  19.6 17.2 %collective-permute-start.4 = (bf16[1280,256]{1,0:T(8,128)(2,1)}, bf16[1280,256]{1,0:T(8,128)(2,1)}, u32[]{:S(2)}, u32[]{:S(2)}) collective-permute-start(bf16[1280,256]{1,0:T(8,128)(2,1)} %get-tuple-element.55), channel_id=1, source_target_pairs={{0,3},{1,0},{2,1},{3,2},{4,7},{5,4},{6,5},{7,6},{8,11},{9,8},{10,9... | collective-permute-start | bytes 1966088 | tf_op jit(solution)/shard_map/ppermute | solution.py:22
  22.6 26.2 %collective-permute-start.8 = (bf16[512,1280]{1,0:T(8,128)(2,1)}, bf16[512,1280]{1,0:T(8,128)(2,1)}, u32[]{:S(2)}, u32[]{:S(2)}) collective-permute-start(bf16[512,1280]{1,0:T(8,128)(2,1)} %pad_maximum_fusion.refs_4_), channel_id=1, source_target_pairs={{0,32},{4,12},{8,40},{12,20},{16,48},{20,28},{24,56},{28,4},{32,64... | collective-permute-start | bytes 3932168 | tf_op jit(solution)/shard_map/ppermute | solution.py:37
  23.9 24.9 %collective-permute-start.9 = (bf16[512,1280]{1,0:T(8,128)(2,1)}, bf16[512,1280]{1,0:T(8,128)(2,1)}, u32[]{:S(2)}, u32[]{:S(2)}) collective-permute-start(bf16[512,1280]{1,0:T(8,128)(2,1)} %pad_maximum_fusion.refs_4_), channel_id=1, source_target_pairs={{0,96},{4,28},{8,104},{12,4},{16,112},{20,12},{24,120},{28,20},{32... | collective-permute-start | bytes 3932168 | tf_op jit(solution)/shard_map/ppermute | solution.py:37
  29.0 16.8 %all-to-all-start = ((f32[32,1,8]{2,1,0:T(1,128)}), f32[32,1,8]{2,1,0:T(1,128)S(1)}, u32[]{:S(2)}, u32[]{:S(2)}) async-start(f32[32,1,8]{2,1,0:T(1,128)} %broadcast_in_dim.16), calls=%async_computation | async-start | bytes 32768 | tf_op jit(solution)/shard_map/all_to_all | solution.py:42
  36.8 9.1 %copy-start.9 = (s32[4]{0:T(128)S(1)}, s32[4]{0:T(128)}, u32[]{:S(2)}) copy-start(s32[4]{0:T(128)} %param.16) | copy-start | bytes 52
  38.5 7.6 %collective-permute-start.5 = (f32[2,256]{1,0:T(2,128)S(1)}, f32[2,256]{1,0:T(2,128)S(1)}, u32[]{:S(2)}, u32[]{:S(2)}) collective-permute-start(f32[2,256]{1,0:T(2,128)S(1)} %pad_maximum_fusion.3), channel_id=1, source_target_pairs={{0,1},{1,2},{2,3},{3,0},{4,5},{5,6},{6,7},{7,4},{8,9},{9,10},{10,1... | collective-permute-start | bytes 6152 | tf_op jit(solution)/shard_map/ppermute | solution.py:22
  38.6 8.5 %collective-permute-start.6 = (f32[2,256]{1,0:T(2,128)S(1)}, f32[2,256]{1,0:T(2,128)S(1)}, u32[]{:S(2)}, u32[]{:S(2)}) collective-permute-start(f32[2,256]{1,0:T(2,128)S(1)} %pad_maximum_fusion.3), channel_id=1, source_target_pairs={{0,2},{1,3},{2,0},{3,1},{4,6},{5,7},{6,4},{7,5},{8,10},{9,11},{10,... | collective-permute-start | bytes 6152 | tf_op jit(solution)/shard_map/ppermute | solution.py:22
  42.3 4.8 %collective-permute-start.7 = (f32[2,256]{1,0:T(2,128)S(1)}, f32[2,256]{1,0:T(2,128)S(1)}, u32[]{:S(2)}, u32[]{:S(2)}) collective-permute-start(f32[2,256]{1,0:T(2,128)S(1)} %pad_maximum_fusion.3), channel_id=1, source_target_pairs={{0,3},{1,0},{2,1},{3,2},{4,7},{5,4},{6,5},{7,6},{8,11},{9,8},{10,9... | collective-permute-start | bytes 6152 | tf_op jit(solution)/shard_map/ppermute | solution.py:22
  46.1 20.2 %collective-permute-start.13 = (bf16[512,1280]{1,0:T(8,128)(2,1)}, bf16[512,1280]{1,0:T(8,128)(2,1)}, u32[]{:S(2)}, u32[]{:S(2)}) collective-permute-start(bf16[512,1280]{1,0:T(8,128)(2,1)} %pad_maximum_fusion.refs_4_), channel_id=1, source_target_pairs={{0,64},{4,20},{8,72},{12,28},{16,80},{20,4},{24,88},{28,12},{32,96... | collective-permute-start | bytes 3932168 | tf_op jit(solution)/shard_map/ppermute | solution.py:37
  48.8 17.5 %collective-permute-start.10 = (bf16[1280,256]{1,0:T(8,128)(2,1)S(1)}, bf16[1280,256]{1,0:T(8,128)(2,1)S(1)}, u32[]{:S(2)}, u32[]{:S(2)}) collective-permute-start(bf16[1280,256]{1,0:T(8,128)(2,1)S(1)} %subtract_convert_fusion.refs_0_.grad_ref), channel_id=1, source_target_pairs={{0,1},{1,2},{2,3},{3,0},{4,5},{5,6},{6,7},{7,4},{8,9},{9,10},{10,1... | collective-permute-start | bytes 1966088 | tf_op jit(solution)/shard_map/ppermute | solution.py:22
  48.9 17.4 %collective-permute-start.11 = (bf16[1280,256]{1,0:T(8,128)(2,1)S(1)}, bf16[1280,256]{1,0:T(8,128)(2,1)S(1)}, u32[]{:S(2)}, u32[]{:S(2)}) collective-permute-start(bf16[1280,256]{1,0:T(8,128)(2,1)S(1)} %subtract_convert_fusion.refs_0_.grad_ref), channel_id=1, source_target_pairs={{0,3},{1,0},{2,1},{3,2},{4,7},{5,4},{6,5},{7,6},{8,11},{9,8},{10,9... | collective-permute-start | bytes 1966088 | tf_op jit(solution)/shard_map/ppermute | solution.py:22
  51.5 6.6 %collective-permute-start.12 = (bf16[640,256]{1,0:T(8,128)(2,1)S(1)}, bf16[640,256]{1,0:T(8,128)(2,1)S(1)}, u32[]{:S(2)}, u32[]{:S(2)}) collective-permute-start(bf16[640,256]{1,0:T(8,128)(2,1)S(1)} %bitcast.61), channel_id=1, source_target_pairs={{0,4},{4,0},{1,5},{5,1},{2,6},{6,2},{3,7},{7,3},{8,12},{12,8},{9,1... | collective-permute-start | bytes 983048 | tf_op jit(solution)/shard_map/ppermute | solution.py:22
  57.1 1.1 copy-start
  58.2 1.6 %copy-start.5 = (bf16[640,256]{1,0:T(8,128)(2,1)}, bf16[640,256]{1,0:T(8,128)(2,1)S(1)}, u32[]{:S(2)}) copy-start(bf16[640,256]{1,0:T(8,128)(2,1)S(1)} %collective-permute-done.12) | copy-start | bytes 983044
  59.8 38.3 %all-to-all-start.1 = ((bf16[32,16,1280]{2,1,0:T(8,128)(2,1)}), bf16[32,16,1280]{2,1,0:T(8,128)(2,1)}, u32[]{:S(2)}, u32[]{:S(2)}) async-start(bf16[32,16,1280]{2,1,0:T(8,128)(2,1)} %bitcast.35), calls=%async_computation.1 | async-start | bytes 2621440 | tf_op jit(solution)/shard_map/all_to_all | solution.py:58
  67.0 12.3 %collective-permute-start.14 = (bf16[640,256]{1,0:T(8,128)(2,1)}, bf16[640,256]{1,0:T(8,128)(2,1)}, u32[]{:S(2)}, u32[]{:S(2)}) collective-permute-start(bf16[640,256]{1,0:T(8,128)(2,1)} %slice.32), channel_id=1, source_target_pairs={{0,1},{1,2},{2,3},{3,0},{4,5},{5,6},{6,7},{7,4},{8,9},{9,10},{10,1... | collective-permute-start | bytes 983048 | tf_op jit(solution)/shard_map/ppermute | solution.py:22
  67.8 11.6 %collective-permute-start.15 = (bf16[640,256]{1,0:T(8,128)(2,1)}, bf16[640,256]{1,0:T(8,128)(2,1)}, u32[]{:S(2)}, u32[]{:S(2)}) collective-permute-start(bf16[640,256]{1,0:T(8,128)(2,1)} %slice.33), channel_id=1, source_target_pairs={{0,3},{1,0},{2,1},{3,2},{4,7},{5,4},{6,5},{7,6},{8,11},{9,8},{10,9... | collective-permute-start | bytes 983048 | tf_op jit(solution)/shard_map/ppermute | solution.py:22
  71.4 9.2 %collective-permute-start.16 = (bf16[1280,256]{1,0:T(8,128)(2,1)}, bf16[1280,256]{1,0:T(8,128)(2,1)}, u32[]{:S(2)}, u32[]{:S(2)}) collective-permute-start(bf16[1280,256]{1,0:T(8,128)(2,1)} %bitcast.23), channel_id=1, source_target_pairs={{0,4},{4,0},{1,5},{5,1},{2,6},{6,2},{3,7},{7,3},{8,12},{12,8},{9,1... | collective-permute-start | bytes 1966088 | tf_op jit(solution)/shard_map/ppermute | solution.py:22
  73.0 1.3 copy-start.1
  79.4 2.8 %copy-start.6 = (bf16[640,256]{1,0:T(8,128)(2,1)S(1)}, bf16[640,256]{1,0:T(8,128)(2,1)}, u32[]{:S(2)}) copy-start(bf16[640,256]{1,0:T(8,128)(2,1)} %copy-done.5) | copy-start | bytes 983044
  80.5 1.7 %collective-permute-start.17 = (bf16[640,256]{1,0:T(8,128)(2,1)S(1)}, bf16[640,256]{1,0:T(8,128)(2,1)S(1)}, u32[]{:S(2)}, u32[]{:S(2)}) collective-permute-start(bf16[640,256]{1,0:T(8,128)(2,1)S(1)} %bitcast.60), channel_id=1, source_target_pairs={{0,4},{4,0},{1,5},{5,1},{2,6},{6,2},{3,7},{7,3},{8,12},{12,8},{9,1... | collective-permute-start | bytes 983048 | tf_op jit(solution)/shard_map/ppermute | solution.py:22
  87.4 0.8 copy-start.2
  88.3 17.2 %collective-permute-start.18 = (bf16[1280,256]{1,0:T(8,128)(2,1)}, bf16[1280,256]{1,0:T(8,128)(2,1)S(1)}, u32[]{:S(2)}, u32[]{:S(2)}) collective-permute-start(bf16[1280,256]{1,0:T(8,128)(2,1)} %bitcast.31), channel_id=1, source_target_pairs={{0,32},{4,12},{8,40},{12,20},{16,48},{20,28},{24,56},{28,4},{32,64... | collective-permute-start | bytes 1966088 | tf_op jit(solution)/shard_map/ppermute | solution.py:37
  89.1 17.7 %collective-permute-start.19 = (bf16[1280,256]{1,0:T(8,128)(2,1)}, bf16[1280,256]{1,0:T(8,128)(2,1)}, u32[]{:S(2)}, u32[]{:S(2)}) collective-permute-start(bf16[1280,256]{1,0:T(8,128)(2,1)} %bitcast.32), channel_id=1, source_target_pairs={{0,64},{4,20},{8,72},{12,28},{16,80},{20,4},{24,88},{28,12},{32,96... | collective-permute-start | bytes 1966088 | tf_op jit(solution)/shard_map/ppermute | solution.py:37
  91.5 15.4 %collective-permute-start.20 = (bf16[1280,256]{1,0:T(8,128)(2,1)}, bf16[1280,256]{1,0:T(8,128)(2,1)}, u32[]{:S(2)}, u32[]{:S(2)}) collective-permute-start(bf16[1280,256]{1,0:T(8,128)(2,1)} %bitcast.33), channel_id=1, source_target_pairs={{0,96},{4,28},{8,104},{12,4},{16,112},{20,12},{24,120},{28,20},{32... | collective-permute-start | bytes 1966088 | tf_op jit(solution)/shard_map/ppermute | solution.py:37
  100.2 33.8 %all-to-all-start.2 = ((bf16[32,16,1280]{2,1,0:T(8,128)(2,1)}), bf16[32,16,1280]{2,1,0:T(8,128)(2,1)S(1)}, u32[]{:S(2)}, u32[]{:S(2)}) async-start(bf16[32,16,1280]{2,1,0:T(8,128)(2,1)} %bitcast.36), calls=%async_computation.2 | async-start | bytes 2621440 | tf_op jit(solution)/shard_map/all_to_all | solution.py:58
  105.5 1.4 %copy-start.7 = (bf16[1280,256]{1,0:T(8,128)(2,1)}, bf16[1280,256]{1,0:T(8,128)(2,1)S(1)}, u32[]{:S(2)}) copy-start(bf16[1280,256]{1,0:T(8,128)(2,1)S(1)} %collective-permute-done.18.refs_1_) | copy-start | bytes 1966084
  115.8 11.4 %collective-permute-start.21 = (bf16[160,1280]{1,0:T(8,128)(2,1)}, bf16[160,1280]{1,0:T(8,128)(2,1)S(1)}, u32[]{:S(2)}, u32[]{:S(2)}) collective-permute-start(bf16[160,1280]{1,0:T(8,128)(2,1)} %get-tuple-element.88), channel_id=1, source_target_pairs={{0,8},{4,36},{8,16},{12,44},{16,24},{20,52},{24,0},{28,60},{32,40}... | collective-permute-start | bytes 1228808 | tf_op jit(solution)/shard_map/ppermute | solution.py:37
  117.0 14.9 %collective-permute-start.22 = (bf16[160,1280]{1,0:T(8,128)(2,1)}, bf16[160,1280]{1,0:T(8,128)(2,1)S(1)}, u32[]{:S(2)}, u32[]{:S(2)}) collective-permute-start(bf16[160,1280]{1,0:T(8,128)(2,1)} %get-tuple-element.89), channel_id=1, source_target_pairs={{0,16},{4,68},{8,24},{12,76},{16,0},{20,84},{24,8},{28,92},{32,48}... | collective-permute-start | bytes 1228808 | tf_op jit(solution)/shard_map/ppermute | solution.py:37
  119.5 12.4 %collective-permute-start.23 = (bf16[160,1280]{1,0:T(8,128)(2,1)}, bf16[160,1280]{1,0:T(8,128)(2,1)S(1)}, u32[]{:S(2)}, u32[]{:S(2)}) collective-permute-start(bf16[160,1280]{1,0:T(8,128)(2,1)} %get-tuple-element.90), channel_id=1, source_target_pairs={{0,24},{4,100},{8,0},{12,108},{16,8},{20,116},{24,16},{28,124},{32... | collective-permute-start | bytes 1228808 | tf_op jit(solution)/shard_map/ppermute | solution.py:37

commit v15 on v14

--- a/solution.py
+++ b/solution.py
@@ -352,7 +352,7 @@
     ready, _, _ = lax.optimization_barrier((context, near, back))
     own, gained_t = hidden_part(out_proj, ready, residual, cotangent, norm_gain, z)
     late_pair, _ = lax.optimization_barrier((pair, near))
-    contexts = [pair] + [cross(late_pair, k, True) for k in (1, 2, 3)]
+    contexts = [pair, cross(late_pair, 1, True), None, cross(late_pair, 3, True)]
     hidden_t = own + shift(near, "z", 1).astype(F32) + shift(back, "z", 3).astype(F32)
 
     stats = jnp.stack(
@@ -383,20 +383,21 @@
         return shift(jnp.concatenate(asked, axis=0).reshape(-1, rows), "c", 1)
 
     slots = slot_matrix(destinations[:, 0], lanes * PAIR, rows, 16)
+    contexts[2] = cross(lax.optimization_barrier((pair, grad_t))[0], 2, True)
     from_left, from_right = shift(grad_t, "z", 1), shift(grad_t, "z", 3)
     swapped = swap(grad_t)
     grad_rows, _ = lax.optimization_barrier((grad_t, swapped))
     d_residual = exchange(place_rows(slots, grad_rows), lanes)
     context_grad = context_product([grad_t], [z], out_proj)
-    from_left, from_right, context_grad, swapped, contexts[2] = lax.optimization_barrier(
-        (from_left, from_right, context_grad, swapped, contexts[2])
+    from_left, from_right, context_grad, swapped = lax.optimization_barrier(
+        (from_left, from_right, context_grad, swapped)
     )
     far_left, far_right = shift(from_left[:top], "z", 1), shift(from_right[top:], "z", 3)
     context_grad = context_product(
         [from_right, from_left], [(z + 1) % NZ, (z + 3) % NZ], out_proj, before=context_grad
     )
-    far_left, far_right, context_grad = lax.optimization_barrier(
-        (far_left, far_right, context_grad)
+    far_left, far_right, context_grad, contexts[2] = lax.optimization_barrier(
+        (far_left, far_right, context_grad, contexts[2])
     )
     swapped_near = swap(from_right, from_left).reshape(8, block, rows)
     swapped_far = swap(far_left, far_right).reshape(4, block, rows)

time: 136 us -> 137 us (level)
    ppermute x9, starting transfers between devices: 13 us -> 14.5 us  [cross(): return lax.ppermute(value, DP, pairs)]
  transfers between devices with their start and end apart: 27 -> 27, of which waited for: 7 -> 6; matrix products, arithmetic and copies ran while one was open for 13% -> 12% of each run, Pallas kernels for 28% -> 28%
where the time goes in v15:
time: 137 us; the launch traced here: 136 us
  starting transfers between devices  53.7 us (39%)
  Pallas kernels  43.3 us (32%)
  waiting for transfers between devices  17 us (12%)
  local copies, waits for them, and re-layouts  11.2 us (8%)
  other arithmetic  10.2 us (7%)
    ppermute x15, starting transfers between devices, shift(): lax.ppermute(value, axis, [(i, (i + step) % size) for i in range(size)])  22 us
    ppermute x9, starting transfers between devices, cross(): return lax.ppermute(value, DP, pairs)  14.5 us
    pallas_call x3, Pallas kernels, context_product(): pl.pallas_call(body, out_shape=jax.ShapeDtypeStruct((out_rows, width), dt...  13.4 us
    ppermute x9, waiting for transfers between devices, cross(): return lax.ppermute(value, DP, pairs)  12.6 us
    all_to_all x2, starting transfers between devices, exchange(): return lax.all_to_all(blocks, DP, split_axis=0, concat_axis=0, tiled=True)  9.88 us
    pallas_call x3, Pallas kernels, forward_product(): pl.pallas_call(body, out_shape=[jax.ShapeDtypeStruct((tile, rows), BF16)]...  9.41 us
    pallas_call x1, Pallas kernels, weight_product(): pl.pallas_call(body, out_shape=[jax.ShapeDtypeStruct((block, width), BF16...  8.91 us
    all_to_all x1, starting transfers between devices, all_shares(): return lax.all_to_all(copies, DP, split_axis=0, concat_axis=0, tiled=True)  7.31 us
  transfers between devices with their start and end apart: 27, of which 6 were waited for; matrix products, arithmetic and copies ran while one was open for 12% of the time, Pallas kernels for 28%

profile of v15, /device:TPU:1, one launch (start us, length us, event | category | flops | bytes accessed | tf_op | source)
XLA Modules:
  0.0 136.4 jit_solution(12555087529127451042)
XLA Ops:
  0.6 2.9 %forward_product.3 = (bf16[640,256]{1,0:T(8,128)(2,1)S(1)}, bf16[640,256]{1,0:T(8,128)(2,1)S(1)}) custom-call(s32[1]{0:T(128)} %bitcast.3.which, bf16[5120,1280]{1,0:T(8,128)(2,1)} %refs_3_.3, bf16[256,1280]{1,0:T(8,128)(2,1)} %context_ref.6), custom_call_target="tpu_custom_call" | custom-call | tf_op jit(solution)/shard_map/forward_product/pallas_call | solution.py:175
  3.6 1.5 %collective-permute-start.2 = (bf16[256,1280]{1,0:T(8,128)(2,1)}, bf16[256,1280]{1,0:T(8,128)(2,1)S(1)}, u32[]{:S(2)}, u32[]{:S(2)}) collective-permute-start(bf16[256,1280]{1,0:T(8,128)(2,1)} %context_ref.6), channel_id=1, source_target_pairs={{0,4},{4,0},{1,5},{5,1},{2,6},{6,2},{3,7},{7,3},{8,12},{12,8},{9,1... | collective-permute-start | bytes 1966088 | tf_op jit(solution)/shard_map/ppermute | solution.py:22
  5.1 1.8 %collective-permute-start = (bf16[640,256]{1,0:T(8,128)(2,1)S(1)}, bf16[640,256]{1,0:T(8,128)(2,1)S(1)}, u32[]{:S(2)}, u32[]{:S(2)}) collective-permute-start(bf16[640,256]{1,0:T(8,128)(2,1)S(1)} %get-tuple-element.48), channel_id=1, source_target_pairs={{0,1},{1,2},{2,3},{3,0},{4,5},{5,6},{6,7},{7,4},{8,9},{9,10},{10,1... | collective-permute-start | bytes 983048 | tf_op jit(solution)/shard_map/ppermute | solution.py:22
  6.8 2.1 %collective-permute-start.1 = (bf16[640,256]{1,0:T(8,128)(2,1)S(1)}, bf16[640,256]{1,0:T(8,128)(2,1)S(1)}, u32[]{:S(2)}, u32[]{:S(2)}) collective-permute-start(bf16[640,256]{1,0:T(8,128)(2,1)S(1)} %get-tuple-element.49), channel_id=1, source_target_pairs={{0,3},{1,0},{2,1},{3,2},{4,7},{5,4},{6,5},{7,6},{8,11},{9,8},{10,9... | collective-permute-start | bytes 983048 | tf_op jit(solution)/shard_map/ppermute | solution.py:22
  8.9 2.9 %forward_product.4.refs_0_ = bf16[1280,256]{1,0:T(8,128)(2,1)S(1)} custom-call(s32[1]{0:T(128)} %bitcast.4.which, bf16[5120,1280]{1,0:T(8,128)(2,1)} %refs_3_.3, bf16[256,1280]{1,0:T(8,128)(2,1)} %context_ref.6), custom_call_target="tpu_custom_call" | custom-call | tf_op jit(solution)/shard_map/forward_product/pallas_call | solution.py:175
  11.8 3.6 %forward_product.5.refs_2_ = bf16[1280,256]{1,0:T(8,128)(2,1)} custom-call(s32[1]{0:T(128)} %bitcast.5.which, bf16[5120,1280]{1,0:T(8,128)(2,1)} %refs_3_.3, bf16[256,1280]{1,0:T(8,128)(2,1)} %context_ref.6), custom_call_target="tpu_custom_call" | custom-call | tf_op jit(solution)/shard_map/forward_product/pallas_call | solution.py:175
  15.4 2.3 %pad_maximum_fusion.refs_4_ = bf16[512,1280]{1,0:T(8,128)(2,1)} fusion(bf16[256,1280]{1,0:T(8,128)(2,1)S(1)} %collective-permute-done.2, bf16[256,1280]{1,0:T(8,128)(2,1)} %context_ref.6), kind=kLoop, calls=%fused_computation | loop fusion | flops 2621440 | bytes 2621440 | tf_op jit(solution)/shard_map/concatenate | solution.py:343
  17.7 1.9 %top_up.1 = (bf16[1280,256]{1,0:T(8,128)(2,1)S(1)}, bf16[1280,256]{1,0:T(8,128)(2,1)}) custom-call(bf16[1280,256]{1,0:T(8,128)(2,1)S(1)} %forward_product.4.refs_0_, bf16[640,256]{1,0:T(8,128)(2,1)S(1)} %collective-permute-done.refs_1_, bf16[1280,256]{1,0:T(8,128)(2,1)} %forward_product.5.refs_2_, ...), custom_call_target="tpu_custom_call", output_to_operand_aliasing={{0}: (0, {}), {1}: (2, {})} | custom-call | tf_op jit(solution)/shard_map/top_up/pallas_call | solution.py:144
  19.6 2.7 %collective-permute-start.4 = (bf16[1280,256]{1,0:T(8,128)(2,1)}, bf16[1280,256]{1,0:T(8,128)(2,1)}, u32[]{:S(2)}, u32[]{:S(2)}) collective-permute-start(bf16[1280,256]{1,0:T(8,128)(2,1)} %get-tuple-element.56), channel_id=1, source_target_pairs={{0,3},{1,0},{2,1},{3,2},{4,7},{5,4},{6,5},{7,6},{8,11},{9,8},{10,9... | collective-permute-start | bytes 1966088 | tf_op jit(solution)/shard_map/ppermute | solution.py:22
  22.6 1.3 collective-permute-start.8
  23.9 1.5 %collective-permute-start.9 = (bf16[512,1280]{1,0:T(8,128)(2,1)}, bf16[512,1280]{1,0:T(8,128)(2,1)}, u32[]{:S(2)}, u32[]{:S(2)}) collective-permute-start(bf16[512,1280]{1,0:T(8,128)(2,1)} %pad_maximum_fusion.refs_4_), channel_id=1, source_target_pairs={{0,96},{4,28},{8,104},{12,4},{16,112},{20,12},{24,120},{28,20},{32... | collective-permute-start | bytes 3932168 | tf_op jit(solution)/shard_map/ppermute | solution.py:37
  25.4 2.9 %hidden_part.1 = (f32[1280,256]{1,0:T(8,128)S(1)}, f32[1280,256]{1,0:T(8,128)S(1)}) custom-call(s32[1]{0:T(128)} %bitcast.2.which, bf16[5120,1280]{1,0:T(8,128)(2,1)} %refs_3_.3, bf16[256,1280]{1,0:T(8,128)(2,1)} %context_ref.6, bf16[256,1280]{1,0:T(8,128)(2,1)S(1)} %copy-done.3, bf16[256,1280]{1,0:T(8,128)(2,1)S(1)} %copy-done.4, ...), custom_call_target="tpu_custom_call" | custom-call | tf_op jit(solution)/shard_map/hidden_part/pallas_call | solution.py:210
  29.0 7.3 %all-to-all-start = ((f32[32,1,8]{2,1,0:T(1,128)}), f32[32,1,8]{2,1,0:T(1,128)S(1)}, u32[]{:S(2)}, u32[]{:S(2)}) async-start(f32[32,1,8]{2,1,0:T(1,128)} %broadcast_in_dim.16), calls=%async_computation | async-start | bytes 32768 | tf_op jit(solution)/shard_map/all_to_all | solution.py:42
  36.8 1.7 %multiply_reduce_fusion.1 = (f32[256]{0:T(256)S(1)}, f32[256]{0:T(256)S(1)}) fusion(bf16[1280,256]{1,0:T(8,128)(2,1)} %collective-permute-done.4, f32[1280,256]{1,0:T(8,128)S(1)} %get-tuple-element.58, bf16[1280,256]{1,0:T(8,128)(2,1)} %collective-permute-done.3, f32[1280,256]{1,0:T(8,128)S(1)} %get-tuple-element.59), kind=kLoop, calls=%fused_computation.3 | loop fusion | flops 2620928 | bytes 3934208 | tf_op jit(solution)/shard_map/reduce_sum | solution.py:359
  38.6 3.7 %collective-permute-start.6 = (f32[2,256]{1,0:T(2,128)S(1)}, f32[2,256]{1,0:T(2,128)S(1)}, u32[]{:S(2)}, u32[]{:S(2)}) collective-permute-start(f32[2,256]{1,0:T(2,128)S(1)} %pad_maximum_fusion.3), channel_id=1, source_target_pairs={{0,2},{1,3},{2,0},{3,1},{4,6},{5,7},{6,4},{7,5},{8,10},{9,11},{10,... | collective-permute-start | bytes 6152 | tf_op jit(solution)/shard_map/ppermute | solution.py:22
  42.3 3.4 %all-to-all-done = f32[32,1,8]{2,1,0:T(1,128)S(1)} async-done(((f32[32,1,8]{2,1,0:T(1,128)}), f32[32,1,8]{2,1,0:T(1,128)S(1)}, u32[]{:S(2)}, u32[]{:S(2)}) %all-to-all-start) | async-done | bytes 1056 | tf_op jit(solution)/shard_map/all_to_all | solution.py:42
  46.2 1.6 %subtract_convert_fusion.refs_0_.grad_ref = bf16[1280,256]{1,0:T(8,128)(2,1)S(1)} fusion(f32[1280,256]{1,0:T(8,128)S(1)} %get-tuple-element.59, f32[256]{0:T(256)S(1)} %bitcast.68, f32[256]{0:T(256)S(1)} %bitcast.67, bf16[1280,256]{1,0:T(8,128)(2,1)} %collective-permute-done.4, f32[1280,256]{1,0:T(8,128)S(1)} %get-tuple-element.58, ...), kind=kLoop, calls=%fused_computation.1 | loop fusion | flops 2621440 | bytes 4589568 | tf_op jit(solution)/shard_map/convert_element_type | solution.py:375
  47.9 2.7 %collective-permute-start.11 = (bf16[1280,256]{1,0:T(8,128)(2,1)S(1)}, bf16[1280,256]{1,0:T(8,128)(2,1)S(1)}, u32[]{:S(2)}, u32[]{:S(2)}) collective-permute-start(bf16[1280,256]{1,0:T(8,128)(2,1)S(1)} %subtract_convert_fusion.refs_0_.grad_ref), channel_id=1, source_target_pairs={{0,3},{1,0},{2,1},{3,2},{4,7},{5,4},{6,5},{7,6},{8,11},{9,8},{10,9... | collective-permute-start | bytes 1966088 | tf_op jit(solution)/shard_map/ppermute | solution.py:22
  50.5 1.8 %collective-permute-start.15 = (bf16[512,1280]{1,0:T(8,128)(2,1)}, bf16[512,1280]{1,0:T(8,128)(2,1)}, u32[]{:S(2)}, u32[]{:S(2)}) collective-permute-start(bf16[512,1280]{1,0:T(8,128)(2,1)} %pad_maximum_fusion.refs_4_), channel_id=1, source_target_pairs={{0,64},{4,20},{8,72},{12,28},{16,80},{20,4},{24,88},{28,12},{32,96... | collective-permute-start | bytes 3932168 | tf_op jit(solution)/shard_map/ppermute | solution.py:37
  52.4 3.8 %collective-permute-start.12 = (bf16[640,256]{1,0:T(8,128)(2,1)S(1)}, bf16[640,256]{1,0:T(8,128)(2,1)S(1)}, u32[]{:S(2)}, u32[]{:S(2)}) collective-permute-start(bf16[640,256]{1,0:T(8,128)(2,1)S(1)} %bitcast.61), channel_id=1, source_target_pairs={{0,4},{4,0},{1,5},{5,1},{2,6},{6,2},{3,7},{7,3},{8,12},{12,8},{9,1... | collective-permute-start | bytes 983048 | tf_op jit(solution)/shard_map/ppermute | solution.py:22
  56.4 3.0 %context_product.3.refs_4_ = f32[256,1280]{1,0:T(8,128)S(1)} custom-call(s32[1]{0:T(128)} %bitcast.2.which, bf16[1280,256]{1,0:T(8,128)(2,1)S(1)} %subtract_convert_fusion.refs_0_.grad_ref, bf16[5120,1280]{1,0:T(8,128)(2,1)} %refs_3_.3), custom_call_target="tpu_custom_call" | custom-call | tf_op jit(solution)/shard_map/context_product/pallas_call | solution.py:104
  59.4 1.1 copy-done
  60.5 1.6 %place_rows.1 = bf16[512,1280]{1,0:T(8,128)(2,1)} custom-call(bf16[512,256]{1,0:T(8,128)(2,1)S(1)} %fusion.refs_5_.slots_ref, bf16[1280,256]{1,0:T(8,128)(2,1)S(1)} %subtract_convert_fusion.refs_0_.grad_ref), custom_call_target="tpu_custom_call" | custom-call | tf_op jit(solution)/shard_map/place_rows/pallas_call | solution.py:125
  62.1 5.3 %all-to-all-start.1 = ((bf16[32,16,1280]{2,1,0:T(8,128)(2,1)}), bf16[32,16,1280]{2,1,0:T(8,128)(2,1)}, u32[]{:S(2)}, u32[]{:S(2)}) async-start(bf16[32,16,1280]{2,1,0:T(8,128)(2,1)} %bitcast.35), calls=%async_computation.1 | async-start | bytes 2621440 | tf_op jit(solution)/shard_map/all_to_all | solution.py:58
  69.0 2.7 %collective-permute-start.14 = (bf16[640,256]{1,0:T(8,128)(2,1)}, bf16[640,256]{1,0:T(8,128)(2,1)}, u32[]{:S(2)}, u32[]{:S(2)}) collective-permute-start(bf16[640,256]{1,0:T(8,128)(2,1)} %slice.33), channel_id=1, source_target_pairs={{0,3},{1,0},{2,1},{3,2},{4,7},{5,4},{6,5},{7,6},{8,11},{9,8},{10,9... | collective-permute-start | bytes 983048 | tf_op jit(solution)/shard_map/ppermute | solution.py:22
  71.7 0.9 pad_maximum_fusion.1
  72.6 0.9 collective-permute-start.16
  73.6 1.3 copy-done.1
  74.9 5.1 %context_product.4.refs_4_ = f32[256,1280]{1,0:T(8,128)S(1)} custom-call(s32[2]{0:T(128)S(1)} %pad_add_fusion.1.which, bf16[1280,256]{1,0:T(8,128)(2,1)S(1)} %collective-permute-done.11.refs_0_, bf16[1280,256]{1,0:T(8,128)(2,1)S(1)} %collective-permute-done.10.refs_1_, bf16[5120,1280]{1,0:T(8,128)(2,1)} %refs_3_.3, bf16[5120,1280]{1,0:T(8,128)(2,1)} %refs_3_.3, ...), custom_call_target="tpu_custom_call" | custom-call | tf_op jit(solution)/shard_map/context_product/pallas_call | solution.py:104
  80.0 1.1 dynamic-slice_bitcast_fusion.2
  81.3 1.1 fusion.8
  82.8 5.2 %lay_out.1 = (bf16[8,160,256]{2,1,0:T(8,128)(2,1)S(1)}, bf16[8,160,256]{2,1,0:T(8,128)(2,1)}, bf16[8,160,256]{2,1,0:T(8,128)(2,1)}, bf16[8,160,256]{2,1,0:T(8,128)(2,1)}) custom-call(s32[4]{0:T(128)S(1)} %pad_add_fusion.2.where, bf16[4,2,160,256]{3,2,1,0:T(8,128)(2,1)S(1)} %bitcast.49, bf16[4,2,160,256]{3,2,1,0:T(8,128)(2,1)S(1)} %bitcast.53, ...), custom_call_target="tpu_custom_call" | custom-call | tf_op jit(solution)/shard_map/lay_out/pallas_call | solution.py:278
  88.1 0.9 copy-done.2
  89.0 1.4 %collective-permute-start.18 = (bf16[1280,256]{1,0:T(8,128)(2,1)}, bf16[1280,256]{1,0:T(8,128)(2,1)S(1)}, u32[]{:S(2)}, u32[]{:S(2)}) collective-permute-start(bf16[1280,256]{1,0:T(8,128)(2,1)} %bitcast.31), channel_id=1, source_target_pairs={{0,32},{4,12},{8,40},{12,20},{16,48},{20,28},{24,56},{28,4},{32,64... | collective-permute-start | bytes 1966088 | tf_op jit(solution)/shard_map/ppermute | solution.py:37
  90.4 2.4 %collective-permute-start.19 = (bf16[1280,256]{1,0:T(8,128)(2,1)}, bf16[1280,256]{1,0:T(8,128)(2,1)}, u32[]{:S(2)}, u32[]{:S(2)}) collective-permute-start(bf16[1280,256]{1,0:T(8,128)(2,1)} %bitcast.32), channel_id=1, source_target_pairs={{0,64},{4,20},{8,72},{12,28},{16,80},{20,4},{24,88},{28,12},{32,96... | collective-permute-start | bytes 1966088 | tf_op jit(solution)/shard_map/ppermute | solution.py:37
  92.8 1.2 collective-permute-start.20
  94.1 2.2 %reshape.171 = bf16[384,1280]{1,0:T(8,128)(2,1)} reshape(bf16[32,12,1280]{2,1,0:T(8,128)(2,1)} %bitcast.46) | data formatting | bytes 1966080 | tf_op jit(solution)/shard_map/reshape | solution.py:63
  96.2 5.3 %context_product.5 = bf16[512,1280]{1,0:T(8,128)(2,1)} custom-call(s32[2]{0:T(128)S(1)} %pad_add_fusion.which, bf16[640,256]{1,0:T(8,128)(2,1)} %collective-permute-done.13.refs_0_, bf16[640,256]{1,0:T(8,128)(2,1)} %collective-permute-done.14.refs_1_, bf16[5120,1280]{1,0:T(8,128)(2,1)} %refs_3_.3, bf16[5120,1280]{1,0:T(8,128)(2,1)} %refs_3_.3, ...), custom_call_target="tpu_custom_call" | custom-call | tf_op jit(solution)/shard_map/context_product/pallas_call | solution.py:104
  101.6 4.5 %all-to-all-start.2 = ((bf16[32,16,1280]{2,1,0:T(8,128)(2,1)}), bf16[32,16,1280]{2,1,0:T(8,128)(2,1)S(1)}, u32[]{:S(2)}, u32[]{:S(2)}) async-start(bf16[32,16,1280]{2,1,0:T(8,128)(2,1)} %bitcast.36), calls=%async_computation.2 | async-start | bytes 2621440 | tf_op jit(solution)/shard_map/all_to_all | solution.py:58
  106.8 1.3 collective-permute-done.19.refs_2_
  108.1 8.9 %weight_product.1 = (f32[160,1280]{1,0:T(8,128)}, bf16[160,1280]{1,0:T(8,128)(2,1)}, bf16[160,1280]{1,0:T(8,128)(2,1)}, bf16[160,1280]{1,0:T(8,128)(2,1)}) custom-call(s32[4]{0:T(128)} %pad_add_fusion.3.order_ref, bf16[1280,256]{1,0:T(8,128)(2,1)} %bitcast.56, bf16[1280,256]{1,0:T(8,128)(2,1)} %copy-done.7, ...), custom_call_target="tpu_custom_call" | custom-call | tf_op jit(solution)/shard_map/weight_product/pallas_call | solution.py:315
  117.0 1.2 collective-permute-start.21
  118.3 2.5 %collective-permute-start.22 = (bf16[160,1280]{1,0:T(8,128)(2,1)}, bf16[160,1280]{1,0:T(8,128)(2,1)S(1)}, u32[]{:S(2)}, u32[]{:S(2)}) collective-permute-start(bf16[160,1280]{1,0:T(8,128)(2,1)} %get-tuple-element.91), channel_id=1, source_target_pairs={{0,16},{4,68},{8,24},{12,76},{16,0},{20,84},{24,8},{28,92},{32,48}... | collective-permute-start | bytes 1228808 | tf_op jit(solution)/shard_map/ppermute | solution.py:37
  120.7 1.1 collective-permute-start.23
  121.9 6.7 %collective-permute-done.21 = bf16[160,1280]{1,0:T(8,128)(2,1)S(1)} collective-permute-done((bf16[160,1280]{1,0:T(8,128)(2,1)}, bf16[160,1280]{1,0:T(8,128)(2,1)S(1)}, u32[]{:S(2)}, u32[]{:S(2)}) %collective-permute-start.21) | collective-permute-done | bytes 409632 | tf_op jit(solution)/shard_map/ppermute | solution.py:37
  128.5 4.6 %collective-permute-done.22 = bf16[160,1280]{1,0:T(8,128)(2,1)S(1)} collective-permute-done((bf16[160,1280]{1,0:T(8,128)(2,1)}, bf16[160,1280]{1,0:T(8,128)(2,1)S(1)}, u32[]{:S(2)}, u32[]{:S(2)}) %collective-permute-start.22) | collective-permute-done | bytes 409632 | tf_op jit(solution)/shard_map/ppermute | solution.py:37
  133.2 2.2 %add_multiply_fusion = f32[160,1280]{1,0:T(8,128)} fusion(bf16[160,1280]{1,0:T(8,128)(2,1)S(1)} %collective-permute-done.23, bf16[160,1280]{1,0:T(8,128)(2,1)S(1)} %collective-permute-done.22, f32[160,1280]{1,0:T(8,128)} %get-tuple-element.89, bf16[160,1280]{1,0:T(8,128)(2,1)S(1)} %collective-permute-done.21), kind=kLoop, calls=%fused_computation.5 | loop fusion | flops 1433600 | bytes 2867200 | tf_op jit(solution)/shard_map/div | solution.py:427
  135.4 1.1 reshape.173
  (78 shorter events, 5.3 us)
Async XLA Ops:
  3.6 11.8 %collective-permute-start.2 = (bf16[256,1280]{1,0:T(8,128)(2,1)}, bf16[256,1280]{1,0:T(8,128)(2,1)S(1)}, u32[]{:S(2)}, u32[]{:S(2)}) collective-permute-start(bf16[256,1280]{1,0:T(8,128)(2,1)} %context_ref.6), channel_id=1, source_target_pairs={{0,4},{4,0},{1,5},{5,1},{2,6},{6,2},{3,7},{7,3},{8,12},{12,8},{9,1... | collective-permute-start | bytes 1966088 | tf_op jit(solution)/shard_map/ppermute | solution.py:22
  5.1 12.6 %collective-permute-start = (bf16[640,256]{1,0:T(8,128)(2,1)S(1)}, bf16[640,256]{1,0:T(8,128)(2,1)S(1)}, u32[]{:S(2)}, u32[]{:S(2)}) collective-permute-start(bf16[640,256]{1,0:T(8,128)(2,1)S(1)} %get-tuple-element.48), channel_id=1, source_target_pairs={{0,1},{1,2},{2,3},{3,0},{4,5},{5,6},{6,7},{7,4},{8,9},{9,10},{10,1... | collective-permute-start | bytes 983048 | tf_op jit(solution)/shard_map/ppermute | solution.py:22
  6.8 10.9 %collective-permute-start.1 = (bf16[640,256]{1,0:T(8,128)(2,1)S(1)}, bf16[640,256]{1,0:T(8,128)(2,1)S(1)}, u32[]{:S(2)}, u32[]{:S(2)}) collective-permute-start(bf16[640,256]{1,0:T(8,128)(2,1)S(1)} %get-tuple-element.49), channel_id=1, source_target_pairs={{0,3},{1,0},{2,1},{3,2},{4,7},{5,4},{6,5},{7,6},{8,11},{9,8},{10,9... | collective-permute-start | bytes 983048 | tf_op jit(solution)/shard_map/ppermute | solution.py:22
  17.7 4.6 %copy-start.8 = (f32[1280]{0:T(1024)S(1)}, f32[1280]{0:T(1024)}, u32[]{:S(2)}) copy-start(f32[1280]{0:T(1024)} %param.13) | copy-start | bytes 15364
  17.7 4.6 %copy-start.12 = (s32[64,1]{0,1:T(1,128)S(1)}, s32[64,1]{0,1:T(1,128)}, u32[]{:S(2)}) copy-start(s32[64,1]{0,1:T(1,128)} %param.17) | copy-start | bytes 772
  17.7 4.8 %copy-start.10 = (f32[4]{0:T(128)S(1)}, f32[4]{0:T(128)}, u32[]{:S(2)}) copy-start(f32[4]{0:T(128)} %param.14) | copy-start | bytes 52
  17.7 4.8 %copy-start.11 = (s32[4]{0:T(128)S(1)}, s32[4]{0:T(128)}, u32[]{:S(2)}) copy-start(s32[4]{0:T(128)} %param.15) | copy-start | bytes 52
  17.7 7.7 %copy-start.3 = (bf16[256,1280]{1,0:T(8,128)(2,1)S(1)}, bf16[256,1280]{1,0:T(8,128)(2,1)}, u32[]{:S(2)}) copy-start(bf16[256,1280]{1,0:T(8,128)(2,1)} %residual_ref.1) | copy-start | bytes 1966084
  17.7 7.7 %copy-start.4 = (bf16[256,1280]{1,0:T(8,128)(2,1)S(1)}, bf16[256,1280]{1,0:T(8,128)(2,1)}, u32[]{:S(2)}) copy-start(bf16[256,1280]{1,0:T(8,128)(2,1)} %cotangent_ref.1) | copy-start | bytes 1966084
  19.6 17.2 %collective-permute-start.3 = (bf16[1280,256]{1,0:T(8,128)(2,1)S(1)}, bf16[1280,256]{1,0:T(8,128)(2,1)}, u32[]{:S(2)}, u32[]{:S(2)}) collective-permute-start(bf16[1280,256]{1,0:T(8,128)(2,1)S(1)} %get-tuple-element.55), channel_id=1, source_target_pairs={{0,1},{1,2},{2,3},{3,0},{4,5},{5,6},{6,7},{7,4},{8,9},{9,10},{10,1... | collective-permute-start | bytes 1966088 | tf_op jit(solution)/shard_map/ppermute | solution.py:22
  19.6 17.2 %collective-permute-start.4 = (bf16[1280,256]{1,0:T(8,128)(2,1)}, bf16[1280,256]{1,0:T(8,128)(2,1)}, u32[]{:S(2)}, u32[]{:S(2)}) collective-permute-start(bf16[1280,256]{1,0:T(8,128)(2,1)} %get-tuple-element.56), channel_id=1, source_target_pairs={{0,3},{1,0},{2,1},{3,2},{4,7},{5,4},{6,5},{7,6},{8,11},{9,8},{10,9... | collective-permute-start | bytes 1966088 | tf_op jit(solution)/shard_map/ppermute | solution.py:22
  22.6 25.2 %collective-permute-start.8 = (bf16[512,1280]{1,0:T(8,128)(2,1)}, bf16[512,1280]{1,0:T(8,128)(2,1)}, u32[]{:S(2)}, u32[]{:S(2)}) collective-permute-start(bf16[512,1280]{1,0:T(8,128)(2,1)} %pad_maximum_fusion.refs_4_), channel_id=1, source_target_pairs={{0,32},{4,12},{8,40},{12,20},{16,48},{20,28},{24,56},{28,4},{32,64... | collective-permute-start | bytes 3932168 | tf_op jit(solution)/shard_map/ppermute | solution.py:37
  23.9 23.9 %collective-permute-start.9 = (bf16[512,1280]{1,0:T(8,128)(2,1)}, bf16[512,1280]{1,0:T(8,128)(2,1)}, u32[]{:S(2)}, u32[]{:S(2)}) collective-permute-start(bf16[512,1280]{1,0:T(8,128)(2,1)} %pad_maximum_fusion.refs_4_), channel_id=1, source_target_pairs={{0,96},{4,28},{8,104},{12,4},{16,112},{20,12},{24,120},{28,20},{32... | collective-permute-start | bytes 3932168 | tf_op jit(solution)/shard_map/ppermute | solution.py:37
  29.0 16.8 %all-to-all-start = ((f32[32,1,8]{2,1,0:T(1,128)}), f32[32,1,8]{2,1,0:T(1,128)S(1)}, u32[]{:S(2)}, u32[]{:S(2)}) async-start(f32[32,1,8]{2,1,0:T(1,128)} %broadcast_in_dim.16), calls=%async_computation | async-start | bytes 32768 | tf_op jit(solution)/shard_map/all_to_all | solution.py:42
  36.8 9.1 %copy-start.9 = (s32[4]{0:T(128)S(1)}, s32[4]{0:T(128)}, u32[]{:S(2)}) copy-start(s32[4]{0:T(128)} %param.16) | copy-start | bytes 52
  38.5 7.6 %collective-permute-start.5 = (f32[2,256]{1,0:T(2,128)S(1)}, f32[2,256]{1,0:T(2,128)S(1)}, u32[]{:S(2)}, u32[]{:S(2)}) collective-permute-start(f32[2,256]{1,0:T(2,128)S(1)} %pad_maximum_fusion.3), channel_id=1, source_target_pairs={{0,1},{1,2},{2,3},{3,0},{4,5},{5,6},{6,7},{7,4},{8,9},{9,10},{10,1... | collective-permute-start | bytes 6152 | tf_op jit(solution)/shard_map/ppermute | solution.py:22
  38.6 7.5 %collective-permute-start.6 = (f32[2,256]{1,0:T(2,128)S(1)}, f32[2,256]{1,0:T(2,128)S(1)}, u32[]{:S(2)}, u32[]{:S(2)}) collective-permute-start(f32[2,256]{1,0:T(2,128)S(1)} %pad_maximum_fusion.3), channel_id=1, source_target_pairs={{0,2},{1,3},{2,0},{3,1},{4,6},{5,7},{6,4},{7,5},{8,10},{9,11},{10,... | collective-permute-start | bytes 6152 | tf_op jit(solution)/shard_map/ppermute | solution.py:22
  42.3 3.8 %collective-permute-start.7 = (f32[2,256]{1,0:T(2,128)S(1)}, f32[2,256]{1,0:T(2,128)S(1)}, u32[]{:S(2)}, u32[]{:S(2)}) collective-permute-start(f32[2,256]{1,0:T(2,128)S(1)} %pad_maximum_fusion.3), channel_id=1, source_target_pairs={{0,3},{1,0},{2,1},{3,2},{4,7},{5,4},{6,5},{7,6},{8,11},{9,8},{10,9... | collective-permute-start | bytes 6152 | tf_op jit(solution)/shard_map/ppermute | solution.py:22
  47.8 19.7 %collective-permute-start.10 = (bf16[1280,256]{1,0:T(8,128)(2,1)S(1)}, bf16[1280,256]{1,0:T(8,128)(2,1)S(1)}, u32[]{:S(2)}, u32[]{:S(2)}) collective-permute-start(bf16[1280,256]{1,0:T(8,128)(2,1)S(1)} %subtract_convert_fusion.refs_0_.grad_ref), channel_id=1, source_target_pairs={{0,1},{1,2},{2,3},{3,0},{4,5},{5,6},{6,7},{7,4},{8,9},{9,10},{10,1... | collective-permute-start | bytes 1966088 | tf_op jit(solution)/shard_map/ppermute | solution.py:22
  47.9 19.6 %collective-permute-start.11 = (bf16[1280,256]{1,0:T(8,128)(2,1)S(1)}, bf16[1280,256]{1,0:T(8,128)(2,1)S(1)}, u32[]{:S(2)}, u32[]{:S(2)}) collective-permute-start(bf16[1280,256]{1,0:T(8,128)(2,1)S(1)} %subtract_convert_fusion.refs_0_.grad_ref), channel_id=1, source_target_pairs={{0,3},{1,0},{2,1},{3,2},{4,7},{5,4},{6,5},{7,6},{8,11},{9,8},{10,9... | collective-permute-start | bytes 1966088 | tf_op jit(solution)/shard_map/ppermute | solution.py:22
  50.5 29.4 %collective-permute-start.15 = (bf16[512,1280]{1,0:T(8,128)(2,1)}, bf16[512,1280]{1,0:T(8,128)(2,1)}, u32[]{:S(2)}, u32[]{:S(2)}) collective-permute-start(bf16[512,1280]{1,0:T(8,128)(2,1)} %pad_maximum_fusion.refs_4_), channel_id=1, source_target_pairs={{0,64},{4,20},{8,72},{12,28},{16,80},{20,4},{24,88},{28,12},{32,96... | collective-permute-start | bytes 3932168 | tf_op jit(solution)/shard_map/ppermute | solution.py:37
  52.4 8.1 %collective-permute-start.12 = (bf16[640,256]{1,0:T(8,128)(2,1)S(1)}, bf16[640,256]{1,0:T(8,128)(2,1)S(1)}, u32[]{:S(2)}, u32[]{:S(2)}) collective-permute-start(bf16[640,256]{1,0:T(8,128)(2,1)S(1)} %bitcast.61), channel_id=1, source_target_pairs={{0,4},{4,0},{1,5},{5,1},{2,6},{6,2},{3,7},{7,3},{8,12},{12,8},{9,1... | collective-permute-start | bytes 983048 | tf_op jit(solution)/shard_map/ppermute | solution.py:22
  59.4 1.1 copy-start
  60.5 1.6 %copy-start.5 = (bf16[640,256]{1,0:T(8,128)(2,1)}, bf16[640,256]{1,0:T(8,128)(2,1)S(1)}, u32[]{:S(2)}) copy-start(bf16[640,256]{1,0:T(8,128)(2,1)S(1)} %collective-permute-done.12) | copy-start | bytes 983044
  62.1 31.9 %all-to-all-start.1 = ((bf16[32,16,1280]{2,1,0:T(8,128)(2,1)}), bf16[32,16,1280]{2,1,0:T(8,128)(2,1)}, u32[]{:S(2)}, u32[]{:S(2)}) async-start(bf16[32,16,1280]{2,1,0:T(8,128)(2,1)} %bitcast.35), calls=%async_computation.1 | async-start | bytes 2621440 | tf_op jit(solution)/shard_map/all_to_all | solution.py:58
  68.2 11.7 %collective-permute-start.13 = (bf16[640,256]{1,0:T(8,128)(2,1)}, bf16[640,256]{1,0:T(8,128)(2,1)}, u32[]{:S(2)}, u32[]{:S(2)}) collective-permute-start(bf16[640,256]{1,0:T(8,128)(2,1)} %slice.32), channel_id=1, source_target_pairs={{0,1},{1,2},{2,3},{3,0},{4,5},{5,6},{6,7},{7,4},{8,9},{9,10},{10,1... | collective-permute-start | bytes 983048 | tf_op jit(solution)/shard_map/ppermute | solution.py:22
  69.0 11.0 %collective-permute-start.14 = (bf16[640,256]{1,0:T(8,128)(2,1)}, bf16[640,256]{1,0:T(8,128)(2,1)}, u32[]{:S(2)}, u32[]{:S(2)}) collective-permute-start(bf16[640,256]{1,0:T(8,128)(2,1)} %slice.33), channel_id=1, source_target_pairs={{0,3},{1,0},{2,1},{3,2},{4,7},{5,4},{6,5},{7,6},{8,11},{9,8},{10,9... | collective-permute-start | bytes 983048 | tf_op jit(solution)/shard_map/ppermute | solution.py:22
  72.6 8.7 %collective-permute-start.16 = (bf16[1280,256]{1,0:T(8,128)(2,1)}, bf16[1280,256]{1,0:T(8,128)(2,1)}, u32[]{:S(2)}, u32[]{:S(2)}) collective-permute-start(bf16[1280,256]{1,0:T(8,128)(2,1)} %bitcast.23), channel_id=1, source_target_pairs={{0,4},{4,0},{1,5},{5,1},{2,6},{6,2},{3,7},{7,3},{8,12},{12,8},{9,1... | collective-permute-start | bytes 1966088 | tf_op jit(solution)/shard_map/ppermute | solution.py:22
  73.6 1.3 copy-start.1
  80.0 2.8 %copy-start.6 = (bf16[640,256]{1,0:T(8,128)(2,1)S(1)}, bf16[640,256]{1,0:T(8,128)(2,1)}, u32[]{:S(2)}) copy-start(bf16[640,256]{1,0:T(8,128)(2,1)} %copy-done.5) | copy-start | bytes 983044
  81.1 1.7 %collective-permute-start.17 = (bf16[640,256]{1,0:T(8,128)(2,1)S(1)}, bf16[640,256]{1,0:T(8,128)(2,1)S(1)}, u32[]{:S(2)}, u32[]{:S(2)}) collective-permute-start(bf16[640,256]{1,0:T(8,128)(2,1)S(1)} %bitcast.60), channel_id=1, source_target_pairs={{0,4},{4,0},{1,5},{5,1},{2,6},{6,2},{3,7},{7,3},{8,12},{12,8},{9,1... | collective-permute-start | bytes 983048 | tf_op jit(solution)/shard_map/ppermute | solution.py:22
  88.0 0.9 copy-start.2
  89.0 17.9 %collective-permute-start.18 = (bf16[1280,256]{1,0:T(8,128)(2,1)}, bf16[1280,256]{1,0:T(8,128)(2,1)S(1)}, u32[]{:S(2)}, u32[]{:S(2)}) collective-permute-start(bf16[1280,256]{1,0:T(8,128)(2,1)} %bitcast.31), channel_id=1, source_target_pairs={{0,32},{4,12},{8,40},{12,20},{16,48},{20,28},{24,56},{28,4},{32,64... | collective-permute-start | bytes 1966088 | tf_op jit(solution)/shard_map/ppermute | solution.py:37
  90.4 17.7 %collective-permute-start.19 = (bf16[1280,256]{1,0:T(8,128)(2,1)}, bf16[1280,256]{1,0:T(8,128)(2,1)}, u32[]{:S(2)}, u32[]{:S(2)}) collective-permute-start(bf16[1280,256]{1,0:T(8,128)(2,1)} %bitcast.32), channel_id=1, source_target_pairs={{0,64},{4,20},{8,72},{12,28},{16,80},{20,4},{24,88},{28,12},{32,96... | collective-permute-start | bytes 1966088 | tf_op jit(solution)/shard_map/ppermute | solution.py:37
  92.8 15.3 %collective-permute-start.20 = (bf16[1280,256]{1,0:T(8,128)(2,1)}, bf16[1280,256]{1,0:T(8,128)(2,1)}, u32[]{:S(2)}, u32[]{:S(2)}) collective-permute-start(bf16[1280,256]{1,0:T(8,128)(2,1)} %bitcast.33), channel_id=1, source_target_pairs={{0,96},{4,28},{8,104},{12,4},{16,112},{20,12},{24,120},{28,20},{32... | collective-permute-start | bytes 1966088 | tf_op jit(solution)/shard_map/ppermute | solution.py:37
  101.6 33.8 %all-to-all-start.2 = ((bf16[32,16,1280]{2,1,0:T(8,128)(2,1)}), bf16[32,16,1280]{2,1,0:T(8,128)(2,1)S(1)}, u32[]{:S(2)}, u32[]{:S(2)}) async-start(bf16[32,16,1280]{2,1,0:T(8,128)(2,1)} %bitcast.36), calls=%async_computation.2 | async-start | bytes 2621440 | tf_op jit(solution)/shard_map/all_to_all | solution.py:58
  106.8 1.3 copy-start.7
  117.0 11.5 %collective-permute-start.21 = (bf16[160,1280]{1,0:T(8,128)(2,1)}, bf16[160,1280]{1,0:T(8,128)(2,1)S(1)}, u32[]{:S(2)}, u32[]{:S(2)}) collective-permute-start(bf16[160,1280]{1,0:T(8,128)(2,1)} %get-tuple-element.90), channel_id=1, source_target_pairs={{0,8},{4,36},{8,16},{12,44},{16,24},{20,52},{24,0},{28,60},{32,40}... | collective-permute-start | bytes 1228808 | tf_op jit(solution)/shard_map/ppermute | solution.py:37
  118.3 14.9 %collective-permute-start.22 = (bf16[160,1280]{1,0:T(8,128)(2,1)}, bf16[160,1280]{1,0:T(8,128)(2,1)S(1)}, u32[]{:S(2)}, u32[]{:S(2)}) collective-permute-start(bf16[160,1280]{1,0:T(8,128)(2,1)} %get-tuple-element.91), channel_id=1, source_target_pairs={{0,16},{4,68},{8,24},{12,76},{16,0},{20,84},{24,8},{28,92},{32,48}... | collective-permute-start | bytes 1228808 | tf_op jit(solution)/shard_map/ppermute | solution.py:37
  120.7 12.4 %collective-permute-start.23 = (bf16[160,1280]{1,0:T(8,128)(2,1)}, bf16[160,1280]{1,0:T(8,128)(2,1)S(1)}, u32[]{:S(2)}, u32[]{:S(2)}) collective-permute-start(bf16[160,1280]{1,0:T(8,128)(2,1)} %get-tuple-element.92), channel_id=1, source_target_pairs={{0,24},{4,100},{8,0},{12,108},{16,8},{20,116},{24,16},{28,124},{32... | collective-permute-start | bytes 1228808 | tf_op jit(solution)/shard_map/ppermute | solution.py:37

commit v16 on v14

--- a/solution.py
+++ b/solution.py
@@ -111,7 +111,7 @@
             out_specs=pl.BlockSpec((out_rows, tile), lambda n, which: (0, n)),
         ),
         cost_estimate=FREE,
-        compiler_params=PARAMS,
+        compiler_params=pltpu.CompilerParams(vmem_limit_bytes=42 * 1024 * 1024),
         name="context_product",
     )(jnp.stack(places), *operands)
 
@@ -324,7 +324,7 @@
             scratch_shapes=[pltpu.VMEM((height, tile), F32)],
         ),
         cost_estimate=FREE,
-        compiler_params=pltpu.CompilerParams(vmem_limit_bytes=56 * 1024 * 1024),
+        compiler_params=pltpu.CompilerParams(vmem_limit_bytes=42 * 1024 * 1024),
         name="weight_product",
     )(order, *pieces, *contexts)
 

time: 136 us -> 135 us (level)
  waiting for transfers between devices: 17.1 us -> 19 us
  other arithmetic: 10.2 us -> 8.56 us
    ppermute x9, waiting for transfers between devices: 12.7 us -> 14.6 us  [cross(): return lax.ppermute(value, DP, pairs)]
    pallas_call x1, Pallas kernels: 8.92 us -> 7.47 us  [weight_product(): pl.pallas_call(body, out_shape=[jax.ShapeDtypeStruct((block, width), BF16...]
  transfers between devices with their start and end apart: 27 -> 27, of which waited for: 7 -> 7; matrix products, arithmetic and copies ran while one was open for 13% -> 11% of each run, Pallas kernels for 28% -> 28%
where the time goes in v16:
time: 135 us; the launch traced here: 134 us
  starting transfers between devices  52.7 us (39%)
  Pallas kernels  41.9 us (31%)
  waiting for transfers between devices  19 us (14%)
  local copies, waits for them, and re-layouts  11.1 us (8%)
  other arithmetic  8.56 us (6%)
    ppermute x15, starting transfers between devices, shift(): lax.ppermute(value, axis, [(i, (i + step) % size) for i in range(size)])  21.1 us
    ppermute x9, waiting for transfers between devices, cross(): return lax.ppermute(value, DP, pairs)  14.6 us
    pallas_call x3, Pallas kernels, context_product(): pl.pallas_call(body, out_shape=jax.ShapeDtypeStruct((out_rows, width), dt...  13.3 us
    ppermute x9, starting transfers between devices, cross(): return lax.ppermute(value, DP, pairs)  13.1 us
    all_to_all x2, starting transfers between devices, exchange(): return lax.all_to_all(blocks, DP, split_axis=0, concat_axis=0, tiled=True)  11.2 us
    pallas_call x3, Pallas kernels, forward_product(): pl.pallas_call(body, out_shape=[jax.ShapeDtypeStruct((tile, rows), BF16)]...  9.41 us
    pallas_call x1, Pallas kernels, weight_product(): pl.pallas_call(body, out_shape=[jax.ShapeDtypeStruct((block, width), BF16...  7.47 us
    all_to_all x1, starting transfers between devices, all_shares(): return lax.all_to_all(copies, DP, split_axis=0, concat_axis=0, tiled=True)  7.31 us
  transfers between devices with their start and end apart: 27, of which 7 were waited for; matrix products, arithmetic and copies ran while one was open for 11% of the time, Pallas kernels for 28%

profile of v16, /device:TPU:1, one launch (start us, length us, event | category | flops | bytes accessed | tf_op | source)
XLA Modules:
  0.0 134.3 jit_solution(18137524345039965492)
XLA Ops:
  0.6 2.9 %forward_product.3 = (bf16[640,256]{1,0:T(8,128)(2,1)S(1)}, bf16[640,256]{1,0:T(8,128)(2,1)S(1)}) custom-call(s32[1]{0:T(128)} %bitcast.3.which, bf16[5120,1280]{1,0:T(8,128)(2,1)} %refs_3_.3, bf16[256,1280]{1,0:T(8,128)(2,1)} %context_ref.6), custom_call_target="tpu_custom_call" | custom-call | tf_op jit(solution)/shard_map/forward_product/pallas_call | solution.py:175
  3.6 1.5 %collective-permute-start.2 = (bf16[256,1280]{1,0:T(8,128)(2,1)}, bf16[256,1280]{1,0:T(8,128)(2,1)S(1)}, u32[]{:S(2)}, u32[]{:S(2)}) collective-permute-start(bf16[256,1280]{1,0:T(8,128)(2,1)} %context_ref.6), channel_id=1, source_target_pairs={{0,4},{4,0},{1,5},{5,1},{2,6},{6,2},{3,7},{7,3},{8,12},{12,8},{9,1... | collective-permute-start | bytes 1966088 | tf_op jit(solution)/shard_map/ppermute | solution.py:22
  5.1 1.8 %collective-permute-start = (bf16[640,256]{1,0:T(8,128)(2,1)S(1)}, bf16[640,256]{1,0:T(8,128)(2,1)S(1)}, u32[]{:S(2)}, u32[]{:S(2)}) collective-permute-start(bf16[640,256]{1,0:T(8,128)(2,1)S(1)} %get-tuple-element.47), channel_id=1, source_target_pairs={{0,1},{1,2},{2,3},{3,0},{4,5},{5,6},{6,7},{7,4},{8,9},{9,10},{10,1... | collective-permute-start | bytes 983048 | tf_op jit(solution)/shard_map/ppermute | solution.py:22
  6.8 2.1 %collective-permute-start.1 = (bf16[640,256]{1,0:T(8,128)(2,1)S(1)}, bf16[640,256]{1,0:T(8,128)(2,1)S(1)}, u32[]{:S(2)}, u32[]{:S(2)}) collective-permute-start(bf16[640,256]{1,0:T(8,128)(2,1)S(1)} %get-tuple-element.48), channel_id=1, source_target_pairs={{0,3},{1,0},{2,1},{3,2},{4,7},{5,4},{6,5},{7,6},{8,11},{9,8},{10,9... | collective-permute-start | bytes 983048 | tf_op jit(solution)/shard_map/ppermute | solution.py:22
  8.9 2.9 %forward_product.4.refs_0_ = bf16[1280,256]{1,0:T(8,128)(2,1)S(1)} custom-call(s32[1]{0:T(128)} %bitcast.4.which, bf16[5120,1280]{1,0:T(8,128)(2,1)} %refs_3_.3, bf16[256,1280]{1,0:T(8,128)(2,1)} %context_ref.6), custom_call_target="tpu_custom_call" | custom-call | tf_op jit(solution)/shard_map/forward_product/pallas_call | solution.py:175
  11.8 3.6 %forward_product.5.refs_2_ = bf16[1280,256]{1,0:T(8,128)(2,1)} custom-call(s32[1]{0:T(128)} %bitcast.5.which, bf16[5120,1280]{1,0:T(8,128)(2,1)} %refs_3_.3, bf16[256,1280]{1,0:T(8,128)(2,1)} %context_ref.6), custom_call_target="tpu_custom_call" | custom-call | tf_op jit(solution)/shard_map/forward_product/pallas_call | solution.py:175
  15.4 2.3 %pad_maximum_fusion.refs_4_ = bf16[512,1280]{1,0:T(8,128)(2,1)} fusion(bf16[256,1280]{1,0:T(8,128)(2,1)S(1)} %collective-permute-done.2, bf16[256,1280]{1,0:T(8,128)(2,1)} %context_ref.6), kind=kLoop, calls=%fused_computation | loop fusion | flops 2621440 | bytes 2621440 | tf_op jit(solution)/shard_map/concatenate | solution.py:343
  17.7 1.9 %top_up.1 = (bf16[1280,256]{1,0:T(8,128)(2,1)S(1)}, bf16[1280,256]{1,0:T(8,128)(2,1)}) custom-call(bf16[1280,256]{1,0:T(8,128)(2,1)S(1)} %forward_product.4.refs_0_, bf16[640,256]{1,0:T(8,128)(2,1)S(1)} %collective-permute-done.refs_1_, bf16[1280,256]{1,0:T(8,128)(2,1)} %forward_product.5.refs_2_, ...), custom_call_target="tpu_custom_call", output_to_operand_aliasing={{0}: (0, {}), {1}: (2, {})} | custom-call | tf_op jit(solution)/shard_map/top_up/pallas_call | solution.py:144
  19.6 2.7 %collective-permute-start.4 = (bf16[1280,256]{1,0:T(8,128)(2,1)}, bf16[1280,256]{1,0:T(8,128)(2,1)}, u32[]{:S(2)}, u32[]{:S(2)}) collective-permute-start(bf16[1280,256]{1,0:T(8,128)(2,1)} %get-tuple-element.55), channel_id=1, source_target_pairs={{0,3},{1,0},{2,1},{3,2},{4,7},{5,4},{6,5},{7,6},{8,11},{9,8},{10,9... | collective-permute-start | bytes 1966088 | tf_op jit(solution)/shard_map/ppermute | solution.py:22
  22.6 1.3 collective-permute-start.8
  23.9 1.5 %collective-permute-start.9 = (bf16[512,1280]{1,0:T(8,128)(2,1)}, bf16[512,1280]{1,0:T(8,128)(2,1)}, u32[]{:S(2)}, u32[]{:S(2)}) collective-permute-start(bf16[512,1280]{1,0:T(8,128)(2,1)} %pad_maximum_fusion.refs_4_), channel_id=1, source_target_pairs={{0,96},{4,28},{8,104},{12,4},{16,112},{20,12},{24,120},{28,20},{32... | collective-permute-start | bytes 3932168 | tf_op jit(solution)/shard_map/ppermute | solution.py:37
  25.4 2.9 %hidden_part.1 = (f32[1280,256]{1,0:T(8,128)S(1)}, f32[1280,256]{1,0:T(8,128)S(1)}) custom-call(s32[1]{0:T(128)} %bitcast.2.which, bf16[5120,1280]{1,0:T(8,128)(2,1)} %refs_3_.3, bf16[256,1280]{1,0:T(8,128)(2,1)} %context_ref.6, bf16[256,1280]{1,0:T(8,128)(2,1)S(1)} %copy-done.4, bf16[256,1280]{1,0:T(8,128)(2,1)S(1)} %copy-done.5, ...), custom_call_target="tpu_custom_call" | custom-call | tf_op jit(solution)/shard_map/hidden_part/pallas_call | solution.py:210
  29.0 7.3 %all-to-all-start = ((f32[32,1,8]{2,1,0:T(1,128)}), f32[32,1,8]{2,1,0:T(1,128)S(1)}, u32[]{:S(2)}, u32[]{:S(2)}) async-start(f32[32,1,8]{2,1,0:T(1,128)} %broadcast_in_dim.16), calls=%async_computation | async-start | bytes 32768 | tf_op jit(solution)/shard_map/all_to_all | solution.py:42
  36.8 1.7 %multiply_reduce_fusion.1 = (f32[256]{0:T(256)S(1)}, f32[256]{0:T(256)S(1)}) fusion(bf16[1280,256]{1,0:T(8,128)(2,1)} %collective-permute-done.4, f32[1280,256]{1,0:T(8,128)S(1)} %get-tuple-element.57, bf16[1280,256]{1,0:T(8,128)(2,1)} %collective-permute-done.3, f32[1280,256]{1,0:T(8,128)S(1)} %get-tuple-element.58), kind=kLoop, calls=%fused_computation.3 | loop fusion | flops 2620928 | bytes 3934208 | tf_op jit(solution)/shard_map/reduce_sum | solution.py:359
  38.6 3.7 %collective-permute-start.6 = (f32[2,256]{1,0:T(2,128)S(1)}, f32[2,256]{1,0:T(2,128)S(1)}, u32[]{:S(2)}, u32[]{:S(2)}) collective-permute-start(f32[2,256]{1,0:T(2,128)S(1)} %pad_maximum_fusion.3), channel_id=1, source_target_pairs={{0,2},{1,3},{2,0},{3,1},{4,6},{5,7},{6,4},{7,5},{8,10},{9,11},{10,... | collective-permute-start | bytes 6152 | tf_op jit(solution)/shard_map/ppermute | solution.py:22
  42.3 3.4 %all-to-all-done = f32[32,1,8]{2,1,0:T(1,128)S(1)} async-done(((f32[32,1,8]{2,1,0:T(1,128)}), f32[32,1,8]{2,1,0:T(1,128)S(1)}, u32[]{:S(2)}, u32[]{:S(2)}) %all-to-all-start) | async-done | bytes 1056 | tf_op jit(solution)/shard_map/all_to_all | solution.py:42
  46.1 1.0 collective-permute-start.13
  47.1 1.6 %subtract_convert_fusion.refs_0_.grad_ref = bf16[1280,256]{1,0:T(8,128)(2,1)S(1)} fusion(f32[1280,256]{1,0:T(8,128)S(1)} %get-tuple-element.58, f32[256]{0:T(256)S(1)} %bitcast.68, f32[256]{0:T(256)S(1)} %bitcast.67, bf16[1280,256]{1,0:T(8,128)(2,1)} %collective-permute-done.4, f32[1280,256]{1,0:T(8,128)S(1)} %get-tuple-element.57, ...), kind=kLoop, calls=%fused_computation.1 | loop fusion | flops 2621440 | bytes 4589568 | tf_op jit(solution)/shard_map/convert_element_type | solution.py:375
  48.9 2.7 %collective-permute-start.11 = (bf16[1280,256]{1,0:T(8,128)(2,1)S(1)}, bf16[1280,256]{1,0:T(8,128)(2,1)S(1)}, u32[]{:S(2)}, u32[]{:S(2)}) collective-permute-start(bf16[1280,256]{1,0:T(8,128)(2,1)S(1)} %subtract_convert_fusion.refs_0_.grad_ref), channel_id=1, source_target_pairs={{0,3},{1,0},{2,1},{3,2},{4,7},{5,4},{6,5},{7,6},{8,11},{9,8},{10,9... | collective-permute-start | bytes 1966088 | tf_op jit(solution)/shard_map/ppermute | solution.py:22
  51.5 2.3 %collective-permute-start.12 = (bf16[640,256]{1,0:T(8,128)(2,1)S(1)}, bf16[640,256]{1,0:T(8,128)(2,1)S(1)}, u32[]{:S(2)}, u32[]{:S(2)}) collective-permute-start(bf16[640,256]{1,0:T(8,128)(2,1)S(1)} %bitcast.61), channel_id=1, source_target_pairs={{0,4},{4,0},{1,5},{5,1},{2,6},{6,2},{3,7},{7,3},{8,12},{12,8},{9,1... | collective-permute-start | bytes 983048 | tf_op jit(solution)/shard_map/ppermute | solution.py:22
  54.2 3.0 %context_product.3.refs_4_ = f32[256,1280]{1,0:T(8,128)S(1)} custom-call(s32[1]{0:T(128)} %bitcast.2.which, bf16[1280,256]{1,0:T(8,128)(2,1)S(1)} %subtract_convert_fusion.refs_0_.grad_ref, bf16[5120,1280]{1,0:T(8,128)(2,1)} %refs_3_.3), custom_call_target="tpu_custom_call" | custom-call | tf_op jit(solution)/shard_map/context_product/pallas_call | solution.py:104
  57.1 1.1 copy-done
  58.2 1.7 %place_rows.1 = bf16[512,1280]{1,0:T(8,128)(2,1)} custom-call(bf16[512,256]{1,0:T(8,128)(2,1)S(1)} %fusion.refs_5_.slots_ref, bf16[1280,256]{1,0:T(8,128)(2,1)S(1)} %subtract_convert_fusion.refs_0_.grad_ref), custom_call_target="tpu_custom_call" | custom-call | tf_op jit(solution)/shard_map/place_rows/pallas_call | solution.py:125
  59.9 6.5 %all-to-all-start.1 = ((bf16[32,16,1280]{2,1,0:T(8,128)(2,1)}), bf16[32,16,1280]{2,1,0:T(8,128)(2,1)}, u32[]{:S(2)}, u32[]{:S(2)}) async-start(bf16[32,16,1280]{2,1,0:T(8,128)(2,1)} %bitcast.35), calls=%async_computation.1 | async-start | bytes 2621440 | tf_op jit(solution)/shard_map/all_to_all | solution.py:58
  67.9 2.7 %collective-permute-start.15 = (bf16[640,256]{1,0:T(8,128)(2,1)}, bf16[640,256]{1,0:T(8,128)(2,1)}, u32[]{:S(2)}, u32[]{:S(2)}) collective-permute-start(bf16[640,256]{1,0:T(8,128)(2,1)} %slice.33), channel_id=1, source_target_pairs={{0,3},{1,0},{2,1},{3,2},{4,7},{5,4},{6,5},{7,6},{8,11},{9,8},{10,9... | collective-permute-start | bytes 983048 | tf_op jit(solution)/shard_map/ppermute | solution.py:22
  70.6 0.9 pad_maximum_fusion.1
  71.5 1.4 %collective-permute-start.16 = (bf16[1280,256]{1,0:T(8,128)(2,1)}, bf16[1280,256]{1,0:T(8,128)(2,1)}, u32[]{:S(2)}, u32[]{:S(2)}) collective-permute-start(bf16[1280,256]{1,0:T(8,128)(2,1)} %bitcast.23), channel_id=1, source_target_pairs={{0,4},{4,0},{1,5},{5,1},{2,6},{6,2},{3,7},{7,3},{8,12},{12,8},{9,1... | collective-permute-start | bytes 1966088 | tf_op jit(solution)/shard_map/ppermute | solution.py:22
  73.0 1.3 copy-done.1
  74.3 5.1 %context_product.4.refs_4_ = f32[256,1280]{1,0:T(8,128)S(1)} custom-call(s32[2]{0:T(128)S(1)} %pad_add_fusion.1.which, bf16[1280,256]{1,0:T(8,128)(2,1)S(1)} %collective-permute-done.11.refs_0_, bf16[1280,256]{1,0:T(8,128)(2,1)S(1)} %collective-permute-done.10.refs_1_, bf16[5120,1280]{1,0:T(8,128)(2,1)} %refs_3_.3, bf16[5120,1280]{1,0:T(8,128)(2,1)} %refs_3_.3, ...), custom_call_target="tpu_custom_call" | custom-call | tf_op jit(solution)/shard_map/context_product/pallas_call | solution.py:104
  79.4 1.1 dynamic-slice_bitcast_fusion.2
  80.7 1.1 fusion.8
  82.2 5.2 %lay_out.1 = (bf16[8,160,256]{2,1,0:T(8,128)(2,1)S(1)}, bf16[8,160,256]{2,1,0:T(8,128)(2,1)}, bf16[8,160,256]{2,1,0:T(8,128)(2,1)}, bf16[8,160,256]{2,1,0:T(8,128)(2,1)}) custom-call(s32[4]{0:T(128)S(1)} %pad_add_fusion.2.where, bf16[4,2,160,256]{3,2,1,0:T(8,128)(2,1)S(1)} %bitcast.49, bf16[4,2,160,256]{3,2,1,0:T(8,128)(2,1)S(1)} %bitcast.53, ...), custom_call_target="tpu_custom_call" | custom-call | tf_op jit(solution)/shard_map/lay_out/pallas_call | solution.py:278
  87.4 0.8 copy-done.2
  88.3 0.9 collective-permute-start.18
  89.2 2.4 %collective-permute-start.19 = (bf16[1280,256]{1,0:T(8,128)(2,1)}, bf16[1280,256]{1,0:T(8,128)(2,1)S(1)}, u32[]{:S(2)}, u32[]{:S(2)}) collective-permute-start(bf16[1280,256]{1,0:T(8,128)(2,1)} %bitcast.32), channel_id=1, source_target_pairs={{0,64},{4,20},{8,72},{12,28},{16,80},{20,4},{24,88},{28,12},{32,96... | collective-permute-start | bytes 1966088 | tf_op jit(solution)/shard_map/ppermute | solution.py:37
  91.6 1.2 collective-permute-start.20
  92.9 5.3 %context_product.5 = bf16[512,1280]{1,0:T(8,128)(2,1)} custom-call(s32[2]{0:T(128)S(1)} %pad_add_fusion.which, bf16[640,256]{1,0:T(8,128)(2,1)} %collective-permute-done.14.refs_0_, bf16[640,256]{1,0:T(8,128)(2,1)} %collective-permute-done.15.refs_1_, bf16[5120,1280]{1,0:T(8,128)(2,1)} %refs_3_.3, bf16[5120,1280]{1,0:T(8,128)(2,1)} %refs_3_.3, ...), custom_call_target="tpu_custom_call" | custom-call | tf_op jit(solution)/shard_map/context_product/pallas_call | solution.py:104
  98.2 2.2 %reshape.171 = bf16[384,1280]{1,0:T(8,128)(2,1)} reshape(bf16[32,12,1280]{2,1,0:T(8,128)(2,1)} %bitcast.46) | data formatting | bytes 1966080 | tf_op jit(solution)/shard_map/reshape | solution.py:63
  100.4 4.7 %all-to-all-start.2 = ((bf16[32,16,1280]{2,1,0:T(8,128)(2,1)}), bf16[32,16,1280]{2,1,0:T(8,128)(2,1)S(1)}, u32[]{:S(2)}, u32[]{:S(2)}) async-start(bf16[32,16,1280]{2,1,0:T(8,128)(2,1)} %bitcast.36), calls=%async_computation.2 | async-start | bytes 2621440 | tf_op jit(solution)/shard_map/all_to_all | solution.py:58
  105.3 1.6 %collective-permute-done.19.refs_2_ = bf16[1280,256]{1,0:T(8,128)(2,1)S(1)} collective-permute-done((bf16[1280,256]{1,0:T(8,128)(2,1)}, bf16[1280,256]{1,0:T(8,128)(2,1)S(1)}, u32[]{:S(2)}, u32[]{:S(2)}) %collective-permute-start.19) | collective-permute-done | bytes 655392 | tf_op jit(solution)/shard_map/ppermute | solution.py:37
  106.9 7.5 %weight_product.1 = (f32[160,1280]{1,0:T(8,128)S(1)}, bf16[160,1280]{1,0:T(8,128)(2,1)S(1)}, bf16[160,1280]{1,0:T(8,128)(2,1)S(1)}, bf16[160,1280]{1,0:T(8,128)(2,1)S(1)}) custom-call(s32[4]{0:T(128)S(1)} %pad_add_fusion.3.order_ref, bf16[1280,256]{1,0:T(8,128)(2,1)S(1)} %bitcast.56, bf16[1280,256]{1,0:T(8,128)(2,1)S(1)} %collective-permute-done.18.refs_1_, ...), custom_call_target="tpu_custom_call" | custom-call | tf_op jit(solution)/shard_map/weight_product/pallas_call | solution.py:315
  114.4 1.2 collective-permute-start.21
  115.6 2.5 %collective-permute-start.22 = (bf16[160,1280]{1,0:T(8,128)(2,1)S(1)}, bf16[160,1280]{1,0:T(8,128)(2,1)S(1)}, u32[]{:S(2)}, u32[]{:S(2)}) collective-permute-start(bf16[160,1280]{1,0:T(8,128)(2,1)S(1)} %get-tuple-element.89), channel_id=1, source_target_pairs={{0,16},{4,68},{8,24},{12,76},{16,0},{20,84},{24,8},{28,92},{32,48}... | collective-permute-start | bytes 1228808 | tf_op jit(solution)/shard_map/ppermute | solution.py:37
  118.0 1.1 collective-permute-start.23
  119.2 8.3 %collective-permute-done.21 = bf16[160,1280]{1,0:T(8,128)(2,1)S(1)} collective-permute-done((bf16[160,1280]{1,0:T(8,128)(2,1)S(1)}, bf16[160,1280]{1,0:T(8,128)(2,1)S(1)}, u32[]{:S(2)}, u32[]{:S(2)}) %collective-permute-start.21) | collective-permute-done | bytes 409632 | tf_op jit(solution)/shard_map/ppermute | solution.py:37
  127.5 4.6 %collective-permute-done.22 = bf16[160,1280]{1,0:T(8,128)(2,1)S(1)} collective-permute-done((bf16[160,1280]{1,0:T(8,128)(2,1)S(1)}, bf16[160,1280]{1,0:T(8,128)(2,1)S(1)}, u32[]{:S(2)}, u32[]{:S(2)}) %collective-permute-start.22) | collective-permute-done | bytes 409632 | tf_op jit(solution)/shard_map/ppermute | solution.py:37
  132.1 1.1 add_multiply_fusion
  133.2 1.1 reshape.173
  (78 shorter events, 4.8 us)
Async XLA Ops:
  3.6 11.8 %collective-permute-start.2 = (bf16[256,1280]{1,0:T(8,128)(2,1)}, bf16[256,1280]{1,0:T(8,128)(2,1)S(1)}, u32[]{:S(2)}, u32[]{:S(2)}) collective-permute-start(bf16[256,1280]{1,0:T(8,128)(2,1)} %context_ref.6), channel_id=1, source_target_pairs={{0,4},{4,0},{1,5},{5,1},{2,6},{6,2},{3,7},{7,3},{8,12},{12,8},{9,1... | collective-permute-start | bytes 1966088 | tf_op jit(solution)/shard_map/ppermute | solution.py:22
  5.1 12.6 %collective-permute-start = (bf16[640,256]{1,0:T(8,128)(2,1)S(1)}, bf16[640,256]{1,0:T(8,128)(2,1)S(1)}, u32[]{:S(2)}, u32[]{:S(2)}) collective-permute-start(bf16[640,256]{1,0:T(8,128)(2,1)S(1)} %get-tuple-element.47), channel_id=1, source_target_pairs={{0,1},{1,2},{2,3},{3,0},{4,5},{5,6},{6,7},{7,4},{8,9},{9,10},{10,1... | collective-permute-start | bytes 983048 | tf_op jit(solution)/shard_map/ppermute | solution.py:22
  6.8 10.9 %collective-permute-start.1 = (bf16[640,256]{1,0:T(8,128)(2,1)S(1)}, bf16[640,256]{1,0:T(8,128)(2,1)S(1)}, u32[]{:S(2)}, u32[]{:S(2)}) collective-permute-start(bf16[640,256]{1,0:T(8,128)(2,1)S(1)} %get-tuple-element.48), channel_id=1, source_target_pairs={{0,3},{1,0},{2,1},{3,2},{4,7},{5,4},{6,5},{7,6},{8,11},{9,8},{10,9... | collective-permute-start | bytes 983048 | tf_op jit(solution)/shard_map/ppermute | solution.py:22
  17.7 4.6 %copy-start.8 = (f32[1280]{0:T(1024)S(1)}, f32[1280]{0:T(1024)}, u32[]{:S(2)}) copy-start(f32[1280]{0:T(1024)} %param.13) | copy-start | bytes 15364
  17.7 4.6 %copy-start.12 = (s32[64,1]{0,1:T(1,128)S(1)}, s32[64,1]{0,1:T(1,128)}, u32[]{:S(2)}) copy-start(s32[64,1]{0,1:T(1,128)} %param.17) | copy-start | bytes 772
  17.7 4.8 %copy-start.10 = (f32[4]{0:T(128)S(1)}, f32[4]{0:T(128)}, u32[]{:S(2)}) copy-start(f32[4]{0:T(128)} %param.14) | copy-start | bytes 52
  17.7 4.8 %copy-start.11 = (s32[4]{0:T(128)S(1)}, s32[4]{0:T(128)}, u32[]{:S(2)}) copy-start(s32[4]{0:T(128)} %param.15) | copy-start | bytes 52
  17.7 7.7 %copy-start.4 = (bf16[256,1280]{1,0:T(8,128)(2,1)S(1)}, bf16[256,1280]{1,0:T(8,128)(2,1)}, u32[]{:S(2)}) copy-start(bf16[256,1280]{1,0:T(8,128)(2,1)} %residual_ref.1) | copy-start | bytes 1966084
  17.7 7.7 %copy-start.5 = (bf16[256,1280]{1,0:T(8,128)(2,1)S(1)}, bf16[256,1280]{1,0:T(8,128)(2,1)}, u32[]{:S(2)}) copy-start(bf16[256,1280]{1,0:T(8,128)(2,1)} %cotangent_ref.1) | copy-start | bytes 1966084
  19.6 17.2 %collective-permute-start.3 = (bf16[1280,256]{1,0:T(8,128)(2,1)S(1)}, bf16[1280,256]{1,0:T(8,128)(2,1)}, u32[]{:S(2)}, u32[]{:S(2)}) collective-permute-start(bf16[1280,256]{1,0:T(8,128)(2,1)S(1)} %get-tuple-element.54), channel_id=1, source_target_pairs={{0,1},{1,2},{2,3},{3,0},{4,5},{5,6},{6,7},{7,4},{8,9},{9,10},{10,1... | collective-permute-start | bytes 1966088 | tf_op jit(solution)/shard_map/ppermute | solution.py:22
  19.6 17.2 %collective-permute-start.4 = (bf16[1280,256]{1,0:T(8,128)(2,1)}, bf16[1280,256]{1,0:T(8,128)(2,1)}, u32[]{:S(2)}, u32[]{:S(2)}) collective-permute-start(bf16[1280,256]{1,0:T(8,128)(2,1)} %get-tuple-element.55), channel_id=1, source_target_pairs={{0,3},{1,0},{2,1},{3,2},{4,7},{5,4},{6,5},{7,6},{8,11},{9,8},{10,9... | collective-permute-start | bytes 1966088 | tf_op jit(solution)/shard_map/ppermute | solution.py:22
  22.6 26.2 %collective-permute-start.8 = (bf16[512,1280]{1,0:T(8,128)(2,1)}, bf16[512,1280]{1,0:T(8,128)(2,1)}, u32[]{:S(2)}, u32[]{:S(2)}) collective-permute-start(bf16[512,1280]{1,0:T(8,128)(2,1)} %pad_maximum_fusion.refs_4_), channel_id=1, source_target_pairs={{0,32},{4,12},{8,40},{12,20},{16,48},{20,28},{24,56},{28,4},{32,64... | collective-permute-start | bytes 3932168 | tf_op jit(solution)/shard_map/ppermute | solution.py:37
  23.9 24.9 %collective-permute-start.9 = (bf16[512,1280]{1,0:T(8,128)(2,1)}, bf16[512,1280]{1,0:T(8,128)(2,1)}, u32[]{:S(2)}, u32[]{:S(2)}) collective-permute-start(bf16[512,1280]{1,0:T(8,128)(2,1)} %pad_maximum_fusion.refs_4_), channel_id=1, source_target_pairs={{0,96},{4,28},{8,104},{12,4},{16,112},{20,12},{24,120},{28,20},{32... | collective-permute-start | bytes 3932168 | tf_op jit(solution)/shard_map/ppermute | solution.py:37
  29.0 16.8 %all-to-all-start = ((f32[32,1,8]{2,1,0:T(1,128)}), f32[32,1,8]{2,1,0:T(1,128)S(1)}, u32[]{:S(2)}, u32[]{:S(2)}) async-start(f32[32,1,8]{2,1,0:T(1,128)} %broadcast_in_dim.16), calls=%async_computation | async-start | bytes 32768 | tf_op jit(solution)/shard_map/all_to_all | solution.py:42
  36.8 9.1 %copy-start.9 = (s32[4]{0:T(128)S(1)}, s32[4]{0:T(128)}, u32[]{:S(2)}) copy-start(s32[4]{0:T(128)} %param.16) | copy-start | bytes 52
  38.5 7.6 %collective-permute-start.5 = (f32[2,256]{1,0:T(2,128)S(1)}, f32[2,256]{1,0:T(2,128)S(1)}, u32[]{:S(2)}, u32[]{:S(2)}) collective-permute-start(f32[2,256]{1,0:T(2,128)S(1)} %pad_maximum_fusion.3), channel_id=1, source_target_pairs={{0,1},{1,2},{2,3},{3,0},{4,5},{5,6},{6,7},{7,4},{8,9},{9,10},{10,1... | collective-permute-start | bytes 6152 | tf_op jit(solution)/shard_map/ppermute | solution.py:22
  38.6 8.5 %collective-permute-start.6 = (f32[2,256]{1,0:T(2,128)S(1)}, f32[2,256]{1,0:T(2,128)S(1)}, u32[]{:S(2)}, u32[]{:S(2)}) collective-permute-start(f32[2,256]{1,0:T(2,128)S(1)} %pad_maximum_fusion.3), channel_id=1, source_target_pairs={{0,2},{1,3},{2,0},{3,1},{4,6},{5,7},{6,4},{7,5},{8,10},{9,11},{10,... | collective-permute-start | bytes 6152 | tf_op jit(solution)/shard_map/ppermute | solution.py:22
  42.3 4.8 %collective-permute-start.7 = (f32[2,256]{1,0:T(2,128)S(1)}, f32[2,256]{1,0:T(2,128)S(1)}, u32[]{:S(2)}, u32[]{:S(2)}) collective-permute-start(f32[2,256]{1,0:T(2,128)S(1)} %pad_maximum_fusion.3), channel_id=1, source_target_pairs={{0,3},{1,0},{2,1},{3,2},{4,7},{5,4},{6,5},{7,6},{8,11},{9,8},{10,9... | collective-permute-start | bytes 6152 | tf_op jit(solution)/shard_map/ppermute | solution.py:22
  46.1 20.3 %collective-permute-start.13 = (bf16[512,1280]{1,0:T(8,128)(2,1)}, bf16[512,1280]{1,0:T(8,128)(2,1)}, u32[]{:S(2)}, u32[]{:S(2)}) collective-permute-start(bf16[512,1280]{1,0:T(8,128)(2,1)} %pad_maximum_fusion.refs_4_), channel_id=1, source_target_pairs={{0,64},{4,20},{8,72},{12,28},{16,80},{20,4},{24,88},{28,12},{32,96... | collective-permute-start | bytes 3932168 | tf_op jit(solution)/shard_map/ppermute | solution.py:37
  48.8 17.6 %collective-permute-start.10 = (bf16[1280,256]{1,0:T(8,128)(2,1)S(1)}, bf16[1280,256]{1,0:T(8,128)(2,1)S(1)}, u32[]{:S(2)}, u32[]{:S(2)}) collective-permute-start(bf16[1280,256]{1,0:T(8,128)(2,1)S(1)} %subtract_convert_fusion.refs_0_.grad_ref), channel_id=1, source_target_pairs={{0,1},{1,2},{2,3},{3,0},{4,5},{5,6},{6,7},{7,4},{8,9},{9,10},{10,1... | collective-permute-start | bytes 1966088 | tf_op jit(solution)/shard_map/ppermute | solution.py:22
  48.9 17.5 %collective-permute-start.11 = (bf16[1280,256]{1,0:T(8,128)(2,1)S(1)}, bf16[1280,256]{1,0:T(8,128)(2,1)S(1)}, u32[]{:S(2)}, u32[]{:S(2)}) collective-permute-start(bf16[1280,256]{1,0:T(8,128)(2,1)S(1)} %subtract_convert_fusion.refs_0_.grad_ref), channel_id=1, source_target_pairs={{0,3},{1,0},{2,1},{3,2},{4,7},{5,4},{6,5},{7,6},{8,11},{9,8},{10,9... | collective-permute-start | bytes 1966088 | tf_op jit(solution)/shard_map/ppermute | solution.py:22
  51.5 6.7 %collective-permute-start.12 = (bf16[640,256]{1,0:T(8,128)(2,1)S(1)}, bf16[640,256]{1,0:T(8,128)(2,1)S(1)}, u32[]{:S(2)}, u32[]{:S(2)}) collective-permute-start(bf16[640,256]{1,0:T(8,128)(2,1)S(1)} %bitcast.61), channel_id=1, source_target_pairs={{0,4},{4,0},{1,5},{5,1},{2,6},{6,2},{3,7},{7,3},{8,12},{12,8},{9,1... | collective-permute-start | bytes 983048 | tf_op jit(solution)/shard_map/ppermute | solution.py:22
  57.1 1.1 copy-start
  58.2 1.7 %copy-start.6 = (bf16[640,256]{1,0:T(8,128)(2,1)}, bf16[640,256]{1,0:T(8,128)(2,1)S(1)}, u32[]{:S(2)}) copy-start(bf16[640,256]{1,0:T(8,128)(2,1)S(1)} %collective-permute-done.12) | copy-start | bytes 983044
  59.9 38.3 %all-to-all-start.1 = ((bf16[32,16,1280]{2,1,0:T(8,128)(2,1)}), bf16[32,16,1280]{2,1,0:T(8,128)(2,1)}, u32[]{:S(2)}, u32[]{:S(2)}) async-start(bf16[32,16,1280]{2,1,0:T(8,128)(2,1)} %bitcast.35), calls=%async_computation.1 | async-start | bytes 2621440 | tf_op jit(solution)/shard_map/all_to_all | solution.py:58
  67.1 12.2 %collective-permute-start.14 = (bf16[640,256]{1,0:T(8,128)(2,1)}, bf16[640,256]{1,0:T(8,128)(2,1)}, u32[]{:S(2)}, u32[]{:S(2)}) collective-permute-start(bf16[640,256]{1,0:T(8,128)(2,1)} %slice.32), channel_id=1, source_target_pairs={{0,1},{1,2},{2,3},{3,0},{4,5},{5,6},{6,7},{7,4},{8,9},{9,10},{10,1... | collective-permute-start | bytes 983048 | tf_op jit(solution)/shard_map/ppermute | solution.py:22
  67.9 11.5 %collective-permute-start.15 = (bf16[640,256]{1,0:T(8,128)(2,1)}, bf16[640,256]{1,0:T(8,128)(2,1)}, u32[]{:S(2)}, u32[]{:S(2)}) collective-permute-start(bf16[640,256]{1,0:T(8,128)(2,1)} %slice.33), channel_id=1, source_target_pairs={{0,3},{1,0},{2,1},{3,2},{4,7},{5,4},{6,5},{7,6},{8,11},{9,8},{10,9... | collective-permute-start | bytes 983048 | tf_op jit(solution)/shard_map/ppermute | solution.py:22
  71.5 9.1 %collective-permute-start.16 = (bf16[1280,256]{1,0:T(8,128)(2,1)}, bf16[1280,256]{1,0:T(8,128)(2,1)}, u32[]{:S(2)}, u32[]{:S(2)}) collective-permute-start(bf16[1280,256]{1,0:T(8,128)(2,1)} %bitcast.23), channel_id=1, source_target_pairs={{0,4},{4,0},{1,5},{5,1},{2,6},{6,2},{3,7},{7,3},{8,12},{12,8},{9,1... | collective-permute-start | bytes 1966088 | tf_op jit(solution)/shard_map/ppermute | solution.py:22
  73.0 1.3 copy-start.1
  79.4 2.8 %copy-start.7 = (bf16[640,256]{1,0:T(8,128)(2,1)S(1)}, bf16[640,256]{1,0:T(8,128)(2,1)}, u32[]{:S(2)}) copy-start(bf16[640,256]{1,0:T(8,128)(2,1)} %copy-done.6) | copy-start | bytes 983044
  80.5 1.7 %collective-permute-start.17 = (bf16[640,256]{1,0:T(8,128)(2,1)S(1)}, bf16[640,256]{1,0:T(8,128)(2,1)S(1)}, u32[]{:S(2)}, u32[]{:S(2)}) collective-permute-start(bf16[640,256]{1,0:T(8,128)(2,1)S(1)} %bitcast.60), channel_id=1, source_target_pairs={{0,4},{4,0},{1,5},{5,1},{2,6},{6,2},{3,7},{7,3},{8,12},{12,8},{9,1... | collective-permute-start | bytes 983048 | tf_op jit(solution)/shard_map/ppermute | solution.py:22
  87.4 0.9 copy-start.2
  88.3 17.0 %collective-permute-start.18 = (bf16[1280,256]{1,0:T(8,128)(2,1)}, bf16[1280,256]{1,0:T(8,128)(2,1)S(1)}, u32[]{:S(2)}, u32[]{:S(2)}) collective-permute-start(bf16[1280,256]{1,0:T(8,128)(2,1)} %bitcast.31), channel_id=1, source_target_pairs={{0,32},{4,12},{8,40},{12,20},{16,48},{20,28},{24,56},{28,4},{32,64... | collective-permute-start | bytes 1966088 | tf_op jit(solution)/shard_map/ppermute | solution.py:37
  89.2 17.6 %collective-permute-start.19 = (bf16[1280,256]{1,0:T(8,128)(2,1)}, bf16[1280,256]{1,0:T(8,128)(2,1)S(1)}, u32[]{:S(2)}, u32[]{:S(2)}) collective-permute-start(bf16[1280,256]{1,0:T(8,128)(2,1)} %bitcast.32), channel_id=1, source_target_pairs={{0,64},{4,20},{8,72},{12,28},{16,80},{20,4},{24,88},{28,12},{32,96... | collective-permute-start | bytes 1966088 | tf_op jit(solution)/shard_map/ppermute | solution.py:37
  91.6 15.3 %collective-permute-start.20 = (bf16[1280,256]{1,0:T(8,128)(2,1)}, bf16[1280,256]{1,0:T(8,128)(2,1)}, u32[]{:S(2)}, u32[]{:S(2)}) collective-permute-start(bf16[1280,256]{1,0:T(8,128)(2,1)} %bitcast.33), channel_id=1, source_target_pairs={{0,96},{4,28},{8,104},{12,4},{16,112},{20,12},{24,120},{28,20},{32... | collective-permute-start | bytes 1966088 | tf_op jit(solution)/shard_map/ppermute | solution.py:37
  100.4 6.5 %copy-start.3 = (bf16[8,160,256]{2,1,0:T(8,128)(2,1)S(1)}, bf16[8,160,256]{2,1,0:T(8,128)(2,1)}, u32[]{:S(2)}) copy-start(bf16[8,160,256]{2,1,0:T(8,128)(2,1)} %copy-done.2) | copy-start | bytes 1966084
  100.4 32.8 %all-to-all-start.2 = ((bf16[32,16,1280]{2,1,0:T(8,128)(2,1)}), bf16[32,16,1280]{2,1,0:T(8,128)(2,1)S(1)}, u32[]{:S(2)}, u32[]{:S(2)}) async-start(bf16[32,16,1280]{2,1,0:T(8,128)(2,1)} %bitcast.36), calls=%async_computation.2 | async-start | bytes 2621440 | tf_op jit(solution)/shard_map/all_to_all | solution.py:58
  114.4 13.1 %collective-permute-start.21 = (bf16[160,1280]{1,0:T(8,128)(2,1)S(1)}, bf16[160,1280]{1,0:T(8,128)(2,1)S(1)}, u32[]{:S(2)}, u32[]{:S(2)}) collective-permute-start(bf16[160,1280]{1,0:T(8,128)(2,1)S(1)} %get-tuple-element.88), channel_id=1, source_target_pairs={{0,8},{4,36},{8,16},{12,44},{16,24},{20,52},{24,0},{28,60},{32,40}... | collective-permute-start | bytes 1228808 | tf_op jit(solution)/shard_map/ppermute | solution.py:37
  115.6 16.6 %collective-permute-start.22 = (bf16[160,1280]{1,0:T(8,128)(2,1)S(1)}, bf16[160,1280]{1,0:T(8,128)(2,1)S(1)}, u32[]{:S(2)}, u32[]{:S(2)}) collective-permute-start(bf16[160,1280]{1,0:T(8,128)(2,1)S(1)} %get-tuple-element.89), channel_id=1, source_target_pairs={{0,16},{4,68},{8,24},{12,76},{16,0},{20,84},{24,8},{28,92},{32,48}... | collective-permute-start | bytes 1228808 | tf_op jit(solution)/shard_map/ppermute | solution.py:37
  118.0 14.1 %collective-permute-start.23 = (bf16[160,1280]{1,0:T(8,128)(2,1)S(1)}, bf16[160,1280]{1,0:T(8,128)(2,1)S(1)}, u32[]{:S(2)}, u32[]{:S(2)}) collective-permute-start(bf16[160,1280]{1,0:T(8,128)(2,1)S(1)} %get-tuple-element.90), channel_id=1, source_target_pairs={{0,24},{4,100},{8,0},{12,108},{16,8},{20,116},{24,16},{28,124},{32... | collective-permute-start | bytes 1228808 | tf_op jit(solution)/shard_map/ppermute | solution.py:37

commit v17 on v16

--- a/solution.py
+++ b/solution.py
@@ -411,7 +411,9 @@
     ]
     sends = lay_out((0, 1, 2, 3), chunks, siblings, x, y, c, z)
     far_left, far_right, sends = lax.optimization_barrier((far_left, far_right, sends))
-    pieces = [sends[0]] + [cross(sends[k], k, True) for k in (1, 2, 3)]
+    pieces = [sends[0], None, None, None]
+    for k in (2, 1, 3):
+        pieces[k] = cross(sends[k], k, True)
     far_place = (z + 2) % NZ * 2
     placed = context_product(
         [far_left, far_right], [far_place, far_place + 1], out_proj, before=context_grad, slots=slots
@@ -420,7 +422,7 @@
     d_context = exchange(placed, lanes)
     order = [jnp.where(c == 0, (y + k) % NY, (x + k - z) % NZ) for k in range(4)]
     d_out_proj, *parts = weight_product(pieces, contexts, jnp.stack(order), block)
-    parts = [cross(part, k, False) for k, part in zip((1, 2, 3), parts)]
+    parts = [cross(parts[k - 1], k, False) for k in (2, 1, 3)]
     for part in parts:
         d_out_proj = d_out_proj + part.astype(F32)
     return (learner_rows(d_context), d_residual, d_out_proj / lanes)

time: 135 us -> 135 us (level)
  no operation moved by 1% of the time
where the time goes in v17:
time: 135 us; the launch traced here: 134 us
  starting transfers between devices  53.3 us (39%)
  Pallas kernels  41.9 us (31%)
  waiting for transfers between devices  18.1 us (13%)
  local copies, waits for them, and re-layouts  11.1 us (8%)
  other arithmetic  8.56 us (6%)
    ppermute x15, starting transfers between devices, shift(): lax.ppermute(value, axis, [(i, (i + step) % size) for i in range(size)])  21.1 us
    ppermute x9, starting transfers between devices, cross(): return lax.ppermute(value, DP, pairs)  13.8 us
    ppermute x9, waiting for transfers between devices, cross(): return lax.ppermute(value, DP, pairs)  13.7 us
    pallas_call x3, Pallas kernels, context_product(): pl.pallas_call(body, out_shape=jax.ShapeDtypeStruct((out_rows, width), dt...  13.3 us
    all_to_all x2, starting transfers between devices, exchange(): return lax.all_to_all(blocks, DP, split_axis=0, concat_axis=0, tiled=True)  11.2 us
    pallas_call x3, Pallas kernels, forward_product(): pl.pallas_call(body, out_shape=[jax.ShapeDtypeStruct((tile, rows), BF16)]...  9.41 us
    pallas_call x1, Pallas kernels, weight_product(): pl.pallas_call(body, out_shape=[jax.ShapeDtypeStruct((block, width), BF16...  7.47 us
    all_to_all x1, starting transfers between devices, all_shares(): return lax.all_to_all(copies, DP, split_axis=0, concat_axis=0, tiled=True)  7.31 us
  transfers between devices with their start and end apart: 27, of which 7 were waited for; matrix products, arithmetic and copies ran while one was open for 11% of the time, Pallas kernels for 28%

profile of v17, /device:TPU:1, one launch (start us, length us, event | category | flops | bytes accessed | tf_op | source)
XLA Modules:
  0.0 134.0 jit_solution(12996371168809976180)
XLA Ops:
  0.6 2.9 %forward_product.3 = (bf16[640,256]{1,0:T(8,128)(2,1)S(1)}, bf16[640,256]{1,0:T(8,128)(2,1)S(1)}) custom-call(s32[1]{0:T(128)} %bitcast.3.which, bf16[5120,1280]{1,0:T(8,128)(2,1)} %refs_3_.3, bf16[256,1280]{1,0:T(8,128)(2,1)} %context_ref.6), custom_call_target="tpu_custom_call" | custom-call | tf_op jit(solution)/shard_map/forward_product/pallas_call | solution.py:175
  3.6 1.5 %collective-permute-start.2 = (bf16[256,1280]{1,0:T(8,128)(2,1)}, bf16[256,1280]{1,0:T(8,128)(2,1)S(1)}, u32[]{:S(2)}, u32[]{:S(2)}) collective-permute-start(bf16[256,1280]{1,0:T(8,128)(2,1)} %context_ref.6), channel_id=1, source_target_pairs={{0,4},{4,0},{1,5},{5,1},{2,6},{6,2},{3,7},{7,3},{8,12},{12,8},{9,1... | collective-permute-start | bytes 1966088 | tf_op jit(solution)/shard_map/ppermute | solution.py:22
  5.1 1.8 %collective-permute-start = (bf16[640,256]{1,0:T(8,128)(2,1)S(1)}, bf16[640,256]{1,0:T(8,128)(2,1)S(1)}, u32[]{:S(2)}, u32[]{:S(2)}) collective-permute-start(bf16[640,256]{1,0:T(8,128)(2,1)S(1)} %get-tuple-element.47), channel_id=1, source_target_pairs={{0,1},{1,2},{2,3},{3,0},{4,5},{5,6},{6,7},{7,4},{8,9},{9,10},{10,1... | collective-permute-start | bytes 983048 | tf_op jit(solution)/shard_map/ppermute | solution.py:22
  6.8 2.1 %collective-permute-start.1 = (bf16[640,256]{1,0:T(8,128)(2,1)S(1)}, bf16[640,256]{1,0:T(8,128)(2,1)S(1)}, u32[]{:S(2)}, u32[]{:S(2)}) collective-permute-start(bf16[640,256]{1,0:T(8,128)(2,1)S(1)} %get-tuple-element.48), channel_id=1, source_target_pairs={{0,3},{1,0},{2,1},{3,2},{4,7},{5,4},{6,5},{7,6},{8,11},{9,8},{10,9... | collective-permute-start | bytes 983048 | tf_op jit(solution)/shard_map/ppermute | solution.py:22
  8.9 2.9 %forward_product.4.refs_0_ = bf16[1280,256]{1,0:T(8,128)(2,1)S(1)} custom-call(s32[1]{0:T(128)} %bitcast.4.which, bf16[5120,1280]{1,0:T(8,128)(2,1)} %refs_3_.3, bf16[256,1280]{1,0:T(8,128)(2,1)} %context_ref.6), custom_call_target="tpu_custom_call" | custom-call | tf_op jit(solution)/shard_map/forward_product/pallas_call | solution.py:175
  11.8 3.6 %forward_product.5.refs_2_ = bf16[1280,256]{1,0:T(8,128)(2,1)} custom-call(s32[1]{0:T(128)} %bitcast.5.which, bf16[5120,1280]{1,0:T(8,128)(2,1)} %refs_3_.3, bf16[256,1280]{1,0:T(8,128)(2,1)} %context_ref.6), custom_call_target="tpu_custom_call" | custom-call | tf_op jit(solution)/shard_map/forward_product/pallas_call | solution.py:175
  15.4 2.3 %pad_maximum_fusion.refs_4_ = bf16[512,1280]{1,0:T(8,128)(2,1)} fusion(bf16[256,1280]{1,0:T(8,128)(2,1)S(1)} %collective-permute-done.2, bf16[256,1280]{1,0:T(8,128)(2,1)} %context_ref.6), kind=kLoop, calls=%fused_computation | loop fusion | flops 2621440 | bytes 2621440 | tf_op jit(solution)/shard_map/concatenate | solution.py:343
  17.7 1.9 %top_up.1 = (bf16[1280,256]{1,0:T(8,128)(2,1)S(1)}, bf16[1280,256]{1,0:T(8,128)(2,1)}) custom-call(bf16[1280,256]{1,0:T(8,128)(2,1)S(1)} %forward_product.4.refs_0_, bf16[640,256]{1,0:T(8,128)(2,1)S(1)} %collective-permute-done.refs_1_, bf16[1280,256]{1,0:T(8,128)(2,1)} %forward_product.5.refs_2_, ...), custom_call_target="tpu_custom_call", output_to_operand_aliasing={{0}: (0, {}), {1}: (2, {})} | custom-call | tf_op jit(solution)/shard_map/top_up/pallas_call | solution.py:144
  19.6 2.7 %collective-permute-start.4 = (bf16[1280,256]{1,0:T(8,128)(2,1)}, bf16[1280,256]{1,0:T(8,128)(2,1)}, u32[]{:S(2)}, u32[]{:S(2)}) collective-permute-start(bf16[1280,256]{1,0:T(8,128)(2,1)} %get-tuple-element.55), channel_id=1, source_target_pairs={{0,3},{1,0},{2,1},{3,2},{4,7},{5,4},{6,5},{7,6},{8,11},{9,8},{10,9... | collective-permute-start | bytes 1966088 | tf_op jit(solution)/shard_map/ppermute | solution.py:22
  22.6 1.3 collective-permute-start.8
  23.9 1.5 %collective-permute-start.9 = (bf16[512,1280]{1,0:T(8,128)(2,1)}, bf16[512,1280]{1,0:T(8,128)(2,1)}, u32[]{:S(2)}, u32[]{:S(2)}) collective-permute-start(bf16[512,1280]{1,0:T(8,128)(2,1)} %pad_maximum_fusion.refs_4_), channel_id=1, source_target_pairs={{0,96},{4,28},{8,104},{12,4},{16,112},{20,12},{24,120},{28,20},{32... | collective-permute-start | bytes 3932168 | tf_op jit(solution)/shard_map/ppermute | solution.py:37
  25.4 2.9 %hidden_part.1 = (f32[1280,256]{1,0:T(8,128)S(1)}, f32[1280,256]{1,0:T(8,128)S(1)}) custom-call(s32[1]{0:T(128)} %bitcast.2.which, bf16[5120,1280]{1,0:T(8,128)(2,1)} %refs_3_.3, bf16[256,1280]{1,0:T(8,128)(2,1)} %context_ref.6, bf16[256,1280]{1,0:T(8,128)(2,1)S(1)} %copy-done.4, bf16[256,1280]{1,0:T(8,128)(2,1)S(1)} %copy-done.5, ...), custom_call_target="tpu_custom_call" | custom-call | tf_op jit(solution)/shard_map/hidden_part/pallas_call | solution.py:210
  29.0 7.3 %all-to-all-start = ((f32[32,1,8]{2,1,0:T(1,128)}), f32[32,1,8]{2,1,0:T(1,128)S(1)}, u32[]{:S(2)}, u32[]{:S(2)}) async-start(f32[32,1,8]{2,1,0:T(1,128)} %broadcast_in_dim.16), calls=%async_computation | async-start | bytes 32768 | tf_op jit(solution)/shard_map/all_to_all | solution.py:42
  36.8 1.7 %multiply_reduce_fusion.1 = (f32[256]{0:T(256)S(1)}, f32[256]{0:T(256)S(1)}) fusion(bf16[1280,256]{1,0:T(8,128)(2,1)} %collective-permute-done.4, f32[1280,256]{1,0:T(8,128)S(1)} %get-tuple-element.57, bf16[1280,256]{1,0:T(8,128)(2,1)} %collective-permute-done.3, f32[1280,256]{1,0:T(8,128)S(1)} %get-tuple-element.58), kind=kLoop, calls=%fused_computation.3 | loop fusion | flops 2620928 | bytes 3934208 | tf_op jit(solution)/shard_map/reduce_sum | solution.py:359
  38.6 3.7 %collective-permute-start.6 = (f32[2,256]{1,0:T(2,128)S(1)}, f32[2,256]{1,0:T(2,128)S(1)}, u32[]{:S(2)}, u32[]{:S(2)}) collective-permute-start(f32[2,256]{1,0:T(2,128)S(1)} %pad_maximum_fusion.3), channel_id=1, source_target_pairs={{0,2},{1,3},{2,0},{3,1},{4,6},{5,7},{6,4},{7,5},{8,10},{9,11},{10,... | collective-permute-start | bytes 6152 | tf_op jit(solution)/shard_map/ppermute | solution.py:22
  42.3 3.4 %all-to-all-done = f32[32,1,8]{2,1,0:T(1,128)S(1)} async-done(((f32[32,1,8]{2,1,0:T(1,128)}), f32[32,1,8]{2,1,0:T(1,128)S(1)}, u32[]{:S(2)}, u32[]{:S(2)}) %all-to-all-start) | async-done | bytes 1056 | tf_op jit(solution)/shard_map/all_to_all | solution.py:42
  46.1 1.0 collective-permute-start.13
  47.1 1.6 %subtract_convert_fusion.refs_0_.grad_ref = bf16[1280,256]{1,0:T(8,128)(2,1)S(1)} fusion(f32[1280,256]{1,0:T(8,128)S(1)} %get-tuple-element.58, f32[256]{0:T(256)S(1)} %bitcast.68, f32[256]{0:T(256)S(1)} %bitcast.67, bf16[1280,256]{1,0:T(8,128)(2,1)} %collective-permute-done.4, f32[1280,256]{1,0:T(8,128)S(1)} %get-tuple-element.57, ...), kind=kLoop, calls=%fused_computation.1 | loop fusion | flops 2621440 | bytes 4589568 | tf_op jit(solution)/shard_map/convert_element_type | solution.py:375
  48.9 2.7 %collective-permute-start.11 = (bf16[1280,256]{1,0:T(8,128)(2,1)S(1)}, bf16[1280,256]{1,0:T(8,128)(2,1)S(1)}, u32[]{:S(2)}, u32[]{:S(2)}) collective-permute-start(bf16[1280,256]{1,0:T(8,128)(2,1)S(1)} %subtract_convert_fusion.refs_0_.grad_ref), channel_id=1, source_target_pairs={{0,3},{1,0},{2,1},{3,2},{4,7},{5,4},{6,5},{7,6},{8,11},{9,8},{10,9... | collective-permute-start | bytes 1966088 | tf_op jit(solution)/shard_map/ppermute | solution.py:22
  51.5 2.3 %collective-permute-start.12 = (bf16[640,256]{1,0:T(8,128)(2,1)S(1)}, bf16[640,256]{1,0:T(8,128)(2,1)S(1)}, u32[]{:S(2)}, u32[]{:S(2)}) collective-permute-start(bf16[640,256]{1,0:T(8,128)(2,1)S(1)} %bitcast.61), channel_id=1, source_target_pairs={{0,4},{4,0},{1,5},{5,1},{2,6},{6,2},{3,7},{7,3},{8,12},{12,8},{9,1... | collective-permute-start | bytes 983048 | tf_op jit(solution)/shard_map/ppermute | solution.py:22
  54.2 3.0 %context_product.3.refs_4_ = f32[256,1280]{1,0:T(8,128)S(1)} custom-call(s32[1]{0:T(128)} %bitcast.2.which, bf16[1280,256]{1,0:T(8,128)(2,1)S(1)} %subtract_convert_fusion.refs_0_.grad_ref, bf16[5120,1280]{1,0:T(8,128)(2,1)} %refs_3_.3), custom_call_target="tpu_custom_call" | custom-call | tf_op jit(solution)/shard_map/context_product/pallas_call | solution.py:104
  57.1 1.1 copy-done
  58.2 1.7 %place_rows.1 = bf16[512,1280]{1,0:T(8,128)(2,1)} custom-call(bf16[512,256]{1,0:T(8,128)(2,1)S(1)} %fusion.refs_5_.slots_ref, bf16[1280,256]{1,0:T(8,128)(2,1)S(1)} %subtract_convert_fusion.refs_0_.grad_ref), custom_call_target="tpu_custom_call" | custom-call | tf_op jit(solution)/shard_map/place_rows/pallas_call | solution.py:125
  59.9 6.5 %all-to-all-start.1 = ((bf16[32,16,1280]{2,1,0:T(8,128)(2,1)}), bf16[32,16,1280]{2,1,0:T(8,128)(2,1)}, u32[]{:S(2)}, u32[]{:S(2)}) async-start(bf16[32,16,1280]{2,1,0:T(8,128)(2,1)} %bitcast.35), calls=%async_computation.1 | async-start | bytes 2621440 | tf_op jit(solution)/shard_map/all_to_all | solution.py:58
  66.4 0.7 slice.32
  67.9 2.7 %collective-permute-start.15 = (bf16[640,256]{1,0:T(8,128)(2,1)}, bf16[640,256]{1,0:T(8,128)(2,1)}, u32[]{:S(2)}, u32[]{:S(2)}) collective-permute-start(bf16[640,256]{1,0:T(8,128)(2,1)} %slice.33), channel_id=1, source_target_pairs={{0,3},{1,0},{2,1},{3,2},{4,7},{5,4},{6,5},{7,6},{8,11},{9,8},{10,9... | collective-permute-start | bytes 983048 | tf_op jit(solution)/shard_map/ppermute | solution.py:22
  70.6 0.9 pad_maximum_fusion.1
  71.5 1.4 %collective-permute-start.16 = (bf16[1280,256]{1,0:T(8,128)(2,1)}, bf16[1280,256]{1,0:T(8,128)(2,1)}, u32[]{:S(2)}, u32[]{:S(2)}) collective-permute-start(bf16[1280,256]{1,0:T(8,128)(2,1)} %bitcast.23), channel_id=1, source_target_pairs={{0,4},{4,0},{1,5},{5,1},{2,6},{6,2},{3,7},{7,3},{8,12},{12,8},{9,1... | collective-permute-start | bytes 1966088 | tf_op jit(solution)/shard_map/ppermute | solution.py:22
  73.0 1.3 copy-done.1
  74.3 5.1 %context_product.4.refs_4_ = f32[256,1280]{1,0:T(8,128)S(1)} custom-call(s32[2]{0:T(128)S(1)} %pad_add_fusion.1.which, bf16[1280,256]{1,0:T(8,128)(2,1)S(1)} %collective-permute-done.11.refs_0_, bf16[1280,256]{1,0:T(8,128)(2,1)S(1)} %collective-permute-done.10.refs_1_, bf16[5120,1280]{1,0:T(8,128)(2,1)} %refs_3_.3, bf16[5120,1280]{1,0:T(8,128)(2,1)} %refs_3_.3, ...), custom_call_target="tpu_custom_call" | custom-call | tf_op jit(solution)/shard_map/context_product/pallas_call | solution.py:104
  79.4 1.1 dynamic-slice_bitcast_fusion.2
  80.7 1.1 fusion.8
  82.2 5.2 %lay_out.1 = (bf16[8,160,256]{2,1,0:T(8,128)(2,1)S(1)}, bf16[8,160,256]{2,1,0:T(8,128)(2,1)}, bf16[8,160,256]{2,1,0:T(8,128)(2,1)}, bf16[8,160,256]{2,1,0:T(8,128)(2,1)}) custom-call(s32[4]{0:T(128)S(1)} %pad_add_fusion.2.where, bf16[4,2,160,256]{3,2,1,0:T(8,128)(2,1)S(1)} %bitcast.49, bf16[4,2,160,256]{3,2,1,0:T(8,128)(2,1)S(1)} %bitcast.53, ...), custom_call_target="tpu_custom_call" | custom-call | tf_op jit(solution)/shard_map/lay_out/pallas_call | solution.py:278
  87.4 0.8 copy-done.2
  88.3 0.9 collective-permute-start.18
  89.2 2.4 %collective-permute-start.19 = (bf16[1280,256]{1,0:T(8,128)(2,1)}, bf16[1280,256]{1,0:T(8,128)(2,1)S(1)}, u32[]{:S(2)}, u32[]{:S(2)}) collective-permute-start(bf16[1280,256]{1,0:T(8,128)(2,1)} %bitcast.32), channel_id=1, source_target_pairs={{0,64},{4,20},{8,72},{12,28},{16,80},{20,4},{24,88},{28,12},{32,96... | collective-permute-start | bytes 1966088 | tf_op jit(solution)/shard_map/ppermute | solution.py:37
  91.6 1.2 collective-permute-start.20
  92.9 5.3 %context_product.5 = bf16[512,1280]{1,0:T(8,128)(2,1)} custom-call(s32[2]{0:T(128)S(1)} %pad_add_fusion.which, bf16[640,256]{1,0:T(8,128)(2,1)} %collective-permute-done.14.refs_0_, bf16[640,256]{1,0:T(8,128)(2,1)} %collective-permute-done.15.refs_1_, bf16[5120,1280]{1,0:T(8,128)(2,1)} %refs_3_.3, bf16[5120,1280]{1,0:T(8,128)(2,1)} %refs_3_.3, ...), custom_call_target="tpu_custom_call" | custom-call | tf_op jit(solution)/shard_map/context_product/pallas_call | solution.py:104
  98.2 2.2 %reshape.171 = bf16[384,1280]{1,0:T(8,128)(2,1)} reshape(bf16[32,12,1280]{2,1,0:T(8,128)(2,1)} %bitcast.46) | data formatting | bytes 1966080 | tf_op jit(solution)/shard_map/reshape | solution.py:63
  100.4 4.7 %all-to-all-start.2 = ((bf16[32,16,1280]{2,1,0:T(8,128)(2,1)}), bf16[32,16,1280]{2,1,0:T(8,128)(2,1)S(1)}, u32[]{:S(2)}, u32[]{:S(2)}) async-start(bf16[32,16,1280]{2,1,0:T(8,128)(2,1)} %bitcast.36), calls=%async_computation.2 | async-start | bytes 2621440 | tf_op jit(solution)/shard_map/all_to_all | solution.py:58
  105.3 1.6 %collective-permute-done.19.refs_2_ = bf16[1280,256]{1,0:T(8,128)(2,1)S(1)} collective-permute-done((bf16[1280,256]{1,0:T(8,128)(2,1)}, bf16[1280,256]{1,0:T(8,128)(2,1)S(1)}, u32[]{:S(2)}, u32[]{:S(2)}) %collective-permute-start.19) | collective-permute-done | bytes 655392 | tf_op jit(solution)/shard_map/ppermute | solution.py:37
  106.9 7.5 %weight_product.1 = (f32[160,1280]{1,0:T(8,128)S(1)}, bf16[160,1280]{1,0:T(8,128)(2,1)S(1)}, bf16[160,1280]{1,0:T(8,128)(2,1)S(1)}, bf16[160,1280]{1,0:T(8,128)(2,1)S(1)}) custom-call(s32[4]{0:T(128)S(1)} %pad_add_fusion.3.order_ref, bf16[1280,256]{1,0:T(8,128)(2,1)S(1)} %bitcast.56, bf16[1280,256]{1,0:T(8,128)(2,1)S(1)} %collective-permute-done.18.refs_1_, ...), custom_call_target="tpu_custom_call" | custom-call | tf_op jit(solution)/shard_map/weight_product/pallas_call | solution.py:315
  114.4 2.7 %collective-permute-start.21 = (bf16[160,1280]{1,0:T(8,128)(2,1)S(1)}, bf16[160,1280]{1,0:T(8,128)(2,1)S(1)}, u32[]{:S(2)}, u32[]{:S(2)}) collective-permute-start(bf16[160,1280]{1,0:T(8,128)(2,1)S(1)} %get-tuple-element.88), channel_id=1, source_target_pairs={{0,16},{4,68},{8,24},{12,76},{16,0},{20,84},{24,8},{28,92},{32,48}... | collective-permute-start | bytes 1228808 | tf_op jit(solution)/shard_map/ppermute | solution.py:37
  117.5 2.3 %collective-permute-start.23 = (bf16[160,1280]{1,0:T(8,128)(2,1)S(1)}, bf16[160,1280]{1,0:T(8,128)(2,1)S(1)}, u32[]{:S(2)}, u32[]{:S(2)}) collective-permute-start(bf16[160,1280]{1,0:T(8,128)(2,1)S(1)} %get-tuple-element.90), channel_id=1, source_target_pairs={{0,24},{4,100},{8,0},{12,108},{16,8},{20,116},{24,16},{28,124},{32... | collective-permute-start | bytes 1228808 | tf_op jit(solution)/shard_map/ppermute | solution.py:37
  119.8 8.0 %collective-permute-done.21 = bf16[160,1280]{1,0:T(8,128)(2,1)S(1)} collective-permute-done((bf16[160,1280]{1,0:T(8,128)(2,1)S(1)}, bf16[160,1280]{1,0:T(8,128)(2,1)S(1)}, u32[]{:S(2)}, u32[]{:S(2)}) %collective-permute-start.21) | collective-permute-done | bytes 409632 | tf_op jit(solution)/shard_map/ppermute | solution.py:37
  127.7 4.1 %collective-permute-done.22 = bf16[160,1280]{1,0:T(8,128)(2,1)S(1)} collective-permute-done((bf16[160,1280]{1,0:T(8,128)(2,1)S(1)}, bf16[160,1280]{1,0:T(8,128)(2,1)S(1)}, u32[]{:S(2)}, u32[]{:S(2)}) %collective-permute-start.22) | collective-permute-done | bytes 409632 | tf_op jit(solution)/shard_map/ppermute | solution.py:37
  131.9 1.1 add_multiply_fusion
  133.0 1.1 reshape.173
  (78 shorter events, 4.4 us)
Async XLA Ops:
  3.6 11.8 %collective-permute-start.2 = (bf16[256,1280]{1,0:T(8,128)(2,1)}, bf16[256,1280]{1,0:T(8,128)(2,1)S(1)}, u32[]{:S(2)}, u32[]{:S(2)}) collective-permute-start(bf16[256,1280]{1,0:T(8,128)(2,1)} %context_ref.6), channel_id=1, source_target_pairs={{0,4},{4,0},{1,5},{5,1},{2,6},{6,2},{3,7},{7,3},{8,12},{12,8},{9,1... | collective-permute-start | bytes 1966088 | tf_op jit(solution)/shard_map/ppermute | solution.py:22
  5.1 12.6 %collective-permute-start = (bf16[640,256]{1,0:T(8,128)(2,1)S(1)}, bf16[640,256]{1,0:T(8,128)(2,1)S(1)}, u32[]{:S(2)}, u32[]{:S(2)}) collective-permute-start(bf16[640,256]{1,0:T(8,128)(2,1)S(1)} %get-tuple-element.47), channel_id=1, source_target_pairs={{0,1},{1,2},{2,3},{3,0},{4,5},{5,6},{6,7},{7,4},{8,9},{9,10},{10,1... | collective-permute-start | bytes 983048 | tf_op jit(solution)/shard_map/ppermute | solution.py:22
  6.8 10.9 %collective-permute-start.1 = (bf16[640,256]{1,0:T(8,128)(2,1)S(1)}, bf16[640,256]{1,0:T(8,128)(2,1)S(1)}, u32[]{:S(2)}, u32[]{:S(2)}) collective-permute-start(bf16[640,256]{1,0:T(8,128)(2,1)S(1)} %get-tuple-element.48), channel_id=1, source_target_pairs={{0,3},{1,0},{2,1},{3,2},{4,7},{5,4},{6,5},{7,6},{8,11},{9,8},{10,9... | collective-permute-start | bytes 983048 | tf_op jit(solution)/shard_map/ppermute | solution.py:22
  17.7 4.6 %copy-start.8 = (f32[1280]{0:T(1024)S(1)}, f32[1280]{0:T(1024)}, u32[]{:S(2)}) copy-start(f32[1280]{0:T(1024)} %param.13) | copy-start | bytes 15364
  17.7 4.6 %copy-start.12 = (s32[64,1]{0,1:T(1,128)S(1)}, s32[64,1]{0,1:T(1,128)}, u32[]{:S(2)}) copy-start(s32[64,1]{0,1:T(1,128)} %param.17) | copy-start | bytes 772
  17.7 4.8 %copy-start.10 = (f32[4]{0:T(128)S(1)}, f32[4]{0:T(128)}, u32[]{:S(2)}) copy-start(f32[4]{0:T(128)} %param.14) | copy-start | bytes 52
  17.7 4.8 %copy-start.11 = (s32[4]{0:T(128)S(1)}, s32[4]{0:T(128)}, u32[]{:S(2)}) copy-start(s32[4]{0:T(128)} %param.15) | copy-start | bytes 52
  17.7 7.7 %copy-start.4 = (bf16[256,1280]{1,0:T(8,128)(2,1)S(1)}, bf16[256,1280]{1,0:T(8,128)(2,1)}, u32[]{:S(2)}) copy-start(bf16[256,1280]{1,0:T(8,128)(2,1)} %residual_ref.1) | copy-start | bytes 1966084
  17.7 7.7 %copy-start.5 = (bf16[256,1280]{1,0:T(8,128)(2,1)S(1)}, bf16[256,1280]{1,0:T(8,128)(2,1)}, u32[]{:S(2)}) copy-start(bf16[256,1280]{1,0:T(8,128)(2,1)} %cotangent_ref.1) | copy-start | bytes 1966084
  19.6 17.2 %collective-permute-start.3 = (bf16[1280,256]{1,0:T(8,128)(2,1)S(1)}, bf16[1280,256]{1,0:T(8,128)(2,1)}, u32[]{:S(2)}, u32[]{:S(2)}) collective-permute-start(bf16[1280,256]{1,0:T(8,128)(2,1)S(1)} %get-tuple-element.54), channel_id=1, source_target_pairs={{0,1},{1,2},{2,3},{3,0},{4,5},{5,6},{6,7},{7,4},{8,9},{9,10},{10,1... | collective-permute-start | bytes 1966088 | tf_op jit(solution)/shard_map/ppermute | solution.py:22
  19.6 17.2 %collective-permute-start.4 = (bf16[1280,256]{1,0:T(8,128)(2,1)}, bf16[1280,256]{1,0:T(8,128)(2,1)}, u32[]{:S(2)}, u32[]{:S(2)}) collective-permute-start(bf16[1280,256]{1,0:T(8,128)(2,1)} %get-tuple-element.55), channel_id=1, source_target_pairs={{0,3},{1,0},{2,1},{3,2},{4,7},{5,4},{6,5},{7,6},{8,11},{9,8},{10,9... | collective-permute-start | bytes 1966088 | tf_op jit(solution)/shard_map/ppermute | solution.py:22
  22.6 26.2 %collective-permute-start.8 = (bf16[512,1280]{1,0:T(8,128)(2,1)}, bf16[512,1280]{1,0:T(8,128)(2,1)}, u32[]{:S(2)}, u32[]{:S(2)}) collective-permute-start(bf16[512,1280]{1,0:T(8,128)(2,1)} %pad_maximum_fusion.refs_4_), channel_id=1, source_target_pairs={{0,32},{4,12},{8,40},{12,20},{16,48},{20,28},{24,56},{28,4},{32,64... | collective-permute-start | bytes 3932168 | tf_op jit(solution)/shard_map/ppermute | solution.py:37
  23.9 24.9 %collective-permute-start.9 = (bf16[512,1280]{1,0:T(8,128)(2,1)}, bf16[512,1280]{1,0:T(8,128)(2,1)}, u32[]{:S(2)}, u32[]{:S(2)}) collective-permute-start(bf16[512,1280]{1,0:T(8,128)(2,1)} %pad_maximum_fusion.refs_4_), channel_id=1, source_target_pairs={{0,96},{4,28},{8,104},{12,4},{16,112},{20,12},{24,120},{28,20},{32... | collective-permute-start | bytes 3932168 | tf_op jit(solution)/shard_map/ppermute | solution.py:37
  29.0 16.8 %all-to-all-start = ((f32[32,1,8]{2,1,0:T(1,128)}), f32[32,1,8]{2,1,0:T(1,128)S(1)}, u32[]{:S(2)}, u32[]{:S(2)}) async-start(f32[32,1,8]{2,1,0:T(1,128)} %broadcast_in_dim.16), calls=%async_computation | async-start | bytes 32768 | tf_op jit(solution)/shard_map/all_to_all | solution.py:42
  36.8 9.1 %copy-start.9 = (s32[4]{0:T(128)S(1)}, s32[4]{0:T(128)}, u32[]{:S(2)}) copy-start(s32[4]{0:T(128)} %param.16) | copy-start | bytes 52
  38.5 7.6 %collective-permute-start.5 = (f32[2,256]{1,0:T(2,128)S(1)}, f32[2,256]{1,0:T(2,128)S(1)}, u32[]{:S(2)}, u32[]{:S(2)}) collective-permute-start(f32[2,256]{1,0:T(2,128)S(1)} %pad_maximum_fusion.3), channel_id=1, source_target_pairs={{0,1},{1,2},{2,3},{3,0},{4,5},{5,6},{6,7},{7,4},{8,9},{9,10},{10,1... | collective-permute-start | bytes 6152 | tf_op jit(solution)/shard_map/ppermute | solution.py:22
  38.6 8.5 %collective-permute-start.6 = (f32[2,256]{1,0:T(2,128)S(1)}, f32[2,256]{1,0:T(2,128)S(1)}, u32[]{:S(2)}, u32[]{:S(2)}) collective-permute-start(f32[2,256]{1,0:T(2,128)S(1)} %pad_maximum_fusion.3), channel_id=1, source_target_pairs={{0,2},{1,3},{2,0},{3,1},{4,6},{5,7},{6,4},{7,5},{8,10},{9,11},{10,... | collective-permute-start | bytes 6152 | tf_op jit(solution)/shard_map/ppermute | solution.py:22
  42.3 4.8 %collective-permute-start.7 = (f32[2,256]{1,0:T(2,128)S(1)}, f32[2,256]{1,0:T(2,128)S(1)}, u32[]{:S(2)}, u32[]{:S(2)}) collective-permute-start(f32[2,256]{1,0:T(2,128)S(1)} %pad_maximum_fusion.3), channel_id=1, source_target_pairs={{0,3},{1,0},{2,1},{3,2},{4,7},{5,4},{6,5},{7,6},{8,11},{9,8},{10,9... | collective-permute-start | bytes 6152 | tf_op jit(solution)/shard_map/ppermute | solution.py:22
  46.1 20.3 %collective-permute-start.13 = (bf16[512,1280]{1,0:T(8,128)(2,1)}, bf16[512,1280]{1,0:T(8,128)(2,1)}, u32[]{:S(2)}, u32[]{:S(2)}) collective-permute-start(bf16[512,1280]{1,0:T(8,128)(2,1)} %pad_maximum_fusion.refs_4_), channel_id=1, source_target_pairs={{0,64},{4,20},{8,72},{12,28},{16,80},{20,4},{24,88},{28,12},{32,96... | collective-permute-start | bytes 3932168 | tf_op jit(solution)/shard_map/ppermute | solution.py:37
  48.8 17.6 %collective-permute-start.10 = (bf16[1280,256]{1,0:T(8,128)(2,1)S(1)}, bf16[1280,256]{1,0:T(8,128)(2,1)S(1)}, u32[]{:S(2)}, u32[]{:S(2)}) collective-permute-start(bf16[1280,256]{1,0:T(8,128)(2,1)S(1)} %subtract_convert_fusion.refs_0_.grad_ref), channel_id=1, source_target_pairs={{0,1},{1,2},{2,3},{3,0},{4,5},{5,6},{6,7},{7,4},{8,9},{9,10},{10,1... | collective-permute-start | bytes 1966088 | tf_op jit(solution)/shard_map/ppermute | solution.py:22
  48.9 17.5 %collective-permute-start.11 = (bf16[1280,256]{1,0:T(8,128)(2,1)S(1)}, bf16[1280,256]{1,0:T(8,128)(2,1)S(1)}, u32[]{:S(2)}, u32[]{:S(2)}) collective-permute-start(bf16[1280,256]{1,0:T(8,128)(2,1)S(1)} %subtract_convert_fusion.refs_0_.grad_ref), channel_id=1, source_target_pairs={{0,3},{1,0},{2,1},{3,2},{4,7},{5,4},{6,5},{7,6},{8,11},{9,8},{10,9... | collective-permute-start | bytes 1966088 | tf_op jit(solution)/shard_map/ppermute | solution.py:22
  51.5 6.7 %collective-permute-start.12 = (bf16[640,256]{1,0:T(8,128)(2,1)S(1)}, bf16[640,256]{1,0:T(8,128)(2,1)S(1)}, u32[]{:S(2)}, u32[]{:S(2)}) collective-permute-start(bf16[640,256]{1,0:T(8,128)(2,1)S(1)} %bitcast.61), channel_id=1, source_target_pairs={{0,4},{4,0},{1,5},{5,1},{2,6},{6,2},{3,7},{7,3},{8,12},{12,8},{9,1... | collective-permute-start | bytes 983048 | tf_op jit(solution)/shard_map/ppermute | solution.py:22
  57.1 1.1 copy-start
  58.2 1.7 %copy-start.6 = (bf16[640,256]{1,0:T(8,128)(2,1)}, bf16[640,256]{1,0:T(8,128)(2,1)S(1)}, u32[]{:S(2)}) copy-start(bf16[640,256]{1,0:T(8,128)(2,1)S(1)} %collective-permute-done.12) | copy-start | bytes 983044
  59.9 38.3 %all-to-all-start.1 = ((bf16[32,16,1280]{2,1,0:T(8,128)(2,1)}), bf16[32,16,1280]{2,1,0:T(8,128)(2,1)}, u32[]{:S(2)}, u32[]{:S(2)}) async-start(bf16[32,16,1280]{2,1,0:T(8,128)(2,1)} %bitcast.35), calls=%async_computation.1 | async-start | bytes 2621440 | tf_op jit(solution)/shard_map/all_to_all | solution.py:58
  67.1 12.2 %collective-permute-start.14 = (bf16[640,256]{1,0:T(8,128)(2,1)}, bf16[640,256]{1,0:T(8,128)(2,1)}, u32[]{:S(2)}, u32[]{:S(2)}) collective-permute-start(bf16[640,256]{1,0:T(8,128)(2,1)} %slice.32), channel_id=1, source_target_pairs={{0,1},{1,2},{2,3},{3,0},{4,5},{5,6},{6,7},{7,4},{8,9},{9,10},{10,1... | collective-permute-start | bytes 983048 | tf_op jit(solution)/shard_map/ppermute | solution.py:22
  67.9 11.5 %collective-permute-start.15 = (bf16[640,256]{1,0:T(8,128)(2,1)}, bf16[640,256]{1,0:T(8,128)(2,1)}, u32[]{:S(2)}, u32[]{:S(2)}) collective-permute-start(bf16[640,256]{1,0:T(8,128)(2,1)} %slice.33), channel_id=1, source_target_pairs={{0,3},{1,0},{2,1},{3,2},{4,7},{5,4},{6,5},{7,6},{8,11},{9,8},{10,9... | collective-permute-start | bytes 983048 | tf_op jit(solution)/shard_map/ppermute | solution.py:22
  71.5 9.1 %collective-permute-start.16 = (bf16[1280,256]{1,0:T(8,128)(2,1)}, bf16[1280,256]{1,0:T(8,128)(2,1)}, u32[]{:S(2)}, u32[]{:S(2)}) collective-permute-start(bf16[1280,256]{1,0:T(8,128)(2,1)} %bitcast.23), channel_id=1, source_target_pairs={{0,4},{4,0},{1,5},{5,1},{2,6},{6,2},{3,7},{7,3},{8,12},{12,8},{9,1... | collective-permute-start | bytes 1966088 | tf_op jit(solution)/shard_map/ppermute | solution.py:22
  73.0 1.3 copy-start.1
  79.4 2.8 %copy-start.7 = (bf16[640,256]{1,0:T(8,128)(2,1)S(1)}, bf16[640,256]{1,0:T(8,128)(2,1)}, u32[]{:S(2)}) copy-start(bf16[640,256]{1,0:T(8,128)(2,1)} %copy-done.6) | copy-start | bytes 983044
  80.5 1.7 %collective-permute-start.17 = (bf16[640,256]{1,0:T(8,128)(2,1)S(1)}, bf16[640,256]{1,0:T(8,128)(2,1)S(1)}, u32[]{:S(2)}, u32[]{:S(2)}) collective-permute-start(bf16[640,256]{1,0:T(8,128)(2,1)S(1)} %bitcast.60), channel_id=1, source_target_pairs={{0,4},{4,0},{1,5},{5,1},{2,6},{6,2},{3,7},{7,3},{8,12},{12,8},{9,1... | collective-permute-start | bytes 983048 | tf_op jit(solution)/shard_map/ppermute | solution.py:22
  87.4 0.9 copy-start.2
  88.3 17.0 %collective-permute-start.18 = (bf16[1280,256]{1,0:T(8,128)(2,1)}, bf16[1280,256]{1,0:T(8,128)(2,1)S(1)}, u32[]{:S(2)}, u32[]{:S(2)}) collective-permute-start(bf16[1280,256]{1,0:T(8,128)(2,1)} %bitcast.31), channel_id=1, source_target_pairs={{0,32},{4,12},{8,40},{12,20},{16,48},{20,28},{24,56},{28,4},{32,64... | collective-permute-start | bytes 1966088 | tf_op jit(solution)/shard_map/ppermute | solution.py:37
  89.2 17.6 %collective-permute-start.19 = (bf16[1280,256]{1,0:T(8,128)(2,1)}, bf16[1280,256]{1,0:T(8,128)(2,1)S(1)}, u32[]{:S(2)}, u32[]{:S(2)}) collective-permute-start(bf16[1280,256]{1,0:T(8,128)(2,1)} %bitcast.32), channel_id=1, source_target_pairs={{0,64},{4,20},{8,72},{12,28},{16,80},{20,4},{24,88},{28,12},{32,96... | collective-permute-start | bytes 1966088 | tf_op jit(solution)/shard_map/ppermute | solution.py:37
  91.6 15.3 %collective-permute-start.20 = (bf16[1280,256]{1,0:T(8,128)(2,1)}, bf16[1280,256]{1,0:T(8,128)(2,1)}, u32[]{:S(2)}, u32[]{:S(2)}) collective-permute-start(bf16[1280,256]{1,0:T(8,128)(2,1)} %bitcast.33), channel_id=1, source_target_pairs={{0,96},{4,28},{8,104},{12,4},{16,112},{20,12},{24,120},{28,20},{32... | collective-permute-start | bytes 1966088 | tf_op jit(solution)/shard_map/ppermute | solution.py:37
  100.4 6.5 %copy-start.3 = (bf16[8,160,256]{2,1,0:T(8,128)(2,1)S(1)}, bf16[8,160,256]{2,1,0:T(8,128)(2,1)}, u32[]{:S(2)}) copy-start(bf16[8,160,256]{2,1,0:T(8,128)(2,1)} %copy-done.2) | copy-start | bytes 1966084
  100.4 32.6 %all-to-all-start.2 = ((bf16[32,16,1280]{2,1,0:T(8,128)(2,1)}), bf16[32,16,1280]{2,1,0:T(8,128)(2,1)S(1)}, u32[]{:S(2)}, u32[]{:S(2)}) async-start(bf16[32,16,1280]{2,1,0:T(8,128)(2,1)} %bitcast.36), calls=%async_computation.2 | async-start | bytes 2621440 | tf_op jit(solution)/shard_map/all_to_all | solution.py:58
  114.4 13.4 %collective-permute-start.21 = (bf16[160,1280]{1,0:T(8,128)(2,1)S(1)}, bf16[160,1280]{1,0:T(8,128)(2,1)S(1)}, u32[]{:S(2)}, u32[]{:S(2)}) collective-permute-start(bf16[160,1280]{1,0:T(8,128)(2,1)S(1)} %get-tuple-element.88), channel_id=1, source_target_pairs={{0,16},{4,68},{8,24},{12,76},{16,0},{20,84},{24,8},{28,92},{32,48}... | collective-permute-start | bytes 1228808 | tf_op jit(solution)/shard_map/ppermute | solution.py:37
  117.1 14.8 %collective-permute-start.22 = (bf16[160,1280]{1,0:T(8,128)(2,1)S(1)}, bf16[160,1280]{1,0:T(8,128)(2,1)S(1)}, u32[]{:S(2)}, u32[]{:S(2)}) collective-permute-start(bf16[160,1280]{1,0:T(8,128)(2,1)S(1)} %get-tuple-element.89), channel_id=1, source_target_pairs={{0,8},{4,36},{8,16},{12,44},{16,24},{20,52},{24,0},{28,60},{32,40}... | collective-permute-start | bytes 1228808 | tf_op jit(solution)/shard_map/ppermute | solution.py:37
  117.5 14.4 %collective-permute-start.23 = (bf16[160,1280]{1,0:T(8,128)(2,1)S(1)}, bf16[160,1280]{1,0:T(8,128)(2,1)S(1)}, u32[]{:S(2)}, u32[]{:S(2)}) collective-permute-start(bf16[160,1280]{1,0:T(8,128)(2,1)S(1)} %get-tuple-element.90), channel_id=1, source_target_pairs={{0,24},{4,100},{8,0},{12,108},{16,8},{20,116},{24,16},{28,124},{32... | collective-permute-start | bytes 1228808 | tf_op jit(solution)/shard_map/ppermute | solution.py:37

commit v18 on v17

--- a/solution.py
+++ b/solution.py
@@ -51,6 +51,19 @@
     target = owner_dest * padded + rank * per_block
     row_target = jnp.repeat(target, per_block) + jnp.tile(jnp.arange(per_block), count)
     return (jnp.arange(slots // PAIR * padded)[:, None] == row_target[None, :]).astype(BF16)
+
+
+def half_slot_matrix(owner_dest, lanes, rows):
+    count = owner_dest.shape[0]
+    per_block = rows // count
+    kept = PAIR * per_block
+    same = owner_dest[:, None] == owner_dest[None, :]
+    earlier = jnp.arange(count)[None, :] < jnp.arange(count)[:, None]
+    rank = jnp.sum((same & earlier).astype(jnp.int32), axis=1)
+    target = owner_dest * 2 * kept + rank * per_block
+    row_target = jnp.repeat(target, per_block) + jnp.tile(jnp.arange(per_block), count)
+    row_target = row_target[None, None, :] + kept * jnp.arange(2)[:, None, None]
+    return (jnp.arange(lanes * 2 * kept)[None, :, None] == row_target).astype(BF16)
 
 
 def exchange(packed, lanes):
@@ -83,9 +96,18 @@
         )
         if before is not None:
             total = total + refs[2 * count][...]
-        if slots is not None:
-            total = jnp.dot(refs[-1][...], total.astype(BF16), preferred_element_type=F32)
-        out_ref[...] = total.astype(dtype)
+        if slots is None:
+            out_ref[...] = total
+            return
+        total = jnp.dot(refs[-1][0], total.astype(BF16), preferred_element_type=F32)
+
+        @pl.when(pl.program_id(0) == 0)
+        def _():
+            out_ref[...] = total.astype(BF16)
+
+        @pl.when(pl.program_id(0) == 1)
+        def _():
+            out_ref[...] += total.astype(BF16)
 
     in_specs = [pl.BlockSpec(chunk.shape, lambda n, which: (0, 0)) for chunk in chunks]
     in_specs += [
@@ -98,22 +120,48 @@
         in_specs.append(pl.BlockSpec((rows, tile), lambda n, which: (0, n)))
         operands.append(before)
     if slots is not None:
-        in_specs.append(pl.BlockSpec(slots.shape, lambda n, which: (0, 0)))
+        in_specs.append(pl.BlockSpec((1,) + slots.shape[1:], lambda n, which: (n, 0, 0)))
         operands.append(slots)
-        out_rows = slots.shape[0]
+        out_rows = slots.shape[1]
     return pl.pallas_call(
         body,
-        out_shape=jax.ShapeDtypeStruct((out_rows, width), dtype),
+        out_shape=jax.ShapeDtypeStruct((out_rows, width if slots is None else tile), dtype),
         grid_spec=pltpu.PrefetchScalarGridSpec(
             num_scalar_prefetch=1,
             grid=(width // tile,),
             in_specs=in_specs,
-            out_specs=pl.BlockSpec((out_rows, tile), lambda n, which: (0, n)),
+            out_specs=pl.BlockSpec(
+                (out_rows, tile), lambda n, which: (0, n if slots is None else 0)
+            ),
         ),
         cost_estimate=FREE,
         compiler_params=pltpu.CompilerParams(vmem_limit_bytes=42 * 1024 * 1024),
         name="context_product",
     )(jnp.stack(places), *operands)
+
+
+def unfold(got):
+    lanes, folded, half = got.shape
+    kept = folded // 2
+
+    def body(got_ref, out_ref):
+        shape = (lanes * kept, lanes * folded)
+        row = lax.broadcasted_iota(jnp.int32, shape, 0)
+        column = lax.broadcasted_iota(jnp.int32, shape, 1)
+        for h in (0, 1):
+            wanted = row + kept * (((row * 5462) >> 16) + h)
+            taken = jnp.where(column == wanted, F32(1.0), F32(0.0)).astype(BF16)
+            out_ref[:, h * half : (h + 1) * half] = jnp.dot(
+                taken, got_ref[...], preferred_element_type=F32
+            ).astype(BF16)
+
+    return pl.pallas_call(
+        body,
+        out_shape=jax.ShapeDtypeStruct((lanes * kept, 2 * half), BF16),
+        cost_estimate=FREE,
+        compiler_params=pltpu.CompilerParams(vmem_limit_bytes=16 * 1024 * 1024),
+        name="unfold",
+    )(got.reshape(lanes * folded, half))
 
 
 def place_rows(slots, grad_t):
@@ -382,6 +430,7 @@
         asked = [lax.dynamic_index_in_dim(value, 1 - c, 1, keepdims=False) for value in parted]
         return shift(jnp.concatenate(asked, axis=0).reshape(-1, rows), "c", 1)
 
+    half_slots = half_slot_matrix(destinations[:, 0], lanes, rows)
     slots = slot_matrix(destinations[:, 0], lanes * PAIR, rows, 16)
     from_left, from_right = shift(grad_t, "z", 1), shift(grad_t, "z", 3)
     swapped = swap(grad_t)
@@ -416,16 +465,17 @@
         pieces[k] = cross(sends[k], k, True)
     far_place = (z + 2) % NZ * 2
     placed = context_product(
-        [far_left, far_right], [far_place, far_place + 1], out_proj, before=context_grad, slots=slots
+        [far_left, far_right], [far_place, far_place + 1], out_proj, before=context_grad, slots=half_slots
     )
     placed, d_residual = lax.optimization_barrier((placed, learner_rows(d_residual)))
     d_context = exchange(placed, lanes)
     order = [jnp.where(c == 0, (y + k) % NY, (x + k - z) % NZ) for k in range(4)]
     d_out_proj, *parts = weight_product(pieces, contexts, jnp.stack(order), block)
     parts = [cross(parts[k - 1], k, False) for k in (2, 1, 3)]
+    parts, d_context = lax.optimization_barrier((parts, unfold(d_context)))
     for part in parts:
         d_out_proj = d_out_proj + part.astype(F32)
-    return (learner_rows(d_context), d_residual, d_out_proj / lanes)
+    return (d_context, d_residual, d_out_proj / lanes)
 
 
 def solution(mesh):

time: 135 us -> 134 us (level)
  waiting for transfers between devices: 18.1 us -> 10.2 us
  Pallas kernels: 41.9 us -> 45.5 us
    ppermute x9, waiting for transfers between devices: 13.7 us -> 5.73 us  [cross(): return lax.ppermute(value, DP, pairs)]
    unnamed x26 -> x38, local copies, waits for them, and re-layouts: 3.27 us -> 8.78 us
    pallas_call x3 -> x4, Pallas kernels: 13.3 us -> 15.8 us  [the longest x3 13.8 us: context_product(): pl.pallas_call(body, out_shape=jax.ShapeDtypeStruct((out_rows, width if s...]
    all_to_all x1, waiting for transfers between devices: 3.42 us -> 1.92 us  [all_shares(): return lax.all_to_all(copies, DP, split_axis=0, concat_axis=0, tiled=True)]
    reshape x2 -> x1, local copies, waits for them, and re-layouts: 3.23 us -> 2.18 us  [learner_rows(): return got[:, :kept].reshape(got.shape[0] * kept, got.shape[2])]
  transfers between devices with their start and end apart: 27 -> 27, of which waited for: 7 -> 7; matrix products, arithmetic and copies ran while one was open for 11% -> 8% of each run, Pallas kernels for 28% -> 31%
where the time goes in v18:
time: 134 us; the launch traced here: 133 us
  starting transfers between devices  54.5 us (41%)
  Pallas kernels  45.5 us (34%)
  local copies, waits for them, and re-layouts  12.1 us (9%)
  waiting for transfers between devices  10.2 us (8%)
  other arithmetic  9.2 us (7%)
    ppermute x15, starting transfers between devices, shift(): lax.ppermute(value, axis, [(i, (i + step) % size) for i in range(size)])  20.8 us
    ppermute x9, starting transfers between devices, cross(): return lax.ppermute(value, DP, pairs)  14.4 us
    pallas_call x3, Pallas kernels, context_product(): pl.pallas_call(body, out_shape=jax.ShapeDtypeStruct((out_rows, width if s...  13.8 us
    all_to_all x2, starting transfers between devices, exchange(): return lax.all_to_all(blocks, DP, split_axis=0, concat_axis=0, tiled=True)  11.8 us
    pallas_call x3, Pallas kernels, forward_product(): pl.pallas_call(body, out_shape=[jax.ShapeDtypeStruct((tile, rows), BF16)]...  9.4 us
    unnamed x38, local copies, waits for them, and re-layouts  8.78 us
    pallas_call x1, Pallas kernels, weight_product(): pl.pallas_call(body, out_shape=[jax.ShapeDtypeStruct((block, width), BF16...  8.28 us
    all_to_all x1, starting transfers between devices, all_shares(): return lax.all_to_all(copies, DP, split_axis=0, concat_axis=0, tiled=True)  7.52 us
  transfers between devices with their start and end apart: 27, of which 7 were waited for; matrix products, arithmetic and copies ran while one was open for 8% of the time, Pallas kernels for 31%

profile of v18, /device:TPU:1, one launch (start us, length us, event | category | flops | bytes accessed | tf_op | source)
XLA Modules:
  0.0 132.7 jit_solution(22773609297645013)
XLA Ops:
  0.6 2.9 %forward_product.3 = (bf16[640,256]{1,0:T(8,128)(2,1)S(1)}, bf16[640,256]{1,0:T(8,128)(2,1)S(1)}) custom-call(s32[1]{0:T(128)} %bitcast.5.which, bf16[5120,1280]{1,0:T(8,128)(2,1)} %refs_3_.3, bf16[256,1280]{1,0:T(8,128)(2,1)} %context_ref.6), custom_call_target="tpu_custom_call" | custom-call | tf_op jit(solution)/shard_map/forward_product/pallas_call | solution.py:223
  3.6 1.5 %collective-permute-start.2 = (bf16[256,1280]{1,0:T(8,128)(2,1)}, bf16[256,1280]{1,0:T(8,128)(2,1)S(1)}, u32[]{:S(2)}, u32[]{:S(2)}) collective-permute-start(bf16[256,1280]{1,0:T(8,128)(2,1)} %context_ref.6), channel_id=1, source_target_pairs={{0,4},{4,0},{1,5},{5,1},{2,6},{6,2},{3,7},{7,3},{8,12},{12,8},{9,1... | collective-permute-start | bytes 1966088 | tf_op jit(solution)/shard_map/ppermute | solution.py:22
  5.1 1.7 %collective-permute-start = (bf16[640,256]{1,0:T(8,128)(2,1)S(1)}, bf16[640,256]{1,0:T(8,128)(2,1)S(1)}, u32[]{:S(2)}, u32[]{:S(2)}) collective-permute-start(bf16[640,256]{1,0:T(8,128)(2,1)S(1)} %get-tuple-element.51), channel_id=1, source_target_pairs={{0,1},{1,2},{2,3},{3,0},{4,5},{5,6},{6,7},{7,4},{8,9},{9,10},{10,1... | collective-permute-start | bytes 983048 | tf_op jit(solution)/shard_map/ppermute | solution.py:22
  6.8 2.1 %collective-permute-start.1 = (bf16[640,256]{1,0:T(8,128)(2,1)S(1)}, bf16[640,256]{1,0:T(8,128)(2,1)S(1)}, u32[]{:S(2)}, u32[]{:S(2)}) collective-permute-start(bf16[640,256]{1,0:T(8,128)(2,1)S(1)} %get-tuple-element.52), channel_id=1, source_target_pairs={{0,3},{1,0},{2,1},{3,2},{4,7},{5,4},{6,5},{7,6},{8,11},{9,8},{10,9... | collective-permute-start | bytes 983048 | tf_op jit(solution)/shard_map/ppermute | solution.py:22
  8.9 2.9 %forward_product.4.refs_0_ = bf16[1280,256]{1,0:T(8,128)(2,1)S(1)} custom-call(s32[1]{0:T(128)} %bitcast.6.which, bf16[5120,1280]{1,0:T(8,128)(2,1)} %refs_3_.3, bf16[256,1280]{1,0:T(8,128)(2,1)} %context_ref.6), custom_call_target="tpu_custom_call" | custom-call | tf_op jit(solution)/shard_map/forward_product/pallas_call | solution.py:223
  11.8 3.6 %forward_product.5.refs_2_ = bf16[1280,256]{1,0:T(8,128)(2,1)} custom-call(s32[1]{0:T(128)} %bitcast.7.which, bf16[5120,1280]{1,0:T(8,128)(2,1)} %refs_3_.3, bf16[256,1280]{1,0:T(8,128)(2,1)} %context_ref.6), custom_call_target="tpu_custom_call" | custom-call | tf_op jit(solution)/shard_map/forward_product/pallas_call | solution.py:223
  15.4 2.3 %pad_maximum_fusion.refs_4_ = bf16[512,1280]{1,0:T(8,128)(2,1)} fusion(bf16[256,1280]{1,0:T(8,128)(2,1)S(1)} %collective-permute-done.2, bf16[256,1280]{1,0:T(8,128)(2,1)} %context_ref.6), kind=kLoop, calls=%fused_computation.2 | loop fusion | flops 2621440 | bytes 2621440 | tf_op jit(solution)/shard_map/concatenate | solution.py:391
  17.7 1.8 %top_up.1 = (bf16[1280,256]{1,0:T(8,128)(2,1)S(1)}, bf16[1280,256]{1,0:T(8,128)(2,1)}) custom-call(bf16[1280,256]{1,0:T(8,128)(2,1)S(1)} %forward_product.4.refs_0_, bf16[640,256]{1,0:T(8,128)(2,1)S(1)} %collective-permute-done.refs_1_, bf16[1280,256]{1,0:T(8,128)(2,1)} %forward_product.5.refs_2_, ...), custom_call_target="tpu_custom_call", output_to_operand_aliasing={{0}: (0, {}), {1}: (2, {})} | custom-call | tf_op jit(solution)/shard_map/top_up/pallas_call | solution.py:192
  19.5 1.5 %collective-permute-start.4 = (bf16[1280,256]{1,0:T(8,128)(2,1)}, bf16[1280,256]{1,0:T(8,128)(2,1)}, u32[]{:S(2)}, u32[]{:S(2)}) collective-permute-start(bf16[1280,256]{1,0:T(8,128)(2,1)} %get-tuple-element.59), channel_id=1, source_target_pairs={{0,3},{1,0},{2,1},{3,2},{4,7},{5,4},{6,5},{7,6},{8,11},{9,8},{10,9... | collective-permute-start | bytes 1966088 | tf_op jit(solution)/shard_map/ppermute | solution.py:22
  21.4 1.4 %collective-permute-start.8 = (bf16[512,1280]{1,0:T(8,128)(2,1)}, bf16[512,1280]{1,0:T(8,128)(2,1)}, u32[]{:S(2)}, u32[]{:S(2)}) collective-permute-start(bf16[512,1280]{1,0:T(8,128)(2,1)} %pad_maximum_fusion.refs_4_), channel_id=1, source_target_pairs={{0,32},{4,12},{8,40},{12,20},{16,48},{20,28},{24,56},{28,4},{32,64... | collective-permute-start | bytes 3932168 | tf_op jit(solution)/shard_map/ppermute | solution.py:37
  22.8 1.5 %collective-permute-start.9 = (bf16[512,1280]{1,0:T(8,128)(2,1)}, bf16[512,1280]{1,0:T(8,128)(2,1)}, u32[]{:S(2)}, u32[]{:S(2)}) collective-permute-start(bf16[512,1280]{1,0:T(8,128)(2,1)} %pad_maximum_fusion.refs_4_), channel_id=1, source_target_pairs={{0,96},{4,28},{8,104},{12,4},{16,112},{20,12},{24,120},{28,20},{32... | collective-permute-start | bytes 3932168 | tf_op jit(solution)/shard_map/ppermute | solution.py:37
  24.3 1.1 copy-done.10
  25.4 1.1 copy-done.11
  26.5 2.9 %hidden_part.1 = (f32[1280,256]{1,0:T(8,128)S(1)}, f32[1280,256]{1,0:T(8,128)S(1)}) custom-call(s32[1]{0:T(128)} %bitcast.4.which, bf16[5120,1280]{1,0:T(8,128)(2,1)} %refs_3_.3, bf16[256,1280]{1,0:T(8,128)(2,1)} %context_ref.6, bf16[256,1280]{1,0:T(8,128)(2,1)S(1)} %copy-done.10, bf16[256,1280]{1,0:T(8,128)(2,1)S(1)} %copy-done.11, ...), custom_call_target="tpu_custom_call" | custom-call | tf_op jit(solution)/shard_map/hidden_part/pallas_call | solution.py:258
  30.0 7.5 %all-to-all-start = ((f32[32,1,8]{2,1,0:T(1,128)}), f32[32,1,8]{2,1,0:T(1,128)S(1)}, u32[]{:S(2)}, u32[]{:S(2)}) async-start(f32[32,1,8]{2,1,0:T(1,128)} %broadcast_in_dim.18), calls=%async_computation | async-start | bytes 32768 | tf_op jit(solution)/shard_map/all_to_all | solution.py:42
  37.5 1.6 %multiply_reduce_fusion.1 = (f32[256]{0:T(256)S(1)}, f32[256]{0:T(256)S(1)}) fusion(bf16[1280,256]{1,0:T(8,128)(2,1)} %collective-permute-done.4, f32[1280,256]{1,0:T(8,128)S(1)} %get-tuple-element.61, bf16[1280,256]{1,0:T(8,128)(2,1)} %collective-permute-done.3, f32[1280,256]{1,0:T(8,128)S(1)} %get-tuple-element.62), kind=kLoop, calls=%fused_computation.5 | loop fusion | flops 2620928 | bytes 3934208 | tf_op jit(solution)/shard_map/reduce_sum | solution.py:407
  39.2 3.0 %collective-permute-start.7 = (f32[2,256]{1,0:T(2,128)S(1)}, f32[2,256]{1,0:T(2,128)S(1)}, u32[]{:S(2)}, u32[]{:S(2)}) collective-permute-start(f32[2,256]{1,0:T(2,128)S(1)} %pad_maximum_fusion.3), channel_id=1, source_target_pairs={{0,3},{1,0},{2,1},{3,2},{4,7},{5,4},{6,5},{7,6},{8,11},{9,8},{10,9... | collective-permute-start | bytes 6152 | tf_op jit(solution)/shard_map/ppermute | solution.py:22
  42.9 1.9 %all-to-all-done = f32[32,1,8]{2,1,0:T(1,128)S(1)} async-done(((f32[32,1,8]{2,1,0:T(1,128)}), f32[32,1,8]{2,1,0:T(1,128)S(1)}, u32[]{:S(2)}, u32[]{:S(2)}) %all-to-all-start) | async-done | bytes 1056 | tf_op jit(solution)/shard_map/all_to_all | solution.py:42
  45.2 1.0 collective-permute-start.13
  46.2 1.6 %subtract_convert_fusion.refs_0_.grad_ref = bf16[1280,256]{1,0:T(8,128)(2,1)S(1)} fusion(f32[1280,256]{1,0:T(8,128)S(1)} %get-tuple-element.62, f32[256]{0:T(256)S(1)} %bitcast.74, f32[256]{0:T(256)S(1)} %bitcast.73, bf16[1280,256]{1,0:T(8,128)(2,1)} %collective-permute-done.4, f32[1280,256]{1,0:T(8,128)S(1)} %get-tuple-element.61, ...), kind=kLoop, calls=%fused_computation.3 | loop fusion | flops 2621440 | bytes 4589568 | tf_op jit(solution)/shard_map/convert_element_type | solution.py:423
  47.8 2.0 %collective-permute-start.10 = (bf16[1280,256]{1,0:T(8,128)(2,1)S(1)}, bf16[1280,256]{1,0:T(8,128)(2,1)S(1)}, u32[]{:S(2)}, u32[]{:S(2)}) collective-permute-start(bf16[1280,256]{1,0:T(8,128)(2,1)S(1)} %subtract_convert_fusion.refs_0_.grad_ref), channel_id=1, source_target_pairs={{0,1},{1,2},{2,3},{3,0},{4,5},{5,6},{6,7},{7,4},{8,9},{9,10},{10,1... | collective-permute-start | bytes 1966088 | tf_op jit(solution)/shard_map/ppermute | solution.py:22
  49.9 1.1 collective-permute-start.11
  51.3 2.1 %collective-permute-start.12 = (bf16[640,256]{1,0:T(8,128)(2,1)S(1)}, bf16[640,256]{1,0:T(8,128)(2,1)S(1)}, u32[]{:S(2)}, u32[]{:S(2)}) collective-permute-start(bf16[640,256]{1,0:T(8,128)(2,1)S(1)} %bitcast.67), channel_id=1, source_target_pairs={{0,4},{4,0},{1,5},{5,1},{2,6},{6,2},{3,7},{7,3},{8,12},{12,8},{9,1... | collective-permute-start | bytes 983048 | tf_op jit(solution)/shard_map/ppermute | solution.py:22
  53.5 3.0 %context_product.3.refs_4_ = f32[256,1280]{1,0:T(8,128)S(1)} custom-call(s32[1]{0:T(128)} %bitcast.4.which, bf16[1280,256]{1,0:T(8,128)(2,1)S(1)} %subtract_convert_fusion.refs_0_.grad_ref, bf16[5120,1280]{1,0:T(8,128)(2,1)} %refs_3_.3), custom_call_target="tpu_custom_call" | custom-call | tf_op jit(solution)/shard_map/context_product/pallas_call | solution.py:126
  56.5 1.1 copy-done
  58.4 1.6 %place_rows.1 = bf16[512,1280]{1,0:T(8,128)(2,1)} custom-call(bf16[512,256]{1,0:T(8,128)(2,1)S(1)} %fusion.1.slots_ref, bf16[1280,256]{1,0:T(8,128)(2,1)S(1)} %subtract_convert_fusion.refs_0_.grad_ref), custom_call_target="tpu_custom_call" | custom-call | tf_op jit(solution)/shard_map/place_rows/pallas_call | solution.py:173
  60.0 7.2 %all-to-all-start.1 = ((bf16[32,16,1280]{2,1,0:T(8,128)(2,1)}), bf16[32,16,1280]{2,1,0:T(8,128)(2,1)}, u32[]{:S(2)}, u32[]{:S(2)}) async-start(bf16[32,16,1280]{2,1,0:T(8,128)(2,1)} %bitcast.39), calls=%async_computation.1 | async-start | bytes 2621440 | tf_op jit(solution)/shard_map/all_to_all | solution.py:71
  67.3 2.7 %collective-permute-start.15 = (bf16[640,256]{1,0:T(8,128)(2,1)S(1)}, bf16[640,256]{1,0:T(8,128)(2,1)S(1)}, u32[]{:S(2)}, u32[]{:S(2)}) collective-permute-start(bf16[640,256]{1,0:T(8,128)(2,1)S(1)} %slice.30), channel_id=1, source_target_pairs={{0,3},{1,0},{2,1},{3,2},{4,7},{5,4},{6,5},{7,6},{8,11},{9,8},{10,9... | collective-permute-start | bytes 983048 | tf_op jit(solution)/shard_map/ppermute | solution.py:22
  70.2 1.1 collective-permute-start.16
  71.4 5.1 %context_product.4.refs_4_ = f32[256,1280]{1,0:T(8,128)S(1)} custom-call(s32[2]{0:T(128)S(1)} %pad_add_fusion.1.which, bf16[1280,256]{1,0:T(8,128)(2,1)S(1)} %collective-permute-done.11.refs_0_, bf16[1280,256]{1,0:T(8,128)(2,1)S(1)} %collective-permute-done.10.refs_1_, bf16[5120,1280]{1,0:T(8,128)(2,1)} %refs_3_.3, bf16[5120,1280]{1,0:T(8,128)(2,1)} %refs_3_.3, ...), custom_call_target="tpu_custom_call" | custom-call | tf_op jit(solution)/shard_map/context_product/pallas_call | solution.py:126
  76.5 1.1 collective-permute-done.14.refs_0_
  77.7 1.1 collective-permute-start.17
  78.9 1.1 collective-permute-done.17
  80.1 5.7 %lay_out.1 = (bf16[8,160,256]{2,1,0:T(8,128)(2,1)S(1)}, bf16[8,160,256]{2,1,0:T(8,128)(2,1)}, bf16[8,160,256]{2,1,0:T(8,128)(2,1)}, bf16[8,160,256]{2,1,0:T(8,128)(2,1)}) custom-call(s32[4]{0:T(128)S(1)} %pad_add_fusion.2.where, bf16[4,2,160,256]{3,2,1,0:T(8,128)(2,1)S(1)} %bitcast.50, bf16[4,2,160,256]{3,2,1,0:T(8,128)(2,1)S(1)} %bitcast.54, ...), custom_call_target="tpu_custom_call" | custom-call | tf_op jit(solution)/shard_map/lay_out/pallas_call | solution.py:326
  86.6 1.4 %collective-permute-start.18 = (bf16[1280,256]{1,0:T(8,128)(2,1)}, bf16[1280,256]{1,0:T(8,128)(2,1)S(1)}, u32[]{:S(2)}, u32[]{:S(2)}) collective-permute-start(bf16[1280,256]{1,0:T(8,128)(2,1)} %bitcast.33), channel_id=1, source_target_pairs={{0,32},{4,12},{8,40},{12,20},{16,48},{20,28},{24,56},{28,4},{32,64... | collective-permute-start | bytes 1966088 | tf_op jit(solution)/shard_map/ppermute | solution.py:37
  88.0 2.4 %collective-permute-start.19 = (bf16[1280,256]{1,0:T(8,128)(2,1)}, bf16[1280,256]{1,0:T(8,128)(2,1)}, u32[]{:S(2)}, u32[]{:S(2)}) collective-permute-start(bf16[1280,256]{1,0:T(8,128)(2,1)} %bitcast.34), channel_id=1, source_target_pairs={{0,64},{4,20},{8,72},{12,28},{16,80},{20,4},{24,88},{28,12},{32,96... | collective-permute-start | bytes 1966088 | tf_op jit(solution)/shard_map/ppermute | solution.py:37
  90.4 1.2 collective-permute-start.20
  91.9 1.0 copy-done.3
  93.8 5.8 %context_product.5 = bf16[768,640]{1,0:T(8,128)(2,1)} custom-call(s32[2]{0:T(128)S(1)} %pad_add_fusion.3.which, bf16[640,256]{1,0:T(8,128)(2,1)S(1)} %copy-done.3, bf16[640,256]{1,0:T(8,128)(2,1)S(1)} %copy-done.5, bf16[5120,1280]{1,0:T(8,128)(2,1)} %refs_3_.3, bf16[5120,1280]{1,0:T(8,128)(2,1)} %refs_3_.3, f32[256,1280]{1,0:T(8,128)S(1)} %context_product.4.refs_4_, ...), custom_call_target="tpu_custom_call" | custom-call | tf_op jit(solution)/shard_map/context_product/pallas_call | solution.py:126
  99.6 2.2 %reshape.217 = bf16[384,1280]{1,0:T(8,128)(2,1)} reshape(bf16[32,12,1280]{2,1,0:T(8,128)(2,1)} %bitcast.48) | data formatting | bytes 1966080 | tf_op jit(solution)/shard_map/reshape | solution.py:76
  101.8 4.7 %all-to-all-start.2 = ((bf16[32,24,640]{2,1,0:T(8,128)(2,1)}), bf16[32,24,640]{2,1,0:T(8,128)(2,1)S(1)}, u32[]{:S(2)}, u32[]{:S(2)}) async-start(bf16[32,24,640]{2,1,0:T(8,128)(2,1)} %bitcast.40), calls=%async_computation.2 | async-start | bytes 1966080 | tf_op jit(solution)/shard_map/all_to_all | solution.py:71
  107.5 1.1 copy-done.9
  108.6 8.3 %weight_product.1 = (f32[160,1280]{1,0:T(8,128)S(1)}, bf16[160,1280]{1,0:T(8,128)(2,1)S(1)}, bf16[160,1280]{1,0:T(8,128)(2,1)}, bf16[160,1280]{1,0:T(8,128)(2,1)S(1)}) custom-call(s32[4]{0:T(128)S(1)} %pad_add_fusion.order_ref, bf16[1280,256]{1,0:T(8,128)(2,1)S(1)} %bitcast.62, bf16[1280,256]{1,0:T(8,128)(2,1)S(1)} %copy-done.9, ...), custom_call_target="tpu_custom_call" | custom-call | tf_op jit(solution)/shard_map/weight_product/pallas_call | solution.py:363
  116.9 2.9 %collective-permute-start.21 = (bf16[160,1280]{1,0:T(8,128)(2,1)}, bf16[160,1280]{1,0:T(8,128)(2,1)S(1)}, u32[]{:S(2)}, u32[]{:S(2)}) collective-permute-start(bf16[160,1280]{1,0:T(8,128)(2,1)} %get-tuple-element.85), channel_id=1, source_target_pairs={{0,16},{4,68},{8,24},{12,76},{16,0},{20,84},{24,8},{28,92},{32,48}... | collective-permute-start | bytes 1228808 | tf_op jit(solution)/shard_map/ppermute | solution.py:37
  120.1 2.4 %collective-permute-start.23 = (bf16[160,1280]{1,0:T(8,128)(2,1)S(1)}, bf16[160,1280]{1,0:T(8,128)(2,1)}, u32[]{:S(2)}, u32[]{:S(2)}) collective-permute-start(bf16[160,1280]{1,0:T(8,128)(2,1)S(1)} %get-tuple-element.87), channel_id=1, source_target_pairs={{0,24},{4,100},{8,0},{12,108},{16,8},{20,116},{24,16},{28,124},{32... | collective-permute-start | bytes 1228808 | tf_op jit(solution)/shard_map/ppermute | solution.py:37
  122.7 2.0 %unfold.1 = bf16[384,1280]{1,0:T(8,128)(2,1)} custom-call(bf16[768,640]{1,0:T(8,128)(2,1)S(1)} %bitcast.55), custom_call_target="tpu_custom_call" | custom-call | tf_op jit(solution)/shard_map/unfold/pallas_call | solution.py:158
  125.7 4.5 %collective-permute-done.22 = bf16[160,1280]{1,0:T(8,128)(2,1)} collective-permute-done((bf16[160,1280]{1,0:T(8,128)(2,1)S(1)}, bf16[160,1280]{1,0:T(8,128)(2,1)}, u32[]{:S(2)}, u32[]{:S(2)}) %collective-permute-start.22) | collective-permute-done | bytes 409632 | tf_op jit(solution)/shard_map/ppermute | solution.py:37
  130.5 2.2 %add_multiply_fusion = f32[160,1280]{1,0:T(8,128)} fusion(bf16[160,1280]{1,0:T(8,128)(2,1)} %collective-permute-done.23, bf16[160,1280]{1,0:T(8,128)(2,1)} %collective-permute-done.22, f32[160,1280]{1,0:T(8,128)S(1)} %get-tuple-element.95, bf16[160,1280]{1,0:T(8,128)(2,1)S(1)} %collective-permute-done.21), kind=kLoop, calls=%fused_computation.7 | loop fusion | flops 1433600 | bytes 2867200 | tf_op jit(solution)/shard_map/div | solution.py:478
  (94 shorter events, 8.6 us)
Async XLA Ops:
  3.6 11.8 %collective-permute-start.2 = (bf16[256,1280]{1,0:T(8,128)(2,1)}, bf16[256,1280]{1,0:T(8,128)(2,1)S(1)}, u32[]{:S(2)}, u32[]{:S(2)}) collective-permute-start(bf16[256,1280]{1,0:T(8,128)(2,1)} %context_ref.6), channel_id=1, source_target_pairs={{0,4},{4,0},{1,5},{5,1},{2,6},{6,2},{3,7},{7,3},{8,12},{12,8},{9,1... | collective-permute-start | bytes 1966088 | tf_op jit(solution)/shard_map/ppermute | solution.py:22
  5.1 12.6 %collective-permute-start = (bf16[640,256]{1,0:T(8,128)(2,1)S(1)}, bf16[640,256]{1,0:T(8,128)(2,1)S(1)}, u32[]{:S(2)}, u32[]{:S(2)}) collective-permute-start(bf16[640,256]{1,0:T(8,128)(2,1)S(1)} %get-tuple-element.51), channel_id=1, source_target_pairs={{0,1},{1,2},{2,3},{3,0},{4,5},{5,6},{6,7},{7,4},{8,9},{9,10},{10,1... | collective-permute-start | bytes 983048 | tf_op jit(solution)/shard_map/ppermute | solution.py:22
  6.8 10.9 %collective-permute-start.1 = (bf16[640,256]{1,0:T(8,128)(2,1)S(1)}, bf16[640,256]{1,0:T(8,128)(2,1)S(1)}, u32[]{:S(2)}, u32[]{:S(2)}) collective-permute-start(bf16[640,256]{1,0:T(8,128)(2,1)S(1)} %get-tuple-element.52), channel_id=1, source_target_pairs={{0,3},{1,0},{2,1},{3,2},{4,7},{5,4},{6,5},{7,6},{8,11},{9,8},{10,9... | collective-permute-start | bytes 983048 | tf_op jit(solution)/shard_map/ppermute | solution.py:22
  17.7 3.4 %copy-start.14 = (f32[1280]{0:T(1024)S(1)}, f32[1280]{0:T(1024)}, u32[]{:S(2)}) copy-start(f32[1280]{0:T(1024)} %param.13) | copy-start | bytes 15364
  17.7 3.4 %copy-start.16 = (s32[64,1]{0,1:T(1,128)S(1)}, s32[64,1]{0,1:T(1,128)}, u32[]{:S(2)}) copy-start(s32[64,1]{0,1:T(1,128)} %param.17) | copy-start | bytes 772
  17.7 3.6 %copy-start.17 = (f32[4]{0:T(128)S(1)}, f32[4]{0:T(128)}, u32[]{:S(2)}) copy-start(f32[4]{0:T(128)} %param.14) | copy-start | bytes 52
  17.7 3.6 %copy-start.18 = (s32[4]{0:T(128)S(1)}, s32[4]{0:T(128)}, u32[]{:S(2)}) copy-start(s32[4]{0:T(128)} %param.15) | copy-start | bytes 52
  19.5 18.0 %collective-permute-start.4 = (bf16[1280,256]{1,0:T(8,128)(2,1)}, bf16[1280,256]{1,0:T(8,128)(2,1)}, u32[]{:S(2)}, u32[]{:S(2)}) collective-permute-start(bf16[1280,256]{1,0:T(8,128)(2,1)} %get-tuple-element.59), channel_id=1, source_target_pairs={{0,3},{1,0},{2,1},{3,2},{4,7},{5,4},{6,5},{7,6},{8,11},{9,8},{10,9... | collective-permute-start | bytes 1966088 | tf_op jit(solution)/shard_map/ppermute | solution.py:22
  21.1 16.4 %collective-permute-start.3 = (bf16[1280,256]{1,0:T(8,128)(2,1)S(1)}, bf16[1280,256]{1,0:T(8,128)(2,1)}, u32[]{:S(2)}, u32[]{:S(2)}) collective-permute-start(bf16[1280,256]{1,0:T(8,128)(2,1)S(1)} %get-tuple-element.58), channel_id=1, source_target_pairs={{0,1},{1,2},{2,3},{3,0},{4,5},{5,6},{6,7},{7,4},{8,9},{9,10},{10,1... | collective-permute-start | bytes 1966088 | tf_op jit(solution)/shard_map/ppermute | solution.py:22
  21.4 26.4 %collective-permute-start.8 = (bf16[512,1280]{1,0:T(8,128)(2,1)}, bf16[512,1280]{1,0:T(8,128)(2,1)}, u32[]{:S(2)}, u32[]{:S(2)}) collective-permute-start(bf16[512,1280]{1,0:T(8,128)(2,1)} %pad_maximum_fusion.refs_4_), channel_id=1, source_target_pairs={{0,32},{4,12},{8,40},{12,20},{16,48},{20,28},{24,56},{28,4},{32,64... | collective-permute-start | bytes 3932168 | tf_op jit(solution)/shard_map/ppermute | solution.py:37
  22.8 25.1 %collective-permute-start.9 = (bf16[512,1280]{1,0:T(8,128)(2,1)}, bf16[512,1280]{1,0:T(8,128)(2,1)}, u32[]{:S(2)}, u32[]{:S(2)}) collective-permute-start(bf16[512,1280]{1,0:T(8,128)(2,1)} %pad_maximum_fusion.refs_4_), channel_id=1, source_target_pairs={{0,96},{4,28},{8,104},{12,4},{16,112},{20,12},{24,120},{28,20},{32... | collective-permute-start | bytes 3932168 | tf_op jit(solution)/shard_map/ppermute | solution.py:37
  24.3 1.1 copy-start.10
  25.4 1.1 copy-start.11
  30.0 14.8 %all-to-all-start = ((f32[32,1,8]{2,1,0:T(1,128)}), f32[32,1,8]{2,1,0:T(1,128)S(1)}, u32[]{:S(2)}, u32[]{:S(2)}) async-start(f32[32,1,8]{2,1,0:T(1,128)} %broadcast_in_dim.18), calls=%async_computation | async-start | bytes 32768 | tf_op jit(solution)/shard_map/all_to_all | solution.py:42
  37.5 7.5 %copy-start.15 = (s32[4]{0:T(128)S(1)}, s32[4]{0:T(128)}, u32[]{:S(2)}) copy-start(s32[4]{0:T(128)} %param.16) | copy-start | bytes 52
  39.2 6.0 %collective-permute-start.7 = (f32[2,256]{1,0:T(2,128)S(1)}, f32[2,256]{1,0:T(2,128)S(1)}, u32[]{:S(2)}, u32[]{:S(2)}) collective-permute-start(f32[2,256]{1,0:T(2,128)S(1)} %pad_maximum_fusion.3), channel_id=1, source_target_pairs={{0,3},{1,0},{2,1},{3,2},{4,7},{5,4},{6,5},{7,6},{8,11},{9,8},{10,9... | collective-permute-start | bytes 6152 | tf_op jit(solution)/shard_map/ppermute | solution.py:22
  42.2 4.0 %collective-permute-start.6 = (f32[2,256]{1,0:T(2,128)S(1)}, f32[2,256]{1,0:T(2,128)S(1)}, u32[]{:S(2)}, u32[]{:S(2)}) collective-permute-start(f32[2,256]{1,0:T(2,128)S(1)} %pad_maximum_fusion.3), channel_id=1, source_target_pairs={{0,2},{1,3},{2,0},{3,1},{4,6},{5,7},{6,4},{7,5},{8,10},{9,11},{10,... | collective-permute-start | bytes 6152 | tf_op jit(solution)/shard_map/ppermute | solution.py:22
  42.2 4.0 %collective-permute-start.5 = (f32[2,256]{1,0:T(2,128)S(1)}, f32[2,256]{1,0:T(2,128)S(1)}, u32[]{:S(2)}, u32[]{:S(2)}) collective-permute-start(f32[2,256]{1,0:T(2,128)S(1)} %pad_maximum_fusion.3), channel_id=1, source_target_pairs={{0,1},{1,2},{2,3},{3,0},{4,5},{5,6},{6,7},{7,4},{8,9},{9,10},{10,1... | collective-permute-start | bytes 6152 | tf_op jit(solution)/shard_map/ppermute | solution.py:22
  45.2 22.0 %collective-permute-start.13 = (bf16[512,1280]{1,0:T(8,128)(2,1)}, bf16[512,1280]{1,0:T(8,128)(2,1)}, u32[]{:S(2)}, u32[]{:S(2)}) collective-permute-start(bf16[512,1280]{1,0:T(8,128)(2,1)} %pad_maximum_fusion.refs_4_), channel_id=1, source_target_pairs={{0,64},{4,20},{8,72},{12,28},{16,80},{20,4},{24,88},{28,12},{32,96... | collective-permute-start | bytes 3932168 | tf_op jit(solution)/shard_map/ppermute | solution.py:37
  47.8 19.3 %collective-permute-start.10 = (bf16[1280,256]{1,0:T(8,128)(2,1)S(1)}, bf16[1280,256]{1,0:T(8,128)(2,1)S(1)}, u32[]{:S(2)}, u32[]{:S(2)}) collective-permute-start(bf16[1280,256]{1,0:T(8,128)(2,1)S(1)} %subtract_convert_fusion.refs_0_.grad_ref), channel_id=1, source_target_pairs={{0,1},{1,2},{2,3},{3,0},{4,5},{5,6},{6,7},{7,4},{8,9},{9,10},{10,1... | collective-permute-start | bytes 1966088 | tf_op jit(solution)/shard_map/ppermute | solution.py:22
  49.9 17.3 %collective-permute-start.11 = (bf16[1280,256]{1,0:T(8,128)(2,1)S(1)}, bf16[1280,256]{1,0:T(8,128)(2,1)S(1)}, u32[]{:S(2)}, u32[]{:S(2)}) collective-permute-start(bf16[1280,256]{1,0:T(8,128)(2,1)S(1)} %subtract_convert_fusion.refs_0_.grad_ref), channel_id=1, source_target_pairs={{0,3},{1,0},{2,1},{3,2},{4,7},{5,4},{6,5},{7,6},{8,11},{9,8},{10,9... | collective-permute-start | bytes 1966088 | tf_op jit(solution)/shard_map/ppermute | solution.py:22
  51.3 6.3 %collective-permute-start.12 = (bf16[640,256]{1,0:T(8,128)(2,1)S(1)}, bf16[640,256]{1,0:T(8,128)(2,1)S(1)}, u32[]{:S(2)}, u32[]{:S(2)}) collective-permute-start(bf16[640,256]{1,0:T(8,128)(2,1)S(1)} %bitcast.67), channel_id=1, source_target_pairs={{0,4},{4,0},{1,5},{5,1},{2,6},{6,2},{3,7},{7,3},{8,12},{12,8},{9,1... | collective-permute-start | bytes 983048 | tf_op jit(solution)/shard_map/ppermute | solution.py:22
  56.5 1.2 copy-start
  57.6 0.7 copy-start.12
  60.0 39.6 %all-to-all-start.1 = ((bf16[32,16,1280]{2,1,0:T(8,128)(2,1)}), bf16[32,16,1280]{2,1,0:T(8,128)(2,1)}, u32[]{:S(2)}, u32[]{:S(2)}) async-start(bf16[32,16,1280]{2,1,0:T(8,128)(2,1)} %bitcast.39), calls=%async_computation.1 | async-start | bytes 2621440 | tf_op jit(solution)/shard_map/all_to_all | solution.py:71
  67.2 10.4 %collective-permute-start.14 = (bf16[640,256]{1,0:T(8,128)(2,1)S(1)}, bf16[640,256]{1,0:T(8,128)(2,1)S(1)}, u32[]{:S(2)}, u32[]{:S(2)}) collective-permute-start(bf16[640,256]{1,0:T(8,128)(2,1)S(1)} %slice.29), channel_id=1, source_target_pairs={{0,1},{1,2},{2,3},{3,0},{4,5},{5,6},{6,7},{7,4},{8,9},{9,10},{10,1... | collective-permute-start | bytes 983048 | tf_op jit(solution)/shard_map/ppermute | solution.py:22
  67.3 10.3 %collective-permute-start.15 = (bf16[640,256]{1,0:T(8,128)(2,1)S(1)}, bf16[640,256]{1,0:T(8,128)(2,1)S(1)}, u32[]{:S(2)}, u32[]{:S(2)}) collective-permute-start(bf16[640,256]{1,0:T(8,128)(2,1)S(1)} %slice.30), channel_id=1, source_target_pairs={{0,3},{1,0},{2,1},{3,2},{4,7},{5,4},{6,5},{7,6},{8,11},{9,8},{10,9... | collective-permute-start | bytes 983048 | tf_op jit(solution)/shard_map/ppermute | solution.py:22
  70.1 1.3 %copy-start.1 = (f32[256,1280]{1,0:T(8,128)S(1)}, f32[256,1280]{1,0:T(8,128)}, u32[]{:S(2)}) copy-start(f32[256,1280]{1,0:T(8,128)} %copy-done) | copy-start | bytes 3932164
  70.2 8.7 %collective-permute-start.16 = (bf16[1280,256]{1,0:T(8,128)(2,1)S(1)}, bf16[1280,256]{1,0:T(8,128)(2,1)S(1)}, u32[]{:S(2)}, u32[]{:S(2)}) collective-permute-start(bf16[1280,256]{1,0:T(8,128)(2,1)S(1)} %bitcast.65), channel_id=1, source_target_pairs={{0,4},{4,0},{1,5},{5,1},{2,6},{6,2},{3,7},{7,3},{8,12},{12,8},{9,1... | collective-permute-start | bytes 1966088 | tf_op jit(solution)/shard_map/ppermute | solution.py:22
  77.6 2.4 %copy-start.2 = (bf16[640,256]{1,0:T(8,128)(2,1)}, bf16[640,256]{1,0:T(8,128)(2,1)S(1)}, u32[]{:S(2)}) copy-start(bf16[640,256]{1,0:T(8,128)(2,1)S(1)} %collective-permute-done.14.refs_0_) | copy-start | bytes 983044
  77.6 2.4 %copy-start.4 = (bf16[640,256]{1,0:T(8,128)(2,1)}, bf16[640,256]{1,0:T(8,128)(2,1)S(1)}, u32[]{:S(2)}) copy-start(bf16[640,256]{1,0:T(8,128)(2,1)S(1)} %collective-permute-done.15.refs_1_) | copy-start | bytes 983044
  77.6 2.4 %copy-start.13 = (bf16[640,256]{1,0:T(8,128)(2,1)S(1)}, bf16[640,256]{1,0:T(8,128)(2,1)}, u32[]{:S(2)}) copy-start(bf16[640,256]{1,0:T(8,128)(2,1)} %copy-done.12) | copy-start | bytes 983044
  77.7 2.3 %collective-permute-start.17 = (bf16[640,256]{1,0:T(8,128)(2,1)S(1)}, bf16[640,256]{1,0:T(8,128)(2,1)S(1)}, u32[]{:S(2)}, u32[]{:S(2)}) collective-permute-start(bf16[640,256]{1,0:T(8,128)(2,1)S(1)} %bitcast.66), channel_id=1, source_target_pairs={{0,4},{4,0},{1,5},{5,1},{2,6},{6,2},{3,7},{7,3},{8,12},{12,8},{9,1... | collective-permute-start | bytes 983048 | tf_op jit(solution)/shard_map/ppermute | solution.py:22
  85.7 0.8 copy-start.6
  86.6 20.1 %collective-permute-start.18 = (bf16[1280,256]{1,0:T(8,128)(2,1)}, bf16[1280,256]{1,0:T(8,128)(2,1)S(1)}, u32[]{:S(2)}, u32[]{:S(2)}) collective-permute-start(bf16[1280,256]{1,0:T(8,128)(2,1)} %bitcast.33), channel_id=1, source_target_pairs={{0,32},{4,12},{8,40},{12,20},{16,48},{20,28},{24,56},{28,4},{32,64... | collective-permute-start | bytes 1966088 | tf_op jit(solution)/shard_map/ppermute | solution.py:37
  88.0 19.5 %collective-permute-start.19 = (bf16[1280,256]{1,0:T(8,128)(2,1)}, bf16[1280,256]{1,0:T(8,128)(2,1)}, u32[]{:S(2)}, u32[]{:S(2)}) collective-permute-start(bf16[1280,256]{1,0:T(8,128)(2,1)} %bitcast.34), channel_id=1, source_target_pairs={{0,64},{4,20},{8,72},{12,28},{16,80},{20,4},{24,88},{28,12},{32,96... | collective-permute-start | bytes 1966088 | tf_op jit(solution)/shard_map/ppermute | solution.py:37
  90.4 17.1 %collective-permute-start.20 = (bf16[1280,256]{1,0:T(8,128)(2,1)}, bf16[1280,256]{1,0:T(8,128)(2,1)}, u32[]{:S(2)}, u32[]{:S(2)}) collective-permute-start(bf16[1280,256]{1,0:T(8,128)(2,1)} %bitcast.35), channel_id=1, source_target_pairs={{0,96},{4,28},{8,104},{12,4},{16,112},{20,12},{24,120},{28,20},{32... | collective-permute-start | bytes 1966088 | tf_op jit(solution)/shard_map/ppermute | solution.py:37
  91.9 1.0 copy-start.3
  92.9 1.0 copy-start.5
  101.8 5.7 %copy-start.7 = (bf16[8,160,256]{2,1,0:T(8,128)(2,1)S(1)}, bf16[8,160,256]{2,1,0:T(8,128)(2,1)}, u32[]{:S(2)}) copy-start(bf16[8,160,256]{2,1,0:T(8,128)(2,1)} %copy-done.6) | copy-start | bytes 1966084
  101.8 20.9 %all-to-all-start.2 = ((bf16[32,24,640]{2,1,0:T(8,128)(2,1)}), bf16[32,24,640]{2,1,0:T(8,128)(2,1)S(1)}, u32[]{:S(2)}, u32[]{:S(2)}) async-start(bf16[32,24,640]{2,1,0:T(8,128)(2,1)} %bitcast.40), calls=%async_computation.2 | async-start | bytes 1966080 | tf_op jit(solution)/shard_map/all_to_all | solution.py:71
  106.7 0.8 copy-start.8
  107.5 1.1 copy-start.9
  116.9 8.8 %collective-permute-start.21 = (bf16[160,1280]{1,0:T(8,128)(2,1)}, bf16[160,1280]{1,0:T(8,128)(2,1)S(1)}, u32[]{:S(2)}, u32[]{:S(2)}) collective-permute-start(bf16[160,1280]{1,0:T(8,128)(2,1)} %get-tuple-element.85), channel_id=1, source_target_pairs={{0,16},{4,68},{8,24},{12,76},{16,0},{20,84},{24,8},{28,92},{32,48}... | collective-permute-start | bytes 1228808 | tf_op jit(solution)/shard_map/ppermute | solution.py:37
  119.8 10.4 %collective-permute-start.22 = (bf16[160,1280]{1,0:T(8,128)(2,1)S(1)}, bf16[160,1280]{1,0:T(8,128)(2,1)}, u32[]{:S(2)}, u32[]{:S(2)}) collective-permute-start(bf16[160,1280]{1,0:T(8,128)(2,1)S(1)} %get-tuple-element.86), channel_id=1, source_target_pairs={{0,8},{4,36},{8,16},{12,44},{16,24},{20,52},{24,0},{28,60},{32,40}... | collective-permute-start | bytes 1228808 | tf_op jit(solution)/shard_map/ppermute | solution.py:37
  120.1 10.4 %collective-permute-start.23 = (bf16[160,1280]{1,0:T(8,128)(2,1)S(1)}, bf16[160,1280]{1,0:T(8,128)(2,1)}, u32[]{:S(2)}, u32[]{:S(2)}) collective-permute-start(bf16[160,1280]{1,0:T(8,128)(2,1)S(1)} %get-tuple-element.87), channel_id=1, source_target_pairs={{0,24},{4,100},{8,0},{12,108},{16,8},{20,116},{24,16},{28,124},{32... | collective-permute-start | bytes 1228808 | tf_op jit(solution)/shard_map/ppermute | solution.py:37

commit v19 on v18

--- a/solution.py
+++ b/solution.py
@@ -372,7 +372,7 @@
             scratch_shapes=[pltpu.VMEM((height, tile), F32)],
         ),
         cost_estimate=FREE,
-        compiler_params=pltpu.CompilerParams(vmem_limit_bytes=42 * 1024 * 1024),
+        compiler_params=pltpu.CompilerParams(vmem_limit_bytes=56 * 1024 * 1024),
         name="weight_product",
     )(order, *pieces, *contexts)
 

time: 134 us -> 132 us (0.985)
    unnamed x38 -> x36, local copies, waits for them, and re-layouts: 8.78 us -> 7.76 us
where the time goes in v19:
time: 132 us; the launch traced here: 131 us
  starting transfers between devices  54.5 us (41%)
  Pallas kernels  46.1 us (35%)
  local copies, waits for them, and re-layouts  11.1 us (8%)
  waiting for transfers between devices  10.1 us (8%)
  other arithmetic  8.58 us (6%)
    ppermute x15, starting transfers between devices, shift(): lax.ppermute(value, axis, [(i, (i + step) % size) for i in range(size)])  20.8 us
    ppermute x9, starting transfers between devices, cross(): return lax.ppermute(value, DP, pairs)  14.5 us
    pallas_call x3, Pallas kernels, context_product(): pl.pallas_call(body, out_shape=jax.ShapeDtypeStruct((out_rows, width if s...  13.8 us
    all_to_all x2, starting transfers between devices, exchange(): return lax.all_to_all(blocks, DP, split_axis=0, concat_axis=0, tiled=True)  11.7 us
    pallas_call x3, Pallas kernels, forward_product(): pl.pallas_call(body, out_shape=[jax.ShapeDtypeStruct((tile, rows), BF16)]...  9.4 us
    pallas_call x1, Pallas kernels, weight_product(): pl.pallas_call(body, out_shape=[jax.ShapeDtypeStruct((block, width), BF16...  8.91 us
    unnamed x36, local copies, waits for them, and re-layouts  7.76 us
    all_to_all x1, starting transfers between devices, all_shares(): return lax.all_to_all(copies, DP, split_axis=0, concat_axis=0, tiled=True)  7.52 us
  transfers between devices with their start and end apart: 27, of which 7 were waited for; matrix products, arithmetic and copies ran while one was open for 8% of the time, Pallas kernels for 31%

profile of v19, /device:TPU:1, one launch (start us, length us, event | category | flops | bytes accessed | tf_op | source)
XLA Modules:
  0.0 131.5 jit_solution(17737266787950522083)
XLA Ops:
  0.6 2.9 %forward_product.3 = (bf16[640,256]{1,0:T(8,128)(2,1)S(1)}, bf16[640,256]{1,0:T(8,128)(2,1)S(1)}) custom-call(s32[1]{0:T(128)} %bitcast.5.which, bf16[5120,1280]{1,0:T(8,128)(2,1)} %refs_3_.3, bf16[256,1280]{1,0:T(8,128)(2,1)} %context_ref.6), custom_call_target="tpu_custom_call" | custom-call | tf_op jit(solution)/shard_map/forward_product/pallas_call | solution.py:223
  3.6 1.5 %collective-permute-start.2 = (bf16[256,1280]{1,0:T(8,128)(2,1)}, bf16[256,1280]{1,0:T(8,128)(2,1)S(1)}, u32[]{:S(2)}, u32[]{:S(2)}) collective-permute-start(bf16[256,1280]{1,0:T(8,128)(2,1)} %context_ref.6), channel_id=1, source_target_pairs={{0,4},{4,0},{1,5},{5,1},{2,6},{6,2},{3,7},{7,3},{8,12},{12,8},{9,1... | collective-permute-start | bytes 1966088 | tf_op jit(solution)/shard_map/ppermute | solution.py:22
  5.1 1.7 %collective-permute-start = (bf16[640,256]{1,0:T(8,128)(2,1)S(1)}, bf16[640,256]{1,0:T(8,128)(2,1)S(1)}, u32[]{:S(2)}, u32[]{:S(2)}) collective-permute-start(bf16[640,256]{1,0:T(8,128)(2,1)S(1)} %get-tuple-element.51), channel_id=1, source_target_pairs={{0,1},{1,2},{2,3},{3,0},{4,5},{5,6},{6,7},{7,4},{8,9},{9,10},{10,1... | collective-permute-start | bytes 983048 | tf_op jit(solution)/shard_map/ppermute | solution.py:22
  6.8 2.1 %collective-permute-start.1 = (bf16[640,256]{1,0:T(8,128)(2,1)S(1)}, bf16[640,256]{1,0:T(8,128)(2,1)S(1)}, u32[]{:S(2)}, u32[]{:S(2)}) collective-permute-start(bf16[640,256]{1,0:T(8,128)(2,1)S(1)} %get-tuple-element.52), channel_id=1, source_target_pairs={{0,3},{1,0},{2,1},{3,2},{4,7},{5,4},{6,5},{7,6},{8,11},{9,8},{10,9... | collective-permute-start | bytes 983048 | tf_op jit(solution)/shard_map/ppermute | solution.py:22
  8.9 2.9 %forward_product.4.refs_0_ = bf16[1280,256]{1,0:T(8,128)(2,1)S(1)} custom-call(s32[1]{0:T(128)} %bitcast.6.which, bf16[5120,1280]{1,0:T(8,128)(2,1)} %refs_3_.3, bf16[256,1280]{1,0:T(8,128)(2,1)} %context_ref.6), custom_call_target="tpu_custom_call" | custom-call | tf_op jit(solution)/shard_map/forward_product/pallas_call | solution.py:223
  11.8 3.6 %forward_product.5.refs_2_ = bf16[1280,256]{1,0:T(8,128)(2,1)} custom-call(s32[1]{0:T(128)} %bitcast.7.which, bf16[5120,1280]{1,0:T(8,128)(2,1)} %refs_3_.3, bf16[256,1280]{1,0:T(8,128)(2,1)} %context_ref.6), custom_call_target="tpu_custom_call" | custom-call | tf_op jit(solution)/shard_map/forward_product/pallas_call | solution.py:223
  15.4 2.3 %pad_maximum_fusion.refs_4_ = bf16[512,1280]{1,0:T(8,128)(2,1)} fusion(bf16[256,1280]{1,0:T(8,128)(2,1)S(1)} %collective-permute-done.2, bf16[256,1280]{1,0:T(8,128)(2,1)} %context_ref.6), kind=kLoop, calls=%fused_computation.2 | loop fusion | flops 2621440 | bytes 2621440 | tf_op jit(solution)/shard_map/concatenate | solution.py:391
  17.7 1.8 %top_up.1 = (bf16[1280,256]{1,0:T(8,128)(2,1)S(1)}, bf16[1280,256]{1,0:T(8,128)(2,1)}) custom-call(bf16[1280,256]{1,0:T(8,128)(2,1)S(1)} %forward_product.4.refs_0_, bf16[640,256]{1,0:T(8,128)(2,1)S(1)} %collective-permute-done.refs_1_, bf16[1280,256]{1,0:T(8,128)(2,1)} %forward_product.5.refs_2_, ...), custom_call_target="tpu_custom_call", output_to_operand_aliasing={{0}: (0, {}), {1}: (2, {})} | custom-call | tf_op jit(solution)/shard_map/top_up/pallas_call | solution.py:192
  19.5 1.6 %collective-permute-start.4 = (bf16[1280,256]{1,0:T(8,128)(2,1)}, bf16[1280,256]{1,0:T(8,128)(2,1)}, u32[]{:S(2)}, u32[]{:S(2)}) collective-permute-start(bf16[1280,256]{1,0:T(8,128)(2,1)} %get-tuple-element.59), channel_id=1, source_target_pairs={{0,3},{1,0},{2,1},{3,2},{4,7},{5,4},{6,5},{7,6},{8,11},{9,8},{10,9... | collective-permute-start | bytes 1966088 | tf_op jit(solution)/shard_map/ppermute | solution.py:22
  21.4 1.4 %collective-permute-start.8 = (bf16[512,1280]{1,0:T(8,128)(2,1)}, bf16[512,1280]{1,0:T(8,128)(2,1)}, u32[]{:S(2)}, u32[]{:S(2)}) collective-permute-start(bf16[512,1280]{1,0:T(8,128)(2,1)} %pad_maximum_fusion.refs_4_), channel_id=1, source_target_pairs={{0,32},{4,12},{8,40},{12,20},{16,48},{20,28},{24,56},{28,4},{32,64... | collective-permute-start | bytes 3932168 | tf_op jit(solution)/shard_map/ppermute | solution.py:37
  22.8 1.5 %collective-permute-start.9 = (bf16[512,1280]{1,0:T(8,128)(2,1)}, bf16[512,1280]{1,0:T(8,128)(2,1)}, u32[]{:S(2)}, u32[]{:S(2)}) collective-permute-start(bf16[512,1280]{1,0:T(8,128)(2,1)} %pad_maximum_fusion.refs_4_), channel_id=1, source_target_pairs={{0,96},{4,28},{8,104},{12,4},{16,112},{20,12},{24,120},{28,20},{32... | collective-permute-start | bytes 3932168 | tf_op jit(solution)/shard_map/ppermute | solution.py:37
  24.3 1.1 copy-done.7
  25.4 1.1 copy-done.8
  26.5 2.9 %hidden_part.1 = (f32[1280,256]{1,0:T(8,128)S(1)}, f32[1280,256]{1,0:T(8,128)S(1)}) custom-call(s32[1]{0:T(128)} %bitcast.4.which, bf16[5120,1280]{1,0:T(8,128)(2,1)} %refs_3_.3, bf16[256,1280]{1,0:T(8,128)(2,1)} %context_ref.6, bf16[256,1280]{1,0:T(8,128)(2,1)S(1)} %copy-done.7, bf16[256,1280]{1,0:T(8,128)(2,1)S(1)} %copy-done.8, ...), custom_call_target="tpu_custom_call" | custom-call | tf_op jit(solution)/shard_map/hidden_part/pallas_call | solution.py:258
  30.0 7.5 %all-to-all-start = ((f32[32,1,8]{2,1,0:T(1,128)}), f32[32,1,8]{2,1,0:T(1,128)S(1)}, u32[]{:S(2)}, u32[]{:S(2)}) async-start(f32[32,1,8]{2,1,0:T(1,128)} %broadcast_in_dim.18), calls=%async_computation | async-start | bytes 32768 | tf_op jit(solution)/shard_map/all_to_all | solution.py:42
  37.5 1.6 %multiply_reduce_fusion.1 = (f32[256]{0:T(256)S(1)}, f32[256]{0:T(256)S(1)}) fusion(bf16[1280,256]{1,0:T(8,128)(2,1)} %collective-permute-done.4, f32[1280,256]{1,0:T(8,128)S(1)} %get-tuple-element.61, bf16[1280,256]{1,0:T(8,128)(2,1)} %collective-permute-done.3, f32[1280,256]{1,0:T(8,128)S(1)} %get-tuple-element.62), kind=kLoop, calls=%fused_computation.5 | loop fusion | flops 2620928 | bytes 3934208 | tf_op jit(solution)/shard_map/reduce_sum | solution.py:407
  39.2 3.0 %collective-permute-start.7 = (f32[2,256]{1,0:T(2,128)S(1)}, f32[2,256]{1,0:T(2,128)S(1)}, u32[]{:S(2)}, u32[]{:S(2)}) collective-permute-start(f32[2,256]{1,0:T(2,128)S(1)} %pad_maximum_fusion.3), channel_id=1, source_target_pairs={{0,3},{1,0},{2,1},{3,2},{4,7},{5,4},{6,5},{7,6},{8,11},{9,8},{10,9... | collective-permute-start | bytes 6152 | tf_op jit(solution)/shard_map/ppermute | solution.py:22
  42.9 1.9 %all-to-all-done = f32[32,1,8]{2,1,0:T(1,128)S(1)} async-done(((f32[32,1,8]{2,1,0:T(1,128)}), f32[32,1,8]{2,1,0:T(1,128)S(1)}, u32[]{:S(2)}, u32[]{:S(2)}) %all-to-all-start) | async-done | bytes 1056 | tf_op jit(solution)/shard_map/all_to_all | solution.py:42
  45.2 1.0 collective-permute-start.13
  46.2 1.6 %subtract_convert_fusion.refs_0_.grad_ref = bf16[1280,256]{1,0:T(8,128)(2,1)S(1)} fusion(f32[1280,256]{1,0:T(8,128)S(1)} %get-tuple-element.62, f32[256]{0:T(256)S(1)} %bitcast.74, f32[256]{0:T(256)S(1)} %bitcast.73, bf16[1280,256]{1,0:T(8,128)(2,1)} %collective-permute-done.4, f32[1280,256]{1,0:T(8,128)S(1)} %get-tuple-element.61, ...), kind=kLoop, calls=%fused_computation.3 | loop fusion | flops 2621440 | bytes 4589568 | tf_op jit(solution)/shard_map/convert_element_type | solution.py:423
  47.8 2.0 %collective-permute-start.10 = (bf16[1280,256]{1,0:T(8,128)(2,1)S(1)}, bf16[1280,256]{1,0:T(8,128)(2,1)S(1)}, u32[]{:S(2)}, u32[]{:S(2)}) collective-permute-start(bf16[1280,256]{1,0:T(8,128)(2,1)S(1)} %subtract_convert_fusion.refs_0_.grad_ref), channel_id=1, source_target_pairs={{0,1},{1,2},{2,3},{3,0},{4,5},{5,6},{6,7},{7,4},{8,9},{9,10},{10,1... | collective-permute-start | bytes 1966088 | tf_op jit(solution)/shard_map/ppermute | solution.py:22
  49.9 1.1 collective-permute-start.11
  51.3 2.1 %collective-permute-start.12 = (bf16[640,256]{1,0:T(8,128)(2,1)S(1)}, bf16[640,256]{1,0:T(8,128)(2,1)S(1)}, u32[]{:S(2)}, u32[]{:S(2)}) collective-permute-start(bf16[640,256]{1,0:T(8,128)(2,1)S(1)} %bitcast.67), channel_id=1, source_target_pairs={{0,4},{4,0},{1,5},{5,1},{2,6},{6,2},{3,7},{7,3},{8,12},{12,8},{9,1... | collective-permute-start | bytes 983048 | tf_op jit(solution)/shard_map/ppermute | solution.py:22
  53.5 3.0 %context_product.3.refs_4_ = f32[256,1280]{1,0:T(8,128)S(1)} custom-call(s32[1]{0:T(128)} %bitcast.4.which, bf16[1280,256]{1,0:T(8,128)(2,1)S(1)} %subtract_convert_fusion.refs_0_.grad_ref, bf16[5120,1280]{1,0:T(8,128)(2,1)} %refs_3_.3), custom_call_target="tpu_custom_call" | custom-call | tf_op jit(solution)/shard_map/context_product/pallas_call | solution.py:126
  56.5 1.2 copy-done
  58.4 1.6 %place_rows.1 = bf16[512,1280]{1,0:T(8,128)(2,1)} custom-call(bf16[512,256]{1,0:T(8,128)(2,1)S(1)} %fusion.1.slots_ref, bf16[1280,256]{1,0:T(8,128)(2,1)S(1)} %subtract_convert_fusion.refs_0_.grad_ref), custom_call_target="tpu_custom_call" | custom-call | tf_op jit(solution)/shard_map/place_rows/pallas_call | solution.py:173
  60.0 7.2 %all-to-all-start.1 = ((bf16[32,16,1280]{2,1,0:T(8,128)(2,1)}), bf16[32,16,1280]{2,1,0:T(8,128)(2,1)}, u32[]{:S(2)}, u32[]{:S(2)}) async-start(bf16[32,16,1280]{2,1,0:T(8,128)(2,1)} %bitcast.39), calls=%async_computation.1 | async-start | bytes 2621440 | tf_op jit(solution)/shard_map/all_to_all | solution.py:71
  67.3 2.7 %collective-permute-start.15 = (bf16[640,256]{1,0:T(8,128)(2,1)S(1)}, bf16[640,256]{1,0:T(8,128)(2,1)S(1)}, u32[]{:S(2)}, u32[]{:S(2)}) collective-permute-start(bf16[640,256]{1,0:T(8,128)(2,1)S(1)} %slice.30), channel_id=1, source_target_pairs={{0,3},{1,0},{2,1},{3,2},{4,7},{5,4},{6,5},{7,6},{8,11},{9,8},{10,9... | collective-permute-start | bytes 983048 | tf_op jit(solution)/shard_map/ppermute | solution.py:22
  70.2 1.1 collective-permute-start.16
  71.4 5.1 %context_product.4.refs_4_ = f32[256,1280]{1,0:T(8,128)S(1)} custom-call(s32[2]{0:T(128)S(1)} %pad_add_fusion.1.which, bf16[1280,256]{1,0:T(8,128)(2,1)S(1)} %collective-permute-done.11.refs_0_, bf16[1280,256]{1,0:T(8,128)(2,1)S(1)} %collective-permute-done.10.refs_1_, bf16[5120,1280]{1,0:T(8,128)(2,1)} %refs_3_.3, bf16[5120,1280]{1,0:T(8,128)(2,1)} %refs_3_.3, ...), custom_call_target="tpu_custom_call" | custom-call | tf_op jit(solution)/shard_map/context_product/pallas_call | solution.py:126
  76.5 1.1 collective-permute-done.14.refs_0_
  77.7 1.1 collective-permute-start.17
  78.9 1.1 collective-permute-done.17
  80.1 5.7 %lay_out.1 = (bf16[8,160,256]{2,1,0:T(8,128)(2,1)S(1)}, bf16[8,160,256]{2,1,0:T(8,128)(2,1)}, bf16[8,160,256]{2,1,0:T(8,128)(2,1)}, bf16[8,160,256]{2,1,0:T(8,128)(2,1)}) custom-call(s32[4]{0:T(128)S(1)} %pad_add_fusion.2.where, bf16[4,2,160,256]{3,2,1,0:T(8,128)(2,1)S(1)} %bitcast.50, bf16[4,2,160,256]{3,2,1,0:T(8,128)(2,1)S(1)} %bitcast.54, ...), custom_call_target="tpu_custom_call" | custom-call | tf_op jit(solution)/shard_map/lay_out/pallas_call | solution.py:326
  86.6 1.4 %collective-permute-start.18 = (bf16[1280,256]{1,0:T(8,128)(2,1)}, bf16[1280,256]{1,0:T(8,128)(2,1)S(1)}, u32[]{:S(2)}, u32[]{:S(2)}) collective-permute-start(bf16[1280,256]{1,0:T(8,128)(2,1)} %bitcast.33), channel_id=1, source_target_pairs={{0,32},{4,12},{8,40},{12,20},{16,48},{20,28},{24,56},{28,4},{32,64... | collective-permute-start | bytes 1966088 | tf_op jit(solution)/shard_map/ppermute | solution.py:37
  88.0 2.4 %collective-permute-start.19 = (bf16[1280,256]{1,0:T(8,128)(2,1)}, bf16[1280,256]{1,0:T(8,128)(2,1)}, u32[]{:S(2)}, u32[]{:S(2)}) collective-permute-start(bf16[1280,256]{1,0:T(8,128)(2,1)} %bitcast.34), channel_id=1, source_target_pairs={{0,64},{4,20},{8,72},{12,28},{16,80},{20,4},{24,88},{28,12},{32,96... | collective-permute-start | bytes 1966088 | tf_op jit(solution)/shard_map/ppermute | solution.py:37
  90.4 1.2 collective-permute-start.20
  91.9 1.0 copy-done.3
  93.9 5.8 %context_product.5 = bf16[768,640]{1,0:T(8,128)(2,1)} custom-call(s32[2]{0:T(128)S(1)} %pad_add_fusion.3.which, bf16[640,256]{1,0:T(8,128)(2,1)S(1)} %copy-done.3, bf16[640,256]{1,0:T(8,128)(2,1)S(1)} %copy-done.5, bf16[5120,1280]{1,0:T(8,128)(2,1)} %refs_3_.3, bf16[5120,1280]{1,0:T(8,128)(2,1)} %refs_3_.3, f32[256,1280]{1,0:T(8,128)S(1)} %context_product.4.refs_4_, ...), custom_call_target="tpu_custom_call" | custom-call | tf_op jit(solution)/shard_map/context_product/pallas_call | solution.py:126
  99.7 2.2 %reshape.217 = bf16[384,1280]{1,0:T(8,128)(2,1)} reshape(bf16[32,12,1280]{2,1,0:T(8,128)(2,1)} %bitcast.48) | data formatting | bytes 1966080 | tf_op jit(solution)/shard_map/reshape | solution.py:76
  101.8 4.5 %all-to-all-start.2 = ((bf16[32,24,640]{2,1,0:T(8,128)(2,1)}), bf16[32,24,640]{2,1,0:T(8,128)(2,1)S(1)}, u32[]{:S(2)}, u32[]{:S(2)}) async-start(bf16[32,24,640]{2,1,0:T(8,128)(2,1)} %bitcast.40), calls=%async_computation.2 | async-start | bytes 1966080 | tf_op jit(solution)/shard_map/all_to_all | solution.py:71
  107.9 8.9 %weight_product.1 = (f32[160,1280]{1,0:T(8,128)}, bf16[160,1280]{1,0:T(8,128)(2,1)}, bf16[160,1280]{1,0:T(8,128)(2,1)}, bf16[160,1280]{1,0:T(8,128)(2,1)}) custom-call(s32[4]{0:T(128)} %pad_add_fusion.order_ref, bf16[1280,256]{1,0:T(8,128)(2,1)} %bitcast.62, bf16[1280,256]{1,0:T(8,128)(2,1)} %copy-done.12, ...), custom_call_target="tpu_custom_call" | custom-call | tf_op jit(solution)/shard_map/weight_product/pallas_call | solution.py:363
  116.9 3.0 %collective-permute-start.21 = (bf16[160,1280]{1,0:T(8,128)(2,1)}, bf16[160,1280]{1,0:T(8,128)(2,1)S(1)}, u32[]{:S(2)}, u32[]{:S(2)}) collective-permute-start(bf16[160,1280]{1,0:T(8,128)(2,1)} %get-tuple-element.85), channel_id=1, source_target_pairs={{0,16},{4,68},{8,24},{12,76},{16,0},{20,84},{24,8},{28,92},{32,48}... | collective-permute-start | bytes 1228808 | tf_op jit(solution)/shard_map/ppermute | solution.py:37
  120.2 2.4 %collective-permute-start.23 = (bf16[160,1280]{1,0:T(8,128)(2,1)}, bf16[160,1280]{1,0:T(8,128)(2,1)S(1)}, u32[]{:S(2)}, u32[]{:S(2)}) collective-permute-start(bf16[160,1280]{1,0:T(8,128)(2,1)} %get-tuple-element.87), channel_id=1, source_target_pairs={{0,24},{4,100},{8,0},{12,108},{16,8},{20,116},{24,16},{28,124},{32... | collective-permute-start | bytes 1228808 | tf_op jit(solution)/shard_map/ppermute | solution.py:37
  122.6 2.0 %unfold.1 = bf16[384,1280]{1,0:T(8,128)(2,1)} custom-call(bf16[768,640]{1,0:T(8,128)(2,1)S(1)} %bitcast.55), custom_call_target="tpu_custom_call" | custom-call | tf_op jit(solution)/shard_map/unfold/pallas_call | solution.py:158
  124.7 1.1 collective-permute-done.21
  125.8 4.4 %collective-permute-done.22 = bf16[160,1280]{1,0:T(8,128)(2,1)S(1)} collective-permute-done((bf16[160,1280]{1,0:T(8,128)(2,1)}, bf16[160,1280]{1,0:T(8,128)(2,1)S(1)}, u32[]{:S(2)}, u32[]{:S(2)}) %collective-permute-start.22) | collective-permute-done | bytes 409632 | tf_op jit(solution)/shard_map/ppermute | solution.py:37
  130.4 1.1 add_multiply_fusion
  (92 shorter events, 8.1 us)
Async XLA Ops:
  3.6 11.8 %collective-permute-start.2 = (bf16[256,1280]{1,0:T(8,128)(2,1)}, bf16[256,1280]{1,0:T(8,128)(2,1)S(1)}, u32[]{:S(2)}, u32[]{:S(2)}) collective-permute-start(bf16[256,1280]{1,0:T(8,128)(2,1)} %context_ref.6), channel_id=1, source_target_pairs={{0,4},{4,0},{1,5},{5,1},{2,6},{6,2},{3,7},{7,3},{8,12},{12,8},{9,1... | collective-permute-start | bytes 1966088 | tf_op jit(solution)/shard_map/ppermute | solution.py:22
  5.1 12.6 %collective-permute-start = (bf16[640,256]{1,0:T(8,128)(2,1)S(1)}, bf16[640,256]{1,0:T(8,128)(2,1)S(1)}, u32[]{:S(2)}, u32[]{:S(2)}) collective-permute-start(bf16[640,256]{1,0:T(8,128)(2,1)S(1)} %get-tuple-element.51), channel_id=1, source_target_pairs={{0,1},{1,2},{2,3},{3,0},{4,5},{5,6},{6,7},{7,4},{8,9},{9,10},{10,1... | collective-permute-start | bytes 983048 | tf_op jit(solution)/shard_map/ppermute | solution.py:22
  6.8 10.9 %collective-permute-start.1 = (bf16[640,256]{1,0:T(8,128)(2,1)S(1)}, bf16[640,256]{1,0:T(8,128)(2,1)S(1)}, u32[]{:S(2)}, u32[]{:S(2)}) collective-permute-start(bf16[640,256]{1,0:T(8,128)(2,1)S(1)} %get-tuple-element.52), channel_id=1, source_target_pairs={{0,3},{1,0},{2,1},{3,2},{4,7},{5,4},{6,5},{7,6},{8,11},{9,8},{10,9... | collective-permute-start | bytes 983048 | tf_op jit(solution)/shard_map/ppermute | solution.py:22
  17.7 3.4 %copy-start.13 = (f32[1280]{0:T(1024)S(1)}, f32[1280]{0:T(1024)}, u32[]{:S(2)}) copy-start(f32[1280]{0:T(1024)} %param.13) | copy-start | bytes 15364
  17.7 3.4 %copy-start.15 = (s32[64,1]{0,1:T(1,128)S(1)}, s32[64,1]{0,1:T(1,128)}, u32[]{:S(2)}) copy-start(s32[64,1]{0,1:T(1,128)} %param.17) | copy-start | bytes 772
  17.7 3.6 %copy-start.16 = (f32[4]{0:T(128)S(1)}, f32[4]{0:T(128)}, u32[]{:S(2)}) copy-start(f32[4]{0:T(128)} %param.14) | copy-start | bytes 52
  17.7 3.6 %copy-start.17 = (s32[4]{0:T(128)S(1)}, s32[4]{0:T(128)}, u32[]{:S(2)}) copy-start(s32[4]{0:T(128)} %param.15) | copy-start | bytes 52
  19.5 18.0 %collective-permute-start.4 = (bf16[1280,256]{1,0:T(8,128)(2,1)}, bf16[1280,256]{1,0:T(8,128)(2,1)}, u32[]{:S(2)}, u32[]{:S(2)}) collective-permute-start(bf16[1280,256]{1,0:T(8,128)(2,1)} %get-tuple-element.59), channel_id=1, source_target_pairs={{0,3},{1,0},{2,1},{3,2},{4,7},{5,4},{6,5},{7,6},{8,11},{9,8},{10,9... | collective-permute-start | bytes 1966088 | tf_op jit(solution)/shard_map/ppermute | solution.py:22
  21.1 16.4 %collective-permute-start.3 = (bf16[1280,256]{1,0:T(8,128)(2,1)S(1)}, bf16[1280,256]{1,0:T(8,128)(2,1)}, u32[]{:S(2)}, u32[]{:S(2)}) collective-permute-start(bf16[1280,256]{1,0:T(8,128)(2,1)S(1)} %get-tuple-element.58), channel_id=1, source_target_pairs={{0,1},{1,2},{2,3},{3,0},{4,5},{5,6},{6,7},{7,4},{8,9},{9,10},{10,1... | collective-permute-start | bytes 1966088 | tf_op jit(solution)/shard_map/ppermute | solution.py:22
  21.4 26.4 %collective-permute-start.8 = (bf16[512,1280]{1,0:T(8,128)(2,1)}, bf16[512,1280]{1,0:T(8,128)(2,1)}, u32[]{:S(2)}, u32[]{:S(2)}) collective-permute-start(bf16[512,1280]{1,0:T(8,128)(2,1)} %pad_maximum_fusion.refs_4_), channel_id=1, source_target_pairs={{0,32},{4,12},{8,40},{12,20},{16,48},{20,28},{24,56},{28,4},{32,64... | collective-permute-start | bytes 3932168 | tf_op jit(solution)/shard_map/ppermute | solution.py:37
  22.8 25.1 %collective-permute-start.9 = (bf16[512,1280]{1,0:T(8,128)(2,1)}, bf16[512,1280]{1,0:T(8,128)(2,1)}, u32[]{:S(2)}, u32[]{:S(2)}) collective-permute-start(bf16[512,1280]{1,0:T(8,128)(2,1)} %pad_maximum_fusion.refs_4_), channel_id=1, source_target_pairs={{0,96},{4,28},{8,104},{12,4},{16,112},{20,12},{24,120},{28,20},{32... | collective-permute-start | bytes 3932168 | tf_op jit(solution)/shard_map/ppermute | solution.py:37
  24.3 1.1 copy-start.7
  25.4 1.1 copy-start.8
  30.0 14.8 %all-to-all-start = ((f32[32,1,8]{2,1,0:T(1,128)}), f32[32,1,8]{2,1,0:T(1,128)S(1)}, u32[]{:S(2)}, u32[]{:S(2)}) async-start(f32[32,1,8]{2,1,0:T(1,128)} %broadcast_in_dim.18), calls=%async_computation | async-start | bytes 32768 | tf_op jit(solution)/shard_map/all_to_all | solution.py:42
  37.5 7.5 %copy-start.14 = (s32[4]{0:T(128)S(1)}, s32[4]{0:T(128)}, u32[]{:S(2)}) copy-start(s32[4]{0:T(128)} %param.16) | copy-start | bytes 52
  39.2 6.0 %collective-permute-start.7 = (f32[2,256]{1,0:T(2,128)S(1)}, f32[2,256]{1,0:T(2,128)S(1)}, u32[]{:S(2)}, u32[]{:S(2)}) collective-permute-start(f32[2,256]{1,0:T(2,128)S(1)} %pad_maximum_fusion.3), channel_id=1, source_target_pairs={{0,3},{1,0},{2,1},{3,2},{4,7},{5,4},{6,5},{7,6},{8,11},{9,8},{10,9... | collective-permute-start | bytes 6152 | tf_op jit(solution)/shard_map/ppermute | solution.py:22
  42.2 4.0 %collective-permute-start.6 = (f32[2,256]{1,0:T(2,128)S(1)}, f32[2,256]{1,0:T(2,128)S(1)}, u32[]{:S(2)}, u32[]{:S(2)}) collective-permute-start(f32[2,256]{1,0:T(2,128)S(1)} %pad_maximum_fusion.3), channel_id=1, source_target_pairs={{0,2},{1,3},{2,0},{3,1},{4,6},{5,7},{6,4},{7,5},{8,10},{9,11},{10,... | collective-permute-start | bytes 6152 | tf_op jit(solution)/shard_map/ppermute | solution.py:22
  42.2 4.0 %collective-permute-start.5 = (f32[2,256]{1,0:T(2,128)S(1)}, f32[2,256]{1,0:T(2,128)S(1)}, u32[]{:S(2)}, u32[]{:S(2)}) collective-permute-start(f32[2,256]{1,0:T(2,128)S(1)} %pad_maximum_fusion.3), channel_id=1, source_target_pairs={{0,1},{1,2},{2,3},{3,0},{4,5},{5,6},{6,7},{7,4},{8,9},{9,10},{10,1... | collective-permute-start | bytes 6152 | tf_op jit(solution)/shard_map/ppermute | solution.py:22
  45.2 22.0 %collective-permute-start.13 = (bf16[512,1280]{1,0:T(8,128)(2,1)}, bf16[512,1280]{1,0:T(8,128)(2,1)}, u32[]{:S(2)}, u32[]{:S(2)}) collective-permute-start(bf16[512,1280]{1,0:T(8,128)(2,1)} %pad_maximum_fusion.refs_4_), channel_id=1, source_target_pairs={{0,64},{4,20},{8,72},{12,28},{16,80},{20,4},{24,88},{28,12},{32,96... | collective-permute-start | bytes 3932168 | tf_op jit(solution)/shard_map/ppermute | solution.py:37
  47.8 19.3 %collective-permute-start.10 = (bf16[1280,256]{1,0:T(8,128)(2,1)S(1)}, bf16[1280,256]{1,0:T(8,128)(2,1)S(1)}, u32[]{:S(2)}, u32[]{:S(2)}) collective-permute-start(bf16[1280,256]{1,0:T(8,128)(2,1)S(1)} %subtract_convert_fusion.refs_0_.grad_ref), channel_id=1, source_target_pairs={{0,1},{1,2},{2,3},{3,0},{4,5},{5,6},{6,7},{7,4},{8,9},{9,10},{10,1... | collective-permute-start | bytes 1966088 | tf_op jit(solution)/shard_map/ppermute | solution.py:22
  49.9 17.3 %collective-permute-start.11 = (bf16[1280,256]{1,0:T(8,128)(2,1)S(1)}, bf16[1280,256]{1,0:T(8,128)(2,1)S(1)}, u32[]{:S(2)}, u32[]{:S(2)}) collective-permute-start(bf16[1280,256]{1,0:T(8,128)(2,1)S(1)} %subtract_convert_fusion.refs_0_.grad_ref), channel_id=1, source_target_pairs={{0,3},{1,0},{2,1},{3,2},{4,7},{5,4},{6,5},{7,6},{8,11},{9,8},{10,9... | collective-permute-start | bytes 1966088 | tf_op jit(solution)/shard_map/ppermute | solution.py:22
  51.3 6.3 %collective-permute-start.12 = (bf16[640,256]{1,0:T(8,128)(2,1)S(1)}, bf16[640,256]{1,0:T(8,128)(2,1)S(1)}, u32[]{:S(2)}, u32[]{:S(2)}) collective-permute-start(bf16[640,256]{1,0:T(8,128)(2,1)S(1)} %bitcast.67), channel_id=1, source_target_pairs={{0,4},{4,0},{1,5},{5,1},{2,6},{6,2},{3,7},{7,3},{8,12},{12,8},{9,1... | collective-permute-start | bytes 983048 | tf_op jit(solution)/shard_map/ppermute | solution.py:22
  56.5 1.2 copy-start
  57.6 0.7 copy-start.9
  60.0 39.7 %all-to-all-start.1 = ((bf16[32,16,1280]{2,1,0:T(8,128)(2,1)}), bf16[32,16,1280]{2,1,0:T(8,128)(2,1)}, u32[]{:S(2)}, u32[]{:S(2)}) async-start(bf16[32,16,1280]{2,1,0:T(8,128)(2,1)} %bitcast.39), calls=%async_computation.1 | async-start | bytes 2621440 | tf_op jit(solution)/shard_map/all_to_all | solution.py:71
  67.2 10.4 %collective-permute-start.14 = (bf16[640,256]{1,0:T(8,128)(2,1)S(1)}, bf16[640,256]{1,0:T(8,128)(2,1)S(1)}, u32[]{:S(2)}, u32[]{:S(2)}) collective-permute-start(bf16[640,256]{1,0:T(8,128)(2,1)S(1)} %slice.29), channel_id=1, source_target_pairs={{0,1},{1,2},{2,3},{3,0},{4,5},{5,6},{6,7},{7,4},{8,9},{9,10},{10,1... | collective-permute-start | bytes 983048 | tf_op jit(solution)/shard_map/ppermute | solution.py:22
  67.3 10.3 %collective-permute-start.15 = (bf16[640,256]{1,0:T(8,128)(2,1)S(1)}, bf16[640,256]{1,0:T(8,128)(2,1)S(1)}, u32[]{:S(2)}, u32[]{:S(2)}) collective-permute-start(bf16[640,256]{1,0:T(8,128)(2,1)S(1)} %slice.30), channel_id=1, source_target_pairs={{0,3},{1,0},{2,1},{3,2},{4,7},{5,4},{6,5},{7,6},{8,11},{9,8},{10,9... | collective-permute-start | bytes 983048 | tf_op jit(solution)/shard_map/ppermute | solution.py:22
  70.1 1.3 %copy-start.1 = (f32[256,1280]{1,0:T(8,128)S(1)}, f32[256,1280]{1,0:T(8,128)}, u32[]{:S(2)}) copy-start(f32[256,1280]{1,0:T(8,128)} %copy-done) | copy-start | bytes 3932164
  70.2 8.7 %collective-permute-start.16 = (bf16[1280,256]{1,0:T(8,128)(2,1)S(1)}, bf16[1280,256]{1,0:T(8,128)(2,1)S(1)}, u32[]{:S(2)}, u32[]{:S(2)}) collective-permute-start(bf16[1280,256]{1,0:T(8,128)(2,1)S(1)} %bitcast.65), channel_id=1, source_target_pairs={{0,4},{4,0},{1,5},{5,1},{2,6},{6,2},{3,7},{7,3},{8,12},{12,8},{9,1... | collective-permute-start | bytes 1966088 | tf_op jit(solution)/shard_map/ppermute | solution.py:22
  77.6 2.4 %copy-start.2 = (bf16[640,256]{1,0:T(8,128)(2,1)}, bf16[640,256]{1,0:T(8,128)(2,1)S(1)}, u32[]{:S(2)}) copy-start(bf16[640,256]{1,0:T(8,128)(2,1)S(1)} %collective-permute-done.14.refs_0_) | copy-start | bytes 983044
  77.6 2.4 %copy-start.4 = (bf16[640,256]{1,0:T(8,128)(2,1)}, bf16[640,256]{1,0:T(8,128)(2,1)S(1)}, u32[]{:S(2)}) copy-start(bf16[640,256]{1,0:T(8,128)(2,1)S(1)} %collective-permute-done.15.refs_1_) | copy-start | bytes 983044
  77.6 2.4 %copy-start.10 = (bf16[640,256]{1,0:T(8,128)(2,1)S(1)}, bf16[640,256]{1,0:T(8,128)(2,1)}, u32[]{:S(2)}) copy-start(bf16[640,256]{1,0:T(8,128)(2,1)} %copy-done.9) | copy-start | bytes 983044
  77.7 2.3 %collective-permute-start.17 = (bf16[640,256]{1,0:T(8,128)(2,1)S(1)}, bf16[640,256]{1,0:T(8,128)(2,1)S(1)}, u32[]{:S(2)}, u32[]{:S(2)}) collective-permute-start(bf16[640,256]{1,0:T(8,128)(2,1)S(1)} %bitcast.66), channel_id=1, source_target_pairs={{0,4},{4,0},{1,5},{5,1},{2,6},{6,2},{3,7},{7,3},{8,12},{12,8},{9,1... | collective-permute-start | bytes 983048 | tf_op jit(solution)/shard_map/ppermute | solution.py:22
  85.7 0.9 copy-start.6
  86.6 20.5 %collective-permute-start.18 = (bf16[1280,256]{1,0:T(8,128)(2,1)}, bf16[1280,256]{1,0:T(8,128)(2,1)S(1)}, u32[]{:S(2)}, u32[]{:S(2)}) collective-permute-start(bf16[1280,256]{1,0:T(8,128)(2,1)} %bitcast.33), channel_id=1, source_target_pairs={{0,32},{4,12},{8,40},{12,20},{16,48},{20,28},{24,56},{28,4},{32,64... | collective-permute-start | bytes 1966088 | tf_op jit(solution)/shard_map/ppermute | solution.py:37
  88.0 19.1 %collective-permute-start.19 = (bf16[1280,256]{1,0:T(8,128)(2,1)}, bf16[1280,256]{1,0:T(8,128)(2,1)}, u32[]{:S(2)}, u32[]{:S(2)}) collective-permute-start(bf16[1280,256]{1,0:T(8,128)(2,1)} %bitcast.34), channel_id=1, source_target_pairs={{0,64},{4,20},{8,72},{12,28},{16,80},{20,4},{24,88},{28,12},{32,96... | collective-permute-start | bytes 1966088 | tf_op jit(solution)/shard_map/ppermute | solution.py:37
  90.4 16.7 %collective-permute-start.20 = (bf16[1280,256]{1,0:T(8,128)(2,1)}, bf16[1280,256]{1,0:T(8,128)(2,1)}, u32[]{:S(2)}, u32[]{:S(2)}) collective-permute-start(bf16[1280,256]{1,0:T(8,128)(2,1)} %bitcast.35), channel_id=1, source_target_pairs={{0,96},{4,28},{8,104},{12,4},{16,112},{20,12},{24,120},{28,20},{32... | collective-permute-start | bytes 1966088 | tf_op jit(solution)/shard_map/ppermute | solution.py:37
  91.9 1.0 copy-start.3
  92.9 1.0 copy-start.5
  101.8 20.8 %all-to-all-start.2 = ((bf16[32,24,640]{2,1,0:T(8,128)(2,1)}), bf16[32,24,640]{2,1,0:T(8,128)(2,1)S(1)}, u32[]{:S(2)}, u32[]{:S(2)}) async-start(bf16[32,24,640]{2,1,0:T(8,128)(2,1)} %bitcast.40), calls=%async_computation.2 | async-start | bytes 1966080 | tf_op jit(solution)/shard_map/all_to_all | solution.py:71
  107.1 0.9 copy-start.12
  116.9 13.6 %copy-start.11 = (f32[160,1280]{1,0:T(8,128)S(1)}, f32[160,1280]{1,0:T(8,128)}, u32[]{:S(2)}) copy-start(f32[160,1280]{1,0:T(8,128)} %get-tuple-element.95) | copy-start | bytes 2457604
  116.9 8.9 %collective-permute-start.21 = (bf16[160,1280]{1,0:T(8,128)(2,1)}, bf16[160,1280]{1,0:T(8,128)(2,1)S(1)}, u32[]{:S(2)}, u32[]{:S(2)}) collective-permute-start(bf16[160,1280]{1,0:T(8,128)(2,1)} %get-tuple-element.85), channel_id=1, source_target_pairs={{0,16},{4,68},{8,24},{12,76},{16,0},{20,84},{24,8},{28,92},{32,48}... | collective-permute-start | bytes 1228808 | tf_op jit(solution)/shard_map/ppermute | solution.py:37
  119.8 10.3 %collective-permute-start.22 = (bf16[160,1280]{1,0:T(8,128)(2,1)}, bf16[160,1280]{1,0:T(8,128)(2,1)S(1)}, u32[]{:S(2)}, u32[]{:S(2)}) collective-permute-start(bf16[160,1280]{1,0:T(8,128)(2,1)} %get-tuple-element.86), channel_id=1, source_target_pairs={{0,8},{4,36},{8,16},{12,44},{16,24},{20,52},{24,0},{28,60},{32,40}... | collective-permute-start | bytes 1228808 | tf_op jit(solution)/shard_map/ppermute | solution.py:37
  120.2 10.3 %collective-permute-start.23 = (bf16[160,1280]{1,0:T(8,128)(2,1)}, bf16[160,1280]{1,0:T(8,128)(2,1)S(1)}, u32[]{:S(2)}, u32[]{:S(2)}) collective-permute-start(bf16[160,1280]{1,0:T(8,128)(2,1)} %get-tuple-element.87), channel_id=1, source_target_pairs={{0,24},{4,100},{8,0},{12,108},{16,8},{20,116},{24,16},{28,124},{32... | collective-permute-start | bytes 1228808 | tf_op jit(solution)/shard_map/ppermute | solution.py:37
